TPU v7x, 32 devices: a whole 2x2x4 slice. The times are simulated.
32 devices in a mesh: seqo: 8 (over y, x, core), seqi: 4 (over z).
Axes of the slice: x: 2, y: 2, z: 4, core: 2. Of those that a mesh axis runs over, the one named last changes fastest.
Arguments:
- query_rows: bfloat16 [4096, 2048], P(('seqo', 'seqi')), may hold values from -88 to 88
- key_rows: bfloat16 [4096, 2048], P(('seqo', 'seqi')), may hold values from -4 to 4
- value_rows: bfloat16 [4096, 2048], P(('seqo', 'seqi')), may hold values from -6 to 6
- upstream: bfloat16 [4096, 2048], P(('seqo', 'seqi')), may hold values from -6 to 6
Outputs:
- attended: bfloat16 [4096, 2048], P(('seqo', 'seqi'))
- grad_queries: bfloat16 [4096, 2048], P(('seqo', 'seqi'))
- grad_keys: bfloat16 [4096, 2048], P(('seqo', 'seqi'))
- grad_values: bfloat16 [4096, 2048], P(('seqo', 'seqi'))
All inputs are finite; a program needn't handle non-finite values.
Results may differ from a plain program's by a relative error of at most 0.025.
Values may be sent and summed in bfloat16 or wider, within the bound.
No kernel may reach another device: no remote copies, remote signals or barrier semaphores. Data moves between devices by JAX's collectives and lax.ppermute only.
A program may use at most 64 MiB of HBM per device.

v0:
```python
from functools import reduce

import jax
import jax.numpy as jnp
import numpy as np
from jax import lax
from jax.sharding import PartitionSpec as P

HEADS = 16
HEAD_DIM = 128
TILE = 128


def forward_level(query_matrix, key_portion_rows, value_portion_rows, score_scale):
    scores = (
        jnp.einsum(
            "ltk,jtk->tlj", query_matrix, key_portion_rows, preferred_element_type=jnp.float32
        )
        * score_scale
    )
    highest = jnp.max(scores, axis=2)
    attention_weights = jnp.exp(scores - highest[:, :, None])
    totals = jnp.sum(attention_weights, axis=2)
    numerator = jnp.einsum(
        "srt,tsx->rsx",
        attention_weights.astype(jnp.bfloat16),
        value_portion_rows,
        preferred_element_type=jnp.float32,
    )
    return (numerator / jnp.transpose(totals)[:, :, None], jnp.transpose(highest + jnp.log(totals)))


def grad_scores(
    query_matrix,
    key_portion_rows,
    value_portion_rows,
    upstream,
    level_log,
    level_delta,
    score_scale,
):
    scores = (
        jnp.einsum(
            "ltk,jtk->tlj", query_matrix, key_portion_rows, preferred_element_type=jnp.float32
        )
        * score_scale
    )
    attention_weights = jnp.exp(scores - jnp.transpose(level_log)[:, :, None])
    weight_grad = jnp.einsum(
        "ltk,jtk->tlj", upstream, value_portion_rows, preferred_element_type=jnp.float32
    )
    score_gradient = (
        attention_weights * (weight_grad - jnp.transpose(level_delta)[:, :, None])
    ).astype(jnp.bfloat16)
    return (attention_weights.astype(jnp.bfloat16), score_gradient)


def query_grad(score_gradient, key_portion_rows, score_scale):
    return (
        jnp.einsum(
            "srt,tsx->rsx", score_gradient, key_portion_rows, preferred_element_type=jnp.float32
        )
        * score_scale
    )


def key_grads(attention_weights_reduced, score_gradient, query_matrix, upstream, score_scale):
    key_grad = (
        jnp.einsum("ibt,big->tig", score_gradient, query_matrix, preferred_element_type=jnp.float32)
        * score_scale
    )
    value_grad = jnp.einsum(
        "ibt,big->tig", attention_weights_reduced, upstream, preferred_element_type=jnp.float32
    )
    return (key_grad, value_grad)


def pick_dilated(tensor):
    head_count = tensor.shape[1]
    grouped = tensor.reshape((tensor.shape[0] // 4, 4) + tensor.shape[1:])
    return grouped[:, np.arange(head_count) % 4, np.arange(head_count)]


def spread_dilated(tensor):
    head_count = tensor.shape[1]
    pattern = (np.arange(4)[:, None] == np.arange(head_count)[None, :] % 4).astype(np.float32)
    pattern = pattern.reshape((1, 4, head_count) + (1,) * (tensor.ndim - 2))
    spread = tensor[:, None] * pattern
    return spread.reshape((tensor.shape[0] * 4,) + tensor.shape[1:])


def combine_levels(outputs, logs, covers):
    safe_logs = [
        jnp.where(covered > 0, level_log, logs[0]) for level_log, covered in zip(logs, covers)
    ]
    highest = reduce(jnp.maximum, safe_logs)
    shares = [
        covered * jnp.exp(level_log - highest) for level_log, covered in zip(safe_logs, covers)
    ]
    summed = reduce(jnp.add, shares)
    merged = reduce(
        jnp.add, [portion[..., None] * output for portion, output in zip(shares, outputs)]
    )
    return (merged / summed[..., None], highest + jnp.log(summed))


def local(query_rows, key_rows, value_rows, upstream):
    row_count = query_rows.shape[0]
    quarter = row_count // 4
    feature_width = HEADS * HEAD_DIM
    score_scale = HEAD_DIM ** (-0.5)
    query_heads = query_rows.reshape(row_count, HEADS, HEAD_DIM)
    key_heads = key_rows.reshape(row_count, HEADS, HEAD_DIM)
    value_heads = value_rows.reshape(row_count, HEADS, HEAD_DIM)
    grad_heads = upstream.reshape(row_count, HEADS, HEAD_DIM)
    near_out, near_log = forward_level(query_heads, key_heads, value_heads, score_scale)
    query_dilated = pick_dilated(query_heads)
    key_dilated = pick_dilated(key_heads)
    value_dilated = pick_dilated(value_heads)
    grad_dilated = pick_dilated(grad_heads)
    group_keys, group_values = (
        lax.all_gather(key_dilated.reshape(quarter, feature_width), "seqi", axis=0, tiled=True),
        lax.all_gather(value_dilated.reshape(quarter, feature_width), "seqi", axis=0, tiled=True),
    )
    group_keys = group_keys.reshape(-1, HEADS, HEAD_DIM)
    group_values = group_values.reshape(-1, HEADS, HEAD_DIM)
    middle_out, middle_log = forward_level(query_dilated, group_keys, group_values, score_scale)
    position = lax.axis_index("seqi")
    inner_count = lax.axis_size("seqi")
    slot_count = max(1, HEADS // inner_count)
    first_head = (position * HEADS + inner_count - 1) // inner_count
    slot_heads = first_head + jnp.arange(slot_count, dtype=jnp.int32)
    slot_valid = (slot_heads * inner_count // HEADS == position) & (slot_heads < HEADS)
    slot_table = (slot_heads[:, None] == jnp.arange(HEADS, dtype=jnp.int32)[None, :]) & slot_valid[
        :, None
    ]
    table_half = slot_table.astype(jnp.bfloat16)
    table_float = slot_table.astype(jnp.float32)
    tile_width = slot_count * HEAD_DIM
    padding = ((0, row_count - TILE), (0, 0), (0, 0))

    def pick_tile(tensor):
        return jnp.einsum(
            "sh,thd->tsd", table_half, tensor, preferred_element_type=jnp.float32
        ).astype(jnp.bfloat16)

    def spread_tile(tensor):
        return jnp.pad(
            jnp.einsum("sh,tsd->thd", table_float, tensor, precision=lax.Precision.HIGHEST), padding
        )

    query_tile = pick_tile(query_heads)
    key_tile = pick_tile(key_heads)
    value_tile = pick_tile(value_heads)
    grad_tile = pick_tile(grad_heads)
    line_keys, line_values = (
        lax.all_gather(key_tile.reshape(TILE, tile_width), "seqo", axis=0, tiled=True),
        lax.all_gather(value_tile.reshape(TILE, tile_width), "seqo", axis=0, tiled=True),
    )
    line_keys = line_keys.reshape(-1, slot_count, HEAD_DIM)
    line_values = line_values.reshape(-1, slot_count, HEAD_DIM)
    far_out, far_log = forward_level(query_tile, line_keys, line_values, score_scale)
    far_cover = jnp.sum(table_float, axis=0)
    tile_cover = jnp.broadcast_to(far_cover[None, :], (TILE, HEADS))
    far_log_heads = jnp.einsum("sh,ts->th", table_float, far_log, precision=lax.Precision.HIGHEST)
    merged, total_log = combine_levels(
        [near_out, spread_dilated(middle_out), spread_tile(far_out)],
        [near_log, spread_dilated(middle_log), far_log_heads],
        [jnp.ones_like(near_log), spread_dilated(jnp.ones_like(middle_log)), tile_cover],
    )
    attended = merged.astype(jnp.bfloat16)
    row_delta = jnp.sum(grad_heads.astype(jnp.float32) * attended.astype(jnp.float32), axis=2)
    near_weights, near_scores = grad_scores(
        query_heads, key_heads, value_heads, grad_heads, total_log, row_delta, score_scale
    )
    near_query = query_grad(near_scores, key_heads, score_scale)
    near_key, near_value = key_grads(
        near_weights, near_scores, query_heads, grad_heads, score_scale
    )
    log_dilated = pick_dilated(total_log)
    delta_dilated = pick_dilated(row_delta)
    group_log, group_delta = (
        lax.all_gather(log_dilated, "seqi", axis=0, tiled=True),
        lax.all_gather(delta_dilated, "seqi", axis=0, tiled=True),
    )
    empty = jnp.zeros((quarter, HEADS, HEAD_DIM), jnp.float32)
    attention_weights_reduced, scores_half = grad_scores(
        query_dilated,
        group_keys,
        group_values,
        grad_dilated,
        log_dilated,
        delta_dilated,
        score_scale,
    )
    middle_query = query_grad(scores_half, group_keys, score_scale)
    totals = (empty, empty)
    pieces = (
        lax.all_gather(query_dilated.reshape(quarter, feature_width), "seqi", axis=0, tiled=True),
        lax.all_gather(grad_dilated.reshape(quarter, feature_width), "seqi", axis=0, tiled=True),
    )
    piece_query, piece_grad = [member.reshape(-1, HEADS, HEAD_DIM) for member in pieces]
    offset = jnp.int32(0)
    piece_rows = piece_query.shape[0]
    piece_log = lax.dynamic_slice_in_dim(group_log, offset, piece_rows, 0)
    piece_delta = lax.dynamic_slice_in_dim(group_delta, offset, piece_rows, 0)
    attention_weights_reduced, scores_half = grad_scores(
        piece_query, key_dilated, value_dilated, piece_grad, piece_log, piece_delta, score_scale
    )
    key_portion_rows, value_portion_rows = key_grads(
        attention_weights_reduced, scores_half, piece_query, piece_grad, score_scale
    )
    middle_key = totals[0] + key_portion_rows
    middle_value = totals[1] + value_portion_rows
    tile_log = jnp.einsum(
        "sh,th->ts", table_float, total_log[:TILE], precision=lax.Precision.HIGHEST
    )
    tile_delta = jnp.einsum(
        "sh,th->ts", table_float, row_delta[:TILE], precision=lax.Precision.HIGHEST
    )
    line_weights, line_scores = grad_scores(
        query_tile, line_keys, line_values, grad_tile, tile_log, tile_delta, score_scale
    )
    far_query = query_grad(line_scores, line_keys, score_scale)
    tile_empty = jnp.zeros((TILE, slot_count, HEAD_DIM), jnp.float32)
    line_log, line_delta = (
        lax.all_gather(tile_log, "seqo", axis=0, tiled=True),
        lax.all_gather(tile_delta, "seqo", axis=0, tiled=True),
    )
    totals = (tile_empty, tile_empty)
    pieces = (
        lax.all_gather(query_tile.reshape(TILE, tile_width), "seqo", axis=0, tiled=True),
        lax.all_gather(grad_tile.reshape(TILE, tile_width), "seqo", axis=0, tiled=True),
    )
    piece_query, piece_grad = [member.reshape(-1, slot_count, HEAD_DIM) for member in pieces]
    piece_rows = piece_query.shape[0]
    piece_log = lax.slice_in_dim(line_log, 0, piece_rows, axis=0)
    piece_delta = lax.slice_in_dim(line_delta, 0, piece_rows, axis=0)
    attention_weights_reduced, scores_half = grad_scores(
        piece_query, key_tile, value_tile, piece_grad, piece_log, piece_delta, score_scale
    )
    key_portion_rows, value_portion_rows = key_grads(
        attention_weights_reduced, scores_half, piece_query, piece_grad, score_scale
    )
    far_key = totals[0] + key_portion_rows
    far_value = totals[1] + value_portion_rows
    grad_query = near_query + spread_dilated(middle_query) + spread_tile(far_query)
    grad_key = near_key + spread_dilated(middle_key) + spread_tile(far_key)
    grad_value = near_value + spread_dilated(middle_value) + spread_tile(far_value)
    return (
        attended.reshape(row_count, feature_width),
        grad_query.astype(jnp.bfloat16).reshape(row_count, feature_width),
        grad_key.astype(jnp.bfloat16).reshape(row_count, feature_width),
        grad_value.astype(jnp.bfloat16).reshape(row_count, feature_width),
    )


def solution(mesh):
    return jax.shard_map(
        local,
        mesh=mesh,
        in_specs=(
            P(("seqo", "seqi"), None),
            P(("seqo", "seqi"), None),
            P(("seqo", "seqi"), None),
            P(("seqo", "seqi"), None),
        ),
        out_specs=(
            P(("seqo", "seqi"), None),
            P(("seqo", "seqi"), None),
            P(("seqo", "seqi"), None),
            P(("seqo", "seqi"), None),
        ),
        check_vma=False,
    )
```

profile of v0, /device:TPU:0, one launch (start us, length us, event | category | flops | bytes accessed | tf_op | source)
XLA Modules:
  0.0 235.9 jit_solution(10120588585347531488)
XLA Ops:
  18.3 17.4 %all_gather.36 = bf16[128,2048]{1,0:T(8,128)(2,1)S(1)} all-gather(bf16[32,2048]{1,0:T(8,128)(2,1)S(1)} %copy_bitcast_fusion.4), channel_id=1, replica_groups=mesh['seqo'=8,'seqi'=4] {'seqi'}, dimensions={0}, use_global_device_ids=true | all-gather | bytes 655360 | tf_op jit(solution)/shard_map/all_gather | solution.py:122
  43.1 16.3 %all_gather.38 = bf16[128,2048]{1,0:T(8,128)(2,1)S(1)} all-gather(bf16[32,2048]{1,0:T(8,128)(2,1)S(1)} %copy_bitcast_fusion.3), channel_id=1, replica_groups=mesh['seqo'=8,'seqi'=4] {'seqi'}, dimensions={0}, use_global_device_ids=true | all-gather | bytes 655360 | tf_op jit(solution)/shard_map/all_gather | solution.py:123
  63.7 16.3 %all_gather.40 = bf16[128,2048]{1,0:T(8,128)(2,1)S(1)} all-gather(bf16[32,2048]{1,0:T(8,128)(2,1)S(1)} %copy-done.27), channel_id=1, replica_groups=mesh['seqo'=8,'seqi'=4] {'seqi'}, dimensions={0}, use_global_device_ids=true | all-gather | bytes 655360 | tf_op jit(solution)/shard_map/all_gather | solution.py:199
  81.0 15.0 %all_gather.42 = bf16[128,2048]{1,0:T(8,128)(2,1)S(1)} all-gather(bf16[32,2048]{1,0:T(8,128)(2,1)S(1)} %copy_bitcast_fusion.1), channel_id=1, replica_groups=mesh['seqo'=8,'seqi'=4] {'seqi'}, dimensions={0}, use_global_device_ids=true | all-gather | bytes 655360 | tf_op jit(solution)/shard_map/all_gather | solution.py:200
  97.0 1.9 multiply_reduce_fusion
  100.6 2.3 copy.302
  102.9 2.6 %fusion.33 = f32[128,4,128]{0,2,1:T(8,128)} fusion(bf16[1024,4,128]{0,2,1:T(8,128)(2,1)} %bitcast.289, f32[4,128,1024]{2,1,0:T(8,128)S(1)} %get-tuple-element.32, f32[4,128]{1,0:T(4,128)} %copy-done.43, f32[128,4]{0,1:T(4,128)} %bitcast.318), kind=kOutput, calls=%fused_computation.60 | convolution fusion | flops 135856128 | bytes 3411968 | tf_op jit(solution)/shard_map/srt,tsx->rsx/dot_general | solution.py:24
  105.5 1.8 copy.303
  107.3 2.5 %fusion.92 = f32[128,128,16]{1,2,0:T(8,128)} fusion(f32[128,4,128]{2,1,0:T(4,128)} %copy.303, pred[4,16]{1,0:T(4,128)(4,1)S(1)} %get-tuple-element.30), kind=kOutput, calls=%fused_computation.137 | convolution fusion | flops 12582912 | bytes 1310784 | tf_op jit(solution)/shard_map/sh,tsd->thd/dot_general | solution.py:149
  109.8 2.6 %copy.304 = f32[128,128,16]{0,1,2:T(8,128)} copy(f32[128,128,16]{1,2,0:T(8,128)} %fusion.92) | data formatting | bytes 2097152 | tf_op jit(solution)/shard_map/sh,tsd->thd/dot_general | solution.py:149
  114.1 3.4 %multiply_reduce_fusion.1 = (f32[128,16]{0,1:T(8,128)S(1)}, bf16[128,16,128]{0,2,1:T(8,128)(2,1)}) fusion(bf16[128,2048]{0,1:T(8,128)(2,1)} %copy-done, f32[128,16]{0,1:T(8,128)S(1)} %get-tuple-element.25, f32[128,128,16]{0,1,2:T(8,128)} %copy.304, f32[128,16]{0,1:T(8,128)S(1)} %get-tuple-element.28, f32[128,16,128]{0,2,1:T(8,128)} %copy.301, ...), kind=kOutput, calls=%fused_computation.80 | convolution fusion | flops 71038976 | bytes 4784128 | tf_op jit(solution)/shard_map/srt,tsx->rsx/dot_general | solution.py:24
  122.3 2.0 copy.352
  124.3 3.5 %fusion.25 = f32[128,4,128]{0,2,1:T(8,128)} fusion(bf16[1024,4,128]{0,2,1:T(8,128)(2,1)} %bitcast.292, f32[4,128,1024]{2,1,0:T(8,128)S(1)} %get-tuple-element.32, bf16[128,4,128]{0,2,1:T(8,128)(2,1)} %copy.376, bf16[1024,4,128]{0,2,1:T(8,128)(2,1)} %bitcast.290, f32[4,128]{1,0:T(4,128)} %bitcast.316, f32[4,128]{1,0:T(4,128)} %bitcast.317), kind=kOutput, calls=%fused_computation.42 | convolution fusion | flops 271122432 | bytes 4591616 | tf_op jit(solution)/shard_map/srt,tsx->rsx/dot_general | solution.py:60
  129.0 1.6 fusion.89
  133.7 1.9 gather_fusion.5
  137.2 1.9 gather_fusion.3
  139.1 2.2 fusion.27
  143.6 2.6 %copy.319 = f32[128,16,128]{0,2,1:T(8,128)} copy(f32[128,16,128]{2,1,0:T(8,128)} %bitcast.272) | data formatting | bytes 2097152 | tf_op jit(solution)/shard_map/mul | solution.py:88
  149.9 8.9 %all_gather.47 = f32[1024,4]{0,1:T(4,128)S(1)} all-gather(f32[128,4]{0,1:T(4,128)S(1)} %copy-done.41), channel_id=1, replica_groups=mesh['seqo'=8,'seqi'=4] {'seqo'}, dimensions={0}, use_global_device_ids=true | all-gather | bytes 18432 | tf_op jit(solution)/shard_map/all_gather | solution.py:228
  158.8 9.1 %all_gather.45 = f32[1024,4]{0,1:T(4,128)S(1)} all-gather(f32[128,4]{0,1:T(4,128)S(1)} %copy-done.42), channel_id=1, replica_groups=mesh['seqo'=8,'seqi'=4] {'seqo'}, dimensions={0}, use_global_device_ids=true | all-gather | bytes 18432 | tf_op jit(solution)/shard_map/all_gather | solution.py:227
  167.9 1.8 fusion.106
  169.7 2.8 %convolution_bitcast_fusion.4 = f32[128,4,128]{0,2,1:T(8,128)} fusion(bf16[1024,4,128]{0,2,1:T(8,128)(2,1)} %bitcast.287, f32[4,1024,128]{2,1,0:T(8,128)S(1)} %fusion.106, f32[4,1024]{1,0:T(4,128)S(1)} %bitcast.309), kind=kOutput, calls=%fused_computation.58 | convolution fusion | flops 135790592 | bytes 3424256 | tf_op jit(solution)/shard_map/ibt,big->tig/dot_general | solution.py:72
  172.5 3.9 %fusion.23 = f32[128,4,128]{0,2,1:T(8,128)} fusion(bf16[1024,4,128]{0,2,1:T(8,128)(2,1)} %bitcast.286, f32[4,1024,128]{2,1,0:T(8,128)S(1)} %fusion.106, bf16[1024,4,128]{0,2,1:T(8,128)(2,1)} %bitcast.288, f32[4,1024]{1,0:T(4,128)S(1)} %bitcast.315, f32[4,1024]{1,0:T(4,128)S(1)} %bitcast.310, bf16[128,4,128]{2,1,0:T(4,128)(2,1)S(1)} %bitcast.299), kind=kOutput, calls=%fused_computation.40 | convolution fusion | flops 271122432 | bytes 4620288 | tf_op jit(solution)/shard_map/ibt,big->tig/dot_general | solution.py:69
  177.6 1.6 fusion.87
  179.2 1.6 copy.345
  180.8 13.3 %all-gather = f32[4,32,16]{1,2,0:T(8,128)S(1)} all-gather(f32[1,32,16]{1,2,0:T(8,128)} %bitcast.307), channel_id=1, replica_groups=mesh['seqo'=8,'seqi'=4] {'seqi'}, dimensions={0}, use_global_device_ids=true | all-gather | bytes 10240 | tf_op jit(solution)/shard_map/all_gather | solution.py:183
  194.8 13.3 %all-gather.1 = f32[4,32,16]{1,2,0:T(8,128)S(1)} all-gather(f32[1,32,16]{1,2,0:T(8,128)} %bitcast.306), channel_id=1, replica_groups=mesh['seqo'=8,'seqi'=4] {'seqi'}, dimensions={0}, use_global_device_ids=true | all-gather | bytes 10240 | tf_op jit(solution)/shard_map/all_gather | solution.py:184
  210.9 2.1 fusion.26
  215.3 2.6 %copy.337 = f32[128,16,128]{0,2,1:T(8,128)} copy(f32[128,16,128]{2,1,0:T(8,128)} %bitcast.273) | data formatting | bytes 2097152 | tf_op jit(solution)/shard_map/mul | solution.py:88
  217.9 2.6 %fusion.20 = bf16[128,16,128]{0,2,1:T(8,128)(2,1)} fusion(bf16[16,128,128]{1,2,0:T(8,128)(2,1)S(1)} %copy-done.4, bf16[128,16,128]{0,2,1:T(8,128)(2,1)S(1)} %copy-done.10, f32[128,128,16]{0,1,2:T(8,128)S(1)} %copy.345, f32[128,16,128]{0,2,1:T(8,128)} %copy.337, f32[128,16]{0,1:T(8,128)S(1)} %copy.281), kind=kOutput, calls=%fused_computation.37 | convolution fusion | flops 68419584 | bytes 3678208 | tf_op jit(solution)/shard_map/ibt,big->tig/dot_general | solution.py:69
  220.4 2.0 copy.354
  226.3 2.0 fusion.18
  (183 shorter events, 56.2 us)
Async XLA Ops:
  7.2 3.0 %copy-start.17 = (bf16[128,2048]{1,0:T(8,128)(2,1)S(1)}, bf16[128,2048]{1,0:T(8,128)(2,1)}, u32[]{:S(2)}) copy-start(bf16[128,2048]{1,0:T(8,128)(2,1)} %param.36) | copy-start | bytes 1572868
  7.2 89.8 %all-gather.7.cloned.1.call-start = ((), (), s32[]{:S(2)}) async-start(), calls=%async_computation | async-start | bytes 1179648 | tf_op jit(solution)/shard_map/all_gather | solution.py:157
  7.3 4.9 %copy-start.28 = (bf16[128,2048]{1,0:T(8,128)(2,1)S(1)}, bf16[128,2048]{1,0:T(8,128)(2,1)}, u32[]{:S(2)}) copy-start(bf16[128,2048]{1,0:T(8,128)(2,1)} %param.34) | copy-start | bytes 1572868
  10.1 90.5 %all-gather.9.cloned.1.call-start = ((), (), s32[]{:S(2)}) async-start(), calls=%async_computation.1 | async-start | bytes 1179648 | tf_op jit(solution)/shard_map/all_gather | solution.py:158
  10.2 3.1 %copy-start.18 = (bf16[128,2048]{1,0:T(8,128)(2,1)S(1)}, bf16[128,2048]{1,0:T(8,128)(2,1)}, u32[]{:S(2)}) copy-start(bf16[128,2048]{1,0:T(8,128)(2,1)} %param.37) | copy-start | bytes 1572868
  12.1 155.8 %all-gather.11.cloned.1.call-start = ((), (), s32[]{:S(2)}) async-start(), calls=%async_computation.2 | async-start | bytes 1179648 | tf_op jit(solution)/shard_map/all_gather | solution.py:232
  13.3 156.4 %all-gather.13.cloned.1.call-start = ((), (), s32[]{:S(2)}) async-start(), calls=%async_computation.3 | async-start | bytes 1179648 | tf_op jit(solution)/shard_map/all_gather | solution.py:233
  13.6 1.9 copy-start
  35.6 5.9 %copy-start.15 = (bf16[16,8,16,128]{3,2,1,0:T(8,128)(2,1)S(1)}, bf16[16,8,16,128]{3,2,1,0:T(8,128)(2,1)}, u32[]{:S(2)}) copy-start(bf16[16,8,16,128]{3,2,1,0:T(8,128)(2,1)} %copy-done.14) | copy-start | bytes 1572868
  35.9 5.9 %copy-start.7 = (bf16[128,2048]{0,1:T(8,128)(2,1)}, bf16[128,2048]{0,1:T(8,128)(2,1)S(1)}, u32[]{:S(2)}) copy-start(bf16[128,2048]{0,1:T(8,128)(2,1)S(1)} %copy.285) | copy-start | bytes 1572868
  37.9 4.0 %copy-start.35 = (f32[16,32]{1,0:T(8,128)}, f32[16,32]{1,0:T(8,128)S(1)}, u32[]{:S(2)}) copy-start(f32[16,32]{1,0:T(8,128)S(1)} %get-tuple-element.33) | copy-start | bytes 6148
  38.1 2.2 copy-start.39
  41.9 17.9 %copy-start.40 = (f32[16,32]{1,0:T(8,128)S(1)}, f32[16,32]{1,0:T(8,128)}, u32[]{:S(2)}) copy-start(f32[16,32]{1,0:T(8,128)} %copy-done.39) | copy-start | bytes 6148
  60.9 1.7 copy-start.19
  63.7 33.3 %copy-start.24 = (bf16[16,32,128]{2,1,0:T(8,128)(2,1)}, bf16[16,32,128]{2,1,0:T(8,128)(2,1)S(1)}, u32[]{:S(2)}) copy-start(bf16[16,32,128]{2,1,0:T(8,128)(2,1)S(1)} %gather_fusion.4) | copy-start | bytes 393220
  114.1 4.7 %copy-start.31 = (f32[128,16]{0,1:T(8,128)}, f32[128,16]{0,1:T(8,128)S(1)}, u32[]{:S(2)}) copy-start(f32[128,16]{0,1:T(8,128)S(1)} %get-tuple-element.24) | copy-start | bytes 24580
  127.8 11.3 %copy-start.8 = (bf16[128,2048]{0,1:T(8,128)(2,1)S(1)}, bf16[128,2048]{0,1:T(8,128)(2,1)}, u32[]{:S(2)}) copy-start(bf16[128,2048]{0,1:T(8,128)(2,1)} %copy-done.7) | copy-start | bytes 1572868
  127.8 11.3 %copy-start.21 = (bf16[128,2048]{0,1:T(8,128)(2,1)S(1)}, bf16[128,2048]{0,1:T(8,128)(2,1)}, u32[]{:S(2)}) copy-start(bf16[128,2048]{0,1:T(8,128)(2,1)} %copy-done.20) | copy-start | bytes 1572868
  141.3 4.9 %copy-start.1 = (bf16[128,2048]{0,1:T(8,128)(2,1)S(1)}, bf16[128,2048]{0,1:T(8,128)(2,1)}, u32[]{:S(2)}) copy-start(bf16[128,2048]{0,1:T(8,128)(2,1)} %copy-done) | copy-start | bytes 1572868
  141.3 4.9 %copy-start.32 = (f32[128,16]{0,1:T(8,128)S(1)}, f32[128,16]{0,1:T(8,128)}, u32[]{:S(2)}) copy-start(f32[128,16]{0,1:T(8,128)} %copy-done.31) | copy-start | bytes 24580
  141.3 4.9 %copy-start.37 = (f32[128,16]{0,1:T(8,128)S(1)}, f32[128,16]{0,1:T(8,128)}, u32[]{:S(2)}) copy-start(f32[128,16]{0,1:T(8,128)} %copy-done.36) | copy-start | bytes 24580
  143.6 4.9 %copy-start.12 = (bf16[128,16,128]{0,2,1:T(8,128)(2,1)S(1)}, bf16[128,16,128]{0,2,1:T(8,128)(2,1)}, u32[]{:S(2)}) copy-start(bf16[128,16,128]{0,2,1:T(8,128)(2,1)} %copy-done.11) | copy-start | bytes 1572868
  146.2 2.3 copy-start.16
  148.5 10.3 %copy-start.42 = (f32[128,4]{0,1:T(4,128)S(1)}, f32[128,4]{0,1:T(4,128)}, u32[]{:S(2)}) copy-start(f32[128,4]{0,1:T(4,128)} %fusion.104) | copy-start | bytes 6148
  148.5 19.4 %copy-start.22 = (bf16[128,4,128]{0,2,1:T(8,128)(2,1)S(1)}, bf16[128,4,128]{0,2,1:T(8,128)(2,1)}, u32[]{:S(2)}) copy-start(bf16[128,4,128]{0,2,1:T(8,128)(2,1)} %copy.374) | copy-start | bytes 393220
  169.7 2.8 %copy-start.30 = (bf16[4,128,128]{2,0,1:T(4,128)(2,1)S(1)}, bf16[4,128,128]{2,0,1:T(4,128)(2,1)}, u32[]{:S(2)}) copy-start(bf16[4,128,128]{2,0,1:T(4,128)(2,1)} %copy-done.29) | copy-start | bytes 393220
  176.4 32.4 %copy-start.6 = (bf16[128,2048]{0,1:T(8,128)(2,1)S(1)}, bf16[128,2048]{0,1:T(8,128)(2,1)}, u32[]{:S(2)}) copy-start(bf16[128,2048]{0,1:T(8,128)(2,1)} %copy.328) | copy-start | bytes 1572868
  177.6 32.2 %copy-start.13 = (bf16[128,2048]{0,1:T(8,128)(2,1)S(1)}, bf16[128,2048]{0,1:T(8,128)(2,1)}, u32[]{:S(2)}) copy-start(bf16[128,2048]{0,1:T(8,128)(2,1)} %copy.332) | copy-start | bytes 1572868
  213.0 4.8 %copy-start.4 = (bf16[16,128,128]{1,2,0:T(8,128)(2,1)S(1)}, bf16[16,128,128]{1,2,0:T(8,128)(2,1)}, u32[]{:S(2)}) copy-start(bf16[16,128,128]{1,2,0:T(8,128)(2,1)} %copy-done.3) | copy-start | bytes 1572868
  213.0 4.8 %copy-start.10 = (bf16[128,16,128]{0,2,1:T(8,128)(2,1)S(1)}, bf16[128,16,128]{0,2,1:T(8,128)(2,1)}, u32[]{:S(2)}) copy-start(bf16[128,16,128]{0,2,1:T(8,128)(2,1)} %copy-done.9) | copy-start | bytes 1572868
  217.9 4.6 %copy-start.26 = (f32[128,4,128]{0,2,1:T(8,128)S(1)}, f32[128,4,128]{0,2,1:T(8,128)}, u32[]{:S(2)}) copy-start(f32[128,4,128]{0,2,1:T(8,128)} %convolution_bitcast_fusion.4) | copy-start | bytes 786436
  222.5 2.2 copy-start.25
  (16 other events, 17.1 us)
Sparse Core Ops, SparseCore 0:
  10.3 26.2 all-gather.6
  39.0 23.4 all-gather.8
  64.4 23.5 all-gather.10
  89.8 23.6 all-gather.12
where the time goes:
time: 237 us; the launch traced here: 236 us
  blocking collectives  109 us (46%)
  local copies, waits for them, and re-layouts  62.4 us (26%)
  matrix products  44 us (19%)
  between operations  14.4 us (6%)
  other arithmetic  5.4 us (2%)
    all_gather x1, blocking collectives, local(): lax.all_gather(key_dilated.reshape(quarter, feature_width), 'seqi', axis=...  17.4 us
    all_gather x1, blocking collectives, local(): lax.all_gather(value_dilated.reshape(quarter, feature_width), 'seqi', axi...  16.3 us
    all_gather x1, blocking collectives, local(): lax.all_gather(query_dilated.reshape(quarter, feature_width), 'seqi', axi...  16.3 us
    all_gather x1, blocking collectives, local(): lax.all_gather(grad_dilated.reshape(quarter, feature_width), 'seqi', axis...  15 us
    unnamed x100, local copies, waits for them, and re-layouts  13.5 us
    all_gather x1, blocking collectives, local(): lax.all_gather(delta_dilated, 'seqi', axis=0, tiled=True)  13.3 us
    all_gather x1, blocking collectives, local(): lax.all_gather(log_dilated, 'seqi', axis=0, tiled=True)  13.3 us
    mul x10, local copies, waits for them, and re-layouts, spread_dilated(): spread = tensor[:, None] * pattern  11.7 us
  transfers between devices with their start and end apart: 4, of which 0 were waited for; matrix products, arithmetic and copies ran while one was open for 31% of the time, Pallas kernels for 0%

commit v1 on v0

v1 whole, which is shorter than its diff:
```python
import functools

import jax
import jax.numpy as jnp
from jax import lax
from jax.experimental import pallas as pl
from jax.experimental.pallas import tpu as pltpu
from jax.sharding import PartitionSpec as P

HEADS = 16
HEAD_DIM = 128
DILATION = 4
SCALE = HEAD_DIM**-0.5
LOWEST = -1e30
VMEM_LIMIT = 48 * 1024 * 1024

NT = (((1,), (1,)), ((), ()))
TN = (((0,), (0,)), ((), ()))


def dot(a, b):
    return jnp.dot(a, b, preferred_element_type=jnp.float32)


def dot_nt(a, b):
    return lax.dot_general(a, b, NT, preferred_element_type=jnp.float32)


def dot_tn(a, b):
    return lax.dot_general(a, b, TN, preferred_element_type=jnp.float32)


def head_columns(head):
    return pl.ds(pl.multiple_of(head * HEAD_DIM, HEAD_DIM), HEAD_DIM)


def pick_kernel(slots, pos_ref, a_ref, b_ref, mid_ref, tile_ref, wide):
    rows = a_ref.shape[0]
    quarter = rows // DILATION
    for which, ref in enumerate((a_ref, b_ref)):
        for head in range(HEADS):
            cols = slice(head * HEAD_DIM, (head + 1) * HEAD_DIM)
            wide[head] = ref[:, cols].astype(jnp.float32)
            picked = wide[head, pl.ds(head % DILATION, quarter, stride=DILATION), :]
            mid_ref[which, :, cols] = picked.astype(jnp.bfloat16)
        width = slots * HEAD_DIM
        start = pl.multiple_of(pos_ref[0] * width, width)
        tile_ref[which] = ref[:, pl.ds(start, width)]


def merge(old, new):
    acc_a, max_a, sum_a = old
    acc_b, max_b, sum_b = new
    top = jnp.maximum(max_a, max_b)
    fa = jnp.exp(max_a - top)
    fb = jnp.exp(max_b - top)
    return acc_a * fa + acc_b * fb, top, sum_a * fa + sum_b * fb


def softmax_state(q, k, v):
    s = dot_nt(q, k) * SCALE
    top = jnp.max(s, axis=1, keepdims=True)
    p = jnp.exp(s - top)
    total = jnp.sum(p, axis=1, keepdims=True)
    return dot(p.astype(jnp.bfloat16), v), top, total


def gathered_mid(own, pairs, which, cols):
    parts = [own[which, :, cols]]
    for left, right in pairs:
        parts.append(left[which, :, cols] + right[which, :, cols])
    return jnp.concatenate(parts, axis=0)


def gathered_tile(tiles, which, slot):
    cols = slice(slot * HEAD_DIM, (slot + 1) * HEAD_DIM)
    return jnp.concatenate([tile[which, :, cols] for tile in tiles], axis=0)


def forward_kernel(n_i, n_o, slots, *refs):
    pos_ref, q_ref, k_ref, v_ref, u_ref, qmid_ref, own_mid = refs[:7]
    rest = refs[7:]
    pairs = [(rest[2 * d], rest[2 * d + 1]) for d in range(n_i - 1)]
    rest = rest[2 * (n_i - 1) :]
    tiles = rest[:n_o]
    rest = rest[n_o:]
    att_ref, comp_ref, midcol_ref, midrow_ref, tilerow_ref, gmid_ref = rest[:6]
    acc, mb, zb, turned = rest[6:]
    rows = q_ref.shape[0]
    quarter = rows // DILATION
    pos = pos_ref[0]

    def near(group, carry):
        for residue in range(DILATION):
            head = group * DILATION + residue
            cols = head_columns(head)
            state = softmax_state(q_ref[:, cols], k_ref[:, cols], v_ref[:, cols])
            acc[head] = state[0]
            mb[head] = jnp.broadcast_to(state[1], (rows, HEAD_DIM))
            zb[head] = jnp.broadcast_to(state[2], (rows, HEAD_DIM))
        return carry

    lax.fori_loop(0, HEADS // DILATION, near, 0)

    for slot in range(slots):
        head = pos * slots + slot
        cols = head_columns(head)
        state = softmax_state(
            q_ref[:, cols], gathered_tile(tiles, 0, slot), gathered_tile(tiles, 1, slot)
        )
        acc[head], mb[head], zb[head] = merge((acc[head], mb[head], zb[head]), state)

    comp_ref[...] = jnp.zeros_like(comp_ref)
    lane = lax.broadcasted_iota(jnp.int32, (rows, HEAD_DIM), 1)

    def middle(group, carry):
        for residue in range(DILATION):
            head = group * DILATION + residue
            cols = head_columns(head)
            keys = gathered_mid(own_mid, pairs, 0, cols)
            values = gathered_mid(own_mid, pairs, 1, cols)
            gmid_ref[0, :, cols] = keys
            gmid_ref[1, :, cols] = values
            state = softmax_state(qmid_ref[0, :, cols], keys, values)
            at = (head, pl.ds(residue, quarter, stride=DILATION), slice(None))
            acc[at], mb[at], zb[at] = merge((acc[at], mb[at], zb[at]), state)
            total = zb[head]
            out = (acc[head] / total).astype(jnp.bfloat16)
            att_ref[:, cols] = out
            lse = mb[head] + jnp.log(total)
            delta = jnp.sum(
                u_ref[:, cols].astype(jnp.float32) * out.astype(jnp.float32), axis=1, keepdims=True
            )
            comp_ref[...] = jnp.where(
                lane == head, lse, jnp.where(lane == HEADS + head, delta, comp_ref[...])
            )
        return carry

    lax.fori_loop(0, HEADS // DILATION, middle, 0)

    lane = lax.broadcasted_iota(jnp.int32, (quarter, HEAD_DIM), 1)
    mid = jnp.zeros((quarter, HEAD_DIM), jnp.float32)
    for residue in range(DILATION):
        part = comp_ref[pl.ds(residue, quarter, stride=DILATION), :]
        mid = jnp.where(lane % DILATION == residue, part, mid)
    midcol_ref[...] = mid
    midrow_ref[...] = mid.T[: 2 * HEADS]
    turned[...] = comp_ref[...].T
    tilerow_ref[:slots] = turned[pl.ds(pos * slots, slots), :]
    tilerow_ref[slots:] = turned[pl.ds(HEADS + pos * slots, slots), :]


def store_heads(out_ref, acc, scale):
    for head in range(HEADS):
        cols = slice(head * HEAD_DIM, (head + 1) * HEAD_DIM)
        out_ref[:, cols] = (acc[head] * scale).astype(jnp.bfloat16)


def column_of(ref, index):
    lane = lax.broadcasted_iota(jnp.int32, ref.shape, 1)
    return jnp.sum(jnp.where(lane == index, ref[...], 0.0), axis=1, keepdims=True)


def score_grads(s, dp, lse, delta):
    g = jnp.exp(s * SCALE - lse)
    return g.astype(jnp.bfloat16), (g * (dp - delta)).astype(jnp.bfloat16)


def query_side_kernel(n_o, slots, *refs):
    pos_ref, q_ref, k_ref, v_ref, u_ref, qmid_ref, gmid_ref, comp_ref, midcol_ref = refs[:9]
    tiles = refs[9 : 9 + n_o]
    dq_ref, dk_ref, dv_ref, acc = refs[9 + n_o :]
    rows = q_ref.shape[0]
    quarter = rows // DILATION
    pos = pos_ref[0]

    def near(group, carry):
        for residue in range(DILATION):
            head = group * DILATION + residue
            cols = head_columns(head)
            q, k, v, u = q_ref[:, cols], k_ref[:, cols], v_ref[:, cols], u_ref[:, cols]
            lse, delta = column_of(comp_ref, head), column_of(comp_ref, HEADS + head)
            p, ds = score_grads(dot_nt(q, k), dot_nt(u, v), lse, delta)
            acc[head] = dot(ds, k)
            dk_ref[head] = dot_tn(ds, q)
            dv_ref[head] = dot_tn(p, u)
            keys, values = gmid_ref[0, :, cols], gmid_ref[1, :, cols]
            q, u = qmid_ref[0, :, cols], qmid_ref[1, :, cols]
            lse, delta = column_of(midcol_ref, head), column_of(midcol_ref, HEADS + head)
            _, ds = score_grads(dot_nt(q, keys), dot_nt(u, values), lse, delta)
            acc[head, pl.ds(residue, quarter, stride=DILATION), :] += dot(ds, keys)
        return carry

    lax.fori_loop(0, HEADS // DILATION, near, 0)

    for slot in range(slots):
        head = pos * slots + slot
        cols = head_columns(head)
        lse, delta = column_of(comp_ref, head), column_of(comp_ref, HEADS + head)
        keys, values = gathered_tile(tiles, 0, slot), gathered_tile(tiles, 1, slot)
        s, dp = dot_nt(q_ref[:, cols], keys), dot_nt(u_ref[:, cols], values)
        _, ds = score_grads(s, dp, lse, delta)
        acc[head] += dot(ds, keys)
    store_heads(dq_ref, acc, SCALE)


def key_side_kernel(n_i, n_o, slots, *refs):
    pos_ref, kmid_ref, ktile_ref, dk0_ref, dv0_ref, own_mid = refs[:6]
    rest = refs[6:]
    pairs = [(rest[2 * d], rest[2 * d + 1]) for d in range(n_i - 1)]
    rest = rest[2 * (n_i - 1) :]
    tiles, rest = rest[:n_o], rest[n_o:]
    midrows, rest = rest[:n_i], rest[n_i:]
    tilerows, rest = rest[:n_o], rest[n_o:]
    dk_ref, dv_ref, dk, dv, stat = rest
    rows = dk0_ref.shape[1]
    quarter = rows // DILATION
    pos = pos_ref[0]
    stat[...] = jnp.concatenate([ref[...] for ref in midrows], axis=1)
    dk[...] = dk0_ref[...]
    dv[...] = dv0_ref[...]

    def middle(group, carry):
        for residue in range(DILATION):
            head = group * DILATION + residue
            cols = head_columns(head)
            k, v = kmid_ref[0, :, cols], kmid_ref[1, :, cols]
            queries = gathered_mid(own_mid, pairs, 0, cols)
            ups = gathered_mid(own_mid, pairs, 1, cols)
            lse, delta = stat[pl.ds(head, 1), :], stat[pl.ds(HEADS + head, 1), :]
            p, ds = score_grads(dot_nt(k, queries), dot_nt(v, ups), lse, delta)
            at = (head, pl.ds(residue, quarter, stride=DILATION), slice(None))
            dk[at] += dot(ds, queries)
            dv[at] += dot(p, ups)
        return carry

    lax.fori_loop(0, HEADS // DILATION, middle, 0)

    for slot in range(slots):
        head = pos * slots + slot
        own = slice(slot * HEAD_DIM, (slot + 1) * HEAD_DIM)
        queries, ups = gathered_tile(tiles, 0, slot), gathered_tile(tiles, 1, slot)
        lse = jnp.concatenate([ref[slot : slot + 1, :] for ref in tilerows], axis=1)
        delta = jnp.concatenate([ref[slots + slot : slots + slot + 1, :] for ref in tilerows], axis=1)
        s, dp = dot_nt(ktile_ref[0, :, own], queries), dot_nt(ktile_ref[1, :, own], ups)
        p, ds = score_grads(s, dp, lse, delta)
        dk[head] += dot(ds, queries)
        dv[head] += dot(p, ups)
    store_heads(dk_ref, dk, SCALE)
    store_heads(dv_ref, dv, 1.0)


def call(kernel, outs, scratch, name, flops, *operands):
    specs = [pl.BlockSpec(memory_space=pltpu.SMEM)]
    specs += [pl.BlockSpec(memory_space=pltpu.VMEM)] * (len(operands) - 1)
    moved = sum(x.size * x.dtype.itemsize for x in operands + tuple(outs))
    return pl.pallas_call(
        kernel,
        out_shape=tuple(outs),
        in_specs=specs,
        out_specs=tuple(pl.BlockSpec(memory_space=pltpu.VMEM) for _ in outs),
        scratch_shapes=scratch,
        compiler_params=pltpu.CompilerParams(vmem_limit_bytes=VMEM_LIMIT),
        cost_estimate=pl.CostEstimate(flops=flops, bytes_accessed=moved, transcendentals=0),
        name=name,
    )(*operands)


def line_gather(x, n):
    right, left = {0: x}, {0: x}
    for hop in range(1, n):
        right[hop] = lax.ppermute(right[hop - 1], "seqi", [(i, i + 1) for i in range(hop - 1, n - 1)])
        left[hop] = lax.ppermute(left[hop - 1], "seqi", [(i + 1, i) for i in range(n - hop)])
    return [t for d in range(1, n) for t in (left[d], right[n - d])]


def plane_gather(x, n):
    found = [x]
    for mask in range(2, n, 2):
        found.append(lax.ppermute(x, "seqo", [(i, i ^ mask) for i in range(n)]))
    return found + [lax.ppermute(t, "seqo", [(i, i ^ 1) for i in range(n)]) for t in found]


def local(query_rows, key_rows, value_rows, upstream):
    rows, width = query_rows.shape
    n_i, n_o = lax.axis_size("seqi"), lax.axis_size("seqo")
    slots = max(1, HEADS // n_i)
    quarter = rows // DILATION
    pos = lax.axis_index("seqi").astype(jnp.int32).reshape(1)
    f32, bf16 = jnp.float32, jnp.bfloat16
    shape = jax.ShapeDtypeStruct
    per_head = (HEADS, rows, HEAD_DIM)
    wide = pltpu.VMEM(per_head, f32)
    unit = 2 * rows * rows * HEAD_DIM

    def pick(a, b, name):
        outs = (shape((2, quarter, width), bf16), shape((2, rows, slots * HEAD_DIM), bf16))
        return call(functools.partial(pick_kernel, slots), outs, [wide], name, unit, pos, a, b)

    kv_mid, kv_tile = pick(key_rows, value_rows, "pick_kv")
    kv_mids = line_gather(kv_mid, n_i)
    kv_tiles = plane_gather(kv_tile, n_o)
    qu_mid, qu_tile = pick(query_rows, upstream, "pick_qu")
    qu_mids = line_gather(qu_mid, n_i)
    qu_tiles = plane_gather(qu_tile, n_o)

    whole = shape((rows, width), bf16)
    attended, comp, midcol, midrow, tilerow, gmid = call(
        functools.partial(forward_kernel, n_i, n_o, slots),
        (
            whole,
            shape((rows, HEAD_DIM), f32),
            shape((quarter, HEAD_DIM), f32),
            shape((2 * HEADS, quarter), f32),
            shape((2 * slots, rows), f32),
            shape((2, n_i * quarter, width), bf16),
        ),
        [wide, wide, wide, pltpu.VMEM((HEAD_DIM, rows), f32)],
        "forward",
        unit * (HEADS * 3 + 2 * slots * n_o),
        pos,
        query_rows,
        key_rows,
        value_rows,
        upstream,
        qu_mid,
        kv_mid,
        *kv_mids,
        *kv_tiles,
    )

    midrows = [midrow] + [
        lax.ppermute(midrow, "seqi", [((i + d) % n_i, i) for i in range(n_i)]) for d in range(1, n_i)
    ]
    tilerows = plane_gather(tilerow, n_o)

    grad_queries, dk0, dv0 = call(
        functools.partial(query_side_kernel, n_o, slots),
        (whole, shape(per_head, f32), shape(per_head, f32)),
        [wide],
        "query_side",
        unit * (HEADS * 6 + 3 * slots * n_o),
        pos,
        query_rows,
        key_rows,
        value_rows,
        upstream,
        qu_mid,
        gmid,
        comp,
        midcol,
        *kv_tiles,
    )
    grad_keys, grad_values = call(
        functools.partial(key_side_kernel, n_i, n_o, slots),
        (whole, whole),
        [wide, wide, pltpu.VMEM((2 * HEADS, n_i * quarter), f32)],
        "key_side",
        unit * (HEADS + 4 * slots * n_o),
        pos,
        kv_mid,
        kv_tile,
        dk0,
        dv0,
        qu_mid,
        *qu_mids,
        *qu_tiles,
        *midrows,
        *tilerows,
    )
    return attended, grad_queries, grad_keys, grad_values


def solution(mesh):
    rows = P(("seqo", "seqi"), None)
    return jax.shard_map(
        local,
        mesh=mesh,
        in_specs=(rows,) * 4,
        out_specs=(rows,) * 4,
        check_vma=False,
    )
```

time: 237 us -> 99.9 us (0.42)
  blocking collectives: 109 us -> 0 us
  local copies, waits for them, and re-layouts: 62.4 us -> 2.09 us
  matrix products: 44 us -> 0 us
  starting transfers between devices: 0.16 us -> 36.3 us
  Pallas kernels: 0 us -> 30.6 us
  waiting for transfers between devices: 0.09 us -> 29.4 us
  between operations: 14.4 us -> 0.89 us
  other arithmetic: 5.4 us -> 0 us
    all_gather x8 -> x0, blocking collectives: 109 us -> none  [the longest x1 17.4 us: local(): lax.all_gather(key_dilated.reshape(quarter, feature_width), 'seqi', axis=...]
    dot_general x29 -> x0, matrix products: 44 us -> none  [the longest x3 8.58 us: key_grads(): jnp.einsum('ibt,big->tig', score_gradient, query_matrix, preferred_elemen...]
    ppermute x0 -> x36, starting transfers between devices: none -> 36.3 us  [the longest x6 12.2 us: line_gather(): lax.ppermute(right[hop - 1], 'seqi', [(i, i + 1) for i in range(hop - 1,...]
    pallas_call x0 -> x5, Pallas kernels: none -> 30.6 us  [call(): pl.pallas_call(kernel, out_shape=tuple(outs), in_specs=specs, out_specs=t...]
    ppermute x0 -> x36, waiting for transfers between devices: none -> 29.4 us  [the longest x6 15.5 us: line_gather(): lax.ppermute(left[hop - 1], 'seqi', [(i + 1, i) for i in range(n - hop)])]
    mul x14 -> x0, local copies, waits for them, and re-layouts: 16.4 us -> none  [the longest x10 11.7 us: spread_dilated(): spread = tensor[:, None] * pattern]
    unnamed x100 -> x12, local copies, waits for them, and re-layouts: 13.5 us -> 2.09 us
    dot_general x4 -> x0, local copies, waits for them, and re-layouts: 7.14 us -> none  [spread_tile(): jnp.einsum('sh,tsd->thd', table_float, tensor, precision=lax.Precision.HI...]
  transfers between devices with their start and end apart: 4 -> 36, of which waited for: 0 -> 12; matrix products, arithmetic and copies ran while one was open for 31% -> 0% of each run, Pallas kernels for 0% -> 23%
where the time goes in v1:
time: 99.9 us; the launch traced here: 99.3 us
  starting transfers between devices  36.3 us (36%)
  Pallas kernels  30.6 us (31%)
  waiting for transfers between devices  29.4 us (29%)
  local copies, waits for them, and re-layouts  2.09 us (2%)
    pallas_call x5, Pallas kernels, call(): pl.pallas_call(kernel, out_shape=tuple(outs), in_specs=specs, out_specs=t...  30.6 us
    ppermute x6, waiting for transfers between devices, line_gather(): lax.ppermute(left[hop - 1], 'seqi', [(i + 1, i) for i in range(n - hop)])  15.5 us
    ppermute x9, waiting for transfers between devices, plane_gather(): found.append(lax.ppermute(x, 'seqo', [(i, i ^ mask) for i in range(n)]))  13 us
    ppermute x6, starting transfers between devices, line_gather(): lax.ppermute(right[hop - 1], 'seqi', [(i, i + 1) for i in range(hop - 1,...  12.2 us
    ppermute x9, starting transfers between devices, plane_gather(): found.append(lax.ppermute(x, 'seqo', [(i, i ^ mask) for i in range(n)]))  10.4 us
    ppermute x6, starting transfers between devices, line_gather(): lax.ppermute(left[hop - 1], 'seqi', [(i + 1, i) for i in range(n - hop)])  7.84 us
    ppermute x3, starting transfers between devices, local(): lax.ppermute(midrow, 'seqi', [((i + d) % n_i, i) for i in range(n_i)])  4.11 us
    unnamed x12, local copies, waits for them, and re-layouts  2.09 us
  transfers between devices with their start and end apart: 36, of which 12 were waited for; matrix products, arithmetic and copies ran while one was open for 0% of the time, Pallas kernels for 23%

profile of v1, /device:TPU:0, one launch (start us, length us, event | category | flops | bytes accessed | tf_op | source)
XLA Modules:
  0.0 99.3 jit_solution(9468830463406245598)
XLA Ops:
  0.6 1.0 %copy-done.1 = bf16[128,2048]{1,0:T(8,128)(2,1)S(1)} copy-done((bf16[128,2048]{1,0:T(8,128)(2,1)S(1)}, bf16[128,2048]{1,0:T(8,128)(2,1)}, u32[]{:S(2)}) %copy-start.1) | copy-done | bytes 524312
  1.7 1.0 %copy-done.2 = bf16[128,2048]{1,0:T(8,128)(2,1)S(1)} copy-done((bf16[128,2048]{1,0:T(8,128)(2,1)S(1)}, bf16[128,2048]{1,0:T(8,128)(2,1)}, u32[]{:S(2)}) %copy-start.2) | copy-done | bytes 524312
  3.0 1.4 %collective-permute-start = (bf16[2,32,2048]{2,1,0:T(8,128)(2,1)S(1)}, bf16[2,32,2048]{2,1,0:T(8,128)(2,1)S(1)}, u32[]{:S(2)}, u32[]{:S(2)}) collective-permute-start(bf16[2,32,2048]{2,1,0:T(8,128)(2,1)S(1)} %get-tuple-element.20.refs_6_.refs_1_), channel_id=1, source_target_pairs={{1,0},{2,1},{3,2},{5,4},{6,5},{7,6},{9,8},{10,9},{11,10},{13,12},{... | collective-permute-start | bytes 786440 | tf_op jit(solution)/shard_map/ppermute | solution.py:273
  4.4 5.6 %collective-permute-start.1 = (bf16[2,32,2048]{2,1,0:T(8,128)(2,1)S(1)}, bf16[2,32,2048]{2,1,0:T(8,128)(2,1)S(1)}, u32[]{:S(2)}, u32[]{:S(2)}) collective-permute-start(bf16[2,32,2048]{2,1,0:T(8,128)(2,1)S(1)} %get-tuple-element.20.refs_6_.refs_1_), channel_id=1, source_target_pairs={{0,1},{1,2},{2,3},{4,5},{5,6},{6,7},{8,9},{9,10},{10,11},{12,13},{... | collective-permute-start | bytes 786440 | tf_op jit(solution)/shard_map/ppermute | solution.py:272
  10.0 2.0 %collective-permute-start.6 = (bf16[2,128,512]{2,1,0:T(8,128)(2,1)S(1)}, bf16[2,128,512]{2,1,0:T(8,128)(2,1)S(1)}, u32[]{:S(2)}, u32[]{:S(2)}) collective-permute-start(bf16[2,128,512]{2,1,0:T(8,128)(2,1)S(1)} %get-tuple-element.21.refs_13_.refs_9_.refs_2_), channel_id=1, source_target_pairs={{0,8},{4,12},{8,0},{12,4},{16,24},{20,28},{24,16},{28,20},{1,9},{5... | collective-permute-start | bytes 786440 | tf_op jit(solution)/shard_map/ppermute | solution.py:280
  12.0 1.5 %collective-permute-start.7 = (bf16[2,128,512]{2,1,0:T(8,128)(2,1)S(1)}, bf16[2,128,512]{2,1,0:T(8,128)(2,1)S(1)}, u32[]{:S(2)}, u32[]{:S(2)}) collective-permute-start(bf16[2,128,512]{2,1,0:T(8,128)(2,1)S(1)} %get-tuple-element.21.refs_13_.refs_9_.refs_2_), channel_id=1, source_target_pairs={{0,16},{4,20},{8,24},{12,28},{16,0},{20,4},{24,8},{28,12},{1,17},{... | collective-permute-start | bytes 786440 | tf_op jit(solution)/shard_map/ppermute | solution.py:280
  13.6 0.8 collective-permute-done.refs_7_
  14.6 0.9 collective-permute-done.1.refs_12_
  15.5 1.3 %collective-permute-start.13 = (bf16[2,32,2048]{2,1,0:T(8,128)(2,1)S(1)}, bf16[2,32,2048]{2,1,0:T(8,128)(2,1)S(1)}, u32[]{:S(2)}, u32[]{:S(2)}) collective-permute-start(bf16[2,32,2048]{2,1,0:T(8,128)(2,1)S(1)} %get-tuple-element.19.refs_5_), channel_id=1, source_target_pairs={{1,0},{2,1},{3,2},{5,4},{6,5},{7,6},{9,8},{10,9},{11,10},{13,12},{... | collective-permute-start | bytes 786440 | tf_op jit(solution)/shard_map/ppermute | solution.py:273
  16.8 2.5 %collective-permute-done.6.refs_14_.refs_10_ = bf16[2,128,512]{2,1,0:T(8,128)(2,1)S(1)} collective-permute-done((bf16[2,128,512]{2,1,0:T(8,128)(2,1)S(1)}, bf16[2,128,512]{2,1,0:T(8,128)(2,1)S(1)}, u32[]{:S(2)}, u32[]{:S(2)}) %collective-permute-start.6) | collective-permute-done | bytes 262176 | tf_op jit(solution)/shard_map/ppermute | solution.py:280
  19.3 3.9 %collective-permute-start.14 = (bf16[2,32,2048]{2,1,0:T(8,128)(2,1)S(1)}, bf16[2,32,2048]{2,1,0:T(8,128)(2,1)S(1)}, u32[]{:S(2)}, u32[]{:S(2)}) collective-permute-start(bf16[2,32,2048]{2,1,0:T(8,128)(2,1)S(1)} %get-tuple-element.19.refs_5_), channel_id=1, source_target_pairs={{0,1},{1,2},{2,3},{4,5},{5,6},{6,7},{8,9},{9,10},{10,11},{12,13},{... | collective-permute-start | bytes 786440 | tf_op jit(solution)/shard_map/ppermute | solution.py:272
  23.2 1.5 %collective-permute-done.7.refs_15_.refs_11_ = bf16[2,128,512]{2,1,0:T(8,128)(2,1)S(1)} collective-permute-done((bf16[2,128,512]{2,1,0:T(8,128)(2,1)S(1)}, bf16[2,128,512]{2,1,0:T(8,128)(2,1)S(1)}, u32[]{:S(2)}, u32[]{:S(2)}) %collective-permute-start.7) | collective-permute-done | bytes 262176 | tf_op jit(solution)/shard_map/ppermute | solution.py:280
  24.9 1.9 %collective-permute-start.20 = (bf16[2,128,512]{2,1,0:T(8,128)(2,1)S(1)}, bf16[2,128,512]{2,1,0:T(8,128)(2,1)S(1)}, u32[]{:S(2)}, u32[]{:S(2)}) collective-permute-start(bf16[2,128,512]{2,1,0:T(8,128)(2,1)S(1)} %get-tuple-element.29.refs_12_), channel_id=1, source_target_pairs={{0,16},{4,20},{8,24},{12,28},{16,0},{20,4},{24,8},{28,12},{1,17},{... | collective-permute-start | bytes 786440 | tf_op jit(solution)/shard_map/ppermute | solution.py:280
  26.9 1.4 %collective-permute-start.21 = (bf16[2,128,512]{2,1,0:T(8,128)(2,1)S(1)}, bf16[2,128,512]{2,1,0:T(8,128)(2,1)S(1)}, u32[]{:S(2)}, u32[]{:S(2)}) collective-permute-start(bf16[2,128,512]{2,1,0:T(8,128)(2,1)S(1)} %get-tuple-element.29.refs_12_), channel_id=1, source_target_pairs={{0,24},{4,28},{8,16},{12,20},{16,8},{20,12},{24,0},{28,4},{1,25},{... | collective-permute-start | bytes 786440 | tf_op jit(solution)/shard_map/ppermute | solution.py:280
  28.2 0.7 collective-permute-start.2
  28.9 3.5 %collective-permute-done.19.refs_13_ = bf16[2,128,512]{2,1,0:T(8,128)(2,1)S(1)} collective-permute-done((bf16[2,128,512]{2,1,0:T(8,128)(2,1)S(1)}, bf16[2,128,512]{2,1,0:T(8,128)(2,1)S(1)}, u32[]{:S(2)}, u32[]{:S(2)}) %collective-permute-start.19) | collective-permute-done | bytes 262176 | tf_op jit(solution)/shard_map/ppermute | solution.py:280
  32.4 1.3 %collective-permute-start.4 = (bf16[2,32,2048]{2,1,0:T(8,128)(2,1)S(1)}, bf16[2,32,2048]{2,1,0:T(8,128)(2,1)S(1)}, u32[]{:S(2)}, u32[]{:S(2)}) collective-permute-start(bf16[2,32,2048]{2,1,0:T(8,128)(2,1)S(1)} %collective-permute-done.refs_7_), channel_id=1, source_target_pairs={{1,0},{2,1},{5,4},{6,5},{9,8},{10,9},{13,12},{14,13},{17,16},{18,1... | collective-permute-start | bytes 786440 | tf_op jit(solution)/shard_map/ppermute | solution.py:273
  33.7 3.1 %collective-permute-done.20.refs_14_ = bf16[2,128,512]{2,1,0:T(8,128)(2,1)S(1)} collective-permute-done((bf16[2,128,512]{2,1,0:T(8,128)(2,1)S(1)}, bf16[2,128,512]{2,1,0:T(8,128)(2,1)S(1)}, u32[]{:S(2)}, u32[]{:S(2)}) %collective-permute-start.20) | collective-permute-done | bytes 262176 | tf_op jit(solution)/shard_map/ppermute | solution.py:280
  38.1 3.9 %collective-permute-done.4.refs_9_ = bf16[2,32,2048]{2,1,0:T(8,128)(2,1)S(1)} collective-permute-done((bf16[2,32,2048]{2,1,0:T(8,128)(2,1)S(1)}, bf16[2,32,2048]{2,1,0:T(8,128)(2,1)S(1)}, u32[]{:S(2)}, u32[]{:S(2)}) %collective-permute-start.4) | collective-permute-done | bytes 262176 | tf_op jit(solution)/shard_map/ppermute | solution.py:273
  41.9 1.3 %collective-permute-start.17 = (bf16[2,32,2048]{2,1,0:T(8,128)(2,1)S(1)}, bf16[2,32,2048]{2,1,0:T(8,128)(2,1)S(1)}, u32[]{:S(2)}, u32[]{:S(2)}) collective-permute-start(bf16[2,32,2048]{2,1,0:T(8,128)(2,1)S(1)} %collective-permute-done.13.refs_6_), channel_id=1, source_target_pairs={{1,0},{2,1},{5,4},{6,5},{9,8},{10,9},{13,12},{14,13},{17,16},{18,1... | collective-permute-start | bytes 786440 | tf_op jit(solution)/shard_map/ppermute | solution.py:273
  43.9 1.3 %collective-permute-start.5 = (bf16[2,32,2048]{2,1,0:T(8,128)(2,1)S(1)}, bf16[2,32,2048]{2,1,0:T(8,128)(2,1)S(1)}, u32[]{:S(2)}, u32[]{:S(2)}) collective-permute-start(bf16[2,32,2048]{2,1,0:T(8,128)(2,1)S(1)} %collective-permute-done.4.refs_9_), channel_id=1, source_target_pairs={{1,0},{5,4},{9,8},{13,12},{17,16},{21,20},{25,24},{29,28}} | collective-permute-start | bytes 786440 | tf_op jit(solution)/shard_map/ppermute | solution.py:273
  45.8 7.2 %collective-permute-done.17.refs_8_ = bf16[2,32,2048]{2,1,0:T(8,128)(2,1)S(1)} collective-permute-done((bf16[2,32,2048]{2,1,0:T(8,128)(2,1)S(1)}, bf16[2,32,2048]{2,1,0:T(8,128)(2,1)S(1)}, u32[]{:S(2)}, u32[]{:S(2)}) %collective-permute-start.17) | collective-permute-done | bytes 262176 | tf_op jit(solution)/shard_map/ppermute | solution.py:273
  53.7 3.7 %collective-permute-done.5.refs_11_ = bf16[2,32,2048]{2,1,0:T(8,128)(2,1)S(1)} collective-permute-done((bf16[2,32,2048]{2,1,0:T(8,128)(2,1)S(1)}, bf16[2,32,2048]{2,1,0:T(8,128)(2,1)S(1)}, u32[]{:S(2)}, u32[]{:S(2)}) %collective-permute-start.5) | collective-permute-done | bytes 262176 | tf_op jit(solution)/shard_map/ppermute | solution.py:273
  57.4 1.3 %collective-permute-start.18 = (bf16[2,32,2048]{2,1,0:T(8,128)(2,1)S(1)}, bf16[2,32,2048]{2,1,0:T(8,128)(2,1)S(1)}, u32[]{:S(2)}, u32[]{:S(2)}) collective-permute-start(bf16[2,32,2048]{2,1,0:T(8,128)(2,1)S(1)} %collective-permute-done.17.refs_8_), channel_id=1, source_target_pairs={{1,0},{5,4},{9,8},{13,12},{17,16},{21,20},{25,24},{29,28}} | collective-permute-start | bytes 786440 | tf_op jit(solution)/shard_map/ppermute | solution.py:273
  58.6 12.6 %forward.1 = (bf16[128,2048]{1,0:T(8,128)(2,1)}, f32[128,128]{1,0:T(8,128)S(1)}, f32[32,128]{1,0:T(8,128)S(1)}, f32[32,32]{1,0:T(8,128)S(1)}, f32[8,128]{1,0:T(8,128)S(1)}, /*index=5*/bf16[2,128,2048]{2,1,0:T(8,128)(2,1)}) custom-call(s32[1]{0:T(128)} %bitcast.pos_ref.refs_0_, bf16[128,2048]{1,0:T(8,128)(2,1)S(1)} %copy-done, ...), custom_call_target="tpu_custom_call" | custom-call | flops 469762048 | bytes 7954436 | tf_op jit(solution)/shard_map/forward/pallas_call | solution.py:257
  71.3 4.1 %collective-permute-start.27 = (f32[32,32]{1,0:T(8,128)S(1)}, f32[32,32]{1,0:T(8,128)S(1)}, u32[]{:S(2)}, u32[]{:S(2)}) collective-permute-start(f32[32,32]{1,0:T(8,128)S(1)} %get-tuple-element.30.refs_20_), channel_id=1, source_target_pairs={{2,0},{3,1},{0,2},{1,3},{6,4},{7,5},{4,6},{5,7},{10,8},{11,9},{8,1... | collective-permute-start | bytes 12296 | tf_op jit(solution)/shard_map/ppermute | solution.py:333
  75.4 0.7 collective-permute-start.29
  76.1 1.2 %collective-permute-start.30 = (f32[8,128]{1,0:T(8,128)S(1)}, f32[8,128]{1,0:T(8,128)S(1)}, u32[]{:S(2)}, u32[]{:S(2)}) collective-permute-start(f32[8,128]{1,0:T(8,128)S(1)} %get-tuple-element.31.refs_24_), channel_id=1, source_target_pairs={{0,16},{4,20},{8,24},{12,28},{16,0},{20,4},{24,8},{28,12},{1,17},{... | collective-permute-start | bytes 12296 | tf_op jit(solution)/shard_map/ppermute | solution.py:280
  77.3 1.6 %collective-permute-start.31 = (f32[8,128]{1,0:T(8,128)S(1)}, f32[8,128]{1,0:T(8,128)S(1)}, u32[]{:S(2)}, u32[]{:S(2)}) collective-permute-start(f32[8,128]{1,0:T(8,128)S(1)} %get-tuple-element.31.refs_24_), channel_id=1, source_target_pairs={{0,24},{4,28},{8,16},{12,20},{16,8},{20,12},{24,0},{28,4},{1,25},{... | collective-permute-start | bytes 12296 | tf_op jit(solution)/shard_map/ppermute | solution.py:280
  79.7 2.1 %collective-permute-done.31.refs_27_ = f32[8,128]{1,0:T(8,128)S(1)} collective-permute-done((f32[8,128]{1,0:T(8,128)S(1)}, f32[8,128]{1,0:T(8,128)S(1)}, u32[]{:S(2)}, u32[]{:S(2)}) %collective-permute-start.31) | collective-permute-done | bytes 4128 | tf_op jit(solution)/shard_map/ppermute | solution.py:280
  81.8 10.3 %query_side.1 = (bf16[128,2048]{1,0:T(8,128)(2,1)}, f32[16,128,128]{2,1,0:T(8,128)S(1)}, f32[16,128,128]{2,1,0:T(8,128)}) custom-call(s32[1]{0:T(128)} %bitcast.pos_ref.refs_0_, bf16[128,2048]{1,0:T(8,128)(2,1)S(1)} %copy-done, bf16[128,2048]{1,0:T(8,128)(2,1)S(1)} %copy-done.1, bf16[128,2048]{1,0:T(8,128)(2,1)S(1)} %copy-done.3, ...), custom_call_target="tpu_custom_call" | custom-call | flops 805306368 | bytes 8208388 | tf_op jit(solution)/shard_map/query_side/pallas_call | solution.py:257
  92.1 7.2 %key_side.1 = (bf16[128,2048]{1,0:T(8,128)(2,1)}, bf16[128,2048]{1,0:T(8,128)(2,1)}) custom-call(s32[1]{0:T(128)} %bitcast.pos_ref.refs_0_, bf16[2,32,2048]{2,1,0:T(8,128)(2,1)S(1)} %get-tuple-element.20.refs_6_.refs_1_, bf16[2,128,512]{2,1,0:T(8,128)(2,1)S(1)} %get-tuple-element.21.refs_13_.refs_9_.refs_2_, f32[16,128,128]{2,1,0:T(8,128)S(1)} %get-tuple-element.27.refs_3_, ...), custom_call_target="tpu_custom_call" | custom-call | flops 603979776 | bytes 7651332 | tf_op jit(solution)/shard_map/key_side/pallas_call | solution.py:257
  (57 shorter events, 4.8 us)
Async XLA Ops:
  3.0 11.4 %collective-permute-start = (bf16[2,32,2048]{2,1,0:T(8,128)(2,1)S(1)}, bf16[2,32,2048]{2,1,0:T(8,128)(2,1)S(1)}, u32[]{:S(2)}, u32[]{:S(2)}) collective-permute-start(bf16[2,32,2048]{2,1,0:T(8,128)(2,1)S(1)} %get-tuple-element.20.refs_6_.refs_1_), channel_id=1, source_target_pairs={{1,0},{2,1},{3,2},{5,4},{6,5},{7,6},{9,8},{10,9},{11,10},{13,12},{... | collective-permute-start | bytes 786440 | tf_op jit(solution)/shard_map/ppermute | solution.py:273
  4.4 11.1 %collective-permute-start.1 = (bf16[2,32,2048]{2,1,0:T(8,128)(2,1)S(1)}, bf16[2,32,2048]{2,1,0:T(8,128)(2,1)S(1)}, u32[]{:S(2)}, u32[]{:S(2)}) collective-permute-start(bf16[2,32,2048]{2,1,0:T(8,128)(2,1)S(1)} %get-tuple-element.20.refs_6_.refs_1_), channel_id=1, source_target_pairs={{0,1},{1,2},{2,3},{4,5},{5,6},{6,7},{8,9},{9,10},{10,11},{12,13},{... | collective-permute-start | bytes 786440 | tf_op jit(solution)/shard_map/ppermute | solution.py:272
  10.0 9.3 %collective-permute-start.6 = (bf16[2,128,512]{2,1,0:T(8,128)(2,1)S(1)}, bf16[2,128,512]{2,1,0:T(8,128)(2,1)S(1)}, u32[]{:S(2)}, u32[]{:S(2)}) collective-permute-start(bf16[2,128,512]{2,1,0:T(8,128)(2,1)S(1)} %get-tuple-element.21.refs_13_.refs_9_.refs_2_), channel_id=1, source_target_pairs={{0,8},{4,12},{8,0},{12,4},{16,24},{20,28},{24,16},{28,20},{1,9},{5... | collective-permute-start | bytes 786440 | tf_op jit(solution)/shard_map/ppermute | solution.py:280
  12.0 12.7 %collective-permute-start.7 = (bf16[2,128,512]{2,1,0:T(8,128)(2,1)S(1)}, bf16[2,128,512]{2,1,0:T(8,128)(2,1)S(1)}, u32[]{:S(2)}, u32[]{:S(2)}) collective-permute-start(bf16[2,128,512]{2,1,0:T(8,128)(2,1)S(1)} %get-tuple-element.21.refs_13_.refs_9_.refs_2_), channel_id=1, source_target_pairs={{0,16},{4,20},{8,24},{12,28},{16,0},{20,4},{24,8},{28,12},{1,17},{... | collective-permute-start | bytes 786440 | tf_op jit(solution)/shard_map/ppermute | solution.py:280
  13.5 11.4 %collective-permute-start.8 = (bf16[2,128,512]{2,1,0:T(8,128)(2,1)S(1)}, bf16[2,128,512]{2,1,0:T(8,128)(2,1)S(1)}, u32[]{:S(2)}, u32[]{:S(2)}) collective-permute-start(bf16[2,128,512]{2,1,0:T(8,128)(2,1)S(1)} %get-tuple-element.21.refs_13_.refs_9_.refs_2_), channel_id=1, source_target_pairs={{0,24},{4,28},{8,16},{12,20},{16,8},{20,12},{24,0},{28,4},{1,25},{... | collective-permute-start | bytes 786440 | tf_op jit(solution)/shard_map/ppermute | solution.py:280
  14.3 12.5 %collective-permute-start.9 = (bf16[2,128,512]{2,1,0:T(8,128)(2,1)S(1)}, bf16[2,128,512]{2,1,0:T(8,128)(2,1)S(1)}, u32[]{:S(2)}, u32[]{:S(2)}) collective-permute-start(bf16[2,128,512]{2,1,0:T(8,128)(2,1)S(1)} %get-tuple-element.21.refs_13_.refs_9_.refs_2_), channel_id=1, source_target_pairs={{0,4},{4,0},{8,12},{12,8},{16,20},{20,16},{24,28},{28,24},{1,5},{5... | collective-permute-start | bytes 786440 | tf_op jit(solution)/shard_map/ppermute | solution.py:281
  15.5 12.7 %collective-permute-start.13 = (bf16[2,32,2048]{2,1,0:T(8,128)(2,1)S(1)}, bf16[2,32,2048]{2,1,0:T(8,128)(2,1)S(1)}, u32[]{:S(2)}, u32[]{:S(2)}) collective-permute-start(bf16[2,32,2048]{2,1,0:T(8,128)(2,1)S(1)} %get-tuple-element.19.refs_5_), channel_id=1, source_target_pairs={{1,0},{2,1},{3,2},{5,4},{6,5},{7,6},{9,8},{10,9},{11,10},{13,12},{... | collective-permute-start | bytes 786440 | tf_op jit(solution)/shard_map/ppermute | solution.py:273
  19.3 8.9 %collective-permute-start.14 = (bf16[2,32,2048]{2,1,0:T(8,128)(2,1)S(1)}, bf16[2,32,2048]{2,1,0:T(8,128)(2,1)S(1)}, u32[]{:S(2)}, u32[]{:S(2)}) collective-permute-start(bf16[2,32,2048]{2,1,0:T(8,128)(2,1)S(1)} %get-tuple-element.19.refs_5_), channel_id=1, source_target_pairs={{0,1},{1,2},{2,3},{4,5},{5,6},{6,7},{8,9},{9,10},{10,11},{12,13},{... | collective-permute-start | bytes 786440 | tf_op jit(solution)/shard_map/ppermute | solution.py:272
  24.7 7.7 %collective-permute-start.19 = (bf16[2,128,512]{2,1,0:T(8,128)(2,1)S(1)}, bf16[2,128,512]{2,1,0:T(8,128)(2,1)S(1)}, u32[]{:S(2)}, u32[]{:S(2)}) collective-permute-start(bf16[2,128,512]{2,1,0:T(8,128)(2,1)S(1)} %get-tuple-element.29.refs_12_), channel_id=1, source_target_pairs={{0,8},{4,12},{8,0},{12,4},{16,24},{20,28},{24,16},{28,20},{1,9},{5... | collective-permute-start | bytes 786440 | tf_op jit(solution)/shard_map/ppermute | solution.py:280
  24.9 11.9 %collective-permute-start.20 = (bf16[2,128,512]{2,1,0:T(8,128)(2,1)S(1)}, bf16[2,128,512]{2,1,0:T(8,128)(2,1)S(1)}, u32[]{:S(2)}, u32[]{:S(2)}) collective-permute-start(bf16[2,128,512]{2,1,0:T(8,128)(2,1)S(1)} %get-tuple-element.29.refs_12_), channel_id=1, source_target_pairs={{0,16},{4,20},{8,24},{12,28},{16,0},{20,4},{24,8},{28,12},{1,17},{... | collective-permute-start | bytes 786440 | tf_op jit(solution)/shard_map/ppermute | solution.py:280
  26.9 9.9 %collective-permute-start.21 = (bf16[2,128,512]{2,1,0:T(8,128)(2,1)S(1)}, bf16[2,128,512]{2,1,0:T(8,128)(2,1)S(1)}, u32[]{:S(2)}, u32[]{:S(2)}) collective-permute-start(bf16[2,128,512]{2,1,0:T(8,128)(2,1)S(1)} %get-tuple-element.29.refs_12_), channel_id=1, source_target_pairs={{0,24},{4,28},{8,16},{12,20},{16,8},{20,12},{24,0},{28,4},{1,25},{... | collective-permute-start | bytes 786440 | tf_op jit(solution)/shard_map/ppermute | solution.py:280
  28.2 9.1 %collective-permute-start.22 = (bf16[2,128,512]{2,1,0:T(8,128)(2,1)S(1)}, bf16[2,128,512]{2,1,0:T(8,128)(2,1)S(1)}, u32[]{:S(2)}, u32[]{:S(2)}) collective-permute-start(bf16[2,128,512]{2,1,0:T(8,128)(2,1)S(1)} %get-tuple-element.29.refs_12_), channel_id=1, source_target_pairs={{0,4},{4,0},{8,12},{12,8},{16,20},{20,16},{24,28},{28,24},{1,5},{5... | collective-permute-start | bytes 786440 | tf_op jit(solution)/shard_map/ppermute | solution.py:281
  28.2 9.1 %collective-permute-start.2 = (bf16[2,32,2048]{2,1,0:T(8,128)(2,1)S(1)}, bf16[2,32,2048]{2,1,0:T(8,128)(2,1)S(1)}, u32[]{:S(2)}, u32[]{:S(2)}) collective-permute-start(bf16[2,32,2048]{2,1,0:T(8,128)(2,1)S(1)} %collective-permute-done.1.refs_12_), channel_id=1, source_target_pairs={{1,2},{2,3},{5,6},{6,7},{9,10},{10,11},{13,14},{14,15},{17,18},{18... | collective-permute-start | bytes 786440 | tf_op jit(solution)/shard_map/ppermute | solution.py:272
  32.4 9.5 %collective-permute-start.4 = (bf16[2,32,2048]{2,1,0:T(8,128)(2,1)S(1)}, bf16[2,32,2048]{2,1,0:T(8,128)(2,1)S(1)}, u32[]{:S(2)}, u32[]{:S(2)}) collective-permute-start(bf16[2,32,2048]{2,1,0:T(8,128)(2,1)S(1)} %collective-permute-done.refs_7_), channel_id=1, source_target_pairs={{1,0},{2,1},{5,4},{6,5},{9,8},{10,9},{13,12},{14,13},{17,16},{18,1... | collective-permute-start | bytes 786440 | tf_op jit(solution)/shard_map/ppermute | solution.py:273
  36.8 7.1 %collective-permute-start.11 = (bf16[2,128,512]{2,1,0:T(8,128)(2,1)S(1)}, bf16[2,128,512]{2,1,0:T(8,128)(2,1)S(1)}, u32[]{:S(2)}, u32[]{:S(2)}) collective-permute-start(bf16[2,128,512]{2,1,0:T(8,128)(2,1)S(1)} %collective-permute-done.7.refs_15_.refs_11_), channel_id=1, source_target_pairs={{0,4},{4,0},{8,12},{12,8},{16,20},{20,16},{24,28},{28,24},{1,5},{5... | collective-permute-start | bytes 786440 | tf_op jit(solution)/shard_map/ppermute | solution.py:281
  37.3 7.9 %collective-permute-start.12 = (bf16[2,128,512]{2,1,0:T(8,128)(2,1)S(1)}, bf16[2,128,512]{2,1,0:T(8,128)(2,1)S(1)}, u32[]{:S(2)}, u32[]{:S(2)}) collective-permute-start(bf16[2,128,512]{2,1,0:T(8,128)(2,1)S(1)} %collective-permute-done.8.refs_16_.refs_12_), channel_id=1, source_target_pairs={{0,4},{4,0},{8,12},{12,8},{16,20},{20,16},{24,28},{28,24},{1,5},{5... | collective-permute-start | bytes 786440 | tf_op jit(solution)/shard_map/ppermute | solution.py:281
  37.4 7.9 %collective-permute-start.15 = (bf16[2,32,2048]{2,1,0:T(8,128)(2,1)S(1)}, bf16[2,32,2048]{2,1,0:T(8,128)(2,1)S(1)}, u32[]{:S(2)}, u32[]{:S(2)}) collective-permute-start(bf16[2,32,2048]{2,1,0:T(8,128)(2,1)S(1)} %collective-permute-done.14.refs_11_), channel_id=1, source_target_pairs={{1,2},{2,3},{5,6},{6,7},{9,10},{10,11},{13,14},{14,15},{17,18},{18... | collective-permute-start | bytes 786440 | tf_op jit(solution)/shard_map/ppermute | solution.py:272
  41.9 11.1 %collective-permute-start.17 = (bf16[2,32,2048]{2,1,0:T(8,128)(2,1)S(1)}, bf16[2,32,2048]{2,1,0:T(8,128)(2,1)S(1)}, u32[]{:S(2)}, u32[]{:S(2)}) collective-permute-start(bf16[2,32,2048]{2,1,0:T(8,128)(2,1)S(1)} %collective-permute-done.13.refs_6_), channel_id=1, source_target_pairs={{1,0},{2,1},{5,4},{6,5},{9,8},{10,9},{13,12},{14,13},{17,16},{18,1... | collective-permute-start | bytes 786440 | tf_op jit(solution)/shard_map/ppermute | solution.py:273
  43.2 9.8 %collective-permute-start.3 = (bf16[2,32,2048]{2,1,0:T(8,128)(2,1)S(1)}, bf16[2,32,2048]{2,1,0:T(8,128)(2,1)S(1)}, u32[]{:S(2)}, u32[]{:S(2)}) collective-permute-start(bf16[2,32,2048]{2,1,0:T(8,128)(2,1)S(1)} %collective-permute-done.2.refs_10_), channel_id=1, source_target_pairs={{2,3},{6,7},{10,11},{14,15},{18,19},{22,23},{26,27},{30,31}} | collective-permute-start | bytes 786440 | tf_op jit(solution)/shard_map/ppermute | solution.py:272
  43.9 13.4 %collective-permute-start.5 = (bf16[2,32,2048]{2,1,0:T(8,128)(2,1)S(1)}, bf16[2,32,2048]{2,1,0:T(8,128)(2,1)S(1)}, u32[]{:S(2)}, u32[]{:S(2)}) collective-permute-start(bf16[2,32,2048]{2,1,0:T(8,128)(2,1)S(1)} %collective-permute-done.4.refs_9_), channel_id=1, source_target_pairs={{1,0},{5,4},{9,8},{13,12},{17,16},{21,20},{25,24},{29,28}} | collective-permute-start | bytes 786440 | tf_op jit(solution)/shard_map/ppermute | solution.py:273
  45.2 26.1 %collective-permute-start.23 = (bf16[2,128,512]{2,1,0:T(8,128)(2,1)S(1)}, bf16[2,128,512]{2,1,0:T(8,128)(2,1)S(1)}, u32[]{:S(2)}, u32[]{:S(2)}) collective-permute-start(bf16[2,128,512]{2,1,0:T(8,128)(2,1)S(1)} %collective-permute-done.19.refs_13_), channel_id=1, source_target_pairs={{0,4},{4,0},{8,12},{12,8},{16,20},{20,16},{24,28},{28,24},{1,5},{5... | collective-permute-start | bytes 786440 | tf_op jit(solution)/shard_map/ppermute | solution.py:281
  45.3 26.0 %collective-permute-start.24 = (bf16[2,128,512]{2,1,0:T(8,128)(2,1)S(1)}, bf16[2,128,512]{2,1,0:T(8,128)(2,1)S(1)}, u32[]{:S(2)}, u32[]{:S(2)}) collective-permute-start(bf16[2,128,512]{2,1,0:T(8,128)(2,1)S(1)} %collective-permute-done.20.refs_14_), channel_id=1, source_target_pairs={{0,4},{4,0},{8,12},{12,8},{16,20},{20,16},{24,28},{28,24},{1,5},{5... | collective-permute-start | bytes 786440 | tf_op jit(solution)/shard_map/ppermute | solution.py:281
  53.0 22.4 %collective-permute-start.25 = (bf16[2,128,512]{2,1,0:T(8,128)(2,1)S(1)}, bf16[2,128,512]{2,1,0:T(8,128)(2,1)S(1)}, u32[]{:S(2)}, u32[]{:S(2)}) collective-permute-start(bf16[2,128,512]{2,1,0:T(8,128)(2,1)S(1)} %collective-permute-done.21.refs_15_), channel_id=1, source_target_pairs={{0,4},{4,0},{8,12},{12,8},{16,20},{20,16},{24,28},{28,24},{1,5},{5... | collective-permute-start | bytes 786440 | tf_op jit(solution)/shard_map/ppermute | solution.py:281
  53.0 23.1 %collective-permute-start.16 = (bf16[2,32,2048]{2,1,0:T(8,128)(2,1)S(1)}, bf16[2,32,2048]{2,1,0:T(8,128)(2,1)S(1)}, u32[]{:S(2)}, u32[]{:S(2)}) collective-permute-start(bf16[2,32,2048]{2,1,0:T(8,128)(2,1)S(1)} %collective-permute-done.15.refs_9_), channel_id=1, source_target_pairs={{2,3},{6,7},{10,11},{14,15},{18,19},{22,23},{26,27},{30,31}} | collective-permute-start | bytes 786440 | tf_op jit(solution)/shard_map/ppermute | solution.py:272
  57.4 20.0 %collective-permute-start.18 = (bf16[2,32,2048]{2,1,0:T(8,128)(2,1)S(1)}, bf16[2,32,2048]{2,1,0:T(8,128)(2,1)S(1)}, u32[]{:S(2)}, u32[]{:S(2)}) collective-permute-start(bf16[2,32,2048]{2,1,0:T(8,128)(2,1)S(1)} %collective-permute-done.17.refs_8_), channel_id=1, source_target_pairs={{1,0},{5,4},{9,8},{13,12},{17,16},{21,20},{25,24},{29,28}} | collective-permute-start | bytes 786440 | tf_op jit(solution)/shard_map/ppermute | solution.py:273
  71.3 7.6 %collective-permute-start.26 = (f32[32,32]{1,0:T(8,128)S(1)}, f32[32,32]{1,0:T(8,128)S(1)}, u32[]{:S(2)}, u32[]{:S(2)}) collective-permute-start(f32[32,32]{1,0:T(8,128)S(1)} %get-tuple-element.30.refs_20_), channel_id=1, source_target_pairs={{1,0},{2,1},{3,2},{0,3},{5,4},{6,5},{7,6},{4,7},{9,8},{10,9},{11,1... | collective-permute-start | bytes 12296 | tf_op jit(solution)/shard_map/ppermute | solution.py:333
  71.3 7.6 %collective-permute-start.27 = (f32[32,32]{1,0:T(8,128)S(1)}, f32[32,32]{1,0:T(8,128)S(1)}, u32[]{:S(2)}, u32[]{:S(2)}) collective-permute-start(f32[32,32]{1,0:T(8,128)S(1)} %get-tuple-element.30.refs_20_), channel_id=1, source_target_pairs={{2,0},{3,1},{0,2},{1,3},{6,4},{7,5},{4,6},{5,7},{10,8},{11,9},{8,1... | collective-permute-start | bytes 12296 | tf_op jit(solution)/shard_map/ppermute | solution.py:333
  78.9 13.2 %collective-permute-start.28 = (f32[32,32]{1,0:T(8,128)S(1)}, f32[32,32]{1,0:T(8,128)S(1)}, u32[]{:S(2)}, u32[]{:S(2)}) collective-permute-start(f32[32,32]{1,0:T(8,128)S(1)} %get-tuple-element.30.refs_20_), channel_id=1, source_target_pairs={{3,0},{0,1},{1,2},{2,3},{7,4},{4,5},{5,6},{6,7},{11,8},{8,9},{9,10... | collective-permute-start | bytes 12296 | tf_op jit(solution)/shard_map/ppermute | solution.py:333
  78.9 13.2 %collective-permute-start.32 = (f32[8,128]{1,0:T(8,128)S(1)}, f32[8,128]{1,0:T(8,128)S(1)}, u32[]{:S(2)}, u32[]{:S(2)}) collective-permute-start(f32[8,128]{1,0:T(8,128)S(1)} %get-tuple-element.31.refs_24_), channel_id=1, source_target_pairs={{0,4},{4,0},{8,12},{12,8},{16,20},{20,16},{24,28},{28,24},{1,5},{5... | collective-permute-start | bytes 12296 | tf_op jit(solution)/shard_map/ppermute | solution.py:281
  79.0 13.1 %collective-permute-start.33 = (f32[8,128]{1,0:T(8,128)S(1)}, f32[8,128]{1,0:T(8,128)S(1)}, u32[]{:S(2)}, u32[]{:S(2)}) collective-permute-start(f32[8,128]{1,0:T(8,128)S(1)} %collective-permute-done.29.refs_25_), channel_id=1, source_target_pairs={{0,4},{4,0},{8,12},{12,8},{16,20},{20,16},{24,28},{28,24},{1,5},{5... | collective-permute-start | bytes 12296 | tf_op jit(solution)/shard_map/ppermute | solution.py:281
  79.7 12.4 %collective-permute-start.34 = (f32[8,128]{1,0:T(8,128)S(1)}, f32[8,128]{1,0:T(8,128)S(1)}, u32[]{:S(2)}, u32[]{:S(2)}) collective-permute-start(f32[8,128]{1,0:T(8,128)S(1)} %collective-permute-done.30.refs_26_), channel_id=1, source_target_pairs={{0,4},{4,0},{8,12},{12,8},{16,20},{20,16},{24,28},{28,24},{1,5},{5... | collective-permute-start | bytes 12296 | tf_op jit(solution)/shard_map/ppermute | solution.py:281
  81.8 10.3 %collective-permute-start.35 = (f32[8,128]{1,0:T(8,128)S(1)}, f32[8,128]{1,0:T(8,128)S(1)}, u32[]{:S(2)}, u32[]{:S(2)}) collective-permute-start(f32[8,128]{1,0:T(8,128)S(1)} %collective-permute-done.31.refs_27_), channel_id=1, source_target_pairs={{0,4},{4,0},{8,12},{12,8},{16,20},{20,16},{24,28},{28,24},{1,5},{5... | collective-permute-start | bytes 12296 | tf_op jit(solution)/shard_map/ppermute | solution.py:281
  (10 other events, 149.2 us)

commit v2 on v1

v2 whole, which is shorter than its diff:
```python
import functools

import jax
import jax.numpy as jnp
from jax import lax
from jax.experimental import pallas as pl
from jax.experimental.pallas import tpu as pltpu
from jax.sharding import PartitionSpec as P

HEADS = 16
HEAD_DIM = 128
DILATION = 4
LANES = 128
SCALE = HEAD_DIM**-0.5
LOWEST = -1e30
VMEM_LIMIT = 32 * 1024 * 1024
F32, BF16 = jnp.float32, jnp.bfloat16
SHAPE = jax.ShapeDtypeStruct

NT = (((1,), (1,)), ((), ()))
TN = (((0,), (0,)), ((), ()))


def dot(a, b):
    return jnp.dot(a, b, preferred_element_type=F32)


def dot_nt(a, b):
    return lax.dot_general(a, b, NT, preferred_element_type=F32)


def dot_tn(a, b):
    return lax.dot_general(a, b, TN, preferred_element_type=F32)


def head_columns(head):
    return pl.ds(pl.multiple_of(head * HEAD_DIM, HEAD_DIM), HEAD_DIM)


def static_columns(index):
    return slice(index * HEAD_DIM, (index + 1) * HEAD_DIM)


def lanes_of(rows):
    return lax.broadcasted_iota(jnp.int32, (rows, LANES), 1)


def level_stats(q, k, v, u):
    s = dot_nt(k, q) * SCALE
    dp = dot_nt(v, u)
    top = jnp.max(s, axis=0, keepdims=True)
    p = jnp.exp(s - top)
    total = jnp.sum(p, axis=0, keepdims=True)
    return top + jnp.log(total), jnp.sum(p * dp, axis=0, keepdims=True) / total


def merge_stats(ea, da, eb, db):
    top = jnp.maximum(ea, eb)
    wa, wb = jnp.exp(ea - top), jnp.exp(eb - top)
    total = wa + wb
    return top + jnp.log(total), (wa * da + wb * db) / total


def level_weights(q, k, v, u, lse, delta):
    g = jnp.exp(dot_nt(k, q) * SCALE - lse)
    return g.astype(BF16), (g * (dot_nt(v, u) - delta)).astype(BF16)


def level_parts(q, k, v, u, lse, delta):
    p, ds = level_weights(q, k, v, u, lse, delta)
    return dot_tn(p, v), dot_tn(ds, k) * SCALE, dot(ds, q) * SCALE, dot(p, u)


def pick_rows(ref, rows):
    quarter = rows // DILATION
    lane = lanes_of(quarter)
    picked = jnp.zeros((quarter, LANES), F32)
    for residue in range(DILATION):
        part = ref[pl.ds(residue, quarter, stride=DILATION), :]
        picked = jnp.where(lane % DILATION == residue, part, picked)
    return picked


def pick_kernel(n_i, slots, at_ref, *refs):
    sources, refs = refs[:4], refs[4:]
    mids, refs = refs[:n_i], refs[n_i:]
    fulls, refs = refs[:slots], refs[slots:]
    kvs, refs = refs[:slots], refs[slots:]
    wide, picked = refs
    rows = sources[0].shape[0]
    quarter = rows // DILATION
    pos, chip = at_ref[0], at_ref[1]
    for which, ref in enumerate(sources):
        for head in range(HEADS):
            cols = static_columns(head)
            wide[head] = ref[:, cols].astype(F32)
            rowset = wide[head, pl.ds(head % DILATION, quarter, stride=DILATION), :]
            picked[:, cols] = rowset.astype(BF16)
        width = slots * HEAD_DIM
        for d in range(n_i):
            start = pl.multiple_of((pos ^ d) * width, width)
            mids[d][which] = picked[:, pl.ds(start, width)]
        for m in range(slots):
            piece = ref[:, head_columns(pos * slots + (chip ^ m))]
            fulls[m][which] = piece
            if which < 2:
                kvs[m][which] = piece


def near_stats_kernel(k_ref, v_ref, q_ref, u_ref, stats_ref, mid_ref, turn):
    rows = q_ref.shape[0]
    turn[...] = jnp.zeros_like(turn)

    def group_step(group, carry):
        for residue in range(DILATION):
            head = group * DILATION + residue
            cols = head_columns(head)
            e, d = level_stats(q_ref[:, cols], k_ref[:, cols], v_ref[:, cols], u_ref[:, cols])
            turn[pl.ds(head, 1), :] = e
            turn[pl.ds(HEADS + head, 1), :] = d
        return carry

    lax.fori_loop(0, HEADS // DILATION, group_step, 0)
    stats_ref[...] = turn[: 2 * HEADS, :]
    turn[...] = turn[...].T
    mid_ref[...] = pick_rows(turn, rows)


def far_stats_kernel(slots, *refs):
    fulls, kvs, stats_ref = refs[:slots], refs[slots:-1], refs[-1]
    keys = jnp.concatenate([ref[0] for ref in fulls + kvs], axis=0)
    values = jnp.concatenate([ref[1] for ref in fulls + kvs], axis=0)
    for m in range(slots):
        e, d = level_stats(fulls[m][2], keys, values, fulls[m][3])
        stats_ref[m : m + 1, :] = e
        stats_ref[slots + m : slots + m + 1, :] = d


def middle_operands(mids, slot):
    cols = static_columns(slot)
    return [jnp.concatenate([ref[which, :, cols] for ref in mids], axis=0) for which in range(4)]


def middle_stats_kernel(n_i, slots, at_ref, *refs):
    mids, refs = refs[:n_i], refs[n_i:]
    near_ref, nearmid_ref, far_ref = refs[:3]
    refs = refs[3:]
    zmsgs, refs = refs[:n_i], refs[n_i:]
    xmsg_ref, stats_ref, turn, spread = refs
    quarter = nearmid_ref.shape[0]
    pos = at_ref[0]
    turn[...] = jnp.zeros_like(turn)
    for slot in range(slots):
        k, v, q, u = middle_operands(mids, slot)
        e, d = level_stats(q, k, v, u)
        turn[slot : slot + 1, :] = e
        turn[slots + slot : slots + slot + 1, :] = d
    stats_ref[...] = turn[: 2 * slots, :]
    columns = turn[...].T
    lane = lanes_of(quarter)
    for d in range(n_i):
        chunk = pltpu.roll(columns[d * quarter : (d + 1) * quarter], 2 * HEADS, 1)
        zmsgs[d][...] = jnp.where(lane < 2 * HEADS, nearmid_ref[...], chunk)
    own = columns[:quarter]
    lane_residue = (pos * slots + lane % slots) % DILATION
    blank = jnp.where(lane < slots, LOWEST, 0.0)
    for residue in range(DILATION):
        spread[pl.ds(residue, quarter, stride=DILATION), :] = jnp.where(
            lane_residue == residue, own, blank
        )
    across = spread[...].T
    e, d = merge_stats(
        near_ref[pl.ds(pos * slots, slots), :],
        near_ref[pl.ds(HEADS + pos * slots, slots), :],
        across[:slots],
        across[slots : 2 * slots],
    )
    xmsg_ref[:slots] = e
    xmsg_ref[slots : 2 * slots] = d
    xmsg_ref[2 * slots :] = far_ref[...]


def middle_parts_kernel(n_i, slots, at_ref, *refs):
    mids, refs = refs[:n_i], refs[n_i:]
    near_ref, stats_ref = refs[:2]
    refs = refs[2:]
    zmsgs, refs = refs[:n_i], refs[n_i:]
    xmsgs, refs = refs[:slots], refs[slots:]
    outs, refs = refs[:n_i], refs[n_i:]
    final_ref, far, turn, spread = refs
    quarter = zmsgs[0].shape[0]
    rows = quarter * DILATION
    pos, chip = at_ref[0], at_ref[1]

    lane = lanes_of(quarter)
    mid = jnp.zeros((quarter, LANES), F32)
    for d in range(n_i):
        place = (pos ^ d) * slots
        e = pltpu.roll(zmsgs[d][...], (place + LANES - 2 * HEADS) % LANES, 1)
        de = pltpu.roll(zmsgs[d][...], (place + LANES - HEADS - slots) % LANES, 1)
        mid = jnp.where((lane >= place) & (lane < place + slots), e, mid)
        mid = jnp.where((lane >= HEADS + place) & (lane < HEADS + place + slots), de, mid)
    blank = jnp.where(lane < HEADS, LOWEST, 0.0)
    for residue in range(DILATION):
        spread[pl.ds(residue, quarter, stride=DILATION), :] = jnp.where(
            lane % DILATION == residue, mid, blank
        )
    across = spread[...].T
    far[:HEADS] = jnp.full((HEADS, rows), LOWEST, F32)
    far[HEADS:] = jnp.zeros((HEADS, rows), F32)
    for m in range(slots):
        head = pos * slots + (chip ^ m)
        far[pl.ds(head, 1), :] = xmsgs[m][2 * slots + m : 2 * slots + m + 1, :]
        far[pl.ds(HEADS + head, 1), :] = xmsgs[m][3 * slots + m : 3 * slots + m + 1, :]
    e, d = merge_stats(
        near_ref[:HEADS], near_ref[HEADS:], across[:HEADS], across[HEADS : 2 * HEADS]
    )
    e, d = merge_stats(e, d, far[:HEADS], far[HEADS:])
    final_ref[:HEADS] = e
    final_ref[HEADS:] = d

    spread[...] = jnp.zeros_like(spread)
    spread[: 2 * HEADS] = final_ref[...]
    spread[...] = spread[...].T
    own = pick_rows(spread, rows)
    turn[...] = jnp.concatenate([own] + [ref[...] for ref in zmsgs[1:]], axis=0).T
    owned = lax.broadcasted_iota(jnp.int32, (1, n_i * quarter), 1) < quarter
    for slot in range(slots):
        lse, delta = merge_stats(
            turn[pl.ds(pos * slots + slot, 1), :],
            turn[pl.ds(HEADS + pos * slots + slot, 1), :],
            jnp.where(owned, LOWEST, stats_ref[slot : slot + 1, :]),
            stats_ref[slots + slot : slots + slot + 1, :],
        )
        k, v, q, u = middle_operands(mids, slot)
        for which, part in enumerate(level_parts(q, k, v, u, lse, delta)):
            part = part.astype(BF16)
            for d in range(n_i):
                outs[d][which, :, static_columns(slot)] = part[d * quarter : (d + 1) * quarter]


def far_parts_kernel(slots, width, at_ref, *refs):
    others = (width - 1) * slots
    fulls, refs = refs[:slots], refs[slots:]
    kvs, refs = refs[:others], refs[others:]
    xmsgs, refs = refs[:slots], refs[slots:]
    outs, refs = refs[:slots], refs[slots:]
    kvouts, refs = refs[:others], refs[others:]
    weights, score_grads = refs
    rows = fulls[0].shape[1]
    chip = at_ref[1]
    keys = jnp.concatenate([ref[0] for ref in fulls + kvs], axis=0)
    values = jnp.concatenate([ref[1] for ref in fulls + kvs], axis=0)
    for m in range(slots):
        lse, delta = merge_stats(
            xmsgs[m][pl.ds(chip, 1), :],
            xmsgs[m][pl.ds(slots + chip, 1), :],
            xmsgs[0][2 * slots + m : 2 * slots + m + 1, :],
            xmsgs[0][3 * slots + m : 3 * slots + m + 1, :],
        )
        p, ds = level_weights(fulls[m][2], keys, values, fulls[m][3], lse, delta)
        outs[m][0] = dot_tn(p, values).astype(BF16)
        outs[m][1] = (dot_tn(ds, keys) * SCALE).astype(BF16)
        weights[:, m * rows : (m + 1) * rows] = p
        score_grads[:, m * rows : (m + 1) * rows] = ds
    queries = jnp.concatenate([ref[2] for ref in fulls], axis=0)
    ups = jnp.concatenate([ref[3] for ref in fulls], axis=0)
    key_part = (dot(score_grads[...], queries) * SCALE).astype(BF16)
    value_part = dot(weights[...], ups).astype(BF16)
    for index, ref in enumerate(outs + kvouts):
        base = 2 if index < slots else 0
        ref[base] = key_part[index * rows : (index + 1) * rows]
        ref[base + 1] = value_part[index * rows : (index + 1) * rows]


def near_parts_kernel(k_ref, v_ref, q_ref, u_ref, stats_ref, out_ref):
    def group_step(group, carry):
        for residue in range(DILATION):
            head = group * DILATION + residue
            cols = head_columns(head)
            parts = level_parts(
                q_ref[:, cols],
                k_ref[:, cols],
                v_ref[:, cols],
                u_ref[:, cols],
                stats_ref[pl.ds(head, 1), :],
                stats_ref[pl.ds(HEADS + head, 1), :],
            )
            for which, part in enumerate(parts):
                out_ref[which, head] = part
        return carry

    lax.fori_loop(0, HEADS // DILATION, group_step, 0)


def final_kernel(n_i, slots, width, at_ref, near_ref, *refs):
    others = (width - 1) * slots
    mids, refs = refs[:n_i], refs[n_i:]
    fulls, refs = refs[:slots], refs[slots:]
    kvs, outs = refs[:others], refs[others:]
    rows = fulls[0].shape[1]
    quarter = rows // DILATION
    pos, chip = at_ref[0], at_ref[1]
    row = lax.broadcasted_iota(jnp.int32, (rows, quarter), 0)
    taken = lax.broadcasted_iota(jnp.int32, (rows, quarter), 1) * DILATION

    def finish(d, slot, m):
        head = (pos ^ d) * slots + slot
        place = jnp.where(row == taken + head % DILATION, 1.0, 0.0).astype(BF16)
        cols = head_columns(slot) if d == 0 else static_columns(slot)
        for which, out in enumerate(outs):
            total = near_ref[which, head] + dot(place, mids[d][which, :, cols])
            if d == 0:
                total += fulls[m][which].astype(F32)
                if which >= 2:
                    for part in range(width - 1):
                        total += kvs[part * slots + m][which - 2].astype(F32)
            out[:, head_columns(head)] = total.astype(BF16)

    for d in range(1, n_i):
        for slot in range(slots):
            finish(d, slot, None)
    for m in range(slots):
        finish(0, chip ^ m, m)


def call(kernel, name, outs, scratch, flops, operands, at=None):
    specs = [pl.BlockSpec(memory_space=pltpu.VMEM)] * len(operands)
    moved = sum(x.size * x.dtype.itemsize for x in tuple(operands) + tuple(outs))
    if at is not None:
        specs = [pl.BlockSpec(memory_space=pltpu.SMEM)] + specs
        operands = (at,) + tuple(operands)
    return pl.pallas_call(
        kernel,
        out_shape=tuple(outs),
        in_specs=specs,
        out_specs=tuple(pl.BlockSpec(memory_space=pltpu.VMEM) for _ in outs),
        scratch_shapes=scratch,
        compiler_params=pltpu.CompilerParams(vmem_limit_bytes=VMEM_LIMIT),
        cost_estimate=pl.CostEstimate(flops=flops, bytes_accessed=moved, transcendentals=0),
        name=name,
    )(*operands)


def swap(x, axis, n, mask):
    return lax.ppermute(x, axis, [(i, i ^ mask) for i in range(n)])


def local(query_rows, key_rows, value_rows, upstream):
    rows, features = query_rows.shape
    n_i, n_o = lax.axis_size("seqi"), lax.axis_size("seqo")
    slots = HEADS // n_i
    width = n_o // slots
    others = (width - 1) * slots
    quarter = rows // DILATION
    pos = lax.axis_index("seqi").astype(jnp.int32)
    chip = lax.axis_index("seqo").astype(jnp.int32) // width
    at = jnp.stack([pos, chip])
    sources = (key_rows, value_rows, query_rows, upstream)
    unit = 2 * rows * rows * HEAD_DIM
    bind = functools.partial

    mid = SHAPE((4, quarter, slots * HEAD_DIM), BF16)
    full = SHAPE((4, rows, HEAD_DIM), BF16)
    half = SHAPE((2, rows, HEAD_DIM), BF16)
    square = pltpu.VMEM((LANES, rows), F32)

    def stats(count, lanes=rows):
        return SHAPE((count, lanes), F32)

    def swap_mids(pieces):
        return [pieces[0]] + [swap(pieces[d], "seqi", n_i, d) for d in range(1, n_i)]

    def swap_fulls(pieces):
        return [pieces[0]] + [swap(pieces[m], "seqo", n_o, m * width) for m in range(1, slots)]

    def swap_halves(pieces):
        return [
            swap(pieces[(part - 1) * slots + m], "seqo", n_o, m * width + part)
            for part in range(1, width)
            for m in range(slots)
        ]

    pieces = call(
        bind(pick_kernel, n_i, slots),
        "pick",
        [mid] * n_i + [full] * slots + [half] * slots,
        [pltpu.VMEM((HEADS, rows, HEAD_DIM), F32), pltpu.VMEM((quarter, features), BF16)],
        unit,
        sources,
        at,
    )
    mids = swap_mids(pieces[:n_i])
    fulls = swap_fulls(pieces[n_i : n_i + slots])
    kvs = swap_halves(list(pieces[n_i + slots :]) * (width - 1))

    near, nearmid = call(
        near_stats_kernel,
        "near_stats",
        [stats(2 * HEADS), SHAPE((quarter, LANES), F32)],
        [square],
        unit * HEADS * 2,
        sources,
    )
    (far,) = call(
        bind(far_stats_kernel, slots),
        "far_stats",
        [stats(2 * slots)],
        [],
        unit * n_o * slots * 2,
        fulls + kvs,
    )
    *zmsgs, xmsg, middle = call(
        bind(middle_stats_kernel, n_i, slots),
        "middle_stats",
        [SHAPE((quarter, LANES), F32)] * n_i
        + [stats(4 * slots), stats(2 * slots, n_i * quarter)],
        [pltpu.VMEM((LANES, n_i * quarter), F32), square],
        unit * slots * 2,
        mids + [near, nearmid, far],
        at,
    )
    zmsgs = swap_mids(zmsgs)
    xmsgs = swap_fulls([xmsg] * slots)

    *midparts, final = call(
        bind(middle_parts_kernel, n_i, slots),
        "middle_parts",
        [mid] * n_i + [stats(2 * HEADS)],
        [
            pltpu.VMEM((2 * HEADS, rows), F32),
            pltpu.VMEM((LANES, n_i * quarter), F32),
            square,
        ],
        unit * slots * 6,
        mids + [near, middle] + zmsgs + xmsgs,
        at,
    )
    midparts = swap_mids(midparts)
    farparts = call(
        bind(far_parts_kernel, slots, width),
        "far_parts",
        [full] * slots + [half] * others,
        [pltpu.VMEM((n_o * rows, slots * rows), BF16)] * 2,
        unit * n_o * slots * 6,
        fulls + kvs + xmsgs,
        at,
    )
    fullparts = swap_fulls(farparts[:slots])
    halfparts = swap_halves(farparts[slots:])

    (nearparts,) = call(
        near_parts_kernel,
        "near_parts",
        [SHAPE((4, HEADS, rows, HEAD_DIM), F32)],
        [],
        unit * HEADS * 6,
        sources + (final,),
    )
    return call(
        bind(final_kernel, n_i, slots, width),
        "final",
        [SHAPE((rows, features), BF16)] * 4,
        [],
        unit * HEADS,
        [nearparts] + midparts + fullparts + halfparts,
        at,
    )


def solution(mesh):
    rows = P(("seqo", "seqi"), None)
    return jax.shard_map(
        local,
        mesh=mesh,
        in_specs=(rows,) * 4,
        out_specs=(rows,) * 4,
        check_vma=False,
    )
```

time: 99.9 us -> 72.5 us (0.73)
  waiting for transfers between devices: 29.4 us -> 12.7 us
  Pallas kernels: 30.6 us -> 17.2 us
  local copies, waits for them, and re-layouts: 2.09 us -> 8.34 us
  starting transfers between devices: 36.3 us -> 32.9 us
    ppermute x36 -> x26, waiting for transfers between devices: 29.4 us -> 12.7 us  [swap(): return lax.ppermute(x, axis, [(i, i ^ mask) for i in range(n)])]
    pallas_call x5 -> x8, Pallas kernels: 30.6 us -> 17.2 us  [call(): pl.pallas_call(kernel, out_shape=tuple(outs), in_specs=specs, out_specs=t...]
    unnamed x12 -> x24, local copies, waits for them, and re-layouts: 2.09 us -> 8.34 us
    ppermute x36 -> x26, starting transfers between devices: 36.3 us -> 32.9 us  [swap(): return lax.ppermute(x, axis, [(i, i ^ mask) for i in range(n)])]
  transfers between devices with their start and end apart: 36 -> 26, of which waited for: 12 -> 7; matrix products, arithmetic and copies ran while one was open for 0% -> 0% of each run, Pallas kernels for 23% -> 13%
where the time goes in v2:
time: 72.5 us; the launch traced here: 72 us
  starting transfers between devices  32.9 us (45%)
  Pallas kernels  17.2 us (24%)
  waiting for transfers between devices  12.7 us (18%)
  local copies, waits for them, and re-layouts  8.34 us (12%)
  between operations  0.78 us (1%)
    ppermute x26, starting transfers between devices, swap(): return lax.ppermute(x, axis, [(i, i ^ mask) for i in range(n)])  32.9 us
    pallas_call x8, Pallas kernels, call(): pl.pallas_call(kernel, out_shape=tuple(outs), in_specs=specs, out_specs=t...  17.2 us
    ppermute x26, waiting for transfers between devices, swap(): return lax.ppermute(x, axis, [(i, i ^ mask) for i in range(n)])  12.7 us
    unnamed x24, local copies, waits for them, and re-layouts  8.34 us
  transfers between devices with their start and end apart: 26, of which 7 were waited for; matrix products, arithmetic and copies ran while one was open for 0% of the time, Pallas kernels for 13%

profile of v2, /device:TPU:0, one launch (start us, length us, event | category | flops | bytes accessed | tf_op | source)
XLA Modules:
  0.0 72.0 jit_solution(10348554480194293738)
XLA Ops:
  0.7 1.0 %copy-done = bf16[128,2048]{1,0:T(8,128)(2,1)S(1)} copy-done((bf16[128,2048]{1,0:T(8,128)(2,1)S(1)}, bf16[128,2048]{1,0:T(8,128)(2,1)}, u32[]{:S(2)}) %copy-start) | copy-done | bytes 524312
  3.8 1.0 %copy-done.9 = bf16[128,2048]{1,0:T(8,128)(2,1)S(1)} copy-done((bf16[128,2048]{1,0:T(8,128)(2,1)S(1)}, bf16[128,2048]{1,0:T(8,128)(2,1)}, u32[]{:S(2)}) %copy-start.9) | copy-done | bytes 524312
  4.9 1.2 %pick.1 = (bf16[4,32,512]{2,1,0:T(8,128)(2,1)S(1)}, bf16[4,32,512]{2,1,0:T(8,128)(2,1)S(1)}, bf16[4,32,512]{2,1,0:T(8,128)(2,1)S(1)}, bf16[4,32,512]{2,1,0:T(8,1...) custom-call(s32[2]{0:T(128)S(1)} %pad_add_fusion.at_ref, ...), custom_call_target="tpu_custom_call" | custom-call | flops 4194304 | bytes 3407872 | tf_op jit(solution)/shard_map/pick/pallas_call | solution.py:333
  6.1 3.0 %collective-permute-start.3 = (bf16[4,128,128]{2,1,0:T(8,128)(2,1)S(1)}, bf16[4,128,128]{2,1,0:T(8,128)(2,1)S(1)}, u32[]{:S(2)}, u32[]{:S(2)}) collective-permute-start(bf16[4,128,128]{2,1,0:T(8,128)(2,1)S(1)} %get-tuple-element.44), channel_id=1, source_target_pairs={{0,8},{4,12},{8,0},{12,4},{16,24},{20,28},{24,16},{28,20},{1,9},{5... | collective-permute-start | bytes 393224 | tf_op jit(solution)/shard_map/ppermute | solution.py:346
  9.3 1.6 %collective-permute-start.8 = (bf16[2,128,128]{2,1,0:T(8,128)(2,1)S(1)}, bf16[2,128,128]{2,1,0:T(8,128)(2,1)S(1)}, u32[]{:S(2)}, u32[]{:S(2)}) collective-permute-start(bf16[2,128,128]{2,1,0:T(8,128)(2,1)S(1)} %get-tuple-element.49), channel_id=1, source_target_pairs={{0,20},{4,16},{8,28},{12,24},{16,4},{20,0},{24,12},{28,8},{1,21},{... | collective-permute-start | bytes 196616 | tf_op jit(solution)/shard_map/ppermute | solution.py:346
  10.8 1.5 %collective-permute-start.9 = (bf16[2,128,128]{2,1,0:T(8,128)(2,1)S(1)}, bf16[2,128,128]{2,1,0:T(8,128)(2,1)S(1)}, u32[]{:S(2)}, u32[]{:S(2)}) collective-permute-start(bf16[2,128,128]{2,1,0:T(8,128)(2,1)S(1)} %get-tuple-element.50), channel_id=1, source_target_pairs={{0,28},{4,24},{8,20},{12,16},{16,12},{20,8},{24,4},{28,0},{1,29},{... | collective-permute-start | bytes 196616 | tf_op jit(solution)/shard_map/ppermute | solution.py:346
  12.4 1.5 %collective-permute-start.4 = (bf16[4,128,128]{2,1,0:T(8,128)(2,1)S(1)}, bf16[4,128,128]{2,1,0:T(8,128)(2,1)S(1)}, u32[]{:S(2)}, u32[]{:S(2)}) collective-permute-start(bf16[4,128,128]{2,1,0:T(8,128)(2,1)S(1)} %get-tuple-element.45), channel_id=1, source_target_pairs={{0,16},{4,20},{8,24},{12,28},{16,0},{20,4},{24,8},{28,12},{1,17},{... | collective-permute-start | bytes 393224 | tf_op jit(solution)/shard_map/ppermute | solution.py:346
  13.9 1.6 %collective-permute-start.5 = (bf16[4,128,128]{2,1,0:T(8,128)(2,1)S(1)}, bf16[4,128,128]{2,1,0:T(8,128)(2,1)S(1)}, u32[]{:S(2)}, u32[]{:S(2)}) collective-permute-start(bf16[4,128,128]{2,1,0:T(8,128)(2,1)S(1)} %get-tuple-element.46), channel_id=1, source_target_pairs={{0,24},{4,28},{8,16},{12,20},{16,8},{20,12},{24,0},{28,4},{1,25},{... | collective-permute-start | bytes 393224 | tf_op jit(solution)/shard_map/ppermute | solution.py:346
  15.5 1.6 %collective-permute-start = (bf16[4,32,512]{2,1,0:T(8,128)(2,1)S(1)}, bf16[4,32,512]{2,1,0:T(8,128)(2,1)S(1)}, u32[]{:S(2)}, u32[]{:S(2)}) collective-permute-start(bf16[4,32,512]{2,1,0:T(8,128)(2,1)S(1)} %get-tuple-element.38), channel_id=1, source_target_pairs={{0,1},{1,0},{2,3},{3,2},{4,5},{5,4},{6,7},{7,6},{8,9},{9,8},{10,11... | collective-permute-start | bytes 393224 | tf_op jit(solution)/shard_map/ppermute | solution.py:346
  17.1 2.6 %collective-permute-start.1 = (bf16[4,32,512]{2,1,0:T(8,128)(2,1)S(1)}, bf16[4,32,512]{2,1,0:T(8,128)(2,1)S(1)}, u32[]{:S(2)}, u32[]{:S(2)}) collective-permute-start(bf16[4,32,512]{2,1,0:T(8,128)(2,1)S(1)} %get-tuple-element.39), channel_id=1, source_target_pairs={{0,2},{1,3},{2,0},{3,1},{4,6},{5,7},{6,4},{7,5},{8,10},{9,11},{10,... | collective-permute-start | bytes 393224 | tf_op jit(solution)/shard_map/ppermute | solution.py:346
  20.3 1.0 %copy-done.1 = bf16[128,2048]{1,0:T(8,128)(2,1)S(1)} copy-done((bf16[128,2048]{1,0:T(8,128)(2,1)S(1)}, bf16[128,2048]{1,0:T(8,128)(2,1)}, u32[]{:S(2)}) %copy-start.1) | copy-done | bytes 524312
  24.4 1.6 %near_stats.1 = (f32[32,128]{1,0:T(8,128)S(1)}, f32[32,128]{1,0:T(8,128)S(1)}) custom-call(bf16[128,2048]{1,0:T(8,128)(2,1)S(1)} %copy-done.1, bf16[128,2048]{1,0:T(8,128)(2,1)S(1)} %copy-done.4, bf16[128,2048]{1,0:T(8,128)(2,1)S(1)} %copy-done.7, bf16[128,2048]{1,0:T(8,128)(2,1)S(1)} %copy-done.10), custom_call_target="tpu_custom_call" | custom-call | flops 134217728 | bytes 2129920 | tf_op jit(solution)/shard_map/near_stats/pallas_call | solution.py:333
  26.0 1.1 %far_stats.1.refs_6_ = f32[8,128]{1,0:T(8,128)S(1)} custom-call(bf16[4,128,128]{2,1,0:T(8,128)(2,1)S(1)} %get-tuple-element.43.refs_0_, bf16[4,128,128]{2,1,0:T(8,128)(2,1)S(1)} %collective-permute-done.3.refs_1_, bf16[4,128,128]{2,1,0:T(8,128)(2,1)S(1)} %collective-permute-done.4.refs_2_, bf16[4,128,128]{2,1,0:T(8,128)(2,1)S(1)} %collective-permute-done.5.refs_3_, ...), custom_call_target="tpu_custom_call" | custom-call | flops 268435456 | bytes 790528 | tf_op jit(solution)/shard_map/far_stats/pallas_call | solution.py:333
  27.1 2.8 %collective-permute-done.1.refs_2_ = bf16[4,32,512]{2,1,0:T(8,128)(2,1)S(1)} collective-permute-done((bf16[4,32,512]{2,1,0:T(8,128)(2,1)S(1)}, bf16[4,32,512]{2,1,0:T(8,128)(2,1)S(1)}, u32[]{:S(2)}, u32[]{:S(2)}) %collective-permute-start.1) | collective-permute-done | bytes 131104 | tf_op jit(solution)/shard_map/ppermute | solution.py:346
  29.9 1.1 %middle_stats.1 = (f32[32,128]{1,0:T(8,128)S(1)}, f32[32,128]{1,0:T(8,128)S(1)}, f32[32,128]{1,0:T(8,128)S(1)}, f32[32,128]{1,0:T(8,128)S(1)}, f32[16,128]{1,0:T(8,128)S(1)}, /*index=5*/f32[8,128]{1,0:T(8,128)S(1)}) custom-call(s32[2]{0:T(128)S(1)} %pad_add_fusion.at_ref, bf16[4,32,512]{2,1,0:T(8,128)(2,1)S(1)} %get-tuple-element.37.refs_0_, ...), custom_call_target="tpu_custom_call" | custom-call | flops 33554432 | bytes 638976 | tf_op jit(solution)/shard_map/middle_stats/pallas_call | solution.py:333
  31.0 1.5 %collective-permute-start.15 = (f32[16,128]{1,0:T(8,128)S(1)}, f32[16,128]{1,0:T(8,128)S(1)}, u32[]{:S(2)}, u32[]{:S(2)}) collective-permute-start(f32[16,128]{1,0:T(8,128)S(1)} %get-tuple-element.56.refs_10_.refs_8_), channel_id=1, source_target_pairs={{0,24},{4,28},{8,16},{12,20},{16,8},{20,12},{24,0},{28,4},{1,25},{... | collective-permute-start | bytes 24584 | tf_op jit(solution)/shard_map/ppermute | solution.py:346
  32.5 1.1 %collective-permute-start.14 = (f32[16,128]{1,0:T(8,128)S(1)}, f32[16,128]{1,0:T(8,128)S(1)}, u32[]{:S(2)}, u32[]{:S(2)}) collective-permute-start(f32[16,128]{1,0:T(8,128)S(1)} %get-tuple-element.56.refs_10_.refs_8_), channel_id=1, source_target_pairs={{0,16},{4,20},{8,24},{12,28},{16,0},{20,4},{24,8},{28,12},{1,17},{... | collective-permute-start | bytes 24584 | tf_op jit(solution)/shard_map/ppermute | solution.py:346
  34.6 1.1 %collective-permute-done.15.refs_13_.refs_11_ = f32[16,128]{1,0:T(8,128)S(1)} collective-permute-done((f32[16,128]{1,0:T(8,128)S(1)}, f32[16,128]{1,0:T(8,128)S(1)}, u32[]{:S(2)}, u32[]{:S(2)}) %collective-permute-start.15) | collective-permute-done | bytes 8224 | tf_op jit(solution)/shard_map/ppermute | solution.py:346
  36.2 1.1 %collective-permute-done.13.refs_11_.refs_9_ = f32[16,128]{1,0:T(8,128)S(1)} collective-permute-done((f32[16,128]{1,0:T(8,128)S(1)}, f32[16,128]{1,0:T(8,128)S(1)}, u32[]{:S(2)}, u32[]{:S(2)}) %collective-permute-start.13) | collective-permute-done | bytes 8224 | tf_op jit(solution)/shard_map/ppermute | solution.py:346
  37.3 2.8 %far_parts.1 = (bf16[4,128,128]{2,1,0:T(8,128)(2,1)S(1)}, bf16[4,128,128]{2,1,0:T(8,128)(2,1)S(1)}, bf16[4,128,128]{2,1,0:T(8,128)(2,1)S(1)}, bf16[4,128,128]{2,...) custom-call(s32[2]{0:T(128)S(1)} %pad_add_fusion.at_ref, ...), custom_call_target="tpu_custom_call" | custom-call | flops 805306368 | bytes 1605632 | tf_op jit(solution)/shard_map/far_parts/pallas_call | solution.py:333
  41.1 3.4 %collective-permute-start.10 = (f32[32,128]{1,0:T(8,128)S(1)}, f32[32,128]{1,0:T(8,128)S(1)}, u32[]{:S(2)}, u32[]{:S(2)}) collective-permute-start(f32[32,128]{1,0:T(8,128)S(1)} %get-tuple-element.53), channel_id=1, source_target_pairs={{0,1},{1,0},{2,3},{3,2},{4,5},{5,4},{6,7},{7,6},{8,9},{9,8},{10,11... | collective-permute-start | bytes 49160 | tf_op jit(solution)/shard_map/ppermute | solution.py:346
  44.5 1.2 %collective-permute-start.11 = (f32[32,128]{1,0:T(8,128)S(1)}, f32[32,128]{1,0:T(8,128)S(1)}, u32[]{:S(2)}, u32[]{:S(2)}) collective-permute-start(f32[32,128]{1,0:T(8,128)S(1)} %get-tuple-element.54), channel_id=1, source_target_pairs={{0,2},{1,3},{2,0},{3,1},{4,6},{5,7},{6,4},{7,5},{8,10},{9,11},{10,... | collective-permute-start | bytes 49160 | tf_op jit(solution)/shard_map/ppermute | solution.py:346
  45.7 1.5 %collective-permute-start.12 = (f32[32,128]{1,0:T(8,128)S(1)}, f32[32,128]{1,0:T(8,128)S(1)}, u32[]{:S(2)}, u32[]{:S(2)}) collective-permute-start(f32[32,128]{1,0:T(8,128)S(1)} %get-tuple-element.55), channel_id=1, source_target_pairs={{0,3},{1,2},{2,1},{3,0},{4,7},{5,6},{6,5},{7,4},{8,11},{9,10},{10,... | collective-permute-start | bytes 49160 | tf_op jit(solution)/shard_map/ppermute | solution.py:346
  47.2 1.1 %collective-permute-start.23 = (bf16[2,128,128]{2,1,0:T(8,128)(2,1)S(1)}, bf16[2,128,128]{2,1,0:T(8,128)(2,1)S(1)}, u32[]{:S(2)}, u32[]{:S(2)}) collective-permute-start(bf16[2,128,128]{2,1,0:T(8,128)(2,1)S(1)} %get-tuple-element.67), channel_id=1, source_target_pairs={{0,12},{4,8},{8,4},{12,0},{16,28},{20,24},{24,20},{28,16},{1,13},{... | collective-permute-start | bytes 196616 | tf_op jit(solution)/shard_map/ppermute | solution.py:346
  49.2 2.0 %collective-permute-done.12.refs_9_ = f32[32,128]{1,0:T(8,128)S(1)} collective-permute-done((f32[32,128]{1,0:T(8,128)S(1)}, f32[32,128]{1,0:T(8,128)S(1)}, u32[]{:S(2)}, u32[]{:S(2)}) %collective-permute-start.12) | collective-permute-done | bytes 16416 | tf_op jit(solution)/shard_map/ppermute | solution.py:346
  51.3 2.0 %middle_parts.1 = (bf16[4,32,512]{2,1,0:T(8,128)(2,1)S(1)}, bf16[4,32,512]{2,1,0:T(8,128)(2,1)S(1)}, bf16[4,32,512]{2,1,0:T(8,128)(2,1)S(1)}, bf16[4,32,512]{2,1,0:T(8,128)(2,1)S(1)}, f32[32,128]{1,0:T(8,128)S(1)}) custom-call(s32[2]{0:T(128)S(1)} %pad_add_fusion.at_ref, bf16[4,32,512]{2,1,0:T(8,128)(2,1)S(1)} %get-tuple-element.37.refs_0_, ...), custom_call_target="tpu_custom_call" | custom-call | flops 100663296 | bytes 1183744 | tf_op jit(solution)/shard_map/middle_parts/pallas_call | solution.py:333
  54.3 1.7 %collective-permute-start.21 = (bf16[4,128,128]{2,1,0:T(8,128)(2,1)S(1)}, bf16[4,128,128]{2,1,0:T(8,128)(2,1)S(1)}, u32[]{:S(2)}, u32[]{:S(2)}) collective-permute-start(bf16[4,128,128]{2,1,0:T(8,128)(2,1)S(1)} %get-tuple-element.65), channel_id=1, source_target_pairs={{0,24},{4,28},{8,16},{12,20},{16,8},{20,12},{24,0},{28,4},{1,25},{... | collective-permute-start | bytes 393224 | tf_op jit(solution)/shard_map/ppermute | solution.py:346
  56.4 2.7 %collective-permute-start.17 = (bf16[4,32,512]{2,1,0:T(8,128)(2,1)S(1)}, bf16[4,32,512]{2,1,0:T(8,128)(2,1)S(1)}, u32[]{:S(2)}, u32[]{:S(2)}) collective-permute-start(bf16[4,32,512]{2,1,0:T(8,128)(2,1)S(1)} %get-tuple-element.60), channel_id=1, source_target_pairs={{0,2},{1,3},{2,0},{3,1},{4,6},{5,7},{6,4},{7,5},{8,10},{9,11},{10,... | collective-permute-start | bytes 393224 | tf_op jit(solution)/shard_map/ppermute | solution.py:346
  59.1 1.3 %collective-permute-start.18 = (bf16[4,32,512]{2,1,0:T(8,128)(2,1)S(1)}, bf16[4,32,512]{2,1,0:T(8,128)(2,1)S(1)}, u32[]{:S(2)}, u32[]{:S(2)}) collective-permute-start(bf16[4,32,512]{2,1,0:T(8,128)(2,1)S(1)} %get-tuple-element.61), channel_id=1, source_target_pairs={{0,3},{1,2},{2,1},{3,0},{4,7},{5,6},{6,5},{7,4},{8,11},{9,10},{10,... | collective-permute-start | bytes 393224 | tf_op jit(solution)/shard_map/ppermute | solution.py:346
  60.4 4.7 %near_parts.1.near_ref = f32[4,16,128,128]{3,2,1,0:T(8,128)S(1)} custom-call(bf16[128,2048]{1,0:T(8,128)(2,1)S(1)} %copy-done.2, bf16[128,2048]{1,0:T(8,128)(2,1)S(1)} %copy-done.5, bf16[128,2048]{1,0:T(8,128)(2,1)S(1)} %copy-done.8, bf16[128,2048]{1,0:T(8,128)(2,1)S(1)} %copy-done.11, f32[32,128]{1,0:T(8,128)S(1)} %get-tuple-element.57.stats_ref), custom_call_target="tpu_custom_call" | custom-call | flops 402653184 | bytes 6307840 | tf_op jit(solution)/shard_map/near_parts/pallas_call | solution.py:333
  65.1 4.1 %collective-permute-done.17.refs_2_ = bf16[4,32,512]{2,1,0:T(8,128)(2,1)S(1)} collective-permute-done((bf16[4,32,512]{2,1,0:T(8,128)(2,1)S(1)}, bf16[4,32,512]{2,1,0:T(8,128)(2,1)S(1)}, u32[]{:S(2)}, u32[]{:S(2)}) %collective-permute-start.17) | collective-permute-done | bytes 131104 | tf_op jit(solution)/shard_map/ppermute | solution.py:346
  69.3 2.7 %final.1 = (bf16[128,2048]{1,0:T(8,128)(2,1)}, bf16[128,2048]{1,0:T(8,128)(2,1)}, bf16[128,2048]{1,0:T(8,128)(2,1)}, bf16[128,2048]{1,0:T(8,128)(2,1)}) custom-call(s32[2]{0:T(128)S(1)} %pad_add_fusion.at_ref, f32[4,16,128,128]{3,2,1,0:T(8,128)S(1)} %near_parts.1.near_ref, bf16[4,32,512]{2,1,0:T(8,128)(2,1)S(1)} %get-tuple-element.58.refs_0_, ...), custom_call_target="tpu_custom_call" | custom-call | flops 67108864 | bytes 7602176 | tf_op jit(solution)/shard_map/final/pallas_call | solution.py:333
  (53 shorter events, 11.0 us)
Async XLA Ops:
  0.7 1.0 %copy-start = (bf16[128,2048]{1,0:T(8,128)(2,1)S(1)}, bf16[128,2048]{1,0:T(8,128)(2,1)}, u32[]{:S(2)}) copy-start(bf16[128,2048]{1,0:T(8,128)(2,1)} %k_ref.3) | copy-start | bytes 1572868
  1.8 1.0 %copy-start.3 = (bf16[128,2048]{1,0:T(8,128)(2,1)S(1)}, bf16[128,2048]{1,0:T(8,128)(2,1)}, u32[]{:S(2)}) copy-start(bf16[128,2048]{1,0:T(8,128)(2,1)} %v_ref.3) | copy-start | bytes 1572868
  4.9 55.5 %copy-start.2 = (bf16[128,2048]{1,0:T(8,128)(2,1)S(1)}, bf16[128,2048]{1,0:T(8,128)(2,1)}, u32[]{:S(2)}) copy-start(bf16[128,2048]{1,0:T(8,128)(2,1)} %k_ref.3) | copy-start | bytes 1572868
  4.9 55.5 %copy-start.5 = (bf16[128,2048]{1,0:T(8,128)(2,1)S(1)}, bf16[128,2048]{1,0:T(8,128)(2,1)}, u32[]{:S(2)}) copy-start(bf16[128,2048]{1,0:T(8,128)(2,1)} %v_ref.3) | copy-start | bytes 1572868
  4.9 55.5 %copy-start.8 = (bf16[128,2048]{1,0:T(8,128)(2,1)S(1)}, bf16[128,2048]{1,0:T(8,128)(2,1)}, u32[]{:S(2)}) copy-start(bf16[128,2048]{1,0:T(8,128)(2,1)} %q_ref.3) | copy-start | bytes 1572868
  4.9 55.5 %copy-start.11 = (bf16[128,2048]{1,0:T(8,128)(2,1)S(1)}, bf16[128,2048]{1,0:T(8,128)(2,1)}, u32[]{:S(2)}) copy-start(bf16[128,2048]{1,0:T(8,128)(2,1)} %u_ref.3) | copy-start | bytes 1572868
  6.1 13.6 %collective-permute-start.3 = (bf16[4,128,128]{2,1,0:T(8,128)(2,1)S(1)}, bf16[4,128,128]{2,1,0:T(8,128)(2,1)S(1)}, u32[]{:S(2)}, u32[]{:S(2)}) collective-permute-start(bf16[4,128,128]{2,1,0:T(8,128)(2,1)S(1)} %get-tuple-element.44), channel_id=1, source_target_pairs={{0,8},{4,12},{8,0},{12,4},{16,24},{20,28},{24,16},{28,20},{1,9},{5... | collective-permute-start | bytes 393224 | tf_op jit(solution)/shard_map/ppermute | solution.py:346
  9.1 3.3 %collective-permute-start.6 = (bf16[2,128,128]{2,1,0:T(8,128)(2,1)S(1)}, bf16[2,128,128]{2,1,0:T(8,128)(2,1)S(1)}, u32[]{:S(2)}, u32[]{:S(2)}) collective-permute-start(bf16[2,128,128]{2,1,0:T(8,128)(2,1)S(1)} %get-tuple-element.47), channel_id=1, source_target_pairs={{0,4},{4,0},{8,12},{12,8},{16,20},{20,16},{24,28},{28,24},{1,5},{5... | collective-permute-start | bytes 196616 | tf_op jit(solution)/shard_map/ppermute | solution.py:346
  9.1 4.8 %collective-permute-start.7 = (bf16[2,128,128]{2,1,0:T(8,128)(2,1)S(1)}, bf16[2,128,128]{2,1,0:T(8,128)(2,1)S(1)}, u32[]{:S(2)}, u32[]{:S(2)}) collective-permute-start(bf16[2,128,128]{2,1,0:T(8,128)(2,1)S(1)} %get-tuple-element.48), channel_id=1, source_target_pairs={{0,12},{4,8},{8,4},{12,0},{16,28},{20,24},{24,20},{28,16},{1,13},{... | collective-permute-start | bytes 196616 | tf_op jit(solution)/shard_map/ppermute | solution.py:346
  9.3 6.2 %collective-permute-start.8 = (bf16[2,128,128]{2,1,0:T(8,128)(2,1)S(1)}, bf16[2,128,128]{2,1,0:T(8,128)(2,1)S(1)}, u32[]{:S(2)}, u32[]{:S(2)}) collective-permute-start(bf16[2,128,128]{2,1,0:T(8,128)(2,1)S(1)} %get-tuple-element.49), channel_id=1, source_target_pairs={{0,20},{4,16},{8,28},{12,24},{16,4},{20,0},{24,12},{28,8},{1,21},{... | collective-permute-start | bytes 196616 | tf_op jit(solution)/shard_map/ppermute | solution.py:346
  10.8 6.3 %collective-permute-start.9 = (bf16[2,128,128]{2,1,0:T(8,128)(2,1)S(1)}, bf16[2,128,128]{2,1,0:T(8,128)(2,1)S(1)}, u32[]{:S(2)}, u32[]{:S(2)}) collective-permute-start(bf16[2,128,128]{2,1,0:T(8,128)(2,1)S(1)} %get-tuple-element.50), channel_id=1, source_target_pairs={{0,28},{4,24},{8,20},{12,16},{16,12},{20,8},{24,4},{28,0},{1,29},{... | collective-permute-start | bytes 196616 | tf_op jit(solution)/shard_map/ppermute | solution.py:346
  12.4 13.6 %collective-permute-start.4 = (bf16[4,128,128]{2,1,0:T(8,128)(2,1)S(1)}, bf16[4,128,128]{2,1,0:T(8,128)(2,1)S(1)}, u32[]{:S(2)}, u32[]{:S(2)}) collective-permute-start(bf16[4,128,128]{2,1,0:T(8,128)(2,1)S(1)} %get-tuple-element.45), channel_id=1, source_target_pairs={{0,16},{4,20},{8,24},{12,28},{16,0},{20,4},{24,8},{28,12},{1,17},{... | collective-permute-start | bytes 393224 | tf_op jit(solution)/shard_map/ppermute | solution.py:346
  13.9 12.1 %collective-permute-start.5 = (bf16[4,128,128]{2,1,0:T(8,128)(2,1)S(1)}, bf16[4,128,128]{2,1,0:T(8,128)(2,1)S(1)}, u32[]{:S(2)}, u32[]{:S(2)}) collective-permute-start(bf16[4,128,128]{2,1,0:T(8,128)(2,1)S(1)} %get-tuple-element.46), channel_id=1, source_target_pairs={{0,24},{4,28},{8,16},{12,20},{16,8},{20,12},{24,0},{28,4},{1,25},{... | collective-permute-start | bytes 393224 | tf_op jit(solution)/shard_map/ppermute | solution.py:346
  15.5 11.6 %collective-permute-start = (bf16[4,32,512]{2,1,0:T(8,128)(2,1)S(1)}, bf16[4,32,512]{2,1,0:T(8,128)(2,1)S(1)}, u32[]{:S(2)}, u32[]{:S(2)}) collective-permute-start(bf16[4,32,512]{2,1,0:T(8,128)(2,1)S(1)} %get-tuple-element.38), channel_id=1, source_target_pairs={{0,1},{1,0},{2,3},{3,2},{4,5},{5,4},{6,7},{7,6},{8,9},{9,8},{10,11... | collective-permute-start | bytes 393224 | tf_op jit(solution)/shard_map/ppermute | solution.py:346
  17.1 12.8 %collective-permute-start.1 = (bf16[4,32,512]{2,1,0:T(8,128)(2,1)S(1)}, bf16[4,32,512]{2,1,0:T(8,128)(2,1)S(1)}, u32[]{:S(2)}, u32[]{:S(2)}) collective-permute-start(bf16[4,32,512]{2,1,0:T(8,128)(2,1)S(1)} %get-tuple-element.39), channel_id=1, source_target_pairs={{0,2},{1,3},{2,0},{3,1},{4,6},{5,7},{6,4},{7,5},{8,10},{9,11},{10,... | collective-permute-start | bytes 393224 | tf_op jit(solution)/shard_map/ppermute | solution.py:346
  19.7 10.2 %collective-permute-start.2 = (bf16[4,32,512]{2,1,0:T(8,128)(2,1)S(1)}, bf16[4,32,512]{2,1,0:T(8,128)(2,1)S(1)}, u32[]{:S(2)}, u32[]{:S(2)}) collective-permute-start(bf16[4,32,512]{2,1,0:T(8,128)(2,1)S(1)} %get-tuple-element.40), channel_id=1, source_target_pairs={{0,3},{1,2},{2,1},{3,0},{4,7},{5,6},{6,5},{7,4},{8,11},{9,10},{10,... | collective-permute-start | bytes 393224 | tf_op jit(solution)/shard_map/ppermute | solution.py:346
  31.0 4.6 %collective-permute-start.15 = (f32[16,128]{1,0:T(8,128)S(1)}, f32[16,128]{1,0:T(8,128)S(1)}, u32[]{:S(2)}, u32[]{:S(2)}) collective-permute-start(f32[16,128]{1,0:T(8,128)S(1)} %get-tuple-element.56.refs_10_.refs_8_), channel_id=1, source_target_pairs={{0,24},{4,28},{8,16},{12,20},{16,8},{20,12},{24,0},{28,4},{1,25},{... | collective-permute-start | bytes 24584 | tf_op jit(solution)/shard_map/ppermute | solution.py:346
  32.5 3.7 %collective-permute-start.14 = (f32[16,128]{1,0:T(8,128)S(1)}, f32[16,128]{1,0:T(8,128)S(1)}, u32[]{:S(2)}, u32[]{:S(2)}) collective-permute-start(f32[16,128]{1,0:T(8,128)S(1)} %get-tuple-element.56.refs_10_.refs_8_), channel_id=1, source_target_pairs={{0,16},{4,20},{8,24},{12,28},{16,0},{20,4},{24,8},{28,12},{1,17},{... | collective-permute-start | bytes 24584 | tf_op jit(solution)/shard_map/ppermute | solution.py:346
  33.7 3.7 %collective-permute-start.13 = (f32[16,128]{1,0:T(8,128)S(1)}, f32[16,128]{1,0:T(8,128)S(1)}, u32[]{:S(2)}, u32[]{:S(2)}) collective-permute-start(f32[16,128]{1,0:T(8,128)S(1)} %get-tuple-element.56.refs_10_.refs_8_), channel_id=1, source_target_pairs={{0,8},{4,12},{8,0},{12,4},{16,24},{20,28},{24,16},{28,20},{1,9},{5... | collective-permute-start | bytes 24584 | tf_op jit(solution)/shard_map/ppermute | solution.py:346
  40.2 19.0 %collective-permute-start.19 = (bf16[4,128,128]{2,1,0:T(8,128)(2,1)S(1)}, bf16[4,128,128]{2,1,0:T(8,128)(2,1)S(1)}, u32[]{:S(2)}, u32[]{:S(2)}) collective-permute-start(bf16[4,128,128]{2,1,0:T(8,128)(2,1)S(1)} %get-tuple-element.63), channel_id=1, source_target_pairs={{0,8},{4,12},{8,0},{12,4},{16,24},{20,28},{24,16},{28,20},{1,9},{5... | collective-permute-start | bytes 393224 | tf_op jit(solution)/shard_map/ppermute | solution.py:346
  41.1 6.0 %collective-permute-start.10 = (f32[32,128]{1,0:T(8,128)S(1)}, f32[32,128]{1,0:T(8,128)S(1)}, u32[]{:S(2)}, u32[]{:S(2)}) collective-permute-start(f32[32,128]{1,0:T(8,128)S(1)} %get-tuple-element.53), channel_id=1, source_target_pairs={{0,1},{1,0},{2,3},{3,2},{4,5},{5,4},{6,7},{7,6},{8,9},{9,8},{10,11... | collective-permute-start | bytes 49160 | tf_op jit(solution)/shard_map/ppermute | solution.py:346
  44.5 4.7 %collective-permute-start.11 = (f32[32,128]{1,0:T(8,128)S(1)}, f32[32,128]{1,0:T(8,128)S(1)}, u32[]{:S(2)}, u32[]{:S(2)}) collective-permute-start(f32[32,128]{1,0:T(8,128)S(1)} %get-tuple-element.54), channel_id=1, source_target_pairs={{0,2},{1,3},{2,0},{3,1},{4,6},{5,7},{6,4},{7,5},{8,10},{9,11},{10,... | collective-permute-start | bytes 49160 | tf_op jit(solution)/shard_map/ppermute | solution.py:346
  45.7 5.5 %collective-permute-start.12 = (f32[32,128]{1,0:T(8,128)S(1)}, f32[32,128]{1,0:T(8,128)S(1)}, u32[]{:S(2)}, u32[]{:S(2)}) collective-permute-start(f32[32,128]{1,0:T(8,128)S(1)} %get-tuple-element.55), channel_id=1, source_target_pairs={{0,3},{1,2},{2,1},{3,0},{4,7},{5,6},{6,5},{7,4},{8,11},{9,10},{10,... | collective-permute-start | bytes 49160 | tf_op jit(solution)/shard_map/ppermute | solution.py:346
  47.2 6.0 %collective-permute-start.22 = (bf16[2,128,128]{2,1,0:T(8,128)(2,1)S(1)}, bf16[2,128,128]{2,1,0:T(8,128)(2,1)S(1)}, u32[]{:S(2)}, u32[]{:S(2)}) collective-permute-start(bf16[2,128,128]{2,1,0:T(8,128)(2,1)S(1)} %get-tuple-element.66), channel_id=1, source_target_pairs={{0,4},{4,0},{8,12},{12,8},{16,20},{20,16},{24,28},{28,24},{1,5},{5... | collective-permute-start | bytes 196616 | tf_op jit(solution)/shard_map/ppermute | solution.py:346
  47.2 7.1 %collective-permute-start.23 = (bf16[2,128,128]{2,1,0:T(8,128)(2,1)S(1)}, bf16[2,128,128]{2,1,0:T(8,128)(2,1)S(1)}, u32[]{:S(2)}, u32[]{:S(2)}) collective-permute-start(bf16[2,128,128]{2,1,0:T(8,128)(2,1)S(1)} %get-tuple-element.67), channel_id=1, source_target_pairs={{0,12},{4,8},{8,4},{12,0},{16,28},{20,24},{24,20},{28,16},{1,13},{... | collective-permute-start | bytes 196616 | tf_op jit(solution)/shard_map/ppermute | solution.py:346
  49.2 6.7 %collective-permute-start.24 = (bf16[2,128,128]{2,1,0:T(8,128)(2,1)S(1)}, bf16[2,128,128]{2,1,0:T(8,128)(2,1)S(1)}, u32[]{:S(2)}, u32[]{:S(2)}) collective-permute-start(bf16[2,128,128]{2,1,0:T(8,128)(2,1)S(1)} %get-tuple-element.68), channel_id=1, source_target_pairs={{0,20},{4,16},{8,28},{12,24},{16,4},{20,0},{24,12},{28,8},{1,21},{... | collective-permute-start | bytes 196616 | tf_op jit(solution)/shard_map/ppermute | solution.py:346
  51.3 5.1 %collective-permute-start.25 = (bf16[2,128,128]{2,1,0:T(8,128)(2,1)S(1)}, bf16[2,128,128]{2,1,0:T(8,128)(2,1)S(1)}, u32[]{:S(2)}, u32[]{:S(2)}) collective-permute-start(bf16[2,128,128]{2,1,0:T(8,128)(2,1)S(1)} %get-tuple-element.69), channel_id=1, source_target_pairs={{0,28},{4,24},{8,20},{12,16},{16,12},{20,8},{24,4},{28,0},{1,29},{... | collective-permute-start | bytes 196616 | tf_op jit(solution)/shard_map/ppermute | solution.py:346
  53.2 11.9 %collective-permute-start.20 = (bf16[4,128,128]{2,1,0:T(8,128)(2,1)S(1)}, bf16[4,128,128]{2,1,0:T(8,128)(2,1)S(1)}, u32[]{:S(2)}, u32[]{:S(2)}) collective-permute-start(bf16[4,128,128]{2,1,0:T(8,128)(2,1)S(1)} %get-tuple-element.64), channel_id=1, source_target_pairs={{0,16},{4,20},{8,24},{12,28},{16,0},{20,4},{24,8},{28,12},{1,17},{... | collective-permute-start | bytes 393224 | tf_op jit(solution)/shard_map/ppermute | solution.py:346
  54.3 10.9 %collective-permute-start.21 = (bf16[4,128,128]{2,1,0:T(8,128)(2,1)S(1)}, bf16[4,128,128]{2,1,0:T(8,128)(2,1)S(1)}, u32[]{:S(2)}, u32[]{:S(2)}) collective-permute-start(bf16[4,128,128]{2,1,0:T(8,128)(2,1)S(1)} %get-tuple-element.65), channel_id=1, source_target_pairs={{0,24},{4,28},{8,16},{12,20},{16,8},{20,12},{24,0},{28,4},{1,25},{... | collective-permute-start | bytes 393224 | tf_op jit(solution)/shard_map/ppermute | solution.py:346
  56.0 9.2 %collective-permute-start.16 = (bf16[4,32,512]{2,1,0:T(8,128)(2,1)S(1)}, bf16[4,32,512]{2,1,0:T(8,128)(2,1)S(1)}, u32[]{:S(2)}, u32[]{:S(2)}) collective-permute-start(bf16[4,32,512]{2,1,0:T(8,128)(2,1)S(1)} %get-tuple-element.59), channel_id=1, source_target_pairs={{0,1},{1,0},{2,3},{3,2},{4,5},{5,4},{6,7},{7,6},{8,9},{9,8},{10,11... | collective-permute-start | bytes 393224 | tf_op jit(solution)/shard_map/ppermute | solution.py:346
  56.4 12.9 %collective-permute-start.17 = (bf16[4,32,512]{2,1,0:T(8,128)(2,1)S(1)}, bf16[4,32,512]{2,1,0:T(8,128)(2,1)S(1)}, u32[]{:S(2)}, u32[]{:S(2)}) collective-permute-start(bf16[4,32,512]{2,1,0:T(8,128)(2,1)S(1)} %get-tuple-element.60), channel_id=1, source_target_pairs={{0,2},{1,3},{2,0},{3,1},{4,6},{5,7},{6,4},{7,5},{8,10},{9,11},{10,... | collective-permute-start | bytes 393224 | tf_op jit(solution)/shard_map/ppermute | solution.py:346
  59.1 10.2 %collective-permute-start.18 = (bf16[4,32,512]{2,1,0:T(8,128)(2,1)S(1)}, bf16[4,32,512]{2,1,0:T(8,128)(2,1)S(1)}, u32[]{:S(2)}, u32[]{:S(2)}) collective-permute-start(bf16[4,32,512]{2,1,0:T(8,128)(2,1)S(1)} %get-tuple-element.61), channel_id=1, source_target_pairs={{0,3},{1,2},{2,1},{3,0},{4,7},{5,6},{6,5},{7,4},{8,11},{9,10},{10,... | collective-permute-start | bytes 393224 | tf_op jit(solution)/shard_map/ppermute | solution.py:346
  (6 other events, 6.2 us)

commit v3 on v2

v3 whole, which is shorter than its diff:
```python
import functools

import jax
import jax.numpy as jnp
from jax import lax
from jax.experimental import pallas as pl
from jax.experimental.pallas import tpu as pltpu
from jax.sharding import PartitionSpec as P

HEADS = 16
HEAD_DIM = 128
DILATION = 4
LANES = 128
SCALE = HEAD_DIM**-0.5
LOWEST = -1e30
VMEM_LIMIT = 32 * 1024 * 1024
F32, BF16 = jnp.float32, jnp.bfloat16
SHAPE = jax.ShapeDtypeStruct

NT = (((1,), (1,)), ((), ()))
TN = (((0,), (0,)), ((), ()))


def dot(a, b):
    return jnp.dot(a, b, preferred_element_type=F32)


def dot_nt(a, b):
    return lax.dot_general(a, b, NT, preferred_element_type=F32)


def dot_tn(a, b):
    return lax.dot_general(a, b, TN, preferred_element_type=F32)


def head_columns(head):
    return pl.ds(pl.multiple_of(head * HEAD_DIM, HEAD_DIM), HEAD_DIM)


def static_columns(index):
    return slice(index * HEAD_DIM, (index + 1) * HEAD_DIM)


def lanes_of(rows):
    return lax.broadcasted_iota(jnp.int32, (rows, LANES), 1)


def level_stats(q, k, v, u):
    s = dot_nt(k, q) * SCALE
    dp = dot_nt(v, u)
    top = jnp.max(s, axis=0, keepdims=True)
    p = jnp.exp(s - top)
    total = jnp.sum(p, axis=0, keepdims=True)
    return top + jnp.log(total), jnp.sum(p * dp, axis=0, keepdims=True) / total


def merge_stats(ea, da, eb, db):
    top = jnp.maximum(ea, eb)
    wa, wb = jnp.exp(ea - top), jnp.exp(eb - top)
    total = wa + wb
    return top + jnp.log(total), (wa * da + wb * db) / total


def level_weights(q, k, v, u, lse, delta):
    g = jnp.exp(dot_nt(k, q) * SCALE - lse)
    return g.astype(BF16), (g * (dot_nt(v, u) - delta)).astype(BF16)


def level_parts(q, k, v, u, lse, delta):
    p, ds = level_weights(q, k, v, u, lse, delta)
    return dot_tn(p, v), dot_tn(ds, k) * SCALE, dot(ds, q) * SCALE, dot(p, u)


def pick_rows(ref, rows):
    quarter = rows // DILATION
    lane = lanes_of(quarter)
    picked = jnp.zeros((quarter, LANES), F32)
    for residue in range(DILATION):
        part = ref[pl.ds(residue, quarter, stride=DILATION), :]
        picked = jnp.where(lane % DILATION == residue, part, picked)
    return picked


def fetch(sources, buffers, sems):
    width = DILATION * HEAD_DIM
    groups = []
    for group in range(HEADS // DILATION):
        cols = pl.ds(group * width, width)
        groups.append(
            [
                pltpu.make_async_copy(
                    source.at[:, cols], buffers.at[which, :, cols], sems.at[which, group]
                )
                for which, source in enumerate(sources)
            ]
        )
        for copy in groups[-1]:
            copy.start()
    return groups


def pick_kernel(n_i, n_o, slots, at_ref, *refs):
    sources, (mid_ref, far_ref, buffers, sems, wide) = refs[:4], refs[4:]
    rows = sources[0].shape[0]
    quarter = rows // DILATION
    width = n_o // slots
    pos = at_ref[0]
    for group, copies in enumerate(fetch(sources, buffers, sems)):
        for which, copy in enumerate(copies):
            copy.wait()
            for residue in range(DILATION):
                head = group * DILATION + residue
                place, slot = head // slots, head % slots
                wide[which, head] = buffers[which, :, static_columns(head)].astype(F32)
                picked = wide[which, head, pl.ds(residue, quarter, stride=DILATION), :]
                mid_ref[place, which, :, static_columns(slot)] = picked.astype(BF16)
    for slot in range(slots):
        for which in range(4):
            piece = buffers[which, :, head_columns(pos * slots + slot)]
            for core in range(width):
                far_ref[slot * width + core, which] = piece


def near_stats_kernel(k_hbm, v_hbm, q_hbm, u_hbm, stats_ref, mid_ref, buffers, sems, turn):
    rows = q_hbm.shape[0]
    turn[...] = jnp.zeros_like(turn)
    for group, copies in enumerate(fetch((k_hbm, v_hbm, q_hbm, u_hbm), buffers, sems)):
        for copy in copies:
            copy.wait()
        for residue in range(DILATION):
            head = group * DILATION + residue
            k, v, q, u = [buffers[which, :, static_columns(head)] for which in range(4)]
            e, d = level_stats(q, k, v, u)
            turn[head : head + 1, :] = e
            turn[HEADS + head : HEADS + head + 1, :] = d
    stats_ref[...] = turn[: 2 * HEADS, :]
    turn[...] = turn[...].T
    mid_ref[...] = pick_rows(turn, rows)


def stacked(ref, which, first=0, step=1):
    return jnp.concatenate(
        [ref[first + step * i, which] for i in range(ref.shape[0] // step)], axis=0
    )


def far_stats_kernel(slots, width, at_ref, far_ref, stats_ref):
    core = at_ref[2]
    keys, values = stacked(far_ref, 0), stacked(far_ref, 1)
    for m in range(slots):
        source = m * width + core
        e, d = level_stats(far_ref[source, 2], keys, values, far_ref[source, 3])
        stats_ref[m : m + 1, :] = e
        stats_ref[slots + m : slots + m + 1, :] = d


def middle_operands(mid_ref, slot):
    cols = static_columns(slot)
    return [
        jnp.concatenate([mid_ref[i, which, :, cols] for i in range(mid_ref.shape[0])], axis=0)
        for which in range(4)
    ]


def middle_stats_kernel(n_i, n_o, slots, at_ref, *refs):
    mid_ref, near_ref, nearmid_ref, far_ref, zmsg_ref, xmsg_ref, stats_ref, turn, spread = refs
    quarter = nearmid_ref.shape[0]
    pos = at_ref[0]
    turn[...] = jnp.zeros_like(turn)
    for slot in range(slots):
        k, v, q, u = middle_operands(mid_ref, slot)
        e, d = level_stats(q, k, v, u)
        turn[slot : slot + 1, :] = e
        turn[slots + slot : slots + slot + 1, :] = d
    stats_ref[...] = turn[: 2 * slots, :]
    columns = turn[...].T
    lane = lanes_of(quarter)
    for i in range(n_i):
        chunk = pltpu.roll(columns[i * quarter : (i + 1) * quarter], 2 * HEADS, 1)
        zmsg_ref[i] = jnp.where(lane < 2 * HEADS, nearmid_ref[...], chunk)
    own = pltpu.roll(zmsg_ref[pos], LANES - 2 * HEADS, 1)
    lane_residue = (pos * slots + lane % slots) % DILATION
    blank = jnp.where(lane < slots, LOWEST, 0.0)
    for residue in range(DILATION):
        spread[pl.ds(residue, quarter, stride=DILATION), :] = jnp.where(
            lane_residue == residue, own, blank
        )
    across = spread[...].T
    e, d = merge_stats(
        near_ref[pl.ds(pos * slots, slots), :],
        near_ref[pl.ds(HEADS + pos * slots, slots), :],
        across[:slots],
        across[slots : 2 * slots],
    )
    for o in range(n_o):
        xmsg_ref[o, :slots] = e
        xmsg_ref[o, slots : 2 * slots] = d
        xmsg_ref[o, 2 * slots :] = far_ref[...]


def middle_parts_kernel(n_i, slots, width, at_ref, *refs):
    mid_ref, near_ref, stats_ref, zmsg_ref, xmsg_ref, out_ref, final_ref, far, turn, spread = refs
    quarter = zmsg_ref.shape[1]
    rows = quarter * DILATION
    pos, chip, core = at_ref[0], at_ref[1], at_ref[2]

    lane = lanes_of(quarter)
    mid = jnp.zeros((quarter, LANES), F32)
    for i in range(n_i):
        place = i * slots
        e = pltpu.roll(zmsg_ref[i], (place + LANES - 2 * HEADS) % LANES, 1)
        de = pltpu.roll(zmsg_ref[i], (place + LANES - HEADS - slots) % LANES, 1)
        mid = jnp.where((lane >= place) & (lane < place + slots), e, mid)
        mid = jnp.where((lane >= HEADS + place) & (lane < HEADS + place + slots), de, mid)
    blank = jnp.where(lane < HEADS, LOWEST, 0.0)
    for residue in range(DILATION):
        spread[pl.ds(residue, quarter, stride=DILATION), :] = jnp.where(
            lane % DILATION == residue, mid, blank
        )
    across = spread[...].T
    far[:HEADS] = jnp.full((HEADS, rows), LOWEST, F32)
    far[HEADS:] = jnp.zeros((HEADS, rows), F32)
    for m in range(slots):
        head = pos * slots + m
        source = m * width + core
        far[pl.ds(head, 1), :] = xmsg_ref[source, pl.ds(2 * slots + chip, 1), :]
        far[pl.ds(HEADS + head, 1), :] = xmsg_ref[source, pl.ds(3 * slots + chip, 1), :]
    e, d = merge_stats(
        near_ref[:HEADS], near_ref[HEADS:], across[:HEADS], across[HEADS : 2 * HEADS]
    )
    e, d = merge_stats(e, d, far[:HEADS], far[HEADS:])
    final_ref[:HEADS] = e
    final_ref[HEADS:] = d

    spread[...] = jnp.zeros_like(spread)
    spread[: 2 * HEADS] = final_ref[...]
    spread[...] = spread[...].T
    own = pick_rows(spread, rows)
    turn[...] = jnp.concatenate(
        [jnp.where(pos == i, own, zmsg_ref[i]) for i in range(n_i)], axis=0
    ).T
    owned = lax.broadcasted_iota(jnp.int32, (1, n_i * quarter), 1) // quarter == pos
    for slot in range(slots):
        lse, delta = merge_stats(
            turn[pl.ds(pos * slots + slot, 1), :],
            turn[pl.ds(HEADS + pos * slots + slot, 1), :],
            jnp.where(owned, LOWEST, stats_ref[slot : slot + 1, :]),
            stats_ref[slots + slot : slots + slot + 1, :],
        )
        k, v, q, u = middle_operands(mid_ref, slot)
        for which, part in enumerate(level_parts(q, k, v, u, lse, delta)):
            part = part.astype(BF16)
            for i in range(n_i):
                out_ref[i, which, :, static_columns(slot)] = part[i * quarter : (i + 1) * quarter]


def far_parts_kernel(slots, width, at_ref, far_ref, xmsg_ref, out_ref, weights, score_grads):
    rows = far_ref.shape[2]
    chip, core = at_ref[1], at_ref[2]
    own = chip * width + core
    keys, values = stacked(far_ref, 0), stacked(far_ref, 1)
    for m in range(slots):
        source = m * width + core
        lse, delta = merge_stats(
            xmsg_ref[source, pl.ds(chip, 1), :],
            xmsg_ref[source, pl.ds(slots + chip, 1), :],
            xmsg_ref[own, 2 * slots + m : 2 * slots + m + 1, :],
            xmsg_ref[own, 3 * slots + m : 3 * slots + m + 1, :],
        )
        p, ds = level_weights(far_ref[source, 2], keys, values, far_ref[source, 3], lse, delta)
        share = dot_tn(p, values).astype(BF16)
        query_part = (dot_tn(ds, keys) * SCALE).astype(BF16)
        for other in range(width):
            out_ref[m * width + other, 0] = share
            out_ref[m * width + other, 1] = query_part
        weights[:, m * rows : (m + 1) * rows] = p
        score_grads[:, m * rows : (m + 1) * rows] = ds
    queries = jnp.concatenate([far_ref[m * width + core, 2] for m in range(slots)], axis=0)
    ups = jnp.concatenate([far_ref[m * width + core, 3] for m in range(slots)], axis=0)
    key_part = (dot(score_grads[...], queries) * SCALE).astype(BF16)
    value_part = dot(weights[...], ups).astype(BF16)
    for index in range(slots * width):
        out_ref[index, 2] = key_part[index * rows : (index + 1) * rows]
        out_ref[index, 3] = value_part[index * rows : (index + 1) * rows]


def near_parts_kernel(k_hbm, v_hbm, q_hbm, u_hbm, stats_ref, out_ref, buffers, sems):
    for group, copies in enumerate(fetch((k_hbm, v_hbm, q_hbm, u_hbm), buffers, sems)):
        for copy in copies:
            copy.wait()
        for residue in range(DILATION):
            head = group * DILATION + residue
            k, v, q, u = [buffers[which, :, static_columns(head)] for which in range(4)]
            lse = stats_ref[head : head + 1, :]
            delta = stats_ref[HEADS + head : HEADS + head + 1, :]
            for which, part in enumerate(level_parts(q, k, v, u, lse, delta)):
                out_ref[which, head] = part


def final_kernel(n_i, slots, width, at_ref, near_ref, mid_ref, far_ref, *outs):
    rows = far_ref.shape[2]
    quarter = rows // DILATION
    pos, core = at_ref[0], at_ref[2]
    row = lax.broadcasted_iota(jnp.int32, (rows, quarter), 0)
    taken = lax.broadcasted_iota(jnp.int32, (rows, quarter), 1) * DILATION

    def finish(place, slot, is_own):
        head = place * slots + slot
        spread = jnp.where(row == taken + head % DILATION, 1.0, 0.0).astype(BF16)
        for which, out in enumerate(outs):
            total = near_ref[which, head] + dot(spread, mid_ref[place, which, :, static_columns(slot)])
            if is_own:
                for other in range(1 if which < 2 else width):
                    source = slot * width + (core ^ other)
                    total += far_ref[source, which].astype(F32)
            out[:, head_columns(head)] = total.astype(BF16)

    for step in range(n_i):
        for slot in range(slots):
            finish((pos + step) % n_i, slot, step == 0)


def call(kernel, name, outs, scratch, flops, operands, at=None, in_hbm=0):
    specs = [pl.BlockSpec(memory_space=pl.ANY if i < in_hbm else pltpu.VMEM) for i in range(len(operands))]
    moved = sum(x.size * x.dtype.itemsize for x in tuple(operands) + tuple(outs))
    if at is not None:
        specs = [pl.BlockSpec(memory_space=pltpu.SMEM)] + specs
        operands = (at,) + tuple(operands)
    return pl.pallas_call(
        kernel,
        out_shape=tuple(outs),
        in_specs=specs,
        out_specs=tuple(pl.BlockSpec(memory_space=pltpu.VMEM) for _ in outs),
        scratch_shapes=scratch,
        compiler_params=pltpu.CompilerParams(vmem_limit_bytes=VMEM_LIMIT),
        cost_estimate=pl.CostEstimate(flops=flops, bytes_accessed=moved, transcendentals=0),
        name=name,
    )(*operands)


def exchange(x, axis):
    return lax.all_to_all(x, axis, 0, 0, tiled=True)


def local(query_rows, key_rows, value_rows, upstream):
    rows, features = query_rows.shape
    n_i, n_o = lax.axis_size("seqi"), lax.axis_size("seqo")
    slots = HEADS // n_i
    width = n_o // slots
    quarter = rows // DILATION
    pos = lax.axis_index("seqi").astype(jnp.int32)
    block = lax.axis_index("seqo").astype(jnp.int32)
    at = jnp.stack([pos, block // width, block % width])
    sources = (key_rows, value_rows, query_rows, upstream)
    unit = 2 * rows * rows * HEAD_DIM
    bind = functools.partial

    mid = SHAPE((n_i, 4, quarter, slots * HEAD_DIM), BF16)
    far = SHAPE((n_o, 4, rows, HEAD_DIM), BF16)
    square = pltpu.VMEM((LANES, rows), F32)
    buffers = [pltpu.VMEM((4, rows, features), BF16), pltpu.SemaphoreType.DMA((4, HEADS // DILATION))]

    def stats(*shape):
        return SHAPE(shape, F32)

    mids, fars = call(
        bind(pick_kernel, n_i, n_o, slots),
        "pick",
        [mid, far],
        buffers + [pltpu.VMEM((4, HEADS, rows, HEAD_DIM), F32)],
        unit,
        sources,
        at,
        in_hbm=4,
    )
    mids = exchange(mids, "seqi")
    fars = exchange(fars, "seqo")

    near, nearmid = call(
        near_stats_kernel,
        "near_stats",
        [stats(2 * HEADS, rows), stats(quarter, LANES)],
        buffers + [square],
        unit * HEADS * 2,
        sources,
        in_hbm=4,
    )
    (farstats,) = call(
        bind(far_stats_kernel, slots, width),
        "far_stats",
        [stats(2 * slots, rows)],
        [],
        unit * n_o * slots * 2,
        [fars],
        at,
    )
    zmsg, xmsg, middle = call(
        bind(middle_stats_kernel, n_i, n_o, slots),
        "middle_stats",
        [stats(n_i, quarter, LANES), stats(n_o, 4 * slots, rows), stats(2 * slots, n_i * quarter)],
        [pltpu.VMEM((LANES, n_i * quarter), F32), square],
        unit * slots * 2,
        [mids, near, nearmid, farstats],
        at,
    )
    zmsg = exchange(zmsg, "seqi")
    xmsg = exchange(xmsg, "seqo")

    midparts, final = call(
        bind(middle_parts_kernel, n_i, slots, width),
        "middle_parts",
        [mid, stats(2 * HEADS, rows)],
        [
            pltpu.VMEM((2 * HEADS, rows), F32),
            pltpu.VMEM((LANES, n_i * quarter), F32),
            square,
        ],
        unit * slots * 6,
        [mids, near, middle, zmsg, xmsg],
        at,
    )
    midparts = exchange(midparts, "seqi")
    (farparts,) = call(
        bind(far_parts_kernel, slots, width),
        "far_parts",
        [far],
        [pltpu.VMEM((n_o * rows, slots * rows), BF16)] * 2,
        unit * n_o * slots * 6,
        [fars, xmsg],
        at,
    )
    farparts = exchange(farparts, "seqo")

    (nearparts,) = call(
        near_parts_kernel,
        "near_parts",
        [stats(4, HEADS, rows, HEAD_DIM)],
        buffers,
        unit * HEADS * 6,
        sources + (final,),
        in_hbm=4,
    )
    return call(
        bind(final_kernel, n_i, slots, width),
        "final",
        [SHAPE((rows, features), BF16)] * 4,
        [],
        unit * HEADS,
        [nearparts, midparts, farparts],
        at,
    )


def solution(mesh):
    rows = P(("seqo", "seqi"), None)
    return jax.shard_map(
        local,
        mesh=mesh,
        in_specs=(rows,) * 4,
        out_specs=(rows,) * 4,
        check_vma=False,
    )
```

time: 72.5 us -> 109 us (1.50)
  blocking collectives: 0 us -> 36.1 us
  starting transfers between devices: 32.9 us -> 11.9 us
  waiting for transfers between devices: 12.7 us -> 25.2 us
  local copies, waits for them, and re-layouts: 8.34 us -> 13.6 us
  Pallas kernels: 17.2 us -> 21 us
    all_to_all x0 -> x3, blocking collectives: none -> 36.1 us  [exchange(): return lax.all_to_all(x, axis, 0, 0, tiled=True)]
    ppermute x26 -> x0, starting transfers between devices: 32.9 us -> none  [swap(): return lax.ppermute(x, axis, [(i, i ^ mask) for i in range(n)])]
    all_to_all x0 -> x3, waiting for transfers between devices: none -> 25.2 us  [exchange(): return lax.all_to_all(x, axis, 0, 0, tiled=True)]
    ppermute x26 -> x0, waiting for transfers between devices: 12.7 us -> none  [swap(): return lax.ppermute(x, axis, [(i, i ^ mask) for i in range(n)])]
    all_to_all x0 -> x3, starting transfers between devices: none -> 11.9 us  [exchange(): return lax.all_to_all(x, axis, 0, 0, tiled=True)]
    unnamed x24 -> x30, local copies, waits for them, and re-layouts: 8.34 us -> 13.6 us
    pallas_call x8, Pallas kernels: 17.2 us -> 21 us  [call(): pl.pallas_call(kernel, out_shape=tuple(outs), in_specs=specs, out_specs=t...]
  transfers between devices with their start and end apart: 26 -> 3, of which waited for: 7 -> 3; matrix products, arithmetic and copies ran while one was open for 0% -> 0% of each run, Pallas kernels for 13% -> 11%
where the time goes in v3:
time: 109 us
  blocking collectives  36.1 us (33%)
  waiting for transfers between devices  25.2 us (23%)
  Pallas kernels  21 us (19%)
  local copies, waits for them, and re-layouts  13.6 us (12%)
  starting transfers between devices  11.9 us (11%)
    all_to_all x3, blocking collectives, exchange(): return lax.all_to_all(x, axis, 0, 0, tiled=True)  36.1 us
    all_to_all x3, waiting for transfers between devices, exchange(): return lax.all_to_all(x, axis, 0, 0, tiled=True)  25.2 us
    pallas_call x8, Pallas kernels, call(): pl.pallas_call(kernel, out_shape=tuple(outs), in_specs=specs, out_specs=t...  21 us
    unnamed x30, local copies, waits for them, and re-layouts  13.6 us
    all_to_all x3, starting transfers between devices, exchange(): return lax.all_to_all(x, axis, 0, 0, tiled=True)  11.9 us
  transfers between devices with their start and end apart: 3, of which 3 were waited for; matrix products, arithmetic and copies ran while one was open for 0% of the time, Pallas kernels for 11%

profile of v3, /device:TPU:0, one launch (start us, length us, event | category | flops | bytes accessed | tf_op | source)
XLA Modules:
  0.0 108.6 jit_solution(6950678294394856709)
XLA Ops:
  0.6 0.1 pad_add_fusion.at_ref
  0.7 1.0 copy-done.2
  1.8 1.0 copy-done.4
  2.8 1.0 copy-done.6
  3.9 1.0 copy-done.8
  4.9 2.6 %pick.1 = (bf16[4,4,32,512]{3,2,1,0:T(8,128)(2,1)}, bf16[8,4,128,128]{3,2,1,0:T(8,128)(2,1)S(1)}) custom-call(s32[3]{0:T(128)S(1)} %pad_add_fusion.at_ref, bf16[128,2048]{1,0:T(8,128)(2,1)S(1)} %copy-done.2, bf16[128,2048]{1,0:T(8,128)(2,1)S(1)} %copy-done.4, bf16[128,2048]{1,0:T(8,128)(2,1)S(1)} %copy-done.6, bf16[128,2048]{1,0:T(8,128)(2,1)S(1)} %copy-done.8), custom_call_target="tpu_custom_call" | custom-call | flops 4194304 | bytes 3670016 | tf_op jit(solution)/shard_map/pick/pallas_call | solution.py:329
  7.5 20.4 %all_to_all.30.far_ref = bf16[8,4,128,128]{3,2,1,0:T(8,128)(2,1)} all-to-all(bf16[8,4,128,128]{3,2,1,0:T(8,128)(2,1)S(1)} %get-tuple-element.16), channel_id=1, replica_groups=mesh['seqo'=8,'seqi'=4] {'seqo'}, dimensions={0} | all-to-all | bytes 2097152 | tf_op jit(solution)/shard_map/all_to_all | solution.py:342
  27.9 4.9 %all-to-all-start = ((bf16[4,4,32,512]{3,2,1,0:T(8,128)(2,1)}), bf16[4,4,32,512]{3,2,1,0:T(8,128)(2,1)S(1)}, u32[]{:S(2)}, u32[]{:S(2)}) async-start(bf16[4,4,32,512]{3,2,1,0:T(8,128)(2,1)} %get-tuple-element.13), calls=%async_computation | async-start | bytes 1048576 | tf_op jit(solution)/shard_map/all_to_all | solution.py:342
  32.8 0.0 copy-done.3
  32.8 0.0 copy-done.7
  32.8 2.0 %near_stats.1 = (f32[32,128]{1,0:T(8,128)S(1)}, f32[32,128]{1,0:T(8,128)S(1)}) custom-call(bf16[128,2048]{1,0:T(8,128)(2,1)S(1)} %copy-done.3, bf16[128,2048]{1,0:T(8,128)(2,1)S(1)} %copy-done.5, bf16[128,2048]{1,0:T(8,128)(2,1)S(1)} %copy-done.7, bf16[128,2048]{1,0:T(8,128)(2,1)S(1)} %copy-done.9), custom_call_target="tpu_custom_call" | custom-call | flops 134217728 | bytes 2129920 | tf_op jit(solution)/shard_map/near_stats/pallas_call | solution.py:329
  34.9 1.2 %copy-done.10 = bf16[8,4,128,128]{3,2,1,0:T(8,128)(2,1)S(1)} copy-done((bf16[8,4,128,128]{3,2,1,0:T(8,128)(2,1)S(1)}, bf16[8,4,128,128]{3,2,1,0:T(8,128)(2,1)}, u32[]{:S(2)}) %copy-start.10) | copy-done | bytes 1048600
  36.1 1.6 %far_stats.1.refs_3_ = f32[8,128]{1,0:T(8,128)S(1)} custom-call(s32[3]{0:T(128)S(1)} %pad_add_fusion.at_ref, bf16[8,4,128,128]{3,2,1,0:T(8,128)(2,1)S(1)} %copy-done.10), custom_call_target="tpu_custom_call" | custom-call | flops 268435456 | bytes 1052672 | tf_op jit(solution)/shard_map/far_stats/pallas_call | solution.py:329
  37.7 8.9 %all-to-all-done.refs_0_ = bf16[4,4,32,512]{3,2,1,0:T(8,128)(2,1)S(1)} async-done(((bf16[4,4,32,512]{3,2,1,0:T(8,128)(2,1)}), bf16[4,4,32,512]{3,2,1,0:T(8,128)(2,1)S(1)}, u32[]{:S(2)}, u32[]{:S(2)}) %all-to-all-start) | async-done | bytes 524320 | tf_op jit(solution)/shard_map/all_to_all | solution.py:342
  46.6 1.2 %middle_stats.1 = (f32[4,32,128]{2,1,0:T(8,128)S(1)}, f32[8,16,128]{2,1,0:T(8,128)S(1)}, f32[8,128]{1,0:T(8,128)S(1)}) custom-call(s32[3]{0:T(128)S(1)} %pad_add_fusion.at_ref, bf16[4,4,32,512]{3,2,1,0:T(8,128)(2,1)S(1)} %all-to-all-done.refs_0_, f32[32,128]{1,0:T(8,128)S(1)} %get-tuple-element.14.refs_1_, f32[32,128]{1,0:T(8,128)S(1)} %get-tuple-element.15.refs_2_, ...), custom_call_target="tpu_custom_call" | custom-call | flops 33554432 | bytes 696320 | tf_op jit(solution)/shard_map/middle_stats/pallas_call | solution.py:329
  47.9 7.4 %all_to_all.31.refs_4_.xmsg_ref = f32[8,16,128]{2,1,0:T(8,128)S(1)} all-to-all(f32[8,16,128]{2,1,0:T(8,128)S(1)} %get-tuple-element.19), channel_id=1, replica_groups=mesh['seqo'=8,'seqi'=4] {'seqo'}, dimensions={0} | all-to-all | bytes 131072 | tf_op jit(solution)/shard_map/all_to_all | solution.py:342
  55.3 8.3 %all_to_all.32.refs_3_ = f32[4,32,128]{2,1,0:T(8,128)S(1)} all-to-all(f32[4,32,128]{2,1,0:T(8,128)S(1)} %get-tuple-element.18), channel_id=1, replica_groups=mesh['seqo'=8,'seqi'=4] {'seqi'}, dimensions={0} | all-to-all | bytes 131072 | tf_op jit(solution)/shard_map/all_to_all | solution.py:342
  63.5 2.7 %middle_parts.1 = (bf16[4,4,32,512]{3,2,1,0:T(8,128)(2,1)}, f32[32,128]{1,0:T(8,128)S(1)}) custom-call(s32[3]{0:T(128)S(1)} %pad_add_fusion.at_ref, bf16[4,4,32,512]{3,2,1,0:T(8,128)(2,1)S(1)} %all-to-all-done.refs_0_, f32[32,128]{1,0:T(8,128)S(1)} %get-tuple-element.14.refs_1_, f32[8,128]{1,0:T(8,128)S(1)} %get-tuple-element.17.refs_2_, ...), custom_call_target="tpu_custom_call" | custom-call | flops 100663296 | bytes 1216512 | tf_op jit(solution)/shard_map/middle_parts/pallas_call | solution.py:329
  66.3 3.5 %all-to-all-start.4 = ((bf16[4,4,32,512]{3,2,1,0:T(8,128)(2,1)}), bf16[4,4,32,512]{3,2,1,0:T(8,128)(2,1)S(1)}, u32[]{:S(2)}, u32[]{:S(2)}) async-start(bf16[4,4,32,512]{3,2,1,0:T(8,128)(2,1)} %get-tuple-element.21), calls=%async_computation.4 | async-start | bytes 1048576 | tf_op jit(solution)/shard_map/all_to_all | solution.py:342
  69.8 1.2 %copy-done.11 = bf16[8,4,128,128]{3,2,1,0:T(8,128)(2,1)S(1)} copy-done((bf16[8,4,128,128]{3,2,1,0:T(8,128)(2,1)S(1)}, bf16[8,4,128,128]{3,2,1,0:T(8,128)(2,1)}, u32[]{:S(2)}) %copy-start.11) | copy-done | bytes 1048600
  71.0 2.8 %far_parts.1 = bf16[8,4,128,128]{3,2,1,0:T(8,128)(2,1)S(1)} custom-call(s32[3]{0:T(128)S(1)} %pad_add_fusion.at_ref, bf16[8,4,128,128]{3,2,1,0:T(8,128)(2,1)S(1)} %copy-done.11, f32[8,16,128]{2,1,0:T(8,128)S(1)} %all_to_all.31.refs_4_.xmsg_ref), custom_call_target="tpu_custom_call" | custom-call | flops 805306368 | bytes 2162688 | tf_op jit(solution)/shard_map/far_parts/pallas_call | solution.py:329
  73.8 1.0 copy-done.14
  74.8 8.1 %all-to-all-done.4.mid_ref = bf16[4,4,32,512]{3,2,1,0:T(8,128)(2,1)S(1)} async-done(((bf16[4,4,32,512]{3,2,1,0:T(8,128)(2,1)}), bf16[4,4,32,512]{3,2,1,0:T(8,128)(2,1)S(1)}, u32[]{:S(2)}, u32[]{:S(2)}) %all-to-all-start.4) | async-done | bytes 524320 | tf_op jit(solution)/shard_map/all_to_all | solution.py:342
  83.0 0.8 copy-done.12
  83.8 3.6 %all-to-all-start.5 = ((bf16[8,4,128,128]{3,2,1,0:T(8,128)(2,1)}), bf16[8,4,128,128]{3,2,1,0:T(8,128)(2,1)S(1)}, u32[]{:S(2)}, u32[]{:S(2)}) async-start(bf16[8,4,128,128]{3,2,1,0:T(8,128)(2,1)} %copy-done.14), calls=%async_computation.5 | async-start | bytes 2097152 | tf_op jit(solution)/shard_map/all_to_all | solution.py:342
  87.3 5.2 %near_parts.1.near_ref = f32[4,16,128,128]{3,2,1,0:T(8,128)S(1)} custom-call(bf16[128,2048]{1,0:T(8,128)(2,1)S(1)} %copy-done.3, bf16[128,2048]{1,0:T(8,128)(2,1)S(1)} %copy-done.5, bf16[128,2048]{1,0:T(8,128)(2,1)S(1)} %copy-done.7, bf16[128,2048]{1,0:T(8,128)(2,1)S(1)} %copy-done.9, f32[32,128]{1,0:T(8,128)S(1)} %get-tuple-element.20.stats_ref), custom_call_target="tpu_custom_call" | custom-call | flops 402653184 | bytes 6307840 | tf_op jit(solution)/shard_map/near_parts/pallas_call | solution.py:329
  92.5 0.0 copy-start
  92.5 1.9 %copy-done = f32[4,16,128,128]{3,2,1,0:T(8,128)} copy-done((f32[4,16,128,128]{3,2,1,0:T(8,128)}, f32[4,16,128,128]{3,2,1,0:T(8,128)S(1)}, u32[]{:S(2)}) %copy-start) | copy-done | bytes 4194328
  94.5 8.2 %all-to-all-done.5.far_ref = bf16[8,4,128,128]{3,2,1,0:T(8,128)(2,1)S(1)} async-done(((bf16[8,4,128,128]{3,2,1,0:T(8,128)(2,1)}), bf16[8,4,128,128]{3,2,1,0:T(8,128)(2,1)S(1)}, u32[]{:S(2)}, u32[]{:S(2)}) %all-to-all-start.5) | async-done | bytes 1048608 | tf_op jit(solution)/shard_map/all_to_all | solution.py:342
  102.7 2.2 %copy-done.1 = f32[4,16,128,128]{3,2,1,0:T(8,128)S(1)} copy-done((f32[4,16,128,128]{3,2,1,0:T(8,128)S(1)}, f32[4,16,128,128]{3,2,1,0:T(8,128)}, u32[]{:S(2)}) %copy-start.1) | copy-done | bytes 4194328
  104.9 1.0 copy-done.13
  105.9 2.7 %final.1 = (bf16[128,2048]{1,0:T(8,128)(2,1)}, bf16[128,2048]{1,0:T(8,128)(2,1)}, bf16[128,2048]{1,0:T(8,128)(2,1)}, bf16[128,2048]{1,0:T(8,128)(2,1)}) custom-call(s32[3]{0:T(128)S(1)} %pad_add_fusion.at_ref, f32[4,16,128,128]{3,2,1,0:T(8,128)S(1)} %copy-done.1, bf16[4,4,32,512]{3,2,1,0:T(8,128)(2,1)S(1)} %copy-done.13, ...), custom_call_target="tpu_custom_call" | custom-call | flops 67108864 | bytes 7864320 | tf_op jit(solution)/shard_map/final/pallas_call | solution.py:329
  (16 shorter events, 0.0 us)
Async XLA Ops:
  0.7 1.0 copy-start.2
  1.8 1.0 copy-start.4
  2.8 1.0 copy-start.6
  3.9 1.0 copy-start.8
  4.9 27.9 %copy-start.3 = (bf16[128,2048]{1,0:T(8,128)(2,1)S(1)}, bf16[128,2048]{1,0:T(8,128)(2,1)}, u32[]{:S(2)}) copy-start(bf16[128,2048]{1,0:T(8,128)(2,1)} %k_hbm.3) | copy-start | bytes 1572868
  4.9 27.9 %copy-start.5 = (bf16[128,2048]{1,0:T(8,128)(2,1)S(1)}, bf16[128,2048]{1,0:T(8,128)(2,1)}, u32[]{:S(2)}) copy-start(bf16[128,2048]{1,0:T(8,128)(2,1)} %v_hbm.3) | copy-start | bytes 1572868
  4.9 27.9 %copy-start.7 = (bf16[128,2048]{1,0:T(8,128)(2,1)S(1)}, bf16[128,2048]{1,0:T(8,128)(2,1)}, u32[]{:S(2)}) copy-start(bf16[128,2048]{1,0:T(8,128)(2,1)} %q_hbm.3) | copy-start | bytes 1572868
  4.9 27.9 %copy-start.9 = (bf16[128,2048]{1,0:T(8,128)(2,1)S(1)}, bf16[128,2048]{1,0:T(8,128)(2,1)}, u32[]{:S(2)}) copy-start(bf16[128,2048]{1,0:T(8,128)(2,1)} %u_hbm.3) | copy-start | bytes 1572868
  27.9 18.7 %all-to-all-start = ((bf16[4,4,32,512]{3,2,1,0:T(8,128)(2,1)}), bf16[4,4,32,512]{3,2,1,0:T(8,128)(2,1)S(1)}, u32[]{:S(2)}, u32[]{:S(2)}) async-start(bf16[4,4,32,512]{3,2,1,0:T(8,128)(2,1)} %get-tuple-element.13), calls=%async_computation | async-start | bytes 1048576 | tf_op jit(solution)/shard_map/all_to_all | solution.py:342
  34.8 1.2 %copy-start.10 = (bf16[8,4,128,128]{3,2,1,0:T(8,128)(2,1)S(1)}, bf16[8,4,128,128]{3,2,1,0:T(8,128)(2,1)}, u32[]{:S(2)}) copy-start(bf16[8,4,128,128]{3,2,1,0:T(8,128)(2,1)} %all_to_all.30.far_ref) | copy-start | bytes 3145732
  66.3 16.7 %all-to-all-start.4 = ((bf16[4,4,32,512]{3,2,1,0:T(8,128)(2,1)}), bf16[4,4,32,512]{3,2,1,0:T(8,128)(2,1)S(1)}, u32[]{:S(2)}, u32[]{:S(2)}) async-start(bf16[4,4,32,512]{3,2,1,0:T(8,128)(2,1)} %get-tuple-element.21), calls=%async_computation.4 | async-start | bytes 1048576 | tf_op jit(solution)/shard_map/all_to_all | solution.py:342
  69.7 1.2 %copy-start.11 = (bf16[8,4,128,128]{3,2,1,0:T(8,128)(2,1)S(1)}, bf16[8,4,128,128]{3,2,1,0:T(8,128)(2,1)}, u32[]{:S(2)}) copy-start(bf16[8,4,128,128]{3,2,1,0:T(8,128)(2,1)} %all_to_all.30.far_ref) | copy-start | bytes 3145732
  73.8 1.0 copy-start.14
  83.0 0.8 copy-start.12
  83.8 18.9 %all-to-all-start.5 = ((bf16[8,4,128,128]{3,2,1,0:T(8,128)(2,1)}), bf16[8,4,128,128]{3,2,1,0:T(8,128)(2,1)S(1)}, u32[]{:S(2)}, u32[]{:S(2)}) async-start(bf16[8,4,128,128]{3,2,1,0:T(8,128)(2,1)} %copy-done.14), calls=%async_computation.5 | async-start | bytes 2097152 | tf_op jit(solution)/shard_map/all_to_all | solution.py:342
  92.5 1.9 %copy-start = (f32[4,16,128,128]{3,2,1,0:T(8,128)}, f32[4,16,128,128]{3,2,1,0:T(8,128)S(1)}, u32[]{:S(2)}) copy-start(f32[4,16,128,128]{3,2,1,0:T(8,128)S(1)} %near_parts.1.near_ref) | copy-start | bytes 12582916
  102.7 2.2 %copy-start.1 = (f32[4,16,128,128]{3,2,1,0:T(8,128)S(1)}, f32[4,16,128,128]{3,2,1,0:T(8,128)}, u32[]{:S(2)}) copy-start(f32[4,16,128,128]{3,2,1,0:T(8,128)} %copy-done) | copy-start | bytes 12582916
  104.9 1.0 copy-start.13

commit v4 on v2

--- a/solution.py
+++ b/solution.py
@@ -14,6 +14,7 @@
 SCALE = HEAD_DIM**-0.5
 LOWEST = -1e30
 VMEM_LIMIT = 32 * 1024 * 1024
+VMEM_ALL = 60 * 1024 * 1024
 F32, BF16 = jnp.float32, jnp.bfloat16
 SHAPE = jax.ShapeDtypeStruct
 
@@ -81,59 +82,75 @@
     return picked
 
 
+def fetch(sources, buffers, sems):
+    width = DILATION * HEAD_DIM
+    groups = []
+    for group in range(HEADS // DILATION):
+        cols = pl.ds(group * width, width)
+        groups.append(
+            [
+                pltpu.make_async_copy(
+                    source.at[:, cols], buffers.at[which, :, cols], sems.at[which, group]
+                )
+                for which, source in enumerate(sources)
+            ]
+        )
+        for copy in groups[-1]:
+            copy.start()
+    return groups
+
+
 def pick_kernel(n_i, slots, at_ref, *refs):
     sources, refs = refs[:4], refs[4:]
     mids, refs = refs[:n_i], refs[n_i:]
     fulls, refs = refs[:slots], refs[slots:]
-    kvs, refs = refs[:slots], refs[slots:]
-    wide, picked = refs
+    buffers, sems, wide, picked = refs
     rows = sources[0].shape[0]
     quarter = rows // DILATION
     pos, chip = at_ref[0], at_ref[1]
-    for which, ref in enumerate(sources):
-        for head in range(HEADS):
-            cols = static_columns(head)
-            wide[head] = ref[:, cols].astype(F32)
-            rowset = wide[head, pl.ds(head % DILATION, quarter, stride=DILATION), :]
-            picked[:, cols] = rowset.astype(BF16)
-        width = slots * HEAD_DIM
-        for d in range(n_i):
-            start = pl.multiple_of((pos ^ d) * width, width)
-            mids[d][which] = picked[:, pl.ds(start, width)]
-        for m in range(slots):
-            piece = ref[:, head_columns(pos * slots + (chip ^ m))]
-            fulls[m][which] = piece
-            if which < 2:
-                kvs[m][which] = piece
-
-
-def near_stats_kernel(k_ref, v_ref, q_ref, u_ref, stats_ref, mid_ref, turn):
-    rows = q_ref.shape[0]
+    for group, copies in enumerate(fetch(sources, buffers, sems)):
+        for which, copy in enumerate(copies):
+            copy.wait()
+            for residue in range(DILATION):
+                head = group * DILATION + residue
+                cols = static_columns(head)
+                wide[which, head] = buffers[which, :, cols].astype(F32)
+                rowset = wide[which, head, pl.ds(residue, quarter, stride=DILATION), :]
+                picked[which, :, cols] = rowset.astype(BF16)
+    width = slots * HEAD_DIM
+    for d in range(n_i):
+        start = pl.multiple_of((pos ^ d) * width, width)
+        mids[d][...] = picked[:, :, pl.ds(start, width)]
+    for m in range(slots):
+        fulls[m][...] = buffers[:, :, head_columns(pos * slots + (chip ^ m))]
+
+
+def near_stats_kernel(k_hbm, v_hbm, q_hbm, u_hbm, stats_ref, mid_ref, buffers, sems, turn):
+    rows = q_hbm.shape[0]
     turn[...] = jnp.zeros_like(turn)
-
-    def group_step(group, carry):
+    for group, copies in enumerate(fetch((k_hbm, v_hbm, q_hbm, u_hbm), buffers, sems)):
+        for copy in copies:
+            copy.wait()
         for residue in range(DILATION):
             head = group * DILATION + residue
-            cols = head_columns(head)
-            e, d = level_stats(q_ref[:, cols], k_ref[:, cols], v_ref[:, cols], u_ref[:, cols])
-            turn[pl.ds(head, 1), :] = e
-            turn[pl.ds(HEADS + head, 1), :] = d
-        return carry
-
-    lax.fori_loop(0, HEADS // DILATION, group_step, 0)
+            k, v, q, u = [buffers[which, :, static_columns(head)] for which in range(4)]
+            e, d = level_stats(q, k, v, u)
+            turn[head : head + 1, :] = e
+            turn[HEADS + head : HEADS + head + 1, :] = d
     stats_ref[...] = turn[: 2 * HEADS, :]
     turn[...] = turn[...].T
     mid_ref[...] = pick_rows(turn, rows)
 
 
-def far_stats_kernel(slots, *refs):
-    fulls, kvs, stats_ref = refs[:slots], refs[slots:-1], refs[-1]
-    keys = jnp.concatenate([ref[0] for ref in fulls + kvs], axis=0)
-    values = jnp.concatenate([ref[1] for ref in fulls + kvs], axis=0)
+def far_stats_kernel(slots, near_ref, *refs):
+    fulls, sibs, xmsg_ref = refs[:slots], refs[slots:-1], refs[-1]
+    keys = jnp.concatenate([ref[0] for ref in fulls + sibs], axis=0)
+    values = jnp.concatenate([ref[1] for ref in fulls + sibs], axis=0)
+    xmsg_ref[: 2 * slots] = near_ref[...]
     for m in range(slots):
         e, d = level_stats(fulls[m][2], keys, values, fulls[m][3])
-        stats_ref[m : m + 1, :] = e
-        stats_ref[slots + m : slots + m + 1, :] = d
+        xmsg_ref[2 * slots + m : 2 * slots + m + 1, :] = e
+        xmsg_ref[3 * slots + m : 3 * slots + m + 1, :] = d
 
 
 def middle_operands(mids, slot):
@@ -143,10 +160,10 @@
 
 def middle_stats_kernel(n_i, slots, at_ref, *refs):
     mids, refs = refs[:n_i], refs[n_i:]
-    near_ref, nearmid_ref, far_ref = refs[:3]
-    refs = refs[3:]
+    near_ref, nearmid_ref = refs[:2]
+    refs = refs[2:]
     zmsgs, refs = refs[:n_i], refs[n_i:]
-    xmsg_ref, stats_ref, turn, spread = refs
+    joint_ref, stats_ref, turn, spread = refs
     quarter = nearmid_ref.shape[0]
     pos = at_ref[0]
     turn[...] = jnp.zeros_like(turn)
@@ -175,9 +192,8 @@
         across[:slots],
         across[slots : 2 * slots],
     )
-    xmsg_ref[:slots] = e
-    xmsg_ref[slots : 2 * slots] = d
-    xmsg_ref[2 * slots :] = far_ref[...]
+    joint_ref[:slots] = e
+    joint_ref[slots:] = d
 
 
 def middle_parts_kernel(n_i, slots, at_ref, *refs):
@@ -244,20 +260,25 @@
     fulls, refs = refs[:slots], refs[slots:]
     kvs, refs = refs[:others], refs[others:]
     xmsgs, refs = refs[:slots], refs[slots:]
+    final_ref, refs = refs[0], refs[1:]
     outs, refs = refs[:slots], refs[slots:]
-    kvouts, refs = refs[:others], refs[others:]
+    kvouts, refs = refs[: width - 1], refs[width - 1 :]
     weights, score_grads = refs
     rows = fulls[0].shape[1]
-    chip = at_ref[1]
+    pos, chip = at_ref[0], at_ref[1]
+    head = pos * slots + chip
     keys = jnp.concatenate([ref[0] for ref in fulls + kvs], axis=0)
     values = jnp.concatenate([ref[1] for ref in fulls + kvs], axis=0)
     for m in range(slots):
-        lse, delta = merge_stats(
-            xmsgs[m][pl.ds(chip, 1), :],
-            xmsgs[m][pl.ds(slots + chip, 1), :],
-            xmsgs[0][2 * slots + m : 2 * slots + m + 1, :],
-            xmsgs[0][3 * slots + m : 3 * slots + m + 1, :],
-        )
+        if m == 0:
+            lse, delta = final_ref[pl.ds(head, 1), :], final_ref[pl.ds(HEADS + head, 1), :]
+        else:
+            lse, delta = merge_stats(
+                xmsgs[m][pl.ds(chip, 1), :],
+                xmsgs[m][pl.ds(slots + chip, 1), :],
+                xmsgs[0][2 * slots + m : 2 * slots + m + 1, :],
+                xmsgs[0][3 * slots + m : 3 * slots + m + 1, :],
+            )
         p, ds = level_weights(fulls[m][2], keys, values, fulls[m][3], lse, delta)
         outs[m][0] = dot_tn(p, values).astype(BF16)
         outs[m][1] = (dot_tn(ds, keys) * SCALE).astype(BF16)
@@ -267,10 +288,24 @@
     ups = jnp.concatenate([ref[3] for ref in fulls], axis=0)
     key_part = (dot(score_grads[...], queries) * SCALE).astype(BF16)
     value_part = dot(weights[...], ups).astype(BF16)
-    for index, ref in enumerate(outs + kvouts):
-        base = 2 if index < slots else 0
-        ref[base] = key_part[index * rows : (index + 1) * rows]
-        ref[base + 1] = value_part[index * rows : (index + 1) * rows]
+    for index in range(width * slots):
+        block = slice(index * rows, (index + 1) * rows)
+        part, m = index // slots, index % slots
+        if part == 0:
+            outs[m][2], outs[m][3] = key_part[block], value_part[block]
+        else:
+            kvouts[part - 1][m, 0], kvouts[part - 1][m, 1] = key_part[block], value_part[block]
+
+
+def far_sum_kernel(slots, *refs):
+    own, refs = refs[:slots], refs[slots:]
+    found, outs = refs[:-slots], refs[-slots:]
+    for m in range(slots):
+        outs[m][:2] = own[m][:2]
+        total = own[m][2:].astype(F32)
+        for ref in found:
+            total += ref[m].astype(F32)
+        outs[m][2:] = total.astype(BF16)
 
 
 def near_parts_kernel(k_ref, v_ref, q_ref, u_ref, stats_ref, out_ref):
@@ -293,11 +328,9 @@
     lax.fori_loop(0, HEADS // DILATION, group_step, 0)
 
 
-def final_kernel(n_i, slots, width, at_ref, near_ref, *refs):
-    others = (width - 1) * slots
+def final_kernel(n_i, slots, at_ref, near_ref, *refs):
     mids, refs = refs[:n_i], refs[n_i:]
-    fulls, refs = refs[:slots], refs[slots:]
-    kvs, outs = refs[:others], refs[others:]
+    fulls, outs = refs[:slots], refs[slots:]
     rows = fulls[0].shape[1]
     quarter = rows // DILATION
     pos, chip = at_ref[0], at_ref[1]
@@ -312,9 +345,6 @@
             total = near_ref[which, head] + dot(place, mids[d][which, :, cols])
             if d == 0:
                 total += fulls[m][which].astype(F32)
-                if which >= 2:
-                    for part in range(width - 1):
-                        total += kvs[part * slots + m][which - 2].astype(F32)
             out[:, head_columns(head)] = total.astype(BF16)
 
     for d in range(1, n_i):
@@ -324,19 +354,21 @@
         finish(0, chip ^ m, m)
 
 
-def call(kernel, name, outs, scratch, flops, operands, at=None):
-    specs = [pl.BlockSpec(memory_space=pltpu.VMEM)] * len(operands)
+def call(kernel, name, outs, scratch, flops, operands, at=None, in_hbm=0, limit=VMEM_LIMIT, cheap=False):
+    spaces = [pl.ANY if i < in_hbm else pltpu.VMEM for i in range(len(operands))]
     moved = sum(x.size * x.dtype.itemsize for x in tuple(operands) + tuple(outs))
+    if cheap:
+        flops, moved = 1, 1
     if at is not None:
-        specs = [pl.BlockSpec(memory_space=pltpu.SMEM)] + specs
+        spaces = [pltpu.SMEM] + spaces
         operands = (at,) + tuple(operands)
     return pl.pallas_call(
         kernel,
         out_shape=tuple(outs),
-        in_specs=specs,
+        in_specs=[pl.BlockSpec(memory_space=space) for space in spaces],
         out_specs=tuple(pl.BlockSpec(memory_space=pltpu.VMEM) for _ in outs),
         scratch_shapes=scratch,
-        compiler_params=pltpu.CompilerParams(vmem_limit_bytes=VMEM_LIMIT),
+        compiler_params=pltpu.CompilerParams(vmem_limit_bytes=limit),
         cost_estimate=pl.CostEstimate(flops=flops, bytes_accessed=moved, transcendentals=0),
         name=name,
     )(*operands)
@@ -362,7 +394,7 @@
 
     mid = SHAPE((4, quarter, slots * HEAD_DIM), BF16)
     full = SHAPE((4, rows, HEAD_DIM), BF16)
-    half = SHAPE((2, rows, HEAD_DIM), BF16)
+    half = SHAPE((slots, 2, rows, HEAD_DIM), BF16)
     square = pltpu.VMEM((LANES, rows), F32)
 
     def stats(count, lanes=rows):
@@ -374,9 +406,9 @@
     def swap_fulls(pieces):
         return [pieces[0]] + [swap(pieces[m], "seqo", n_o, m * width) for m in range(1, slots)]
 
-    def swap_halves(pieces):
+    def swap_cores(pieces):
         return [
-            swap(pieces[(part - 1) * slots + m], "seqo", n_o, m * width + part)
+            swap(pieces[m], "seqo", n_o, part)
             for part in range(1, width)
             for m in range(slots)
         ]
@@ -384,41 +416,54 @@
     pieces = call(
         bind(pick_kernel, n_i, slots),
         "pick",
-        [mid] * n_i + [full] * slots + [half] * slots,
-        [pltpu.VMEM((HEADS, rows, HEAD_DIM), F32), pltpu.VMEM((quarter, features), BF16)],
+        [mid] * n_i + [full] * slots,
+        [
+            pltpu.VMEM((4, rows, features), BF16),
+            pltpu.SemaphoreType.DMA((4, HEADS // DILATION)),
+            pltpu.VMEM((4, HEADS, rows, HEAD_DIM), F32),
+            pltpu.VMEM((4, quarter, features), BF16),
+        ],
         unit,
         sources,
         at,
+        in_hbm=4,
+        limit=VMEM_ALL,
     )
     mids = swap_mids(pieces[:n_i])
-    fulls = swap_fulls(pieces[n_i : n_i + slots])
-    kvs = swap_halves(list(pieces[n_i + slots :]) * (width - 1))
+    fulls = swap_fulls(pieces[n_i:])
+    sibs = swap_cores(fulls)
 
     near, nearmid = call(
         near_stats_kernel,
         "near_stats",
-        [stats(2 * HEADS), SHAPE((quarter, LANES), F32)],
-        [square],
+        [stats(2 * HEADS, rows), stats(quarter, LANES)],
+        [
+            pltpu.VMEM((4, rows, features), BF16),
+            pltpu.SemaphoreType.DMA((4, HEADS // DILATION)),
+            square,
+        ],
         unit * HEADS * 2,
         sources,
-    )
-    (far,) = call(
-        bind(far_stats_kernel, slots),
-        "far_stats",
-        [stats(2 * slots)],
-        [],
-        unit * n_o * slots * 2,
-        fulls + kvs,
-    )
-    *zmsgs, xmsg, middle = call(
+        in_hbm=4,
+        limit=VMEM_ALL,
+    )
+    *zmsgs, joint, middle = call(
         bind(middle_stats_kernel, n_i, slots),
         "middle_stats",
         [SHAPE((quarter, LANES), F32)] * n_i
-        + [stats(4 * slots), stats(2 * slots, n_i * quarter)],
+        + [stats(2 * slots), stats(2 * slots, n_i * quarter)],
         [pltpu.VMEM((LANES, n_i * quarter), F32), square],
         unit * slots * 2,
-        mids + [near, nearmid, far],
+        mids + [near, nearmid],
         at,
+    )
+    (xmsg,) = call(
+        bind(far_stats_kernel, slots),
+        "far_stats",
+        [stats(4 * slots)],
+        [],
+        unit * n_o * slots * 2,
+        [joint] + fulls + sibs,
     )
     zmsgs = swap_mids(zmsgs)
     xmsgs = swap_fulls([xmsg] * slots)
@@ -440,14 +485,23 @@
     farparts = call(
         bind(far_parts_kernel, slots, width),
         "far_parts",
-        [full] * slots + [half] * others,
+        [full] * slots + [half] * (width - 1),
         [pltpu.VMEM((n_o * rows, slots * rows), BF16)] * 2,
         unit * n_o * slots * 6,
-        fulls + kvs + xmsgs,
+        fulls + sibs + xmsgs + [final],
         at,
     )
-    fullparts = swap_fulls(farparts[:slots])
-    halfparts = swap_halves(farparts[slots:])
+    fullparts = call(
+        bind(far_sum_kernel, slots),
+        "far_sum",
+        [full] * slots,
+        [],
+        unit,
+        list(farparts[:slots])
+        + [swap(x, "seqo", n_o, part + 1) for part, x in enumerate(farparts[slots:])],
+        cheap=True,
+    )
+    fullparts = swap_fulls(fullparts)
 
     (nearparts,) = call(
         near_parts_kernel,
@@ -456,14 +510,15 @@
         [],
         unit * HEADS * 6,
         sources + (final,),
+        cheap=True,
     )
     return call(
-        bind(final_kernel, n_i, slots, width),
+        bind(final_kernel, n_i, slots),
         "final",
         [SHAPE((rows, features), BF16)] * 4,
         [],
         unit * HEADS,
-        [nearparts] + midparts + fullparts + halfparts,
+        [nearparts] + midparts + fullparts,
         at,
     )
 

time: 72.5 us -> 63.8 us (0.88)
  waiting for transfers between devices: 12.7 us -> 5.21 us
  Pallas kernels: 17.2 us -> 21.4 us
  local copies, waits for them, and re-layouts: 8.34 us -> 5.07 us
  starting transfers between devices: 32.9 us -> 30.3 us
    ppermute x26 -> x23, waiting for transfers between devices: 12.7 us -> 5.21 us  [swap(): return lax.ppermute(x, axis, [(i, i ^ mask) for i in range(n)])]
    pallas_call x8 -> x9, Pallas kernels: 17.2 us -> 21.4 us  [call(): pl.pallas_call(kernel, out_shape=tuple(outs), in_specs=[pl.BlockSpec(memo...]
    unnamed x24 -> x22, local copies, waits for them, and re-layouts: 8.34 us -> 5.07 us
    ppermute x26 -> x23, starting transfers between devices: 32.9 us -> 30.3 us  [swap(): return lax.ppermute(x, axis, [(i, i ^ mask) for i in range(n)])]
  transfers between devices with their start and end apart: 26 -> 23, of which waited for: 7 -> 5; matrix products, arithmetic and copies ran while one was open for 0% -> 0% of each run, Pallas kernels for 13% -> 16%
where the time goes in v4:
time: 63.8 us; the launch traced here: 63.4 us
  starting transfers between devices  30.3 us (47%)
  Pallas kernels  21.4 us (34%)
  waiting for transfers between devices  5.21 us (8%)
  local copies, waits for them, and re-layouts  5.07 us (8%)
  between operations  0.84 us (1%)
  other arithmetic  0.65 us (1%)
    ppermute x23, starting transfers between devices, swap(): return lax.ppermute(x, axis, [(i, i ^ mask) for i in range(n)])  30.3 us
    pallas_call x9, Pallas kernels, call(): pl.pallas_call(kernel, out_shape=tuple(outs), in_specs=[pl.BlockSpec(memo...  21.4 us
    ppermute x23, waiting for transfers between devices, swap(): return lax.ppermute(x, axis, [(i, i ^ mask) for i in range(n)])  5.21 us
    unnamed x22, local copies, waits for them, and re-layouts  5.07 us
  transfers between devices with their start and end apart: 23, of which 5 were waited for; matrix products, arithmetic and copies ran while one was open for 0% of the time, Pallas kernels for 16%

profile of v4, /device:TPU:0, one launch (start us, length us, event | category | flops | bytes accessed | tf_op | source)
XLA Modules:
  0.0 63.4 jit_solution(153296508186123389)
XLA Ops:
  1.3 3.5 %pick.1 = (bf16[4,32,512]{2,1,0:T(8,128)(2,1)}, bf16[4,32,512]{2,1,0:T(8,128)(2,1)}, bf16[4,32,512]{2,1,0:T(8,128)(2,1)}, bf16[4,32,512]{2,1,0:T(8,128)(2,1)}, b...) custom-call(s32[2]{0:T(128)} %pad_add_fusion.at_ref, ...), custom_call_target="tpu_custom_call" | custom-call | flops 4194304 | bytes 3145728 | tf_op jit(solution)/shard_map/pick/pallas_call | solution.py:365
  4.8 3.1 %collective-permute-start = (bf16[4,32,512]{2,1,0:T(8,128)(2,1)}, bf16[4,32,512]{2,1,0:T(8,128)(2,1)S(1)}, u32[]{:S(2)}, u32[]{:S(2)}) collective-permute-start(bf16[4,32,512]{2,1,0:T(8,128)(2,1)} %get-tuple-element.35), channel_id=1, source_target_pairs={{0,1},{1,0},{2,3},{3,2},{4,5},{5,4},{6,7},{7,6},{8,9},{9,8},{10,11... | collective-permute-start | bytes 393224 | tf_op jit(solution)/shard_map/ppermute | solution.py:378
  7.9 2.6 %collective-permute-start.1 = (bf16[4,32,512]{2,1,0:T(8,128)(2,1)}, bf16[4,32,512]{2,1,0:T(8,128)(2,1)S(1)}, u32[]{:S(2)}, u32[]{:S(2)}) collective-permute-start(bf16[4,32,512]{2,1,0:T(8,128)(2,1)} %get-tuple-element.36), channel_id=1, source_target_pairs={{0,2},{1,3},{2,0},{3,1},{4,6},{5,7},{6,4},{7,5},{8,10},{9,11},{10,... | collective-permute-start | bytes 393224 | tf_op jit(solution)/shard_map/ppermute | solution.py:378
  10.5 1.5 %collective-permute-start.6 = (bf16[4,128,128]{2,1,0:T(8,128)(2,1)}, bf16[4,128,128]{2,1,0:T(8,128)(2,1)S(1)}, u32[]{:S(2)}, u32[]{:S(2)}) collective-permute-start(bf16[4,128,128]{2,1,0:T(8,128)(2,1)} %get-tuple-element.47), channel_id=1, source_target_pairs={{0,8},{4,12},{8,0},{12,4},{16,24},{20,28},{24,16},{28,20},{1,9},{5... | collective-permute-start | bytes 393224 | tf_op jit(solution)/shard_map/ppermute | solution.py:378
  12.0 1.5 %collective-permute-start.7 = (bf16[4,128,128]{2,1,0:T(8,128)(2,1)}, bf16[4,128,128]{2,1,0:T(8,128)(2,1)S(1)}, u32[]{:S(2)}, u32[]{:S(2)}) collective-permute-start(bf16[4,128,128]{2,1,0:T(8,128)(2,1)} %get-tuple-element.48), channel_id=1, source_target_pairs={{0,16},{4,20},{8,24},{12,28},{16,0},{20,4},{24,8},{28,12},{1,17},{... | collective-permute-start | bytes 393224 | tf_op jit(solution)/shard_map/ppermute | solution.py:378
  14.0 3.0 %collective-permute-start.2 = (bf16[4,32,512]{2,1,0:T(8,128)(2,1)}, bf16[4,32,512]{2,1,0:T(8,128)(2,1)S(1)}, u32[]{:S(2)}, u32[]{:S(2)}) collective-permute-start(bf16[4,32,512]{2,1,0:T(8,128)(2,1)} %get-tuple-element.37), channel_id=1, source_target_pairs={{0,3},{1,2},{2,1},{3,0},{4,7},{5,6},{6,5},{7,4},{8,11},{9,10},{10,... | collective-permute-start | bytes 393224 | tf_op jit(solution)/shard_map/ppermute | solution.py:378
  17.5 2.5 %collective-permute-done.7.refs_2_ = bf16[4,128,128]{2,1,0:T(8,128)(2,1)S(1)} collective-permute-done((bf16[4,128,128]{2,1,0:T(8,128)(2,1)}, bf16[4,128,128]{2,1,0:T(8,128)(2,1)S(1)}, u32[]{:S(2)}, u32[]{:S(2)}) %collective-permute-start.7) | collective-permute-done | bytes 131104 | tf_op jit(solution)/shard_map/ppermute | solution.py:378
  20.5 3.4 %near_stats.1 = (f32[32,128]{1,0:T(8,128)}, f32[32,128]{1,0:T(8,128)}) custom-call(bf16[128,2048]{1,0:T(8,128)(2,1)} %k_ref.1, bf16[128,2048]{1,0:T(8,128)(2,1)} %v_ref.1, bf16[128,2048]{1,0:T(8,128)(2,1)} %q_ref.1, bf16[128,2048]{1,0:T(8,128)(2,1)} %u_ref.1), custom_call_target="tpu_custom_call" | custom-call | flops 134217728 | bytes 2129920 | tf_op jit(solution)/shard_map/near_stats/pallas_call | solution.py:365
  24.0 0.9 %copy-done.4 = bf16[4,32,512]{2,1,0:T(8,128)(2,1)S(1)} copy-done((bf16[4,32,512]{2,1,0:T(8,128)(2,1)S(1)}, bf16[4,32,512]{2,1,0:T(8,128)(2,1)}, u32[]{:S(2)}) %copy-start.4) | copy-done | bytes 131096
  24.9 0.7 %copy-done.8 = f32[32,128]{1,0:T(8,128)S(1)} copy-done((f32[32,128]{1,0:T(8,128)S(1)}, f32[32,128]{1,0:T(8,128)}, u32[]{:S(2)}) %copy-start.8) | copy-done | bytes 16408
  25.6 0.7 %copy-done.9 = f32[32,128]{1,0:T(8,128)S(1)} copy-done((f32[32,128]{1,0:T(8,128)S(1)}, f32[32,128]{1,0:T(8,128)}, u32[]{:S(2)}) %copy-start.9) | copy-done | bytes 16408
  26.3 1.1 %middle_stats.1 = (f32[32,128]{1,0:T(8,128)S(1)}, f32[32,128]{1,0:T(8,128)S(1)}, f32[32,128]{1,0:T(8,128)S(1)}, f32[32,128]{1,0:T(8,128)S(1)}, f32[8,128]{1,0:T(8,128)S(1)}, /*index=5*/f32[8,128]{1,0:T(8,128)S(1)}) custom-call(s32[2]{0:T(128)S(1)} %copy-done.10, bf16[4,32,512]{2,1,0:T(8,128)(2,1)S(1)} %copy-done.4, ...), custom_call_target="tpu_custom_call" | custom-call | flops 33554432 | bytes 630784 | tf_op jit(solution)/shard_map/middle_stats/pallas_call | solution.py:365
  27.9 1.2 %collective-permute-start.4 = (f32[32,128]{1,0:T(8,128)S(1)}, f32[32,128]{1,0:T(8,128)S(1)}, u32[]{:S(2)}, u32[]{:S(2)}) collective-permute-start(f32[32,128]{1,0:T(8,128)S(1)} %get-tuple-element.43), channel_id=1, source_target_pairs={{0,2},{1,3},{2,0},{3,1},{4,6},{5,7},{6,4},{7,5},{8,10},{9,11},{10,... | collective-permute-start | bytes 49160 | tf_op jit(solution)/shard_map/ppermute | solution.py:378
  29.1 2.7 %collective-permute-start.5 = (f32[32,128]{1,0:T(8,128)S(1)}, f32[32,128]{1,0:T(8,128)S(1)}, u32[]{:S(2)}, u32[]{:S(2)}) collective-permute-start(f32[32,128]{1,0:T(8,128)S(1)} %get-tuple-element.44), channel_id=1, source_target_pairs={{0,3},{1,2},{2,1},{3,0},{4,7},{5,6},{6,5},{7,4},{8,11},{9,10},{10,... | collective-permute-start | bytes 49160 | tf_op jit(solution)/shard_map/ppermute | solution.py:378
  31.9 0.9 %copy-done.6 = bf16[4,128,128]{2,1,0:T(8,128)(2,1)S(1)} copy-done((bf16[4,128,128]{2,1,0:T(8,128)(2,1)S(1)}, bf16[4,128,128]{2,1,0:T(8,128)(2,1)}, u32[]{:S(2)}) %copy-start.6) | copy-done | bytes 131096
  32.8 1.1 %far_stats.1.refs_10_.refs_8_ = f32[16,128]{1,0:T(8,128)S(1)} custom-call(f32[8,128]{1,0:T(8,128)S(1)} %get-tuple-element.45.near_ref, bf16[4,128,128]{2,1,0:T(8,128)(2,1)S(1)} %copy-done.6, bf16[4,128,128]{2,1,0:T(8,128)(2,1)S(1)} %collective-permute-done.6.refs_1_, bf16[4,128,128]{2,1,0:T(8,128)(2,1)S(1)} %collective-permute-done.7.refs_2_, ...), custom_call_target="tpu_custom_call" | custom-call | flops 268435456 | bytes 1060864 | tf_op jit(solution)/shard_map/far_stats/pallas_call | solution.py:365
  33.9 1.0 %collective-permute-start.15 = (f32[16,128]{1,0:T(8,128)S(1)}, f32[16,128]{1,0:T(8,128)S(1)}, u32[]{:S(2)}, u32[]{:S(2)}) collective-permute-start(f32[16,128]{1,0:T(8,128)S(1)} %far_stats.1.refs_10_.refs_8_), channel_id=1, source_target_pairs={{0,24},{4,28},{8,16},{12,20},{16,8},{20,12},{24,0},{28,4},{1,25},{... | collective-permute-start | bytes 24584 | tf_op jit(solution)/shard_map/ppermute | solution.py:378
  34.9 0.7 %collective-permute-start.14 = (f32[16,128]{1,0:T(8,128)S(1)}, f32[16,128]{1,0:T(8,128)S(1)}, u32[]{:S(2)}, u32[]{:S(2)}) collective-permute-start(f32[16,128]{1,0:T(8,128)S(1)} %far_stats.1.refs_10_.refs_8_), channel_id=1, source_target_pairs={{0,16},{4,20},{8,24},{12,28},{16,0},{20,4},{24,8},{28,12},{1,17},{... | collective-permute-start | bytes 24584 | tf_op jit(solution)/shard_map/ppermute | solution.py:378
  35.6 1.8 %collective-permute-start.13 = (f32[16,128]{1,0:T(8,128)S(1)}, f32[16,128]{1,0:T(8,128)S(1)}, u32[]{:S(2)}, u32[]{:S(2)}) collective-permute-start(f32[16,128]{1,0:T(8,128)S(1)} %far_stats.1.refs_10_.refs_8_), channel_id=1, source_target_pairs={{0,8},{4,12},{8,0},{12,4},{16,24},{20,28},{24,16},{28,20},{1,9},{5... | collective-permute-start | bytes 24584 | tf_op jit(solution)/shard_map/ppermute | solution.py:378
  37.4 1.1 %collective-permute-done.15.refs_13_.refs_11_ = f32[16,128]{1,0:T(8,128)S(1)} collective-permute-done((f32[16,128]{1,0:T(8,128)S(1)}, f32[16,128]{1,0:T(8,128)S(1)}, u32[]{:S(2)}, u32[]{:S(2)}) %collective-permute-start.15) | collective-permute-done | bytes 8224 | tf_op jit(solution)/shard_map/ppermute | solution.py:378
  39.2 0.9 %copy-done.5 = bf16[4,32,512]{2,1,0:T(8,128)(2,1)S(1)} copy-done((bf16[4,32,512]{2,1,0:T(8,128)(2,1)S(1)}, bf16[4,32,512]{2,1,0:T(8,128)(2,1)}, u32[]{:S(2)}) %copy-start.5) | copy-done | bytes 131096
  40.1 2.0 %middle_parts.1 = (bf16[4,32,512]{2,1,0:T(8,128)(2,1)S(1)}, bf16[4,32,512]{2,1,0:T(8,128)(2,1)S(1)}, bf16[4,32,512]{2,1,0:T(8,128)(2,1)S(1)}, bf16[4,32,512]{2,1,0:T(8,128)(2,1)S(1)}, f32[32,128]{1,0:T(8,128)S(1)}) custom-call(s32[2]{0:T(128)S(1)} %copy-done.10, bf16[4,32,512]{2,1,0:T(8,128)(2,1)S(1)} %copy-done.5, ...), custom_call_target="tpu_custom_call" | custom-call | flops 100663296 | bytes 1183744 | tf_op jit(solution)/shard_map/middle_parts/pallas_call | solution.py:365
  42.1 0.9 %copy-done.7 = bf16[4,128,128]{2,1,0:T(8,128)(2,1)S(1)} copy-done((bf16[4,128,128]{2,1,0:T(8,128)(2,1)S(1)}, bf16[4,128,128]{2,1,0:T(8,128)(2,1)}, u32[]{:S(2)}) %copy-start.7) | copy-done | bytes 131096
  43.0 2.8 %far_parts.1 = (bf16[4,128,128]{2,1,0:T(8,128)(2,1)S(1)}, bf16[4,128,128]{2,1,0:T(8,128)(2,1)S(1)}, bf16[4,128,128]{2,1,0:T(8,128)(2,1)S(1)}, bf16[4,128,128]{2,...) custom-call(s32[2]{0:T(128)S(1)} %copy-done.10, bf16[4,128,128]{2,1,0:T(8,128)(2,1)S(1)} %copy-done.7, ...), custom_call_target="tpu_custom_call" | custom-call | flops 805306368 | bytes 1884160 | tf_op jit(solution)/shard_map/far_parts/pallas_call | solution.py:365
  46.0 2.9 %collective-permute-start.17 = (bf16[4,32,512]{2,1,0:T(8,128)(2,1)S(1)}, bf16[4,32,512]{2,1,0:T(8,128)(2,1)S(1)}, u32[]{:S(2)}, u32[]{:S(2)}) collective-permute-start(bf16[4,32,512]{2,1,0:T(8,128)(2,1)S(1)} %get-tuple-element.53), channel_id=1, source_target_pairs={{0,2},{1,3},{2,0},{3,1},{4,6},{5,7},{6,4},{7,5},{8,10},{9,11},{10,... | collective-permute-start | bytes 393224 | tf_op jit(solution)/shard_map/ppermute | solution.py:378
  49.0 1.4 %collective-permute-start.18 = (bf16[4,32,512]{2,1,0:T(8,128)(2,1)S(1)}, bf16[4,32,512]{2,1,0:T(8,128)(2,1)S(1)}, u32[]{:S(2)}, u32[]{:S(2)}) collective-permute-start(bf16[4,32,512]{2,1,0:T(8,128)(2,1)S(1)} %get-tuple-element.54), channel_id=1, source_target_pairs={{0,3},{1,2},{2,1},{3,0},{4,7},{5,6},{6,5},{7,4},{8,11},{9,10},{10,... | collective-permute-start | bytes 393224 | tf_op jit(solution)/shard_map/ppermute | solution.py:378
  50.5 1.9 %collective-permute-start.20 = (bf16[4,128,128]{2,1,0:T(8,128)(2,1)S(1)}, bf16[4,128,128]{2,1,0:T(8,128)(2,1)S(1)}, u32[]{:S(2)}, u32[]{:S(2)}) collective-permute-start(bf16[4,128,128]{2,1,0:T(8,128)(2,1)S(1)} %get-tuple-element.61), channel_id=1, source_target_pairs={{0,8},{4,12},{8,0},{12,4},{16,24},{20,28},{24,16},{28,20},{1,9},{5... | collective-permute-start | bytes 393224 | tf_op jit(solution)/shard_map/ppermute | solution.py:378
  52.4 1.1 %collective-permute-start.21 = (bf16[4,128,128]{2,1,0:T(8,128)(2,1)S(1)}, bf16[4,128,128]{2,1,0:T(8,128)(2,1)S(1)}, u32[]{:S(2)}, u32[]{:S(2)}) collective-permute-start(bf16[4,128,128]{2,1,0:T(8,128)(2,1)S(1)} %get-tuple-element.62), channel_id=1, source_target_pairs={{0,16},{4,20},{8,24},{12,28},{16,0},{20,4},{24,8},{28,12},{1,17},{... | collective-permute-start | bytes 393224 | tf_op jit(solution)/shard_map/ppermute | solution.py:378
  53.4 0.8 %collective-permute-done.16.refs_1_ = bf16[4,32,512]{2,1,0:T(8,128)(2,1)S(1)} collective-permute-done((bf16[4,32,512]{2,1,0:T(8,128)(2,1)S(1)}, bf16[4,32,512]{2,1,0:T(8,128)(2,1)S(1)}, u32[]{:S(2)}, u32[]{:S(2)}) %collective-permute-start.16) | collective-permute-done | bytes 131104 | tf_op jit(solution)/shard_map/ppermute | solution.py:378
  54.3 1.7 %collective-permute-start.22 = (bf16[4,128,128]{2,1,0:T(8,128)(2,1)S(1)}, bf16[4,128,128]{2,1,0:T(8,128)(2,1)S(1)}, u32[]{:S(2)}, u32[]{:S(2)}) collective-permute-start(bf16[4,128,128]{2,1,0:T(8,128)(2,1)S(1)} %get-tuple-element.63), channel_id=1, source_target_pairs={{0,24},{4,28},{8,16},{12,20},{16,8},{20,12},{24,0},{28,4},{1,25},{... | collective-permute-start | bytes 393224 | tf_op jit(solution)/shard_map/ppermute | solution.py:378
  56.0 4.7 %near_parts.1.near_ref = f32[4,16,128,128]{3,2,1,0:T(8,128)S(1)} custom-call(bf16[128,2048]{1,0:T(8,128)(2,1)S(1)} %copy-done, bf16[128,2048]{1,0:T(8,128)(2,1)S(1)} %copy-done.1, bf16[128,2048]{1,0:T(8,128)(2,1)S(1)} %copy-done.2, bf16[128,2048]{1,0:T(8,128)(2,1)S(1)} %copy-done.3, f32[32,128]{1,0:T(8,128)S(1)} %get-tuple-element.50.stats_ref.refs_12_), custom_call_target="tpu_custom_call" | custom-call | flops 1 | bytes 1 | tf_op jit(solution)/shard_map/near_parts/pallas_call | solution.py:365
  60.8 2.7 %final.1 = (bf16[128,2048]{1,0:T(8,128)(2,1)}, bf16[128,2048]{1,0:T(8,128)(2,1)}, bf16[128,2048]{1,0:T(8,128)(2,1)}, bf16[128,2048]{1,0:T(8,128)(2,1)}) custom-call(s32[2]{0:T(128)S(1)} %copy-done.10, f32[4,16,128,128]{3,2,1,0:T(8,128)S(1)} %near_parts.1.near_ref, bf16[4,32,512]{2,1,0:T(8,128)(2,1)S(1)} %get-tuple-element.51.refs_0_, ...), custom_call_target="tpu_custom_call" | custom-call | flops 67108864 | bytes 7340032 | tf_op jit(solution)/shard_map/final/pallas_call | solution.py:365
  (46 shorter events, 3.7 us)
Async XLA Ops:
  1.3 22.7 %copy-start.10 = (s32[2]{0:T(128)S(1)}, s32[2]{0:T(128)}, u32[]{:S(2)}) copy-start(s32[2]{0:T(128)} %pad_add_fusion.at_ref) | copy-start | bytes 28
  4.8 51.2 %copy-start = (bf16[128,2048]{1,0:T(8,128)(2,1)S(1)}, bf16[128,2048]{1,0:T(8,128)(2,1)}, u32[]{:S(2)}) copy-start(bf16[128,2048]{1,0:T(8,128)(2,1)} %k_ref.1) | copy-start | bytes 1572868
  4.8 51.2 %copy-start.1 = (bf16[128,2048]{1,0:T(8,128)(2,1)S(1)}, bf16[128,2048]{1,0:T(8,128)(2,1)}, u32[]{:S(2)}) copy-start(bf16[128,2048]{1,0:T(8,128)(2,1)} %v_ref.1) | copy-start | bytes 1572868
  4.8 51.2 %copy-start.2 = (bf16[128,2048]{1,0:T(8,128)(2,1)S(1)}, bf16[128,2048]{1,0:T(8,128)(2,1)}, u32[]{:S(2)}) copy-start(bf16[128,2048]{1,0:T(8,128)(2,1)} %q_ref.1) | copy-start | bytes 1572868
  4.8 51.2 %copy-start.3 = (bf16[128,2048]{1,0:T(8,128)(2,1)S(1)}, bf16[128,2048]{1,0:T(8,128)(2,1)}, u32[]{:S(2)}) copy-start(bf16[128,2048]{1,0:T(8,128)(2,1)} %u_ref.1) | copy-start | bytes 1572868
  4.8 9.2 %collective-permute-start = (bf16[4,32,512]{2,1,0:T(8,128)(2,1)}, bf16[4,32,512]{2,1,0:T(8,128)(2,1)S(1)}, u32[]{:S(2)}, u32[]{:S(2)}) collective-permute-start(bf16[4,32,512]{2,1,0:T(8,128)(2,1)} %get-tuple-element.35), channel_id=1, source_target_pairs={{0,1},{1,0},{2,3},{3,2},{4,5},{5,4},{6,7},{7,6},{8,9},{9,8},{10,11... | collective-permute-start | bytes 393224 | tf_op jit(solution)/shard_map/ppermute | solution.py:378
  7.9 9.0 %collective-permute-start.1 = (bf16[4,32,512]{2,1,0:T(8,128)(2,1)}, bf16[4,32,512]{2,1,0:T(8,128)(2,1)S(1)}, u32[]{:S(2)}, u32[]{:S(2)}) collective-permute-start(bf16[4,32,512]{2,1,0:T(8,128)(2,1)} %get-tuple-element.36), channel_id=1, source_target_pairs={{0,2},{1,3},{2,0},{3,1},{4,6},{5,7},{6,4},{7,5},{8,10},{9,11},{10,... | collective-permute-start | bytes 393224 | tf_op jit(solution)/shard_map/ppermute | solution.py:378
  10.5 6.5 %collective-permute-start.6 = (bf16[4,128,128]{2,1,0:T(8,128)(2,1)}, bf16[4,128,128]{2,1,0:T(8,128)(2,1)S(1)}, u32[]{:S(2)}, u32[]{:S(2)}) collective-permute-start(bf16[4,128,128]{2,1,0:T(8,128)(2,1)} %get-tuple-element.47), channel_id=1, source_target_pairs={{0,8},{4,12},{8,0},{12,4},{16,24},{20,28},{24,16},{28,20},{1,9},{5... | collective-permute-start | bytes 393224 | tf_op jit(solution)/shard_map/ppermute | solution.py:378
  12.0 8.0 %collective-permute-start.7 = (bf16[4,128,128]{2,1,0:T(8,128)(2,1)}, bf16[4,128,128]{2,1,0:T(8,128)(2,1)S(1)}, u32[]{:S(2)}, u32[]{:S(2)}) collective-permute-start(bf16[4,128,128]{2,1,0:T(8,128)(2,1)} %get-tuple-element.48), channel_id=1, source_target_pairs={{0,16},{4,20},{8,24},{12,28},{16,0},{20,4},{24,8},{28,12},{1,17},{... | collective-permute-start | bytes 393224 | tf_op jit(solution)/shard_map/ppermute | solution.py:378
  13.5 6.5 %collective-permute-start.8 = (bf16[4,128,128]{2,1,0:T(8,128)(2,1)}, bf16[4,128,128]{2,1,0:T(8,128)(2,1)S(1)}, u32[]{:S(2)}, u32[]{:S(2)}) collective-permute-start(bf16[4,128,128]{2,1,0:T(8,128)(2,1)} %get-tuple-element.49), channel_id=1, source_target_pairs={{0,24},{4,28},{8,16},{12,20},{16,8},{20,12},{24,0},{28,4},{1,25},{... | collective-permute-start | bytes 393224 | tf_op jit(solution)/shard_map/ppermute | solution.py:378
  14.0 9.9 %collective-permute-start.2 = (bf16[4,32,512]{2,1,0:T(8,128)(2,1)}, bf16[4,32,512]{2,1,0:T(8,128)(2,1)S(1)}, u32[]{:S(2)}, u32[]{:S(2)}) collective-permute-start(bf16[4,32,512]{2,1,0:T(8,128)(2,1)} %get-tuple-element.37), channel_id=1, source_target_pairs={{0,3},{1,2},{2,1},{3,0},{4,7},{5,6},{6,5},{7,4},{8,11},{9,10},{10,... | collective-permute-start | bytes 393224 | tf_op jit(solution)/shard_map/ppermute | solution.py:378
  17.0 10.9 %collective-permute-start.9 = (bf16[4,128,128]{2,1,0:T(8,128)(2,1)}, bf16[4,128,128]{2,1,0:T(8,128)(2,1)S(1)}, u32[]{:S(2)}, u32[]{:S(2)}) collective-permute-start(bf16[4,128,128]{2,1,0:T(8,128)(2,1)} %get-tuple-element.46.refs_0_), channel_id=1, source_target_pairs={{0,4},{4,0},{8,12},{12,8},{16,20},{20,16},{24,28},{28,24},{1,5},{5... | collective-permute-start | bytes 393224 | tf_op jit(solution)/shard_map/ppermute | solution.py:378
  17.0 12.1 %collective-permute-start.10 = (bf16[4,128,128]{2,1,0:T(8,128)(2,1)S(1)}, bf16[4,128,128]{2,1,0:T(8,128)(2,1)S(1)}, u32[]{:S(2)}, u32[]{:S(2)}) collective-permute-start(bf16[4,128,128]{2,1,0:T(8,128)(2,1)S(1)} %collective-permute-done.6.refs_1_), channel_id=1, source_target_pairs={{0,4},{4,0},{8,12},{12,8},{16,20},{20,16},{24,28},{28,24},{1,5},{5... | collective-permute-start | bytes 393224 | tf_op jit(solution)/shard_map/ppermute | solution.py:378
  20.0 11.8 %collective-permute-start.11 = (bf16[4,128,128]{2,1,0:T(8,128)(2,1)S(1)}, bf16[4,128,128]{2,1,0:T(8,128)(2,1)S(1)}, u32[]{:S(2)}, u32[]{:S(2)}) collective-permute-start(bf16[4,128,128]{2,1,0:T(8,128)(2,1)S(1)} %collective-permute-done.7.refs_2_), channel_id=1, source_target_pairs={{0,4},{4,0},{8,12},{12,8},{16,20},{20,16},{24,28},{28,24},{1,5},{5... | collective-permute-start | bytes 393224 | tf_op jit(solution)/shard_map/ppermute | solution.py:378
  20.0 11.8 %collective-permute-start.12 = (bf16[4,128,128]{2,1,0:T(8,128)(2,1)S(1)}, bf16[4,128,128]{2,1,0:T(8,128)(2,1)S(1)}, u32[]{:S(2)}, u32[]{:S(2)}) collective-permute-start(bf16[4,128,128]{2,1,0:T(8,128)(2,1)S(1)} %collective-permute-done.8.refs_3_), channel_id=1, source_target_pairs={{0,4},{4,0},{8,12},{12,8},{16,20},{20,16},{24,28},{28,24},{1,5},{5... | collective-permute-start | bytes 393224 | tf_op jit(solution)/shard_map/ppermute | solution.py:378
  24.0 0.9 %copy-start.4 = (bf16[4,32,512]{2,1,0:T(8,128)(2,1)S(1)}, bf16[4,32,512]{2,1,0:T(8,128)(2,1)}, u32[]{:S(2)}) copy-start(bf16[4,32,512]{2,1,0:T(8,128)(2,1)} %get-tuple-element.34.refs_0_) | copy-start | bytes 393220
  27.4 8.2 %collective-permute-start.3 = (f32[32,128]{1,0:T(8,128)S(1)}, f32[32,128]{1,0:T(8,128)S(1)}, u32[]{:S(2)}, u32[]{:S(2)}) collective-permute-start(f32[32,128]{1,0:T(8,128)S(1)} %get-tuple-element.42), channel_id=1, source_target_pairs={{0,1},{1,0},{2,3},{3,2},{4,5},{5,4},{6,7},{7,6},{8,9},{9,8},{10,11... | collective-permute-start | bytes 49160 | tf_op jit(solution)/shard_map/ppermute | solution.py:378
  27.9 9.5 %collective-permute-start.4 = (f32[32,128]{1,0:T(8,128)S(1)}, f32[32,128]{1,0:T(8,128)S(1)}, u32[]{:S(2)}, u32[]{:S(2)}) collective-permute-start(f32[32,128]{1,0:T(8,128)S(1)} %get-tuple-element.43), channel_id=1, source_target_pairs={{0,2},{1,3},{2,0},{3,1},{4,6},{5,7},{6,4},{7,5},{8,10},{9,11},{10,... | collective-permute-start | bytes 49160 | tf_op jit(solution)/shard_map/ppermute | solution.py:378
  29.1 8.3 %collective-permute-start.5 = (f32[32,128]{1,0:T(8,128)S(1)}, f32[32,128]{1,0:T(8,128)S(1)}, u32[]{:S(2)}, u32[]{:S(2)}) collective-permute-start(f32[32,128]{1,0:T(8,128)S(1)} %get-tuple-element.44), channel_id=1, source_target_pairs={{0,3},{1,2},{2,1},{3,0},{4,7},{5,6},{6,5},{7,4},{8,11},{9,10},{10,... | collective-permute-start | bytes 49160 | tf_op jit(solution)/shard_map/ppermute | solution.py:378
  31.9 0.9 %copy-start.6 = (bf16[4,128,128]{2,1,0:T(8,128)(2,1)S(1)}, bf16[4,128,128]{2,1,0:T(8,128)(2,1)}, u32[]{:S(2)}) copy-start(bf16[4,128,128]{2,1,0:T(8,128)(2,1)} %get-tuple-element.46.refs_0_) | copy-start | bytes 393220
  33.9 4.6 %collective-permute-start.15 = (f32[16,128]{1,0:T(8,128)S(1)}, f32[16,128]{1,0:T(8,128)S(1)}, u32[]{:S(2)}, u32[]{:S(2)}) collective-permute-start(f32[16,128]{1,0:T(8,128)S(1)} %far_stats.1.refs_10_.refs_8_), channel_id=1, source_target_pairs={{0,24},{4,28},{8,16},{12,20},{16,8},{20,12},{24,0},{28,4},{1,25},{... | collective-permute-start | bytes 24584 | tf_op jit(solution)/shard_map/ppermute | solution.py:378
  34.9 3.7 %collective-permute-start.14 = (f32[16,128]{1,0:T(8,128)S(1)}, f32[16,128]{1,0:T(8,128)S(1)}, u32[]{:S(2)}, u32[]{:S(2)}) collective-permute-start(f32[16,128]{1,0:T(8,128)S(1)} %far_stats.1.refs_10_.refs_8_), channel_id=1, source_target_pairs={{0,16},{4,20},{8,24},{12,28},{16,0},{20,4},{24,8},{28,12},{1,17},{... | collective-permute-start | bytes 24584 | tf_op jit(solution)/shard_map/ppermute | solution.py:378
  35.6 3.7 %collective-permute-start.13 = (f32[16,128]{1,0:T(8,128)S(1)}, f32[16,128]{1,0:T(8,128)S(1)}, u32[]{:S(2)}, u32[]{:S(2)}) collective-permute-start(f32[16,128]{1,0:T(8,128)S(1)} %far_stats.1.refs_10_.refs_8_), channel_id=1, source_target_pairs={{0,8},{4,12},{8,0},{12,4},{16,24},{20,28},{24,16},{28,20},{1,9},{5... | collective-permute-start | bytes 24584 | tf_op jit(solution)/shard_map/ppermute | solution.py:378
  39.2 0.9 %copy-start.5 = (bf16[4,32,512]{2,1,0:T(8,128)(2,1)S(1)}, bf16[4,32,512]{2,1,0:T(8,128)(2,1)}, u32[]{:S(2)}) copy-start(bf16[4,32,512]{2,1,0:T(8,128)(2,1)} %get-tuple-element.34.refs_0_) | copy-start | bytes 393220
  42.1 0.9 %copy-start.7 = (bf16[4,128,128]{2,1,0:T(8,128)(2,1)S(1)}, bf16[4,128,128]{2,1,0:T(8,128)(2,1)}, u32[]{:S(2)}) copy-start(bf16[4,128,128]{2,1,0:T(8,128)(2,1)} %get-tuple-element.46.refs_0_) | copy-start | bytes 393220
  45.9 4.5 %collective-permute-start.19 = (bf16[4,2,128,128]{3,2,1,0:T(8,128)(2,1)S(1)}, bf16[4,2,128,128]{3,2,1,0:T(8,128)(2,1)S(1)}, u32[]{:S(2)}, u32[]{:S(2)}) collective-permute-start(bf16[4,2,128,128]{3,2,1,0:T(8,128)(2,1)S(1)} %get-tuple-element.59), channel_id=1, source_target_pairs={{0,4},{4,0},{8,12},{12,8},{16,20},{20,16},{24,28},{28,24},{1,5},{5... | collective-permute-start | bytes 786440 | tf_op jit(solution)/shard_map/ppermute | solution.py:378
  46.0 8.3 %collective-permute-start.16 = (bf16[4,32,512]{2,1,0:T(8,128)(2,1)S(1)}, bf16[4,32,512]{2,1,0:T(8,128)(2,1)S(1)}, u32[]{:S(2)}, u32[]{:S(2)}) collective-permute-start(bf16[4,32,512]{2,1,0:T(8,128)(2,1)S(1)} %get-tuple-element.52), channel_id=1, source_target_pairs={{0,1},{1,0},{2,3},{3,2},{4,5},{5,4},{6,7},{7,6},{8,9},{9,8},{10,11... | collective-permute-start | bytes 393224 | tf_op jit(solution)/shard_map/ppermute | solution.py:378
  46.0 14.7 %collective-permute-start.17 = (bf16[4,32,512]{2,1,0:T(8,128)(2,1)S(1)}, bf16[4,32,512]{2,1,0:T(8,128)(2,1)S(1)}, u32[]{:S(2)}, u32[]{:S(2)}) collective-permute-start(bf16[4,32,512]{2,1,0:T(8,128)(2,1)S(1)} %get-tuple-element.53), channel_id=1, source_target_pairs={{0,2},{1,3},{2,0},{3,1},{4,6},{5,7},{6,4},{7,5},{8,10},{9,11},{10,... | collective-permute-start | bytes 393224 | tf_op jit(solution)/shard_map/ppermute | solution.py:378
  49.0 11.8 %collective-permute-start.18 = (bf16[4,32,512]{2,1,0:T(8,128)(2,1)S(1)}, bf16[4,32,512]{2,1,0:T(8,128)(2,1)S(1)}, u32[]{:S(2)}, u32[]{:S(2)}) collective-permute-start(bf16[4,32,512]{2,1,0:T(8,128)(2,1)S(1)} %get-tuple-element.54), channel_id=1, source_target_pairs={{0,3},{1,2},{2,1},{3,0},{4,7},{5,6},{6,5},{7,4},{8,11},{9,10},{10,... | collective-permute-start | bytes 393224 | tf_op jit(solution)/shard_map/ppermute | solution.py:378
  50.5 10.3 %collective-permute-start.20 = (bf16[4,128,128]{2,1,0:T(8,128)(2,1)S(1)}, bf16[4,128,128]{2,1,0:T(8,128)(2,1)S(1)}, u32[]{:S(2)}, u32[]{:S(2)}) collective-permute-start(bf16[4,128,128]{2,1,0:T(8,128)(2,1)S(1)} %get-tuple-element.61), channel_id=1, source_target_pairs={{0,8},{4,12},{8,0},{12,4},{16,24},{20,28},{24,16},{28,20},{1,9},{5... | collective-permute-start | bytes 393224 | tf_op jit(solution)/shard_map/ppermute | solution.py:378
  52.4 8.4 %collective-permute-start.21 = (bf16[4,128,128]{2,1,0:T(8,128)(2,1)S(1)}, bf16[4,128,128]{2,1,0:T(8,128)(2,1)S(1)}, u32[]{:S(2)}, u32[]{:S(2)}) collective-permute-start(bf16[4,128,128]{2,1,0:T(8,128)(2,1)S(1)} %get-tuple-element.62), channel_id=1, source_target_pairs={{0,16},{4,20},{8,24},{12,28},{16,0},{20,4},{24,8},{28,12},{1,17},{... | collective-permute-start | bytes 393224 | tf_op jit(solution)/shard_map/ppermute | solution.py:378
  54.3 6.5 %collective-permute-start.22 = (bf16[4,128,128]{2,1,0:T(8,128)(2,1)S(1)}, bf16[4,128,128]{2,1,0:T(8,128)(2,1)S(1)}, u32[]{:S(2)}, u32[]{:S(2)}) collective-permute-start(bf16[4,128,128]{2,1,0:T(8,128)(2,1)S(1)} %get-tuple-element.63), channel_id=1, source_target_pairs={{0,24},{4,28},{8,16},{12,20},{16,8},{20,12},{24,0},{28,4},{1,25},{... | collective-permute-start | bytes 393224 | tf_op jit(solution)/shard_map/ppermute | solution.py:378
  (2 other events, 1.4 us)

commit v5 on v4

--- a/solution.py
+++ b/solution.py
@@ -14,7 +14,8 @@
 SCALE = HEAD_DIM**-0.5
 LOWEST = -1e30
 VMEM_LIMIT = 32 * 1024 * 1024
-VMEM_ALL = 60 * 1024 * 1024
+PICK_LIMIT = 53 * 1024 * 1024
+NEAR_LIMIT = 54784 * 1024
 F32, BF16 = jnp.float32, jnp.bfloat16
 SHAPE = jax.ShapeDtypeStruct
 
@@ -42,17 +43,24 @@
     return slice(index * HEAD_DIM, (index + 1) * HEAD_DIM)
 
 
+def position(slots):
+    width = lax.axis_size("seqo") // slots
+    return lax.axis_index("seqi"), lax.axis_index("seqo") // width
+
+
 def lanes_of(rows):
     return lax.broadcasted_iota(jnp.int32, (rows, LANES), 1)
 
 
-def level_stats(q, k, v, u):
-    s = dot_nt(k, q) * SCALE
-    dp = dot_nt(v, u)
-    top = jnp.max(s, axis=0, keepdims=True)
-    p = jnp.exp(s - top)
-    total = jnp.sum(p, axis=0, keepdims=True)
-    return top + jnp.log(total), jnp.sum(p * dp, axis=0, keepdims=True) / total
+def level_stats(operands):
+    products = [(dot_nt(k, q) * SCALE, dot_nt(v, u)) for k, v, q, u in operands]
+    tops = [jnp.max(s, axis=0, keepdims=True) for s, _ in products]
+    weights = [jnp.exp(s - top) for (s, _), top in zip(products, tops)]
+    totals = [jnp.sum(p, axis=0, keepdims=True) for p in weights]
+    return [
+        (top + jnp.log(total), jnp.sum(p * dp, axis=0, keepdims=True) / total)
+        for (_, dp), top, p, total in zip(products, tops, weights, totals)
+    ]
 
 
 def merge_stats(ea, da, eb, db):
@@ -62,14 +70,24 @@
     return top + jnp.log(total), (wa * da + wb * db) / total
 
 
-def level_weights(q, k, v, u, lse, delta):
-    g = jnp.exp(dot_nt(k, q) * SCALE - lse)
-    return g.astype(BF16), (g * (dot_nt(v, u) - delta)).astype(BF16)
-
-
-def level_parts(q, k, v, u, lse, delta):
-    p, ds = level_weights(q, k, v, u, lse, delta)
-    return dot_tn(p, v), dot_tn(ds, k) * SCALE, dot(ds, q) * SCALE, dot(p, u)
+def level_weights(operands, stats):
+    products = [(dot_nt(k, q) * SCALE, dot_nt(v, u)) for k, v, q, u in operands]
+    found = []
+    for (s, dp), (lse, delta) in zip(products, stats):
+        g = jnp.exp(s - lse)
+        found.append((g.astype(BF16), (g * (dp - delta)).astype(BF16)))
+    return found
+
+
+def level_parts(operands, stats):
+    found = level_weights(operands, stats)
+    keyed = [
+        (dot(ds, q) * SCALE, dot(p, u)) for (p, ds), (k, v, q, u) in zip(found, operands)
+    ]
+    queried = [
+        (dot_tn(p, v), dot_tn(ds, k) * SCALE) for (p, ds), (k, v, q, u) in zip(found, operands)
+    ]
+    return [a + b for a, b in zip(queried, keyed)]
 
 
 def pick_rows(ref, rows):
@@ -100,14 +118,14 @@
     return groups
 
 
-def pick_kernel(n_i, slots, at_ref, *refs):
+def pick_kernel(n_i, slots, *refs):
     sources, refs = refs[:4], refs[4:]
     mids, refs = refs[:n_i], refs[n_i:]
     fulls, refs = refs[:slots], refs[slots:]
     buffers, sems, wide, picked = refs
     rows = sources[0].shape[0]
     quarter = rows // DILATION
-    pos, chip = at_ref[0], at_ref[1]
+    pos, chip = position(slots)
     for group, copies in enumerate(fetch(sources, buffers, sems)):
         for which, copy in enumerate(copies):
             copy.wait()
@@ -125,16 +143,19 @@
         fulls[m][...] = buffers[:, :, head_columns(pos * slots + (chip ^ m))]
 
 
+def near_operands(ref, group):
+    heads = range(group * DILATION, (group + 1) * DILATION)
+    return [[ref[which, :, static_columns(head)] for which in range(4)] for head in heads]
+
+
 def near_stats_kernel(k_hbm, v_hbm, q_hbm, u_hbm, stats_ref, mid_ref, buffers, sems, turn):
     rows = q_hbm.shape[0]
     turn[...] = jnp.zeros_like(turn)
     for group, copies in enumerate(fetch((k_hbm, v_hbm, q_hbm, u_hbm), buffers, sems)):
         for copy in copies:
             copy.wait()
-        for residue in range(DILATION):
+        for residue, (e, d) in enumerate(level_stats(near_operands(buffers, group))):
             head = group * DILATION + residue
-            k, v, q, u = [buffers[which, :, static_columns(head)] for which in range(4)]
-            e, d = level_stats(q, k, v, u)
             turn[head : head + 1, :] = e
             turn[HEADS + head : HEADS + head + 1, :] = d
     stats_ref[...] = turn[: 2 * HEADS, :]
@@ -148,7 +169,7 @@
     values = jnp.concatenate([ref[1] for ref in fulls + sibs], axis=0)
     xmsg_ref[: 2 * slots] = near_ref[...]
     for m in range(slots):
-        e, d = level_stats(fulls[m][2], keys, values, fulls[m][3])
+        ((e, d),) = level_stats([(keys, values, fulls[m][2], fulls[m][3])])
         xmsg_ref[2 * slots + m : 2 * slots + m + 1, :] = e
         xmsg_ref[3 * slots + m : 3 * slots + m + 1, :] = d
 
@@ -158,18 +179,17 @@
     return [jnp.concatenate([ref[which, :, cols] for ref in mids], axis=0) for which in range(4)]
 
 
-def middle_stats_kernel(n_i, slots, at_ref, *refs):
-    mids, refs = refs[:n_i], refs[n_i:]
+def middle_stats_kernel(n_i, slots, *refs):
+    mids, refs = (refs[0], *refs[n_i - 1 : 0 : -1]), refs[n_i:]
     near_ref, nearmid_ref = refs[:2]
     refs = refs[2:]
     zmsgs, refs = refs[:n_i], refs[n_i:]
     joint_ref, stats_ref, turn, spread = refs
     quarter = nearmid_ref.shape[0]
-    pos = at_ref[0]
+    pos, _ = position(slots)
     turn[...] = jnp.zeros_like(turn)
-    for slot in range(slots):
-        k, v, q, u = middle_operands(mids, slot)
-        e, d = level_stats(q, k, v, u)
+    operands = [middle_operands(mids, slot) for slot in range(slots)]
+    for slot, (e, d) in enumerate(level_stats(operands)):
         turn[slot : slot + 1, :] = e
         turn[slots + slot : slots + slot + 1, :] = d
     stats_ref[...] = turn[: 2 * slots, :]
@@ -196,8 +216,8 @@
     joint_ref[slots:] = d
 
 
-def middle_parts_kernel(n_i, slots, at_ref, *refs):
-    mids, refs = refs[:n_i], refs[n_i:]
+def middle_parts_kernel(n_i, slots, *refs):
+    mids, refs = (refs[0], *refs[n_i - 1 : 0 : -1]), refs[n_i:]
     near_ref, stats_ref = refs[:2]
     refs = refs[2:]
     zmsgs, refs = refs[:n_i], refs[n_i:]
@@ -206,7 +226,7 @@
     final_ref, far, turn, spread = refs
     quarter = zmsgs[0].shape[0]
     rows = quarter * DILATION
-    pos, chip = at_ref[0], at_ref[1]
+    pos, chip = position(slots)
 
     lane = lanes_of(quarter)
     mid = jnp.zeros((quarter, LANES), F32)
@@ -241,21 +261,24 @@
     own = pick_rows(spread, rows)
     turn[...] = jnp.concatenate([own] + [ref[...] for ref in zmsgs[1:]], axis=0).T
     owned = lax.broadcasted_iota(jnp.int32, (1, n_i * quarter), 1) < quarter
-    for slot in range(slots):
-        lse, delta = merge_stats(
+    operands = [middle_operands(mids, slot) for slot in range(slots)]
+    merged = [
+        merge_stats(
             turn[pl.ds(pos * slots + slot, 1), :],
             turn[pl.ds(HEADS + pos * slots + slot, 1), :],
             jnp.where(owned, LOWEST, stats_ref[slot : slot + 1, :]),
             stats_ref[slots + slot : slots + slot + 1, :],
         )
-        k, v, q, u = middle_operands(mids, slot)
-        for which, part in enumerate(level_parts(q, k, v, u, lse, delta)):
+        for slot in range(slots)
+    ]
+    for slot, parts in enumerate(level_parts(operands, merged)):
+        for which, part in enumerate(parts):
             part = part.astype(BF16)
             for d in range(n_i):
                 outs[d][which, :, static_columns(slot)] = part[d * quarter : (d + 1) * quarter]
 
 
-def far_parts_kernel(slots, width, at_ref, *refs):
+def far_parts_kernel(slots, width, *refs):
     others = (width - 1) * slots
     fulls, refs = refs[:slots], refs[slots:]
     kvs, refs = refs[:others], refs[others:]
@@ -265,7 +288,7 @@
     kvouts, refs = refs[: width - 1], refs[width - 1 :]
     weights, score_grads = refs
     rows = fulls[0].shape[1]
-    pos, chip = at_ref[0], at_ref[1]
+    pos, chip = position(slots)
     head = pos * slots + chip
     keys = jnp.concatenate([ref[0] for ref in fulls + kvs], axis=0)
     values = jnp.concatenate([ref[1] for ref in fulls + kvs], axis=0)
@@ -279,7 +302,8 @@
                 xmsgs[0][2 * slots + m : 2 * slots + m + 1, :],
                 xmsgs[0][3 * slots + m : 3 * slots + m + 1, :],
             )
-        p, ds = level_weights(fulls[m][2], keys, values, fulls[m][3], lse, delta)
+        operands = (keys, values, fulls[m][2], fulls[m][3])
+        ((p, ds),) = level_weights([operands], [(lse, delta)])
         outs[m][0] = dot_tn(p, values).astype(BF16)
         outs[m][1] = (dot_tn(ds, keys) * SCALE).astype(BF16)
         weights[:, m * rows : (m + 1) * rows] = p
@@ -309,69 +333,79 @@
 
 
 def near_parts_kernel(k_ref, v_ref, q_ref, u_ref, stats_ref, out_ref):
-    def group_step(group, carry):
-        for residue in range(DILATION):
-            head = group * DILATION + residue
-            cols = head_columns(head)
-            parts = level_parts(
-                q_ref[:, cols],
-                k_ref[:, cols],
-                v_ref[:, cols],
-                u_ref[:, cols],
-                stats_ref[pl.ds(head, 1), :],
-                stats_ref[pl.ds(HEADS + head, 1), :],
-            )
+    for group in range(HEADS // DILATION):
+        heads = range(group * DILATION, (group + 1) * DILATION)
+        operands = [
+            [ref[:, static_columns(head)] for ref in (k_ref, v_ref, q_ref, u_ref)] for head in heads
+        ]
+        stats = [
+            (stats_ref[head : head + 1, :], stats_ref[HEADS + head : HEADS + head + 1, :])
+            for head in heads
+        ]
+        for head, parts in zip(heads, level_parts(operands, stats)):
             for which, part in enumerate(parts):
                 out_ref[which, head] = part
-        return carry
-
-    lax.fori_loop(0, HEADS // DILATION, group_step, 0)
-
-
-def final_kernel(n_i, slots, at_ref, near_ref, *refs):
-    mids, refs = refs[:n_i], refs[n_i:]
-    fulls, outs = refs[:slots], refs[slots:]
+
+
+def final_kernel(n_i, slots, near_ref, *refs):
+    mids, refs = (refs[0], *refs[n_i - 1 : 0 : -1]), refs[n_i:]
+    fulls, refs = refs[:slots], refs[slots:]
+    outs, (ready, sems) = refs[:4], refs[4:]
     rows = fulls[0].shape[1]
     quarter = rows // DILATION
-    pos, chip = at_ref[0], at_ref[1]
+    pos, chip = position(slots)
     row = lax.broadcasted_iota(jnp.int32, (rows, quarter), 0)
     taken = lax.broadcasted_iota(jnp.int32, (rows, quarter), 1) * DILATION
 
-    def finish(d, slot, m):
+    def spread(d, slot):
         head = (pos ^ d) * slots + slot
         place = jnp.where(row == taken + head % DILATION, 1.0, 0.0).astype(BF16)
         cols = head_columns(slot) if d == 0 else static_columns(slot)
+        picked = jnp.concatenate([mids[d][which, :, cols] for which in range(4)], axis=1)
+        return head, dot(place, picked)
+
+    copies = []
+    for d in reversed(range(n_i)):
+        found = [spread(d, chip ^ slot if d == 0 else slot) for slot in range(slots)]
+        for slot, (head, parts) in enumerate(found):
+            for which in range(4):
+                total = near_ref[which, head] + parts[:, static_columns(which)]
+                if d == 0:
+                    total += fulls[slot][which].astype(F32)
+                ready[which, :, head_columns(head)] = total.astype(BF16)
+        width = slots * HEAD_DIM
+        cols = pl.ds(pl.multiple_of((pos ^ d) * width, width), width)
         for which, out in enumerate(outs):
-            total = near_ref[which, head] + dot(place, mids[d][which, :, cols])
-            if d == 0:
-                total += fulls[m][which].astype(F32)
-            out[:, head_columns(head)] = total.astype(BF16)
-
-    for d in range(1, n_i):
-        for slot in range(slots):
-            finish(d, slot, None)
-    for m in range(slots):
-        finish(0, chip ^ m, m)
-
-
-def call(kernel, name, outs, scratch, flops, operands, at=None, in_hbm=0, limit=VMEM_LIMIT, cheap=False):
-    spaces = [pl.ANY if i < in_hbm else pltpu.VMEM for i in range(len(operands))]
+            copy = pltpu.make_async_copy(
+                ready.at[which, :, cols], out.at[:, cols], sems.at[which, d]
+            )
+            copy.start()
+            copies.append(copy)
+    for copy in copies:
+        copy.wait()
+
+
+def call(kernel, name, outs, scratch, flops, operands, hbm_in=(), hbm_out=False, cheap=False, limit=VMEM_LIMIT):
     moved = sum(x.size * x.dtype.itemsize for x in tuple(operands) + tuple(outs))
     if cheap:
         flops, moved = 1, 1
-    if at is not None:
-        spaces = [pltpu.SMEM] + spaces
-        operands = (at,) + tuple(operands)
+    spaces = [pltpu.HBM if i in hbm_in else pltpu.VMEM for i in range(len(operands))]
     return pl.pallas_call(
         kernel,
         out_shape=tuple(outs),
         in_specs=[pl.BlockSpec(memory_space=space) for space in spaces],
-        out_specs=tuple(pl.BlockSpec(memory_space=pltpu.VMEM) for _ in outs),
+        out_specs=tuple(
+            pl.BlockSpec(memory_space=pltpu.HBM if hbm_out else pltpu.VMEM) for _ in outs
+        ),
         scratch_shapes=scratch,
         compiler_params=pltpu.CompilerParams(vmem_limit_bytes=limit),
         cost_estimate=pl.CostEstimate(flops=flops, bytes_accessed=moved, transcendentals=0),
         name=name,
     )(*operands)
+
+
+def last_first(pieces):
+    return [pieces[0]] + pieces[:0:-1]
 
 
 def swap(x, axis, n, mask):
@@ -385,9 +419,6 @@
     width = n_o // slots
     others = (width - 1) * slots
     quarter = rows // DILATION
-    pos = lax.axis_index("seqi").astype(jnp.int32)
-    chip = lax.axis_index("seqo").astype(jnp.int32) // width
-    at = jnp.stack([pos, chip])
     sources = (key_rows, value_rows, query_rows, upstream)
     unit = 2 * rows * rows * HEAD_DIM
     bind = functools.partial
@@ -401,7 +432,8 @@
         return SHAPE((count, lanes), F32)
 
     def swap_mids(pieces):
-        return [pieces[0]] + [swap(pieces[d], "seqi", n_i, d) for d in range(1, n_i)]
+        found = {d: swap(pieces[d], "seqi", n_i, d) for d in reversed(range(1, n_i))}
+        return [pieces[0]] + [found[d] for d in range(1, n_i)]
 
     def swap_fulls(pieces):
         return [pieces[0]] + [swap(pieces[m], "seqo", n_o, m * width) for m in range(1, slots)]
@@ -413,21 +445,23 @@
             for m in range(slots)
         ]
 
+    buffers = [
+        pltpu.VMEM((4, rows, features), BF16),
+        pltpu.SemaphoreType.DMA((4, HEADS // DILATION)),
+    ]
     pieces = call(
         bind(pick_kernel, n_i, slots),
         "pick",
         [mid] * n_i + [full] * slots,
-        [
-            pltpu.VMEM((4, rows, features), BF16),
-            pltpu.SemaphoreType.DMA((4, HEADS // DILATION)),
+        buffers
+        + [
             pltpu.VMEM((4, HEADS, rows, HEAD_DIM), F32),
             pltpu.VMEM((4, quarter, features), BF16),
         ],
         unit,
         sources,
-        at,
-        in_hbm=4,
-        limit=VMEM_ALL,
+        hbm_in=range(4),
+        limit=PICK_LIMIT,
     )
     mids = swap_mids(pieces[:n_i])
     fulls = swap_fulls(pieces[n_i:])
@@ -436,16 +470,12 @@
     near, nearmid = call(
         near_stats_kernel,
         "near_stats",
-        [stats(2 * HEADS, rows), stats(quarter, LANES)],
-        [
-            pltpu.VMEM((4, rows, features), BF16),
-            pltpu.SemaphoreType.DMA((4, HEADS // DILATION)),
-            square,
-        ],
+        [stats(2 * HEADS), stats(quarter, LANES)],
+        buffers + [square],
         unit * HEADS * 2,
         sources,
-        in_hbm=4,
-        limit=VMEM_ALL,
+        hbm_in=range(4),
+        limit=NEAR_LIMIT,
     )
     *zmsgs, joint, middle = call(
         bind(middle_stats_kernel, n_i, slots),
@@ -454,8 +484,7 @@
         + [stats(2 * slots), stats(2 * slots, n_i * quarter)],
         [pltpu.VMEM((LANES, n_i * quarter), F32), square],
         unit * slots * 2,
-        mids + [near, nearmid],
-        at,
+        last_first(mids) + [near, nearmid],
     )
     (xmsg,) = call(
         bind(far_stats_kernel, slots),
@@ -478,8 +507,7 @@
             square,
         ],
         unit * slots * 6,
-        mids + [near, middle] + zmsgs + xmsgs,
-        at,
+        last_first(mids) + [near, middle] + zmsgs + xmsgs,
     )
     midparts = swap_mids(midparts)
     farparts = call(
@@ -489,7 +517,6 @@
         [pltpu.VMEM((n_o * rows, slots * rows), BF16)] * 2,
         unit * n_o * slots * 6,
         fulls + sibs + xmsgs + [final],
-        at,
     )
     fullparts = call(
         bind(far_sum_kernel, slots),
@@ -516,10 +543,10 @@
         bind(final_kernel, n_i, slots),
         "final",
         [SHAPE((rows, features), BF16)] * 4,
-        [],
+        [pltpu.VMEM((4, rows, features), BF16), pltpu.SemaphoreType.DMA((4, n_i))],
         unit * HEADS,
-        [nearparts] + midparts + fullparts,
-        at,
+        [nearparts] + last_first(midparts) + fullparts,
+        hbm_out=True,
     )
 
 

time: 63.8 us -> 55.5 us (0.87)
  Pallas kernels: 21.4 us -> 13.9 us
  local copies, waits for them, and re-layouts: 5.07 us -> 0.03 us
  waiting for transfers between devices: 5.21 us -> 9.61 us
  starting transfers between devices: 30.3 us -> 31.1 us
  other arithmetic: 0.65 us -> 0 us
    pallas_call x9, Pallas kernels: 21.4 us -> 13.9 us  [call(): pl.pallas_call(kernel, out_shape=tuple(outs), in_specs=[pl.BlockSpec(memo...]
    unnamed x22 -> x8, local copies, waits for them, and re-layouts: 5.07 us -> 0.03 us
    ppermute x23, waiting for transfers between devices: 5.21 us -> 9.61 us  [swap(): return lax.ppermute(x, axis, [(i, i ^ mask) for i in range(n)])]
    ppermute x23, starting transfers between devices: 30.3 us -> 31.1 us  [swap(): return lax.ppermute(x, axis, [(i, i ^ mask) for i in range(n)])]
    another operation x1 -> x0, other arithmetic: 0.65 us -> none  [local(): at = jnp.stack([pos, chip])]
  transfers between devices with their start and end apart: 23 -> 23, of which waited for: 5 -> 8; matrix products, arithmetic and copies ran while one was open for 0% -> 0% of each run, Pallas kernels for 16% -> 12%
where the time goes in v5:
time: 55.5 us; the launch traced here: 55.4 us
  starting transfers between devices  31.1 us (56%)
  Pallas kernels  13.9 us (25%)
  waiting for transfers between devices  9.61 us (17%)
  between operations  0.77 us (1%)
    ppermute x23, starting transfers between devices, swap(): return lax.ppermute(x, axis, [(i, i ^ mask) for i in range(n)])  31.1 us
    pallas_call x9, Pallas kernels, call(): pl.pallas_call(kernel, out_shape=tuple(outs), in_specs=[pl.BlockSpec(memo...  13.9 us
    ppermute x23, waiting for transfers between devices, swap(): return lax.ppermute(x, axis, [(i, i ^ mask) for i in range(n)])  9.61 us
  transfers between devices with their start and end apart: 23, of which 8 were waited for; matrix products, arithmetic and copies ran while one was open for 0% of the time, Pallas kernels for 12%

profile of v5, /device:TPU:0, one launch (start us, length us, event | category | flops | bytes accessed | tf_op | source)
XLA Modules:
  0.0 55.4 jit_solution(17804530991887379527)
XLA Ops:
  0.6 2.6 %pick.1 = (bf16[4,32,512]{2,1,0:T(8,128)(2,1)S(1)}, bf16[4,32,512]{2,1,0:T(8,128)(2,1)S(1)}, bf16[4,32,512]{2,1,0:T(8,128)(2,1)S(1)}, bf16[4,32,512]{2,1,0:T(8,1...) custom-call(bf16[128,2048]{1,0:T(8,128)(2,1)} %k_ref.1, ...), custom_call_target="tpu_custom_call" | custom-call | flops 4194304 | bytes 3145728 | tf_op jit(solution)/shard_map/pick/pallas_call | solution.py:393
  3.3 5.1 %collective-permute-start = (bf16[4,32,512]{2,1,0:T(8,128)(2,1)S(1)}, bf16[4,32,512]{2,1,0:T(8,128)(2,1)S(1)}, u32[]{:S(2)}, u32[]{:S(2)}) collective-permute-start(bf16[4,32,512]{2,1,0:T(8,128)(2,1)S(1)} %get-tuple-element.35), channel_id=1, source_target_pairs={{0,3},{1,2},{2,1},{3,0},{4,7},{5,6},{6,5},{7,4},{8,11},{9,10},{10,... | collective-permute-start | bytes 393224 | tf_op jit(solution)/shard_map/ppermute | solution.py:412
  8.4 1.5 %collective-permute-start.6 = (bf16[4,128,128]{2,1,0:T(8,128)(2,1)S(1)}, bf16[4,128,128]{2,1,0:T(8,128)(2,1)S(1)}, u32[]{:S(2)}, u32[]{:S(2)}) collective-permute-start(bf16[4,128,128]{2,1,0:T(8,128)(2,1)S(1)} %get-tuple-element.47), channel_id=1, source_target_pairs={{0,8},{4,12},{8,0},{12,4},{16,24},{20,28},{24,16},{28,20},{1,9},{5... | collective-permute-start | bytes 393224 | tf_op jit(solution)/shard_map/ppermute | solution.py:412
  9.9 1.5 %collective-permute-start.7 = (bf16[4,128,128]{2,1,0:T(8,128)(2,1)S(1)}, bf16[4,128,128]{2,1,0:T(8,128)(2,1)S(1)}, u32[]{:S(2)}, u32[]{:S(2)}) collective-permute-start(bf16[4,128,128]{2,1,0:T(8,128)(2,1)S(1)} %get-tuple-element.48), channel_id=1, source_target_pairs={{0,16},{4,20},{8,24},{12,28},{16,0},{20,4},{24,8},{28,12},{1,17},{... | collective-permute-start | bytes 393224 | tf_op jit(solution)/shard_map/ppermute | solution.py:412
  11.4 0.5 collective-permute-start.8
  11.9 0.9 %collective-permute-done.refs_1_ = bf16[4,32,512]{2,1,0:T(8,128)(2,1)S(1)} collective-permute-done((bf16[4,32,512]{2,1,0:T(8,128)(2,1)S(1)}, bf16[4,32,512]{2,1,0:T(8,128)(2,1)S(1)}, u32[]{:S(2)}, u32[]{:S(2)}) %collective-permute-start) | collective-permute-done | bytes 131104 | tf_op jit(solution)/shard_map/ppermute | solution.py:412
  12.8 5.4 %collective-permute-start.2 = (bf16[4,32,512]{2,1,0:T(8,128)(2,1)S(1)}, bf16[4,32,512]{2,1,0:T(8,128)(2,1)S(1)}, u32[]{:S(2)}, u32[]{:S(2)}) collective-permute-start(bf16[4,32,512]{2,1,0:T(8,128)(2,1)S(1)} %get-tuple-element.37), channel_id=1, source_target_pairs={{0,1},{1,0},{2,3},{3,2},{4,5},{5,4},{6,7},{7,6},{8,9},{9,8},{10,11... | collective-permute-start | bytes 393224 | tf_op jit(solution)/shard_map/ppermute | solution.py:412
  18.2 1.4 %collective-permute-done.1.refs_2_ = bf16[4,32,512]{2,1,0:T(8,128)(2,1)S(1)} collective-permute-done((bf16[4,32,512]{2,1,0:T(8,128)(2,1)S(1)}, bf16[4,32,512]{2,1,0:T(8,128)(2,1)S(1)}, u32[]{:S(2)}, u32[]{:S(2)}) %collective-permute-start.1) | collective-permute-done | bytes 131104 | tf_op jit(solution)/shard_map/ppermute | solution.py:412
  19.6 0.5 collective-permute-start.10
  20.6 2.8 %near_stats.1 = (f32[32,128]{1,0:T(8,128)S(1)}, f32[32,128]{1,0:T(8,128)S(1)}) custom-call(bf16[128,2048]{1,0:T(8,128)(2,1)} %k_ref.1, bf16[128,2048]{1,0:T(8,128)(2,1)} %v_ref.1, bf16[128,2048]{1,0:T(8,128)(2,1)} %q_ref.1, bf16[128,2048]{1,0:T(8,128)(2,1)} %u_ref.1), custom_call_target="tpu_custom_call" | custom-call | flops 134217728 | bytes 2129920 | tf_op jit(solution)/shard_map/near_stats/pallas_call | solution.py:393
  23.5 0.6 %middle_stats.1 = (f32[32,128]{1,0:T(8,128)S(1)}, f32[32,128]{1,0:T(8,128)S(1)}, f32[32,128]{1,0:T(8,128)S(1)}, f32[32,128]{1,0:T(8,128)S(1)}, f32[8,128]{1,0:T(8,128)S(1)}, /*index=5*/f32[8,128]{1,0:T(8,128)S(1)}) custom-call(bf16[4,32,512]{2,1,0:T(8,128)(2,1)S(1)} %get-tuple-element.34.refs_0_, bf16[4,32,512]{2,1,0:T(8,128)(2,1)S(1)} %collective-permute-done.refs_1_, ...), custom_call_target="tpu_custom_call" | custom-call | flops 33554432 | bytes 630784 | tf_op jit(solution)/shard_map/middle_stats/pallas_call | solution.py:393
  24.1 2.9 %collective-permute-start.4 = (f32[32,128]{1,0:T(8,128)S(1)}, f32[32,128]{1,0:T(8,128)S(1)}, u32[]{:S(2)}, u32[]{:S(2)}) collective-permute-start(f32[32,128]{1,0:T(8,128)S(1)} %get-tuple-element.43), channel_id=1, source_target_pairs={{0,2},{1,3},{2,0},{3,1},{4,6},{5,7},{6,4},{7,5},{8,10},{9,11},{10,... | collective-permute-start | bytes 49160 | tf_op jit(solution)/shard_map/ppermute | solution.py:412
  27.0 1.5 %collective-permute-start.5 = (f32[32,128]{1,0:T(8,128)S(1)}, f32[32,128]{1,0:T(8,128)S(1)}, u32[]{:S(2)}, u32[]{:S(2)}) collective-permute-start(f32[32,128]{1,0:T(8,128)S(1)} %get-tuple-element.44), channel_id=1, source_target_pairs={{0,3},{1,2},{2,1},{3,0},{4,7},{5,6},{6,5},{7,4},{8,11},{9,10},{10,... | collective-permute-start | bytes 49160 | tf_op jit(solution)/shard_map/ppermute | solution.py:412
  28.5 1.1 %far_stats.1.refs_10_.refs_8_ = f32[16,128]{1,0:T(8,128)S(1)} custom-call(f32[8,128]{1,0:T(8,128)S(1)} %get-tuple-element.45.near_ref, bf16[4,128,128]{2,1,0:T(8,128)(2,1)S(1)} %get-tuple-element.46.refs_0_, bf16[4,128,128]{2,1,0:T(8,128)(2,1)S(1)} %collective-permute-done.6.refs_1_, bf16[4,128,128]{2,1,0:T(8,128)(2,1)S(1)} %collective-permute-done.7.refs_2_, ...), custom_call_target="tpu_custom_call" | custom-call | flops 268435456 | bytes 1060864 | tf_op jit(solution)/shard_map/far_stats/pallas_call | solution.py:393
  29.6 2.5 %collective-permute-start.15 = (f32[16,128]{1,0:T(8,128)S(1)}, f32[16,128]{1,0:T(8,128)S(1)}, u32[]{:S(2)}, u32[]{:S(2)}) collective-permute-start(f32[16,128]{1,0:T(8,128)S(1)} %far_stats.1.refs_10_.refs_8_), channel_id=1, source_target_pairs={{0,24},{4,28},{8,16},{12,20},{16,8},{20,12},{24,0},{28,4},{1,25},{... | collective-permute-start | bytes 24584 | tf_op jit(solution)/shard_map/ppermute | solution.py:412
  32.1 0.5 collective-permute-start.14
  32.6 0.5 collective-permute-start.13
  33.2 1.1 %collective-permute-done.15.refs_13_.refs_11_ = f32[16,128]{1,0:T(8,128)S(1)} collective-permute-done((f32[16,128]{1,0:T(8,128)S(1)}, f32[16,128]{1,0:T(8,128)S(1)}, u32[]{:S(2)}, u32[]{:S(2)}) %collective-permute-start.15) | collective-permute-done | bytes 8224 | tf_op jit(solution)/shard_map/ppermute | solution.py:412
  34.2 1.5 %collective-permute-done.14.refs_12_.refs_10_ = f32[16,128]{1,0:T(8,128)S(1)} collective-permute-done((f32[16,128]{1,0:T(8,128)S(1)}, f32[16,128]{1,0:T(8,128)S(1)}, u32[]{:S(2)}, u32[]{:S(2)}) %collective-permute-start.14) | collective-permute-done | bytes 8224 | tf_op jit(solution)/shard_map/ppermute | solution.py:412
  35.7 0.5 collective-permute-done.13.refs_11_.refs_9_
  36.3 0.8 %middle_parts.1 = (bf16[4,32,512]{2,1,0:T(8,128)(2,1)S(1)}, bf16[4,32,512]{2,1,0:T(8,128)(2,1)S(1)}, bf16[4,32,512]{2,1,0:T(8,128)(2,1)S(1)}, bf16[4,32,512]{2,1,0:T(8,128)(2,1)S(1)}, f32[32,128]{1,0:T(8,128)S(1)}) custom-call(bf16[4,32,512]{2,1,0:T(8,128)(2,1)S(1)} %get-tuple-element.34.refs_0_, bf16[4,32,512]{2,1,0:T(8,128)(2,1)S(1)} %collective-permute-done.refs_1_, ...), custom_call_target="tpu_custom_call" | custom-call | flops 100663296 | bytes 1183744 | tf_op jit(solution)/shard_map/middle_parts/pallas_call | solution.py:393
  37.1 2.3 %far_parts.1 = (bf16[4,128,128]{2,1,0:T(8,128)(2,1)S(1)}, bf16[4,128,128]{2,1,0:T(8,128)(2,1)S(1)}, bf16[4,128,128]{2,1,0:T(8,128)(2,1)S(1)}, bf16[4,128,128]{2,...) custom-call(bf16[4,128,128]{2,1,0:T(8,128)(2,1)S(1)} %get-tuple-element.46.refs_0_, ...), custom_call_target="tpu_custom_call" | custom-call | flops 805306368 | bytes 1884160 | tf_op jit(solution)/shard_map/far_parts/pallas_call | solution.py:393
  39.4 2.4 %collective-permute-start.16 = (bf16[4,32,512]{2,1,0:T(8,128)(2,1)S(1)}, bf16[4,32,512]{2,1,0:T(8,128)(2,1)S(1)}, u32[]{:S(2)}, u32[]{:S(2)}) collective-permute-start(bf16[4,32,512]{2,1,0:T(8,128)(2,1)S(1)} %get-tuple-element.52), channel_id=1, source_target_pairs={{0,3},{1,2},{2,1},{3,0},{4,7},{5,6},{6,5},{7,4},{8,11},{9,10},{10,... | collective-permute-start | bytes 393224 | tf_op jit(solution)/shard_map/ppermute | solution.py:412
  41.9 2.0 %collective-permute-start.18 = (bf16[4,32,512]{2,1,0:T(8,128)(2,1)S(1)}, bf16[4,32,512]{2,1,0:T(8,128)(2,1)S(1)}, u32[]{:S(2)}, u32[]{:S(2)}) collective-permute-start(bf16[4,32,512]{2,1,0:T(8,128)(2,1)S(1)} %get-tuple-element.54), channel_id=1, source_target_pairs={{0,1},{1,0},{2,3},{3,2},{4,5},{5,4},{6,7},{7,6},{8,9},{9,8},{10,11... | collective-permute-start | bytes 393224 | tf_op jit(solution)/shard_map/ppermute | solution.py:412
  44.0 0.6 %collective-permute-start.20 = (bf16[4,128,128]{2,1,0:T(8,128)(2,1)S(1)}, bf16[4,128,128]{2,1,0:T(8,128)(2,1)S(1)}, u32[]{:S(2)}, u32[]{:S(2)}) collective-permute-start(bf16[4,128,128]{2,1,0:T(8,128)(2,1)S(1)} %get-tuple-element.61), channel_id=1, source_target_pairs={{0,8},{4,12},{8,0},{12,4},{16,24},{20,28},{24,16},{28,20},{1,9},{5... | collective-permute-start | bytes 393224 | tf_op jit(solution)/shard_map/ppermute | solution.py:412
  44.6 1.5 %collective-permute-start.21 = (bf16[4,128,128]{2,1,0:T(8,128)(2,1)S(1)}, bf16[4,128,128]{2,1,0:T(8,128)(2,1)S(1)}, u32[]{:S(2)}, u32[]{:S(2)}) collective-permute-start(bf16[4,128,128]{2,1,0:T(8,128)(2,1)S(1)} %get-tuple-element.62), channel_id=1, source_target_pairs={{0,16},{4,20},{8,24},{12,28},{16,0},{20,4},{24,8},{28,12},{1,17},{... | collective-permute-start | bytes 393224 | tf_op jit(solution)/shard_map/ppermute | solution.py:412
  46.1 1.7 %collective-permute-done.16.refs_1_ = bf16[4,32,512]{2,1,0:T(8,128)(2,1)S(1)} collective-permute-done((bf16[4,32,512]{2,1,0:T(8,128)(2,1)S(1)}, bf16[4,32,512]{2,1,0:T(8,128)(2,1)S(1)}, u32[]{:S(2)}, u32[]{:S(2)}) %collective-permute-start.16) | collective-permute-done | bytes 131104 | tf_op jit(solution)/shard_map/ppermute | solution.py:412
  47.7 1.5 %collective-permute-start.22 = (bf16[4,128,128]{2,1,0:T(8,128)(2,1)S(1)}, bf16[4,128,128]{2,1,0:T(8,128)(2,1)S(1)}, u32[]{:S(2)}, u32[]{:S(2)}) collective-permute-start(bf16[4,128,128]{2,1,0:T(8,128)(2,1)S(1)} %get-tuple-element.63), channel_id=1, source_target_pairs={{0,24},{4,28},{8,16},{12,20},{16,8},{20,12},{24,0},{28,4},{1,25},{... | collective-permute-start | bytes 393224 | tf_op jit(solution)/shard_map/ppermute | solution.py:412
  49.2 1.9 %near_parts.1.near_ref = f32[4,16,128,128]{3,2,1,0:T(8,128)S(1)} custom-call(bf16[128,2048]{1,0:T(8,128)(2,1)S(1)} %copy-done, bf16[128,2048]{1,0:T(8,128)(2,1)S(1)} %copy-done.1, bf16[128,2048]{1,0:T(8,128)(2,1)S(1)} %copy-done.2, bf16[128,2048]{1,0:T(8,128)(2,1)S(1)} %copy-done.3, f32[32,128]{1,0:T(8,128)S(1)} %get-tuple-element.50.stats_ref.refs_12_), custom_call_target="tpu_custom_call" | custom-call | flops 1 | bytes 1 | tf_op jit(solution)/shard_map/near_parts/pallas_call | solution.py:393
  51.1 1.7 %collective-permute-done.17.refs_2_ = bf16[4,32,512]{2,1,0:T(8,128)(2,1)S(1)} collective-permute-done((bf16[4,32,512]{2,1,0:T(8,128)(2,1)S(1)}, bf16[4,32,512]{2,1,0:T(8,128)(2,1)S(1)}, u32[]{:S(2)}, u32[]{:S(2)}) %collective-permute-start.17) | collective-permute-done | bytes 131104 | tf_op jit(solution)/shard_map/ppermute | solution.py:412
  52.8 0.8 %collective-permute-done.22.refs_7_ = bf16[4,128,128]{2,1,0:T(8,128)(2,1)S(1)} collective-permute-done((bf16[4,128,128]{2,1,0:T(8,128)(2,1)S(1)}, bf16[4,128,128]{2,1,0:T(8,128)(2,1)S(1)}, u32[]{:S(2)}, u32[]{:S(2)}) %collective-permute-start.22) | collective-permute-done | bytes 131104 | tf_op jit(solution)/shard_map/ppermute | solution.py:412
  53.6 1.8 %final.1 = (bf16[128,2048]{1,0:T(8,128)(2,1)}, bf16[128,2048]{1,0:T(8,128)(2,1)}, bf16[128,2048]{1,0:T(8,128)(2,1)}, bf16[128,2048]{1,0:T(8,128)(2,1)}) custom-call(f32[4,16,128,128]{3,2,1,0:T(8,128)S(1)} %near_parts.1.near_ref, bf16[4,32,512]{2,1,0:T(8,128)(2,1)S(1)} %get-tuple-element.51.refs_0_, bf16[4,32,512]{2,1,0:T(8,128)(2,1)S(1)} %collective-permute-done.16.refs_1_, ...), custom_call_target="tpu_custom_call" | custom-call | flops 67108864 | bytes 7340032 | tf_op jit(solution)/shard_map/final/pallas_call | solution.py:393
  (31 shorter events, 0.8 us)
Async XLA Ops:
  3.2 46.0 %copy-start = (bf16[128,2048]{1,0:T(8,128)(2,1)S(1)}, bf16[128,2048]{1,0:T(8,128)(2,1)}, u32[]{:S(2)}) copy-start(bf16[128,2048]{1,0:T(8,128)(2,1)} %k_ref.1) | copy-start | bytes 1572868
  3.3 46.0 %copy-start.1 = (bf16[128,2048]{1,0:T(8,128)(2,1)S(1)}, bf16[128,2048]{1,0:T(8,128)(2,1)}, u32[]{:S(2)}) copy-start(bf16[128,2048]{1,0:T(8,128)(2,1)} %v_ref.1) | copy-start | bytes 1572868
  3.3 46.0 %copy-start.2 = (bf16[128,2048]{1,0:T(8,128)(2,1)S(1)}, bf16[128,2048]{1,0:T(8,128)(2,1)}, u32[]{:S(2)}) copy-start(bf16[128,2048]{1,0:T(8,128)(2,1)} %q_ref.1) | copy-start | bytes 1572868
  3.3 46.0 %copy-start.3 = (bf16[128,2048]{1,0:T(8,128)(2,1)S(1)}, bf16[128,2048]{1,0:T(8,128)(2,1)}, u32[]{:S(2)}) copy-start(bf16[128,2048]{1,0:T(8,128)(2,1)} %u_ref.1) | copy-start | bytes 1572868
  3.3 9.5 %collective-permute-start = (bf16[4,32,512]{2,1,0:T(8,128)(2,1)S(1)}, bf16[4,32,512]{2,1,0:T(8,128)(2,1)S(1)}, u32[]{:S(2)}, u32[]{:S(2)}) collective-permute-start(bf16[4,32,512]{2,1,0:T(8,128)(2,1)S(1)} %get-tuple-element.35), channel_id=1, source_target_pairs={{0,3},{1,2},{2,1},{3,0},{4,7},{5,6},{6,5},{7,4},{8,11},{9,10},{10,... | collective-permute-start | bytes 393224 | tf_op jit(solution)/shard_map/ppermute | solution.py:412
  8.4 11.2 %collective-permute-start.1 = (bf16[4,32,512]{2,1,0:T(8,128)(2,1)S(1)}, bf16[4,32,512]{2,1,0:T(8,128)(2,1)S(1)}, u32[]{:S(2)}, u32[]{:S(2)}) collective-permute-start(bf16[4,32,512]{2,1,0:T(8,128)(2,1)S(1)} %get-tuple-element.36), channel_id=1, source_target_pairs={{0,2},{1,3},{2,0},{3,1},{4,6},{5,7},{6,4},{7,5},{8,10},{9,11},{10,... | collective-permute-start | bytes 393224 | tf_op jit(solution)/shard_map/ppermute | solution.py:412
  8.4 11.2 %collective-permute-start.6 = (bf16[4,128,128]{2,1,0:T(8,128)(2,1)S(1)}, bf16[4,128,128]{2,1,0:T(8,128)(2,1)S(1)}, u32[]{:S(2)}, u32[]{:S(2)}) collective-permute-start(bf16[4,128,128]{2,1,0:T(8,128)(2,1)S(1)} %get-tuple-element.47), channel_id=1, source_target_pairs={{0,8},{4,12},{8,0},{12,4},{16,24},{20,28},{24,16},{28,20},{1,9},{5... | collective-permute-start | bytes 393224 | tf_op jit(solution)/shard_map/ppermute | solution.py:412
  9.9 10.2 %collective-permute-start.7 = (bf16[4,128,128]{2,1,0:T(8,128)(2,1)S(1)}, bf16[4,128,128]{2,1,0:T(8,128)(2,1)S(1)}, u32[]{:S(2)}, u32[]{:S(2)}) collective-permute-start(bf16[4,128,128]{2,1,0:T(8,128)(2,1)S(1)} %get-tuple-element.48), channel_id=1, source_target_pairs={{0,16},{4,20},{8,24},{12,28},{16,0},{20,4},{24,8},{28,12},{1,17},{... | collective-permute-start | bytes 393224 | tf_op jit(solution)/shard_map/ppermute | solution.py:412
  11.4 8.8 %collective-permute-start.8 = (bf16[4,128,128]{2,1,0:T(8,128)(2,1)}, bf16[4,128,128]{2,1,0:T(8,128)(2,1)S(1)}, u32[]{:S(2)}, u32[]{:S(2)}) collective-permute-start(bf16[4,128,128]{2,1,0:T(8,128)(2,1)} %get-tuple-element.49), channel_id=1, source_target_pairs={{0,24},{4,28},{8,16},{12,20},{16,8},{20,12},{24,0},{28,4},{1,25},{... | collective-permute-start | bytes 393224 | tf_op jit(solution)/shard_map/ppermute | solution.py:412
  12.8 10.6 %collective-permute-start.2 = (bf16[4,32,512]{2,1,0:T(8,128)(2,1)S(1)}, bf16[4,32,512]{2,1,0:T(8,128)(2,1)S(1)}, u32[]{:S(2)}, u32[]{:S(2)}) collective-permute-start(bf16[4,32,512]{2,1,0:T(8,128)(2,1)S(1)} %get-tuple-element.37), channel_id=1, source_target_pairs={{0,1},{1,0},{2,3},{3,2},{4,5},{5,4},{6,7},{7,6},{8,9},{9,8},{10,11... | collective-permute-start | bytes 393224 | tf_op jit(solution)/shard_map/ppermute | solution.py:412
  19.6 4.5 %collective-permute-start.9 = (bf16[4,128,128]{2,1,0:T(8,128)(2,1)S(1)}, bf16[4,128,128]{2,1,0:T(8,128)(2,1)S(1)}, u32[]{:S(2)}, u32[]{:S(2)}) collective-permute-start(bf16[4,128,128]{2,1,0:T(8,128)(2,1)S(1)} %get-tuple-element.46.refs_0_), channel_id=1, source_target_pairs={{0,4},{4,0},{8,12},{12,8},{16,20},{20,16},{24,28},{28,24},{1,5},{5... | collective-permute-start | bytes 393224 | tf_op jit(solution)/shard_map/ppermute | solution.py:412
  19.6 7.4 %collective-permute-start.10 = (bf16[4,128,128]{2,1,0:T(8,128)(2,1)S(1)}, bf16[4,128,128]{2,1,0:T(8,128)(2,1)S(1)}, u32[]{:S(2)}, u32[]{:S(2)}) collective-permute-start(bf16[4,128,128]{2,1,0:T(8,128)(2,1)S(1)} %collective-permute-done.6.refs_1_), channel_id=1, source_target_pairs={{0,4},{4,0},{8,12},{12,8},{16,20},{20,16},{24,28},{28,24},{1,5},{5... | collective-permute-start | bytes 393224 | tf_op jit(solution)/shard_map/ppermute | solution.py:412
  20.1 8.4 %collective-permute-start.11 = (bf16[4,128,128]{2,1,0:T(8,128)(2,1)S(1)}, bf16[4,128,128]{2,1,0:T(8,128)(2,1)S(1)}, u32[]{:S(2)}, u32[]{:S(2)}) collective-permute-start(bf16[4,128,128]{2,1,0:T(8,128)(2,1)S(1)} %collective-permute-done.7.refs_2_), channel_id=1, source_target_pairs={{0,4},{4,0},{8,12},{12,8},{16,20},{20,16},{24,28},{28,24},{1,5},{5... | collective-permute-start | bytes 393224 | tf_op jit(solution)/shard_map/ppermute | solution.py:412
  20.2 8.3 %collective-permute-start.12 = (bf16[4,128,128]{2,1,0:T(8,128)(2,1)S(1)}, bf16[4,128,128]{2,1,0:T(8,128)(2,1)S(1)}, u32[]{:S(2)}, u32[]{:S(2)}) collective-permute-start(bf16[4,128,128]{2,1,0:T(8,128)(2,1)S(1)} %collective-permute-done.8.refs_3_), channel_id=1, source_target_pairs={{0,4},{4,0},{8,12},{12,8},{16,20},{20,16},{24,28},{28,24},{1,5},{5... | collective-permute-start | bytes 393224 | tf_op jit(solution)/shard_map/ppermute | solution.py:412
  24.0 8.6 %collective-permute-start.3 = (f32[32,128]{1,0:T(8,128)S(1)}, f32[32,128]{1,0:T(8,128)S(1)}, u32[]{:S(2)}, u32[]{:S(2)}) collective-permute-start(f32[32,128]{1,0:T(8,128)S(1)} %get-tuple-element.42), channel_id=1, source_target_pairs={{0,1},{1,0},{2,3},{3,2},{4,5},{5,4},{6,7},{7,6},{8,9},{9,8},{10,11... | collective-permute-start | bytes 49160 | tf_op jit(solution)/shard_map/ppermute | solution.py:412
  24.1 9.1 %collective-permute-start.4 = (f32[32,128]{1,0:T(8,128)S(1)}, f32[32,128]{1,0:T(8,128)S(1)}, u32[]{:S(2)}, u32[]{:S(2)}) collective-permute-start(f32[32,128]{1,0:T(8,128)S(1)} %get-tuple-element.43), channel_id=1, source_target_pairs={{0,2},{1,3},{2,0},{3,1},{4,6},{5,7},{6,4},{7,5},{8,10},{9,11},{10,... | collective-permute-start | bytes 49160 | tf_op jit(solution)/shard_map/ppermute | solution.py:412
  27.0 6.1 %collective-permute-start.5 = (f32[32,128]{1,0:T(8,128)S(1)}, f32[32,128]{1,0:T(8,128)S(1)}, u32[]{:S(2)}, u32[]{:S(2)}) collective-permute-start(f32[32,128]{1,0:T(8,128)S(1)} %get-tuple-element.44), channel_id=1, source_target_pairs={{0,3},{1,2},{2,1},{3,0},{4,7},{5,6},{6,5},{7,4},{8,11},{9,10},{10,... | collective-permute-start | bytes 49160 | tf_op jit(solution)/shard_map/ppermute | solution.py:412
  29.6 4.6 %collective-permute-start.15 = (f32[16,128]{1,0:T(8,128)S(1)}, f32[16,128]{1,0:T(8,128)S(1)}, u32[]{:S(2)}, u32[]{:S(2)}) collective-permute-start(f32[16,128]{1,0:T(8,128)S(1)} %far_stats.1.refs_10_.refs_8_), channel_id=1, source_target_pairs={{0,24},{4,28},{8,16},{12,20},{16,8},{20,12},{24,0},{28,4},{1,25},{... | collective-permute-start | bytes 24584 | tf_op jit(solution)/shard_map/ppermute | solution.py:412
  32.1 3.7 %collective-permute-start.14 = (f32[16,128]{1,0:T(8,128)S(1)}, f32[16,128]{1,0:T(8,128)S(1)}, u32[]{:S(2)}, u32[]{:S(2)}) collective-permute-start(f32[16,128]{1,0:T(8,128)S(1)} %far_stats.1.refs_10_.refs_8_), channel_id=1, source_target_pairs={{0,16},{4,20},{8,24},{12,28},{16,0},{20,4},{24,8},{28,12},{1,17},{... | collective-permute-start | bytes 24584 | tf_op jit(solution)/shard_map/ppermute | solution.py:412
  32.6 3.7 %collective-permute-start.13 = (f32[16,128]{1,0:T(8,128)S(1)}, f32[16,128]{1,0:T(8,128)S(1)}, u32[]{:S(2)}, u32[]{:S(2)}) collective-permute-start(f32[16,128]{1,0:T(8,128)S(1)} %far_stats.1.refs_10_.refs_8_), channel_id=1, source_target_pairs={{0,8},{4,12},{8,0},{12,4},{16,24},{20,28},{24,16},{28,20},{1,9},{5... | collective-permute-start | bytes 24584 | tf_op jit(solution)/shard_map/ppermute | solution.py:412
  39.4 4.5 %collective-permute-start.19 = (bf16[4,2,128,128]{3,2,1,0:T(8,128)(2,1)S(1)}, bf16[4,2,128,128]{3,2,1,0:T(8,128)(2,1)S(1)}, u32[]{:S(2)}, u32[]{:S(2)}) collective-permute-start(bf16[4,2,128,128]{3,2,1,0:T(8,128)(2,1)S(1)} %get-tuple-element.59), channel_id=1, source_target_pairs={{0,4},{4,0},{8,12},{12,8},{16,20},{20,16},{24,28},{28,24},{1,5},{5... | collective-permute-start | bytes 786440 | tf_op jit(solution)/shard_map/ppermute | solution.py:412
  39.4 8.3 %collective-permute-start.16 = (bf16[4,32,512]{2,1,0:T(8,128)(2,1)S(1)}, bf16[4,32,512]{2,1,0:T(8,128)(2,1)S(1)}, u32[]{:S(2)}, u32[]{:S(2)}) collective-permute-start(bf16[4,32,512]{2,1,0:T(8,128)(2,1)S(1)} %get-tuple-element.52), channel_id=1, source_target_pairs={{0,3},{1,2},{2,1},{3,0},{4,7},{5,6},{6,5},{7,4},{8,11},{9,10},{10,... | collective-permute-start | bytes 393224 | tf_op jit(solution)/shard_map/ppermute | solution.py:412
  41.9 10.9 %collective-permute-start.17 = (bf16[4,32,512]{2,1,0:T(8,128)(2,1)S(1)}, bf16[4,32,512]{2,1,0:T(8,128)(2,1)S(1)}, u32[]{:S(2)}, u32[]{:S(2)}) collective-permute-start(bf16[4,32,512]{2,1,0:T(8,128)(2,1)S(1)} %get-tuple-element.53), channel_id=1, source_target_pairs={{0,2},{1,3},{2,0},{3,1},{4,6},{5,7},{6,4},{7,5},{8,10},{9,11},{10,... | collective-permute-start | bytes 393224 | tf_op jit(solution)/shard_map/ppermute | solution.py:412
  41.9 10.9 %collective-permute-start.18 = (bf16[4,32,512]{2,1,0:T(8,128)(2,1)S(1)}, bf16[4,32,512]{2,1,0:T(8,128)(2,1)S(1)}, u32[]{:S(2)}, u32[]{:S(2)}) collective-permute-start(bf16[4,32,512]{2,1,0:T(8,128)(2,1)S(1)} %get-tuple-element.54), channel_id=1, source_target_pairs={{0,1},{1,0},{2,3},{3,2},{4,5},{5,4},{6,7},{7,6},{8,9},{9,8},{10,11... | collective-permute-start | bytes 393224 | tf_op jit(solution)/shard_map/ppermute | solution.py:412
  44.0 8.9 %collective-permute-start.20 = (bf16[4,128,128]{2,1,0:T(8,128)(2,1)S(1)}, bf16[4,128,128]{2,1,0:T(8,128)(2,1)S(1)}, u32[]{:S(2)}, u32[]{:S(2)}) collective-permute-start(bf16[4,128,128]{2,1,0:T(8,128)(2,1)S(1)} %get-tuple-element.61), channel_id=1, source_target_pairs={{0,8},{4,12},{8,0},{12,4},{16,24},{20,28},{24,16},{28,20},{1,9},{5... | collective-permute-start | bytes 393224 | tf_op jit(solution)/shard_map/ppermute | solution.py:412
  44.6 8.3 %collective-permute-start.21 = (bf16[4,128,128]{2,1,0:T(8,128)(2,1)S(1)}, bf16[4,128,128]{2,1,0:T(8,128)(2,1)S(1)}, u32[]{:S(2)}, u32[]{:S(2)}) collective-permute-start(bf16[4,128,128]{2,1,0:T(8,128)(2,1)S(1)} %get-tuple-element.62), channel_id=1, source_target_pairs={{0,16},{4,20},{8,24},{12,28},{16,0},{20,4},{24,8},{28,12},{1,17},{... | collective-permute-start | bytes 393224 | tf_op jit(solution)/shard_map/ppermute | solution.py:412
  47.7 5.9 %collective-permute-start.22 = (bf16[4,128,128]{2,1,0:T(8,128)(2,1)S(1)}, bf16[4,128,128]{2,1,0:T(8,128)(2,1)S(1)}, u32[]{:S(2)}, u32[]{:S(2)}) collective-permute-start(bf16[4,128,128]{2,1,0:T(8,128)(2,1)S(1)} %get-tuple-element.63), channel_id=1, source_target_pairs={{0,24},{4,28},{8,16},{12,20},{16,8},{20,12},{24,0},{28,4},{1,25},{... | collective-permute-start | bytes 393224 | tf_op jit(solution)/shard_map/ppermute | solution.py:412

commit v6 on v5

--- a/solution.py
+++ b/solution.py
@@ -163,10 +163,20 @@
     mid_ref[...] = pick_rows(turn, rows)
 
 
+def pack_kernel(slots, *refs):
+    packed_ref = refs[-1]
+    for m, ref in enumerate(refs[:slots]):
+        packed_ref[m] = ref[:2]
+
+
+def far_keys(fulls, sibs, which):
+    blocks = [ref[which] for ref in fulls]
+    return jnp.concatenate(blocks + [ref[m, which] for ref in sibs for m in range(len(fulls))], axis=0)
+
+
 def far_stats_kernel(slots, near_ref, *refs):
     fulls, sibs, xmsg_ref = refs[:slots], refs[slots:-1], refs[-1]
-    keys = jnp.concatenate([ref[0] for ref in fulls + sibs], axis=0)
-    values = jnp.concatenate([ref[1] for ref in fulls + sibs], axis=0)
+    keys, values = far_keys(fulls, sibs, 0), far_keys(fulls, sibs, 1)
     xmsg_ref[: 2 * slots] = near_ref[...]
     for m in range(slots):
         ((e, d),) = level_stats([(keys, values, fulls[m][2], fulls[m][3])])
@@ -180,7 +190,7 @@
 
 
 def middle_stats_kernel(n_i, slots, *refs):
-    mids, refs = (refs[0], *refs[n_i - 1 : 0 : -1]), refs[n_i:]
+    mids, refs = in_order(refs[:n_i]), refs[n_i:]
     near_ref, nearmid_ref = refs[:2]
     refs = refs[2:]
     zmsgs, refs = refs[:n_i], refs[n_i:]
@@ -217,7 +227,7 @@
 
 
 def middle_parts_kernel(n_i, slots, *refs):
-    mids, refs = (refs[0], *refs[n_i - 1 : 0 : -1]), refs[n_i:]
+    mids, refs = in_order(refs[:n_i]), refs[n_i:]
     near_ref, stats_ref = refs[:2]
     refs = refs[2:]
     zmsgs, refs = refs[:n_i], refs[n_i:]
@@ -279,9 +289,8 @@
 
 
 def far_parts_kernel(slots, width, *refs):
-    others = (width - 1) * slots
     fulls, refs = refs[:slots], refs[slots:]
-    kvs, refs = refs[:others], refs[others:]
+    sibs, refs = refs[: width - 1], refs[width - 1 :]
     xmsgs, refs = refs[:slots], refs[slots:]
     final_ref, refs = refs[0], refs[1:]
     outs, refs = refs[:slots], refs[slots:]
@@ -290,8 +299,7 @@
     rows = fulls[0].shape[1]
     pos, chip = position(slots)
     head = pos * slots + chip
-    keys = jnp.concatenate([ref[0] for ref in fulls + kvs], axis=0)
-    values = jnp.concatenate([ref[1] for ref in fulls + kvs], axis=0)
+    keys, values = far_keys(fulls, sibs, 0), far_keys(fulls, sibs, 1)
     for m in range(slots):
         if m == 0:
             lse, delta = final_ref[pl.ds(head, 1), :], final_ref[pl.ds(HEADS + head, 1), :]
@@ -348,7 +356,7 @@
 
 
 def final_kernel(n_i, slots, near_ref, *refs):
-    mids, refs = (refs[0], *refs[n_i - 1 : 0 : -1]), refs[n_i:]
+    mids, refs = in_order(refs[:n_i]), refs[n_i:]
     fulls, refs = refs[:slots], refs[slots:]
     outs, (ready, sems) = refs[:4], refs[4:]
     rows = fulls[0].shape[1]
@@ -404,8 +412,12 @@
     )(*operands)
 
 
-def last_first(pieces):
-    return [pieces[0]] + pieces[:0:-1]
+def far_first(pieces):
+    return [*pieces[:2], *pieces[:1:-1]]
+
+
+def in_order(pieces):
+    return [*pieces[:2], *pieces[:1:-1]]
 
 
 def swap(x, axis, n, mask):
@@ -437,13 +449,6 @@
 
     def swap_fulls(pieces):
         return [pieces[0]] + [swap(pieces[m], "seqo", n_o, m * width) for m in range(1, slots)]
-
-    def swap_cores(pieces):
-        return [
-            swap(pieces[m], "seqo", n_o, part)
-            for part in range(1, width)
-            for m in range(slots)
-        ]
 
     buffers = [
         pltpu.VMEM((4, rows, features), BF16),
@@ -465,7 +470,6 @@
     )
     mids = swap_mids(pieces[:n_i])
     fulls = swap_fulls(pieces[n_i:])
-    sibs = swap_cores(fulls)
 
     near, nearmid = call(
         near_stats_kernel,
@@ -477,6 +481,8 @@
         hbm_in=range(4),
         limit=NEAR_LIMIT,
     )
+    (packed,) = call(bind(pack_kernel, slots), "pack", [half], [], unit, fulls + mids[1:] + [near])
+    sibs = [swap(packed, "seqo", n_o, part) for part in range(1, width)]
     *zmsgs, joint, middle = call(
         bind(middle_stats_kernel, n_i, slots),
         "middle_stats",
@@ -484,7 +490,7 @@
         + [stats(2 * slots), stats(2 * slots, n_i * quarter)],
         [pltpu.VMEM((LANES, n_i * quarter), F32), square],
         unit * slots * 2,
-        last_first(mids) + [near, nearmid],
+        far_first(mids) + [near, nearmid],
     )
     (xmsg,) = call(
         bind(far_stats_kernel, slots),
@@ -507,7 +513,7 @@
             square,
         ],
         unit * slots * 6,
-        last_first(mids) + [near, middle] + zmsgs + xmsgs,
+        far_first(mids) + [near, middle] + zmsgs + xmsgs,
     )
     midparts = swap_mids(midparts)
     farparts = call(
@@ -545,7 +551,7 @@
         [SHAPE((rows, features), BF16)] * 4,
         [pltpu.VMEM((4, rows, features), BF16), pltpu.SemaphoreType.DMA((4, n_i))],
         unit * HEADS,
-        [nearparts] + last_first(midparts) + fullparts,
+        [nearparts] + far_first(midparts) + fullparts,
         hbm_out=True,
     )
 

time: 55.5 us -> 54.1 us (0.975)
  starting transfers between devices: 31.1 us -> 24.5 us
  waiting for transfers between devices: 9.61 us -> 14.7 us
    ppermute x23 -> x20, starting transfers between devices: 31.1 us -> 24.5 us  [swap(): return lax.ppermute(x, axis, [(i, i ^ mask) for i in range(n)])]
    ppermute x23 -> x20, waiting for transfers between devices: 9.61 us -> 14.7 us  [swap(): return lax.ppermute(x, axis, [(i, i ^ mask) for i in range(n)])]
    pallas_call x9 -> x10, Pallas kernels: 13.9 us -> 14 us  [call(): pl.pallas_call(kernel, out_shape=tuple(outs), in_specs=[pl.BlockSpec(memo...]
  transfers between devices with their start and end apart: 23 -> 20, of which waited for: 8 -> 8; matrix products, arithmetic and copies ran while one was open for 0% -> 0% of each run, Pallas kernels for 12% -> 12%
where the time goes in v6:
time: 54.1 us; the launch traced here: 54 us
  starting transfers between devices  24.5 us (45%)
  waiting for transfers between devices  14.7 us (27%)
  Pallas kernels  14 us (26%)
  between operations  0.76 us (1%)
    ppermute x20, starting transfers between devices, swap(): return lax.ppermute(x, axis, [(i, i ^ mask) for i in range(n)])  24.5 us
    ppermute x20, waiting for transfers between devices, swap(): return lax.ppermute(x, axis, [(i, i ^ mask) for i in range(n)])  14.7 us
    pallas_call x10, Pallas kernels, call(): pl.pallas_call(kernel, out_shape=tuple(outs), in_specs=[pl.BlockSpec(memo...  14 us
  transfers between devices with their start and end apart: 20, of which 8 were waited for; matrix products, arithmetic and copies ran while one was open for 0% of the time, Pallas kernels for 12%

profile of v6, /device:TPU:0, one launch (start us, length us, event | category | flops | bytes accessed | tf_op | source)
XLA Modules:
  0.0 54.0 jit_solution(11377084667943415448)
XLA Ops:
  0.6 2.6 %pick.1 = (bf16[4,32,512]{2,1,0:T(8,128)(2,1)S(1)}, bf16[4,32,512]{2,1,0:T(8,128)(2,1)S(1)}, bf16[4,32,512]{2,1,0:T(8,128)(2,1)S(1)}, bf16[4,32,512]{2,1,0:T(8,1...) custom-call(bf16[128,2048]{1,0:T(8,128)(2,1)} %k_ref.1, ...), custom_call_target="tpu_custom_call" | custom-call | flops 4194304 | bytes 3145728 | tf_op jit(solution)/shard_map/pick/pallas_call | solution.py:401
  3.2 3.1 %collective-permute-start = (bf16[4,32,512]{2,1,0:T(8,128)(2,1)S(1)}, bf16[4,32,512]{2,1,0:T(8,128)(2,1)S(1)}, u32[]{:S(2)}, u32[]{:S(2)}) collective-permute-start(bf16[4,32,512]{2,1,0:T(8,128)(2,1)S(1)} %get-tuple-element.35), channel_id=1, source_target_pairs={{0,1},{1,0},{2,3},{3,2},{4,5},{5,4},{6,7},{7,6},{8,9},{9,8},{10,11... | collective-permute-start | bytes 393224 | tf_op jit(solution)/shard_map/ppermute | solution.py:424
  6.3 2.5 %collective-permute-start.1 = (bf16[4,32,512]{2,1,0:T(8,128)(2,1)S(1)}, bf16[4,32,512]{2,1,0:T(8,128)(2,1)S(1)}, u32[]{:S(2)}, u32[]{:S(2)}) collective-permute-start(bf16[4,32,512]{2,1,0:T(8,128)(2,1)S(1)} %get-tuple-element.36), channel_id=1, source_target_pairs={{0,3},{1,2},{2,1},{3,0},{4,7},{5,6},{6,5},{7,4},{8,11},{9,10},{10,... | collective-permute-start | bytes 393224 | tf_op jit(solution)/shard_map/ppermute | solution.py:424
  8.8 0.1 collective-permute-start.2
  8.9 1.5 %collective-permute-start.6 = (bf16[4,128,128]{2,1,0:T(8,128)(2,1)S(1)}, bf16[4,128,128]{2,1,0:T(8,128)(2,1)S(1)}, u32[]{:S(2)}, u32[]{:S(2)}) collective-permute-start(bf16[4,128,128]{2,1,0:T(8,128)(2,1)S(1)} %get-tuple-element.47), channel_id=1, source_target_pairs={{0,8},{4,12},{8,0},{12,4},{16,24},{20,28},{24,16},{28,20},{1,9},{5... | collective-permute-start | bytes 393224 | tf_op jit(solution)/shard_map/ppermute | solution.py:424
  10.4 1.5 %collective-permute-start.7 = (bf16[4,128,128]{2,1,0:T(8,128)(2,1)S(1)}, bf16[4,128,128]{2,1,0:T(8,128)(2,1)S(1)}, u32[]{:S(2)}, u32[]{:S(2)}) collective-permute-start(bf16[4,128,128]{2,1,0:T(8,128)(2,1)S(1)} %get-tuple-element.48), channel_id=1, source_target_pairs={{0,16},{4,20},{8,24},{12,28},{16,0},{20,4},{24,8},{28,12},{1,17},{... | collective-permute-start | bytes 393224 | tf_op jit(solution)/shard_map/ppermute | solution.py:424
  12.0 0.5 %collective-permute-start.8 = (bf16[4,128,128]{2,1,0:T(8,128)(2,1)}, bf16[4,128,128]{2,1,0:T(8,128)(2,1)S(1)}, u32[]{:S(2)}, u32[]{:S(2)}) collective-permute-start(bf16[4,128,128]{2,1,0:T(8,128)(2,1)} %get-tuple-element.49), channel_id=1, source_target_pairs={{0,24},{4,28},{8,16},{12,20},{16,8},{20,12},{24,0},{28,4},{1,25},{... | collective-permute-start | bytes 393224 | tf_op jit(solution)/shard_map/ppermute | solution.py:424
  12.5 2.9 %near_stats.1 = (f32[32,128]{1,0:T(8,128)S(1)}, f32[32,128]{1,0:T(8,128)S(1)}) custom-call(bf16[128,2048]{1,0:T(8,128)(2,1)} %k_ref.1, bf16[128,2048]{1,0:T(8,128)(2,1)} %v_ref.1, bf16[128,2048]{1,0:T(8,128)(2,1)} %q_ref.1, bf16[128,2048]{1,0:T(8,128)(2,1)} %u_ref.1), custom_call_target="tpu_custom_call" | custom-call | flops 134217728 | bytes 2129920 | tf_op jit(solution)/shard_map/near_stats/pallas_call | solution.py:401
  15.4 0.7 %collective-permute-done.1.refs_2_.refs_6_ = bf16[4,32,512]{2,1,0:T(8,128)(2,1)S(1)} collective-permute-done((bf16[4,32,512]{2,1,0:T(8,128)(2,1)S(1)}, bf16[4,32,512]{2,1,0:T(8,128)(2,1)S(1)}, u32[]{:S(2)}, u32[]{:S(2)}) %collective-permute-start.1) | collective-permute-done | bytes 131104 | tf_op jit(solution)/shard_map/ppermute | solution.py:424
  16.1 4.5 %collective-permute-done.2.refs_3_.refs_5_ = bf16[4,32,512]{2,1,0:T(8,128)(2,1)S(1)} collective-permute-done((bf16[4,32,512]{2,1,0:T(8,128)(2,1)S(1)}, bf16[4,32,512]{2,1,0:T(8,128)(2,1)S(1)}, u32[]{:S(2)}, u32[]{:S(2)}) %collective-permute-start.2) | collective-permute-done | bytes 131104 | tf_op jit(solution)/shard_map/ppermute | solution.py:424
  20.7 0.6 %middle_stats.1 = (f32[32,128]{1,0:T(8,128)S(1)}, f32[32,128]{1,0:T(8,128)S(1)}, f32[32,128]{1,0:T(8,128)S(1)}, f32[32,128]{1,0:T(8,128)S(1)}, f32[8,128]{1,0:T(8,128)S(1)}, /*index=5*/f32[8,128]{1,0:T(8,128)S(1)}) custom-call(bf16[4,32,512]{2,1,0:T(8,128)(2,1)S(1)} %get-tuple-element.34.refs_0_, ...), custom_call_target="tpu_custom_call" | custom-call | flops 33554432 | bytes 630784 | tf_op jit(solution)/shard_map/middle_stats/pallas_call | solution.py:401
  21.3 3.2 %collective-permute-start.4 = (f32[32,128]{1,0:T(8,128)S(1)}, f32[32,128]{1,0:T(8,128)S(1)}, u32[]{:S(2)}, u32[]{:S(2)}) collective-permute-start(f32[32,128]{1,0:T(8,128)S(1)} %get-tuple-element.43), channel_id=1, source_target_pairs={{0,2},{1,3},{2,0},{3,1},{4,6},{5,7},{6,4},{7,5},{8,10},{9,11},{10,... | collective-permute-start | bytes 49160 | tf_op jit(solution)/shard_map/ppermute | solution.py:424
  24.5 1.2 %collective-permute-start.5 = (f32[32,128]{1,0:T(8,128)S(1)}, f32[32,128]{1,0:T(8,128)S(1)}, u32[]{:S(2)}, u32[]{:S(2)}) collective-permute-start(f32[32,128]{1,0:T(8,128)S(1)} %get-tuple-element.44), channel_id=1, source_target_pairs={{0,3},{1,2},{2,1},{3,0},{4,7},{5,6},{6,5},{7,4},{8,11},{9,10},{10,... | collective-permute-start | bytes 49160 | tf_op jit(solution)/shard_map/ppermute | solution.py:424
  25.7 1.1 %far_stats.1.refs_10_.refs_5_ = f32[16,128]{1,0:T(8,128)S(1)} custom-call(f32[8,128]{1,0:T(8,128)S(1)} %get-tuple-element.45.near_ref, bf16[4,128,128]{2,1,0:T(8,128)(2,1)S(1)} %get-tuple-element.46.refs_0_, bf16[4,128,128]{2,1,0:T(8,128)(2,1)S(1)} %collective-permute-done.6.refs_1_, bf16[4,128,128]{2,1,0:T(8,128)(2,1)S(1)} %collective-permute-done.7.refs_2_, ...), custom_call_target="tpu_custom_call" | custom-call | flops 268435456 | bytes 798720 | tf_op jit(solution)/shard_map/far_stats/pallas_call | solution.py:401
  26.8 2.5 %collective-permute-start.12 = (f32[16,128]{1,0:T(8,128)S(1)}, f32[16,128]{1,0:T(8,128)S(1)}, u32[]{:S(2)}, u32[]{:S(2)}) collective-permute-start(f32[16,128]{1,0:T(8,128)S(1)} %far_stats.1.refs_10_.refs_5_), channel_id=1, source_target_pairs={{0,24},{4,28},{8,16},{12,20},{16,8},{20,12},{24,0},{28,4},{1,25},{... | collective-permute-start | bytes 24584 | tf_op jit(solution)/shard_map/ppermute | solution.py:424
  29.3 0.5 collective-permute-start.11
  29.8 0.5 collective-permute-start.10
  30.4 1.1 %collective-permute-done.12.refs_13_.refs_8_ = f32[16,128]{1,0:T(8,128)S(1)} collective-permute-done((f32[16,128]{1,0:T(8,128)S(1)}, f32[16,128]{1,0:T(8,128)S(1)}, u32[]{:S(2)}, u32[]{:S(2)}) %collective-permute-start.12) | collective-permute-done | bytes 8224 | tf_op jit(solution)/shard_map/ppermute | solution.py:424
  31.5 1.5 %collective-permute-done.11.refs_12_.refs_7_ = f32[16,128]{1,0:T(8,128)S(1)} collective-permute-done((f32[16,128]{1,0:T(8,128)S(1)}, f32[16,128]{1,0:T(8,128)S(1)}, u32[]{:S(2)}, u32[]{:S(2)}) %collective-permute-start.11) | collective-permute-done | bytes 8224 | tf_op jit(solution)/shard_map/ppermute | solution.py:424
  33.0 0.5 collective-permute-done.10.refs_11_.refs_6_
  33.5 0.8 %middle_parts.1 = (bf16[4,32,512]{2,1,0:T(8,128)(2,1)S(1)}, bf16[4,32,512]{2,1,0:T(8,128)(2,1)S(1)}, bf16[4,32,512]{2,1,0:T(8,128)(2,1)S(1)}, bf16[4,32,512]{2,1,0:T(8,128)(2,1)S(1)}, f32[32,128]{1,0:T(8,128)S(1)}) custom-call(bf16[4,32,512]{2,1,0:T(8,128)(2,1)S(1)} %get-tuple-element.34.refs_0_, ...), custom_call_target="tpu_custom_call" | custom-call | flops 100663296 | bytes 1183744 | tf_op jit(solution)/shard_map/middle_parts/pallas_call | solution.py:401
  34.3 2.3 %far_parts.1 = (bf16[4,128,128]{2,1,0:T(8,128)(2,1)S(1)}, bf16[4,128,128]{2,1,0:T(8,128)(2,1)S(1)}, bf16[4,128,128]{2,1,0:T(8,128)(2,1)S(1)}, bf16[4,128,128]{2,...) custom-call(bf16[4,128,128]{2,1,0:T(8,128)(2,1)S(1)} %get-tuple-element.46.refs_0_, ...), custom_call_target="tpu_custom_call" | custom-call | flops 805306368 | bytes 1622016 | tf_op jit(solution)/shard_map/far_parts/pallas_call | solution.py:401
  36.7 2.7 %collective-permute-start.14 = (bf16[4,32,512]{2,1,0:T(8,128)(2,1)S(1)}, bf16[4,32,512]{2,1,0:T(8,128)(2,1)S(1)}, u32[]{:S(2)}, u32[]{:S(2)}) collective-permute-start(bf16[4,32,512]{2,1,0:T(8,128)(2,1)S(1)} %get-tuple-element.53), channel_id=1, source_target_pairs={{0,3},{1,2},{2,1},{3,0},{4,7},{5,6},{6,5},{7,4},{8,11},{9,10},{10,... | collective-permute-start | bytes 393224 | tf_op jit(solution)/shard_map/ppermute | solution.py:424
  39.5 0.8 %collective-permute-start.15 = (bf16[4,32,512]{2,1,0:T(8,128)(2,1)S(1)}, bf16[4,32,512]{2,1,0:T(8,128)(2,1)S(1)}, u32[]{:S(2)}, u32[]{:S(2)}) collective-permute-start(bf16[4,32,512]{2,1,0:T(8,128)(2,1)S(1)} %get-tuple-element.54), channel_id=1, source_target_pairs={{0,2},{1,3},{2,0},{3,1},{4,6},{5,7},{6,4},{7,5},{8,10},{9,11},{10,... | collective-permute-start | bytes 393224 | tf_op jit(solution)/shard_map/ppermute | solution.py:424
  40.3 0.6 %collective-permute-start.17 = (bf16[4,128,128]{2,1,0:T(8,128)(2,1)S(1)}, bf16[4,128,128]{2,1,0:T(8,128)(2,1)S(1)}, u32[]{:S(2)}, u32[]{:S(2)}) collective-permute-start(bf16[4,128,128]{2,1,0:T(8,128)(2,1)S(1)} %get-tuple-element.61), channel_id=1, source_target_pairs={{0,8},{4,12},{8,0},{12,4},{16,24},{20,28},{24,16},{28,20},{1,9},{5... | collective-permute-start | bytes 393224 | tf_op jit(solution)/shard_map/ppermute | solution.py:424
  40.9 1.5 %collective-permute-start.18 = (bf16[4,128,128]{2,1,0:T(8,128)(2,1)S(1)}, bf16[4,128,128]{2,1,0:T(8,128)(2,1)S(1)}, u32[]{:S(2)}, u32[]{:S(2)}) collective-permute-start(bf16[4,128,128]{2,1,0:T(8,128)(2,1)S(1)} %get-tuple-element.62), channel_id=1, source_target_pairs={{0,16},{4,20},{8,24},{12,28},{16,0},{20,4},{24,8},{28,12},{1,17},{... | collective-permute-start | bytes 393224 | tf_op jit(solution)/shard_map/ppermute | solution.py:424
  42.4 0.2 collective-permute-done.13.refs_1_
  42.6 1.5 %collective-permute-start.19 = (bf16[4,128,128]{2,1,0:T(8,128)(2,1)S(1)}, bf16[4,128,128]{2,1,0:T(8,128)(2,1)S(1)}, u32[]{:S(2)}, u32[]{:S(2)}) collective-permute-start(bf16[4,128,128]{2,1,0:T(8,128)(2,1)S(1)} %get-tuple-element.63), channel_id=1, source_target_pairs={{0,24},{4,28},{8,16},{12,20},{16,8},{20,12},{24,0},{28,4},{1,25},{... | collective-permute-start | bytes 393224 | tf_op jit(solution)/shard_map/ppermute | solution.py:424
  44.1 1.9 %near_parts.1.near_ref = f32[4,16,128,128]{3,2,1,0:T(8,128)S(1)} custom-call(bf16[128,2048]{1,0:T(8,128)(2,1)S(1)} %copy-done, bf16[128,2048]{1,0:T(8,128)(2,1)S(1)} %copy-done.1, bf16[128,2048]{1,0:T(8,128)(2,1)S(1)} %copy-done.2, bf16[128,2048]{1,0:T(8,128)(2,1)S(1)} %copy-done.3, f32[32,128]{1,0:T(8,128)S(1)} %get-tuple-element.50.stats_ref.refs_9_), custom_call_target="tpu_custom_call" | custom-call | flops 1 | bytes 1 | tf_op jit(solution)/shard_map/near_parts/pallas_call | solution.py:401
  46.0 0.7 %collective-permute-done.14.refs_2_ = bf16[4,32,512]{2,1,0:T(8,128)(2,1)S(1)} collective-permute-done((bf16[4,32,512]{2,1,0:T(8,128)(2,1)S(1)}, bf16[4,32,512]{2,1,0:T(8,128)(2,1)S(1)}, u32[]{:S(2)}, u32[]{:S(2)}) %collective-permute-start.14) | collective-permute-done | bytes 131104 | tf_op jit(solution)/shard_map/ppermute | solution.py:424
  46.6 5.6 %collective-permute-done.15.refs_3_ = bf16[4,32,512]{2,1,0:T(8,128)(2,1)S(1)} collective-permute-done((bf16[4,32,512]{2,1,0:T(8,128)(2,1)S(1)}, bf16[4,32,512]{2,1,0:T(8,128)(2,1)S(1)}, u32[]{:S(2)}, u32[]{:S(2)}) %collective-permute-start.15) | collective-permute-done | bytes 131104 | tf_op jit(solution)/shard_map/ppermute | solution.py:424
  52.2 1.8 %final.1 = (bf16[128,2048]{1,0:T(8,128)(2,1)}, bf16[128,2048]{1,0:T(8,128)(2,1)}, bf16[128,2048]{1,0:T(8,128)(2,1)}, bf16[128,2048]{1,0:T(8,128)(2,1)}) custom-call(f32[4,16,128,128]{3,2,1,0:T(8,128)S(1)} %near_parts.1.near_ref, bf16[4,32,512]{2,1,0:T(8,128)(2,1)S(1)} %get-tuple-element.51.refs_0_, bf16[4,32,512]{2,1,0:T(8,128)(2,1)S(1)} %collective-permute-done.13.refs_1_, ...), custom_call_target="tpu_custom_call" | custom-call | flops 67108864 | bytes 7340032 | tf_op jit(solution)/shard_map/final/pallas_call | solution.py:401
  (26 shorter events, 0.4 us)
Async XLA Ops:
  3.2 8.7 %collective-permute-start = (bf16[4,32,512]{2,1,0:T(8,128)(2,1)S(1)}, bf16[4,32,512]{2,1,0:T(8,128)(2,1)S(1)}, u32[]{:S(2)}, u32[]{:S(2)}) collective-permute-start(bf16[4,32,512]{2,1,0:T(8,128)(2,1)S(1)} %get-tuple-element.35), channel_id=1, source_target_pairs={{0,1},{1,0},{2,3},{3,2},{4,5},{5,4},{6,7},{7,6},{8,9},{9,8},{10,11... | collective-permute-start | bytes 393224 | tf_op jit(solution)/shard_map/ppermute | solution.py:424
  6.3 9.7 %collective-permute-start.1 = (bf16[4,32,512]{2,1,0:T(8,128)(2,1)S(1)}, bf16[4,32,512]{2,1,0:T(8,128)(2,1)S(1)}, u32[]{:S(2)}, u32[]{:S(2)}) collective-permute-start(bf16[4,32,512]{2,1,0:T(8,128)(2,1)S(1)} %get-tuple-element.36), channel_id=1, source_target_pairs={{0,3},{1,2},{2,1},{3,0},{4,7},{5,6},{6,5},{7,4},{8,11},{9,10},{10,... | collective-permute-start | bytes 393224 | tf_op jit(solution)/shard_map/ppermute | solution.py:424
  8.8 11.8 %collective-permute-start.2 = (bf16[4,32,512]{2,1,0:T(8,128)(2,1)S(1)}, bf16[4,32,512]{2,1,0:T(8,128)(2,1)S(1)}, u32[]{:S(2)}, u32[]{:S(2)}) collective-permute-start(bf16[4,32,512]{2,1,0:T(8,128)(2,1)S(1)} %get-tuple-element.37), channel_id=1, source_target_pairs={{0,2},{1,3},{2,0},{3,1},{4,6},{5,7},{6,4},{7,5},{8,10},{9,11},{10,... | collective-permute-start | bytes 393224 | tf_op jit(solution)/shard_map/ppermute | solution.py:424
  8.9 11.6 %collective-permute-start.6 = (bf16[4,128,128]{2,1,0:T(8,128)(2,1)S(1)}, bf16[4,128,128]{2,1,0:T(8,128)(2,1)S(1)}, u32[]{:S(2)}, u32[]{:S(2)}) collective-permute-start(bf16[4,128,128]{2,1,0:T(8,128)(2,1)S(1)} %get-tuple-element.47), channel_id=1, source_target_pairs={{0,8},{4,12},{8,0},{12,4},{16,24},{20,28},{24,16},{28,20},{1,9},{5... | collective-permute-start | bytes 393224 | tf_op jit(solution)/shard_map/ppermute | solution.py:424
  10.4 10.2 %collective-permute-start.7 = (bf16[4,128,128]{2,1,0:T(8,128)(2,1)S(1)}, bf16[4,128,128]{2,1,0:T(8,128)(2,1)S(1)}, u32[]{:S(2)}, u32[]{:S(2)}) collective-permute-start(bf16[4,128,128]{2,1,0:T(8,128)(2,1)S(1)} %get-tuple-element.48), channel_id=1, source_target_pairs={{0,16},{4,20},{8,24},{12,28},{16,0},{20,4},{24,8},{28,12},{1,17},{... | collective-permute-start | bytes 393224 | tf_op jit(solution)/shard_map/ppermute | solution.py:424
  12.0 32.1 %copy-start = (bf16[128,2048]{1,0:T(8,128)(2,1)S(1)}, bf16[128,2048]{1,0:T(8,128)(2,1)}, u32[]{:S(2)}) copy-start(bf16[128,2048]{1,0:T(8,128)(2,1)} %k_ref.1) | copy-start | bytes 1572868
  12.0 32.1 %copy-start.1 = (bf16[128,2048]{1,0:T(8,128)(2,1)S(1)}, bf16[128,2048]{1,0:T(8,128)(2,1)}, u32[]{:S(2)}) copy-start(bf16[128,2048]{1,0:T(8,128)(2,1)} %v_ref.1) | copy-start | bytes 1572868
  12.0 32.1 %copy-start.2 = (bf16[128,2048]{1,0:T(8,128)(2,1)S(1)}, bf16[128,2048]{1,0:T(8,128)(2,1)}, u32[]{:S(2)}) copy-start(bf16[128,2048]{1,0:T(8,128)(2,1)} %q_ref.1) | copy-start | bytes 1572868
  12.0 32.1 %copy-start.3 = (bf16[128,2048]{1,0:T(8,128)(2,1)S(1)}, bf16[128,2048]{1,0:T(8,128)(2,1)}, u32[]{:S(2)}) copy-start(bf16[128,2048]{1,0:T(8,128)(2,1)} %u_ref.1) | copy-start | bytes 1572868
  12.0 8.6 %collective-permute-start.8 = (bf16[4,128,128]{2,1,0:T(8,128)(2,1)}, bf16[4,128,128]{2,1,0:T(8,128)(2,1)S(1)}, u32[]{:S(2)}, u32[]{:S(2)}) collective-permute-start(bf16[4,128,128]{2,1,0:T(8,128)(2,1)} %get-tuple-element.49), channel_id=1, source_target_pairs={{0,24},{4,28},{8,16},{12,20},{16,8},{20,12},{24,0},{28,4},{1,25},{... | collective-permute-start | bytes 393224 | tf_op jit(solution)/shard_map/ppermute | solution.py:424
  20.6 5.1 %collective-permute-start.9 = (bf16[4,2,128,128]{3,2,1,0:T(8,128)(2,1)S(1)}, bf16[4,2,128,128]{3,2,1,0:T(8,128)(2,1)S(1)}, u32[]{:S(2)}, u32[]{:S(2)}) collective-permute-start(bf16[4,2,128,128]{3,2,1,0:T(8,128)(2,1)S(1)} %pack.1), channel_id=1, source_target_pairs={{0,4},{4,0},{8,12},{12,8},{16,20},{20,16},{24,28},{28,24},{1,5},{5... | collective-permute-start | bytes 786440 | tf_op jit(solution)/shard_map/ppermute | solution.py:424
  21.3 8.6 %collective-permute-start.3 = (f32[32,128]{1,0:T(8,128)S(1)}, f32[32,128]{1,0:T(8,128)S(1)}, u32[]{:S(2)}, u32[]{:S(2)}) collective-permute-start(f32[32,128]{1,0:T(8,128)S(1)} %get-tuple-element.42), channel_id=1, source_target_pairs={{0,1},{1,0},{2,3},{3,2},{4,5},{5,4},{6,7},{7,6},{8,9},{9,8},{10,11... | collective-permute-start | bytes 49160 | tf_op jit(solution)/shard_map/ppermute | solution.py:424
  21.3 9.0 %collective-permute-start.4 = (f32[32,128]{1,0:T(8,128)S(1)}, f32[32,128]{1,0:T(8,128)S(1)}, u32[]{:S(2)}, u32[]{:S(2)}) collective-permute-start(f32[32,128]{1,0:T(8,128)S(1)} %get-tuple-element.43), channel_id=1, source_target_pairs={{0,2},{1,3},{2,0},{3,1},{4,6},{5,7},{6,4},{7,5},{8,10},{9,11},{10,... | collective-permute-start | bytes 49160 | tf_op jit(solution)/shard_map/ppermute | solution.py:424
  24.5 5.9 %collective-permute-start.5 = (f32[32,128]{1,0:T(8,128)S(1)}, f32[32,128]{1,0:T(8,128)S(1)}, u32[]{:S(2)}, u32[]{:S(2)}) collective-permute-start(f32[32,128]{1,0:T(8,128)S(1)} %get-tuple-element.44), channel_id=1, source_target_pairs={{0,3},{1,2},{2,1},{3,0},{4,7},{5,6},{6,5},{7,4},{8,11},{9,10},{10,... | collective-permute-start | bytes 49160 | tf_op jit(solution)/shard_map/ppermute | solution.py:424
  26.8 4.7 %collective-permute-start.12 = (f32[16,128]{1,0:T(8,128)S(1)}, f32[16,128]{1,0:T(8,128)S(1)}, u32[]{:S(2)}, u32[]{:S(2)}) collective-permute-start(f32[16,128]{1,0:T(8,128)S(1)} %far_stats.1.refs_10_.refs_5_), channel_id=1, source_target_pairs={{0,24},{4,28},{8,16},{12,20},{16,8},{20,12},{24,0},{28,4},{1,25},{... | collective-permute-start | bytes 24584 | tf_op jit(solution)/shard_map/ppermute | solution.py:424
  29.3 3.7 %collective-permute-start.11 = (f32[16,128]{1,0:T(8,128)S(1)}, f32[16,128]{1,0:T(8,128)S(1)}, u32[]{:S(2)}, u32[]{:S(2)}) collective-permute-start(f32[16,128]{1,0:T(8,128)S(1)} %far_stats.1.refs_10_.refs_5_), channel_id=1, source_target_pairs={{0,16},{4,20},{8,24},{12,28},{16,0},{20,4},{24,8},{28,12},{1,17},{... | collective-permute-start | bytes 24584 | tf_op jit(solution)/shard_map/ppermute | solution.py:424
  29.8 3.7 %collective-permute-start.10 = (f32[16,128]{1,0:T(8,128)S(1)}, f32[16,128]{1,0:T(8,128)S(1)}, u32[]{:S(2)}, u32[]{:S(2)}) collective-permute-start(f32[16,128]{1,0:T(8,128)S(1)} %far_stats.1.refs_10_.refs_5_), channel_id=1, source_target_pairs={{0,8},{4,12},{8,0},{12,4},{16,24},{20,28},{24,16},{28,20},{1,9},{5... | collective-permute-start | bytes 24584 | tf_op jit(solution)/shard_map/ppermute | solution.py:424
  36.6 3.6 %collective-permute-start.16 = (bf16[4,2,128,128]{3,2,1,0:T(8,128)(2,1)S(1)}, bf16[4,2,128,128]{3,2,1,0:T(8,128)(2,1)S(1)}, u32[]{:S(2)}, u32[]{:S(2)}) collective-permute-start(bf16[4,2,128,128]{3,2,1,0:T(8,128)(2,1)S(1)} %get-tuple-element.59), channel_id=1, source_target_pairs={{0,4},{4,0},{8,12},{12,8},{16,20},{20,16},{24,28},{28,24},{1,5},{5... | collective-permute-start | bytes 786440 | tf_op jit(solution)/shard_map/ppermute | solution.py:424
  36.7 5.9 %collective-permute-start.13 = (bf16[4,32,512]{2,1,0:T(8,128)(2,1)S(1)}, bf16[4,32,512]{2,1,0:T(8,128)(2,1)S(1)}, u32[]{:S(2)}, u32[]{:S(2)}) collective-permute-start(bf16[4,32,512]{2,1,0:T(8,128)(2,1)S(1)} %get-tuple-element.52), channel_id=1, source_target_pairs={{0,1},{1,0},{2,3},{3,2},{4,5},{5,4},{6,7},{7,6},{8,9},{9,8},{10,11... | collective-permute-start | bytes 393224 | tf_op jit(solution)/shard_map/ppermute | solution.py:424
  36.7 9.9 %collective-permute-start.14 = (bf16[4,32,512]{2,1,0:T(8,128)(2,1)S(1)}, bf16[4,32,512]{2,1,0:T(8,128)(2,1)S(1)}, u32[]{:S(2)}, u32[]{:S(2)}) collective-permute-start(bf16[4,32,512]{2,1,0:T(8,128)(2,1)S(1)} %get-tuple-element.53), channel_id=1, source_target_pairs={{0,3},{1,2},{2,1},{3,0},{4,7},{5,6},{6,5},{7,4},{8,11},{9,10},{10,... | collective-permute-start | bytes 393224 | tf_op jit(solution)/shard_map/ppermute | solution.py:424
  39.5 12.7 %collective-permute-start.15 = (bf16[4,32,512]{2,1,0:T(8,128)(2,1)S(1)}, bf16[4,32,512]{2,1,0:T(8,128)(2,1)S(1)}, u32[]{:S(2)}, u32[]{:S(2)}) collective-permute-start(bf16[4,32,512]{2,1,0:T(8,128)(2,1)S(1)} %get-tuple-element.54), channel_id=1, source_target_pairs={{0,2},{1,3},{2,0},{3,1},{4,6},{5,7},{6,4},{7,5},{8,10},{9,11},{10,... | collective-permute-start | bytes 393224 | tf_op jit(solution)/shard_map/ppermute | solution.py:424
  40.3 11.9 %collective-permute-start.17 = (bf16[4,128,128]{2,1,0:T(8,128)(2,1)S(1)}, bf16[4,128,128]{2,1,0:T(8,128)(2,1)S(1)}, u32[]{:S(2)}, u32[]{:S(2)}) collective-permute-start(bf16[4,128,128]{2,1,0:T(8,128)(2,1)S(1)} %get-tuple-element.61), channel_id=1, source_target_pairs={{0,8},{4,12},{8,0},{12,4},{16,24},{20,28},{24,16},{28,20},{1,9},{5... | collective-permute-start | bytes 393224 | tf_op jit(solution)/shard_map/ppermute | solution.py:424
  40.9 11.3 %collective-permute-start.18 = (bf16[4,128,128]{2,1,0:T(8,128)(2,1)S(1)}, bf16[4,128,128]{2,1,0:T(8,128)(2,1)S(1)}, u32[]{:S(2)}, u32[]{:S(2)}) collective-permute-start(bf16[4,128,128]{2,1,0:T(8,128)(2,1)S(1)} %get-tuple-element.62), channel_id=1, source_target_pairs={{0,16},{4,20},{8,24},{12,28},{16,0},{20,4},{24,8},{28,12},{1,17},{... | collective-permute-start | bytes 393224 | tf_op jit(solution)/shard_map/ppermute | solution.py:424
  42.6 9.6 %collective-permute-start.19 = (bf16[4,128,128]{2,1,0:T(8,128)(2,1)S(1)}, bf16[4,128,128]{2,1,0:T(8,128)(2,1)S(1)}, u32[]{:S(2)}, u32[]{:S(2)}) collective-permute-start(bf16[4,128,128]{2,1,0:T(8,128)(2,1)S(1)} %get-tuple-element.63), channel_id=1, source_target_pairs={{0,24},{4,28},{8,16},{12,20},{16,8},{20,12},{24,0},{28,4},{1,25},{... | collective-permute-start | bytes 393224 | tf_op jit(solution)/shard_map/ppermute | solution.py:424

commit v7 on v6

--- a/solution.py
+++ b/solution.py
@@ -13,6 +13,7 @@
 LANES = 128
 SCALE = HEAD_DIM**-0.5
 LOWEST = -1e30
+LONG = 4 * 10**10
 VMEM_LIMIT = 32 * 1024 * 1024
 PICK_LIMIT = 53 * 1024 * 1024
 NEAR_LIMIT = 54784 * 1024
@@ -356,8 +357,8 @@
 
 
 def final_kernel(n_i, slots, near_ref, *refs):
-    mids, refs = in_order(refs[:n_i]), refs[n_i:]
-    fulls, refs = refs[:slots], refs[slots:]
+    mids, refs = (refs[0], *refs[n_i - 1 : 0 : -1]), refs[n_i:]
+    fulls, refs = refs[:slots], refs[slots + 1 :]
     outs, (ready, sems) = refs[:4], refs[4:]
     rows = fulls[0].shape[1]
     quarter = rows // DILATION
@@ -393,6 +394,10 @@
         copy.wait()
 
 
+def settle_kernel(*refs):
+    refs[-1][...] = jnp.zeros_like(refs[-1])
+
+
 def call(kernel, name, outs, scratch, flops, operands, hbm_in=(), hbm_out=False, cheap=False, limit=VMEM_LIMIT):
     moved = sum(x.size * x.dtype.itemsize for x in tuple(operands) + tuple(outs))
     if cheap:
@@ -523,6 +528,7 @@
         [pltpu.VMEM((n_o * rows, slots * rows), BF16)] * 2,
         unit * n_o * slots * 6,
         fulls + sibs + xmsgs + [final],
+        cheap=True,
     )
     fullparts = call(
         bind(far_sum_kernel, slots),
@@ -541,9 +547,11 @@
         "near_parts",
         [SHAPE((4, HEADS, rows, HEAD_DIM), F32)],
         [],
-        unit * HEADS * 6,
+        LONG,
         sources + (final,),
-        cheap=True,
+    )
+    (settled,) = call(
+        settle_kernel, "settle_parts", [stats(8)], [], LONG, midparts[:0:-1]
     )
     return call(
         bind(final_kernel, n_i, slots),
@@ -551,7 +559,7 @@
         [SHAPE((rows, features), BF16)] * 4,
         [pltpu.VMEM((4, rows, features), BF16), pltpu.SemaphoreType.DMA((4, n_i))],
         unit * HEADS,
-        [nearparts] + far_first(midparts) + fullparts,
+        [nearparts, midparts[0]] + midparts[:0:-1] + fullparts + [settled],
         hbm_out=True,
     )
 

time: 54.1 us -> 54.9 us (1.015)
  starting transfers between devices: 24.5 us -> 25.3 us
    ppermute x20, starting transfers between devices: 24.5 us -> 25.3 us  [swap(): return lax.ppermute(x, axis, [(i, i ^ mask) for i in range(n)])]
    pallas_call x10 -> x11, Pallas kernels: 14 us -> 14 us  [call(): pl.pallas_call(kernel, out_shape=tuple(outs), in_specs=[pl.BlockSpec(memo...]
  transfers between devices with their start and end apart: 20 -> 20, of which waited for: 8 -> 8; matrix products, arithmetic and copies ran while one was open for 0% -> 0% of each run, Pallas kernels for 12% -> 16%
where the time goes in v7:
time: 54.9 us; the launch traced here: 54.7 us
  starting transfers between devices  25.3 us (46%)
  waiting for transfers between devices  14.6 us (27%)
  Pallas kernels  14 us (26%)
  between operations  0.81 us (1%)
    ppermute x20, starting transfers between devices, swap(): return lax.ppermute(x, axis, [(i, i ^ mask) for i in range(n)])  25.3 us
    ppermute x20, waiting for transfers between devices, swap(): return lax.ppermute(x, axis, [(i, i ^ mask) for i in range(n)])  14.6 us
    pallas_call x11, Pallas kernels, call(): pl.pallas_call(kernel, out_shape=tuple(outs), in_specs=[pl.BlockSpec(memo...  14 us
  transfers between devices with their start and end apart: 20, of which 8 were waited for; matrix products, arithmetic and copies ran while one was open for 0% of the time, Pallas kernels for 16%

profile of v7, /device:TPU:0, one launch (start us, length us, event | category | flops | bytes accessed | tf_op | source)
XLA Modules:
  0.0 54.7 jit_solution(7135636993464882732)
XLA Ops:
  0.7 2.7 %pick.1 = (bf16[4,32,512]{2,1,0:T(8,128)(2,1)S(1)}, bf16[4,32,512]{2,1,0:T(8,128)(2,1)S(1)}, bf16[4,32,512]{2,1,0:T(8,128)(2,1)S(1)}, bf16[4,32,512]{2,1,0:T(8,1...) custom-call(bf16[128,2048]{1,0:T(8,128)(2,1)} %k_ref.1, ...), custom_call_target="tpu_custom_call" | custom-call | flops 4194304 | bytes 3145728 | tf_op jit(solution)/shard_map/pick/pallas_call | solution.py:406
  3.4 3.1 %collective-permute-start = (bf16[4,32,512]{2,1,0:T(8,128)(2,1)S(1)}, bf16[4,32,512]{2,1,0:T(8,128)(2,1)S(1)}, u32[]{:S(2)}, u32[]{:S(2)}) collective-permute-start(bf16[4,32,512]{2,1,0:T(8,128)(2,1)S(1)} %get-tuple-element.35), channel_id=1, source_target_pairs={{0,1},{1,0},{2,3},{3,2},{4,5},{5,4},{6,7},{7,6},{8,9},{9,8},{10,11... | collective-permute-start | bytes 393224 | tf_op jit(solution)/shard_map/ppermute | solution.py:429
  6.5 2.5 %collective-permute-start.1 = (bf16[4,32,512]{2,1,0:T(8,128)(2,1)S(1)}, bf16[4,32,512]{2,1,0:T(8,128)(2,1)S(1)}, u32[]{:S(2)}, u32[]{:S(2)}) collective-permute-start(bf16[4,32,512]{2,1,0:T(8,128)(2,1)S(1)} %get-tuple-element.36), channel_id=1, source_target_pairs={{0,3},{1,2},{2,1},{3,0},{4,7},{5,6},{6,5},{7,4},{8,11},{9,10},{10,... | collective-permute-start | bytes 393224 | tf_op jit(solution)/shard_map/ppermute | solution.py:429
  9.0 0.1 collective-permute-start.2
  9.1 1.5 %collective-permute-start.6 = (bf16[4,128,128]{2,1,0:T(8,128)(2,1)S(1)}, bf16[4,128,128]{2,1,0:T(8,128)(2,1)S(1)}, u32[]{:S(2)}, u32[]{:S(2)}) collective-permute-start(bf16[4,128,128]{2,1,0:T(8,128)(2,1)S(1)} %get-tuple-element.47), channel_id=1, source_target_pairs={{0,8},{4,12},{8,0},{12,4},{16,24},{20,28},{24,16},{28,20},{1,9},{5... | collective-permute-start | bytes 393224 | tf_op jit(solution)/shard_map/ppermute | solution.py:429
  10.6 1.5 %collective-permute-start.7 = (bf16[4,128,128]{2,1,0:T(8,128)(2,1)S(1)}, bf16[4,128,128]{2,1,0:T(8,128)(2,1)S(1)}, u32[]{:S(2)}, u32[]{:S(2)}) collective-permute-start(bf16[4,128,128]{2,1,0:T(8,128)(2,1)S(1)} %get-tuple-element.48), channel_id=1, source_target_pairs={{0,16},{4,20},{8,24},{12,28},{16,0},{20,4},{24,8},{28,12},{1,17},{... | collective-permute-start | bytes 393224 | tf_op jit(solution)/shard_map/ppermute | solution.py:429
  12.1 0.5 collective-permute-start.8
  12.6 2.8 %near_stats.1 = (f32[32,128]{1,0:T(8,128)S(1)}, f32[32,128]{1,0:T(8,128)S(1)}) custom-call(bf16[128,2048]{1,0:T(8,128)(2,1)} %k_ref.1, bf16[128,2048]{1,0:T(8,128)(2,1)} %v_ref.1, bf16[128,2048]{1,0:T(8,128)(2,1)} %q_ref.1, bf16[128,2048]{1,0:T(8,128)(2,1)} %u_ref.1), custom_call_target="tpu_custom_call" | custom-call | flops 134217728 | bytes 2129920 | tf_op jit(solution)/shard_map/near_stats/pallas_call | solution.py:406
  15.4 0.8 %collective-permute-done.1.refs_2_.refs_6_ = bf16[4,32,512]{2,1,0:T(8,128)(2,1)S(1)} collective-permute-done((bf16[4,32,512]{2,1,0:T(8,128)(2,1)S(1)}, bf16[4,32,512]{2,1,0:T(8,128)(2,1)S(1)}, u32[]{:S(2)}, u32[]{:S(2)}) %collective-permute-start.1) | collective-permute-done | bytes 131104 | tf_op jit(solution)/shard_map/ppermute | solution.py:429
  16.3 4.5 %collective-permute-done.2.refs_3_.refs_5_ = bf16[4,32,512]{2,1,0:T(8,128)(2,1)S(1)} collective-permute-done((bf16[4,32,512]{2,1,0:T(8,128)(2,1)S(1)}, bf16[4,32,512]{2,1,0:T(8,128)(2,1)S(1)}, u32[]{:S(2)}, u32[]{:S(2)}) %collective-permute-start.2) | collective-permute-done | bytes 131104 | tf_op jit(solution)/shard_map/ppermute | solution.py:429
  20.9 0.6 %middle_stats.1 = (f32[32,128]{1,0:T(8,128)S(1)}, f32[32,128]{1,0:T(8,128)S(1)}, f32[32,128]{1,0:T(8,128)S(1)}, f32[32,128]{1,0:T(8,128)S(1)}, f32[8,128]{1,0:T(8,128)S(1)}, /*index=5*/f32[8,128]{1,0:T(8,128)S(1)}) custom-call(bf16[4,32,512]{2,1,0:T(8,128)(2,1)S(1)} %get-tuple-element.34.refs_0_, ...), custom_call_target="tpu_custom_call" | custom-call | flops 33554432 | bytes 630784 | tf_op jit(solution)/shard_map/middle_stats/pallas_call | solution.py:406
  21.5 3.2 %collective-permute-start.4 = (f32[32,128]{1,0:T(8,128)S(1)}, f32[32,128]{1,0:T(8,128)S(1)}, u32[]{:S(2)}, u32[]{:S(2)}) collective-permute-start(f32[32,128]{1,0:T(8,128)S(1)} %get-tuple-element.43), channel_id=1, source_target_pairs={{0,2},{1,3},{2,0},{3,1},{4,6},{5,7},{6,4},{7,5},{8,10},{9,11},{10,... | collective-permute-start | bytes 49160 | tf_op jit(solution)/shard_map/ppermute | solution.py:429
  24.7 1.2 %collective-permute-start.5 = (f32[32,128]{1,0:T(8,128)S(1)}, f32[32,128]{1,0:T(8,128)S(1)}, u32[]{:S(2)}, u32[]{:S(2)}) collective-permute-start(f32[32,128]{1,0:T(8,128)S(1)} %get-tuple-element.44), channel_id=1, source_target_pairs={{0,3},{1,2},{2,1},{3,0},{4,7},{5,6},{6,5},{7,4},{8,11},{9,10},{10,... | collective-permute-start | bytes 49160 | tf_op jit(solution)/shard_map/ppermute | solution.py:429
  25.9 1.1 %far_stats.1.refs_10_.refs_5_ = f32[16,128]{1,0:T(8,128)S(1)} custom-call(f32[8,128]{1,0:T(8,128)S(1)} %get-tuple-element.45.near_ref, bf16[4,128,128]{2,1,0:T(8,128)(2,1)S(1)} %get-tuple-element.46.refs_0_, bf16[4,128,128]{2,1,0:T(8,128)(2,1)S(1)} %collective-permute-done.6.refs_1_, bf16[4,128,128]{2,1,0:T(8,128)(2,1)S(1)} %collective-permute-done.7.refs_2_, ...), custom_call_target="tpu_custom_call" | custom-call | flops 268435456 | bytes 798720 | tf_op jit(solution)/shard_map/far_stats/pallas_call | solution.py:406
  27.0 2.5 %collective-permute-start.12 = (f32[16,128]{1,0:T(8,128)S(1)}, f32[16,128]{1,0:T(8,128)S(1)}, u32[]{:S(2)}, u32[]{:S(2)}) collective-permute-start(f32[16,128]{1,0:T(8,128)S(1)} %far_stats.1.refs_10_.refs_5_), channel_id=1, source_target_pairs={{0,24},{4,28},{8,16},{12,20},{16,8},{20,12},{24,0},{28,4},{1,25},{... | collective-permute-start | bytes 24584 | tf_op jit(solution)/shard_map/ppermute | solution.py:429
  29.5 0.5 collective-permute-start.11
  30.0 0.5 collective-permute-start.10
  30.5 1.1 %collective-permute-done.12.refs_13_.refs_8_ = f32[16,128]{1,0:T(8,128)S(1)} collective-permute-done((f32[16,128]{1,0:T(8,128)S(1)}, f32[16,128]{1,0:T(8,128)S(1)}, u32[]{:S(2)}, u32[]{:S(2)}) %collective-permute-start.12) | collective-permute-done | bytes 8224 | tf_op jit(solution)/shard_map/ppermute | solution.py:429
  31.6 1.5 %collective-permute-done.11.refs_12_.refs_7_ = f32[16,128]{1,0:T(8,128)S(1)} collective-permute-done((f32[16,128]{1,0:T(8,128)S(1)}, f32[16,128]{1,0:T(8,128)S(1)}, u32[]{:S(2)}, u32[]{:S(2)}) %collective-permute-start.11) | collective-permute-done | bytes 8224 | tf_op jit(solution)/shard_map/ppermute | solution.py:429
  33.1 0.5 collective-permute-done.10.refs_11_.refs_6_
  33.7 0.8 %middle_parts.1 = (bf16[4,32,512]{2,1,0:T(8,128)(2,1)S(1)}, bf16[4,32,512]{2,1,0:T(8,128)(2,1)S(1)}, bf16[4,32,512]{2,1,0:T(8,128)(2,1)S(1)}, bf16[4,32,512]{2,1,0:T(8,128)(2,1)S(1)}, f32[32,128]{1,0:T(8,128)S(1)}) custom-call(bf16[4,32,512]{2,1,0:T(8,128)(2,1)S(1)} %get-tuple-element.34.refs_0_, ...), custom_call_target="tpu_custom_call" | custom-call | flops 100663296 | bytes 1183744 | tf_op jit(solution)/shard_map/middle_parts/pallas_call | solution.py:406
  34.5 2.7 %collective-permute-start.13 = (bf16[4,32,512]{2,1,0:T(8,128)(2,1)S(1)}, bf16[4,32,512]{2,1,0:T(8,128)(2,1)S(1)}, u32[]{:S(2)}, u32[]{:S(2)}) collective-permute-start(bf16[4,32,512]{2,1,0:T(8,128)(2,1)S(1)} %get-tuple-element.52), channel_id=1, source_target_pairs={{0,3},{1,2},{2,1},{3,0},{4,7},{5,6},{6,5},{7,4},{8,11},{9,10},{10,... | collective-permute-start | bytes 393224 | tf_op jit(solution)/shard_map/ppermute | solution.py:429
  37.2 1.7 %collective-permute-start.15 = (bf16[4,32,512]{2,1,0:T(8,128)(2,1)S(1)}, bf16[4,32,512]{2,1,0:T(8,128)(2,1)S(1)}, u32[]{:S(2)}, u32[]{:S(2)}) collective-permute-start(bf16[4,32,512]{2,1,0:T(8,128)(2,1)S(1)} %get-tuple-element.54), channel_id=1, source_target_pairs={{0,1},{1,0},{2,3},{3,2},{4,5},{5,4},{6,7},{7,6},{8,9},{9,8},{10,11... | collective-permute-start | bytes 393224 | tf_op jit(solution)/shard_map/ppermute | solution.py:429
  38.9 2.3 %far_parts.1 = (bf16[4,128,128]{2,1,0:T(8,128)(2,1)S(1)}, bf16[4,128,128]{2,1,0:T(8,128)(2,1)S(1)}, bf16[4,128,128]{2,1,0:T(8,128)(2,1)S(1)}, bf16[4,128,128]{2,...) custom-call(bf16[4,128,128]{2,1,0:T(8,128)(2,1)S(1)} %get-tuple-element.46.refs_0_, ...), custom_call_target="tpu_custom_call" | custom-call | flops 1 | bytes 1 | tf_op jit(solution)/shard_map/far_parts/pallas_call | solution.py:406
  41.3 1.8 %near_parts.1.near_ref = f32[4,16,128,128]{3,2,1,0:T(8,128)S(1)} custom-call(bf16[128,2048]{1,0:T(8,128)(2,1)S(1)} %copy-done, bf16[128,2048]{1,0:T(8,128)(2,1)S(1)} %copy-done.1, bf16[128,2048]{1,0:T(8,128)(2,1)S(1)} %copy-done.2, bf16[128,2048]{1,0:T(8,128)(2,1)S(1)} %copy-done.3, f32[32,128]{1,0:T(8,128)S(1)} %get-tuple-element.50.stats_ref.refs_9_), custom_call_target="tpu_custom_call" | custom-call | flops 40000000000 | bytes 6307840 | tf_op jit(solution)/shard_map/near_parts/pallas_call | solution.py:406
  43.3 0.6 %collective-permute-start.17 = (bf16[4,128,128]{2,1,0:T(8,128)(2,1)S(1)}, bf16[4,128,128]{2,1,0:T(8,128)(2,1)S(1)}, u32[]{:S(2)}, u32[]{:S(2)}) collective-permute-start(bf16[4,128,128]{2,1,0:T(8,128)(2,1)S(1)} %get-tuple-element.61), channel_id=1, source_target_pairs={{0,8},{4,12},{8,0},{12,4},{16,24},{20,28},{24,16},{28,20},{1,9},{5... | collective-permute-start | bytes 393224 | tf_op jit(solution)/shard_map/ppermute | solution.py:429
  43.9 1.5 %collective-permute-start.18 = (bf16[4,128,128]{2,1,0:T(8,128)(2,1)S(1)}, bf16[4,128,128]{2,1,0:T(8,128)(2,1)S(1)}, u32[]{:S(2)}, u32[]{:S(2)}) collective-permute-start(bf16[4,128,128]{2,1,0:T(8,128)(2,1)S(1)} %get-tuple-element.62), channel_id=1, source_target_pairs={{0,16},{4,20},{8,24},{12,28},{16,0},{20,4},{24,8},{28,12},{1,17},{... | collective-permute-start | bytes 393224 | tf_op jit(solution)/shard_map/ppermute | solution.py:429
  45.4 1.4 %collective-permute-start.19 = (bf16[4,128,128]{2,1,0:T(8,128)(2,1)S(1)}, bf16[4,128,128]{2,1,0:T(8,128)(2,1)S(1)}, u32[]{:S(2)}, u32[]{:S(2)}) collective-permute-start(bf16[4,128,128]{2,1,0:T(8,128)(2,1)S(1)} %get-tuple-element.63), channel_id=1, source_target_pairs={{0,24},{4,28},{8,16},{12,20},{16,8},{20,12},{24,0},{28,4},{1,25},{... | collective-permute-start | bytes 393224 | tf_op jit(solution)/shard_map/ppermute | solution.py:429
  46.8 2.8 %collective-permute-done.17.refs_5_ = bf16[4,128,128]{2,1,0:T(8,128)(2,1)S(1)} collective-permute-done((bf16[4,128,128]{2,1,0:T(8,128)(2,1)S(1)}, bf16[4,128,128]{2,1,0:T(8,128)(2,1)S(1)}, u32[]{:S(2)}, u32[]{:S(2)}) %collective-permute-start.17) | collective-permute-done | bytes 131104 | tf_op jit(solution)/shard_map/ppermute | solution.py:429
  49.6 1.7 %collective-permute-done.18.refs_6_ = bf16[4,128,128]{2,1,0:T(8,128)(2,1)S(1)} collective-permute-done((bf16[4,128,128]{2,1,0:T(8,128)(2,1)S(1)}, bf16[4,128,128]{2,1,0:T(8,128)(2,1)S(1)}, u32[]{:S(2)}, u32[]{:S(2)}) %collective-permute-start.18) | collective-permute-done | bytes 131104 | tf_op jit(solution)/shard_map/ppermute | solution.py:429
  51.3 1.6 %collective-permute-done.19.refs_7_ = bf16[4,128,128]{2,1,0:T(8,128)(2,1)S(1)} collective-permute-done((bf16[4,128,128]{2,1,0:T(8,128)(2,1)S(1)}, bf16[4,128,128]{2,1,0:T(8,128)(2,1)S(1)}, u32[]{:S(2)}, u32[]{:S(2)}) %collective-permute-start.19) | collective-permute-done | bytes 131104 | tf_op jit(solution)/shard_map/ppermute | solution.py:429
  53.0 1.8 %final.1 = (bf16[128,2048]{1,0:T(8,128)(2,1)}, bf16[128,2048]{1,0:T(8,128)(2,1)}, bf16[128,2048]{1,0:T(8,128)(2,1)}, bf16[128,2048]{1,0:T(8,128)(2,1)}) custom-call(f32[4,16,128,128]{3,2,1,0:T(8,128)S(1)} %near_parts.1.near_ref, bf16[4,32,512]{2,1,0:T(8,128)(2,1)S(1)} %get-tuple-element.51.refs_0_, ...), custom_call_target="tpu_custom_call" | custom-call | flops 67108864 | bytes 7344128 | tf_op jit(solution)/shard_map/final/pallas_call | solution.py:406
  (27 shorter events, 0.3 us)
Async XLA Ops:
  0.6 40.7 %copy-start.3 = (bf16[128,2048]{1,0:T(8,128)(2,1)S(1)}, bf16[128,2048]{1,0:T(8,128)(2,1)}, u32[]{:S(2)}) copy-start(bf16[128,2048]{1,0:T(8,128)(2,1)} %u_ref.1) | copy-start | bytes 1572868
  0.6 40.7 %copy-start.1 = (bf16[128,2048]{1,0:T(8,128)(2,1)S(1)}, bf16[128,2048]{1,0:T(8,128)(2,1)}, u32[]{:S(2)}) copy-start(bf16[128,2048]{1,0:T(8,128)(2,1)} %v_ref.1) | copy-start | bytes 1572868
  0.7 40.7 %copy-start = (bf16[128,2048]{1,0:T(8,128)(2,1)S(1)}, bf16[128,2048]{1,0:T(8,128)(2,1)}, u32[]{:S(2)}) copy-start(bf16[128,2048]{1,0:T(8,128)(2,1)} %k_ref.1) | copy-start | bytes 1572868
  0.7 40.7 %copy-start.2 = (bf16[128,2048]{1,0:T(8,128)(2,1)S(1)}, bf16[128,2048]{1,0:T(8,128)(2,1)}, u32[]{:S(2)}) copy-start(bf16[128,2048]{1,0:T(8,128)(2,1)} %q_ref.1) | copy-start | bytes 1572868
  3.4 8.7 %collective-permute-start = (bf16[4,32,512]{2,1,0:T(8,128)(2,1)S(1)}, bf16[4,32,512]{2,1,0:T(8,128)(2,1)S(1)}, u32[]{:S(2)}, u32[]{:S(2)}) collective-permute-start(bf16[4,32,512]{2,1,0:T(8,128)(2,1)S(1)} %get-tuple-element.35), channel_id=1, source_target_pairs={{0,1},{1,0},{2,3},{3,2},{4,5},{5,4},{6,7},{7,6},{8,9},{9,8},{10,11... | collective-permute-start | bytes 393224 | tf_op jit(solution)/shard_map/ppermute | solution.py:429
  6.5 9.7 %collective-permute-start.1 = (bf16[4,32,512]{2,1,0:T(8,128)(2,1)S(1)}, bf16[4,32,512]{2,1,0:T(8,128)(2,1)S(1)}, u32[]{:S(2)}, u32[]{:S(2)}) collective-permute-start(bf16[4,32,512]{2,1,0:T(8,128)(2,1)S(1)} %get-tuple-element.36), channel_id=1, source_target_pairs={{0,3},{1,2},{2,1},{3,0},{4,7},{5,6},{6,5},{7,4},{8,11},{9,10},{10,... | collective-permute-start | bytes 393224 | tf_op jit(solution)/shard_map/ppermute | solution.py:429
  9.0 11.8 %collective-permute-start.2 = (bf16[4,32,512]{2,1,0:T(8,128)(2,1)S(1)}, bf16[4,32,512]{2,1,0:T(8,128)(2,1)S(1)}, u32[]{:S(2)}, u32[]{:S(2)}) collective-permute-start(bf16[4,32,512]{2,1,0:T(8,128)(2,1)S(1)} %get-tuple-element.37), channel_id=1, source_target_pairs={{0,2},{1,3},{2,0},{3,1},{4,6},{5,7},{6,4},{7,5},{8,10},{9,11},{10,... | collective-permute-start | bytes 393224 | tf_op jit(solution)/shard_map/ppermute | solution.py:429
  9.1 11.6 %collective-permute-start.6 = (bf16[4,128,128]{2,1,0:T(8,128)(2,1)S(1)}, bf16[4,128,128]{2,1,0:T(8,128)(2,1)S(1)}, u32[]{:S(2)}, u32[]{:S(2)}) collective-permute-start(bf16[4,128,128]{2,1,0:T(8,128)(2,1)S(1)} %get-tuple-element.47), channel_id=1, source_target_pairs={{0,8},{4,12},{8,0},{12,4},{16,24},{20,28},{24,16},{28,20},{1,9},{5... | collective-permute-start | bytes 393224 | tf_op jit(solution)/shard_map/ppermute | solution.py:429
  10.6 10.2 %collective-permute-start.7 = (bf16[4,128,128]{2,1,0:T(8,128)(2,1)S(1)}, bf16[4,128,128]{2,1,0:T(8,128)(2,1)S(1)}, u32[]{:S(2)}, u32[]{:S(2)}) collective-permute-start(bf16[4,128,128]{2,1,0:T(8,128)(2,1)S(1)} %get-tuple-element.48), channel_id=1, source_target_pairs={{0,16},{4,20},{8,24},{12,28},{16,0},{20,4},{24,8},{28,12},{1,17},{... | collective-permute-start | bytes 393224 | tf_op jit(solution)/shard_map/ppermute | solution.py:429
  12.1 8.6 %collective-permute-start.8 = (bf16[4,128,128]{2,1,0:T(8,128)(2,1)}, bf16[4,128,128]{2,1,0:T(8,128)(2,1)S(1)}, u32[]{:S(2)}, u32[]{:S(2)}) collective-permute-start(bf16[4,128,128]{2,1,0:T(8,128)(2,1)} %get-tuple-element.49), channel_id=1, source_target_pairs={{0,24},{4,28},{8,16},{12,20},{16,8},{20,12},{24,0},{28,4},{1,25},{... | collective-permute-start | bytes 393224 | tf_op jit(solution)/shard_map/ppermute | solution.py:429
  20.8 5.1 %collective-permute-start.9 = (bf16[4,2,128,128]{3,2,1,0:T(8,128)(2,1)S(1)}, bf16[4,2,128,128]{3,2,1,0:T(8,128)(2,1)S(1)}, u32[]{:S(2)}, u32[]{:S(2)}) collective-permute-start(bf16[4,2,128,128]{3,2,1,0:T(8,128)(2,1)S(1)} %pack.1), channel_id=1, source_target_pairs={{0,4},{4,0},{8,12},{12,8},{16,20},{20,16},{24,28},{28,24},{1,5},{5... | collective-permute-start | bytes 786440 | tf_op jit(solution)/shard_map/ppermute | solution.py:429
  21.4 8.6 %collective-permute-start.3 = (f32[32,128]{1,0:T(8,128)S(1)}, f32[32,128]{1,0:T(8,128)S(1)}, u32[]{:S(2)}, u32[]{:S(2)}) collective-permute-start(f32[32,128]{1,0:T(8,128)S(1)} %get-tuple-element.42), channel_id=1, source_target_pairs={{0,1},{1,0},{2,3},{3,2},{4,5},{5,4},{6,7},{7,6},{8,9},{9,8},{10,11... | collective-permute-start | bytes 49160 | tf_op jit(solution)/shard_map/ppermute | solution.py:429
  21.5 9.0 %collective-permute-start.4 = (f32[32,128]{1,0:T(8,128)S(1)}, f32[32,128]{1,0:T(8,128)S(1)}, u32[]{:S(2)}, u32[]{:S(2)}) collective-permute-start(f32[32,128]{1,0:T(8,128)S(1)} %get-tuple-element.43), channel_id=1, source_target_pairs={{0,2},{1,3},{2,0},{3,1},{4,6},{5,7},{6,4},{7,5},{8,10},{9,11},{10,... | collective-permute-start | bytes 49160 | tf_op jit(solution)/shard_map/ppermute | solution.py:429
  24.7 5.9 %collective-permute-start.5 = (f32[32,128]{1,0:T(8,128)S(1)}, f32[32,128]{1,0:T(8,128)S(1)}, u32[]{:S(2)}, u32[]{:S(2)}) collective-permute-start(f32[32,128]{1,0:T(8,128)S(1)} %get-tuple-element.44), channel_id=1, source_target_pairs={{0,3},{1,2},{2,1},{3,0},{4,7},{5,6},{6,5},{7,4},{8,11},{9,10},{10,... | collective-permute-start | bytes 49160 | tf_op jit(solution)/shard_map/ppermute | solution.py:429
  27.0 4.7 %collective-permute-start.12 = (f32[16,128]{1,0:T(8,128)S(1)}, f32[16,128]{1,0:T(8,128)S(1)}, u32[]{:S(2)}, u32[]{:S(2)}) collective-permute-start(f32[16,128]{1,0:T(8,128)S(1)} %far_stats.1.refs_10_.refs_5_), channel_id=1, source_target_pairs={{0,24},{4,28},{8,16},{12,20},{16,8},{20,12},{24,0},{28,4},{1,25},{... | collective-permute-start | bytes 24584 | tf_op jit(solution)/shard_map/ppermute | solution.py:429
  29.5 3.7 %collective-permute-start.11 = (f32[16,128]{1,0:T(8,128)S(1)}, f32[16,128]{1,0:T(8,128)S(1)}, u32[]{:S(2)}, u32[]{:S(2)}) collective-permute-start(f32[16,128]{1,0:T(8,128)S(1)} %far_stats.1.refs_10_.refs_5_), channel_id=1, source_target_pairs={{0,16},{4,20},{8,24},{12,28},{16,0},{20,4},{24,8},{28,12},{1,17},{... | collective-permute-start | bytes 24584 | tf_op jit(solution)/shard_map/ppermute | solution.py:429
  30.0 3.7 %collective-permute-start.10 = (f32[16,128]{1,0:T(8,128)S(1)}, f32[16,128]{1,0:T(8,128)S(1)}, u32[]{:S(2)}, u32[]{:S(2)}) collective-permute-start(f32[16,128]{1,0:T(8,128)S(1)} %far_stats.1.refs_10_.refs_5_), channel_id=1, source_target_pairs={{0,8},{4,12},{8,0},{12,4},{16,24},{20,28},{24,16},{28,20},{1,9},{5... | collective-permute-start | bytes 24584 | tf_op jit(solution)/shard_map/ppermute | solution.py:429
  34.5 10.9 %collective-permute-start.13 = (bf16[4,32,512]{2,1,0:T(8,128)(2,1)S(1)}, bf16[4,32,512]{2,1,0:T(8,128)(2,1)S(1)}, u32[]{:S(2)}, u32[]{:S(2)}) collective-permute-start(bf16[4,32,512]{2,1,0:T(8,128)(2,1)S(1)} %get-tuple-element.52), channel_id=1, source_target_pairs={{0,3},{1,2},{2,1},{3,0},{4,7},{5,6},{6,5},{7,4},{8,11},{9,10},{10,... | collective-permute-start | bytes 393224 | tf_op jit(solution)/shard_map/ppermute | solution.py:429
  37.2 9.7 %collective-permute-start.14 = (bf16[4,32,512]{2,1,0:T(8,128)(2,1)S(1)}, bf16[4,32,512]{2,1,0:T(8,128)(2,1)S(1)}, u32[]{:S(2)}, u32[]{:S(2)}) collective-permute-start(bf16[4,32,512]{2,1,0:T(8,128)(2,1)S(1)} %get-tuple-element.53), channel_id=1, source_target_pairs={{0,2},{1,3},{2,0},{3,1},{4,6},{5,7},{6,4},{7,5},{8,10},{9,11},{10,... | collective-permute-start | bytes 393224 | tf_op jit(solution)/shard_map/ppermute | solution.py:429
  37.2 9.7 %collective-permute-start.15 = (bf16[4,32,512]{2,1,0:T(8,128)(2,1)S(1)}, bf16[4,32,512]{2,1,0:T(8,128)(2,1)S(1)}, u32[]{:S(2)}, u32[]{:S(2)}) collective-permute-start(bf16[4,32,512]{2,1,0:T(8,128)(2,1)S(1)} %get-tuple-element.54), channel_id=1, source_target_pairs={{0,1},{1,0},{2,3},{3,2},{4,5},{5,4},{6,7},{7,6},{8,9},{9,8},{10,11... | collective-permute-start | bytes 393224 | tf_op jit(solution)/shard_map/ppermute | solution.py:429
  41.2 2.0 %collective-permute-start.16 = (bf16[4,2,128,128]{3,2,1,0:T(8,128)(2,1)S(1)}, bf16[4,2,128,128]{3,2,1,0:T(8,128)(2,1)S(1)}, u32[]{:S(2)}, u32[]{:S(2)}) collective-permute-start(bf16[4,2,128,128]{3,2,1,0:T(8,128)(2,1)S(1)} %get-tuple-element.59), channel_id=1, source_target_pairs={{0,4},{4,0},{8,12},{12,8},{16,20},{20,16},{24,28},{28,24},{1,5},{5... | collective-permute-start | bytes 786440 | tf_op jit(solution)/shard_map/ppermute | solution.py:429
  43.3 6.4 %collective-permute-start.17 = (bf16[4,128,128]{2,1,0:T(8,128)(2,1)S(1)}, bf16[4,128,128]{2,1,0:T(8,128)(2,1)S(1)}, u32[]{:S(2)}, u32[]{:S(2)}) collective-permute-start(bf16[4,128,128]{2,1,0:T(8,128)(2,1)S(1)} %get-tuple-element.61), channel_id=1, source_target_pairs={{0,8},{4,12},{8,0},{12,4},{16,24},{20,28},{24,16},{28,20},{1,9},{5... | collective-permute-start | bytes 393224 | tf_op jit(solution)/shard_map/ppermute | solution.py:429
  43.9 7.5 %collective-permute-start.18 = (bf16[4,128,128]{2,1,0:T(8,128)(2,1)S(1)}, bf16[4,128,128]{2,1,0:T(8,128)(2,1)S(1)}, u32[]{:S(2)}, u32[]{:S(2)}) collective-permute-start(bf16[4,128,128]{2,1,0:T(8,128)(2,1)S(1)} %get-tuple-element.62), channel_id=1, source_target_pairs={{0,16},{4,20},{8,24},{12,28},{16,0},{20,4},{24,8},{28,12},{1,17},{... | collective-permute-start | bytes 393224 | tf_op jit(solution)/shard_map/ppermute | solution.py:429
  45.4 7.6 %collective-permute-start.19 = (bf16[4,128,128]{2,1,0:T(8,128)(2,1)S(1)}, bf16[4,128,128]{2,1,0:T(8,128)(2,1)S(1)}, u32[]{:S(2)}, u32[]{:S(2)}) collective-permute-start(bf16[4,128,128]{2,1,0:T(8,128)(2,1)S(1)} %get-tuple-element.63), channel_id=1, source_target_pairs={{0,24},{4,28},{8,16},{12,20},{16,8},{20,12},{24,0},{28,4},{1,25},{... | collective-permute-start | bytes 393224 | tf_op jit(solution)/shard_map/ppermute | solution.py:429

commit v8 on v7

--- a/solution.py
+++ b/solution.py
@@ -119,49 +119,50 @@
     return groups
 
 
+def split(x):
+    high = x.astype(BF16).astype(F32)
+    rest = x - high
+    middle = rest.astype(BF16).astype(F32)
+    low = rest - middle
+    return (high + pltpu.roll(middle, 2 * HEADS, 1) + pltpu.roll(low, 4 * HEADS, 1)).astype(BF16)
+
+
+def join(ref):
+    x = ref[ref.shape[0] - 1].astype(F32)
+    x = x + (pltpu.roll(x, LANES - 2 * HEADS, 1) + pltpu.roll(x, LANES - 4 * HEADS, 1))
+    return jnp.where(lanes_of(x.shape[0]) < 2 * HEADS, x, 0.0)
+
+
 def pick_kernel(n_i, slots, *refs):
     sources, refs = refs[:4], refs[4:]
     mids, refs = refs[:n_i], refs[n_i:]
     fulls, refs = refs[:slots], refs[slots:]
-    buffers, sems, wide, picked = refs
+    stats_ref, buffers, sems, wide, picked, turn = refs
     rows = sources[0].shape[0]
     quarter = rows // DILATION
     pos, chip = position(slots)
+    turn[...] = jnp.zeros_like(turn)
     for group, copies in enumerate(fetch(sources, buffers, sems)):
         for which, copy in enumerate(copies):
             copy.wait()
             for residue in range(DILATION):
                 head = group * DILATION + residue
-                cols = static_columns(head)
-                wide[which, head] = buffers[which, :, cols].astype(F32)
+                wide[which, head] = buffers[which, :, static_columns(head)].astype(F32)
                 rowset = wide[which, head, pl.ds(residue, quarter, stride=DILATION), :]
-                picked[which, :, cols] = rowset.astype(BF16)
-    width = slots * HEAD_DIM
-    for d in range(n_i):
-        start = pl.multiple_of((pos ^ d) * width, width)
-        mids[d][...] = picked[:, :, pl.ds(start, width)]
-    for m in range(slots):
-        fulls[m][...] = buffers[:, :, head_columns(pos * slots + (chip ^ m))]
-
-
-def near_operands(ref, group):
-    heads = range(group * DILATION, (group + 1) * DILATION)
-    return [[ref[which, :, static_columns(head)] for which in range(4)] for head in heads]
-
-
-def near_stats_kernel(k_hbm, v_hbm, q_hbm, u_hbm, stats_ref, mid_ref, buffers, sems, turn):
-    rows = q_hbm.shape[0]
-    turn[...] = jnp.zeros_like(turn)
-    for group, copies in enumerate(fetch((k_hbm, v_hbm, q_hbm, u_hbm), buffers, sems)):
-        for copy in copies:
-            copy.wait()
-        for residue, (e, d) in enumerate(level_stats(near_operands(buffers, group))):
-            head = group * DILATION + residue
+                picked[head // slots, which * slots + head % slots] = rowset.astype(BF16)
+        heads = range(group * DILATION, (group + 1) * DILATION)
+        operands = [[buffers[which, :, static_columns(head)] for which in range(4)] for head in heads]
+        for head, (e, d) in zip(heads, level_stats(operands)):
             turn[head : head + 1, :] = e
             turn[HEADS + head : HEADS + head + 1, :] = d
     stats_ref[...] = turn[: 2 * HEADS, :]
     turn[...] = turn[...].T
-    mid_ref[...] = pick_rows(turn, rows)
+    near = split(pick_rows(turn, rows))
+    for d in range(n_i):
+        mids[d][: 4 * slots] = picked[pos ^ d]
+        mids[d][4 * slots] = near
+    for m in range(slots):
+        fulls[m][...] = buffers[:, :, head_columns(pos * slots + (chip ^ m))]
 
 
 def pack_kernel(slots, *refs):
@@ -185,36 +186,31 @@
         xmsg_ref[3 * slots + m : 3 * slots + m + 1, :] = d
 
 
-def middle_operands(mids, slot):
-    cols = static_columns(slot)
-    return [jnp.concatenate([ref[which, :, cols] for ref in mids], axis=0) for which in range(4)]
+def middle_operands(slots, mids, slot):
+    return [
+        jnp.concatenate([ref[which * slots + slot] for ref in mids], axis=0) for which in range(4)
+    ]
 
 
 def middle_stats_kernel(n_i, slots, *refs):
     mids, refs = in_order(refs[:n_i]), refs[n_i:]
-    near_ref, nearmid_ref = refs[:2]
-    refs = refs[2:]
-    zmsgs, refs = refs[:n_i], refs[n_i:]
-    joint_ref, stats_ref, turn, spread = refs
-    quarter = nearmid_ref.shape[0]
+    near_ref, joint_ref, stats_ref, columns_ref, turn, spread = refs
+    rows = near_ref.shape[1]
+    quarter = rows // DILATION
     pos, _ = position(slots)
     turn[...] = jnp.zeros_like(turn)
-    operands = [middle_operands(mids, slot) for slot in range(slots)]
+    operands = [middle_operands(slots, mids, slot) for slot in range(slots)]
     for slot, (e, d) in enumerate(level_stats(operands)):
         turn[slot : slot + 1, :] = e
         turn[slots + slot : slots + slot + 1, :] = d
     stats_ref[...] = turn[: 2 * slots, :]
-    columns = turn[...].T
+    columns_ref[...] = turn[...].T
     lane = lanes_of(quarter)
-    for d in range(n_i):
-        chunk = pltpu.roll(columns[d * quarter : (d + 1) * quarter], 2 * HEADS, 1)
-        zmsgs[d][...] = jnp.where(lane < 2 * HEADS, nearmid_ref[...], chunk)
-    own = columns[:quarter]
     lane_residue = (pos * slots + lane % slots) % DILATION
     blank = jnp.where(lane < slots, LOWEST, 0.0)
     for residue in range(DILATION):
         spread[pl.ds(residue, quarter, stride=DILATION), :] = jnp.where(
-            lane_residue == residue, own, blank
+            lane_residue == residue, columns_ref[:quarter], blank
         )
     across = spread[...].T
     e, d = merge_stats(
@@ -229,50 +225,25 @@
 
 def middle_parts_kernel(n_i, slots, *refs):
     mids, refs = in_order(refs[:n_i]), refs[n_i:]
-    near_ref, stats_ref = refs[:2]
-    refs = refs[2:]
-    zmsgs, refs = refs[:n_i], refs[n_i:]
+    joint_ref, stats_ref, columns_ref = refs[:3]
+    refs = refs[3:]
     xmsgs, refs = refs[:slots], refs[slots:]
-    outs, refs = refs[:n_i], refs[n_i:]
-    final_ref, far, turn, spread = refs
-    quarter = zmsgs[0].shape[0]
-    rows = quarter * DILATION
+    outs, (far, turn, spread) = refs[:n_i], refs[n_i:]
+    rows = joint_ref.shape[1]
+    quarter = rows // DILATION
     pos, chip = position(slots)
-
-    lane = lanes_of(quarter)
-    mid = jnp.zeros((quarter, LANES), F32)
-    for d in range(n_i):
-        place = (pos ^ d) * slots
-        e = pltpu.roll(zmsgs[d][...], (place + LANES - 2 * HEADS) % LANES, 1)
-        de = pltpu.roll(zmsgs[d][...], (place + LANES - HEADS - slots) % LANES, 1)
-        mid = jnp.where((lane >= place) & (lane < place + slots), e, mid)
-        mid = jnp.where((lane >= HEADS + place) & (lane < HEADS + place + slots), de, mid)
-    blank = jnp.where(lane < HEADS, LOWEST, 0.0)
-    for residue in range(DILATION):
-        spread[pl.ds(residue, quarter, stride=DILATION), :] = jnp.where(
-            lane % DILATION == residue, mid, blank
-        )
-    across = spread[...].T
-    far[:HEADS] = jnp.full((HEADS, rows), LOWEST, F32)
-    far[HEADS:] = jnp.zeros((HEADS, rows), F32)
     for m in range(slots):
-        head = pos * slots + (chip ^ m)
-        far[pl.ds(head, 1), :] = xmsgs[m][2 * slots + m : 2 * slots + m + 1, :]
-        far[pl.ds(HEADS + head, 1), :] = xmsgs[m][3 * slots + m : 3 * slots + m + 1, :]
-    e, d = merge_stats(
-        near_ref[:HEADS], near_ref[HEADS:], across[:HEADS], across[HEADS : 2 * HEADS]
-    )
-    e, d = merge_stats(e, d, far[:HEADS], far[HEADS:])
-    final_ref[:HEADS] = e
-    final_ref[HEADS:] = d
-
+        far[pl.ds(chip ^ m, 1), :] = xmsgs[m][2 * slots + m : 2 * slots + m + 1, :]
+        far[pl.ds(slots + (chip ^ m), 1), :] = xmsgs[m][3 * slots + m : 3 * slots + m + 1, :]
+    e, d = merge_stats(joint_ref[:slots], joint_ref[slots:], far[:slots], far[slots:])
     spread[...] = jnp.zeros_like(spread)
-    spread[: 2 * HEADS] = final_ref[...]
+    spread[pl.ds(pos * slots, slots), :] = e
+    spread[pl.ds(HEADS + pos * slots, slots), :] = d
     spread[...] = spread[...].T
     own = pick_rows(spread, rows)
-    turn[...] = jnp.concatenate([own] + [ref[...] for ref in zmsgs[1:]], axis=0).T
+    turn[...] = jnp.concatenate([own] + [join(ref) for ref in mids[1:]], axis=0).T
     owned = lax.broadcasted_iota(jnp.int32, (1, n_i * quarter), 1) < quarter
-    operands = [middle_operands(mids, slot) for slot in range(slots)]
+    operands = [middle_operands(slots, mids, slot) for slot in range(slots)]
     merged = [
         merge_stats(
             turn[pl.ds(pos * slots + slot, 1), :],
@@ -286,31 +257,28 @@
         for which, part in enumerate(parts):
             part = part.astype(BF16)
             for d in range(n_i):
-                outs[d][which, :, static_columns(slot)] = part[d * quarter : (d + 1) * quarter]
+                outs[d][which * slots + slot] = part[d * quarter : (d + 1) * quarter]
+    for d in range(n_i):
+        outs[d][4 * slots] = split(columns_ref[d * quarter : (d + 1) * quarter])
 
 
 def far_parts_kernel(slots, width, *refs):
     fulls, refs = refs[:slots], refs[slots:]
     sibs, refs = refs[: width - 1], refs[width - 1 :]
-    xmsgs, refs = refs[:slots], refs[slots:]
-    final_ref, refs = refs[0], refs[1:]
+    xmsgs, refs = refs[:slots], refs[slots + 1 :]
     outs, refs = refs[:slots], refs[slots:]
     kvouts, refs = refs[: width - 1], refs[width - 1 :]
     weights, score_grads = refs
     rows = fulls[0].shape[1]
-    pos, chip = position(slots)
-    head = pos * slots + chip
+    _, chip = position(slots)
     keys, values = far_keys(fulls, sibs, 0), far_keys(fulls, sibs, 1)
     for m in range(slots):
-        if m == 0:
-            lse, delta = final_ref[pl.ds(head, 1), :], final_ref[pl.ds(HEADS + head, 1), :]
-        else:
-            lse, delta = merge_stats(
-                xmsgs[m][pl.ds(chip, 1), :],
-                xmsgs[m][pl.ds(slots + chip, 1), :],
-                xmsgs[0][2 * slots + m : 2 * slots + m + 1, :],
-                xmsgs[0][3 * slots + m : 3 * slots + m + 1, :],
-            )
+        lse, delta = merge_stats(
+            xmsgs[m][pl.ds(chip, 1), :],
+            xmsgs[m][pl.ds(slots + chip, 1), :],
+            xmsgs[0][2 * slots + m : 2 * slots + m + 1, :],
+            xmsgs[0][3 * slots + m : 3 * slots + m + 1, :],
+        )
         operands = (keys, values, fulls[m][2], fulls[m][3])
         ((p, ds),) = level_weights([operands], [(lse, delta)])
         outs[m][0] = dot_tn(p, values).astype(BF16)
@@ -332,7 +300,7 @@
 
 def far_sum_kernel(slots, *refs):
     own, refs = refs[:slots], refs[slots:]
-    found, outs = refs[:-slots], refs[-slots:]
+    found, outs = refs[: -slots - 1], refs[-slots:]
     for m in range(slots):
         outs[m][:2] = own[m][:2]
         total = own[m][2:].astype(F32)
@@ -341,11 +309,44 @@
         outs[m][2:] = total.astype(BF16)
 
 
-def near_parts_kernel(k_ref, v_ref, q_ref, u_ref, stats_ref, out_ref):
+def near_parts_kernel(n_i, slots, *refs):
+    sources, near_ref, refs = refs[:4], refs[4], refs[5:]
+    mids, refs = in_order(refs[:n_i]), refs[n_i:]
+    xmsgs, (out_ref, stats_ref, spread) = refs[:slots], refs[slots:]
+    rows = near_ref.shape[1]
+    quarter = rows // DILATION
+    pos, chip = position(slots)
+    lane = lanes_of(quarter)
+    mid = jnp.zeros((quarter, LANES), F32)
+    for d in range(n_i):
+        place = (pos ^ d) * slots
+        found = join(mids[d])
+        e = pltpu.roll(found, place, 1)
+        de = pltpu.roll(found, place + HEADS - slots, 1)
+        mid = jnp.where((lane >= place) & (lane < place + slots), e, mid)
+        mid = jnp.where((lane >= HEADS + place) & (lane < HEADS + place + slots), de, mid)
+    blank = jnp.where(lane < HEADS, LOWEST, 0.0)
+    for residue in range(DILATION):
+        spread[pl.ds(residue, quarter, stride=DILATION), :] = jnp.where(
+            lane % DILATION == residue, mid, blank
+        )
+    across = spread[...].T
+    stats_ref[:HEADS] = jnp.full((HEADS, rows), LOWEST, F32)
+    stats_ref[HEADS:] = jnp.zeros((HEADS, rows), F32)
+    for m in range(slots):
+        head = pos * slots + (chip ^ m)
+        stats_ref[pl.ds(head, 1), :] = xmsgs[m][2 * slots + m : 2 * slots + m + 1, :]
+        stats_ref[pl.ds(HEADS + head, 1), :] = xmsgs[m][3 * slots + m : 3 * slots + m + 1, :]
+    e, d = merge_stats(
+        near_ref[:HEADS], near_ref[HEADS:], across[:HEADS], across[HEADS : 2 * HEADS]
+    )
+    e, d = merge_stats(e, d, stats_ref[:HEADS], stats_ref[HEADS:])
+    stats_ref[:HEADS] = e
+    stats_ref[HEADS:] = d
     for group in range(HEADS // DILATION):
         heads = range(group * DILATION, (group + 1) * DILATION)
         operands = [
-            [ref[:, static_columns(head)] for ref in (k_ref, v_ref, q_ref, u_ref)] for head in heads
+            [ref[:, static_columns(head)] for ref in sources] for head in heads
         ]
         stats = [
             (stats_ref[head : head + 1, :], stats_ref[HEADS + head : HEADS + head + 1, :])
@@ -357,8 +358,8 @@
 
 
 def final_kernel(n_i, slots, near_ref, *refs):
-    mids, refs = (refs[0], *refs[n_i - 1 : 0 : -1]), refs[n_i:]
-    fulls, refs = refs[:slots], refs[slots + 1 :]
+    mids, refs = in_order(refs[:n_i]), refs[n_i:]
+    fulls, refs = (refs[0], *refs[slots - 1 : 0 : -1]), refs[slots:]
     outs, (ready, sems) = refs[:4], refs[4:]
     rows = fulls[0].shape[1]
     quarter = rows // DILATION
@@ -369,8 +370,7 @@
     def spread(d, slot):
         head = (pos ^ d) * slots + slot
         place = jnp.where(row == taken + head % DILATION, 1.0, 0.0).astype(BF16)
-        cols = head_columns(slot) if d == 0 else static_columns(slot)
-        picked = jnp.concatenate([mids[d][which, :, cols] for which in range(4)], axis=1)
+        picked = jnp.concatenate([mids[d][which * slots + slot] for which in range(4)], axis=1)
         return head, dot(place, picked)
 
     copies = []
@@ -440,7 +440,7 @@
     unit = 2 * rows * rows * HEAD_DIM
     bind = functools.partial
 
-    mid = SHAPE((4, quarter, slots * HEAD_DIM), BF16)
+    mid = SHAPE((4 * slots + 1, quarter, HEAD_DIM), BF16)
     full = SHAPE((4, rows, HEAD_DIM), BF16)
     half = SHAPE((slots, 2, rows, HEAD_DIM), BF16)
     square = pltpu.VMEM((LANES, rows), F32)
@@ -455,47 +455,36 @@
     def swap_fulls(pieces):
         return [pieces[0]] + [swap(pieces[m], "seqo", n_o, m * width) for m in range(1, slots)]
 
-    buffers = [
-        pltpu.VMEM((4, rows, features), BF16),
-        pltpu.SemaphoreType.DMA((4, HEADS // DILATION)),
-    ]
     pieces = call(
         bind(pick_kernel, n_i, slots),
         "pick",
-        [mid] * n_i + [full] * slots,
-        buffers
-        + [
+        [mid] * n_i + [full] * slots + [stats(2 * HEADS)],
+        [
+            pltpu.VMEM((4, rows, features), BF16),
+            pltpu.SemaphoreType.DMA((4, HEADS // DILATION)),
             pltpu.VMEM((4, HEADS, rows, HEAD_DIM), F32),
-            pltpu.VMEM((4, quarter, features), BF16),
+            pltpu.VMEM((n_i, 4 * slots, quarter, HEAD_DIM), BF16),
+            square,
         ],
-        unit,
+        unit * HEADS * 2,
         sources,
         hbm_in=range(4),
         limit=PICK_LIMIT,
     )
     mids = swap_mids(pieces[:n_i])
-    fulls = swap_fulls(pieces[n_i:])
-
-    near, nearmid = call(
-        near_stats_kernel,
-        "near_stats",
-        [stats(2 * HEADS), stats(quarter, LANES)],
-        buffers + [square],
-        unit * HEADS * 2,
-        sources,
-        hbm_in=range(4),
-        limit=NEAR_LIMIT,
-    )
-    (packed,) = call(bind(pack_kernel, slots), "pack", [half], [], unit, fulls + mids[1:] + [near])
+    fulls = swap_fulls(pieces[n_i : n_i + slots])
+    near = pieces[-1]
+
+    (arrived,) = call(settle_kernel, "arrive", [stats(8)], [], LONG, far_first(mids)[1:])
+    (packed,) = call(bind(pack_kernel, slots), "pack", [half], [], unit, fulls + [arrived])
     sibs = [swap(packed, "seqo", n_o, part) for part in range(1, width)]
-    *zmsgs, joint, middle = call(
+    joint, middle, columns = call(
         bind(middle_stats_kernel, n_i, slots),
         "middle_stats",
-        [SHAPE((quarter, LANES), F32)] * n_i
-        + [stats(2 * slots), stats(2 * slots, n_i * quarter)],
+        [stats(2 * slots), stats(2 * slots, n_i * quarter), stats(n_i * quarter, LANES)],
         [pltpu.VMEM((LANES, n_i * quarter), F32), square],
         unit * slots * 2,
-        far_first(mids) + [near, nearmid],
+        far_first(mids) + [near],
     )
     (xmsg,) = call(
         bind(far_stats_kernel, slots),
@@ -505,20 +494,15 @@
         unit * n_o * slots * 2,
         [joint] + fulls + sibs,
     )
-    zmsgs = swap_mids(zmsgs)
     xmsgs = swap_fulls([xmsg] * slots)
 
-    *midparts, final = call(
+    midparts = call(
         bind(middle_parts_kernel, n_i, slots),
         "middle_parts",
-        [mid] * n_i + [stats(2 * HEADS)],
-        [
-            pltpu.VMEM((2 * HEADS, rows), F32),
-            pltpu.VMEM((LANES, n_i * quarter), F32),
-            square,
-        ],
+        [mid] * n_i,
+        [pltpu.VMEM((2 * slots, rows), F32), pltpu.VMEM((LANES, n_i * quarter), F32), square],
         unit * slots * 6,
-        far_first(mids) + [near, middle] + zmsgs + xmsgs,
+        far_first(mids) + [joint, middle, columns] + xmsgs,
     )
     midparts = swap_mids(midparts)
     farparts = call(
@@ -527,9 +511,10 @@
         [full] * slots + [half] * (width - 1),
         [pltpu.VMEM((n_o * rows, slots * rows), BF16)] * 2,
         unit * n_o * slots * 6,
-        fulls + sibs + xmsgs + [final],
+        fulls + sibs + xmsgs + [midparts[0]],
         cheap=True,
     )
+    (settled,) = call(settle_kernel, "settle", [stats(8)], [], LONG, [xmsg])
     fullparts = call(
         bind(far_sum_kernel, slots),
         "far_sum",
@@ -537,21 +522,19 @@
         [],
         unit,
         list(farparts[:slots])
-        + [swap(x, "seqo", n_o, part + 1) for part, x in enumerate(farparts[slots:])],
+        + [swap(x, "seqo", n_o, part + 1) for part, x in enumerate(farparts[slots:])]
+        + [settled],
         cheap=True,
     )
     fullparts = swap_fulls(fullparts)
 
     (nearparts,) = call(
-        near_parts_kernel,
+        bind(near_parts_kernel, n_i, slots),
         "near_parts",
         [SHAPE((4, HEADS, rows, HEAD_DIM), F32)],
-        [],
+        [pltpu.VMEM((2 * HEADS, rows), F32), square],
         LONG,
-        sources + (final,),
-    )
-    (settled,) = call(
-        settle_kernel, "settle_parts", [stats(8)], [], LONG, midparts[:0:-1]
+        [*sources, near] + far_first(midparts) + xmsgs,
     )
     return call(
         bind(final_kernel, n_i, slots),
@@ -559,7 +542,7 @@
         [SHAPE((rows, features), BF16)] * 4,
         [pltpu.VMEM((4, rows, features), BF16), pltpu.SemaphoreType.DMA((4, n_i))],
         unit * HEADS,
-        [nearparts, midparts[0]] + midparts[:0:-1] + fullparts + [settled],
+        [nearparts] + far_first(midparts) + [fullparts[0]] + fullparts[:0:-1],
         hbm_out=True,
     )
 

time: 54.9 us -> 51.8 us (0.944)
  starting transfers between devices: 25.3 us -> 20.2 us
  waiting for transfers between devices: 14.6 us -> 18.5 us
  Pallas kernels: 14 us -> 12.2 us
    ppermute x20 -> x17, starting transfers between devices: 25.3 us -> 20.2 us  [swap(): return lax.ppermute(x, axis, [(i, i ^ mask) for i in range(n)])]
    ppermute x20 -> x17, waiting for transfers between devices: 14.6 us -> 18.5 us  [swap(): return lax.ppermute(x, axis, [(i, i ^ mask) for i in range(n)])]
    pallas_call x11, Pallas kernels: 14 us -> 12.2 us  [call(): pl.pallas_call(kernel, out_shape=tuple(outs), in_specs=[pl.BlockSpec(memo...]
  transfers between devices with their start and end apart: 20 -> 17, of which waited for: 8 -> 10; matrix products, arithmetic and copies ran while one was open for 0% -> 0% of each run, Pallas kernels for 16% -> 9%
where the time goes in v8:
time: 51.8 us; the launch traced here: 51.7 us
  starting transfers between devices  20.2 us (39%)
  waiting for transfers between devices  18.5 us (36%)
  Pallas kernels  12.2 us (24%)
  between operations  0.78 us (2%)
    ppermute x17, starting transfers between devices, swap(): return lax.ppermute(x, axis, [(i, i ^ mask) for i in range(n)])  20.2 us
    ppermute x17, waiting for transfers between devices, swap(): return lax.ppermute(x, axis, [(i, i ^ mask) for i in range(n)])  18.5 us
    pallas_call x11, Pallas kernels, call(): pl.pallas_call(kernel, out_shape=tuple(outs), in_specs=[pl.BlockSpec(memo...  12.2 us
  transfers between devices with their start and end apart: 17, of which 10 were waited for; matrix products, arithmetic and copies ran while one was open for 0% of the time, Pallas kernels for 9%

profile of v8, /device:TPU:0, one launch (start us, length us, event | category | flops | bytes accessed | tf_op | source)
XLA Modules:
  0.0 51.7 jit_solution(13247508836790278726)
XLA Ops:
  0.6 3.9 %pick.1 = (bf16[17,32,128]{2,1,0:T(8,128)(2,1)S(1)}, bf16[17,32,128]{2,1,0:T(8,128)(2,1)S(1)}, bf16[17,32,128]{2,1,0:T(8,128)(2,1)S(1)}, bf16[17,32,128]{2,1,0:T...) custom-call(bf16[128,2048]{1,0:T(8,128)(2,1)} %refs_0_.3, ...), custom_call_target="tpu_custom_call" | custom-call | flops 134217728 | bytes 3194880 | tf_op jit(solution)/shard_map/pick/pallas_call | solution.py:406
  4.6 3.1 %collective-permute-start = (bf16[17,32,128]{2,1,0:T(8,128)(2,1)S(1)}, bf16[17,32,128]{2,1,0:T(8,128)(2,1)S(1)}, u32[]{:S(2)}, u32[]{:S(2)}) collective-permute-start(bf16[17,32,128]{2,1,0:T(8,128)(2,1)S(1)} %get-tuple-element.31), channel_id=1, source_target_pairs={{0,1},{1,0},{2,3},{3,2},{4,5},{5,4},{6,7},{7,6},{8,9},{9,8},{10,11... | collective-permute-start | bytes 417800 | tf_op jit(solution)/shard_map/ppermute | solution.py:429
  7.7 2.5 %collective-permute-start.1 = (bf16[17,32,128]{2,1,0:T(8,128)(2,1)}, bf16[17,32,128]{2,1,0:T(8,128)(2,1)S(1)}, u32[]{:S(2)}, u32[]{:S(2)}) collective-permute-start(bf16[17,32,128]{2,1,0:T(8,128)(2,1)} %get-tuple-element.32), channel_id=1, source_target_pairs={{0,3},{1,2},{2,1},{3,0},{4,7},{5,6},{6,5},{7,4},{8,11},{9,10},{10,... | collective-permute-start | bytes 417800 | tf_op jit(solution)/shard_map/ppermute | solution.py:429
  10.2 0.1 collective-permute-start.2
  10.3 1.5 %collective-permute-start.3 = (bf16[4,128,128]{2,1,0:T(8,128)(2,1)S(1)}, bf16[4,128,128]{2,1,0:T(8,128)(2,1)S(1)}, u32[]{:S(2)}, u32[]{:S(2)}) collective-permute-start(bf16[4,128,128]{2,1,0:T(8,128)(2,1)S(1)} %get-tuple-element.38), channel_id=1, source_target_pairs={{0,8},{4,12},{8,0},{12,4},{16,24},{20,28},{24,16},{28,20},{1,9},{5... | collective-permute-start | bytes 393224 | tf_op jit(solution)/shard_map/ppermute | solution.py:429
  11.8 1.5 %collective-permute-start.4 = (bf16[4,128,128]{2,1,0:T(8,128)(2,1)S(1)}, bf16[4,128,128]{2,1,0:T(8,128)(2,1)S(1)}, u32[]{:S(2)}, u32[]{:S(2)}) collective-permute-start(bf16[4,128,128]{2,1,0:T(8,128)(2,1)S(1)} %get-tuple-element.39), channel_id=1, source_target_pairs={{0,16},{4,20},{8,24},{12,28},{16,0},{20,4},{24,8},{28,12},{1,17},{... | collective-permute-start | bytes 393224 | tf_op jit(solution)/shard_map/ppermute | solution.py:429
  13.3 0.6 %collective-permute-start.5 = (bf16[4,128,128]{2,1,0:T(8,128)(2,1)S(1)}, bf16[4,128,128]{2,1,0:T(8,128)(2,1)S(1)}, u32[]{:S(2)}, u32[]{:S(2)}) collective-permute-start(bf16[4,128,128]{2,1,0:T(8,128)(2,1)S(1)} %get-tuple-element.40), channel_id=1, source_target_pairs={{0,24},{4,28},{8,16},{12,20},{16,8},{20,12},{24,0},{28,4},{1,25},{... | collective-permute-start | bytes 393224 | tf_op jit(solution)/shard_map/ppermute | solution.py:429
  14.0 3.8 %collective-permute-done.1.refs_2_.refs_1_ = bf16[17,32,128]{2,1,0:T(8,128)(2,1)S(1)} collective-permute-done((bf16[17,32,128]{2,1,0:T(8,128)(2,1)}, bf16[17,32,128]{2,1,0:T(8,128)(2,1)S(1)}, u32[]{:S(2)}, u32[]{:S(2)}) %collective-permute-start.1) | collective-permute-done | bytes 139296 | tf_op jit(solution)/shard_map/ppermute | solution.py:429
  17.8 5.1 %collective-permute-done.2.refs_3_.refs_2_ = bf16[17,32,128]{2,1,0:T(8,128)(2,1)S(1)} collective-permute-done((bf16[17,32,128]{2,1,0:T(8,128)(2,1)S(1)}, bf16[17,32,128]{2,1,0:T(8,128)(2,1)S(1)}, u32[]{:S(2)}, u32[]{:S(2)}) %collective-permute-start.2) | collective-permute-done | bytes 139296 | tf_op jit(solution)/shard_map/ppermute | solution.py:429
  23.0 0.5 middle_stats.1
  23.5 1.0 %collective-permute-done.6.refs_4_ = bf16[4,2,128,128]{3,2,1,0:T(8,128)(2,1)S(1)} collective-permute-done((bf16[4,2,128,128]{3,2,1,0:T(8,128)(2,1)S(1)}, bf16[4,2,128,128]{3,2,1,0:T(8,128)(2,1)S(1)}, u32[]{:S(2)}, u32[]{:S(2)}) %collective-permute-start.6) | collective-permute-done | bytes 262176 | tf_op jit(solution)/shard_map/ppermute | solution.py:429
  24.5 1.1 %far_stats.1.refs_7_.refs_9_.refs_5_.refs_0_ = f32[16,128]{1,0:T(8,128)S(1)} custom-call(f32[8,128]{1,0:T(8,128)S(1)} %get-tuple-element.34.near_ref.refs_4_, bf16[4,128,128]{2,1,0:T(8,128)(2,1)S(1)} %get-tuple-element.37.refs_0_, bf16[4,128,128]{2,1,0:T(8,128)(2,1)S(1)} %collective-permute-done.3.refs_1_, ...), custom_call_target="tpu_custom_call" | custom-call | flops 268435456 | bytes 798720 | tf_op jit(solution)/shard_map/far_stats/pallas_call | solution.py:406
  25.6 2.5 %collective-permute-start.9 = (f32[16,128]{1,0:T(8,128)S(1)}, f32[16,128]{1,0:T(8,128)S(1)}, u32[]{:S(2)}, u32[]{:S(2)}) collective-permute-start(f32[16,128]{1,0:T(8,128)S(1)} %far_stats.1.refs_7_.refs_9_.refs_5_.refs_0_), channel_id=1, source_target_pairs={{0,24},{4,28},{8,16},{12,20},{16,8},{20,12},{24,0},{28,4},{1,25},{... | collective-permute-start | bytes 24584 | tf_op jit(solution)/shard_map/ppermute | solution.py:429
  28.1 0.5 collective-permute-start.8
  28.6 0.5 %collective-permute-start.7 = (f32[16,128]{1,0:T(8,128)S(1)}, f32[16,128]{1,0:T(8,128)S(1)}, u32[]{:S(2)}, u32[]{:S(2)}) collective-permute-start(f32[16,128]{1,0:T(8,128)S(1)} %far_stats.1.refs_7_.refs_9_.refs_5_.refs_0_), channel_id=1, source_target_pairs={{0,8},{4,12},{8,0},{12,4},{16,24},{20,28},{24,16},{28,20},{1,9},{5... | collective-permute-start | bytes 24584 | tf_op jit(solution)/shard_map/ppermute | solution.py:429
  29.2 1.1 %collective-permute-done.9.refs_10_.refs_12_.refs_8_ = f32[16,128]{1,0:T(8,128)S(1)} collective-permute-done((f32[16,128]{1,0:T(8,128)S(1)}, f32[16,128]{1,0:T(8,128)S(1)}, u32[]{:S(2)}, u32[]{:S(2)}) %collective-permute-start.9) | collective-permute-done | bytes 8224 | tf_op jit(solution)/shard_map/ppermute | solution.py:429
  30.2 1.6 %collective-permute-done.8.refs_9_.refs_11_.refs_7_ = f32[16,128]{1,0:T(8,128)S(1)} collective-permute-done((f32[16,128]{1,0:T(8,128)S(1)}, f32[16,128]{1,0:T(8,128)S(1)}, u32[]{:S(2)}, u32[]{:S(2)}) %collective-permute-start.8) | collective-permute-done | bytes 8224 | tf_op jit(solution)/shard_map/ppermute | solution.py:429
  31.8 0.5 collective-permute-done.7.refs_8_.refs_10_.refs_6_
  32.3 0.6 %middle_parts.1 = (bf16[17,32,128]{2,1,0:T(8,128)(2,1)S(1)}, bf16[17,32,128]{2,1,0:T(8,128)(2,1)S(1)}, bf16[17,32,128]{2,1,0:T(8,128)(2,1)S(1)}, bf16[17,32,128]{2,1,0:T(8,128)(2,1)S(1)}) custom-call(bf16[17,32,128]{2,1,0:T(8,128)(2,1)S(1)} %get-tuple-element.30.refs_0_, bf16[17,32,128]{2,1,0:T(8,128)(2,1)S(1)} %collective-permute-done.refs_1_.refs_0_, ...), custom_call_target="tpu_custom_call" | custom-call | flops 100663296 | bytes 1220608 | tf_op jit(solution)/shard_map/middle_parts/pallas_call | solution.py:406
  33.0 2.7 %collective-permute-start.11 = (bf16[17,32,128]{2,1,0:T(8,128)(2,1)S(1)}, bf16[17,32,128]{2,1,0:T(8,128)(2,1)S(1)}, u32[]{:S(2)}, u32[]{:S(2)}) collective-permute-start(bf16[17,32,128]{2,1,0:T(8,128)(2,1)S(1)} %get-tuple-element.43), channel_id=1, source_target_pairs={{0,3},{1,2},{2,1},{3,0},{4,7},{5,6},{6,5},{7,4},{8,11},{9,10},{10,... | collective-permute-start | bytes 417800 | tf_op jit(solution)/shard_map/ppermute | solution.py:429
  35.7 0.8 %collective-permute-start.12 = (bf16[17,32,128]{2,1,0:T(8,128)(2,1)S(1)}, bf16[17,32,128]{2,1,0:T(8,128)(2,1)S(1)}, u32[]{:S(2)}, u32[]{:S(2)}) collective-permute-start(bf16[17,32,128]{2,1,0:T(8,128)(2,1)S(1)} %get-tuple-element.44), channel_id=1, source_target_pairs={{0,2},{1,3},{2,0},{3,1},{4,6},{5,7},{6,4},{7,5},{8,10},{9,11},{10,... | collective-permute-start | bytes 417800 | tf_op jit(solution)/shard_map/ppermute | solution.py:429
  36.4 2.3 %far_parts.1 = (bf16[4,128,128]{2,1,0:T(8,128)(2,1)S(1)}, bf16[4,128,128]{2,1,0:T(8,128)(2,1)S(1)}, bf16[4,128,128]{2,1,0:T(8,128)(2,1)S(1)}, bf16[4,128,128]{2,...) custom-call(bf16[4,128,128]{2,1,0:T(8,128)(2,1)S(1)} %get-tuple-element.37.refs_0_, ...), custom_call_target="tpu_custom_call" | custom-call | flops 1 | bytes 1 | tf_op jit(solution)/shard_map/far_parts/pallas_call | solution.py:406
  38.9 1.5 %collective-permute-done.13.refs_4_ = bf16[4,2,128,128]{3,2,1,0:T(8,128)(2,1)S(1)} collective-permute-done((bf16[4,2,128,128]{3,2,1,0:T(8,128)(2,1)S(1)}, bf16[4,2,128,128]{3,2,1,0:T(8,128)(2,1)S(1)}, u32[]{:S(2)}, u32[]{:S(2)}) %collective-permute-start.13) | collective-permute-done | bytes 262176 | tf_op jit(solution)/shard_map/ppermute | solution.py:429
  40.4 0.1 far_sum.1
  40.5 1.6 %collective-permute-start.14 = (bf16[4,128,128]{2,1,0:T(8,128)(2,1)S(1)}, bf16[4,128,128]{2,1,0:T(8,128)(2,1)S(1)}, u32[]{:S(2)}, u32[]{:S(2)}) collective-permute-start(bf16[4,128,128]{2,1,0:T(8,128)(2,1)S(1)} %get-tuple-element.51), channel_id=1, source_target_pairs={{0,24},{4,28},{8,16},{12,20},{16,8},{20,12},{24,0},{28,4},{1,25},{... | collective-permute-start | bytes 393224 | tf_op jit(solution)/shard_map/ppermute | solution.py:429
  42.0 0.5 collective-permute-start.15
  42.5 1.5 %collective-permute-start.16 = (bf16[4,128,128]{2,1,0:T(8,128)(2,1)S(1)}, bf16[4,128,128]{2,1,0:T(8,128)(2,1)S(1)}, u32[]{:S(2)}, u32[]{:S(2)}) collective-permute-start(bf16[4,128,128]{2,1,0:T(8,128)(2,1)S(1)} %get-tuple-element.53), channel_id=1, source_target_pairs={{0,8},{4,12},{8,0},{12,4},{16,24},{20,28},{24,16},{28,20},{1,9},{5... | collective-permute-start | bytes 393224 | tf_op jit(solution)/shard_map/ppermute | solution.py:429
  44.0 3.1 %collective-permute-done.12.refs_8_.refs_3_ = bf16[17,32,128]{2,1,0:T(8,128)(2,1)S(1)} collective-permute-done((bf16[17,32,128]{2,1,0:T(8,128)(2,1)S(1)}, bf16[17,32,128]{2,1,0:T(8,128)(2,1)S(1)}, u32[]{:S(2)}, u32[]{:S(2)}) %collective-permute-start.12) | collective-permute-done | bytes 139296 | tf_op jit(solution)/shard_map/ppermute | solution.py:429
  47.1 1.9 %near_parts.1.near_ref = f32[4,16,128,128]{3,2,1,0:T(8,128)S(1)} custom-call(bf16[128,2048]{1,0:T(8,128)(2,1)S(1)} %copy-done, bf16[128,2048]{1,0:T(8,128)(2,1)S(1)} %copy-done.1, bf16[128,2048]{1,0:T(8,128)(2,1)S(1)} %copy-done.2, bf16[128,2048]{1,0:T(8,128)(2,1)S(1)} %copy-done.3, f32[32,128]{1,0:T(8,128)S(1)} %get-tuple-element.29.refs_4_, ...), custom_call_target="tpu_custom_call" | custom-call | flops 40000000000 | bytes 6897664 | tf_op jit(solution)/shard_map/near_parts/pallas_call | solution.py:406
  49.0 0.8 %collective-permute-done.15.refs_6_ = bf16[4,128,128]{2,1,0:T(8,128)(2,1)S(1)} collective-permute-done((bf16[4,128,128]{2,1,0:T(8,128)(2,1)S(1)}, bf16[4,128,128]{2,1,0:T(8,128)(2,1)S(1)}, u32[]{:S(2)}, u32[]{:S(2)}) %collective-permute-start.15) | collective-permute-done | bytes 131104 | tf_op jit(solution)/shard_map/ppermute | solution.py:429
  49.8 0.1 collective-permute-done.16.refs_7_
  49.9 1.8 %final.1 = (bf16[128,2048]{1,0:T(8,128)(2,1)}, bf16[128,2048]{1,0:T(8,128)(2,1)}, bf16[128,2048]{1,0:T(8,128)(2,1)}, bf16[128,2048]{1,0:T(8,128)(2,1)}) custom-call(f32[4,16,128,128]{3,2,1,0:T(8,128)S(1)} %near_parts.1.near_ref, bf16[17,32,128]{2,1,0:T(8,128)(2,1)S(1)} %get-tuple-element.41.refs_5_.refs_9_.refs_0_, ...), custom_call_target="tpu_custom_call" | custom-call | flops 67108864 | bytes 7372800 | tf_op jit(solution)/shard_map/final/pallas_call | solution.py:406
  (21 shorter events, 0.3 us)
Async XLA Ops:
  4.6 8.7 %collective-permute-start = (bf16[17,32,128]{2,1,0:T(8,128)(2,1)S(1)}, bf16[17,32,128]{2,1,0:T(8,128)(2,1)S(1)}, u32[]{:S(2)}, u32[]{:S(2)}) collective-permute-start(bf16[17,32,128]{2,1,0:T(8,128)(2,1)S(1)} %get-tuple-element.31), channel_id=1, source_target_pairs={{0,1},{1,0},{2,3},{3,2},{4,5},{5,4},{6,7},{7,6},{8,9},{9,8},{10,11... | collective-permute-start | bytes 417800 | tf_op jit(solution)/shard_map/ppermute | solution.py:429
  7.7 10.1 %collective-permute-start.1 = (bf16[17,32,128]{2,1,0:T(8,128)(2,1)}, bf16[17,32,128]{2,1,0:T(8,128)(2,1)S(1)}, u32[]{:S(2)}, u32[]{:S(2)}) collective-permute-start(bf16[17,32,128]{2,1,0:T(8,128)(2,1)} %get-tuple-element.32), channel_id=1, source_target_pairs={{0,3},{1,2},{2,1},{3,0},{4,7},{5,6},{6,5},{7,4},{8,11},{9,10},{10,... | collective-permute-start | bytes 417800 | tf_op jit(solution)/shard_map/ppermute | solution.py:429
  10.2 12.7 %collective-permute-start.2 = (bf16[17,32,128]{2,1,0:T(8,128)(2,1)S(1)}, bf16[17,32,128]{2,1,0:T(8,128)(2,1)S(1)}, u32[]{:S(2)}, u32[]{:S(2)}) collective-permute-start(bf16[17,32,128]{2,1,0:T(8,128)(2,1)S(1)} %get-tuple-element.33), channel_id=1, source_target_pairs={{0,2},{1,3},{2,0},{3,1},{4,6},{5,7},{6,4},{7,5},{8,10},{9,11},{10,... | collective-permute-start | bytes 417800 | tf_op jit(solution)/shard_map/ppermute | solution.py:429
  10.3 12.6 %collective-permute-start.3 = (bf16[4,128,128]{2,1,0:T(8,128)(2,1)S(1)}, bf16[4,128,128]{2,1,0:T(8,128)(2,1)S(1)}, u32[]{:S(2)}, u32[]{:S(2)}) collective-permute-start(bf16[4,128,128]{2,1,0:T(8,128)(2,1)S(1)} %get-tuple-element.38), channel_id=1, source_target_pairs={{0,8},{4,12},{8,0},{12,4},{16,24},{20,28},{24,16},{28,20},{1,9},{5... | collective-permute-start | bytes 393224 | tf_op jit(solution)/shard_map/ppermute | solution.py:429
  11.8 11.1 %collective-permute-start.4 = (bf16[4,128,128]{2,1,0:T(8,128)(2,1)S(1)}, bf16[4,128,128]{2,1,0:T(8,128)(2,1)S(1)}, u32[]{:S(2)}, u32[]{:S(2)}) collective-permute-start(bf16[4,128,128]{2,1,0:T(8,128)(2,1)S(1)} %get-tuple-element.39), channel_id=1, source_target_pairs={{0,16},{4,20},{8,24},{12,28},{16,0},{20,4},{24,8},{28,12},{1,17},{... | collective-permute-start | bytes 393224 | tf_op jit(solution)/shard_map/ppermute | solution.py:429
  13.3 9.5 %collective-permute-start.5 = (bf16[4,128,128]{2,1,0:T(8,128)(2,1)S(1)}, bf16[4,128,128]{2,1,0:T(8,128)(2,1)S(1)}, u32[]{:S(2)}, u32[]{:S(2)}) collective-permute-start(bf16[4,128,128]{2,1,0:T(8,128)(2,1)S(1)} %get-tuple-element.40), channel_id=1, source_target_pairs={{0,24},{4,28},{8,16},{12,20},{16,8},{20,12},{24,0},{28,4},{1,25},{... | collective-permute-start | bytes 393224 | tf_op jit(solution)/shard_map/ppermute | solution.py:429
  22.9 1.6 %collective-permute-start.6 = (bf16[4,2,128,128]{3,2,1,0:T(8,128)(2,1)S(1)}, bf16[4,2,128,128]{3,2,1,0:T(8,128)(2,1)S(1)}, u32[]{:S(2)}, u32[]{:S(2)}) collective-permute-start(bf16[4,2,128,128]{3,2,1,0:T(8,128)(2,1)S(1)} %pack.1), channel_id=1, source_target_pairs={{0,4},{4,0},{8,12},{12,8},{16,20},{20,16},{24,28},{28,24},{1,5},{5... | collective-permute-start | bytes 786440 | tf_op jit(solution)/shard_map/ppermute | solution.py:429
  25.6 4.6 %collective-permute-start.9 = (f32[16,128]{1,0:T(8,128)S(1)}, f32[16,128]{1,0:T(8,128)S(1)}, u32[]{:S(2)}, u32[]{:S(2)}) collective-permute-start(f32[16,128]{1,0:T(8,128)S(1)} %far_stats.1.refs_7_.refs_9_.refs_5_.refs_0_), channel_id=1, source_target_pairs={{0,24},{4,28},{8,16},{12,20},{16,8},{20,12},{24,0},{28,4},{1,25},{... | collective-permute-start | bytes 24584 | tf_op jit(solution)/shard_map/ppermute | solution.py:429
  28.1 3.7 %collective-permute-start.8 = (f32[16,128]{1,0:T(8,128)S(1)}, f32[16,128]{1,0:T(8,128)S(1)}, u32[]{:S(2)}, u32[]{:S(2)}) collective-permute-start(f32[16,128]{1,0:T(8,128)S(1)} %far_stats.1.refs_7_.refs_9_.refs_5_.refs_0_), channel_id=1, source_target_pairs={{0,16},{4,20},{8,24},{12,28},{16,0},{20,4},{24,8},{28,12},{1,17},{... | collective-permute-start | bytes 24584 | tf_op jit(solution)/shard_map/ppermute | solution.py:429
  28.6 3.7 %collective-permute-start.7 = (f32[16,128]{1,0:T(8,128)S(1)}, f32[16,128]{1,0:T(8,128)S(1)}, u32[]{:S(2)}, u32[]{:S(2)}) collective-permute-start(f32[16,128]{1,0:T(8,128)S(1)} %far_stats.1.refs_7_.refs_9_.refs_5_.refs_0_), channel_id=1, source_target_pairs={{0,8},{4,12},{8,0},{12,4},{16,24},{20,28},{24,16},{28,20},{1,9},{5... | collective-permute-start | bytes 24584 | tf_op jit(solution)/shard_map/ppermute | solution.py:429
  32.9 9.7 %collective-permute-start.10 = (bf16[17,32,128]{2,1,0:T(8,128)(2,1)S(1)}, bf16[17,32,128]{2,1,0:T(8,128)(2,1)S(1)}, u32[]{:S(2)}, u32[]{:S(2)}) collective-permute-start(bf16[17,32,128]{2,1,0:T(8,128)(2,1)S(1)} %get-tuple-element.42), channel_id=1, source_target_pairs={{0,1},{1,0},{2,3},{3,2},{4,5},{5,4},{6,7},{7,6},{8,9},{9,8},{10,11... | collective-permute-start | bytes 417800 | tf_op jit(solution)/shard_map/ppermute | solution.py:429
  33.0 11.1 %collective-permute-start.11 = (bf16[17,32,128]{2,1,0:T(8,128)(2,1)S(1)}, bf16[17,32,128]{2,1,0:T(8,128)(2,1)S(1)}, u32[]{:S(2)}, u32[]{:S(2)}) collective-permute-start(bf16[17,32,128]{2,1,0:T(8,128)(2,1)S(1)} %get-tuple-element.43), channel_id=1, source_target_pairs={{0,3},{1,2},{2,1},{3,0},{4,7},{5,6},{6,5},{7,4},{8,11},{9,10},{10,... | collective-permute-start | bytes 417800 | tf_op jit(solution)/shard_map/ppermute | solution.py:429
  35.7 11.4 %collective-permute-start.12 = (bf16[17,32,128]{2,1,0:T(8,128)(2,1)S(1)}, bf16[17,32,128]{2,1,0:T(8,128)(2,1)S(1)}, u32[]{:S(2)}, u32[]{:S(2)}) collective-permute-start(bf16[17,32,128]{2,1,0:T(8,128)(2,1)S(1)} %get-tuple-element.44), channel_id=1, source_target_pairs={{0,2},{1,3},{2,0},{3,1},{4,6},{5,7},{6,4},{7,5},{8,10},{9,11},{10,... | collective-permute-start | bytes 417800 | tf_op jit(solution)/shard_map/ppermute | solution.py:429
  38.7 8.4 %copy-start = (bf16[128,2048]{1,0:T(8,128)(2,1)S(1)}, bf16[128,2048]{1,0:T(8,128)(2,1)}, u32[]{:S(2)}) copy-start(bf16[128,2048]{1,0:T(8,128)(2,1)} %refs_0_.3) | copy-start | bytes 1572868
  38.8 8.3 %copy-start.1 = (bf16[128,2048]{1,0:T(8,128)(2,1)S(1)}, bf16[128,2048]{1,0:T(8,128)(2,1)}, u32[]{:S(2)}) copy-start(bf16[128,2048]{1,0:T(8,128)(2,1)} %refs_1_.3) | copy-start | bytes 1572868
  38.8 8.3 %copy-start.2 = (bf16[128,2048]{1,0:T(8,128)(2,1)S(1)}, bf16[128,2048]{1,0:T(8,128)(2,1)}, u32[]{:S(2)}) copy-start(bf16[128,2048]{1,0:T(8,128)(2,1)} %refs_2_.3) | copy-start | bytes 1572868
  38.8 8.3 %copy-start.3 = (bf16[128,2048]{1,0:T(8,128)(2,1)S(1)}, bf16[128,2048]{1,0:T(8,128)(2,1)}, u32[]{:S(2)}) copy-start(bf16[128,2048]{1,0:T(8,128)(2,1)} %refs_3_.3) | copy-start | bytes 1572868
  38.8 1.6 %collective-permute-start.13 = (bf16[4,2,128,128]{3,2,1,0:T(8,128)(2,1)S(1)}, bf16[4,2,128,128]{3,2,1,0:T(8,128)(2,1)S(1)}, u32[]{:S(2)}, u32[]{:S(2)}) collective-permute-start(bf16[4,2,128,128]{3,2,1,0:T(8,128)(2,1)S(1)} %get-tuple-element.49), channel_id=1, source_target_pairs={{0,4},{4,0},{8,12},{12,8},{16,20},{20,16},{24,28},{28,24},{1,5},{5... | collective-permute-start | bytes 786440 | tf_op jit(solution)/shard_map/ppermute | solution.py:429
  40.5 8.5 %collective-permute-start.14 = (bf16[4,128,128]{2,1,0:T(8,128)(2,1)S(1)}, bf16[4,128,128]{2,1,0:T(8,128)(2,1)S(1)}, u32[]{:S(2)}, u32[]{:S(2)}) collective-permute-start(bf16[4,128,128]{2,1,0:T(8,128)(2,1)S(1)} %get-tuple-element.51), channel_id=1, source_target_pairs={{0,24},{4,28},{8,16},{12,20},{16,8},{20,12},{24,0},{28,4},{1,25},{... | collective-permute-start | bytes 393224 | tf_op jit(solution)/shard_map/ppermute | solution.py:429
  42.0 7.7 %collective-permute-start.15 = (bf16[4,128,128]{2,1,0:T(8,128)(2,1)S(1)}, bf16[4,128,128]{2,1,0:T(8,128)(2,1)S(1)}, u32[]{:S(2)}, u32[]{:S(2)}) collective-permute-start(bf16[4,128,128]{2,1,0:T(8,128)(2,1)S(1)} %get-tuple-element.52), channel_id=1, source_target_pairs={{0,16},{4,20},{8,24},{12,28},{16,0},{20,4},{24,8},{28,12},{1,17},{... | collective-permute-start | bytes 393224 | tf_op jit(solution)/shard_map/ppermute | solution.py:429
  42.5 7.4 %collective-permute-start.16 = (bf16[4,128,128]{2,1,0:T(8,128)(2,1)S(1)}, bf16[4,128,128]{2,1,0:T(8,128)(2,1)S(1)}, u32[]{:S(2)}, u32[]{:S(2)}) collective-permute-start(bf16[4,128,128]{2,1,0:T(8,128)(2,1)S(1)} %get-tuple-element.53), channel_id=1, source_target_pairs={{0,8},{4,12},{8,0},{12,4},{16,24},{20,28},{24,16},{28,20},{1,9},{5... | collective-permute-start | bytes 393224 | tf_op jit(solution)/shard_map/ppermute | solution.py:429

commit v9 on v8

--- a/solution.py
+++ b/solution.py
@@ -14,6 +14,7 @@
 SCALE = HEAD_DIM**-0.5
 LOWEST = -1e30
 LONG = 4 * 10**10
+SHORT = 2 * 10**9
 VMEM_LIMIT = 32 * 1024 * 1024
 PICK_LIMIT = 53 * 1024 * 1024
 NEAR_LIMIT = 54784 * 1024
@@ -176,14 +177,13 @@
     return jnp.concatenate(blocks + [ref[m, which] for ref in sibs for m in range(len(fulls))], axis=0)
 
 
-def far_stats_kernel(slots, near_ref, *refs):
-    fulls, sibs, xmsg_ref = refs[:slots], refs[slots:-1], refs[-1]
+def far_stats_kernel(slots, *refs):
+    fulls, sibs, stats_ref = refs[:slots], refs[slots:-2], refs[-1]
     keys, values = far_keys(fulls, sibs, 0), far_keys(fulls, sibs, 1)
-    xmsg_ref[: 2 * slots] = near_ref[...]
     for m in range(slots):
         ((e, d),) = level_stats([(keys, values, fulls[m][2], fulls[m][3])])
-        xmsg_ref[2 * slots + m : 2 * slots + m + 1, :] = e
-        xmsg_ref[3 * slots + m : 3 * slots + m + 1, :] = d
+        stats_ref[m : m + 1, :] = e
+        stats_ref[slots + m : slots + m + 1, :] = d
 
 
 def middle_operands(slots, mids, slot):
@@ -193,8 +193,8 @@
 
 
 def middle_stats_kernel(n_i, slots, *refs):
-    mids, refs = in_order(refs[:n_i]), refs[n_i:]
-    near_ref, joint_ref, stats_ref, columns_ref, turn, spread = refs
+    mids, refs = (refs[0], *refs[n_i - 1 : 0 : -1]), refs[n_i:]
+    near_ref, far_ref, xmsg_ref, stats_ref, columns_ref, turn, spread = refs
     rows = near_ref.shape[1]
     quarter = rows // DILATION
     pos, _ = position(slots)
@@ -219,23 +219,26 @@
         across[:slots],
         across[slots : 2 * slots],
     )
-    joint_ref[:slots] = e
-    joint_ref[slots:] = d
+    xmsg_ref[:slots] = e
+    xmsg_ref[slots : 2 * slots] = d
+    xmsg_ref[2 * slots :] = far_ref[...]
 
 
 def middle_parts_kernel(n_i, slots, *refs):
-    mids, refs = in_order(refs[:n_i]), refs[n_i:]
-    joint_ref, stats_ref, columns_ref = refs[:3]
-    refs = refs[3:]
+    mids, refs = (refs[0], *refs[n_i - 1 : 0 : -1]), refs[n_i:]
+    stats_ref, columns_ref = refs[:2]
+    refs = refs[2:]
     xmsgs, refs = refs[:slots], refs[slots:]
     outs, (far, turn, spread) = refs[:n_i], refs[n_i:]
-    rows = joint_ref.shape[1]
+    rows = xmsgs[0].shape[1]
     quarter = rows // DILATION
     pos, chip = position(slots)
     for m in range(slots):
         far[pl.ds(chip ^ m, 1), :] = xmsgs[m][2 * slots + m : 2 * slots + m + 1, :]
         far[pl.ds(slots + (chip ^ m), 1), :] = xmsgs[m][3 * slots + m : 3 * slots + m + 1, :]
-    e, d = merge_stats(joint_ref[:slots], joint_ref[slots:], far[:slots], far[slots:])
+    e, d = merge_stats(
+        xmsgs[0][:slots], xmsgs[0][slots : 2 * slots], far[:slots], far[slots:]
+    )
     spread[...] = jnp.zeros_like(spread)
     spread[pl.ds(pos * slots, slots), :] = e
     spread[pl.ds(HEADS + pos * slots, slots), :] = d
@@ -311,7 +314,7 @@
 
 def near_parts_kernel(n_i, slots, *refs):
     sources, near_ref, refs = refs[:4], refs[4], refs[5:]
-    mids, refs = in_order(refs[:n_i]), refs[n_i:]
+    mids, refs = (refs[0], *refs[n_i - 1 : 0 : -1]), refs[n_i:]
     xmsgs, (out_ref, stats_ref, spread) = refs[:slots], refs[slots:]
     rows = near_ref.shape[1]
     quarter = rows // DILATION
@@ -358,7 +361,7 @@
 
 
 def final_kernel(n_i, slots, near_ref, *refs):
-    mids, refs = in_order(refs[:n_i]), refs[n_i:]
+    mids, refs = (refs[0], *refs[n_i - 1 : 0 : -1]), refs[n_i:]
     fulls, refs = (refs[0], *refs[slots - 1 : 0 : -1]), refs[slots:]
     outs, (ready, sems) = refs[:4], refs[4:]
     rows = fulls[0].shape[1]
@@ -475,24 +478,26 @@
     fulls = swap_fulls(pieces[n_i : n_i + slots])
     near = pieces[-1]
 
-    (arrived,) = call(settle_kernel, "arrive", [stats(8)], [], LONG, far_first(mids)[1:])
-    (packed,) = call(bind(pack_kernel, slots), "pack", [half], [], unit, fulls + [arrived])
+    (settled,) = call(settle_kernel, "far_in", [stats(8)], [], SHORT, [mids[-1]])
+    (settled,) = call(settle_kernel, "chips_back", [stats(8)], [], LONG, [settled])
+    (packed,) = call(bind(pack_kernel, slots), "pack", [half], [], 1, fulls + [settled])
     sibs = [swap(packed, "seqo", n_o, part) for part in range(1, width)]
-    joint, middle, columns = call(
+    (settled,) = call(settle_kernel, "packed_back", [stats(8)], [], LONG, [near])
+    (far,) = call(
+        bind(far_stats_kernel, slots),
+        "far_stats",
+        [stats(2 * slots)],
+        [],
+        1,
+        fulls + sibs + [settled],
+    )
+    xmsg, middle, columns = call(
         bind(middle_stats_kernel, n_i, slots),
         "middle_stats",
-        [stats(2 * slots), stats(2 * slots, n_i * quarter), stats(n_i * quarter, LANES)],
+        [stats(4 * slots), stats(2 * slots, n_i * quarter), stats(n_i * quarter, LANES)],
         [pltpu.VMEM((LANES, n_i * quarter), F32), square],
         unit * slots * 2,
-        far_first(mids) + [near],
-    )
-    (xmsg,) = call(
-        bind(far_stats_kernel, slots),
-        "far_stats",
-        [stats(4 * slots)],
-        [],
-        unit * n_o * slots * 2,
-        [joint] + fulls + sibs,
+        [mids[0]] + mids[:0:-1] + [near, far],
     )
     xmsgs = swap_fulls([xmsg] * slots)
 
@@ -502,7 +507,7 @@
         [mid] * n_i,
         [pltpu.VMEM((2 * slots, rows), F32), pltpu.VMEM((LANES, n_i * quarter), F32), square],
         unit * slots * 6,
-        far_first(mids) + [joint, middle, columns] + xmsgs,
+        [mids[0]] + mids[:0:-1] + [middle, columns] + xmsgs,
     )
     midparts = swap_mids(midparts)
     farparts = call(
@@ -514,16 +519,17 @@
         fulls + sibs + xmsgs + [midparts[0]],
         cheap=True,
     )
-    (settled,) = call(settle_kernel, "settle", [stats(8)], [], LONG, [xmsg])
+    sibparts = [swap(x, "seqo", n_o, part + 1) for part, x in enumerate(farparts[slots:])]
+    (settled,) = call(settle_kernel, "far_back", [stats(8)], [], SHORT, [midparts[-1]])
+    (settled,) = call(settle_kernel, "sib_back", [stats(8)], [], 1, sibparts + [settled])
+    (settled,) = call(settle_kernel, "settle", [stats(8)], [], LONG, [settled])
     fullparts = call(
         bind(far_sum_kernel, slots),
         "far_sum",
         [full] * slots,
         [],
         unit,
-        list(farparts[:slots])
-        + [swap(x, "seqo", n_o, part + 1) for part, x in enumerate(farparts[slots:])]
-        + [settled],
+        list(farparts[:slots]) + sibparts + [settled],
         cheap=True,
     )
     fullparts = swap_fulls(fullparts)
@@ -534,7 +540,7 @@
         [SHAPE((4, HEADS, rows, HEAD_DIM), F32)],
         [pltpu.VMEM((2 * HEADS, rows), F32), square],
         LONG,
-        [*sources, near] + far_first(midparts) + xmsgs,
+        [*sources, near, midparts[0]] + midparts[:0:-1] + xmsgs,
     )
     return call(
         bind(final_kernel, n_i, slots),
@@ -542,7 +548,7 @@
         [SHAPE((rows, features), BF16)] * 4,
         [pltpu.VMEM((4, rows, features), BF16), pltpu.SemaphoreType.DMA((4, n_i))],
         unit * HEADS,
-        [nearparts] + far_first(midparts) + [fullparts[0]] + fullparts[:0:-1],
+        [nearparts, midparts[0]] + midparts[:0:-1] + [fullparts[0]] + fullparts[:0:-1],
         hbm_out=True,
     )
 

time: 51.8 us -> 49.8 us (0.961)
  waiting for transfers between devices: 18.5 us -> 9.63 us
  starting transfers between devices: 20.2 us -> 26.9 us
    ppermute x17, waiting for transfers between devices: 18.5 us -> 9.63 us  [swap(): return lax.ppermute(x, axis, [(i, i ^ mask) for i in range(n)])]
    ppermute x17, starting transfers between devices: 20.2 us -> 26.9 us  [swap(): return lax.ppermute(x, axis, [(i, i ^ mask) for i in range(n)])]
    pallas_call x11 -> x15, Pallas kernels: 12.2 us -> 12.2 us  [call(): pl.pallas_call(kernel, out_shape=tuple(outs), in_specs=[pl.BlockSpec(memo...]
  transfers between devices with their start and end apart: 17 -> 17, of which waited for: 10 -> 8; matrix products, arithmetic and copies ran while one was open for 0% -> 0% of each run, Pallas kernels for 9% -> 11%
where the time goes in v9:
time: 49.8 us; the launch traced here: 49.6 us
  starting transfers between devices  26.9 us (54%)
  Pallas kernels  12.2 us (24%)
  waiting for transfers between devices  9.63 us (19%)
  between operations  0.81 us (2%)
    ppermute x17, starting transfers between devices, swap(): return lax.ppermute(x, axis, [(i, i ^ mask) for i in range(n)])  26.9 us
    pallas_call x15, Pallas kernels, call(): pl.pallas_call(kernel, out_shape=tuple(outs), in_specs=[pl.BlockSpec(memo...  12.2 us
    ppermute x17, waiting for transfers between devices, swap(): return lax.ppermute(x, axis, [(i, i ^ mask) for i in range(n)])  9.63 us
  transfers between devices with their start and end apart: 17, of which 8 were waited for; matrix products, arithmetic and copies ran while one was open for 0% of the time, Pallas kernels for 11%

profile of v9, /device:TPU:0, one launch (start us, length us, event | category | flops | bytes accessed | tf_op | source)
XLA Modules:
  0.0 49.6 jit_solution(4509952035381720697)
XLA Ops:
  0.6 3.9 %pick.1 = (bf16[17,32,128]{2,1,0:T(8,128)(2,1)S(1)}, bf16[17,32,128]{2,1,0:T(8,128)(2,1)S(1)}, bf16[17,32,128]{2,1,0:T(8,128)(2,1)S(1)}, bf16[17,32,128]{2,1,0:T...) custom-call(bf16[128,2048]{1,0:T(8,128)(2,1)} %refs_0_.3, ...), custom_call_target="tpu_custom_call" | custom-call | flops 134217728 | bytes 3194880 | tf_op jit(solution)/shard_map/pick/pallas_call | solution.py:409
  4.6 5.1 %collective-permute-start = (bf16[17,32,128]{2,1,0:T(8,128)(2,1)}, bf16[17,32,128]{2,1,0:T(8,128)(2,1)S(1)}, u32[]{:S(2)}, u32[]{:S(2)}) collective-permute-start(bf16[17,32,128]{2,1,0:T(8,128)(2,1)} %get-tuple-element.31), channel_id=1, source_target_pairs={{0,3},{1,2},{2,1},{3,0},{4,7},{5,6},{6,5},{7,4},{8,11},{9,10},{10,... | collective-permute-start | bytes 417800 | tf_op jit(solution)/shard_map/ppermute | solution.py:432
  9.7 1.5 %collective-permute-start.3 = (bf16[4,128,128]{2,1,0:T(8,128)(2,1)S(1)}, bf16[4,128,128]{2,1,0:T(8,128)(2,1)S(1)}, u32[]{:S(2)}, u32[]{:S(2)}) collective-permute-start(bf16[4,128,128]{2,1,0:T(8,128)(2,1)S(1)} %get-tuple-element.35), channel_id=1, source_target_pairs={{0,8},{4,12},{8,0},{12,4},{16,24},{20,28},{24,16},{28,20},{1,9},{5... | collective-permute-start | bytes 393224 | tf_op jit(solution)/shard_map/ppermute | solution.py:432
  11.2 1.5 %collective-permute-start.4 = (bf16[4,128,128]{2,1,0:T(8,128)(2,1)S(1)}, bf16[4,128,128]{2,1,0:T(8,128)(2,1)S(1)}, u32[]{:S(2)}, u32[]{:S(2)}) collective-permute-start(bf16[4,128,128]{2,1,0:T(8,128)(2,1)S(1)} %get-tuple-element.36), channel_id=1, source_target_pairs={{0,16},{4,20},{8,24},{12,28},{16,0},{20,4},{24,8},{28,12},{1,17},{... | collective-permute-start | bytes 393224 | tf_op jit(solution)/shard_map/ppermute | solution.py:432
  12.7 0.4 collective-permute-start.5
  13.2 0.5 %collective-permute-done.refs_0_.refs_1_ = bf16[17,32,128]{2,1,0:T(8,128)(2,1)S(1)} collective-permute-done((bf16[17,32,128]{2,1,0:T(8,128)(2,1)}, bf16[17,32,128]{2,1,0:T(8,128)(2,1)S(1)}, u32[]{:S(2)}, u32[]{:S(2)}) %collective-permute-start) | collective-permute-done | bytes 139296 | tf_op jit(solution)/shard_map/ppermute | solution.py:432
  13.7 6.5 %collective-permute-start.2 = (bf16[17,32,128]{2,1,0:T(8,128)(2,1)S(1)}, bf16[17,32,128]{2,1,0:T(8,128)(2,1)S(1)}, u32[]{:S(2)}, u32[]{:S(2)}) collective-permute-start(bf16[17,32,128]{2,1,0:T(8,128)(2,1)S(1)} %get-tuple-element.33), channel_id=1, source_target_pairs={{0,1},{1,0},{2,3},{3,2},{4,5},{5,4},{6,7},{7,6},{8,9},{9,8},{10,11... | collective-permute-start | bytes 417800 | tf_op jit(solution)/shard_map/ppermute | solution.py:432
  20.3 0.1 collective-permute-start.6
  20.4 1.5 %collective-permute-done.6.refs_4_ = bf16[4,2,128,128]{3,2,1,0:T(8,128)(2,1)S(1)} collective-permute-done((bf16[4,2,128,128]{3,2,1,0:T(8,128)(2,1)S(1)}, bf16[4,2,128,128]{3,2,1,0:T(8,128)(2,1)S(1)}, u32[]{:S(2)}, u32[]{:S(2)}) %collective-permute-start.6) | collective-permute-done | bytes 262176 | tf_op jit(solution)/shard_map/ppermute | solution.py:432
  21.9 1.1 %far_stats.1.refs_5_ = f32[8,128]{1,0:T(8,128)S(1)} custom-call(bf16[4,128,128]{2,1,0:T(8,128)(2,1)S(1)} %get-tuple-element.34.refs_0_, bf16[4,128,128]{2,1,0:T(8,128)(2,1)S(1)} %collective-permute-done.3.refs_1_, bf16[4,128,128]{2,1,0:T(8,128)(2,1)S(1)} %collective-permute-done.4.refs_2_, bf16[4,128,128]{2,1,0:T(8,128)(2,1)S(1)} %collective-permute-done.5.refs_3_, ...), custom_call_target="tpu_custom_call" | custom-call | flops 1 | bytes 794624 | tf_op jit(solution)/shard_map/far_stats/pallas_call | solution.py:409
  23.0 0.3 collective-permute-done.2.refs_3_
  23.3 0.5 %middle_stats.1 = (f32[16,128]{1,0:T(8,128)S(1)}, f32[8,128]{1,0:T(8,128)S(1)}, f32[128,128]{1,0:T(8,128)S(1)}) custom-call(bf16[17,32,128]{2,1,0:T(8,128)(2,1)S(1)} %get-tuple-element.30.refs_0_, bf16[17,32,128]{2,1,0:T(8,128)(2,1)S(1)} %collective-permute-done.refs_0_.refs_1_, bf16[17,32,128]{2,1,0:T(8,128)(2,1)S(1)} %collective-permute-done.1.refs_2_, ...), custom_call_target="tpu_custom_call" | custom-call | flops 33554432 | bytes 655360 | tf_op jit(solution)/shard_map/middle_stats/pallas_call | solution.py:409
  23.8 2.5 %collective-permute-start.9 = (f32[16,128]{1,0:T(8,128)S(1)}, f32[16,128]{1,0:T(8,128)S(1)}, u32[]{:S(2)}, u32[]{:S(2)}) collective-permute-start(f32[16,128]{1,0:T(8,128)S(1)} %get-tuple-element.40.refs_6_.refs_9_.refs_5_), channel_id=1, source_target_pairs={{0,24},{4,28},{8,16},{12,20},{16,8},{20,12},{24,0},{28,4},{1,25},{... | collective-permute-start | bytes 24584 | tf_op jit(solution)/shard_map/ppermute | solution.py:432
  26.4 0.5 collective-permute-start.8
  26.9 0.5 %collective-permute-start.7 = (f32[16,128]{1,0:T(8,128)S(1)}, f32[16,128]{1,0:T(8,128)S(1)}, u32[]{:S(2)}, u32[]{:S(2)}) collective-permute-start(f32[16,128]{1,0:T(8,128)S(1)} %get-tuple-element.40.refs_6_.refs_9_.refs_5_), channel_id=1, source_target_pairs={{0,8},{4,12},{8,0},{12,4},{16,24},{20,28},{24,16},{28,20},{1,9},{5... | collective-permute-start | bytes 24584 | tf_op jit(solution)/shard_map/ppermute | solution.py:432
  27.4 1.1 %collective-permute-done.9.refs_9_.refs_12_.refs_8_ = f32[16,128]{1,0:T(8,128)S(1)} collective-permute-done((f32[16,128]{1,0:T(8,128)S(1)}, f32[16,128]{1,0:T(8,128)S(1)}, u32[]{:S(2)}, u32[]{:S(2)}) %collective-permute-start.9) | collective-permute-done | bytes 8224 | tf_op jit(solution)/shard_map/ppermute | solution.py:432
  28.5 1.6 %collective-permute-done.8.refs_8_.refs_11_.refs_7_ = f32[16,128]{1,0:T(8,128)S(1)} collective-permute-done((f32[16,128]{1,0:T(8,128)S(1)}, f32[16,128]{1,0:T(8,128)S(1)}, u32[]{:S(2)}, u32[]{:S(2)}) %collective-permute-start.8) | collective-permute-done | bytes 8224 | tf_op jit(solution)/shard_map/ppermute | solution.py:432
  30.0 0.5 collective-permute-done.7.refs_7_.refs_10_.refs_6_
  30.5 0.6 %middle_parts.1 = (bf16[17,32,128]{2,1,0:T(8,128)(2,1)S(1)}, bf16[17,32,128]{2,1,0:T(8,128)(2,1)S(1)}, bf16[17,32,128]{2,1,0:T(8,128)(2,1)S(1)}, bf16[17,32,128]{2,1,0:T(8,128)(2,1)S(1)}) custom-call(bf16[17,32,128]{2,1,0:T(8,128)(2,1)S(1)} %get-tuple-element.30.refs_0_, bf16[17,32,128]{2,1,0:T(8,128)(2,1)S(1)} %collective-permute-done.refs_0_.refs_1_, ...), custom_call_target="tpu_custom_call" | custom-call | flops 100663296 | bytes 1216512 | tf_op jit(solution)/shard_map/middle_parts/pallas_call | solution.py:409
  31.1 2.4 %collective-permute-start.10 = (bf16[17,32,128]{2,1,0:T(8,128)(2,1)S(1)}, bf16[17,32,128]{2,1,0:T(8,128)(2,1)S(1)}, u32[]{:S(2)}, u32[]{:S(2)}) collective-permute-start(bf16[17,32,128]{2,1,0:T(8,128)(2,1)S(1)} %get-tuple-element.42), channel_id=1, source_target_pairs={{0,3},{1,2},{2,1},{3,0},{4,7},{5,6},{6,5},{7,4},{8,11},{9,10},{10,... | collective-permute-start | bytes 417800 | tf_op jit(solution)/shard_map/ppermute | solution.py:432
  33.5 2.3 %far_parts.1 = (bf16[4,128,128]{2,1,0:T(8,128)(2,1)S(1)}, bf16[4,128,128]{2,1,0:T(8,128)(2,1)S(1)}, bf16[4,128,128]{2,1,0:T(8,128)(2,1)S(1)}, bf16[4,128,128]{2,...) custom-call(bf16[4,128,128]{2,1,0:T(8,128)(2,1)S(1)} %get-tuple-element.34.refs_0_, ...), custom_call_target="tpu_custom_call" | custom-call | flops 1 | bytes 1 | tf_op jit(solution)/shard_map/far_parts/pallas_call | solution.py:409
  35.8 0.1 collective-permute-start.13
  35.9 1.1 %collective-permute-start.11 = (bf16[17,32,128]{2,1,0:T(8,128)(2,1)S(1)}, bf16[17,32,128]{2,1,0:T(8,128)(2,1)S(1)}, u32[]{:S(2)}, u32[]{:S(2)}) collective-permute-start(bf16[17,32,128]{2,1,0:T(8,128)(2,1)S(1)} %get-tuple-element.43), channel_id=1, source_target_pairs={{0,2},{1,3},{2,0},{3,1},{4,6},{5,7},{6,4},{7,5},{8,10},{9,11},{10,... | collective-permute-start | bytes 417800 | tf_op jit(solution)/shard_map/ppermute | solution.py:432
  37.1 1.0 %collective-permute-start.12 = (bf16[17,32,128]{2,1,0:T(8,128)(2,1)S(1)}, bf16[17,32,128]{2,1,0:T(8,128)(2,1)S(1)}, u32[]{:S(2)}, u32[]{:S(2)}) collective-permute-start(bf16[17,32,128]{2,1,0:T(8,128)(2,1)S(1)} %get-tuple-element.44), channel_id=1, source_target_pairs={{0,1},{1,0},{2,3},{3,2},{4,5},{5,4},{6,7},{7,6},{8,9},{9,8},{10,11... | collective-permute-start | bytes 417800 | tf_op jit(solution)/shard_map/ppermute | solution.py:432
  38.0 0.1 collective-permute-done.10.refs_6_.refs_0_.refs_1_
  38.2 0.1 far_sum.1
  38.3 1.6 %collective-permute-start.14 = (bf16[4,128,128]{2,1,0:T(8,128)(2,1)S(1)}, bf16[4,128,128]{2,1,0:T(8,128)(2,1)S(1)}, u32[]{:S(2)}, u32[]{:S(2)}) collective-permute-start(bf16[4,128,128]{2,1,0:T(8,128)(2,1)S(1)} %get-tuple-element.51), channel_id=1, source_target_pairs={{0,24},{4,28},{8,16},{12,20},{16,8},{20,12},{24,0},{28,4},{1,25},{... | collective-permute-start | bytes 393224 | tf_op jit(solution)/shard_map/ppermute | solution.py:432
  39.9 0.5 %collective-permute-start.15 = (bf16[4,128,128]{2,1,0:T(8,128)(2,1)S(1)}, bf16[4,128,128]{2,1,0:T(8,128)(2,1)S(1)}, u32[]{:S(2)}, u32[]{:S(2)}) collective-permute-start(bf16[4,128,128]{2,1,0:T(8,128)(2,1)S(1)} %get-tuple-element.52), channel_id=1, source_target_pairs={{0,16},{4,20},{8,24},{12,28},{16,0},{20,4},{24,8},{28,12},{1,17},{... | collective-permute-start | bytes 393224 | tf_op jit(solution)/shard_map/ppermute | solution.py:432
  40.4 1.5 %collective-permute-start.16 = (bf16[4,128,128]{2,1,0:T(8,128)(2,1)S(1)}, bf16[4,128,128]{2,1,0:T(8,128)(2,1)S(1)}, u32[]{:S(2)}, u32[]{:S(2)}) collective-permute-start(bf16[4,128,128]{2,1,0:T(8,128)(2,1)S(1)} %get-tuple-element.53), channel_id=1, source_target_pairs={{0,8},{4,12},{8,0},{12,4},{16,24},{20,28},{24,16},{28,20},{1,9},{5... | collective-permute-start | bytes 393224 | tf_op jit(solution)/shard_map/ppermute | solution.py:432
  41.9 4.0 %collective-permute-done.11.refs_7_.refs_2_ = bf16[17,32,128]{2,1,0:T(8,128)(2,1)S(1)} collective-permute-done((bf16[17,32,128]{2,1,0:T(8,128)(2,1)S(1)}, bf16[17,32,128]{2,1,0:T(8,128)(2,1)S(1)}, u32[]{:S(2)}, u32[]{:S(2)}) %collective-permute-start.11) | collective-permute-done | bytes 139296 | tf_op jit(solution)/shard_map/ppermute | solution.py:432
  45.9 1.9 %near_parts.1.near_ref = f32[4,16,128,128]{3,2,1,0:T(8,128)S(1)} custom-call(bf16[128,2048]{1,0:T(8,128)(2,1)S(1)} %copy-done, bf16[128,2048]{1,0:T(8,128)(2,1)S(1)} %copy-done.1, bf16[128,2048]{1,0:T(8,128)(2,1)S(1)} %copy-done.2, bf16[128,2048]{1,0:T(8,128)(2,1)S(1)} %copy-done.3, f32[32,128]{1,0:T(8,128)S(1)} %get-tuple-element.29.refs_0_.refs_4_, ...), custom_call_target="tpu_custom_call" | custom-call | flops 40000000000 | bytes 6897664 | tf_op jit(solution)/shard_map/near_parts/pallas_call | solution.py:409
  47.8 1.8 %final.1 = (bf16[128,2048]{1,0:T(8,128)(2,1)}, bf16[128,2048]{1,0:T(8,128)(2,1)}, bf16[128,2048]{1,0:T(8,128)(2,1)}, bf16[128,2048]{1,0:T(8,128)(2,1)}) custom-call(f32[4,16,128,128]{3,2,1,0:T(8,128)S(1)} %near_parts.1.near_ref, bf16[17,32,128]{2,1,0:T(8,128)(2,1)S(1)} %get-tuple-element.41.refs_5_.refs_9_.refs_0_, ...), custom_call_target="tpu_custom_call" | custom-call | flops 67108864 | bytes 7372800 | tf_op jit(solution)/shard_map/final/pallas_call | solution.py:409
  (25 shorter events, 0.1 us)
Async XLA Ops:
  4.6 9.1 %collective-permute-start = (bf16[17,32,128]{2,1,0:T(8,128)(2,1)}, bf16[17,32,128]{2,1,0:T(8,128)(2,1)S(1)}, u32[]{:S(2)}, u32[]{:S(2)}) collective-permute-start(bf16[17,32,128]{2,1,0:T(8,128)(2,1)} %get-tuple-element.31), channel_id=1, source_target_pairs={{0,3},{1,2},{2,1},{3,0},{4,7},{5,6},{6,5},{7,4},{8,11},{9,10},{10,... | collective-permute-start | bytes 417800 | tf_op jit(solution)/shard_map/ppermute | solution.py:432
  9.7 10.5 %collective-permute-start.3 = (bf16[4,128,128]{2,1,0:T(8,128)(2,1)S(1)}, bf16[4,128,128]{2,1,0:T(8,128)(2,1)S(1)}, u32[]{:S(2)}, u32[]{:S(2)}) collective-permute-start(bf16[4,128,128]{2,1,0:T(8,128)(2,1)S(1)} %get-tuple-element.35), channel_id=1, source_target_pairs={{0,8},{4,12},{8,0},{12,4},{16,24},{20,28},{24,16},{28,20},{1,9},{5... | collective-permute-start | bytes 393224 | tf_op jit(solution)/shard_map/ppermute | solution.py:432
  11.2 9.0 %collective-permute-start.4 = (bf16[4,128,128]{2,1,0:T(8,128)(2,1)S(1)}, bf16[4,128,128]{2,1,0:T(8,128)(2,1)S(1)}, u32[]{:S(2)}, u32[]{:S(2)}) collective-permute-start(bf16[4,128,128]{2,1,0:T(8,128)(2,1)S(1)} %get-tuple-element.36), channel_id=1, source_target_pairs={{0,16},{4,20},{8,24},{12,28},{16,0},{20,4},{24,8},{28,12},{1,17},{... | collective-permute-start | bytes 393224 | tf_op jit(solution)/shard_map/ppermute | solution.py:432
  12.7 7.5 %collective-permute-start.5 = (bf16[4,128,128]{2,1,0:T(8,128)(2,1)S(1)}, bf16[4,128,128]{2,1,0:T(8,128)(2,1)S(1)}, u32[]{:S(2)}, u32[]{:S(2)}) collective-permute-start(bf16[4,128,128]{2,1,0:T(8,128)(2,1)S(1)} %get-tuple-element.37), channel_id=1, source_target_pairs={{0,24},{4,28},{8,16},{12,20},{16,8},{20,12},{24,0},{28,4},{1,25},{... | collective-permute-start | bytes 393224 | tf_op jit(solution)/shard_map/ppermute | solution.py:432
  13.2 9.8 %collective-permute-start.1 = (bf16[17,32,128]{2,1,0:T(8,128)(2,1)S(1)}, bf16[17,32,128]{2,1,0:T(8,128)(2,1)S(1)}, u32[]{:S(2)}, u32[]{:S(2)}) collective-permute-start(bf16[17,32,128]{2,1,0:T(8,128)(2,1)S(1)} %get-tuple-element.32), channel_id=1, source_target_pairs={{0,2},{1,3},{2,0},{3,1},{4,6},{5,7},{6,4},{7,5},{8,10},{9,11},{10,... | collective-permute-start | bytes 417800 | tf_op jit(solution)/shard_map/ppermute | solution.py:432
  13.7 9.6 %collective-permute-start.2 = (bf16[17,32,128]{2,1,0:T(8,128)(2,1)S(1)}, bf16[17,32,128]{2,1,0:T(8,128)(2,1)S(1)}, u32[]{:S(2)}, u32[]{:S(2)}) collective-permute-start(bf16[17,32,128]{2,1,0:T(8,128)(2,1)S(1)} %get-tuple-element.33), channel_id=1, source_target_pairs={{0,1},{1,0},{2,3},{3,2},{4,5},{5,4},{6,7},{7,6},{8,9},{9,8},{10,11... | collective-permute-start | bytes 417800 | tf_op jit(solution)/shard_map/ppermute | solution.py:432
  20.3 1.6 %collective-permute-start.6 = (bf16[4,2,128,128]{3,2,1,0:T(8,128)(2,1)S(1)}, bf16[4,2,128,128]{3,2,1,0:T(8,128)(2,1)S(1)}, u32[]{:S(2)}, u32[]{:S(2)}) collective-permute-start(bf16[4,2,128,128]{3,2,1,0:T(8,128)(2,1)S(1)} %pack.1), channel_id=1, source_target_pairs={{0,4},{4,0},{8,12},{12,8},{16,20},{20,16},{24,28},{28,24},{1,5},{5... | collective-permute-start | bytes 786440 | tf_op jit(solution)/shard_map/ppermute | solution.py:432
  23.8 4.6 %collective-permute-start.9 = (f32[16,128]{1,0:T(8,128)S(1)}, f32[16,128]{1,0:T(8,128)S(1)}, u32[]{:S(2)}, u32[]{:S(2)}) collective-permute-start(f32[16,128]{1,0:T(8,128)S(1)} %get-tuple-element.40.refs_6_.refs_9_.refs_5_), channel_id=1, source_target_pairs={{0,24},{4,28},{8,16},{12,20},{16,8},{20,12},{24,0},{28,4},{1,25},{... | collective-permute-start | bytes 24584 | tf_op jit(solution)/shard_map/ppermute | solution.py:432
  26.4 3.7 %collective-permute-start.8 = (f32[16,128]{1,0:T(8,128)S(1)}, f32[16,128]{1,0:T(8,128)S(1)}, u32[]{:S(2)}, u32[]{:S(2)}) collective-permute-start(f32[16,128]{1,0:T(8,128)S(1)} %get-tuple-element.40.refs_6_.refs_9_.refs_5_), channel_id=1, source_target_pairs={{0,16},{4,20},{8,24},{12,28},{16,0},{20,4},{24,8},{28,12},{1,17},{... | collective-permute-start | bytes 24584 | tf_op jit(solution)/shard_map/ppermute | solution.py:432
  26.9 3.7 %collective-permute-start.7 = (f32[16,128]{1,0:T(8,128)S(1)}, f32[16,128]{1,0:T(8,128)S(1)}, u32[]{:S(2)}, u32[]{:S(2)}) collective-permute-start(f32[16,128]{1,0:T(8,128)S(1)} %get-tuple-element.40.refs_6_.refs_9_.refs_5_), channel_id=1, source_target_pairs={{0,8},{4,12},{8,0},{12,4},{16,24},{20,28},{24,16},{28,20},{1,9},{5... | collective-permute-start | bytes 24584 | tf_op jit(solution)/shard_map/ppermute | solution.py:432
  31.1 7.0 %collective-permute-start.10 = (bf16[17,32,128]{2,1,0:T(8,128)(2,1)S(1)}, bf16[17,32,128]{2,1,0:T(8,128)(2,1)S(1)}, u32[]{:S(2)}, u32[]{:S(2)}) collective-permute-start(bf16[17,32,128]{2,1,0:T(8,128)(2,1)S(1)} %get-tuple-element.42), channel_id=1, source_target_pairs={{0,3},{1,2},{2,1},{3,0},{4,7},{5,6},{6,5},{7,4},{8,11},{9,10},{10,... | collective-permute-start | bytes 417800 | tf_op jit(solution)/shard_map/ppermute | solution.py:432
  35.8 2.3 %collective-permute-start.13 = (bf16[4,2,128,128]{3,2,1,0:T(8,128)(2,1)S(1)}, bf16[4,2,128,128]{3,2,1,0:T(8,128)(2,1)S(1)}, u32[]{:S(2)}, u32[]{:S(2)}) collective-permute-start(bf16[4,2,128,128]{3,2,1,0:T(8,128)(2,1)S(1)} %get-tuple-element.49), channel_id=1, source_target_pairs={{0,4},{4,0},{8,12},{12,8},{16,20},{20,16},{24,28},{28,24},{1,5},{5... | collective-permute-start | bytes 786440 | tf_op jit(solution)/shard_map/ppermute | solution.py:432
  35.9 10.0 %collective-permute-start.11 = (bf16[17,32,128]{2,1,0:T(8,128)(2,1)S(1)}, bf16[17,32,128]{2,1,0:T(8,128)(2,1)S(1)}, u32[]{:S(2)}, u32[]{:S(2)}) collective-permute-start(bf16[17,32,128]{2,1,0:T(8,128)(2,1)S(1)} %get-tuple-element.43), channel_id=1, source_target_pairs={{0,2},{1,3},{2,0},{3,1},{4,6},{5,7},{6,4},{7,5},{8,10},{9,11},{10,... | collective-permute-start | bytes 417800 | tf_op jit(solution)/shard_map/ppermute | solution.py:432
  37.1 8.8 %collective-permute-start.12 = (bf16[17,32,128]{2,1,0:T(8,128)(2,1)S(1)}, bf16[17,32,128]{2,1,0:T(8,128)(2,1)S(1)}, u32[]{:S(2)}, u32[]{:S(2)}) collective-permute-start(bf16[17,32,128]{2,1,0:T(8,128)(2,1)S(1)} %get-tuple-element.44), channel_id=1, source_target_pairs={{0,1},{1,0},{2,3},{3,2},{4,5},{5,4},{6,7},{7,6},{8,9},{9,8},{10,11... | collective-permute-start | bytes 417800 | tf_op jit(solution)/shard_map/ppermute | solution.py:432
  38.2 7.7 %copy-start = (bf16[128,2048]{1,0:T(8,128)(2,1)S(1)}, bf16[128,2048]{1,0:T(8,128)(2,1)}, u32[]{:S(2)}) copy-start(bf16[128,2048]{1,0:T(8,128)(2,1)} %refs_0_.3) | copy-start | bytes 1572868
  38.2 7.7 %copy-start.1 = (bf16[128,2048]{1,0:T(8,128)(2,1)S(1)}, bf16[128,2048]{1,0:T(8,128)(2,1)}, u32[]{:S(2)}) copy-start(bf16[128,2048]{1,0:T(8,128)(2,1)} %refs_1_.3) | copy-start | bytes 1572868
  38.2 7.7 %copy-start.2 = (bf16[128,2048]{1,0:T(8,128)(2,1)S(1)}, bf16[128,2048]{1,0:T(8,128)(2,1)}, u32[]{:S(2)}) copy-start(bf16[128,2048]{1,0:T(8,128)(2,1)} %refs_2_.3) | copy-start | bytes 1572868
  38.2 7.7 %copy-start.3 = (bf16[128,2048]{1,0:T(8,128)(2,1)S(1)}, bf16[128,2048]{1,0:T(8,128)(2,1)}, u32[]{:S(2)}) copy-start(bf16[128,2048]{1,0:T(8,128)(2,1)} %refs_3_.3) | copy-start | bytes 1572868
  38.3 9.5 %collective-permute-start.14 = (bf16[4,128,128]{2,1,0:T(8,128)(2,1)S(1)}, bf16[4,128,128]{2,1,0:T(8,128)(2,1)S(1)}, u32[]{:S(2)}, u32[]{:S(2)}) collective-permute-start(bf16[4,128,128]{2,1,0:T(8,128)(2,1)S(1)} %get-tuple-element.51), channel_id=1, source_target_pairs={{0,24},{4,28},{8,16},{12,20},{16,8},{20,12},{24,0},{28,4},{1,25},{... | collective-permute-start | bytes 393224 | tf_op jit(solution)/shard_map/ppermute | solution.py:432
  39.9 7.9 %collective-permute-start.15 = (bf16[4,128,128]{2,1,0:T(8,128)(2,1)S(1)}, bf16[4,128,128]{2,1,0:T(8,128)(2,1)S(1)}, u32[]{:S(2)}, u32[]{:S(2)}) collective-permute-start(bf16[4,128,128]{2,1,0:T(8,128)(2,1)S(1)} %get-tuple-element.52), channel_id=1, source_target_pairs={{0,16},{4,20},{8,24},{12,28},{16,0},{20,4},{24,8},{28,12},{1,17},{... | collective-permute-start | bytes 393224 | tf_op jit(solution)/shard_map/ppermute | solution.py:432
  40.4 7.5 %collective-permute-start.16 = (bf16[4,128,128]{2,1,0:T(8,128)(2,1)S(1)}, bf16[4,128,128]{2,1,0:T(8,128)(2,1)S(1)}, u32[]{:S(2)}, u32[]{:S(2)}) collective-permute-start(bf16[4,128,128]{2,1,0:T(8,128)(2,1)S(1)} %get-tuple-element.53), channel_id=1, source_target_pairs={{0,8},{4,12},{8,0},{12,4},{16,24},{20,28},{24,16},{28,20},{1,9},{5... | collective-permute-start | bytes 393224 | tf_op jit(solution)/shard_map/ppermute | solution.py:432

commit v10 on v9

--- a/solution.py
+++ b/solution.py
@@ -193,7 +193,7 @@
 
 
 def middle_stats_kernel(n_i, slots, *refs):
-    mids, refs = (refs[0], *refs[n_i - 1 : 0 : -1]), refs[n_i:]
+    mids, refs = in_order(refs[:n_i]), refs[n_i:]
     near_ref, far_ref, xmsg_ref, stats_ref, columns_ref, turn, spread = refs
     rows = near_ref.shape[1]
     quarter = rows // DILATION
@@ -225,7 +225,7 @@
 
 
 def middle_parts_kernel(n_i, slots, *refs):
-    mids, refs = (refs[0], *refs[n_i - 1 : 0 : -1]), refs[n_i:]
+    mids, refs = in_order(refs[:n_i]), refs[n_i:]
     stats_ref, columns_ref = refs[:2]
     refs = refs[2:]
     xmsgs, refs = refs[:slots], refs[slots:]
@@ -420,12 +420,12 @@
     )(*operands)
 
 
-def far_first(pieces):
-    return [*pieces[:2], *pieces[:1:-1]]
+def in_turn(pieces):
+    return [pieces[0], pieces[-1], *pieces[1:-1]]
 
 
 def in_order(pieces):
-    return [*pieces[:2], *pieces[:1:-1]]
+    return [pieces[0], *pieces[2:], pieces[1]]
 
 
 def swap(x, axis, n, mask):
@@ -497,7 +497,7 @@
         [stats(4 * slots), stats(2 * slots, n_i * quarter), stats(n_i * quarter, LANES)],
         [pltpu.VMEM((LANES, n_i * quarter), F32), square],
         unit * slots * 2,
-        [mids[0]] + mids[:0:-1] + [near, far],
+        in_turn(mids) + [near, far],
     )
     xmsgs = swap_fulls([xmsg] * slots)
 
@@ -507,7 +507,7 @@
         [mid] * n_i,
         [pltpu.VMEM((2 * slots, rows), F32), pltpu.VMEM((LANES, n_i * quarter), F32), square],
         unit * slots * 6,
-        [mids[0]] + mids[:0:-1] + [middle, columns] + xmsgs,
+        in_turn(mids) + [middle, columns] + xmsgs,
     )
     midparts = swap_mids(midparts)
     farparts = call(

time: 49.8 us -> 48.8 us (0.980)
  starting transfers between devices: 26.9 us -> 23.8 us
  waiting for transfers between devices: 9.63 us -> 11.8 us
    ppermute x17, starting transfers between devices: 26.9 us -> 23.8 us  [swap(): return lax.ppermute(x, axis, [(i, i ^ mask) for i in range(n)])]
    ppermute x17, waiting for transfers between devices: 9.63 us -> 11.8 us  [swap(): return lax.ppermute(x, axis, [(i, i ^ mask) for i in range(n)])]
  transfers between devices with their start and end apart: 17 -> 17, of which waited for: 8 -> 11; matrix products, arithmetic and copies ran while one was open for 0% -> 0% of each run, Pallas kernels for 11% -> 11%
where the time goes in v10:
time: 48.8 us; the launch traced here: 48.6 us
  starting transfers between devices  23.8 us (49%)
  Pallas kernels  12.2 us (25%)
  waiting for transfers between devices  11.8 us (24%)
  between operations  0.79 us (2%)
    ppermute x17, starting transfers between devices, swap(): return lax.ppermute(x, axis, [(i, i ^ mask) for i in range(n)])  23.8 us
    pallas_call x15, Pallas kernels, call(): pl.pallas_call(kernel, out_shape=tuple(outs), in_specs=[pl.BlockSpec(memo...  12.2 us
    ppermute x17, waiting for transfers between devices, swap(): return lax.ppermute(x, axis, [(i, i ^ mask) for i in range(n)])  11.8 us
  transfers between devices with their start and end apart: 17, of which 11 were waited for; matrix products, arithmetic and copies ran while one was open for 0% of the time, Pallas kernels for 11%

profile of v10, /device:TPU:0, one launch (start us, length us, event | category | flops | bytes accessed | tf_op | source)
XLA Modules:
  0.0 48.6 jit_solution(144638808890705024)
XLA Ops:
  0.6 3.9 %pick.1 = (bf16[17,32,128]{2,1,0:T(8,128)(2,1)S(1)}, bf16[17,32,128]{2,1,0:T(8,128)(2,1)S(1)}, bf16[17,32,128]{2,1,0:T(8,128)(2,1)S(1)}, bf16[17,32,128]{2,1,0:T...) custom-call(bf16[128,2048]{1,0:T(8,128)(2,1)} %refs_0_.3, ...), custom_call_target="tpu_custom_call" | custom-call | flops 134217728 | bytes 3194880 | tf_op jit(solution)/shard_map/pick/pallas_call | solution.py:409
  4.6 5.1 %collective-permute-start = (bf16[17,32,128]{2,1,0:T(8,128)(2,1)}, bf16[17,32,128]{2,1,0:T(8,128)(2,1)S(1)}, u32[]{:S(2)}, u32[]{:S(2)}) collective-permute-start(bf16[17,32,128]{2,1,0:T(8,128)(2,1)} %get-tuple-element.31), channel_id=1, source_target_pairs={{0,3},{1,2},{2,1},{3,0},{4,7},{5,6},{6,5},{7,4},{8,11},{9,10},{10,... | collective-permute-start | bytes 417800 | tf_op jit(solution)/shard_map/ppermute | solution.py:432
  9.7 1.5 %collective-permute-start.3 = (bf16[4,128,128]{2,1,0:T(8,128)(2,1)S(1)}, bf16[4,128,128]{2,1,0:T(8,128)(2,1)S(1)}, u32[]{:S(2)}, u32[]{:S(2)}) collective-permute-start(bf16[4,128,128]{2,1,0:T(8,128)(2,1)S(1)} %get-tuple-element.35), channel_id=1, source_target_pairs={{0,8},{4,12},{8,0},{12,4},{16,24},{20,28},{24,16},{28,20},{1,9},{5... | collective-permute-start | bytes 393224 | tf_op jit(solution)/shard_map/ppermute | solution.py:432
  11.2 1.5 %collective-permute-start.4 = (bf16[4,128,128]{2,1,0:T(8,128)(2,1)S(1)}, bf16[4,128,128]{2,1,0:T(8,128)(2,1)S(1)}, u32[]{:S(2)}, u32[]{:S(2)}) collective-permute-start(bf16[4,128,128]{2,1,0:T(8,128)(2,1)S(1)} %get-tuple-element.36), channel_id=1, source_target_pairs={{0,16},{4,20},{8,24},{12,28},{16,0},{20,4},{24,8},{28,12},{1,17},{... | collective-permute-start | bytes 393224 | tf_op jit(solution)/shard_map/ppermute | solution.py:432
  12.7 0.4 collective-permute-start.5
  13.2 0.6 %collective-permute-done.refs_0_.refs_1_ = bf16[17,32,128]{2,1,0:T(8,128)(2,1)S(1)} collective-permute-done((bf16[17,32,128]{2,1,0:T(8,128)(2,1)}, bf16[17,32,128]{2,1,0:T(8,128)(2,1)S(1)}, u32[]{:S(2)}, u32[]{:S(2)}) %collective-permute-start) | collective-permute-done | bytes 139296 | tf_op jit(solution)/shard_map/ppermute | solution.py:432
  13.8 3.5 %collective-permute-start.2 = (bf16[17,32,128]{2,1,0:T(8,128)(2,1)S(1)}, bf16[17,32,128]{2,1,0:T(8,128)(2,1)S(1)}, u32[]{:S(2)}, u32[]{:S(2)}) collective-permute-start(bf16[17,32,128]{2,1,0:T(8,128)(2,1)S(1)} %get-tuple-element.33), channel_id=1, source_target_pairs={{0,2},{1,3},{2,0},{3,1},{4,6},{5,7},{6,4},{7,5},{8,10},{9,11},{10,... | collective-permute-start | bytes 417800 | tf_op jit(solution)/shard_map/ppermute | solution.py:432
  17.3 1.7 %collective-permute-done.4.refs_2_ = bf16[4,128,128]{2,1,0:T(8,128)(2,1)S(1)} collective-permute-done((bf16[4,128,128]{2,1,0:T(8,128)(2,1)S(1)}, bf16[4,128,128]{2,1,0:T(8,128)(2,1)S(1)}, u32[]{:S(2)}, u32[]{:S(2)}) %collective-permute-start.4) | collective-permute-done | bytes 131104 | tf_op jit(solution)/shard_map/ppermute | solution.py:432
  19.1 1.5 %collective-permute-done.6.refs_4_ = bf16[4,2,128,128]{3,2,1,0:T(8,128)(2,1)S(1)} collective-permute-done((bf16[4,2,128,128]{3,2,1,0:T(8,128)(2,1)S(1)}, bf16[4,2,128,128]{3,2,1,0:T(8,128)(2,1)S(1)}, u32[]{:S(2)}, u32[]{:S(2)}) %collective-permute-start.6) | collective-permute-done | bytes 262176 | tf_op jit(solution)/shard_map/ppermute | solution.py:432
  20.6 1.1 %far_stats.1.refs_5_ = f32[8,128]{1,0:T(8,128)S(1)} custom-call(bf16[4,128,128]{2,1,0:T(8,128)(2,1)S(1)} %get-tuple-element.34.refs_0_, bf16[4,128,128]{2,1,0:T(8,128)(2,1)S(1)} %collective-permute-done.3.refs_1_, bf16[4,128,128]{2,1,0:T(8,128)(2,1)S(1)} %collective-permute-done.4.refs_2_, bf16[4,128,128]{2,1,0:T(8,128)(2,1)S(1)} %collective-permute-done.5.refs_3_, ...), custom_call_target="tpu_custom_call" | custom-call | flops 1 | bytes 794624 | tf_op jit(solution)/shard_map/far_stats/pallas_call | solution.py:409
  21.7 1.1 %collective-permute-done.2.refs_3_ = bf16[17,32,128]{2,1,0:T(8,128)(2,1)S(1)} collective-permute-done((bf16[17,32,128]{2,1,0:T(8,128)(2,1)S(1)}, bf16[17,32,128]{2,1,0:T(8,128)(2,1)S(1)}, u32[]{:S(2)}, u32[]{:S(2)}) %collective-permute-start.2) | collective-permute-done | bytes 139296 | tf_op jit(solution)/shard_map/ppermute | solution.py:432
  22.8 0.5 %middle_stats.1 = (f32[16,128]{1,0:T(8,128)S(1)}, f32[8,128]{1,0:T(8,128)S(1)}, f32[128,128]{1,0:T(8,128)S(1)}) custom-call(bf16[17,32,128]{2,1,0:T(8,128)(2,1)S(1)} %get-tuple-element.30.refs_0_, bf16[17,32,128]{2,1,0:T(8,128)(2,1)S(1)} %collective-permute-done.refs_0_.refs_1_, bf16[17,32,128]{2,1,0:T(8,128)(2,1)S(1)} %collective-permute-done.1.refs_2_, ...), custom_call_target="tpu_custom_call" | custom-call | flops 33554432 | bytes 655360 | tf_op jit(solution)/shard_map/middle_stats/pallas_call | solution.py:409
  23.3 2.5 %collective-permute-start.9 = (f32[16,128]{1,0:T(8,128)S(1)}, f32[16,128]{1,0:T(8,128)S(1)}, u32[]{:S(2)}, u32[]{:S(2)}) collective-permute-start(f32[16,128]{1,0:T(8,128)S(1)} %get-tuple-element.40.refs_6_.refs_9_.refs_5_), channel_id=1, source_target_pairs={{0,24},{4,28},{8,16},{12,20},{16,8},{20,12},{24,0},{28,4},{1,25},{... | collective-permute-start | bytes 24584 | tf_op jit(solution)/shard_map/ppermute | solution.py:432
  25.9 0.5 collective-permute-start.8
  26.4 0.5 %collective-permute-start.7 = (f32[16,128]{1,0:T(8,128)S(1)}, f32[16,128]{1,0:T(8,128)S(1)}, u32[]{:S(2)}, u32[]{:S(2)}) collective-permute-start(f32[16,128]{1,0:T(8,128)S(1)} %get-tuple-element.40.refs_6_.refs_9_.refs_5_), channel_id=1, source_target_pairs={{0,8},{4,12},{8,0},{12,4},{16,24},{20,28},{24,16},{28,20},{1,9},{5... | collective-permute-start | bytes 24584 | tf_op jit(solution)/shard_map/ppermute | solution.py:432
  26.9 1.1 %collective-permute-done.9.refs_9_.refs_12_.refs_8_ = f32[16,128]{1,0:T(8,128)S(1)} collective-permute-done((f32[16,128]{1,0:T(8,128)S(1)}, f32[16,128]{1,0:T(8,128)S(1)}, u32[]{:S(2)}, u32[]{:S(2)}) %collective-permute-start.9) | collective-permute-done | bytes 8224 | tf_op jit(solution)/shard_map/ppermute | solution.py:432
  28.0 1.6 %collective-permute-done.8.refs_8_.refs_11_.refs_7_ = f32[16,128]{1,0:T(8,128)S(1)} collective-permute-done((f32[16,128]{1,0:T(8,128)S(1)}, f32[16,128]{1,0:T(8,128)S(1)}, u32[]{:S(2)}, u32[]{:S(2)}) %collective-permute-start.8) | collective-permute-done | bytes 8224 | tf_op jit(solution)/shard_map/ppermute | solution.py:432
  29.5 0.5 collective-permute-done.7.refs_7_.refs_10_.refs_6_
  30.0 0.6 %middle_parts.1 = (bf16[17,32,128]{2,1,0:T(8,128)(2,1)S(1)}, bf16[17,32,128]{2,1,0:T(8,128)(2,1)S(1)}, bf16[17,32,128]{2,1,0:T(8,128)(2,1)S(1)}, bf16[17,32,128]{2,1,0:T(8,128)(2,1)S(1)}) custom-call(bf16[17,32,128]{2,1,0:T(8,128)(2,1)S(1)} %get-tuple-element.30.refs_0_, bf16[17,32,128]{2,1,0:T(8,128)(2,1)S(1)} %collective-permute-done.refs_0_.refs_1_, ...), custom_call_target="tpu_custom_call" | custom-call | flops 100663296 | bytes 1216512 | tf_op jit(solution)/shard_map/middle_parts/pallas_call | solution.py:409
  30.6 2.5 %collective-permute-start.10 = (bf16[17,32,128]{2,1,0:T(8,128)(2,1)S(1)}, bf16[17,32,128]{2,1,0:T(8,128)(2,1)S(1)}, u32[]{:S(2)}, u32[]{:S(2)}) collective-permute-start(bf16[17,32,128]{2,1,0:T(8,128)(2,1)S(1)} %get-tuple-element.42), channel_id=1, source_target_pairs={{0,3},{1,2},{2,1},{3,0},{4,7},{5,6},{6,5},{7,4},{8,11},{9,10},{10,... | collective-permute-start | bytes 417800 | tf_op jit(solution)/shard_map/ppermute | solution.py:432
  33.1 2.3 %far_parts.1 = (bf16[4,128,128]{2,1,0:T(8,128)(2,1)S(1)}, bf16[4,128,128]{2,1,0:T(8,128)(2,1)S(1)}, bf16[4,128,128]{2,1,0:T(8,128)(2,1)S(1)}, bf16[4,128,128]{2,...) custom-call(bf16[4,128,128]{2,1,0:T(8,128)(2,1)S(1)} %get-tuple-element.34.refs_0_, ...), custom_call_target="tpu_custom_call" | custom-call | flops 1 | bytes 1 | tf_op jit(solution)/shard_map/far_parts/pallas_call | solution.py:409
  35.6 1.9 %collective-permute-start.12 = (bf16[17,32,128]{2,1,0:T(8,128)(2,1)S(1)}, bf16[17,32,128]{2,1,0:T(8,128)(2,1)S(1)}, u32[]{:S(2)}, u32[]{:S(2)}) collective-permute-start(bf16[17,32,128]{2,1,0:T(8,128)(2,1)S(1)} %get-tuple-element.44), channel_id=1, source_target_pairs={{0,1},{1,0},{2,3},{3,2},{4,5},{5,4},{6,7},{7,6},{8,9},{9,8},{10,11... | collective-permute-start | bytes 417800 | tf_op jit(solution)/shard_map/ppermute | solution.py:432
  37.6 0.1 far_sum.1
  37.7 1.6 %collective-permute-start.14 = (bf16[4,128,128]{2,1,0:T(8,128)(2,1)S(1)}, bf16[4,128,128]{2,1,0:T(8,128)(2,1)S(1)}, u32[]{:S(2)}, u32[]{:S(2)}) collective-permute-start(bf16[4,128,128]{2,1,0:T(8,128)(2,1)S(1)} %get-tuple-element.51), channel_id=1, source_target_pairs={{0,24},{4,28},{8,16},{12,20},{16,8},{20,12},{24,0},{28,4},{1,25},{... | collective-permute-start | bytes 393224 | tf_op jit(solution)/shard_map/ppermute | solution.py:432
  39.3 0.5 %collective-permute-start.15 = (bf16[4,128,128]{2,1,0:T(8,128)(2,1)S(1)}, bf16[4,128,128]{2,1,0:T(8,128)(2,1)S(1)}, u32[]{:S(2)}, u32[]{:S(2)}) collective-permute-start(bf16[4,128,128]{2,1,0:T(8,128)(2,1)S(1)} %get-tuple-element.52), channel_id=1, source_target_pairs={{0,16},{4,20},{8,24},{12,28},{16,0},{20,4},{24,8},{28,12},{1,17},{... | collective-permute-start | bytes 393224 | tf_op jit(solution)/shard_map/ppermute | solution.py:432
  39.8 1.5 %collective-permute-start.16 = (bf16[4,128,128]{2,1,0:T(8,128)(2,1)S(1)}, bf16[4,128,128]{2,1,0:T(8,128)(2,1)S(1)}, u32[]{:S(2)}, u32[]{:S(2)}) collective-permute-start(bf16[4,128,128]{2,1,0:T(8,128)(2,1)S(1)} %get-tuple-element.53), channel_id=1, source_target_pairs={{0,8},{4,12},{8,0},{12,4},{16,24},{20,28},{24,16},{28,20},{1,9},{5... | collective-permute-start | bytes 393224 | tf_op jit(solution)/shard_map/ppermute | solution.py:432
  41.2 3.1 %collective-permute-done.11.refs_7_.refs_2_ = bf16[17,32,128]{2,1,0:T(8,128)(2,1)S(1)} collective-permute-done((bf16[17,32,128]{2,1,0:T(8,128)(2,1)S(1)}, bf16[17,32,128]{2,1,0:T(8,128)(2,1)S(1)}, u32[]{:S(2)}, u32[]{:S(2)}) %collective-permute-start.11) | collective-permute-done | bytes 139296 | tf_op jit(solution)/shard_map/ppermute | solution.py:432
  44.3 0.2 collective-permute-done.12.refs_8_.refs_3_
  44.6 1.9 %near_parts.1.near_ref = f32[4,16,128,128]{3,2,1,0:T(8,128)S(1)} custom-call(bf16[128,2048]{1,0:T(8,128)(2,1)S(1)} %copy-done, bf16[128,2048]{1,0:T(8,128)(2,1)S(1)} %copy-done.1, bf16[128,2048]{1,0:T(8,128)(2,1)S(1)} %copy-done.2, bf16[128,2048]{1,0:T(8,128)(2,1)S(1)} %copy-done.3, f32[32,128]{1,0:T(8,128)S(1)} %get-tuple-element.29.refs_0_.refs_4_, ...), custom_call_target="tpu_custom_call" | custom-call | flops 40000000000 | bytes 6897664 | tf_op jit(solution)/shard_map/near_parts/pallas_call | solution.py:409
  46.5 0.3 collective-permute-done.15.refs_6_
  46.7 0.1 collective-permute-done.16.refs_7_
  46.9 1.8 %final.1 = (bf16[128,2048]{1,0:T(8,128)(2,1)}, bf16[128,2048]{1,0:T(8,128)(2,1)}, bf16[128,2048]{1,0:T(8,128)(2,1)}, bf16[128,2048]{1,0:T(8,128)(2,1)}) custom-call(f32[4,16,128,128]{3,2,1,0:T(8,128)S(1)} %near_parts.1.near_ref, bf16[17,32,128]{2,1,0:T(8,128)(2,1)S(1)} %get-tuple-element.41.refs_5_.refs_9_.refs_0_, ...), custom_call_target="tpu_custom_call" | custom-call | flops 67108864 | bytes 7372800 | tf_op jit(solution)/shard_map/final/pallas_call | solution.py:409
  (25 shorter events, 0.3 us)
Async XLA Ops:
  4.6 9.2 %collective-permute-start = (bf16[17,32,128]{2,1,0:T(8,128)(2,1)}, bf16[17,32,128]{2,1,0:T(8,128)(2,1)S(1)}, u32[]{:S(2)}, u32[]{:S(2)}) collective-permute-start(bf16[17,32,128]{2,1,0:T(8,128)(2,1)} %get-tuple-element.31), channel_id=1, source_target_pairs={{0,3},{1,2},{2,1},{3,0},{4,7},{5,6},{6,5},{7,4},{8,11},{9,10},{10,... | collective-permute-start | bytes 417800 | tf_op jit(solution)/shard_map/ppermute | solution.py:432
  9.7 7.6 %collective-permute-start.3 = (bf16[4,128,128]{2,1,0:T(8,128)(2,1)S(1)}, bf16[4,128,128]{2,1,0:T(8,128)(2,1)S(1)}, u32[]{:S(2)}, u32[]{:S(2)}) collective-permute-start(bf16[4,128,128]{2,1,0:T(8,128)(2,1)S(1)} %get-tuple-element.35), channel_id=1, source_target_pairs={{0,8},{4,12},{8,0},{12,4},{16,24},{20,28},{24,16},{28,20},{1,9},{5... | collective-permute-start | bytes 393224 | tf_op jit(solution)/shard_map/ppermute | solution.py:432
  11.2 7.8 %collective-permute-start.4 = (bf16[4,128,128]{2,1,0:T(8,128)(2,1)S(1)}, bf16[4,128,128]{2,1,0:T(8,128)(2,1)S(1)}, u32[]{:S(2)}, u32[]{:S(2)}) collective-permute-start(bf16[4,128,128]{2,1,0:T(8,128)(2,1)S(1)} %get-tuple-element.36), channel_id=1, source_target_pairs={{0,16},{4,20},{8,24},{12,28},{16,0},{20,4},{24,8},{28,12},{1,17},{... | collective-permute-start | bytes 393224 | tf_op jit(solution)/shard_map/ppermute | solution.py:432
  12.7 6.2 %collective-permute-start.5 = (bf16[4,128,128]{2,1,0:T(8,128)(2,1)S(1)}, bf16[4,128,128]{2,1,0:T(8,128)(2,1)S(1)}, u32[]{:S(2)}, u32[]{:S(2)}) collective-permute-start(bf16[4,128,128]{2,1,0:T(8,128)(2,1)S(1)} %get-tuple-element.37), channel_id=1, source_target_pairs={{0,24},{4,28},{8,16},{12,20},{16,8},{20,12},{24,0},{28,4},{1,25},{... | collective-permute-start | bytes 393224 | tf_op jit(solution)/shard_map/ppermute | solution.py:432
  13.2 8.5 %collective-permute-start.1 = (bf16[17,32,128]{2,1,0:T(8,128)(2,1)S(1)}, bf16[17,32,128]{2,1,0:T(8,128)(2,1)S(1)}, u32[]{:S(2)}, u32[]{:S(2)}) collective-permute-start(bf16[17,32,128]{2,1,0:T(8,128)(2,1)S(1)} %get-tuple-element.32), channel_id=1, source_target_pairs={{0,1},{1,0},{2,3},{3,2},{4,5},{5,4},{6,7},{7,6},{8,9},{9,8},{10,11... | collective-permute-start | bytes 417800 | tf_op jit(solution)/shard_map/ppermute | solution.py:432
  13.8 9.0 %collective-permute-start.2 = (bf16[17,32,128]{2,1,0:T(8,128)(2,1)S(1)}, bf16[17,32,128]{2,1,0:T(8,128)(2,1)S(1)}, u32[]{:S(2)}, u32[]{:S(2)}) collective-permute-start(bf16[17,32,128]{2,1,0:T(8,128)(2,1)S(1)} %get-tuple-element.33), channel_id=1, source_target_pairs={{0,2},{1,3},{2,0},{3,1},{4,6},{5,7},{6,4},{7,5},{8,10},{9,11},{10,... | collective-permute-start | bytes 417800 | tf_op jit(solution)/shard_map/ppermute | solution.py:432
  19.0 1.6 %collective-permute-start.6 = (bf16[4,2,128,128]{3,2,1,0:T(8,128)(2,1)S(1)}, bf16[4,2,128,128]{3,2,1,0:T(8,128)(2,1)S(1)}, u32[]{:S(2)}, u32[]{:S(2)}) collective-permute-start(bf16[4,2,128,128]{3,2,1,0:T(8,128)(2,1)S(1)} %pack.1), channel_id=1, source_target_pairs={{0,4},{4,0},{8,12},{12,8},{16,20},{20,16},{24,28},{28,24},{1,5},{5... | collective-permute-start | bytes 786440 | tf_op jit(solution)/shard_map/ppermute | solution.py:432
  23.3 4.6 %collective-permute-start.9 = (f32[16,128]{1,0:T(8,128)S(1)}, f32[16,128]{1,0:T(8,128)S(1)}, u32[]{:S(2)}, u32[]{:S(2)}) collective-permute-start(f32[16,128]{1,0:T(8,128)S(1)} %get-tuple-element.40.refs_6_.refs_9_.refs_5_), channel_id=1, source_target_pairs={{0,24},{4,28},{8,16},{12,20},{16,8},{20,12},{24,0},{28,4},{1,25},{... | collective-permute-start | bytes 24584 | tf_op jit(solution)/shard_map/ppermute | solution.py:432
  25.9 3.7 %collective-permute-start.8 = (f32[16,128]{1,0:T(8,128)S(1)}, f32[16,128]{1,0:T(8,128)S(1)}, u32[]{:S(2)}, u32[]{:S(2)}) collective-permute-start(f32[16,128]{1,0:T(8,128)S(1)} %get-tuple-element.40.refs_6_.refs_9_.refs_5_), channel_id=1, source_target_pairs={{0,16},{4,20},{8,24},{12,28},{16,0},{20,4},{24,8},{28,12},{1,17},{... | collective-permute-start | bytes 24584 | tf_op jit(solution)/shard_map/ppermute | solution.py:432
  26.4 3.7 %collective-permute-start.7 = (f32[16,128]{1,0:T(8,128)S(1)}, f32[16,128]{1,0:T(8,128)S(1)}, u32[]{:S(2)}, u32[]{:S(2)}) collective-permute-start(f32[16,128]{1,0:T(8,128)S(1)} %get-tuple-element.40.refs_6_.refs_9_.refs_5_), channel_id=1, source_target_pairs={{0,8},{4,12},{8,0},{12,4},{16,24},{20,28},{24,16},{28,20},{1,9},{5... | collective-permute-start | bytes 24584 | tf_op jit(solution)/shard_map/ppermute | solution.py:432
  30.6 6.9 %collective-permute-start.10 = (bf16[17,32,128]{2,1,0:T(8,128)(2,1)S(1)}, bf16[17,32,128]{2,1,0:T(8,128)(2,1)S(1)}, u32[]{:S(2)}, u32[]{:S(2)}) collective-permute-start(bf16[17,32,128]{2,1,0:T(8,128)(2,1)S(1)} %get-tuple-element.42), channel_id=1, source_target_pairs={{0,3},{1,2},{2,1},{3,0},{4,7},{5,6},{6,5},{7,4},{8,11},{9,10},{10,... | collective-permute-start | bytes 417800 | tf_op jit(solution)/shard_map/ppermute | solution.py:432
  35.4 2.1 %collective-permute-start.13 = (bf16[4,2,128,128]{3,2,1,0:T(8,128)(2,1)S(1)}, bf16[4,2,128,128]{3,2,1,0:T(8,128)(2,1)S(1)}, u32[]{:S(2)}, u32[]{:S(2)}) collective-permute-start(bf16[4,2,128,128]{3,2,1,0:T(8,128)(2,1)S(1)} %get-tuple-element.49), channel_id=1, source_target_pairs={{0,4},{4,0},{8,12},{12,8},{16,20},{20,16},{24,28},{28,24},{1,5},{5... | collective-permute-start | bytes 786440 | tf_op jit(solution)/shard_map/ppermute | solution.py:432
  35.5 8.8 %collective-permute-start.11 = (bf16[17,32,128]{2,1,0:T(8,128)(2,1)S(1)}, bf16[17,32,128]{2,1,0:T(8,128)(2,1)S(1)}, u32[]{:S(2)}, u32[]{:S(2)}) collective-permute-start(bf16[17,32,128]{2,1,0:T(8,128)(2,1)S(1)} %get-tuple-element.43), channel_id=1, source_target_pairs={{0,2},{1,3},{2,0},{3,1},{4,6},{5,7},{6,4},{7,5},{8,10},{9,11},{10,... | collective-permute-start | bytes 417800 | tf_op jit(solution)/shard_map/ppermute | solution.py:432
  35.6 9.0 %collective-permute-start.12 = (bf16[17,32,128]{2,1,0:T(8,128)(2,1)S(1)}, bf16[17,32,128]{2,1,0:T(8,128)(2,1)S(1)}, u32[]{:S(2)}, u32[]{:S(2)}) collective-permute-start(bf16[17,32,128]{2,1,0:T(8,128)(2,1)S(1)} %get-tuple-element.44), channel_id=1, source_target_pairs={{0,1},{1,0},{2,3},{3,2},{4,5},{5,4},{6,7},{7,6},{8,9},{9,8},{10,11... | collective-permute-start | bytes 417800 | tf_op jit(solution)/shard_map/ppermute | solution.py:432
  37.6 7.0 %copy-start = (bf16[128,2048]{1,0:T(8,128)(2,1)S(1)}, bf16[128,2048]{1,0:T(8,128)(2,1)}, u32[]{:S(2)}) copy-start(bf16[128,2048]{1,0:T(8,128)(2,1)} %refs_0_.3) | copy-start | bytes 1572868
  37.6 7.0 %copy-start.1 = (bf16[128,2048]{1,0:T(8,128)(2,1)S(1)}, bf16[128,2048]{1,0:T(8,128)(2,1)}, u32[]{:S(2)}) copy-start(bf16[128,2048]{1,0:T(8,128)(2,1)} %refs_1_.3) | copy-start | bytes 1572868
  37.6 7.0 %copy-start.2 = (bf16[128,2048]{1,0:T(8,128)(2,1)S(1)}, bf16[128,2048]{1,0:T(8,128)(2,1)}, u32[]{:S(2)}) copy-start(bf16[128,2048]{1,0:T(8,128)(2,1)} %refs_2_.3) | copy-start | bytes 1572868
  37.6 7.0 %copy-start.3 = (bf16[128,2048]{1,0:T(8,128)(2,1)S(1)}, bf16[128,2048]{1,0:T(8,128)(2,1)}, u32[]{:S(2)}) copy-start(bf16[128,2048]{1,0:T(8,128)(2,1)} %refs_3_.3) | copy-start | bytes 1572868
  37.7 8.8 %collective-permute-start.14 = (bf16[4,128,128]{2,1,0:T(8,128)(2,1)S(1)}, bf16[4,128,128]{2,1,0:T(8,128)(2,1)S(1)}, u32[]{:S(2)}, u32[]{:S(2)}) collective-permute-start(bf16[4,128,128]{2,1,0:T(8,128)(2,1)S(1)} %get-tuple-element.51), channel_id=1, source_target_pairs={{0,24},{4,28},{8,16},{12,20},{16,8},{20,12},{24,0},{28,4},{1,25},{... | collective-permute-start | bytes 393224 | tf_op jit(solution)/shard_map/ppermute | solution.py:432
  39.3 7.5 %collective-permute-start.15 = (bf16[4,128,128]{2,1,0:T(8,128)(2,1)S(1)}, bf16[4,128,128]{2,1,0:T(8,128)(2,1)S(1)}, u32[]{:S(2)}, u32[]{:S(2)}) collective-permute-start(bf16[4,128,128]{2,1,0:T(8,128)(2,1)S(1)} %get-tuple-element.52), channel_id=1, source_target_pairs={{0,16},{4,20},{8,24},{12,28},{16,0},{20,4},{24,8},{28,12},{1,17},{... | collective-permute-start | bytes 393224 | tf_op jit(solution)/shard_map/ppermute | solution.py:432
  39.8 7.1 %collective-permute-start.16 = (bf16[4,128,128]{2,1,0:T(8,128)(2,1)S(1)}, bf16[4,128,128]{2,1,0:T(8,128)(2,1)S(1)}, u32[]{:S(2)}, u32[]{:S(2)}) collective-permute-start(bf16[4,128,128]{2,1,0:T(8,128)(2,1)S(1)} %get-tuple-element.53), channel_id=1, source_target_pairs={{0,8},{4,12},{8,0},{12,4},{16,24},{20,28},{24,16},{28,20},{1,9},{5... | collective-permute-start | bytes 393224 | tf_op jit(solution)/shard_map/ppermute | solution.py:432

commit v11 on v10

--- a/solution.py
+++ b/solution.py
@@ -312,6 +312,71 @@
         outs[m][2:] = total.astype(BF16)
 
 
+def near_statistics(slots, places, near_ref, mids, xmsgs, stats_ref, spread):
+    rows = near_ref.shape[1]
+    quarter = rows // DILATION
+    pos, chip = position(slots)
+    lane = lanes_of(quarter)
+    mid = jnp.zeros((quarter, LANES), F32)
+    for d, ref in zip(places, mids):
+        place = (pos ^ d) * slots
+        found = join(ref)
+        e = pltpu.roll(found, place, 1)
+        de = pltpu.roll(found, place + HEADS - slots, 1)
+        mid = jnp.where((lane >= place) & (lane < place + slots), e, mid)
+        mid = jnp.where((lane >= HEADS + place) & (lane < HEADS + place + slots), de, mid)
+    blank = jnp.where(lane < HEADS, LOWEST, 0.0)
+    for residue in range(DILATION):
+        spread[pl.ds(residue, quarter, stride=DILATION), :] = jnp.where(
+            lane % DILATION == residue, mid, blank
+        )
+    across = spread[...].T
+    e, d = merge_stats(
+        near_ref[:HEADS], near_ref[HEADS:], across[:HEADS], across[HEADS : 2 * HEADS]
+    )
+    if xmsgs:
+        stats_ref[:HEADS] = jnp.full((HEADS, rows), LOWEST, F32)
+        stats_ref[HEADS:] = jnp.zeros((HEADS, rows), F32)
+        for m in range(slots):
+            head = pos * slots + (chip ^ m)
+            stats_ref[pl.ds(head, 1), :] = xmsgs[m][2 * slots + m : 2 * slots + m + 1, :]
+            stats_ref[pl.ds(HEADS + head, 1), :] = xmsgs[m][3 * slots + m : 3 * slots + m + 1, :]
+        e, d = merge_stats(e, d, stats_ref[:HEADS], stats_ref[HEADS:])
+    stats_ref[:HEADS] = e
+    stats_ref[HEADS:] = d
+
+
+def near_place(slots, d, sources, stats_ref):
+    pos, _ = position(slots)
+    heads = [(pos ^ d) * slots + slot for slot in range(slots)]
+    operands = [[ref[:, head_columns(head)] for ref in sources] for head in heads]
+    stats = [(stats_ref[pl.ds(head, 1), :], stats_ref[pl.ds(HEADS + head, 1), :]) for head in heads]
+    return level_parts(operands, stats)
+
+
+def near_early_kernel(n_i, slots, *refs):
+    sources, near_ref, refs = refs[:4], refs[4], refs[5:]
+    mids, refs = refs[: n_i - 1], refs[n_i - 1 :]
+    xmsgs, (out_ref, stats_ref, spread) = refs[:slots], refs[slots:]
+    places = in_turn(list(range(n_i)))[:-1]
+    near_statistics(slots, places, near_ref, mids, xmsgs, stats_ref, spread)
+    for index, d in enumerate(places):
+        for slot, parts in enumerate(near_place(slots, d, sources, stats_ref)):
+            for which, part in enumerate(parts):
+                out_ref[which, index * slots + slot] = part
+
+
+def far_sum_kernel(slots, *refs):
+    own, refs = refs[:slots], refs[slots:]
+    found, outs = refs[: -slots - 1], refs[-slots:]
+    for m in range(slots):
+        outs[m][:2] = own[m][:2]
+        total = own[m][2:].astype(F32)
+        for ref in found:
+            total += ref[m].astype(F32)
+        outs[m][2:] = total.astype(BF16)
+
+
 def near_parts_kernel(n_i, slots, *refs):
     sources, near_ref, refs = refs[:4], refs[4], refs[5:]
     mids, refs = (refs[0], *refs[n_i - 1 : 0 : -1]), refs[n_i:]
@@ -360,48 +425,73 @@
                 out_ref[which, head] = part
 
 
-def final_kernel(n_i, slots, near_ref, *refs):
-    mids, refs = (refs[0], *refs[n_i - 1 : 0 : -1]), refs[n_i:]
-    fulls, refs = (refs[0], *refs[slots - 1 : 0 : -1]), refs[slots:]
-    outs, (ready, sems) = refs[:4], refs[4:]
-    rows = fulls[0].shape[1]
-    quarter = rows // DILATION
-    pos, chip = position(slots)
+def spread_rows(slots, d, slot, ref):
+    quarter = ref.shape[1]
+    rows = quarter * DILATION
+    pos, _ = position(slots)
+    head = (pos ^ d) * slots + slot
     row = lax.broadcasted_iota(jnp.int32, (rows, quarter), 0)
     taken = lax.broadcasted_iota(jnp.int32, (rows, quarter), 1) * DILATION
-
-    def spread(d, slot):
-        head = (pos ^ d) * slots + slot
-        place = jnp.where(row == taken + head % DILATION, 1.0, 0.0).astype(BF16)
-        picked = jnp.concatenate([mids[d][which * slots + slot] for which in range(4)], axis=1)
-        return head, dot(place, picked)
-
+    place = jnp.where(row == taken + head % DILATION, 1.0, 0.0).astype(BF16)
+    return dot(place, jnp.concatenate([ref[which * slots + slot] for which in range(4)], axis=1))
+
+
+def send_place(slots, d, ready, outs, sems):
+    pos, _ = position(slots)
+    width = slots * HEAD_DIM
+    cols = pl.ds(pl.multiple_of((pos ^ d) * width, width), width)
+    copies = [
+        pltpu.make_async_copy(ready.at[which], out.at[:, cols], sems.at[which])
+        for which, out in enumerate(outs)
+    ]
+    for copy in copies:
+        copy.start()
+    return copies
+
+
+def final_others_kernel(n_i, slots, *refs):
+    sources, near_ref, early_ref, refs = refs[:4], refs[4], refs[5], refs[6:]
+    mids, refs = refs[: n_i - 1], refs[n_i - 1 :]
+    outs, (ready, sems, stats_ref, spread) = refs[:4], refs[4:]
+    places = in_turn(list(range(n_i)))[1:]
+    near_statistics(slots, places[-1:], near_ref, mids[-1:], (), stats_ref, spread)
+    late = near_place(slots, places[-1], sources, stats_ref)
     copies = []
-    for d in reversed(range(n_i)):
-        found = [spread(d, chip ^ slot if d == 0 else slot) for slot in range(slots)]
-        for slot, (head, parts) in enumerate(found):
+    for index, d in enumerate(places):
+        found = [spread_rows(slots, d, slot, mids[index]) for slot in range(slots)]
+        for slot, parts in enumerate(found):
             for which in range(4):
-                total = near_ref[which, head] + parts[:, static_columns(which)]
-                if d == 0:
-                    total += fulls[slot][which].astype(F32)
-                ready[which, :, head_columns(head)] = total.astype(BF16)
-        width = slots * HEAD_DIM
-        cols = pl.ds(pl.multiple_of((pos ^ d) * width, width), width)
-        for which, out in enumerate(outs):
-            copy = pltpu.make_async_copy(
-                ready.at[which, :, cols], out.at[:, cols], sems.at[which, d]
-            )
-            copy.start()
-            copies.append(copy)
+                if d == places[-1]:
+                    near = late[slot][which]
+                else:
+                    near = early_ref[which, (index + 1) * slots + slot]
+                total = near + parts[:, static_columns(which)]
+                ready[index, which, :, static_columns(slot)] = total.astype(BF16)
+        copies += send_place(slots, d, ready.at[index], outs, sems.at[index])
     for copy in copies:
         copy.wait()
 
 
+def final_own_kernel(slots, early_ref, mid_ref, *refs):
+    fulls, refs = in_back(refs[:slots]), refs[slots:]
+    outs, (ready, sems) = refs[4:8], refs[8:]
+    _, chip = position(slots)
+    found = [spread_rows(slots, 0, chip ^ m, mid_ref) for m in range(slots)]
+    for m, parts in enumerate(found):
+        slot = chip ^ m
+        for which in range(4):
+            total = early_ref[which, slot] + parts[:, static_columns(which)]
+            total += fulls[m][which].astype(F32)
+            ready[which, :, head_columns(slot)] = total.astype(BF16)
+    for copy in send_place(slots, 0, ready, outs, sems):
+        copy.wait()
+
+
 def settle_kernel(*refs):
     refs[-1][...] = jnp.zeros_like(refs[-1])
 
 
-def call(kernel, name, outs, scratch, flops, operands, hbm_in=(), hbm_out=False, cheap=False, limit=VMEM_LIMIT):
+def call(kernel, name, outs, scratch, flops, operands, hbm_in=(), hbm_out=False, cheap=False, limit=VMEM_LIMIT, aliases=None):
     moved = sum(x.size * x.dtype.itemsize for x in tuple(operands) + tuple(outs))
     if cheap:
         flops, moved = 1, 1
@@ -414,6 +504,7 @@
             pl.BlockSpec(memory_space=pltpu.HBM if hbm_out else pltpu.VMEM) for _ in outs
         ),
         scratch_shapes=scratch,
+        input_output_aliases=aliases or {},
         compiler_params=pltpu.CompilerParams(vmem_limit_bytes=limit),
         cost_estimate=pl.CostEstimate(flops=flops, bytes_accessed=moved, transcendentals=0),
         name=name,
@@ -422,6 +513,10 @@
 
 def in_turn(pieces):
     return [pieces[0], pieces[-1], *pieces[1:-1]]
+
+
+def in_back(pieces):
+    return [pieces[0], *pieces[:0:-1]]
 
 
 def in_order(pieces):
@@ -534,22 +629,40 @@
     )
     fullparts = swap_fulls(fullparts)
 
-    (nearparts,) = call(
-        bind(near_parts_kernel, n_i, slots),
-        "near_parts",
-        [SHAPE((4, HEADS, rows, HEAD_DIM), F32)],
-        [pltpu.VMEM((2 * HEADS, rows), F32), square],
-        LONG,
-        [*sources, near, midparts[0]] + midparts[:0:-1] + xmsgs,
+    back = in_turn(midparts)
+    kept = [pltpu.VMEM((2 * HEADS, rows), F32), square]
+    (early,) = call(
+        bind(near_early_kernel, n_i, slots),
+        "near_early",
+        [SHAPE((4, (n_i - 1) * slots, rows, HEAD_DIM), F32)],
+        kept,
+        SHORT,
+        [*sources, near, *back[:-1], *xmsgs],
+    )
+    whole = [SHAPE((rows, features), BF16)] * 4
+    outs = call(
+        bind(final_others_kernel, n_i, slots),
+        "final_others",
+        whole,
+        [
+            pltpu.VMEM((n_i - 1, 4, rows, slots * HEAD_DIM), BF16),
+            pltpu.SemaphoreType.DMA((n_i - 1, 4)),
+            *kept,
+        ],
+        SHORT // 2,
+        [*sources, near, early, *back[1:]],
+        hbm_out=True,
     )
     return call(
-        bind(final_kernel, n_i, slots),
-        "final",
-        [SHAPE((rows, features), BF16)] * 4,
-        [pltpu.VMEM((4, rows, features), BF16), pltpu.SemaphoreType.DMA((4, n_i))],
-        unit * HEADS,
-        [nearparts, midparts[0]] + midparts[:0:-1] + [fullparts[0]] + fullparts[:0:-1],
+        bind(final_own_kernel, slots),
+        "final_own",
+        whole,
+        [pltpu.VMEM((4, rows, slots * HEAD_DIM), BF16), pltpu.SemaphoreType.DMA((4,))],
+        unit * slots,
+        [early, midparts[0], *in_back(fullparts), *outs],
+        hbm_in=range(2 + slots, 6 + slots),
         hbm_out=True,
+        aliases={2 + slots + which: which for which in range(4)},
     )
 
 

time: 48.8 us -> 48.8 us (level)
  Pallas kernels: 12.2 us -> 13.1 us
  waiting for transfers between devices: 11.8 us -> 10.9 us
    ppermute x17, waiting for transfers between devices: 11.8 us -> 10.9 us  [swap(): return lax.ppermute(x, axis, [(i, i ^ mask) for i in range(n)])]
    pallas_call x15 -> x16, Pallas kernels: 12.2 us -> 13.1 us  [call(): pl.pallas_call(kernel, out_shape=tuple(outs), in_specs=[pl.BlockSpec(memo...]
  transfers between devices with their start and end apart: 17 -> 17, of which waited for: 11 -> 9; matrix products, arithmetic and copies ran while one was open for 0% -> 0% of each run, Pallas kernels for 11% -> 14%
where the time goes in v11:
time: 48.8 us; the launch traced here: 48.6 us
  starting transfers between devices  23.8 us (49%)
  Pallas kernels  13.1 us (27%)
  waiting for transfers between devices  10.9 us (22%)
  between operations  0.81 us (2%)
    ppermute x17, starting transfers between devices, swap(): return lax.ppermute(x, axis, [(i, i ^ mask) for i in range(n)])  23.8 us
    pallas_call x16, Pallas kernels, call(): pl.pallas_call(kernel, out_shape=tuple(outs), in_specs=[pl.BlockSpec(memo...  13.1 us
    ppermute x17, waiting for transfers between devices, swap(): return lax.ppermute(x, axis, [(i, i ^ mask) for i in range(n)])  10.9 us
  transfers between devices with their start and end apart: 17, of which 9 were waited for; matrix products, arithmetic and copies ran while one was open for 0% of the time, Pallas kernels for 14%

profile of v11, /device:TPU:0, one launch (start us, length us, event | category | flops | bytes accessed | tf_op | source)
XLA Modules:
  0.0 48.6 jit_solution(5929982148700483391)
XLA Ops:
  0.6 3.9 %pick.1 = (bf16[17,32,128]{2,1,0:T(8,128)(2,1)S(1)}, bf16[17,32,128]{2,1,0:T(8,128)(2,1)S(1)}, bf16[17,32,128]{2,1,0:T(8,128)(2,1)S(1)}, bf16[17,32,128]{2,1,0:T...) custom-call(bf16[128,2048]{1,0:T(8,128)(2,1)} %refs_0_.5, ...), custom_call_target="tpu_custom_call" | custom-call | flops 134217728 | bytes 3194880 | tf_op jit(solution)/shard_map/pick/pallas_call | solution.py:499
  4.6 5.1 %collective-permute-start = (bf16[17,32,128]{2,1,0:T(8,128)(2,1)}, bf16[17,32,128]{2,1,0:T(8,128)(2,1)S(1)}, u32[]{:S(2)}, u32[]{:S(2)}) collective-permute-start(bf16[17,32,128]{2,1,0:T(8,128)(2,1)} %get-tuple-element.35), channel_id=1, source_target_pairs={{0,3},{1,2},{2,1},{3,0},{4,7},{5,6},{6,5},{7,4},{8,11},{9,10},{10,... | collective-permute-start | bytes 417800 | tf_op jit(solution)/shard_map/ppermute | solution.py:527
  9.7 1.5 %collective-permute-start.3 = (bf16[4,128,128]{2,1,0:T(8,128)(2,1)S(1)}, bf16[4,128,128]{2,1,0:T(8,128)(2,1)S(1)}, u32[]{:S(2)}, u32[]{:S(2)}) collective-permute-start(bf16[4,128,128]{2,1,0:T(8,128)(2,1)S(1)} %get-tuple-element.39), channel_id=1, source_target_pairs={{0,8},{4,12},{8,0},{12,4},{16,24},{20,28},{24,16},{28,20},{1,9},{5... | collective-permute-start | bytes 393224 | tf_op jit(solution)/shard_map/ppermute | solution.py:527
  11.2 1.5 %collective-permute-start.4 = (bf16[4,128,128]{2,1,0:T(8,128)(2,1)S(1)}, bf16[4,128,128]{2,1,0:T(8,128)(2,1)S(1)}, u32[]{:S(2)}, u32[]{:S(2)}) collective-permute-start(bf16[4,128,128]{2,1,0:T(8,128)(2,1)S(1)} %get-tuple-element.40), channel_id=1, source_target_pairs={{0,16},{4,20},{8,24},{12,28},{16,0},{20,4},{24,8},{28,12},{1,17},{... | collective-permute-start | bytes 393224 | tf_op jit(solution)/shard_map/ppermute | solution.py:527
  12.7 0.4 collective-permute-start.5
  13.2 0.6 %collective-permute-done.refs_0_.refs_1_ = bf16[17,32,128]{2,1,0:T(8,128)(2,1)S(1)} collective-permute-done((bf16[17,32,128]{2,1,0:T(8,128)(2,1)}, bf16[17,32,128]{2,1,0:T(8,128)(2,1)S(1)}, u32[]{:S(2)}, u32[]{:S(2)}) %collective-permute-start) | collective-permute-done | bytes 139296 | tf_op jit(solution)/shard_map/ppermute | solution.py:527
  13.8 3.5 %collective-permute-start.2 = (bf16[17,32,128]{2,1,0:T(8,128)(2,1)S(1)}, bf16[17,32,128]{2,1,0:T(8,128)(2,1)S(1)}, u32[]{:S(2)}, u32[]{:S(2)}) collective-permute-start(bf16[17,32,128]{2,1,0:T(8,128)(2,1)S(1)} %get-tuple-element.37), channel_id=1, source_target_pairs={{0,2},{1,3},{2,0},{3,1},{4,6},{5,7},{6,4},{7,5},{8,10},{9,11},{10,... | collective-permute-start | bytes 417800 | tf_op jit(solution)/shard_map/ppermute | solution.py:527
  17.3 1.7 %collective-permute-done.4.refs_2_ = bf16[4,128,128]{2,1,0:T(8,128)(2,1)S(1)} collective-permute-done((bf16[4,128,128]{2,1,0:T(8,128)(2,1)S(1)}, bf16[4,128,128]{2,1,0:T(8,128)(2,1)S(1)}, u32[]{:S(2)}, u32[]{:S(2)}) %collective-permute-start.4) | collective-permute-done | bytes 131104 | tf_op jit(solution)/shard_map/ppermute | solution.py:527
  19.1 1.5 %collective-permute-done.6.refs_4_ = bf16[4,2,128,128]{3,2,1,0:T(8,128)(2,1)S(1)} collective-permute-done((bf16[4,2,128,128]{3,2,1,0:T(8,128)(2,1)S(1)}, bf16[4,2,128,128]{3,2,1,0:T(8,128)(2,1)S(1)}, u32[]{:S(2)}, u32[]{:S(2)}) %collective-permute-start.6) | collective-permute-done | bytes 262176 | tf_op jit(solution)/shard_map/ppermute | solution.py:527
  20.6 1.1 %far_stats.1.refs_5_ = f32[8,128]{1,0:T(8,128)S(1)} custom-call(bf16[4,128,128]{2,1,0:T(8,128)(2,1)S(1)} %get-tuple-element.38.refs_0_, bf16[4,128,128]{2,1,0:T(8,128)(2,1)S(1)} %collective-permute-done.3.refs_1_, bf16[4,128,128]{2,1,0:T(8,128)(2,1)S(1)} %collective-permute-done.4.refs_2_, bf16[4,128,128]{2,1,0:T(8,128)(2,1)S(1)} %collective-permute-done.5.refs_3_, ...), custom_call_target="tpu_custom_call" | custom-call | flops 1 | bytes 794624 | tf_op jit(solution)/shard_map/far_stats/pallas_call | solution.py:499
  21.7 1.1 %collective-permute-done.2.refs_3_ = bf16[17,32,128]{2,1,0:T(8,128)(2,1)S(1)} collective-permute-done((bf16[17,32,128]{2,1,0:T(8,128)(2,1)S(1)}, bf16[17,32,128]{2,1,0:T(8,128)(2,1)S(1)}, u32[]{:S(2)}, u32[]{:S(2)}) %collective-permute-start.2) | collective-permute-done | bytes 139296 | tf_op jit(solution)/shard_map/ppermute | solution.py:527
  22.8 0.5 %middle_stats.1 = (f32[16,128]{1,0:T(8,128)S(1)}, f32[8,128]{1,0:T(8,128)S(1)}, f32[128,128]{1,0:T(8,128)S(1)}) custom-call(bf16[17,32,128]{2,1,0:T(8,128)(2,1)S(1)} %get-tuple-element.34.refs_0_, bf16[17,32,128]{2,1,0:T(8,128)(2,1)S(1)} %collective-permute-done.refs_0_.refs_1_, bf16[17,32,128]{2,1,0:T(8,128)(2,1)S(1)} %collective-permute-done.1.refs_2_, ...), custom_call_target="tpu_custom_call" | custom-call | flops 33554432 | bytes 655360 | tf_op jit(solution)/shard_map/middle_stats/pallas_call | solution.py:499
  23.3 2.5 %collective-permute-start.9 = (f32[16,128]{1,0:T(8,128)S(1)}, f32[16,128]{1,0:T(8,128)S(1)}, u32[]{:S(2)}, u32[]{:S(2)}) collective-permute-start(f32[16,128]{1,0:T(8,128)S(1)} %get-tuple-element.44.refs_6_.refs_8_.refs_5_), channel_id=1, source_target_pairs={{0,24},{4,28},{8,16},{12,20},{16,8},{20,12},{24,0},{28,4},{1,25},{... | collective-permute-start | bytes 24584 | tf_op jit(solution)/shard_map/ppermute | solution.py:527
  25.9 0.5 collective-permute-start.8
  26.4 0.5 %collective-permute-start.7 = (f32[16,128]{1,0:T(8,128)S(1)}, f32[16,128]{1,0:T(8,128)S(1)}, u32[]{:S(2)}, u32[]{:S(2)}) collective-permute-start(f32[16,128]{1,0:T(8,128)S(1)} %get-tuple-element.44.refs_6_.refs_8_.refs_5_), channel_id=1, source_target_pairs={{0,8},{4,12},{8,0},{12,4},{16,24},{20,28},{24,16},{28,20},{1,9},{5... | collective-permute-start | bytes 24584 | tf_op jit(solution)/shard_map/ppermute | solution.py:527
  26.9 1.1 %collective-permute-done.9.refs_9_.refs_11_.refs_8_ = f32[16,128]{1,0:T(8,128)S(1)} collective-permute-done((f32[16,128]{1,0:T(8,128)S(1)}, f32[16,128]{1,0:T(8,128)S(1)}, u32[]{:S(2)}, u32[]{:S(2)}) %collective-permute-start.9) | collective-permute-done | bytes 8224 | tf_op jit(solution)/shard_map/ppermute | solution.py:527
  28.0 1.6 %collective-permute-done.8.refs_8_.refs_10_.refs_7_ = f32[16,128]{1,0:T(8,128)S(1)} collective-permute-done((f32[16,128]{1,0:T(8,128)S(1)}, f32[16,128]{1,0:T(8,128)S(1)}, u32[]{:S(2)}, u32[]{:S(2)}) %collective-permute-start.8) | collective-permute-done | bytes 8224 | tf_op jit(solution)/shard_map/ppermute | solution.py:527
  29.5 0.5 collective-permute-done.7.refs_7_.refs_9_.refs_6_
  30.0 0.6 %middle_parts.1 = (bf16[17,32,128]{2,1,0:T(8,128)(2,1)S(1)}, bf16[17,32,128]{2,1,0:T(8,128)(2,1)S(1)}, bf16[17,32,128]{2,1,0:T(8,128)(2,1)S(1)}, bf16[17,32,128]{2,1,0:T(8,128)(2,1)S(1)}) custom-call(bf16[17,32,128]{2,1,0:T(8,128)(2,1)S(1)} %get-tuple-element.34.refs_0_, bf16[17,32,128]{2,1,0:T(8,128)(2,1)S(1)} %collective-permute-done.refs_0_.refs_1_, ...), custom_call_target="tpu_custom_call" | custom-call | flops 100663296 | bytes 1216512 | tf_op jit(solution)/shard_map/middle_parts/pallas_call | solution.py:499
  30.6 2.5 %collective-permute-start.10 = (bf16[17,32,128]{2,1,0:T(8,128)(2,1)S(1)}, bf16[17,32,128]{2,1,0:T(8,128)(2,1)S(1)}, u32[]{:S(2)}, u32[]{:S(2)}) collective-permute-start(bf16[17,32,128]{2,1,0:T(8,128)(2,1)S(1)} %get-tuple-element.46), channel_id=1, source_target_pairs={{0,3},{1,2},{2,1},{3,0},{4,7},{5,6},{6,5},{7,4},{8,11},{9,10},{10,... | collective-permute-start | bytes 417800 | tf_op jit(solution)/shard_map/ppermute | solution.py:527
  33.1 2.3 %far_parts.1 = (bf16[4,128,128]{2,1,0:T(8,128)(2,1)S(1)}, bf16[4,128,128]{2,1,0:T(8,128)(2,1)S(1)}, bf16[4,128,128]{2,1,0:T(8,128)(2,1)S(1)}, bf16[4,128,128]{2,...) custom-call(bf16[4,128,128]{2,1,0:T(8,128)(2,1)S(1)} %get-tuple-element.38.refs_0_, ...), custom_call_target="tpu_custom_call" | custom-call | flops 1 | bytes 1 | tf_op jit(solution)/shard_map/far_parts/pallas_call | solution.py:499
  35.4 0.1 collective-permute-start.12
  35.6 1.9 %collective-permute-start.16 = (bf16[17,32,128]{2,1,0:T(8,128)(2,1)S(1)}, bf16[17,32,128]{2,1,0:T(8,128)(2,1)S(1)}, u32[]{:S(2)}, u32[]{:S(2)}) collective-permute-start(bf16[17,32,128]{2,1,0:T(8,128)(2,1)S(1)} %get-tuple-element.57), channel_id=1, source_target_pairs={{0,2},{1,3},{2,0},{3,1},{4,6},{5,7},{6,4},{7,5},{8,10},{9,11},{10,... | collective-permute-start | bytes 417800 | tf_op jit(solution)/shard_map/ppermute | solution.py:527
  37.6 0.1 far_sum.1
  37.7 1.6 %collective-permute-start.13 = (bf16[4,128,128]{2,1,0:T(8,128)(2,1)S(1)}, bf16[4,128,128]{2,1,0:T(8,128)(2,1)S(1)}, u32[]{:S(2)}, u32[]{:S(2)}) collective-permute-start(bf16[4,128,128]{2,1,0:T(8,128)(2,1)S(1)} %get-tuple-element.54), channel_id=1, source_target_pairs={{0,24},{4,28},{8,16},{12,20},{16,8},{20,12},{24,0},{28,4},{1,25},{... | collective-permute-start | bytes 393224 | tf_op jit(solution)/shard_map/ppermute | solution.py:527
  39.2 0.5 %collective-permute-start.14 = (bf16[4,128,128]{2,1,0:T(8,128)(2,1)S(1)}, bf16[4,128,128]{2,1,0:T(8,128)(2,1)S(1)}, u32[]{:S(2)}, u32[]{:S(2)}) collective-permute-start(bf16[4,128,128]{2,1,0:T(8,128)(2,1)S(1)} %get-tuple-element.55), channel_id=1, source_target_pairs={{0,16},{4,20},{8,24},{12,28},{16,0},{20,4},{24,8},{28,12},{1,17},{... | collective-permute-start | bytes 393224 | tf_op jit(solution)/shard_map/ppermute | solution.py:527
  39.7 1.5 %collective-permute-start.15 = (bf16[4,128,128]{2,1,0:T(8,128)(2,1)S(1)}, bf16[4,128,128]{2,1,0:T(8,128)(2,1)S(1)}, u32[]{:S(2)}, u32[]{:S(2)}) collective-permute-start(bf16[4,128,128]{2,1,0:T(8,128)(2,1)S(1)} %get-tuple-element.56), channel_id=1, source_target_pairs={{0,8},{4,12},{8,0},{12,4},{16,24},{20,28},{24,16},{28,20},{1,9},{5... | collective-permute-start | bytes 393224 | tf_op jit(solution)/shard_map/ppermute | solution.py:527
  41.2 2.1 %collective-permute-done.11.refs_7_ = bf16[17,32,128]{2,1,0:T(8,128)(2,1)S(1)} collective-permute-done((bf16[17,32,128]{2,1,0:T(8,128)(2,1)S(1)}, bf16[17,32,128]{2,1,0:T(8,128)(2,1)S(1)}, u32[]{:S(2)}, u32[]{:S(2)}) %collective-permute-start.11) | collective-permute-done | bytes 139296 | tf_op jit(solution)/shard_map/ppermute | solution.py:527
  43.4 1.4 %near_early.1.refs_5_.early_ref = f32[4,12,128,128]{3,2,1,0:T(8,128)S(1)} custom-call(bf16[128,2048]{1,0:T(8,128)(2,1)S(1)} %copy-done, bf16[128,2048]{1,0:T(8,128)(2,1)S(1)} %copy-done.1, bf16[128,2048]{1,0:T(8,128)(2,1)S(1)} %copy-done.2, bf16[128,2048]{1,0:T(8,128)(2,1)S(1)} %copy-done.3, f32[32,128]{1,0:T(8,128)S(1)} %get-tuple-element.33.refs_0_.refs_4_, ...), custom_call_target="tpu_custom_call" | custom-call | flops 2000000000 | bytes 5709824 | tf_op jit(solution)/shard_map/near_early/pallas_call | solution.py:499
  44.8 0.7 %collective-permute-done.16.refs_8_ = bf16[17,32,128]{2,1,0:T(8,128)(2,1)S(1)} collective-permute-done((bf16[17,32,128]{2,1,0:T(8,128)(2,1)S(1)}, bf16[17,32,128]{2,1,0:T(8,128)(2,1)S(1)}, u32[]{:S(2)}, u32[]{:S(2)}) %collective-permute-start.16) | collective-permute-done | bytes 139296 | tf_op jit(solution)/shard_map/ppermute | solution.py:527
  45.5 1.9 %final_others.1 = (bf16[128,2048]{1,0:T(8,128)(2,1)}, bf16[128,2048]{1,0:T(8,128)(2,1)}, bf16[128,2048]{1,0:T(8,128)(2,1)}, bf16[128,2048]{1,0:T(8,128)(2,1)}) custom-call(bf16[128,2048]{1,0:T(8,128)(2,1)S(1)} %copy-done, bf16[128,2048]{1,0:T(8,128)(2,1)S(1)} %copy-done.1, bf16[128,2048]{1,0:T(8,128)(2,1)S(1)} %copy-done.2, bf16[128,2048]{1,0:T(8,128)(2,1)S(1)} %copy-done.3, ...), custom_call_target="tpu_custom_call" | custom-call | flops 1000000000 | bytes 7774208 | tf_op jit(solution)/shard_map/final_others/pallas_call | solution.py:499
  47.5 1.1 %final_own.1 = (bf16[128,2048]{1,0:T(8,128)(2,1)}, bf16[128,2048]{1,0:T(8,128)(2,1)}, bf16[128,2048]{1,0:T(8,128)(2,1)}, bf16[128,2048]{1,0:T(8,128)(2,1)}) custom-call(f32[4,12,128,128]{3,2,1,0:T(8,128)S(1)} %near_early.1.refs_5_.early_ref, ...), custom_call_target="tpu_custom_call", output_to_operand_aliasing={{0}: (6, {}), {1}: (7, {}), {2}: (8, {}), {3}: (9, {})} | custom-call | flops 16777216 | bytes 8003584 | tf_op jit(solution)/shard_map/final_own/pallas_call | solution.py:499
  (26 shorter events, 0.2 us)
Async XLA Ops:
  4.6 9.2 %collective-permute-start = (bf16[17,32,128]{2,1,0:T(8,128)(2,1)}, bf16[17,32,128]{2,1,0:T(8,128)(2,1)S(1)}, u32[]{:S(2)}, u32[]{:S(2)}) collective-permute-start(bf16[17,32,128]{2,1,0:T(8,128)(2,1)} %get-tuple-element.35), channel_id=1, source_target_pairs={{0,3},{1,2},{2,1},{3,0},{4,7},{5,6},{6,5},{7,4},{8,11},{9,10},{10,... | collective-permute-start | bytes 417800 | tf_op jit(solution)/shard_map/ppermute | solution.py:527
  9.7 7.6 %collective-permute-start.3 = (bf16[4,128,128]{2,1,0:T(8,128)(2,1)S(1)}, bf16[4,128,128]{2,1,0:T(8,128)(2,1)S(1)}, u32[]{:S(2)}, u32[]{:S(2)}) collective-permute-start(bf16[4,128,128]{2,1,0:T(8,128)(2,1)S(1)} %get-tuple-element.39), channel_id=1, source_target_pairs={{0,8},{4,12},{8,0},{12,4},{16,24},{20,28},{24,16},{28,20},{1,9},{5... | collective-permute-start | bytes 393224 | tf_op jit(solution)/shard_map/ppermute | solution.py:527
  11.2 7.8 %collective-permute-start.4 = (bf16[4,128,128]{2,1,0:T(8,128)(2,1)S(1)}, bf16[4,128,128]{2,1,0:T(8,128)(2,1)S(1)}, u32[]{:S(2)}, u32[]{:S(2)}) collective-permute-start(bf16[4,128,128]{2,1,0:T(8,128)(2,1)S(1)} %get-tuple-element.40), channel_id=1, source_target_pairs={{0,16},{4,20},{8,24},{12,28},{16,0},{20,4},{24,8},{28,12},{1,17},{... | collective-permute-start | bytes 393224 | tf_op jit(solution)/shard_map/ppermute | solution.py:527
  12.7 6.2 %collective-permute-start.5 = (bf16[4,128,128]{2,1,0:T(8,128)(2,1)S(1)}, bf16[4,128,128]{2,1,0:T(8,128)(2,1)S(1)}, u32[]{:S(2)}, u32[]{:S(2)}) collective-permute-start(bf16[4,128,128]{2,1,0:T(8,128)(2,1)S(1)} %get-tuple-element.41), channel_id=1, source_target_pairs={{0,24},{4,28},{8,16},{12,20},{16,8},{20,12},{24,0},{28,4},{1,25},{... | collective-permute-start | bytes 393224 | tf_op jit(solution)/shard_map/ppermute | solution.py:527
  13.2 8.5 %collective-permute-start.1 = (bf16[17,32,128]{2,1,0:T(8,128)(2,1)S(1)}, bf16[17,32,128]{2,1,0:T(8,128)(2,1)S(1)}, u32[]{:S(2)}, u32[]{:S(2)}) collective-permute-start(bf16[17,32,128]{2,1,0:T(8,128)(2,1)S(1)} %get-tuple-element.36), channel_id=1, source_target_pairs={{0,1},{1,0},{2,3},{3,2},{4,5},{5,4},{6,7},{7,6},{8,9},{9,8},{10,11... | collective-permute-start | bytes 417800 | tf_op jit(solution)/shard_map/ppermute | solution.py:527
  13.8 9.0 %collective-permute-start.2 = (bf16[17,32,128]{2,1,0:T(8,128)(2,1)S(1)}, bf16[17,32,128]{2,1,0:T(8,128)(2,1)S(1)}, u32[]{:S(2)}, u32[]{:S(2)}) collective-permute-start(bf16[17,32,128]{2,1,0:T(8,128)(2,1)S(1)} %get-tuple-element.37), channel_id=1, source_target_pairs={{0,2},{1,3},{2,0},{3,1},{4,6},{5,7},{6,4},{7,5},{8,10},{9,11},{10,... | collective-permute-start | bytes 417800 | tf_op jit(solution)/shard_map/ppermute | solution.py:527
  19.0 1.6 %collective-permute-start.6 = (bf16[4,2,128,128]{3,2,1,0:T(8,128)(2,1)S(1)}, bf16[4,2,128,128]{3,2,1,0:T(8,128)(2,1)S(1)}, u32[]{:S(2)}, u32[]{:S(2)}) collective-permute-start(bf16[4,2,128,128]{3,2,1,0:T(8,128)(2,1)S(1)} %pack.1), channel_id=1, source_target_pairs={{0,4},{4,0},{8,12},{12,8},{16,20},{20,16},{24,28},{28,24},{1,5},{5... | collective-permute-start | bytes 786440 | tf_op jit(solution)/shard_map/ppermute | solution.py:527
  23.3 4.6 %collective-permute-start.9 = (f32[16,128]{1,0:T(8,128)S(1)}, f32[16,128]{1,0:T(8,128)S(1)}, u32[]{:S(2)}, u32[]{:S(2)}) collective-permute-start(f32[16,128]{1,0:T(8,128)S(1)} %get-tuple-element.44.refs_6_.refs_8_.refs_5_), channel_id=1, source_target_pairs={{0,24},{4,28},{8,16},{12,20},{16,8},{20,12},{24,0},{28,4},{1,25},{... | collective-permute-start | bytes 24584 | tf_op jit(solution)/shard_map/ppermute | solution.py:527
  25.9 3.7 %collective-permute-start.8 = (f32[16,128]{1,0:T(8,128)S(1)}, f32[16,128]{1,0:T(8,128)S(1)}, u32[]{:S(2)}, u32[]{:S(2)}) collective-permute-start(f32[16,128]{1,0:T(8,128)S(1)} %get-tuple-element.44.refs_6_.refs_8_.refs_5_), channel_id=1, source_target_pairs={{0,16},{4,20},{8,24},{12,28},{16,0},{20,4},{24,8},{28,12},{1,17},{... | collective-permute-start | bytes 24584 | tf_op jit(solution)/shard_map/ppermute | solution.py:527
  26.4 3.7 %collective-permute-start.7 = (f32[16,128]{1,0:T(8,128)S(1)}, f32[16,128]{1,0:T(8,128)S(1)}, u32[]{:S(2)}, u32[]{:S(2)}) collective-permute-start(f32[16,128]{1,0:T(8,128)S(1)} %get-tuple-element.44.refs_6_.refs_8_.refs_5_), channel_id=1, source_target_pairs={{0,8},{4,12},{8,0},{12,4},{16,24},{20,28},{24,16},{28,20},{1,9},{5... | collective-permute-start | bytes 24584 | tf_op jit(solution)/shard_map/ppermute | solution.py:527
  30.6 6.9 %collective-permute-start.10 = (bf16[17,32,128]{2,1,0:T(8,128)(2,1)S(1)}, bf16[17,32,128]{2,1,0:T(8,128)(2,1)S(1)}, u32[]{:S(2)}, u32[]{:S(2)}) collective-permute-start(bf16[17,32,128]{2,1,0:T(8,128)(2,1)S(1)} %get-tuple-element.46), channel_id=1, source_target_pairs={{0,3},{1,2},{2,1},{3,0},{4,7},{5,6},{6,5},{7,4},{8,11},{9,10},{10,... | collective-permute-start | bytes 417800 | tf_op jit(solution)/shard_map/ppermute | solution.py:527
  35.4 2.1 %collective-permute-start.12 = (bf16[4,2,128,128]{3,2,1,0:T(8,128)(2,1)S(1)}, bf16[4,2,128,128]{3,2,1,0:T(8,128)(2,1)S(1)}, u32[]{:S(2)}, u32[]{:S(2)}) collective-permute-start(bf16[4,2,128,128]{3,2,1,0:T(8,128)(2,1)S(1)} %get-tuple-element.52), channel_id=1, source_target_pairs={{0,4},{4,0},{8,12},{12,8},{16,20},{20,16},{24,28},{28,24},{1,5},{5... | collective-permute-start | bytes 786440 | tf_op jit(solution)/shard_map/ppermute | solution.py:527
  35.5 7.9 %collective-permute-start.11 = (bf16[17,32,128]{2,1,0:T(8,128)(2,1)S(1)}, bf16[17,32,128]{2,1,0:T(8,128)(2,1)S(1)}, u32[]{:S(2)}, u32[]{:S(2)}) collective-permute-start(bf16[17,32,128]{2,1,0:T(8,128)(2,1)S(1)} %get-tuple-element.47), channel_id=1, source_target_pairs={{0,1},{1,0},{2,3},{3,2},{4,5},{5,4},{6,7},{7,6},{8,9},{9,8},{10,11... | collective-permute-start | bytes 417800 | tf_op jit(solution)/shard_map/ppermute | solution.py:527
  35.6 9.9 %collective-permute-start.16 = (bf16[17,32,128]{2,1,0:T(8,128)(2,1)S(1)}, bf16[17,32,128]{2,1,0:T(8,128)(2,1)S(1)}, u32[]{:S(2)}, u32[]{:S(2)}) collective-permute-start(bf16[17,32,128]{2,1,0:T(8,128)(2,1)S(1)} %get-tuple-element.57), channel_id=1, source_target_pairs={{0,2},{1,3},{2,0},{3,1},{4,6},{5,7},{6,4},{7,5},{8,10},{9,11},{10,... | collective-permute-start | bytes 417800 | tf_op jit(solution)/shard_map/ppermute | solution.py:527
  37.6 5.8 %copy-start = (bf16[128,2048]{1,0:T(8,128)(2,1)S(1)}, bf16[128,2048]{1,0:T(8,128)(2,1)}, u32[]{:S(2)}) copy-start(bf16[128,2048]{1,0:T(8,128)(2,1)} %refs_0_.5) | copy-start | bytes 1572868
  37.6 5.8 %copy-start.1 = (bf16[128,2048]{1,0:T(8,128)(2,1)S(1)}, bf16[128,2048]{1,0:T(8,128)(2,1)}, u32[]{:S(2)}) copy-start(bf16[128,2048]{1,0:T(8,128)(2,1)} %refs_1_.5) | copy-start | bytes 1572868
  37.6 5.8 %copy-start.2 = (bf16[128,2048]{1,0:T(8,128)(2,1)S(1)}, bf16[128,2048]{1,0:T(8,128)(2,1)}, u32[]{:S(2)}) copy-start(bf16[128,2048]{1,0:T(8,128)(2,1)} %refs_2_.5) | copy-start | bytes 1572868
  37.6 5.8 %copy-start.3 = (bf16[128,2048]{1,0:T(8,128)(2,1)S(1)}, bf16[128,2048]{1,0:T(8,128)(2,1)}, u32[]{:S(2)}) copy-start(bf16[128,2048]{1,0:T(8,128)(2,1)} %refs_3_.5) | copy-start | bytes 1572868
  37.7 9.8 %collective-permute-start.13 = (bf16[4,128,128]{2,1,0:T(8,128)(2,1)S(1)}, bf16[4,128,128]{2,1,0:T(8,128)(2,1)S(1)}, u32[]{:S(2)}, u32[]{:S(2)}) collective-permute-start(bf16[4,128,128]{2,1,0:T(8,128)(2,1)S(1)} %get-tuple-element.54), channel_id=1, source_target_pairs={{0,24},{4,28},{8,16},{12,20},{16,8},{20,12},{24,0},{28,4},{1,25},{... | collective-permute-start | bytes 393224 | tf_op jit(solution)/shard_map/ppermute | solution.py:527
  39.2 8.2 %collective-permute-start.14 = (bf16[4,128,128]{2,1,0:T(8,128)(2,1)S(1)}, bf16[4,128,128]{2,1,0:T(8,128)(2,1)S(1)}, u32[]{:S(2)}, u32[]{:S(2)}) collective-permute-start(bf16[4,128,128]{2,1,0:T(8,128)(2,1)S(1)} %get-tuple-element.55), channel_id=1, source_target_pairs={{0,16},{4,20},{8,24},{12,28},{16,0},{20,4},{24,8},{28,12},{1,17},{... | collective-permute-start | bytes 393224 | tf_op jit(solution)/shard_map/ppermute | solution.py:527
  39.7 7.7 %collective-permute-start.15 = (bf16[4,128,128]{2,1,0:T(8,128)(2,1)S(1)}, bf16[4,128,128]{2,1,0:T(8,128)(2,1)S(1)}, u32[]{:S(2)}, u32[]{:S(2)}) collective-permute-start(bf16[4,128,128]{2,1,0:T(8,128)(2,1)S(1)} %get-tuple-element.56), channel_id=1, source_target_pairs={{0,8},{4,12},{8,0},{12,4},{16,24},{20,28},{24,16},{28,20},{1,9},{5... | collective-permute-start | bytes 393224 | tf_op jit(solution)/shard_map/ppermute | solution.py:527

commit v12 on v11

--- a/solution.py
+++ b/solution.py
@@ -138,18 +138,20 @@
     sources, refs = refs[:4], refs[4:]
     mids, refs = refs[:n_i], refs[n_i:]
     fulls, refs = refs[:slots], refs[slots:]
-    stats_ref, buffers, sems, wide, picked, turn = refs
+    stats_ref, buffers, sems, picked, turn = refs
     rows = sources[0].shape[0]
     quarter = rows // DILATION
     pos, chip = position(slots)
     turn[...] = jnp.zeros_like(turn)
+    row = lax.broadcasted_iota(jnp.int32, (quarter, rows), 0) * DILATION
+    taken = lax.broadcasted_iota(jnp.int32, (quarter, rows), 1)
+    chosen = [jnp.where(taken == row + i, 1.0, 0.0).astype(BF16) for i in range(DILATION)]
     for group, copies in enumerate(fetch(sources, buffers, sems)):
         for which, copy in enumerate(copies):
             copy.wait()
             for residue in range(DILATION):
                 head = group * DILATION + residue
-                wide[which, head] = buffers[which, :, static_columns(head)].astype(F32)
-                rowset = wide[which, head, pl.ds(residue, quarter, stride=DILATION), :]
+                rowset = dot(chosen[residue], buffers[which, :, static_columns(head)])
                 picked[head // slots, which * slots + head % slots] = rowset.astype(BF16)
         heads = range(group * DILATION, (group + 1) * DILATION)
         operands = [[buffers[which, :, static_columns(head)] for which in range(4)] for head in heads]
@@ -354,6 +356,59 @@
     return level_parts(operands, stats)
 
 
+def far_sum_kernel(slots, *refs):
+    own, refs = refs[:slots], refs[slots:]
+    found, outs = refs[: -slots - 1], refs[-slots:]
+    for m in range(slots):
+        outs[m][:2] = own[m][:2]
+        total = own[m][2:].astype(F32)
+        for ref in found:
+            total += ref[m].astype(F32)
+        outs[m][2:] = total.astype(BF16)
+
+
+def near_statistics(slots, places, near_ref, mids, xmsgs, stats_ref, spread):
+    rows = near_ref.shape[1]
+    quarter = rows // DILATION
+    pos, chip = position(slots)
+    lane = lanes_of(quarter)
+    mid = jnp.zeros((quarter, LANES), F32)
+    for d, ref in zip(places, mids):
+        place = (pos ^ d) * slots
+        found = join(ref)
+        e = pltpu.roll(found, place, 1)
+        de = pltpu.roll(found, place + HEADS - slots, 1)
+        mid = jnp.where((lane >= place) & (lane < place + slots), e, mid)
+        mid = jnp.where((lane >= HEADS + place) & (lane < HEADS + place + slots), de, mid)
+    blank = jnp.where(lane < HEADS, LOWEST, 0.0)
+    for residue in range(DILATION):
+        spread[pl.ds(residue, quarter, stride=DILATION), :] = jnp.where(
+            lane % DILATION == residue, mid, blank
+        )
+    across = spread[...].T
+    e, d = merge_stats(
+        near_ref[:HEADS], near_ref[HEADS:], across[:HEADS], across[HEADS : 2 * HEADS]
+    )
+    if xmsgs:
+        stats_ref[:HEADS] = jnp.full((HEADS, rows), LOWEST, F32)
+        stats_ref[HEADS:] = jnp.zeros((HEADS, rows), F32)
+        for m in range(slots):
+            head = pos * slots + (chip ^ m)
+            stats_ref[pl.ds(head, 1), :] = xmsgs[m][2 * slots + m : 2 * slots + m + 1, :]
+            stats_ref[pl.ds(HEADS + head, 1), :] = xmsgs[m][3 * slots + m : 3 * slots + m + 1, :]
+        e, d = merge_stats(e, d, stats_ref[:HEADS], stats_ref[HEADS:])
+    stats_ref[:HEADS] = e
+    stats_ref[HEADS:] = d
+
+
+def near_place(slots, d, sources, stats_ref):
+    pos, _ = position(slots)
+    heads = [(pos ^ d) * slots + slot for slot in range(slots)]
+    operands = [[ref[:, head_columns(head)] for ref in sources] for head in heads]
+    stats = [(stats_ref[pl.ds(head, 1), :], stats_ref[pl.ds(HEADS + head, 1), :]) for head in heads]
+    return level_parts(operands, stats)
+
+
 def near_early_kernel(n_i, slots, *refs):
     sources, near_ref, refs = refs[:4], refs[4], refs[5:]
     mids, refs = refs[: n_i - 1], refs[n_i - 1 :]
@@ -449,30 +504,46 @@
     return copies
 
 
-def final_others_kernel(n_i, slots, *refs):
-    sources, near_ref, early_ref, refs = refs[:4], refs[4], refs[5], refs[6:]
+def finish_place(slots, d, near, mid_ref, ready, outs, sems):
+    found = [spread_rows(slots, d, slot, mid_ref) for slot in range(slots)]
+    for slot, parts in enumerate(found):
+        for which in range(4):
+            total = near[slot][which] + parts[:, static_columns(which)]
+            ready[which, :, static_columns(slot)] = total.astype(BF16)
+    return send_place(slots, d, ready, outs, sems)
+
+
+def near_early_kernel(n_i, slots, *refs):
+    sources, near_ref, refs = refs[:4], refs[4], refs[5:]
     mids, refs = refs[: n_i - 1], refs[n_i - 1 :]
-    outs, (ready, sems, stats_ref, spread) = refs[:4], refs[4:]
-    places = in_turn(list(range(n_i)))[1:]
-    near_statistics(slots, places[-1:], near_ref, mids[-1:], (), stats_ref, spread)
-    late = near_place(slots, places[-1], sources, stats_ref)
+    xmsgs, refs = refs[:slots], refs[slots:]
+    outs, (own_ref, ready, sems, stats_ref, spread) = refs[:4], refs[4:]
+    places = in_turn(list(range(n_i)))[:-1]
+    near_statistics(slots, places, near_ref, mids, xmsgs, stats_ref, spread)
     copies = []
-    for index, d in enumerate(places):
-        found = [spread_rows(slots, d, slot, mids[index]) for slot in range(slots)]
-        for slot, parts in enumerate(found):
-            for which in range(4):
-                if d == places[-1]:
-                    near = late[slot][which]
-                else:
-                    near = early_ref[which, (index + 1) * slots + slot]
-                total = near + parts[:, static_columns(which)]
-                ready[index, which, :, static_columns(slot)] = total.astype(BF16)
-        copies += send_place(slots, d, ready.at[index], outs, sems.at[index])
+    for index, d in enumerate(places[1:]):
+        near = near_place(slots, d, sources, stats_ref)
+        copies += finish_place(
+            slots, d, near, mids[index + 1], ready.at[index], outs, sems.at[index]
+        )
+    for slot, parts in enumerate(near_place(slots, 0, sources, stats_ref)):
+        for which, part in enumerate(parts):
+            own_ref[which, slot] = part
     for copy in copies:
         copy.wait()
 
 
-def final_own_kernel(slots, early_ref, mid_ref, *refs):
+def final_last_kernel(n_i, slots, *refs):
+    sources, near_ref, mid_ref, refs = refs[:4], refs[4], refs[5], refs[6 + 4 :]
+    outs, (ready, sems, stats_ref, spread) = refs[:4], refs[4:]
+    d = in_turn(list(range(n_i)))[-1]
+    near_statistics(slots, [d], near_ref, [mid_ref], (), stats_ref, spread)
+    near = near_place(slots, d, sources, stats_ref)
+    for copy in finish_place(slots, d, near, mid_ref, ready, outs, sems):
+        copy.wait()
+
+
+def final_own_kernel(slots, own_ref, mid_ref, *refs):
     fulls, refs = in_back(refs[:slots]), refs[slots:]
     outs, (ready, sems) = refs[4:8], refs[8:]
     _, chip = position(slots)
@@ -480,7 +551,7 @@
     for m, parts in enumerate(found):
         slot = chip ^ m
         for which in range(4):
-            total = early_ref[which, slot] + parts[:, static_columns(which)]
+            total = own_ref[which, slot] + parts[:, static_columns(which)]
             total += fulls[m][which].astype(F32)
             ready[which, :, head_columns(slot)] = total.astype(BF16)
     for copy in send_place(slots, 0, ready, outs, sems):
@@ -491,7 +562,7 @@
     refs[-1][...] = jnp.zeros_like(refs[-1])
 
 
-def call(kernel, name, outs, scratch, flops, operands, hbm_in=(), hbm_out=False, cheap=False, limit=VMEM_LIMIT, aliases=None):
+def call(kernel, name, outs, scratch, flops, operands, hbm_in=(), hbm_out=0, cheap=False, limit=VMEM_LIMIT, aliases=None):
     moved = sum(x.size * x.dtype.itemsize for x in tuple(operands) + tuple(outs))
     if cheap:
         flops, moved = 1, 1
@@ -501,7 +572,8 @@
         out_shape=tuple(outs),
         in_specs=[pl.BlockSpec(memory_space=space) for space in spaces],
         out_specs=tuple(
-            pl.BlockSpec(memory_space=pltpu.HBM if hbm_out else pltpu.VMEM) for _ in outs
+            pl.BlockSpec(memory_space=pltpu.HBM if i < hbm_out else pltpu.VMEM)
+            for i in range(len(outs))
         ),
         scratch_shapes=scratch,
         input_output_aliases=aliases or {},
@@ -560,7 +632,6 @@
         [
             pltpu.VMEM((4, rows, features), BF16),
             pltpu.SemaphoreType.DMA((4, HEADS // DILATION)),
-            pltpu.VMEM((4, HEADS, rows, HEAD_DIM), F32),
             pltpu.VMEM((n_i, 4 * slots, quarter, HEAD_DIM), BF16),
             square,
         ],
@@ -631,37 +702,41 @@
 
     back = in_turn(midparts)
     kept = [pltpu.VMEM((2 * HEADS, rows), F32), square]
-    (early,) = call(
+    whole = [SHAPE((rows, features), BF16)] * 4
+    ready = pltpu.VMEM((4, rows, slots * HEAD_DIM), BF16)
+    *outs, own = call(
         bind(near_early_kernel, n_i, slots),
         "near_early",
-        [SHAPE((4, (n_i - 1) * slots, rows, HEAD_DIM), F32)],
-        kept,
+        whole + [SHAPE((4, slots, rows, HEAD_DIM), F32)],
+        [
+            pltpu.VMEM((n_i - 2, 4, rows, slots * HEAD_DIM), BF16),
+            pltpu.SemaphoreType.DMA((n_i - 2, 4)),
+            *kept,
+        ],
         SHORT,
         [*sources, near, *back[:-1], *xmsgs],
-    )
-    whole = [SHAPE((rows, features), BF16)] * 4
+        hbm_out=4,
+    )
     outs = call(
-        bind(final_others_kernel, n_i, slots),
-        "final_others",
+        bind(final_last_kernel, n_i, slots),
+        "final_last",
         whole,
-        [
-            pltpu.VMEM((n_i - 1, 4, rows, slots * HEAD_DIM), BF16),
-            pltpu.SemaphoreType.DMA((n_i - 1, 4)),
-            *kept,
-        ],
+        [ready, pltpu.SemaphoreType.DMA((4,)), *kept],
         SHORT // 2,
-        [*sources, near, early, *back[1:]],
-        hbm_out=True,
+        [*sources, near, back[-1], *outs],
+        hbm_in=range(6, 10),
+        hbm_out=4,
+        aliases={6 + which: which for which in range(4)},
     )
     return call(
         bind(final_own_kernel, slots),
         "final_own",
         whole,
-        [pltpu.VMEM((4, rows, slots * HEAD_DIM), BF16), pltpu.SemaphoreType.DMA((4,))],
+        [ready, pltpu.SemaphoreType.DMA((4,))],
         unit * slots,
-        [early, midparts[0], *in_back(fullparts), *outs],
+        [own, midparts[0], *in_back(fullparts), *outs],
         hbm_in=range(2 + slots, 6 + slots),
-        hbm_out=True,
+        hbm_out=4,
         aliases={2 + slots + which: which for which in range(4)},
     )
 

time: 48.8 us -> 50.2 us (1.029)
  Pallas kernels: 13.1 us -> 15.2 us
  waiting for transfers between devices: 10.9 us -> 10.2 us
    pallas_call x16, Pallas kernels: 13.1 us -> 15.2 us  [call(): pl.pallas_call(kernel, out_shape=tuple(outs), in_specs=[pl.BlockSpec(memo...]
    ppermute x17, waiting for transfers between devices: 10.9 us -> 10.2 us  [swap(): return lax.ppermute(x, axis, [(i, i ^ mask) for i in range(n)])]
  transfers between devices with their start and end apart: 17 -> 17, of which waited for: 9 -> 8; matrix products, arithmetic and copies ran while one was open for 0% -> 0% of each run, Pallas kernels for 14% -> 15%
where the time goes in v12:
time: 50.2 us; the launch traced here: 50 us
  starting transfers between devices  23.8 us (47%)
  Pallas kernels  15.2 us (30%)
  waiting for transfers between devices  10.2 us (20%)
  between operations  0.82 us (2%)
    ppermute x17, starting transfers between devices, swap(): return lax.ppermute(x, axis, [(i, i ^ mask) for i in range(n)])  23.8 us
    pallas_call x16, Pallas kernels, call(): pl.pallas_call(kernel, out_shape=tuple(outs), in_specs=[pl.BlockSpec(memo...  15.2 us
    ppermute x17, waiting for transfers between devices, swap(): return lax.ppermute(x, axis, [(i, i ^ mask) for i in range(n)])  10.2 us
  transfers between devices with their start and end apart: 17, of which 8 were waited for; matrix products, arithmetic and copies ran while one was open for 0% of the time, Pallas kernels for 15%

profile of v12, /device:TPU:0, one launch (start us, length us, event | category | flops | bytes accessed | tf_op | source)
XLA Modules:
  0.0 50.0 jit_solution(2526243109677366408)
XLA Ops:
  0.6 5.5 %pick.1 = (bf16[17,32,128]{2,1,0:T(8,128)(2,1)S(1)}, bf16[17,32,128]{2,1,0:T(8,128)(2,1)S(1)}, bf16[17,32,128]{2,1,0:T(8,128)(2,1)S(1)}, bf16[17,32,128]{2,1,0:T...) custom-call(bf16[128,2048]{1,0:T(8,128)(2,1)} %refs_0_.5, ...), custom_call_target="tpu_custom_call" | custom-call | flops 134217728 | bytes 3194880 | tf_op jit(solution)/shard_map/pick/pallas_call | solution.py:570
  6.1 5.1 %collective-permute-start = (bf16[17,32,128]{2,1,0:T(8,128)(2,1)}, bf16[17,32,128]{2,1,0:T(8,128)(2,1)S(1)}, u32[]{:S(2)}, u32[]{:S(2)}) collective-permute-start(bf16[17,32,128]{2,1,0:T(8,128)(2,1)} %get-tuple-element.40), channel_id=1, source_target_pairs={{0,3},{1,2},{2,1},{3,0},{4,7},{5,6},{6,5},{7,4},{8,11},{9,10},{10,... | collective-permute-start | bytes 417800 | tf_op jit(solution)/shard_map/ppermute | solution.py:599
  11.2 1.5 %collective-permute-start.3 = (bf16[4,128,128]{2,1,0:T(8,128)(2,1)S(1)}, bf16[4,128,128]{2,1,0:T(8,128)(2,1)S(1)}, u32[]{:S(2)}, u32[]{:S(2)}) collective-permute-start(bf16[4,128,128]{2,1,0:T(8,128)(2,1)S(1)} %get-tuple-element.44), channel_id=1, source_target_pairs={{0,8},{4,12},{8,0},{12,4},{16,24},{20,28},{24,16},{28,20},{1,9},{5... | collective-permute-start | bytes 393224 | tf_op jit(solution)/shard_map/ppermute | solution.py:599
  12.7 1.5 %collective-permute-start.4 = (bf16[4,128,128]{2,1,0:T(8,128)(2,1)S(1)}, bf16[4,128,128]{2,1,0:T(8,128)(2,1)S(1)}, u32[]{:S(2)}, u32[]{:S(2)}) collective-permute-start(bf16[4,128,128]{2,1,0:T(8,128)(2,1)S(1)} %get-tuple-element.45), channel_id=1, source_target_pairs={{0,16},{4,20},{8,24},{12,28},{16,0},{20,4},{24,8},{28,12},{1,17},{... | collective-permute-start | bytes 393224 | tf_op jit(solution)/shard_map/ppermute | solution.py:599
  14.2 0.5 collective-permute-start.5
  14.7 0.6 %collective-permute-done.refs_0_.refs_1_ = bf16[17,32,128]{2,1,0:T(8,128)(2,1)S(1)} collective-permute-done((bf16[17,32,128]{2,1,0:T(8,128)(2,1)}, bf16[17,32,128]{2,1,0:T(8,128)(2,1)S(1)}, u32[]{:S(2)}, u32[]{:S(2)}) %collective-permute-start) | collective-permute-done | bytes 139296 | tf_op jit(solution)/shard_map/ppermute | solution.py:599
  15.3 3.5 %collective-permute-start.2 = (bf16[17,32,128]{2,1,0:T(8,128)(2,1)S(1)}, bf16[17,32,128]{2,1,0:T(8,128)(2,1)S(1)}, u32[]{:S(2)}, u32[]{:S(2)}) collective-permute-start(bf16[17,32,128]{2,1,0:T(8,128)(2,1)S(1)} %get-tuple-element.42), channel_id=1, source_target_pairs={{0,2},{1,3},{2,0},{3,1},{4,6},{5,7},{6,4},{7,5},{8,10},{9,11},{10,... | collective-permute-start | bytes 417800 | tf_op jit(solution)/shard_map/ppermute | solution.py:599
  18.8 1.7 %collective-permute-done.4.refs_2_ = bf16[4,128,128]{2,1,0:T(8,128)(2,1)S(1)} collective-permute-done((bf16[4,128,128]{2,1,0:T(8,128)(2,1)S(1)}, bf16[4,128,128]{2,1,0:T(8,128)(2,1)S(1)}, u32[]{:S(2)}, u32[]{:S(2)}) %collective-permute-start.4) | collective-permute-done | bytes 131104 | tf_op jit(solution)/shard_map/ppermute | solution.py:599
  20.5 0.1 collective-permute-start.6
  20.6 1.5 %collective-permute-done.6.refs_4_ = bf16[4,2,128,128]{3,2,1,0:T(8,128)(2,1)S(1)} collective-permute-done((bf16[4,2,128,128]{3,2,1,0:T(8,128)(2,1)S(1)}, bf16[4,2,128,128]{3,2,1,0:T(8,128)(2,1)S(1)}, u32[]{:S(2)}, u32[]{:S(2)}) %collective-permute-start.6) | collective-permute-done | bytes 262176 | tf_op jit(solution)/shard_map/ppermute | solution.py:599
  22.1 1.1 %far_stats.1.refs_5_ = f32[8,128]{1,0:T(8,128)S(1)} custom-call(bf16[4,128,128]{2,1,0:T(8,128)(2,1)S(1)} %get-tuple-element.43.refs_0_, bf16[4,128,128]{2,1,0:T(8,128)(2,1)S(1)} %collective-permute-done.3.refs_1_, bf16[4,128,128]{2,1,0:T(8,128)(2,1)S(1)} %collective-permute-done.4.refs_2_, bf16[4,128,128]{2,1,0:T(8,128)(2,1)S(1)} %collective-permute-done.5.refs_3_, ...), custom_call_target="tpu_custom_call" | custom-call | flops 1 | bytes 794624 | tf_op jit(solution)/shard_map/far_stats/pallas_call | solution.py:570
  23.2 1.1 %collective-permute-done.2.refs_3_ = bf16[17,32,128]{2,1,0:T(8,128)(2,1)S(1)} collective-permute-done((bf16[17,32,128]{2,1,0:T(8,128)(2,1)S(1)}, bf16[17,32,128]{2,1,0:T(8,128)(2,1)S(1)}, u32[]{:S(2)}, u32[]{:S(2)}) %collective-permute-start.2) | collective-permute-done | bytes 139296 | tf_op jit(solution)/shard_map/ppermute | solution.py:599
  24.4 0.5 %middle_stats.1 = (f32[16,128]{1,0:T(8,128)S(1)}, f32[8,128]{1,0:T(8,128)S(1)}, f32[128,128]{1,0:T(8,128)S(1)}) custom-call(bf16[17,32,128]{2,1,0:T(8,128)(2,1)S(1)} %get-tuple-element.39.refs_0_, bf16[17,32,128]{2,1,0:T(8,128)(2,1)S(1)} %collective-permute-done.refs_0_.refs_1_, bf16[17,32,128]{2,1,0:T(8,128)(2,1)S(1)} %collective-permute-done.1.refs_2_, ...), custom_call_target="tpu_custom_call" | custom-call | flops 33554432 | bytes 655360 | tf_op jit(solution)/shard_map/middle_stats/pallas_call | solution.py:570
  24.9 2.5 %collective-permute-start.9 = (f32[16,128]{1,0:T(8,128)S(1)}, f32[16,128]{1,0:T(8,128)S(1)}, u32[]{:S(2)}, u32[]{:S(2)}) collective-permute-start(f32[16,128]{1,0:T(8,128)S(1)} %get-tuple-element.49.refs_6_.refs_8_.refs_5_), channel_id=1, source_target_pairs={{0,24},{4,28},{8,16},{12,20},{16,8},{20,12},{24,0},{28,4},{1,25},{... | collective-permute-start | bytes 24584 | tf_op jit(solution)/shard_map/ppermute | solution.py:599
  27.4 0.5 collective-permute-start.8
  27.9 0.5 %collective-permute-start.7 = (f32[16,128]{1,0:T(8,128)S(1)}, f32[16,128]{1,0:T(8,128)S(1)}, u32[]{:S(2)}, u32[]{:S(2)}) collective-permute-start(f32[16,128]{1,0:T(8,128)S(1)} %get-tuple-element.49.refs_6_.refs_8_.refs_5_), channel_id=1, source_target_pairs={{0,8},{4,12},{8,0},{12,4},{16,24},{20,28},{24,16},{28,20},{1,9},{5... | collective-permute-start | bytes 24584 | tf_op jit(solution)/shard_map/ppermute | solution.py:599
  28.4 1.1 %collective-permute-done.9.refs_9_.refs_11_.refs_8_ = f32[16,128]{1,0:T(8,128)S(1)} collective-permute-done((f32[16,128]{1,0:T(8,128)S(1)}, f32[16,128]{1,0:T(8,128)S(1)}, u32[]{:S(2)}, u32[]{:S(2)}) %collective-permute-start.9) | collective-permute-done | bytes 8224 | tf_op jit(solution)/shard_map/ppermute | solution.py:599
  29.5 1.6 %collective-permute-done.8.refs_8_.refs_10_.refs_7_ = f32[16,128]{1,0:T(8,128)S(1)} collective-permute-done((f32[16,128]{1,0:T(8,128)S(1)}, f32[16,128]{1,0:T(8,128)S(1)}, u32[]{:S(2)}, u32[]{:S(2)}) %collective-permute-start.8) | collective-permute-done | bytes 8224 | tf_op jit(solution)/shard_map/ppermute | solution.py:599
  31.0 0.5 collective-permute-done.7.refs_7_.refs_9_.refs_6_
  31.5 0.6 %middle_parts.1 = (bf16[17,32,128]{2,1,0:T(8,128)(2,1)S(1)}, bf16[17,32,128]{2,1,0:T(8,128)(2,1)S(1)}, bf16[17,32,128]{2,1,0:T(8,128)(2,1)S(1)}, bf16[17,32,128]{2,1,0:T(8,128)(2,1)S(1)}) custom-call(bf16[17,32,128]{2,1,0:T(8,128)(2,1)S(1)} %get-tuple-element.39.refs_0_, bf16[17,32,128]{2,1,0:T(8,128)(2,1)S(1)} %collective-permute-done.refs_0_.refs_1_, ...), custom_call_target="tpu_custom_call" | custom-call | flops 100663296 | bytes 1216512 | tf_op jit(solution)/shard_map/middle_parts/pallas_call | solution.py:570
  32.1 2.5 %collective-permute-start.10 = (bf16[17,32,128]{2,1,0:T(8,128)(2,1)S(1)}, bf16[17,32,128]{2,1,0:T(8,128)(2,1)S(1)}, u32[]{:S(2)}, u32[]{:S(2)}) collective-permute-start(bf16[17,32,128]{2,1,0:T(8,128)(2,1)S(1)} %get-tuple-element.51), channel_id=1, source_target_pairs={{0,3},{1,2},{2,1},{3,0},{4,7},{5,6},{6,5},{7,4},{8,11},{9,10},{10,... | collective-permute-start | bytes 417800 | tf_op jit(solution)/shard_map/ppermute | solution.py:599
  34.6 2.3 %far_parts.1 = (bf16[4,128,128]{2,1,0:T(8,128)(2,1)S(1)}, bf16[4,128,128]{2,1,0:T(8,128)(2,1)S(1)}, bf16[4,128,128]{2,1,0:T(8,128)(2,1)S(1)}, bf16[4,128,128]{2,...) custom-call(bf16[4,128,128]{2,1,0:T(8,128)(2,1)S(1)} %get-tuple-element.43.refs_0_, ...), custom_call_target="tpu_custom_call" | custom-call | flops 1 | bytes 1 | tf_op jit(solution)/shard_map/far_parts/pallas_call | solution.py:570
  37.0 0.1 collective-permute-start.11
  37.1 1.9 %collective-permute-start.16 = (bf16[17,32,128]{2,1,0:T(8,128)(2,1)S(1)}, bf16[17,32,128]{2,1,0:T(8,128)(2,1)S(1)}, u32[]{:S(2)}, u32[]{:S(2)}) collective-permute-start(bf16[17,32,128]{2,1,0:T(8,128)(2,1)S(1)} %get-tuple-element.63), channel_id=1, source_target_pairs={{0,2},{1,3},{2,0},{3,1},{4,6},{5,7},{6,4},{7,5},{8,10},{9,11},{10,... | collective-permute-start | bytes 417800 | tf_op jit(solution)/shard_map/ppermute | solution.py:599
  39.1 0.1 far_sum.1
  39.2 1.6 %collective-permute-start.13 = (bf16[4,128,128]{2,1,0:T(8,128)(2,1)S(1)}, bf16[4,128,128]{2,1,0:T(8,128)(2,1)S(1)}, u32[]{:S(2)}, u32[]{:S(2)}) collective-permute-start(bf16[4,128,128]{2,1,0:T(8,128)(2,1)S(1)} %get-tuple-element.60), channel_id=1, source_target_pairs={{0,24},{4,28},{8,16},{12,20},{16,8},{20,12},{24,0},{28,4},{1,25},{... | collective-permute-start | bytes 393224 | tf_op jit(solution)/shard_map/ppermute | solution.py:599
  40.8 0.5 %collective-permute-start.14 = (bf16[4,128,128]{2,1,0:T(8,128)(2,1)S(1)}, bf16[4,128,128]{2,1,0:T(8,128)(2,1)S(1)}, u32[]{:S(2)}, u32[]{:S(2)}) collective-permute-start(bf16[4,128,128]{2,1,0:T(8,128)(2,1)S(1)} %get-tuple-element.61), channel_id=1, source_target_pairs={{0,16},{4,20},{8,24},{12,28},{16,0},{20,4},{24,8},{28,12},{1,17},{... | collective-permute-start | bytes 393224 | tf_op jit(solution)/shard_map/ppermute | solution.py:599
  41.3 1.5 %collective-permute-start.15 = (bf16[4,128,128]{2,1,0:T(8,128)(2,1)S(1)}, bf16[4,128,128]{2,1,0:T(8,128)(2,1)S(1)}, u32[]{:S(2)}, u32[]{:S(2)}) collective-permute-start(bf16[4,128,128]{2,1,0:T(8,128)(2,1)S(1)} %get-tuple-element.62), channel_id=1, source_target_pairs={{0,8},{4,12},{8,0},{12,4},{16,24},{20,28},{24,16},{28,20},{1,9},{5... | collective-permute-start | bytes 393224 | tf_op jit(solution)/shard_map/ppermute | solution.py:599
  42.8 2.1 %collective-permute-done.11.refs_7_ = bf16[17,32,128]{2,1,0:T(8,128)(2,1)S(1)} collective-permute-done((bf16[17,32,128]{2,1,0:T(8,128)(2,1)S(1)}, bf16[17,32,128]{2,1,0:T(8,128)(2,1)S(1)}, u32[]{:S(2)}, u32[]{:S(2)}) %collective-permute-start.11) | collective-permute-done | bytes 139296 | tf_op jit(solution)/shard_map/ppermute | solution.py:599
  44.9 2.3 %near_early.1 = (bf16[128,2048]{1,0:T(8,128)(2,1)}, bf16[128,2048]{1,0:T(8,128)(2,1)}, bf16[128,2048]{1,0:T(8,128)(2,1)}, bf16[128,2048]{1,0:T(8,128)(2,1)}, f32[4,4,128,128]{3,2,1,0:T(8,128)S(1)}) custom-call(bf16[128,2048]{1,0:T(8,128)(2,1)S(1)} %copy-done, bf16[128,2048]{1,0:T(8,128)(2,1)S(1)} %copy-done.1, bf16[128,2048]{1,0:T(8,128)(2,1)S(1)} %copy-done.2, ...), custom_call_target="tpu_custom_call" | custom-call | flops 2000000000 | bytes 5709824 | tf_op jit(solution)/shard_map/near_early/pallas_call | solution.py:570
  47.3 1.6 %final_last.1 = (bf16[128,2048]{1,0:T(8,128)(2,1)}, bf16[128,2048]{1,0:T(8,128)(2,1)}, bf16[128,2048]{1,0:T(8,128)(2,1)}, bf16[128,2048]{1,0:T(8,128)(2,1)}) custom-call(bf16[128,2048]{1,0:T(8,128)(2,1)S(1)} %copy-done, bf16[128,2048]{1,0:T(8,128)(2,1)S(1)} %copy-done.1, ...), custom_call_target="tpu_custom_call", output_to_operand_aliasing={{0}: (6, {}), {1}: (7, {}), {2}: (8, {}), {3}: (9, {})} | custom-call | flops 1000000000 | bytes 6447104 | tf_op jit(solution)/shard_map/final_last/pallas_call | solution.py:570
  48.9 1.1 %final_own.1 = (bf16[128,2048]{1,0:T(8,128)(2,1)}, bf16[128,2048]{1,0:T(8,128)(2,1)}, bf16[128,2048]{1,0:T(8,128)(2,1)}, bf16[128,2048]{1,0:T(8,128)(2,1)}) custom-call(f32[4,4,128,128]{3,2,1,0:T(8,128)S(1)} %get-tuple-element.53.own_ref, ...), custom_call_target="tpu_custom_call", output_to_operand_aliasing={{0}: (6, {}), {1}: (7, {}), {2}: (8, {}), {3}: (9, {})} | custom-call | flops 16777216 | bytes 5906432 | tf_op jit(solution)/shard_map/final_own/pallas_call | solution.py:570
  (26 shorter events, 0.2 us)
Async XLA Ops:
  6.1 9.2 %collective-permute-start = (bf16[17,32,128]{2,1,0:T(8,128)(2,1)}, bf16[17,32,128]{2,1,0:T(8,128)(2,1)S(1)}, u32[]{:S(2)}, u32[]{:S(2)}) collective-permute-start(bf16[17,32,128]{2,1,0:T(8,128)(2,1)} %get-tuple-element.40), channel_id=1, source_target_pairs={{0,3},{1,2},{2,1},{3,0},{4,7},{5,6},{6,5},{7,4},{8,11},{9,10},{10,... | collective-permute-start | bytes 417800 | tf_op jit(solution)/shard_map/ppermute | solution.py:599
  11.2 7.6 %collective-permute-start.3 = (bf16[4,128,128]{2,1,0:T(8,128)(2,1)S(1)}, bf16[4,128,128]{2,1,0:T(8,128)(2,1)S(1)}, u32[]{:S(2)}, u32[]{:S(2)}) collective-permute-start(bf16[4,128,128]{2,1,0:T(8,128)(2,1)S(1)} %get-tuple-element.44), channel_id=1, source_target_pairs={{0,8},{4,12},{8,0},{12,4},{16,24},{20,28},{24,16},{28,20},{1,9},{5... | collective-permute-start | bytes 393224 | tf_op jit(solution)/shard_map/ppermute | solution.py:599
  12.7 7.8 %collective-permute-start.4 = (bf16[4,128,128]{2,1,0:T(8,128)(2,1)S(1)}, bf16[4,128,128]{2,1,0:T(8,128)(2,1)S(1)}, u32[]{:S(2)}, u32[]{:S(2)}) collective-permute-start(bf16[4,128,128]{2,1,0:T(8,128)(2,1)S(1)} %get-tuple-element.45), channel_id=1, source_target_pairs={{0,16},{4,20},{8,24},{12,28},{16,0},{20,4},{24,8},{28,12},{1,17},{... | collective-permute-start | bytes 393224 | tf_op jit(solution)/shard_map/ppermute | solution.py:599
  14.2 6.3 %collective-permute-start.5 = (bf16[4,128,128]{2,1,0:T(8,128)(2,1)S(1)}, bf16[4,128,128]{2,1,0:T(8,128)(2,1)S(1)}, u32[]{:S(2)}, u32[]{:S(2)}) collective-permute-start(bf16[4,128,128]{2,1,0:T(8,128)(2,1)S(1)} %get-tuple-element.46), channel_id=1, source_target_pairs={{0,24},{4,28},{8,16},{12,20},{16,8},{20,12},{24,0},{28,4},{1,25},{... | collective-permute-start | bytes 393224 | tf_op jit(solution)/shard_map/ppermute | solution.py:599
  14.7 8.5 %collective-permute-start.1 = (bf16[17,32,128]{2,1,0:T(8,128)(2,1)S(1)}, bf16[17,32,128]{2,1,0:T(8,128)(2,1)S(1)}, u32[]{:S(2)}, u32[]{:S(2)}) collective-permute-start(bf16[17,32,128]{2,1,0:T(8,128)(2,1)S(1)} %get-tuple-element.41), channel_id=1, source_target_pairs={{0,1},{1,0},{2,3},{3,2},{4,5},{5,4},{6,7},{7,6},{8,9},{9,8},{10,11... | collective-permute-start | bytes 417800 | tf_op jit(solution)/shard_map/ppermute | solution.py:599
  15.3 9.0 %collective-permute-start.2 = (bf16[17,32,128]{2,1,0:T(8,128)(2,1)S(1)}, bf16[17,32,128]{2,1,0:T(8,128)(2,1)S(1)}, u32[]{:S(2)}, u32[]{:S(2)}) collective-permute-start(bf16[17,32,128]{2,1,0:T(8,128)(2,1)S(1)} %get-tuple-element.42), channel_id=1, source_target_pairs={{0,2},{1,3},{2,0},{3,1},{4,6},{5,7},{6,4},{7,5},{8,10},{9,11},{10,... | collective-permute-start | bytes 417800 | tf_op jit(solution)/shard_map/ppermute | solution.py:599
  20.5 1.6 %collective-permute-start.6 = (bf16[4,2,128,128]{3,2,1,0:T(8,128)(2,1)S(1)}, bf16[4,2,128,128]{3,2,1,0:T(8,128)(2,1)S(1)}, u32[]{:S(2)}, u32[]{:S(2)}) collective-permute-start(bf16[4,2,128,128]{3,2,1,0:T(8,128)(2,1)S(1)} %pack.1), channel_id=1, source_target_pairs={{0,4},{4,0},{8,12},{12,8},{16,20},{20,16},{24,28},{28,24},{1,5},{5... | collective-permute-start | bytes 786440 | tf_op jit(solution)/shard_map/ppermute | solution.py:599
  24.9 4.6 %collective-permute-start.9 = (f32[16,128]{1,0:T(8,128)S(1)}, f32[16,128]{1,0:T(8,128)S(1)}, u32[]{:S(2)}, u32[]{:S(2)}) collective-permute-start(f32[16,128]{1,0:T(8,128)S(1)} %get-tuple-element.49.refs_6_.refs_8_.refs_5_), channel_id=1, source_target_pairs={{0,24},{4,28},{8,16},{12,20},{16,8},{20,12},{24,0},{28,4},{1,25},{... | collective-permute-start | bytes 24584 | tf_op jit(solution)/shard_map/ppermute | solution.py:599
  27.4 3.7 %collective-permute-start.8 = (f32[16,128]{1,0:T(8,128)S(1)}, f32[16,128]{1,0:T(8,128)S(1)}, u32[]{:S(2)}, u32[]{:S(2)}) collective-permute-start(f32[16,128]{1,0:T(8,128)S(1)} %get-tuple-element.49.refs_6_.refs_8_.refs_5_), channel_id=1, source_target_pairs={{0,16},{4,20},{8,24},{12,28},{16,0},{20,4},{24,8},{28,12},{1,17},{... | collective-permute-start | bytes 24584 | tf_op jit(solution)/shard_map/ppermute | solution.py:599
  27.9 3.7 %collective-permute-start.7 = (f32[16,128]{1,0:T(8,128)S(1)}, f32[16,128]{1,0:T(8,128)S(1)}, u32[]{:S(2)}, u32[]{:S(2)}) collective-permute-start(f32[16,128]{1,0:T(8,128)S(1)} %get-tuple-element.49.refs_6_.refs_8_.refs_5_), channel_id=1, source_target_pairs={{0,8},{4,12},{8,0},{12,4},{16,24},{20,28},{24,16},{28,20},{1,9},{5... | collective-permute-start | bytes 24584 | tf_op jit(solution)/shard_map/ppermute | solution.py:599
  32.1 6.9 %collective-permute-start.10 = (bf16[17,32,128]{2,1,0:T(8,128)(2,1)S(1)}, bf16[17,32,128]{2,1,0:T(8,128)(2,1)S(1)}, u32[]{:S(2)}, u32[]{:S(2)}) collective-permute-start(bf16[17,32,128]{2,1,0:T(8,128)(2,1)S(1)} %get-tuple-element.51), channel_id=1, source_target_pairs={{0,3},{1,2},{2,1},{3,0},{4,7},{5,6},{6,5},{7,4},{8,11},{9,10},{10,... | collective-permute-start | bytes 417800 | tf_op jit(solution)/shard_map/ppermute | solution.py:599
  36.9 2.1 %collective-permute-start.12 = (bf16[4,2,128,128]{3,2,1,0:T(8,128)(2,1)S(1)}, bf16[4,2,128,128]{3,2,1,0:T(8,128)(2,1)S(1)}, u32[]{:S(2)}, u32[]{:S(2)}) collective-permute-start(bf16[4,2,128,128]{3,2,1,0:T(8,128)(2,1)S(1)} %get-tuple-element.58), channel_id=1, source_target_pairs={{0,4},{4,0},{8,12},{12,8},{16,20},{20,16},{24,28},{28,24},{1,5},{5... | collective-permute-start | bytes 786440 | tf_op jit(solution)/shard_map/ppermute | solution.py:599
  37.0 7.9 %collective-permute-start.11 = (bf16[17,32,128]{2,1,0:T(8,128)(2,1)S(1)}, bf16[17,32,128]{2,1,0:T(8,128)(2,1)S(1)}, u32[]{:S(2)}, u32[]{:S(2)}) collective-permute-start(bf16[17,32,128]{2,1,0:T(8,128)(2,1)S(1)} %get-tuple-element.52), channel_id=1, source_target_pairs={{0,1},{1,0},{2,3},{3,2},{4,5},{5,4},{6,7},{7,6},{8,9},{9,8},{10,11... | collective-permute-start | bytes 417800 | tf_op jit(solution)/shard_map/ppermute | solution.py:599
  37.1 10.2 %collective-permute-start.16 = (bf16[17,32,128]{2,1,0:T(8,128)(2,1)S(1)}, bf16[17,32,128]{2,1,0:T(8,128)(2,1)S(1)}, u32[]{:S(2)}, u32[]{:S(2)}) collective-permute-start(bf16[17,32,128]{2,1,0:T(8,128)(2,1)S(1)} %get-tuple-element.63), channel_id=1, source_target_pairs={{0,2},{1,3},{2,0},{3,1},{4,6},{5,7},{6,4},{7,5},{8,10},{9,11},{10,... | collective-permute-start | bytes 417800 | tf_op jit(solution)/shard_map/ppermute | solution.py:599
  39.1 5.8 %copy-start.1 = (bf16[128,2048]{1,0:T(8,128)(2,1)S(1)}, bf16[128,2048]{1,0:T(8,128)(2,1)}, u32[]{:S(2)}) copy-start(bf16[128,2048]{1,0:T(8,128)(2,1)} %refs_1_.5) | copy-start | bytes 1572868
  39.1 5.8 %copy-start.2 = (bf16[128,2048]{1,0:T(8,128)(2,1)S(1)}, bf16[128,2048]{1,0:T(8,128)(2,1)}, u32[]{:S(2)}) copy-start(bf16[128,2048]{1,0:T(8,128)(2,1)} %refs_2_.5) | copy-start | bytes 1572868
  39.1 5.8 %copy-start.3 = (bf16[128,2048]{1,0:T(8,128)(2,1)S(1)}, bf16[128,2048]{1,0:T(8,128)(2,1)}, u32[]{:S(2)}) copy-start(bf16[128,2048]{1,0:T(8,128)(2,1)} %refs_3_.5) | copy-start | bytes 1572868
  39.1 5.8 %copy-start = (bf16[128,2048]{1,0:T(8,128)(2,1)S(1)}, bf16[128,2048]{1,0:T(8,128)(2,1)}, u32[]{:S(2)}) copy-start(bf16[128,2048]{1,0:T(8,128)(2,1)} %refs_0_.5) | copy-start | bytes 1572868
  39.2 9.7 %collective-permute-start.13 = (bf16[4,128,128]{2,1,0:T(8,128)(2,1)S(1)}, bf16[4,128,128]{2,1,0:T(8,128)(2,1)S(1)}, u32[]{:S(2)}, u32[]{:S(2)}) collective-permute-start(bf16[4,128,128]{2,1,0:T(8,128)(2,1)S(1)} %get-tuple-element.60), channel_id=1, source_target_pairs={{0,24},{4,28},{8,16},{12,20},{16,8},{20,12},{24,0},{28,4},{1,25},{... | collective-permute-start | bytes 393224 | tf_op jit(solution)/shard_map/ppermute | solution.py:599
  40.8 8.1 %collective-permute-start.14 = (bf16[4,128,128]{2,1,0:T(8,128)(2,1)S(1)}, bf16[4,128,128]{2,1,0:T(8,128)(2,1)S(1)}, u32[]{:S(2)}, u32[]{:S(2)}) collective-permute-start(bf16[4,128,128]{2,1,0:T(8,128)(2,1)S(1)} %get-tuple-element.61), channel_id=1, source_target_pairs={{0,16},{4,20},{8,24},{12,28},{16,0},{20,4},{24,8},{28,12},{1,17},{... | collective-permute-start | bytes 393224 | tf_op jit(solution)/shard_map/ppermute | solution.py:599
  41.3 7.6 %collective-permute-start.15 = (bf16[4,128,128]{2,1,0:T(8,128)(2,1)S(1)}, bf16[4,128,128]{2,1,0:T(8,128)(2,1)S(1)}, u32[]{:S(2)}, u32[]{:S(2)}) collective-permute-start(bf16[4,128,128]{2,1,0:T(8,128)(2,1)S(1)} %get-tuple-element.62), channel_id=1, source_target_pairs={{0,8},{4,12},{8,0},{12,4},{16,24},{20,28},{24,16},{28,20},{1,9},{5... | collective-permute-start | bytes 393224 | tf_op jit(solution)/shard_map/ppermute | solution.py:599

commit v13 on v11

--- a/solution.py
+++ b/solution.py
@@ -48,6 +48,20 @@
 def position(slots):
     width = lax.axis_size("seqo") // slots
     return lax.axis_index("seqi"), lax.axis_index("seqo") // width
+
+
+def distance(n_i, step, odd):
+    order = [1, *range(n_i - 1, 1, -1)] if odd else list(range(n_i - 1, 0, -1))
+    return order[step - 1]
+
+
+def place_at(n_i, slots, step):
+    pos, _ = position(slots)
+    if step == 0:
+        return pos * slots
+    odd = lax.axis_index("seqo") % 2 == 1
+    far = jnp.where(odd, distance(n_i, step, True), distance(n_i, step, False))
+    return (pos ^ far) * slots
 
 
 def lanes_of(rows):
@@ -160,7 +174,7 @@
     turn[...] = turn[...].T
     near = split(pick_rows(turn, rows))
     for d in range(n_i):
-        mids[d][: 4 * slots] = picked[pos ^ d]
+        mids[d][: 4 * slots] = picked[place_at(n_i, slots, d) // slots]
         mids[d][4 * slots] = near
     for m in range(slots):
         fulls[m][...] = buffers[:, :, head_columns(pos * slots + (chip ^ m))]
@@ -193,7 +207,7 @@
 
 
 def middle_stats_kernel(n_i, slots, *refs):
-    mids, refs = in_order(refs[:n_i]), refs[n_i:]
+    mids, refs = refs[:n_i], refs[n_i:]
     near_ref, far_ref, xmsg_ref, stats_ref, columns_ref, turn, spread = refs
     rows = near_ref.shape[1]
     quarter = rows // DILATION
@@ -225,7 +239,7 @@
 
 
 def middle_parts_kernel(n_i, slots, *refs):
-    mids, refs = in_order(refs[:n_i]), refs[n_i:]
+    mids, refs = refs[:n_i], refs[n_i:]
     stats_ref, columns_ref = refs[:2]
     refs = refs[2:]
     xmsgs, refs = refs[:slots], refs[slots:]
@@ -312,14 +326,14 @@
         outs[m][2:] = total.astype(BF16)
 
 
-def near_statistics(slots, places, near_ref, mids, xmsgs, stats_ref, spread):
+def near_statistics(n_i, slots, steps, near_ref, mids, xmsgs, stats_ref, spread):
     rows = near_ref.shape[1]
     quarter = rows // DILATION
     pos, chip = position(slots)
     lane = lanes_of(quarter)
     mid = jnp.zeros((quarter, LANES), F32)
-    for d, ref in zip(places, mids):
-        place = (pos ^ d) * slots
+    for step, ref in zip(steps, mids):
+        place = place_at(n_i, slots, step)
         found = join(ref)
         e = pltpu.roll(found, place, 1)
         de = pltpu.roll(found, place + HEADS - slots, 1)
@@ -346,9 +360,8 @@
     stats_ref[HEADS:] = d
 
 
-def near_place(slots, d, sources, stats_ref):
-    pos, _ = position(slots)
-    heads = [(pos ^ d) * slots + slot for slot in range(slots)]
+def near_place(n_i, slots, step, sources, stats_ref):
+    heads = [place_at(n_i, slots, step) + slot for slot in range(slots)]
     operands = [[ref[:, head_columns(head)] for ref in sources] for head in heads]
     stats = [(stats_ref[pl.ds(head, 1), :], stats_ref[pl.ds(HEADS + head, 1), :]) for head in heads]
     return level_parts(operands, stats)
@@ -358,12 +371,11 @@
     sources, near_ref, refs = refs[:4], refs[4], refs[5:]
     mids, refs = refs[: n_i - 1], refs[n_i - 1 :]
     xmsgs, (out_ref, stats_ref, spread) = refs[:slots], refs[slots:]
-    places = in_turn(list(range(n_i)))[:-1]
-    near_statistics(slots, places, near_ref, mids, xmsgs, stats_ref, spread)
-    for index, d in enumerate(places):
-        for slot, parts in enumerate(near_place(slots, d, sources, stats_ref)):
+    near_statistics(n_i, slots, range(n_i - 1), near_ref, mids, xmsgs, stats_ref, spread)
+    for step in range(n_i - 1):
+        for slot, parts in enumerate(near_place(n_i, slots, step, sources, stats_ref)):
             for which, part in enumerate(parts):
-                out_ref[which, index * slots + slot] = part
+                out_ref[which, step * slots + slot] = part
 
 
 def far_sum_kernel(slots, *refs):
@@ -425,21 +437,18 @@
                 out_ref[which, head] = part
 
 
-def spread_rows(slots, d, slot, ref):
+def spread_rows(slots, head, slot, ref):
     quarter = ref.shape[1]
     rows = quarter * DILATION
-    pos, _ = position(slots)
-    head = (pos ^ d) * slots + slot
     row = lax.broadcasted_iota(jnp.int32, (rows, quarter), 0)
     taken = lax.broadcasted_iota(jnp.int32, (rows, quarter), 1) * DILATION
     place = jnp.where(row == taken + head % DILATION, 1.0, 0.0).astype(BF16)
     return dot(place, jnp.concatenate([ref[which * slots + slot] for which in range(4)], axis=1))
 
 
-def send_place(slots, d, ready, outs, sems):
-    pos, _ = position(slots)
+def send_place(slots, first, ready, outs, sems):
     width = slots * HEAD_DIM
-    cols = pl.ds(pl.multiple_of((pos ^ d) * width, width), width)
+    cols = pl.ds(pl.multiple_of(first * HEAD_DIM, width), width)
     copies = [
         pltpu.make_async_copy(ready.at[which], out.at[:, cols], sems.at[which])
         for which, out in enumerate(outs)
@@ -453,21 +462,19 @@
     sources, near_ref, early_ref, refs = refs[:4], refs[4], refs[5], refs[6:]
     mids, refs = refs[: n_i - 1], refs[n_i - 1 :]
     outs, (ready, sems, stats_ref, spread) = refs[:4], refs[4:]
-    places = in_turn(list(range(n_i)))[1:]
-    near_statistics(slots, places[-1:], near_ref, mids[-1:], (), stats_ref, spread)
-    late = near_place(slots, places[-1], sources, stats_ref)
+    last = n_i - 1
+    near_statistics(n_i, slots, [last], near_ref, mids[-1:], (), stats_ref, spread)
+    late = near_place(n_i, slots, last, sources, stats_ref)
     copies = []
-    for index, d in enumerate(places):
-        found = [spread_rows(slots, d, slot, mids[index]) for slot in range(slots)]
+    for step in range(1, n_i):
+        first = place_at(n_i, slots, step)
+        found = [spread_rows(slots, first + slot, slot, mids[step - 1]) for slot in range(slots)]
         for slot, parts in enumerate(found):
             for which in range(4):
-                if d == places[-1]:
-                    near = late[slot][which]
-                else:
-                    near = early_ref[which, (index + 1) * slots + slot]
+                near = late[slot][which] if step == last else early_ref[which, step * slots + slot]
                 total = near + parts[:, static_columns(which)]
-                ready[index, which, :, static_columns(slot)] = total.astype(BF16)
-        copies += send_place(slots, d, ready.at[index], outs, sems.at[index])
+                ready[step - 1, which, :, static_columns(slot)] = total.astype(BF16)
+        copies += send_place(slots, first, ready.at[step - 1], outs, sems.at[step - 1])
     for copy in copies:
         copy.wait()
 
@@ -475,15 +482,16 @@
 def final_own_kernel(slots, early_ref, mid_ref, *refs):
     fulls, refs = in_back(refs[:slots]), refs[slots:]
     outs, (ready, sems) = refs[4:8], refs[8:]
-    _, chip = position(slots)
-    found = [spread_rows(slots, 0, chip ^ m, mid_ref) for m in range(slots)]
+    pos, chip = position(slots)
+    first = pos * slots
+    found = [spread_rows(slots, first + (chip ^ m), chip ^ m, mid_ref) for m in range(slots)]
     for m, parts in enumerate(found):
         slot = chip ^ m
         for which in range(4):
             total = early_ref[which, slot] + parts[:, static_columns(which)]
             total += fulls[m][which].astype(F32)
             ready[which, :, head_columns(slot)] = total.astype(BF16)
-    for copy in send_place(slots, 0, ready, outs, sems):
+    for copy in send_place(slots, first, ready, outs, sems):
         copy.wait()
 
 
@@ -511,16 +519,8 @@
     )(*operands)
 
 
-def in_turn(pieces):
-    return [pieces[0], pieces[-1], *pieces[1:-1]]
-
-
 def in_back(pieces):
     return [pieces[0], *pieces[:0:-1]]
-
-
-def in_order(pieces):
-    return [pieces[0], *pieces[2:], pieces[1]]
 
 
 def swap(x, axis, n, mask):
@@ -547,8 +547,15 @@
         return SHAPE((count, lanes), F32)
 
     def swap_mids(pieces):
-        found = {d: swap(pieces[d], "seqi", n_i, d) for d in reversed(range(1, n_i))}
-        return [pieces[0]] + [found[d] for d in range(1, n_i)]
+        found = [pieces[0]]
+        for step in range(1, n_i):
+            pairs = [
+                (o * n_i + i, o * n_i + (i ^ distance(n_i, step, o % 2 == 1)))
+                for o in range(n_o)
+                for i in range(n_i)
+            ]
+            found.append(lax.ppermute(pieces[step], ("seqo", "seqi"), pairs))
+        return found
 
     def swap_fulls(pieces):
         return [pieces[0]] + [swap(pieces[m], "seqo", n_o, m * width) for m in range(1, slots)]
@@ -573,7 +580,7 @@
     fulls = swap_fulls(pieces[n_i : n_i + slots])
     near = pieces[-1]
 
-    (settled,) = call(settle_kernel, "far_in", [stats(8)], [], SHORT, [mids[-1]])
+    (settled,) = call(settle_kernel, "far_in", [stats(8)], [], SHORT, [mids[1]])
     (settled,) = call(settle_kernel, "chips_back", [stats(8)], [], LONG, [settled])
     (packed,) = call(bind(pack_kernel, slots), "pack", [half], [], 1, fulls + [settled])
     sibs = [swap(packed, "seqo", n_o, part) for part in range(1, width)]
@@ -592,7 +599,7 @@
         [stats(4 * slots), stats(2 * slots, n_i * quarter), stats(n_i * quarter, LANES)],
         [pltpu.VMEM((LANES, n_i * quarter), F32), square],
         unit * slots * 2,
-        in_turn(mids) + [near, far],
+        mids + [near, far],
     )
     xmsgs = swap_fulls([xmsg] * slots)
 
@@ -602,7 +609,7 @@
         [mid] * n_i,
         [pltpu.VMEM((2 * slots, rows), F32), pltpu.VMEM((LANES, n_i * quarter), F32), square],
         unit * slots * 6,
-        in_turn(mids) + [middle, columns] + xmsgs,
+        mids + [middle, columns] + xmsgs,
     )
     midparts = swap_mids(midparts)
     farparts = call(
@@ -615,7 +622,7 @@
         cheap=True,
     )
     sibparts = [swap(x, "seqo", n_o, part + 1) for part, x in enumerate(farparts[slots:])]
-    (settled,) = call(settle_kernel, "far_back", [stats(8)], [], SHORT, [midparts[-1]])
+    (settled,) = call(settle_kernel, "far_back", [stats(8)], [], SHORT, [midparts[1]])
     (settled,) = call(settle_kernel, "sib_back", [stats(8)], [], 1, sibparts + [settled])
     (settled,) = call(settle_kernel, "settle", [stats(8)], [], LONG, [settled])
     fullparts = call(
@@ -629,7 +636,7 @@
     )
     fullparts = swap_fulls(fullparts)
 
-    back = in_turn(midparts)
+    back = midparts
     kept = [pltpu.VMEM((2 * HEADS, rows), F32), square]
     (early,) = call(
         bind(near_early_kernel, n_i, slots),

time: 48.8 us -> 50 us (1.025)
  waiting for transfers between devices: 10.9 us -> 15 us
  starting transfers between devices: 23.8 us -> 21 us
    ppermute x17 -> x11, starting transfers between devices: 23.8 us -> 10.7 us  [swap(): return lax.ppermute(x, axis, [(i, i ^ mask) for i in range(n)])]
    ppermute x0 -> x6, starting transfers between devices: none -> 10.3 us  [swap_mids(): found.append(lax.ppermute(pieces[step], ('seqo', 'seqi'), pairs))]
    ppermute x0 -> x6, waiting for transfers between devices: none -> 6 us  [swap_mids(): found.append(lax.ppermute(pieces[step], ('seqo', 'seqi'), pairs))]
    ppermute x17 -> x11, waiting for transfers between devices: 10.9 us -> 9 us  [swap(): return lax.ppermute(x, axis, [(i, i ^ mask) for i in range(n)])]
  transfers between devices with their start and end apart: 17 -> 17, of which waited for: 9 -> 11; matrix products, arithmetic and copies ran while one was open for 0% -> 0% of each run, Pallas kernels for 14% -> 14%
where the time goes in v13:
time: 50 us; the launch traced here: 49.9 us
  starting transfers between devices  21 us (42%)
  waiting for transfers between devices  15 us (30%)
  Pallas kernels  13 us (26%)
  between operations  0.81 us (2%)
    pallas_call x16, Pallas kernels, call(): pl.pallas_call(kernel, out_shape=tuple(outs), in_specs=[pl.BlockSpec(memo...  13 us
    ppermute x11, starting transfers between devices, swap(): return lax.ppermute(x, axis, [(i, i ^ mask) for i in range(n)])  10.7 us
    ppermute x6, starting transfers between devices, swap_mids(): found.append(lax.ppermute(pieces[step], ('seqo', 'seqi'), pairs))  10.3 us
    ppermute x11, waiting for transfers between devices, swap(): return lax.ppermute(x, axis, [(i, i ^ mask) for i in range(n)])  9 us
    ppermute x6, waiting for transfers between devices, swap_mids(): found.append(lax.ppermute(pieces[step], ('seqo', 'seqi'), pairs))  6 us
  transfers between devices with their start and end apart: 17, of which 11 were waited for; matrix products, arithmetic and copies ran while one was open for 0% of the time, Pallas kernels for 14%

profile of v13, /device:TPU:0, one launch (start us, length us, event | category | flops | bytes accessed | tf_op | source)
XLA Modules:
  0.0 49.9 jit_solution(14090579112571013399)
XLA Ops:
  0.6 3.9 %pick.1 = (bf16[17,32,128]{2,1,0:T(8,128)(2,1)S(1)}, bf16[17,32,128]{2,1,0:T(8,128)(2,1)S(1)}, bf16[17,32,128]{2,1,0:T(8,128)(2,1)S(1)}, bf16[17,32,128]{2,1,0:T...) custom-call(bf16[128,2048]{1,0:T(8,128)(2,1)} %refs_0_.5, ...), custom_call_target="tpu_custom_call" | custom-call | flops 134217728 | bytes 3194880 | tf_op jit(solution)/shard_map/pick/pallas_call | solution.py:507
  4.6 5.1 %collective-permute-start = (bf16[17,32,128]{2,1,0:T(8,128)(2,1)S(1)}, bf16[17,32,128]{2,1,0:T(8,128)(2,1)S(1)}, u32[]{:S(2)}, u32[]{:S(2)}) collective-permute-start(bf16[17,32,128]{2,1,0:T(8,128)(2,1)S(1)} %get-tuple-element.35), channel_id=1, source_target_pairs={{0,3},{1,2},{2,1},{3,0},{4,5},{5,4},{6,7},{7,6},{8,11},{9,10},{10,... | collective-permute-start | bytes 417800 | tf_op jit(solution)/shard_map/ppermute | solution.py:557
  9.7 1.5 %collective-permute-start.3 = (bf16[4,128,128]{2,1,0:T(8,128)(2,1)S(1)}, bf16[4,128,128]{2,1,0:T(8,128)(2,1)S(1)}, u32[]{:S(2)}, u32[]{:S(2)}) collective-permute-start(bf16[4,128,128]{2,1,0:T(8,128)(2,1)S(1)} %get-tuple-element.39), channel_id=1, source_target_pairs={{0,8},{4,12},{8,0},{12,4},{16,24},{20,28},{24,16},{28,20},{1,9},{5... | collective-permute-start | bytes 393224 | tf_op jit(solution)/shard_map/ppermute | solution.py:527
  11.2 1.5 %collective-permute-start.4 = (bf16[4,128,128]{2,1,0:T(8,128)(2,1)S(1)}, bf16[4,128,128]{2,1,0:T(8,128)(2,1)S(1)}, u32[]{:S(2)}, u32[]{:S(2)}) collective-permute-start(bf16[4,128,128]{2,1,0:T(8,128)(2,1)S(1)} %get-tuple-element.40), channel_id=1, source_target_pairs={{0,16},{4,20},{8,24},{12,28},{16,0},{20,4},{24,8},{28,12},{1,17},{... | collective-permute-start | bytes 393224 | tf_op jit(solution)/shard_map/ppermute | solution.py:527
  12.7 0.5 collective-permute-start.5
  13.2 0.4 collective-permute-done.refs_0_.refs_1_
  13.6 0.7 %collective-permute-start.2 = (bf16[17,32,128]{2,1,0:T(8,128)(2,1)}, bf16[17,32,128]{2,1,0:T(8,128)(2,1)S(1)}, u32[]{:S(2)}, u32[]{:S(2)}) collective-permute-start(bf16[17,32,128]{2,1,0:T(8,128)(2,1)} %get-tuple-element.37), channel_id=1, source_target_pairs={{0,1},{1,0},{2,3},{3,2},{4,6},{5,7},{6,4},{7,5},{8,9},{9,8},{10,11... | collective-permute-start | bytes 417800 | tf_op jit(solution)/shard_map/ppermute | solution.py:557
  14.2 0.8 %collective-permute-done.3.refs_1_ = bf16[4,128,128]{2,1,0:T(8,128)(2,1)S(1)} collective-permute-done((bf16[4,128,128]{2,1,0:T(8,128)(2,1)S(1)}, bf16[4,128,128]{2,1,0:T(8,128)(2,1)S(1)}, u32[]{:S(2)}, u32[]{:S(2)}) %collective-permute-start.3) | collective-permute-done | bytes 131104 | tf_op jit(solution)/shard_map/ppermute | solution.py:527
  15.1 1.2 %collective-permute-done.4.refs_2_ = bf16[4,128,128]{2,1,0:T(8,128)(2,1)S(1)} collective-permute-done((bf16[4,128,128]{2,1,0:T(8,128)(2,1)S(1)}, bf16[4,128,128]{2,1,0:T(8,128)(2,1)S(1)}, u32[]{:S(2)}, u32[]{:S(2)}) %collective-permute-start.4) | collective-permute-done | bytes 131104 | tf_op jit(solution)/shard_map/ppermute | solution.py:527
  16.3 2.3 %collective-permute-done.5.refs_3_ = bf16[4,128,128]{2,1,0:T(8,128)(2,1)S(1)} collective-permute-done((bf16[4,128,128]{2,1,0:T(8,128)(2,1)S(1)}, bf16[4,128,128]{2,1,0:T(8,128)(2,1)S(1)}, u32[]{:S(2)}, u32[]{:S(2)}) %collective-permute-start.5) | collective-permute-done | bytes 131104 | tf_op jit(solution)/shard_map/ppermute | solution.py:527
  18.7 1.5 %collective-permute-done.6.refs_4_ = bf16[4,2,128,128]{3,2,1,0:T(8,128)(2,1)S(1)} collective-permute-done((bf16[4,2,128,128]{3,2,1,0:T(8,128)(2,1)S(1)}, bf16[4,2,128,128]{3,2,1,0:T(8,128)(2,1)S(1)}, u32[]{:S(2)}, u32[]{:S(2)}) %collective-permute-start.6) | collective-permute-done | bytes 262176 | tf_op jit(solution)/shard_map/ppermute | solution.py:527
  20.2 1.1 %far_stats.1.refs_5_ = f32[8,128]{1,0:T(8,128)S(1)} custom-call(bf16[4,128,128]{2,1,0:T(8,128)(2,1)S(1)} %get-tuple-element.38.refs_0_, bf16[4,128,128]{2,1,0:T(8,128)(2,1)S(1)} %collective-permute-done.3.refs_1_, bf16[4,128,128]{2,1,0:T(8,128)(2,1)S(1)} %collective-permute-done.4.refs_2_, bf16[4,128,128]{2,1,0:T(8,128)(2,1)S(1)} %collective-permute-done.5.refs_3_, ...), custom_call_target="tpu_custom_call" | custom-call | flops 1 | bytes 794624 | tf_op jit(solution)/shard_map/far_stats/pallas_call | solution.py:507
  21.3 0.7 %collective-permute-done.1.refs_2_ = bf16[17,32,128]{2,1,0:T(8,128)(2,1)S(1)} collective-permute-done((bf16[17,32,128]{2,1,0:T(8,128)(2,1)S(1)}, bf16[17,32,128]{2,1,0:T(8,128)(2,1)S(1)}, u32[]{:S(2)}, u32[]{:S(2)}) %collective-permute-start.1) | collective-permute-done | bytes 139296 | tf_op jit(solution)/shard_map/ppermute | solution.py:557
  22.0 0.5 %middle_stats.1 = (f32[16,128]{1,0:T(8,128)S(1)}, f32[8,128]{1,0:T(8,128)S(1)}, f32[128,128]{1,0:T(8,128)S(1)}) custom-call(bf16[17,32,128]{2,1,0:T(8,128)(2,1)S(1)} %get-tuple-element.34.refs_0_, bf16[17,32,128]{2,1,0:T(8,128)(2,1)S(1)} %collective-permute-done.refs_0_.refs_1_, bf16[17,32,128]{2,1,0:T(8,128)(2,1)S(1)} %collective-permute-done.1.refs_2_, ...), custom_call_target="tpu_custom_call" | custom-call | flops 33554432 | bytes 655360 | tf_op jit(solution)/shard_map/middle_stats/pallas_call | solution.py:507
  22.5 2.5 %collective-permute-start.9 = (f32[16,128]{1,0:T(8,128)S(1)}, f32[16,128]{1,0:T(8,128)S(1)}, u32[]{:S(2)}, u32[]{:S(2)}) collective-permute-start(f32[16,128]{1,0:T(8,128)S(1)} %get-tuple-element.44.refs_6_.refs_8_.refs_5_), channel_id=1, source_target_pairs={{0,24},{4,28},{8,16},{12,20},{16,8},{20,12},{24,0},{28,4},{1,25},{... | collective-permute-start | bytes 24584 | tf_op jit(solution)/shard_map/ppermute | solution.py:527
  25.0 0.5 collective-permute-start.8
  25.5 0.5 %collective-permute-start.7 = (f32[16,128]{1,0:T(8,128)S(1)}, f32[16,128]{1,0:T(8,128)S(1)}, u32[]{:S(2)}, u32[]{:S(2)}) collective-permute-start(f32[16,128]{1,0:T(8,128)S(1)} %get-tuple-element.44.refs_6_.refs_8_.refs_5_), channel_id=1, source_target_pairs={{0,8},{4,12},{8,0},{12,4},{16,24},{20,28},{24,16},{28,20},{1,9},{5... | collective-permute-start | bytes 24584 | tf_op jit(solution)/shard_map/ppermute | solution.py:527
  26.0 1.1 %collective-permute-done.9.refs_9_.refs_11_.refs_8_ = f32[16,128]{1,0:T(8,128)S(1)} collective-permute-done((f32[16,128]{1,0:T(8,128)S(1)}, f32[16,128]{1,0:T(8,128)S(1)}, u32[]{:S(2)}, u32[]{:S(2)}) %collective-permute-start.9) | collective-permute-done | bytes 8224 | tf_op jit(solution)/shard_map/ppermute | solution.py:527
  27.1 1.6 %collective-permute-done.8.refs_8_.refs_10_.refs_7_ = f32[16,128]{1,0:T(8,128)S(1)} collective-permute-done((f32[16,128]{1,0:T(8,128)S(1)}, f32[16,128]{1,0:T(8,128)S(1)}, u32[]{:S(2)}, u32[]{:S(2)}) %collective-permute-start.8) | collective-permute-done | bytes 8224 | tf_op jit(solution)/shard_map/ppermute | solution.py:527
  28.7 0.5 collective-permute-done.7.refs_7_.refs_9_.refs_6_
  29.2 0.6 %middle_parts.1 = (bf16[17,32,128]{2,1,0:T(8,128)(2,1)S(1)}, bf16[17,32,128]{2,1,0:T(8,128)(2,1)S(1)}, bf16[17,32,128]{2,1,0:T(8,128)(2,1)S(1)}, bf16[17,32,128]{2,1,0:T(8,128)(2,1)S(1)}) custom-call(bf16[17,32,128]{2,1,0:T(8,128)(2,1)S(1)} %get-tuple-element.34.refs_0_, bf16[17,32,128]{2,1,0:T(8,128)(2,1)S(1)} %collective-permute-done.refs_0_.refs_1_, ...), custom_call_target="tpu_custom_call" | custom-call | flops 100663296 | bytes 1216512 | tf_op jit(solution)/shard_map/middle_parts/pallas_call | solution.py:507
  29.8 2.3 %collective-permute-start.10 = (bf16[17,32,128]{2,1,0:T(8,128)(2,1)S(1)}, bf16[17,32,128]{2,1,0:T(8,128)(2,1)S(1)}, u32[]{:S(2)}, u32[]{:S(2)}) collective-permute-start(bf16[17,32,128]{2,1,0:T(8,128)(2,1)S(1)} %get-tuple-element.46), channel_id=1, source_target_pairs={{0,3},{1,2},{2,1},{3,0},{4,5},{5,4},{6,7},{7,6},{8,11},{9,10},{10,... | collective-permute-start | bytes 417800 | tf_op jit(solution)/shard_map/ppermute | solution.py:557
  32.1 2.3 %far_parts.1 = (bf16[4,128,128]{2,1,0:T(8,128)(2,1)S(1)}, bf16[4,128,128]{2,1,0:T(8,128)(2,1)S(1)}, bf16[4,128,128]{2,1,0:T(8,128)(2,1)S(1)}, bf16[4,128,128]{2,...) custom-call(bf16[4,128,128]{2,1,0:T(8,128)(2,1)S(1)} %get-tuple-element.38.refs_0_, ...), custom_call_target="tpu_custom_call" | custom-call | flops 1 | bytes 1 | tf_op jit(solution)/shard_map/far_parts/pallas_call | solution.py:507
  34.6 2.1 %collective-permute-start.16 = (bf16[17,32,128]{2,1,0:T(8,128)(2,1)S(1)}, bf16[17,32,128]{2,1,0:T(8,128)(2,1)S(1)}, u32[]{:S(2)}, u32[]{:S(2)}) collective-permute-start(bf16[17,32,128]{2,1,0:T(8,128)(2,1)S(1)} %get-tuple-element.57), channel_id=1, source_target_pairs={{0,1},{1,0},{2,3},{3,2},{4,6},{5,7},{6,4},{7,5},{8,9},{9,8},{10,11... | collective-permute-start | bytes 417800 | tf_op jit(solution)/shard_map/ppermute | solution.py:557
  36.7 0.1 collective-permute-done.10.refs_6_.refs_0_
  36.9 1.6 %collective-permute-start.13 = (bf16[4,128,128]{2,1,0:T(8,128)(2,1)S(1)}, bf16[4,128,128]{2,1,0:T(8,128)(2,1)S(1)}, u32[]{:S(2)}, u32[]{:S(2)}) collective-permute-start(bf16[4,128,128]{2,1,0:T(8,128)(2,1)S(1)} %get-tuple-element.54), channel_id=1, source_target_pairs={{0,24},{4,28},{8,16},{12,20},{16,8},{20,12},{24,0},{28,4},{1,25},{... | collective-permute-start | bytes 393224 | tf_op jit(solution)/shard_map/ppermute | solution.py:527
  38.5 0.5 collective-permute-start.14
  39.0 1.5 %collective-permute-start.15 = (bf16[4,128,128]{2,1,0:T(8,128)(2,1)S(1)}, bf16[4,128,128]{2,1,0:T(8,128)(2,1)S(1)}, u32[]{:S(2)}, u32[]{:S(2)}) collective-permute-start(bf16[4,128,128]{2,1,0:T(8,128)(2,1)S(1)} %get-tuple-element.56), channel_id=1, source_target_pairs={{0,8},{4,12},{8,0},{12,4},{16,24},{20,28},{24,16},{28,20},{1,9},{5... | collective-permute-start | bytes 393224 | tf_op jit(solution)/shard_map/ppermute | solution.py:527
  40.5 4.8 %collective-permute-done.11.refs_7_ = bf16[17,32,128]{2,1,0:T(8,128)(2,1)S(1)} collective-permute-done((bf16[17,32,128]{2,1,0:T(8,128)(2,1)S(1)}, bf16[17,32,128]{2,1,0:T(8,128)(2,1)S(1)}, u32[]{:S(2)}, u32[]{:S(2)}) %collective-permute-start.11) | collective-permute-done | bytes 139296 | tf_op jit(solution)/shard_map/ppermute | solution.py:557
  45.3 1.4 %near_early.1.refs_5_.early_ref = f32[4,12,128,128]{3,2,1,0:T(8,128)S(1)} custom-call(bf16[128,2048]{1,0:T(8,128)(2,1)S(1)} %copy-done, bf16[128,2048]{1,0:T(8,128)(2,1)S(1)} %copy-done.1, bf16[128,2048]{1,0:T(8,128)(2,1)S(1)} %copy-done.2, bf16[128,2048]{1,0:T(8,128)(2,1)S(1)} %copy-done.3, f32[32,128]{1,0:T(8,128)S(1)} %get-tuple-element.33.refs_0_.refs_4_, ...), custom_call_target="tpu_custom_call" | custom-call | flops 2000000000 | bytes 5709824 | tf_op jit(solution)/shard_map/near_early/pallas_call | solution.py:507
  46.8 1.9 %final_others.1 = (bf16[128,2048]{1,0:T(8,128)(2,1)}, bf16[128,2048]{1,0:T(8,128)(2,1)}, bf16[128,2048]{1,0:T(8,128)(2,1)}, bf16[128,2048]{1,0:T(8,128)(2,1)}) custom-call(bf16[128,2048]{1,0:T(8,128)(2,1)S(1)} %copy-done, bf16[128,2048]{1,0:T(8,128)(2,1)S(1)} %copy-done.1, bf16[128,2048]{1,0:T(8,128)(2,1)S(1)} %copy-done.2, bf16[128,2048]{1,0:T(8,128)(2,1)S(1)} %copy-done.3, ...), custom_call_target="tpu_custom_call" | custom-call | flops 1000000000 | bytes 7774208 | tf_op jit(solution)/shard_map/final_others/pallas_call | solution.py:507
  48.7 1.1 %final_own.1 = (bf16[128,2048]{1,0:T(8,128)(2,1)}, bf16[128,2048]{1,0:T(8,128)(2,1)}, bf16[128,2048]{1,0:T(8,128)(2,1)}, bf16[128,2048]{1,0:T(8,128)(2,1)}) custom-call(f32[4,12,128,128]{3,2,1,0:T(8,128)S(1)} %near_early.1.refs_5_.early_ref, ...), custom_call_target="tpu_custom_call", output_to_operand_aliasing={{0}: (6, {}), {1}: (7, {}), {2}: (8, {}), {3}: (9, {})} | custom-call | flops 16777216 | bytes 8003584 | tf_op jit(solution)/shard_map/final_own/pallas_call | solution.py:507
  (26 shorter events, 0.4 us)
Async XLA Ops:
  4.6 9.0 %collective-permute-start = (bf16[17,32,128]{2,1,0:T(8,128)(2,1)S(1)}, bf16[17,32,128]{2,1,0:T(8,128)(2,1)S(1)}, u32[]{:S(2)}, u32[]{:S(2)}) collective-permute-start(bf16[17,32,128]{2,1,0:T(8,128)(2,1)S(1)} %get-tuple-element.35), channel_id=1, source_target_pairs={{0,3},{1,2},{2,1},{3,0},{4,5},{5,4},{6,7},{7,6},{8,11},{9,10},{10,... | collective-permute-start | bytes 417800 | tf_op jit(solution)/shard_map/ppermute | solution.py:557
  9.7 5.4 %collective-permute-start.3 = (bf16[4,128,128]{2,1,0:T(8,128)(2,1)S(1)}, bf16[4,128,128]{2,1,0:T(8,128)(2,1)S(1)}, u32[]{:S(2)}, u32[]{:S(2)}) collective-permute-start(bf16[4,128,128]{2,1,0:T(8,128)(2,1)S(1)} %get-tuple-element.39), channel_id=1, source_target_pairs={{0,8},{4,12},{8,0},{12,4},{16,24},{20,28},{24,16},{28,20},{1,9},{5... | collective-permute-start | bytes 393224 | tf_op jit(solution)/shard_map/ppermute | solution.py:527
  11.2 5.1 %collective-permute-start.4 = (bf16[4,128,128]{2,1,0:T(8,128)(2,1)S(1)}, bf16[4,128,128]{2,1,0:T(8,128)(2,1)S(1)}, u32[]{:S(2)}, u32[]{:S(2)}) collective-permute-start(bf16[4,128,128]{2,1,0:T(8,128)(2,1)S(1)} %get-tuple-element.40), channel_id=1, source_target_pairs={{0,16},{4,20},{8,24},{12,28},{16,0},{20,4},{24,8},{28,12},{1,17},{... | collective-permute-start | bytes 393224 | tf_op jit(solution)/shard_map/ppermute | solution.py:527
  12.7 5.9 %collective-permute-start.5 = (bf16[4,128,128]{2,1,0:T(8,128)(2,1)S(1)}, bf16[4,128,128]{2,1,0:T(8,128)(2,1)S(1)}, u32[]{:S(2)}, u32[]{:S(2)}) collective-permute-start(bf16[4,128,128]{2,1,0:T(8,128)(2,1)S(1)} %get-tuple-element.41), channel_id=1, source_target_pairs={{0,24},{4,28},{8,16},{12,20},{16,8},{20,12},{24,0},{28,4},{1,25},{... | collective-permute-start | bytes 393224 | tf_op jit(solution)/shard_map/ppermute | solution.py:527
  13.2 8.8 %collective-permute-start.1 = (bf16[17,32,128]{2,1,0:T(8,128)(2,1)S(1)}, bf16[17,32,128]{2,1,0:T(8,128)(2,1)S(1)}, u32[]{:S(2)}, u32[]{:S(2)}) collective-permute-start(bf16[17,32,128]{2,1,0:T(8,128)(2,1)S(1)} %get-tuple-element.36), channel_id=1, source_target_pairs={{0,2},{1,3},{2,0},{3,1},{4,7},{5,6},{6,5},{7,4},{8,10},{9,11},{10,... | collective-permute-start | bytes 417800 | tf_op jit(solution)/shard_map/ppermute | solution.py:557
  13.6 8.4 %collective-permute-start.2 = (bf16[17,32,128]{2,1,0:T(8,128)(2,1)}, bf16[17,32,128]{2,1,0:T(8,128)(2,1)S(1)}, u32[]{:S(2)}, u32[]{:S(2)}) collective-permute-start(bf16[17,32,128]{2,1,0:T(8,128)(2,1)} %get-tuple-element.37), channel_id=1, source_target_pairs={{0,1},{1,0},{2,3},{3,2},{4,6},{5,7},{6,4},{7,5},{8,9},{9,8},{10,11... | collective-permute-start | bytes 417800 | tf_op jit(solution)/shard_map/ppermute | solution.py:557
  18.6 1.6 %collective-permute-start.6 = (bf16[4,2,128,128]{3,2,1,0:T(8,128)(2,1)S(1)}, bf16[4,2,128,128]{3,2,1,0:T(8,128)(2,1)S(1)}, u32[]{:S(2)}, u32[]{:S(2)}) collective-permute-start(bf16[4,2,128,128]{3,2,1,0:T(8,128)(2,1)S(1)} %pack.1), channel_id=1, source_target_pairs={{0,4},{4,0},{8,12},{12,8},{16,20},{20,16},{24,28},{28,24},{1,5},{5... | collective-permute-start | bytes 786440 | tf_op jit(solution)/shard_map/ppermute | solution.py:527
  22.5 4.6 %collective-permute-start.9 = (f32[16,128]{1,0:T(8,128)S(1)}, f32[16,128]{1,0:T(8,128)S(1)}, u32[]{:S(2)}, u32[]{:S(2)}) collective-permute-start(f32[16,128]{1,0:T(8,128)S(1)} %get-tuple-element.44.refs_6_.refs_8_.refs_5_), channel_id=1, source_target_pairs={{0,24},{4,28},{8,16},{12,20},{16,8},{20,12},{24,0},{28,4},{1,25},{... | collective-permute-start | bytes 24584 | tf_op jit(solution)/shard_map/ppermute | solution.py:527
  25.0 3.7 %collective-permute-start.8 = (f32[16,128]{1,0:T(8,128)S(1)}, f32[16,128]{1,0:T(8,128)S(1)}, u32[]{:S(2)}, u32[]{:S(2)}) collective-permute-start(f32[16,128]{1,0:T(8,128)S(1)} %get-tuple-element.44.refs_6_.refs_8_.refs_5_), channel_id=1, source_target_pairs={{0,16},{4,20},{8,24},{12,28},{16,0},{20,4},{24,8},{28,12},{1,17},{... | collective-permute-start | bytes 24584 | tf_op jit(solution)/shard_map/ppermute | solution.py:527
  25.5 3.7 %collective-permute-start.7 = (f32[16,128]{1,0:T(8,128)S(1)}, f32[16,128]{1,0:T(8,128)S(1)}, u32[]{:S(2)}, u32[]{:S(2)}) collective-permute-start(f32[16,128]{1,0:T(8,128)S(1)} %get-tuple-element.44.refs_6_.refs_8_.refs_5_), channel_id=1, source_target_pairs={{0,8},{4,12},{8,0},{12,4},{16,24},{20,28},{24,16},{28,20},{1,9},{5... | collective-permute-start | bytes 24584 | tf_op jit(solution)/shard_map/ppermute | solution.py:527
  29.8 7.0 %collective-permute-start.10 = (bf16[17,32,128]{2,1,0:T(8,128)(2,1)S(1)}, bf16[17,32,128]{2,1,0:T(8,128)(2,1)S(1)}, u32[]{:S(2)}, u32[]{:S(2)}) collective-permute-start(bf16[17,32,128]{2,1,0:T(8,128)(2,1)S(1)} %get-tuple-element.46), channel_id=1, source_target_pairs={{0,3},{1,2},{2,1},{3,0},{4,5},{5,4},{6,7},{7,6},{8,11},{9,10},{10,... | collective-permute-start | bytes 417800 | tf_op jit(solution)/shard_map/ppermute | solution.py:557
  34.4 2.4 %collective-permute-start.12 = (bf16[4,2,128,128]{3,2,1,0:T(8,128)(2,1)S(1)}, bf16[4,2,128,128]{3,2,1,0:T(8,128)(2,1)S(1)}, u32[]{:S(2)}, u32[]{:S(2)}) collective-permute-start(bf16[4,2,128,128]{3,2,1,0:T(8,128)(2,1)S(1)} %get-tuple-element.52), channel_id=1, source_target_pairs={{0,4},{4,0},{8,12},{12,8},{16,20},{20,16},{24,28},{28,24},{1,5},{5... | collective-permute-start | bytes 786440 | tf_op jit(solution)/shard_map/ppermute | solution.py:527
  34.5 10.8 %collective-permute-start.11 = (bf16[17,32,128]{2,1,0:T(8,128)(2,1)S(1)}, bf16[17,32,128]{2,1,0:T(8,128)(2,1)S(1)}, u32[]{:S(2)}, u32[]{:S(2)}) collective-permute-start(bf16[17,32,128]{2,1,0:T(8,128)(2,1)S(1)} %get-tuple-element.47), channel_id=1, source_target_pairs={{0,2},{1,3},{2,0},{3,1},{4,7},{5,6},{6,5},{7,4},{8,10},{9,11},{10,... | collective-permute-start | bytes 417800 | tf_op jit(solution)/shard_map/ppermute | solution.py:557
  34.6 12.2 %collective-permute-start.16 = (bf16[17,32,128]{2,1,0:T(8,128)(2,1)S(1)}, bf16[17,32,128]{2,1,0:T(8,128)(2,1)S(1)}, u32[]{:S(2)}, u32[]{:S(2)}) collective-permute-start(bf16[17,32,128]{2,1,0:T(8,128)(2,1)S(1)} %get-tuple-element.57), channel_id=1, source_target_pairs={{0,1},{1,0},{2,3},{3,2},{4,6},{5,7},{6,4},{7,5},{8,9},{9,8},{10,11... | collective-permute-start | bytes 417800 | tf_op jit(solution)/shard_map/ppermute | solution.py:557
  36.8 8.5 %copy-start = (bf16[128,2048]{1,0:T(8,128)(2,1)S(1)}, bf16[128,2048]{1,0:T(8,128)(2,1)}, u32[]{:S(2)}) copy-start(bf16[128,2048]{1,0:T(8,128)(2,1)} %refs_0_.5) | copy-start | bytes 1572868
  36.8 8.5 %copy-start.1 = (bf16[128,2048]{1,0:T(8,128)(2,1)S(1)}, bf16[128,2048]{1,0:T(8,128)(2,1)}, u32[]{:S(2)}) copy-start(bf16[128,2048]{1,0:T(8,128)(2,1)} %refs_1_.5) | copy-start | bytes 1572868
  36.8 8.5 %copy-start.2 = (bf16[128,2048]{1,0:T(8,128)(2,1)S(1)}, bf16[128,2048]{1,0:T(8,128)(2,1)}, u32[]{:S(2)}) copy-start(bf16[128,2048]{1,0:T(8,128)(2,1)} %refs_2_.5) | copy-start | bytes 1572868
  36.8 8.5 %copy-start.3 = (bf16[128,2048]{1,0:T(8,128)(2,1)S(1)}, bf16[128,2048]{1,0:T(8,128)(2,1)}, u32[]{:S(2)}) copy-start(bf16[128,2048]{1,0:T(8,128)(2,1)} %refs_3_.5) | copy-start | bytes 1572868
  36.9 11.8 %collective-permute-start.13 = (bf16[4,128,128]{2,1,0:T(8,128)(2,1)S(1)}, bf16[4,128,128]{2,1,0:T(8,128)(2,1)S(1)}, u32[]{:S(2)}, u32[]{:S(2)}) collective-permute-start(bf16[4,128,128]{2,1,0:T(8,128)(2,1)S(1)} %get-tuple-element.54), channel_id=1, source_target_pairs={{0,24},{4,28},{8,16},{12,20},{16,8},{20,12},{24,0},{28,4},{1,25},{... | collective-permute-start | bytes 393224 | tf_op jit(solution)/shard_map/ppermute | solution.py:527
  38.5 10.2 %collective-permute-start.14 = (bf16[4,128,128]{2,1,0:T(8,128)(2,1)S(1)}, bf16[4,128,128]{2,1,0:T(8,128)(2,1)S(1)}, u32[]{:S(2)}, u32[]{:S(2)}) collective-permute-start(bf16[4,128,128]{2,1,0:T(8,128)(2,1)S(1)} %get-tuple-element.55), channel_id=1, source_target_pairs={{0,16},{4,20},{8,24},{12,28},{16,0},{20,4},{24,8},{28,12},{1,17},{... | collective-permute-start | bytes 393224 | tf_op jit(solution)/shard_map/ppermute | solution.py:527
  39.0 9.7 %collective-permute-start.15 = (bf16[4,128,128]{2,1,0:T(8,128)(2,1)S(1)}, bf16[4,128,128]{2,1,0:T(8,128)(2,1)S(1)}, u32[]{:S(2)}, u32[]{:S(2)}) collective-permute-start(bf16[4,128,128]{2,1,0:T(8,128)(2,1)S(1)} %get-tuple-element.56), channel_id=1, source_target_pairs={{0,8},{4,12},{8,0},{12,4},{16,24},{20,28},{24,16},{28,20},{1,9},{5... | collective-permute-start | bytes 393224 | tf_op jit(solution)/shard_map/ppermute | solution.py:527

commit v14 on v13

--- a/solution.py
+++ b/solution.py
@@ -55,13 +55,35 @@
     return order[step - 1]
 
 
-def place_at(n_i, slots, step):
+def distance_back(n_i, step):
+    return n_i - 1 if step == 1 else step - 1
+
+
+def is_odd():
+    return lax.axis_index("seqo") % 2 == 1
+
+
+def place_in(n_i, slots, step):
     pos, _ = position(slots)
     if step == 0:
-        return pos * slots
-    odd = lax.axis_index("seqo") % 2 == 1
-    far = jnp.where(odd, distance(n_i, step, True), distance(n_i, step, False))
-    return (pos ^ far) * slots
+        return pos
+    return pos ^ jnp.where(is_odd(), distance(n_i, step, True), distance(n_i, step, False))
+
+
+def first_back(n_i, slots, step):
+    pos, _ = position(slots)
+    return (pos if step == 0 else pos ^ distance_back(n_i, step)) * slots
+
+
+def in_back_order(n_i, chunks):
+    found = [chunks[0]]
+    for step in range(1, n_i):
+        even, odd = [
+            [distance(n_i, k, parity) for k in range(1, n_i)].index(distance_back(n_i, step)) + 1
+            for parity in (False, True)
+        ]
+        found.append(jnp.where(is_odd(), chunks[odd], chunks[even]))
+    return found
 
 
 def lanes_of(rows):
@@ -174,7 +196,7 @@
     turn[...] = turn[...].T
     near = split(pick_rows(turn, rows))
     for d in range(n_i):
-        mids[d][: 4 * slots] = picked[place_at(n_i, slots, d) // slots]
+        mids[d][: 4 * slots] = picked[place_in(n_i, slots, d)]
         mids[d][4 * slots] = near
     for m in range(slots):
         fulls[m][...] = buffers[:, :, head_columns(pos * slots + (chip ^ m))]
@@ -273,10 +295,12 @@
     for slot, parts in enumerate(level_parts(operands, merged)):
         for which, part in enumerate(parts):
             part = part.astype(BF16)
-            for d in range(n_i):
-                outs[d][which * slots + slot] = part[d * quarter : (d + 1) * quarter]
-    for d in range(n_i):
-        outs[d][4 * slots] = split(columns_ref[d * quarter : (d + 1) * quarter])
+            chunks = [part[d * quarter : (d + 1) * quarter] for d in range(n_i)]
+            for out, chunk in zip(outs, in_back_order(n_i, chunks)):
+                out[which * slots + slot] = chunk
+    chunks = [columns_ref[d * quarter : (d + 1) * quarter] for d in range(n_i)]
+    for out, chunk in zip(outs, in_back_order(n_i, chunks)):
+        out[4 * slots] = split(chunk)
 
 
 def far_parts_kernel(slots, width, *refs):
@@ -333,7 +357,7 @@
     lane = lanes_of(quarter)
     mid = jnp.zeros((quarter, LANES), F32)
     for step, ref in zip(steps, mids):
-        place = place_at(n_i, slots, step)
+        place = first_back(n_i, slots, step)
         found = join(ref)
         e = pltpu.roll(found, place, 1)
         de = pltpu.roll(found, place + HEADS - slots, 1)
@@ -361,7 +385,7 @@
 
 
 def near_place(n_i, slots, step, sources, stats_ref):
-    heads = [place_at(n_i, slots, step) + slot for slot in range(slots)]
+    heads = [first_back(n_i, slots, step) + slot for slot in range(slots)]
     operands = [[ref[:, head_columns(head)] for ref in sources] for head in heads]
     stats = [(stats_ref[pl.ds(head, 1), :], stats_ref[pl.ds(HEADS + head, 1), :]) for head in heads]
     return level_parts(operands, stats)
@@ -467,7 +491,7 @@
     late = near_place(n_i, slots, last, sources, stats_ref)
     copies = []
     for step in range(1, n_i):
-        first = place_at(n_i, slots, step)
+        first = first_back(n_i, slots, step)
         found = [spread_rows(slots, first + slot, slot, mids[step - 1]) for slot in range(slots)]
         for slot, parts in enumerate(found):
             for which in range(4):
@@ -557,6 +581,11 @@
             found.append(lax.ppermute(pieces[step], ("seqo", "seqi"), pairs))
         return found
 
+    def swap_back(pieces):
+        return [pieces[0]] + [
+            swap(pieces[step], "seqi", n_i, distance_back(n_i, step)) for step in range(1, n_i)
+        ]
+
     def swap_fulls(pieces):
         return [pieces[0]] + [swap(pieces[m], "seqo", n_o, m * width) for m in range(1, slots)]
 
@@ -611,7 +640,7 @@
         unit * slots * 6,
         mids + [middle, columns] + xmsgs,
     )
-    midparts = swap_mids(midparts)
+    midparts = swap_back(midparts)
     farparts = call(
         bind(far_parts_kernel, slots, width),
         "far_parts",

time: 50 us -> 47.7 us (0.954)
  waiting for transfers between devices: 15 us -> 12.7 us
    ppermute x6 -> x3, waiting for transfers between devices: 6 us -> 1.05 us  [swap_mids(): found.append(lax.ppermute(pieces[step], ('seqo', 'seqi'), pairs))]
    ppermute x6 -> x3, starting transfers between devices: 10.3 us -> 5.76 us  [swap_mids(): found.append(lax.ppermute(pieces[step], ('seqo', 'seqi'), pairs))]
    ppermute x11 -> x14, starting transfers between devices: 10.7 us -> 15.2 us  [swap(): return lax.ppermute(x, axis, [(i, i ^ mask) for i in range(n)])]
    ppermute x11 -> x14, waiting for transfers between devices: 9 us -> 11.7 us  [swap(): return lax.ppermute(x, axis, [(i, i ^ mask) for i in range(n)])]
  transfers between devices with their start and end apart: 17 -> 17, of which waited for: 11 -> 12; matrix products, arithmetic and copies ran while one was open for 0% -> 0% of each run, Pallas kernels for 14% -> 14%
where the time goes in v14:
time: 47.7 us; the launch traced here: 47.6 us
  starting transfers between devices  21 us (44%)
  Pallas kernels  13.1 us (27%)
  waiting for transfers between devices  12.7 us (27%)
  between operations  0.8 us (2%)
    ppermute x14, starting transfers between devices, swap(): return lax.ppermute(x, axis, [(i, i ^ mask) for i in range(n)])  15.2 us
    pallas_call x16, Pallas kernels, call(): pl.pallas_call(kernel, out_shape=tuple(outs), in_specs=[pl.BlockSpec(memo...  13.1 us
    ppermute x14, waiting for transfers between devices, swap(): return lax.ppermute(x, axis, [(i, i ^ mask) for i in range(n)])  11.7 us
    ppermute x3, starting transfers between devices, swap_mids(): found.append(lax.ppermute(pieces[step], ('seqo', 'seqi'), pairs))  5.76 us
    ppermute x3, waiting for transfers between devices, swap_mids(): found.append(lax.ppermute(pieces[step], ('seqo', 'seqi'), pairs))  1.05 us
  transfers between devices with their start and end apart: 17, of which 12 were waited for; matrix products, arithmetic and copies ran while one was open for 0% of the time, Pallas kernels for 14%

profile of v14, /device:TPU:0, one launch (start us, length us, event | category | flops | bytes accessed | tf_op | source)
XLA Modules:
  0.0 47.6 jit_solution(12161786683440633733)
XLA Ops:
  0.6 3.9 %pick.1 = (bf16[17,32,128]{2,1,0:T(8,128)(2,1)S(1)}, bf16[17,32,128]{2,1,0:T(8,128)(2,1)S(1)}, bf16[17,32,128]{2,1,0:T(8,128)(2,1)S(1)}, bf16[17,32,128]{2,1,0:T...) custom-call(bf16[128,2048]{1,0:T(8,128)(2,1)} %refs_0_.5, ...), custom_call_target="tpu_custom_call" | custom-call | flops 134217728 | bytes 3194880 | tf_op jit(solution)/shard_map/pick/pallas_call | solution.py:531
  4.6 5.1 %collective-permute-start = (bf16[17,32,128]{2,1,0:T(8,128)(2,1)S(1)}, bf16[17,32,128]{2,1,0:T(8,128)(2,1)S(1)}, u32[]{:S(2)}, u32[]{:S(2)}) collective-permute-start(bf16[17,32,128]{2,1,0:T(8,128)(2,1)S(1)} %get-tuple-element.35), channel_id=1, source_target_pairs={{0,3},{1,2},{2,1},{3,0},{4,5},{5,4},{6,7},{7,6},{8,11},{9,10},{10,... | collective-permute-start | bytes 417800 | tf_op jit(solution)/shard_map/ppermute | solution.py:581
  9.7 1.5 %collective-permute-start.3 = (bf16[4,128,128]{2,1,0:T(8,128)(2,1)S(1)}, bf16[4,128,128]{2,1,0:T(8,128)(2,1)S(1)}, u32[]{:S(2)}, u32[]{:S(2)}) collective-permute-start(bf16[4,128,128]{2,1,0:T(8,128)(2,1)S(1)} %get-tuple-element.39), channel_id=1, source_target_pairs={{0,8},{4,12},{8,0},{12,4},{16,24},{20,28},{24,16},{28,20},{1,9},{5... | collective-permute-start | bytes 393224 | tf_op jit(solution)/shard_map/ppermute | solution.py:551
  11.2 1.5 %collective-permute-start.4 = (bf16[4,128,128]{2,1,0:T(8,128)(2,1)S(1)}, bf16[4,128,128]{2,1,0:T(8,128)(2,1)S(1)}, u32[]{:S(2)}, u32[]{:S(2)}) collective-permute-start(bf16[4,128,128]{2,1,0:T(8,128)(2,1)S(1)} %get-tuple-element.40), channel_id=1, source_target_pairs={{0,16},{4,20},{8,24},{12,28},{16,0},{20,4},{24,8},{28,12},{1,17},{... | collective-permute-start | bytes 393224 | tf_op jit(solution)/shard_map/ppermute | solution.py:551
  12.7 0.4 collective-permute-start.5
  13.2 0.4 collective-permute-done.refs_0_.refs_1_
  13.6 0.6 %collective-permute-start.2 = (bf16[17,32,128]{2,1,0:T(8,128)(2,1)}, bf16[17,32,128]{2,1,0:T(8,128)(2,1)S(1)}, u32[]{:S(2)}, u32[]{:S(2)}) collective-permute-start(bf16[17,32,128]{2,1,0:T(8,128)(2,1)} %get-tuple-element.37), channel_id=1, source_target_pairs={{0,1},{1,0},{2,3},{3,2},{4,6},{5,7},{6,4},{7,5},{8,9},{9,8},{10,11... | collective-permute-start | bytes 417800 | tf_op jit(solution)/shard_map/ppermute | solution.py:581
  14.2 0.8 %collective-permute-done.3.refs_1_ = bf16[4,128,128]{2,1,0:T(8,128)(2,1)S(1)} collective-permute-done((bf16[4,128,128]{2,1,0:T(8,128)(2,1)S(1)}, bf16[4,128,128]{2,1,0:T(8,128)(2,1)S(1)}, u32[]{:S(2)}, u32[]{:S(2)}) %collective-permute-start.3) | collective-permute-done | bytes 131104 | tf_op jit(solution)/shard_map/ppermute | solution.py:551
  15.1 1.2 %collective-permute-done.4.refs_2_ = bf16[4,128,128]{2,1,0:T(8,128)(2,1)S(1)} collective-permute-done((bf16[4,128,128]{2,1,0:T(8,128)(2,1)S(1)}, bf16[4,128,128]{2,1,0:T(8,128)(2,1)S(1)}, u32[]{:S(2)}, u32[]{:S(2)}) %collective-permute-start.4) | collective-permute-done | bytes 131104 | tf_op jit(solution)/shard_map/ppermute | solution.py:551
  16.3 2.3 %collective-permute-done.5.refs_3_ = bf16[4,128,128]{2,1,0:T(8,128)(2,1)S(1)} collective-permute-done((bf16[4,128,128]{2,1,0:T(8,128)(2,1)S(1)}, bf16[4,128,128]{2,1,0:T(8,128)(2,1)S(1)}, u32[]{:S(2)}, u32[]{:S(2)}) %collective-permute-start.5) | collective-permute-done | bytes 131104 | tf_op jit(solution)/shard_map/ppermute | solution.py:551
  18.7 1.5 %collective-permute-done.6.refs_4_ = bf16[4,2,128,128]{3,2,1,0:T(8,128)(2,1)S(1)} collective-permute-done((bf16[4,2,128,128]{3,2,1,0:T(8,128)(2,1)S(1)}, bf16[4,2,128,128]{3,2,1,0:T(8,128)(2,1)S(1)}, u32[]{:S(2)}, u32[]{:S(2)}) %collective-permute-start.6) | collective-permute-done | bytes 262176 | tf_op jit(solution)/shard_map/ppermute | solution.py:551
  20.2 1.1 %far_stats.1.refs_5_ = f32[8,128]{1,0:T(8,128)S(1)} custom-call(bf16[4,128,128]{2,1,0:T(8,128)(2,1)S(1)} %get-tuple-element.38.refs_0_, bf16[4,128,128]{2,1,0:T(8,128)(2,1)S(1)} %collective-permute-done.3.refs_1_, bf16[4,128,128]{2,1,0:T(8,128)(2,1)S(1)} %collective-permute-done.4.refs_2_, bf16[4,128,128]{2,1,0:T(8,128)(2,1)S(1)} %collective-permute-done.5.refs_3_, ...), custom_call_target="tpu_custom_call" | custom-call | flops 1 | bytes 794624 | tf_op jit(solution)/shard_map/far_stats/pallas_call | solution.py:531
  21.3 0.7 %collective-permute-done.1.refs_2_ = bf16[17,32,128]{2,1,0:T(8,128)(2,1)S(1)} collective-permute-done((bf16[17,32,128]{2,1,0:T(8,128)(2,1)S(1)}, bf16[17,32,128]{2,1,0:T(8,128)(2,1)S(1)}, u32[]{:S(2)}, u32[]{:S(2)}) %collective-permute-start.1) | collective-permute-done | bytes 139296 | tf_op jit(solution)/shard_map/ppermute | solution.py:581
  22.0 0.5 %middle_stats.1 = (f32[16,128]{1,0:T(8,128)S(1)}, f32[8,128]{1,0:T(8,128)S(1)}, f32[128,128]{1,0:T(8,128)S(1)}) custom-call(bf16[17,32,128]{2,1,0:T(8,128)(2,1)S(1)} %get-tuple-element.34.refs_0_, bf16[17,32,128]{2,1,0:T(8,128)(2,1)S(1)} %collective-permute-done.refs_0_.refs_1_, bf16[17,32,128]{2,1,0:T(8,128)(2,1)S(1)} %collective-permute-done.1.refs_2_, ...), custom_call_target="tpu_custom_call" | custom-call | flops 33554432 | bytes 655360 | tf_op jit(solution)/shard_map/middle_stats/pallas_call | solution.py:531
  22.5 2.5 %collective-permute-start.9 = (f32[16,128]{1,0:T(8,128)S(1)}, f32[16,128]{1,0:T(8,128)S(1)}, u32[]{:S(2)}, u32[]{:S(2)}) collective-permute-start(f32[16,128]{1,0:T(8,128)S(1)} %get-tuple-element.44.refs_6_.refs_8_.refs_5_), channel_id=1, source_target_pairs={{0,24},{4,28},{8,16},{12,20},{16,8},{20,12},{24,0},{28,4},{1,25},{... | collective-permute-start | bytes 24584 | tf_op jit(solution)/shard_map/ppermute | solution.py:551
  25.0 0.5 %collective-permute-start.8 = (f32[16,128]{1,0:T(8,128)S(1)}, f32[16,128]{1,0:T(8,128)S(1)}, u32[]{:S(2)}, u32[]{:S(2)}) collective-permute-start(f32[16,128]{1,0:T(8,128)S(1)} %get-tuple-element.44.refs_6_.refs_8_.refs_5_), channel_id=1, source_target_pairs={{0,16},{4,20},{8,24},{12,28},{16,0},{20,4},{24,8},{28,12},{1,17},{... | collective-permute-start | bytes 24584 | tf_op jit(solution)/shard_map/ppermute | solution.py:551
  25.5 0.5 %collective-permute-start.7 = (f32[16,128]{1,0:T(8,128)S(1)}, f32[16,128]{1,0:T(8,128)S(1)}, u32[]{:S(2)}, u32[]{:S(2)}) collective-permute-start(f32[16,128]{1,0:T(8,128)S(1)} %get-tuple-element.44.refs_6_.refs_8_.refs_5_), channel_id=1, source_target_pairs={{0,8},{4,12},{8,0},{12,4},{16,24},{20,28},{24,16},{28,20},{1,9},{5... | collective-permute-start | bytes 24584 | tf_op jit(solution)/shard_map/ppermute | solution.py:551
  26.0 1.1 %collective-permute-done.9.refs_9_.refs_11_.refs_8_ = f32[16,128]{1,0:T(8,128)S(1)} collective-permute-done((f32[16,128]{1,0:T(8,128)S(1)}, f32[16,128]{1,0:T(8,128)S(1)}, u32[]{:S(2)}, u32[]{:S(2)}) %collective-permute-start.9) | collective-permute-done | bytes 8224 | tf_op jit(solution)/shard_map/ppermute | solution.py:551
  27.1 1.6 %collective-permute-done.8.refs_8_.refs_10_.refs_7_ = f32[16,128]{1,0:T(8,128)S(1)} collective-permute-done((f32[16,128]{1,0:T(8,128)S(1)}, f32[16,128]{1,0:T(8,128)S(1)}, u32[]{:S(2)}, u32[]{:S(2)}) %collective-permute-start.8) | collective-permute-done | bytes 8224 | tf_op jit(solution)/shard_map/ppermute | solution.py:551
  28.7 0.5 %collective-permute-done.7.refs_7_.refs_9_.refs_6_ = f32[16,128]{1,0:T(8,128)S(1)} collective-permute-done((f32[16,128]{1,0:T(8,128)S(1)}, f32[16,128]{1,0:T(8,128)S(1)}, u32[]{:S(2)}, u32[]{:S(2)}) %collective-permute-start.7) | collective-permute-done | bytes 8224 | tf_op jit(solution)/shard_map/ppermute | solution.py:551
  29.2 0.6 %middle_parts.1 = (bf16[17,32,128]{2,1,0:T(8,128)(2,1)S(1)}, bf16[17,32,128]{2,1,0:T(8,128)(2,1)S(1)}, bf16[17,32,128]{2,1,0:T(8,128)(2,1)S(1)}, bf16[17,32,128]{2,1,0:T(8,128)(2,1)S(1)}) custom-call(bf16[17,32,128]{2,1,0:T(8,128)(2,1)S(1)} %get-tuple-element.34.refs_0_, bf16[17,32,128]{2,1,0:T(8,128)(2,1)S(1)} %collective-permute-done.refs_0_.refs_1_, ...), custom_call_target="tpu_custom_call" | custom-call | flops 100663296 | bytes 1216512 | tf_op jit(solution)/shard_map/middle_parts/pallas_call | solution.py:531
  29.8 2.3 %collective-permute-start.10 = (bf16[17,32,128]{2,1,0:T(8,128)(2,1)S(1)}, bf16[17,32,128]{2,1,0:T(8,128)(2,1)S(1)}, u32[]{:S(2)}, u32[]{:S(2)}) collective-permute-start(bf16[17,32,128]{2,1,0:T(8,128)(2,1)S(1)} %get-tuple-element.46), channel_id=1, source_target_pairs={{0,3},{1,2},{2,1},{3,0},{4,7},{5,6},{6,5},{7,4},{8,11},{9,10},{10,... | collective-permute-start | bytes 417800 | tf_op jit(solution)/shard_map/ppermute | solution.py:551
  32.1 2.3 %far_parts.1 = (bf16[4,128,128]{2,1,0:T(8,128)(2,1)S(1)}, bf16[4,128,128]{2,1,0:T(8,128)(2,1)S(1)}, bf16[4,128,128]{2,1,0:T(8,128)(2,1)S(1)}, bf16[4,128,128]{2,...) custom-call(bf16[4,128,128]{2,1,0:T(8,128)(2,1)S(1)} %get-tuple-element.38.refs_0_, ...), custom_call_target="tpu_custom_call" | custom-call | flops 1 | bytes 1 | tf_op jit(solution)/shard_map/far_parts/pallas_call | solution.py:531
  34.6 2.1 %collective-permute-start.16 = (bf16[17,32,128]{2,1,0:T(8,128)(2,1)S(1)}, bf16[17,32,128]{2,1,0:T(8,128)(2,1)S(1)}, u32[]{:S(2)}, u32[]{:S(2)}) collective-permute-start(bf16[17,32,128]{2,1,0:T(8,128)(2,1)S(1)} %get-tuple-element.57), channel_id=1, source_target_pairs={{0,2},{1,3},{2,0},{3,1},{4,6},{5,7},{6,4},{7,5},{8,10},{9,11},{10,... | collective-permute-start | bytes 417800 | tf_op jit(solution)/shard_map/ppermute | solution.py:551
  37.0 1.5 %collective-permute-start.13 = (bf16[4,128,128]{2,1,0:T(8,128)(2,1)S(1)}, bf16[4,128,128]{2,1,0:T(8,128)(2,1)S(1)}, u32[]{:S(2)}, u32[]{:S(2)}) collective-permute-start(bf16[4,128,128]{2,1,0:T(8,128)(2,1)S(1)} %get-tuple-element.54), channel_id=1, source_target_pairs={{0,24},{4,28},{8,16},{12,20},{16,8},{20,12},{24,0},{28,4},{1,25},{... | collective-permute-start | bytes 393224 | tf_op jit(solution)/shard_map/ppermute | solution.py:551
  38.5 0.5 %collective-permute-start.14 = (bf16[4,128,128]{2,1,0:T(8,128)(2,1)S(1)}, bf16[4,128,128]{2,1,0:T(8,128)(2,1)S(1)}, u32[]{:S(2)}, u32[]{:S(2)}) collective-permute-start(bf16[4,128,128]{2,1,0:T(8,128)(2,1)S(1)} %get-tuple-element.55), channel_id=1, source_target_pairs={{0,16},{4,20},{8,24},{12,28},{16,0},{20,4},{24,8},{28,12},{1,17},{... | collective-permute-start | bytes 393224 | tf_op jit(solution)/shard_map/ppermute | solution.py:551
  39.0 1.5 %collective-permute-start.15 = (bf16[4,128,128]{2,1,0:T(8,128)(2,1)S(1)}, bf16[4,128,128]{2,1,0:T(8,128)(2,1)S(1)}, u32[]{:S(2)}, u32[]{:S(2)}) collective-permute-start(bf16[4,128,128]{2,1,0:T(8,128)(2,1)S(1)} %get-tuple-element.56), channel_id=1, source_target_pairs={{0,8},{4,12},{8,0},{12,4},{16,24},{20,28},{24,16},{28,20},{1,9},{5... | collective-permute-start | bytes 393224 | tf_op jit(solution)/shard_map/ppermute | solution.py:551
  40.5 2.0 %collective-permute-done.11.refs_7_ = bf16[17,32,128]{2,1,0:T(8,128)(2,1)S(1)} collective-permute-done((bf16[17,32,128]{2,1,0:T(8,128)(2,1)S(1)}, bf16[17,32,128]{2,1,0:T(8,128)(2,1)S(1)}, u32[]{:S(2)}, u32[]{:S(2)}) %collective-permute-start.11) | collective-permute-done | bytes 139296 | tf_op jit(solution)/shard_map/ppermute | solution.py:551
  42.6 1.4 %near_early.1.refs_5_.early_ref = f32[4,12,128,128]{3,2,1,0:T(8,128)S(1)} custom-call(bf16[128,2048]{1,0:T(8,128)(2,1)S(1)} %copy-done, bf16[128,2048]{1,0:T(8,128)(2,1)S(1)} %copy-done.1, bf16[128,2048]{1,0:T(8,128)(2,1)S(1)} %copy-done.2, bf16[128,2048]{1,0:T(8,128)(2,1)S(1)} %copy-done.3, f32[32,128]{1,0:T(8,128)S(1)} %get-tuple-element.33.refs_0_.refs_4_, ...), custom_call_target="tpu_custom_call" | custom-call | flops 2000000000 | bytes 5709824 | tf_op jit(solution)/shard_map/near_early/pallas_call | solution.py:531
  44.0 0.5 %collective-permute-done.16.refs_8_ = bf16[17,32,128]{2,1,0:T(8,128)(2,1)S(1)} collective-permute-done((bf16[17,32,128]{2,1,0:T(8,128)(2,1)S(1)}, bf16[17,32,128]{2,1,0:T(8,128)(2,1)S(1)}, u32[]{:S(2)}, u32[]{:S(2)}) %collective-permute-start.16) | collective-permute-done | bytes 139296 | tf_op jit(solution)/shard_map/ppermute | solution.py:551
  44.5 1.9 %final_others.1 = (bf16[128,2048]{1,0:T(8,128)(2,1)}, bf16[128,2048]{1,0:T(8,128)(2,1)}, bf16[128,2048]{1,0:T(8,128)(2,1)}, bf16[128,2048]{1,0:T(8,128)(2,1)}) custom-call(bf16[128,2048]{1,0:T(8,128)(2,1)S(1)} %copy-done, bf16[128,2048]{1,0:T(8,128)(2,1)S(1)} %copy-done.1, bf16[128,2048]{1,0:T(8,128)(2,1)S(1)} %copy-done.2, bf16[128,2048]{1,0:T(8,128)(2,1)S(1)} %copy-done.3, ...), custom_call_target="tpu_custom_call" | custom-call | flops 1000000000 | bytes 7774208 | tf_op jit(solution)/shard_map/final_others/pallas_call | solution.py:531
  46.5 1.1 %final_own.1 = (bf16[128,2048]{1,0:T(8,128)(2,1)}, bf16[128,2048]{1,0:T(8,128)(2,1)}, bf16[128,2048]{1,0:T(8,128)(2,1)}, bf16[128,2048]{1,0:T(8,128)(2,1)}) custom-call(f32[4,12,128,128]{3,2,1,0:T(8,128)S(1)} %near_early.1.refs_5_.early_ref, ...), custom_call_target="tpu_custom_call", output_to_operand_aliasing={{0}: (6, {}), {1}: (7, {}), {2}: (8, {}), {3}: (9, {})} | custom-call | flops 16777216 | bytes 8003584 | tf_op jit(solution)/shard_map/final_own/pallas_call | solution.py:531
  (26 shorter events, 0.5 us)
Async XLA Ops:
  4.6 9.0 %collective-permute-start = (bf16[17,32,128]{2,1,0:T(8,128)(2,1)S(1)}, bf16[17,32,128]{2,1,0:T(8,128)(2,1)S(1)}, u32[]{:S(2)}, u32[]{:S(2)}) collective-permute-start(bf16[17,32,128]{2,1,0:T(8,128)(2,1)S(1)} %get-tuple-element.35), channel_id=1, source_target_pairs={{0,3},{1,2},{2,1},{3,0},{4,5},{5,4},{6,7},{7,6},{8,11},{9,10},{10,... | collective-permute-start | bytes 417800 | tf_op jit(solution)/shard_map/ppermute | solution.py:581
  9.7 5.4 %collective-permute-start.3 = (bf16[4,128,128]{2,1,0:T(8,128)(2,1)S(1)}, bf16[4,128,128]{2,1,0:T(8,128)(2,1)S(1)}, u32[]{:S(2)}, u32[]{:S(2)}) collective-permute-start(bf16[4,128,128]{2,1,0:T(8,128)(2,1)S(1)} %get-tuple-element.39), channel_id=1, source_target_pairs={{0,8},{4,12},{8,0},{12,4},{16,24},{20,28},{24,16},{28,20},{1,9},{5... | collective-permute-start | bytes 393224 | tf_op jit(solution)/shard_map/ppermute | solution.py:551
  11.2 5.1 %collective-permute-start.4 = (bf16[4,128,128]{2,1,0:T(8,128)(2,1)S(1)}, bf16[4,128,128]{2,1,0:T(8,128)(2,1)S(1)}, u32[]{:S(2)}, u32[]{:S(2)}) collective-permute-start(bf16[4,128,128]{2,1,0:T(8,128)(2,1)S(1)} %get-tuple-element.40), channel_id=1, source_target_pairs={{0,16},{4,20},{8,24},{12,28},{16,0},{20,4},{24,8},{28,12},{1,17},{... | collective-permute-start | bytes 393224 | tf_op jit(solution)/shard_map/ppermute | solution.py:551
  12.7 5.9 %collective-permute-start.5 = (bf16[4,128,128]{2,1,0:T(8,128)(2,1)S(1)}, bf16[4,128,128]{2,1,0:T(8,128)(2,1)S(1)}, u32[]{:S(2)}, u32[]{:S(2)}) collective-permute-start(bf16[4,128,128]{2,1,0:T(8,128)(2,1)S(1)} %get-tuple-element.41), channel_id=1, source_target_pairs={{0,24},{4,28},{8,16},{12,20},{16,8},{20,12},{24,0},{28,4},{1,25},{... | collective-permute-start | bytes 393224 | tf_op jit(solution)/shard_map/ppermute | solution.py:551
  13.2 8.8 %collective-permute-start.1 = (bf16[17,32,128]{2,1,0:T(8,128)(2,1)S(1)}, bf16[17,32,128]{2,1,0:T(8,128)(2,1)S(1)}, u32[]{:S(2)}, u32[]{:S(2)}) collective-permute-start(bf16[17,32,128]{2,1,0:T(8,128)(2,1)S(1)} %get-tuple-element.36), channel_id=1, source_target_pairs={{0,2},{1,3},{2,0},{3,1},{4,7},{5,6},{6,5},{7,4},{8,10},{9,11},{10,... | collective-permute-start | bytes 417800 | tf_op jit(solution)/shard_map/ppermute | solution.py:581
  13.6 8.4 %collective-permute-start.2 = (bf16[17,32,128]{2,1,0:T(8,128)(2,1)}, bf16[17,32,128]{2,1,0:T(8,128)(2,1)S(1)}, u32[]{:S(2)}, u32[]{:S(2)}) collective-permute-start(bf16[17,32,128]{2,1,0:T(8,128)(2,1)} %get-tuple-element.37), channel_id=1, source_target_pairs={{0,1},{1,0},{2,3},{3,2},{4,6},{5,7},{6,4},{7,5},{8,9},{9,8},{10,11... | collective-permute-start | bytes 417800 | tf_op jit(solution)/shard_map/ppermute | solution.py:581
  18.6 1.6 %collective-permute-start.6 = (bf16[4,2,128,128]{3,2,1,0:T(8,128)(2,1)S(1)}, bf16[4,2,128,128]{3,2,1,0:T(8,128)(2,1)S(1)}, u32[]{:S(2)}, u32[]{:S(2)}) collective-permute-start(bf16[4,2,128,128]{3,2,1,0:T(8,128)(2,1)S(1)} %pack.1), channel_id=1, source_target_pairs={{0,4},{4,0},{8,12},{12,8},{16,20},{20,16},{24,28},{28,24},{1,5},{5... | collective-permute-start | bytes 786440 | tf_op jit(solution)/shard_map/ppermute | solution.py:551
  22.5 4.6 %collective-permute-start.9 = (f32[16,128]{1,0:T(8,128)S(1)}, f32[16,128]{1,0:T(8,128)S(1)}, u32[]{:S(2)}, u32[]{:S(2)}) collective-permute-start(f32[16,128]{1,0:T(8,128)S(1)} %get-tuple-element.44.refs_6_.refs_8_.refs_5_), channel_id=1, source_target_pairs={{0,24},{4,28},{8,16},{12,20},{16,8},{20,12},{24,0},{28,4},{1,25},{... | collective-permute-start | bytes 24584 | tf_op jit(solution)/shard_map/ppermute | solution.py:551
  25.0 3.7 %collective-permute-start.8 = (f32[16,128]{1,0:T(8,128)S(1)}, f32[16,128]{1,0:T(8,128)S(1)}, u32[]{:S(2)}, u32[]{:S(2)}) collective-permute-start(f32[16,128]{1,0:T(8,128)S(1)} %get-tuple-element.44.refs_6_.refs_8_.refs_5_), channel_id=1, source_target_pairs={{0,16},{4,20},{8,24},{12,28},{16,0},{20,4},{24,8},{28,12},{1,17},{... | collective-permute-start | bytes 24584 | tf_op jit(solution)/shard_map/ppermute | solution.py:551
  25.5 3.7 %collective-permute-start.7 = (f32[16,128]{1,0:T(8,128)S(1)}, f32[16,128]{1,0:T(8,128)S(1)}, u32[]{:S(2)}, u32[]{:S(2)}) collective-permute-start(f32[16,128]{1,0:T(8,128)S(1)} %get-tuple-element.44.refs_6_.refs_8_.refs_5_), channel_id=1, source_target_pairs={{0,8},{4,12},{8,0},{12,4},{16,24},{20,28},{24,16},{28,20},{1,9},{5... | collective-permute-start | bytes 24584 | tf_op jit(solution)/shard_map/ppermute | solution.py:551
  29.8 7.0 %collective-permute-start.10 = (bf16[17,32,128]{2,1,0:T(8,128)(2,1)S(1)}, bf16[17,32,128]{2,1,0:T(8,128)(2,1)S(1)}, u32[]{:S(2)}, u32[]{:S(2)}) collective-permute-start(bf16[17,32,128]{2,1,0:T(8,128)(2,1)S(1)} %get-tuple-element.46), channel_id=1, source_target_pairs={{0,3},{1,2},{2,1},{3,0},{4,7},{5,6},{6,5},{7,4},{8,11},{9,10},{10,... | collective-permute-start | bytes 417800 | tf_op jit(solution)/shard_map/ppermute | solution.py:551
  34.4 2.4 %collective-permute-start.12 = (bf16[4,2,128,128]{3,2,1,0:T(8,128)(2,1)S(1)}, bf16[4,2,128,128]{3,2,1,0:T(8,128)(2,1)S(1)}, u32[]{:S(2)}, u32[]{:S(2)}) collective-permute-start(bf16[4,2,128,128]{3,2,1,0:T(8,128)(2,1)S(1)} %get-tuple-element.52), channel_id=1, source_target_pairs={{0,4},{4,0},{8,12},{12,8},{16,20},{20,16},{24,28},{28,24},{1,5},{5... | collective-permute-start | bytes 786440 | tf_op jit(solution)/shard_map/ppermute | solution.py:551
  34.5 8.1 %collective-permute-start.11 = (bf16[17,32,128]{2,1,0:T(8,128)(2,1)S(1)}, bf16[17,32,128]{2,1,0:T(8,128)(2,1)S(1)}, u32[]{:S(2)}, u32[]{:S(2)}) collective-permute-start(bf16[17,32,128]{2,1,0:T(8,128)(2,1)S(1)} %get-tuple-element.47), channel_id=1, source_target_pairs={{0,1},{1,0},{2,3},{3,2},{4,5},{5,4},{6,7},{7,6},{8,9},{9,8},{10,11... | collective-permute-start | bytes 417800 | tf_op jit(solution)/shard_map/ppermute | solution.py:551
  34.6 9.9 %collective-permute-start.16 = (bf16[17,32,128]{2,1,0:T(8,128)(2,1)S(1)}, bf16[17,32,128]{2,1,0:T(8,128)(2,1)S(1)}, u32[]{:S(2)}, u32[]{:S(2)}) collective-permute-start(bf16[17,32,128]{2,1,0:T(8,128)(2,1)S(1)} %get-tuple-element.57), channel_id=1, source_target_pairs={{0,2},{1,3},{2,0},{3,1},{4,6},{5,7},{6,4},{7,5},{8,10},{9,11},{10,... | collective-permute-start | bytes 417800 | tf_op jit(solution)/shard_map/ppermute | solution.py:551
  36.8 5.7 %copy-start = (bf16[128,2048]{1,0:T(8,128)(2,1)S(1)}, bf16[128,2048]{1,0:T(8,128)(2,1)}, u32[]{:S(2)}) copy-start(bf16[128,2048]{1,0:T(8,128)(2,1)} %refs_0_.5) | copy-start | bytes 1572868
  36.8 5.7 %copy-start.1 = (bf16[128,2048]{1,0:T(8,128)(2,1)S(1)}, bf16[128,2048]{1,0:T(8,128)(2,1)}, u32[]{:S(2)}) copy-start(bf16[128,2048]{1,0:T(8,128)(2,1)} %refs_1_.5) | copy-start | bytes 1572868
  36.8 5.7 %copy-start.2 = (bf16[128,2048]{1,0:T(8,128)(2,1)S(1)}, bf16[128,2048]{1,0:T(8,128)(2,1)}, u32[]{:S(2)}) copy-start(bf16[128,2048]{1,0:T(8,128)(2,1)} %refs_2_.5) | copy-start | bytes 1572868
  36.9 5.7 %copy-start.3 = (bf16[128,2048]{1,0:T(8,128)(2,1)S(1)}, bf16[128,2048]{1,0:T(8,128)(2,1)}, u32[]{:S(2)}) copy-start(bf16[128,2048]{1,0:T(8,128)(2,1)} %refs_3_.5) | copy-start | bytes 1572868
  37.0 9.5 %collective-permute-start.13 = (bf16[4,128,128]{2,1,0:T(8,128)(2,1)S(1)}, bf16[4,128,128]{2,1,0:T(8,128)(2,1)S(1)}, u32[]{:S(2)}, u32[]{:S(2)}) collective-permute-start(bf16[4,128,128]{2,1,0:T(8,128)(2,1)S(1)} %get-tuple-element.54), channel_id=1, source_target_pairs={{0,24},{4,28},{8,16},{12,20},{16,8},{20,12},{24,0},{28,4},{1,25},{... | collective-permute-start | bytes 393224 | tf_op jit(solution)/shard_map/ppermute | solution.py:551
  38.5 8.0 %collective-permute-start.14 = (bf16[4,128,128]{2,1,0:T(8,128)(2,1)S(1)}, bf16[4,128,128]{2,1,0:T(8,128)(2,1)S(1)}, u32[]{:S(2)}, u32[]{:S(2)}) collective-permute-start(bf16[4,128,128]{2,1,0:T(8,128)(2,1)S(1)} %get-tuple-element.55), channel_id=1, source_target_pairs={{0,16},{4,20},{8,24},{12,28},{16,0},{20,4},{24,8},{28,12},{1,17},{... | collective-permute-start | bytes 393224 | tf_op jit(solution)/shard_map/ppermute | solution.py:551
  39.0 7.5 %collective-permute-start.15 = (bf16[4,128,128]{2,1,0:T(8,128)(2,1)S(1)}, bf16[4,128,128]{2,1,0:T(8,128)(2,1)S(1)}, u32[]{:S(2)}, u32[]{:S(2)}) collective-permute-start(bf16[4,128,128]{2,1,0:T(8,128)(2,1)S(1)} %get-tuple-element.56), channel_id=1, source_target_pairs={{0,8},{4,12},{8,0},{12,4},{16,24},{20,28},{24,16},{28,20},{1,9},{5... | collective-permute-start | bytes 393224 | tf_op jit(solution)/shard_map/ppermute | solution.py:551

commit v15 on v14

--- a/solution.py
+++ b/solution.py
@@ -609,7 +609,7 @@
     fulls = swap_fulls(pieces[n_i : n_i + slots])
     near = pieces[-1]
 
-    (settled,) = call(settle_kernel, "far_in", [stats(8)], [], SHORT, [mids[1]])
+    (settled,) = call(settle_kernel, "far_in", [stats(8)], [], SHORT, mids[1:3])
     (settled,) = call(settle_kernel, "chips_back", [stats(8)], [], LONG, [settled])
     (packed,) = call(bind(pack_kernel, slots), "pack", [half], [], 1, fulls + [settled])
     sibs = [swap(packed, "seqo", n_o, part) for part in range(1, width)]

time: 47.7 us -> 51.3 us (1.075)
  starting transfers between devices: 21 us -> 26.3 us
  waiting for transfers between devices: 12.7 us -> 10.9 us
    ppermute x3, starting transfers between devices: 5.76 us -> 11.1 us  [swap_mids(): found.append(lax.ppermute(pieces[step], ('seqo', 'seqi'), pairs))]
    ppermute x14, waiting for transfers between devices: 11.7 us -> 7.36 us  [swap(): return lax.ppermute(x, axis, [(i, i ^ mask) for i in range(n)])]
    ppermute x3, waiting for transfers between devices: 1.05 us -> 3.53 us  [swap_mids(): found.append(lax.ppermute(pieces[step], ('seqo', 'seqi'), pairs))]
  transfers between devices with their start and end apart: 17 -> 17, of which waited for: 12 -> 9; matrix products, arithmetic and copies ran while one was open for 0% -> 0% of each run, Pallas kernels for 14% -> 13%
where the time goes in v15:
time: 51.3 us; the launch traced here: 51.1 us
  starting transfers between devices  26.3 us (51%)
  Pallas kernels  13.1 us (26%)
  waiting for transfers between devices  10.9 us (21%)
  between operations  0.82 us (2%)
    ppermute x14, starting transfers between devices, swap(): return lax.ppermute(x, axis, [(i, i ^ mask) for i in range(n)])  15.2 us
    pallas_call x16, Pallas kernels, call(): pl.pallas_call(kernel, out_shape=tuple(outs), in_specs=[pl.BlockSpec(memo...  13.1 us
    ppermute x3, starting transfers between devices, swap_mids(): found.append(lax.ppermute(pieces[step], ('seqo', 'seqi'), pairs))  11.1 us
    ppermute x14, waiting for transfers between devices, swap(): return lax.ppermute(x, axis, [(i, i ^ mask) for i in range(n)])  7.36 us
    ppermute x3, waiting for transfers between devices, swap_mids(): found.append(lax.ppermute(pieces[step], ('seqo', 'seqi'), pairs))  3.53 us
  transfers between devices with their start and end apart: 17, of which 9 were waited for; matrix products, arithmetic and copies ran while one was open for 0% of the time, Pallas kernels for 13%

profile of v15, /device:TPU:0, one launch (start us, length us, event | category | flops | bytes accessed | tf_op | source)
XLA Modules:
  0.0 51.1 jit_solution(2305534485375481201)
XLA Ops:
  0.6 3.9 %pick.1 = (bf16[17,32,128]{2,1,0:T(8,128)(2,1)S(1)}, bf16[17,32,128]{2,1,0:T(8,128)(2,1)S(1)}, bf16[17,32,128]{2,1,0:T(8,128)(2,1)S(1)}, bf16[17,32,128]{2,1,0:T...) custom-call(bf16[128,2048]{1,0:T(8,128)(2,1)} %refs_0_.5, ...), custom_call_target="tpu_custom_call" | custom-call | flops 134217728 | bytes 3194880 | tf_op jit(solution)/shard_map/pick/pallas_call | solution.py:531
  4.6 5.1 %collective-permute-start = (bf16[17,32,128]{2,1,0:T(8,128)(2,1)S(1)}, bf16[17,32,128]{2,1,0:T(8,128)(2,1)S(1)}, u32[]{:S(2)}, u32[]{:S(2)}) collective-permute-start(bf16[17,32,128]{2,1,0:T(8,128)(2,1)S(1)} %get-tuple-element.35), channel_id=1, source_target_pairs={{0,3},{1,2},{2,1},{3,0},{4,5},{5,4},{6,7},{7,6},{8,11},{9,10},{10,... | collective-permute-start | bytes 417800 | tf_op jit(solution)/shard_map/ppermute | solution.py:581
  9.7 1.5 %collective-permute-start.3 = (bf16[4,128,128]{2,1,0:T(8,128)(2,1)S(1)}, bf16[4,128,128]{2,1,0:T(8,128)(2,1)S(1)}, u32[]{:S(2)}, u32[]{:S(2)}) collective-permute-start(bf16[4,128,128]{2,1,0:T(8,128)(2,1)S(1)} %get-tuple-element.39), channel_id=1, source_target_pairs={{0,8},{4,12},{8,0},{12,4},{16,24},{20,28},{24,16},{28,20},{1,9},{5... | collective-permute-start | bytes 393224 | tf_op jit(solution)/shard_map/ppermute | solution.py:551
  11.2 1.5 %collective-permute-start.4 = (bf16[4,128,128]{2,1,0:T(8,128)(2,1)S(1)}, bf16[4,128,128]{2,1,0:T(8,128)(2,1)S(1)}, u32[]{:S(2)}, u32[]{:S(2)}) collective-permute-start(bf16[4,128,128]{2,1,0:T(8,128)(2,1)S(1)} %get-tuple-element.40), channel_id=1, source_target_pairs={{0,16},{4,20},{8,24},{12,28},{16,0},{20,4},{24,8},{28,12},{1,17},{... | collective-permute-start | bytes 393224 | tf_op jit(solution)/shard_map/ppermute | solution.py:551
  12.7 0.4 collective-permute-start.5
  13.2 1.0 %collective-permute-done.refs_0_.refs_1_ = bf16[17,32,128]{2,1,0:T(8,128)(2,1)S(1)} collective-permute-done((bf16[17,32,128]{2,1,0:T(8,128)(2,1)S(1)}, bf16[17,32,128]{2,1,0:T(8,128)(2,1)S(1)}, u32[]{:S(2)}, u32[]{:S(2)}) %collective-permute-start) | collective-permute-done | bytes 139296 | tf_op jit(solution)/shard_map/ppermute | solution.py:581
  14.2 6.0 %collective-permute-start.2 = (bf16[17,32,128]{2,1,0:T(8,128)(2,1)}, bf16[17,32,128]{2,1,0:T(8,128)(2,1)S(1)}, u32[]{:S(2)}, u32[]{:S(2)}) collective-permute-start(bf16[17,32,128]{2,1,0:T(8,128)(2,1)} %get-tuple-element.37), channel_id=1, source_target_pairs={{0,1},{1,0},{2,3},{3,2},{4,6},{5,7},{6,4},{7,5},{8,9},{9,8},{10,11... | collective-permute-start | bytes 417800 | tf_op jit(solution)/shard_map/ppermute | solution.py:581
  20.2 2.5 %collective-permute-done.1.refs_1_.refs_2_ = bf16[17,32,128]{2,1,0:T(8,128)(2,1)S(1)} collective-permute-done((bf16[17,32,128]{2,1,0:T(8,128)(2,1)S(1)}, bf16[17,32,128]{2,1,0:T(8,128)(2,1)S(1)}, u32[]{:S(2)}, u32[]{:S(2)}) %collective-permute-start.1) | collective-permute-done | bytes 139296 | tf_op jit(solution)/shard_map/ppermute | solution.py:581
  22.7 0.1 collective-permute-start.6
  22.8 1.5 %collective-permute-done.6.refs_4_ = bf16[4,2,128,128]{3,2,1,0:T(8,128)(2,1)S(1)} collective-permute-done((bf16[4,2,128,128]{3,2,1,0:T(8,128)(2,1)S(1)}, bf16[4,2,128,128]{3,2,1,0:T(8,128)(2,1)S(1)}, u32[]{:S(2)}, u32[]{:S(2)}) %collective-permute-start.6) | collective-permute-done | bytes 262176 | tf_op jit(solution)/shard_map/ppermute | solution.py:551
  24.3 1.1 %far_stats.1.refs_5_ = f32[8,128]{1,0:T(8,128)S(1)} custom-call(bf16[4,128,128]{2,1,0:T(8,128)(2,1)S(1)} %get-tuple-element.38.refs_0_, bf16[4,128,128]{2,1,0:T(8,128)(2,1)S(1)} %collective-permute-done.3.refs_1_, bf16[4,128,128]{2,1,0:T(8,128)(2,1)S(1)} %collective-permute-done.4.refs_2_, bf16[4,128,128]{2,1,0:T(8,128)(2,1)S(1)} %collective-permute-done.5.refs_3_, ...), custom_call_target="tpu_custom_call" | custom-call | flops 1 | bytes 794624 | tf_op jit(solution)/shard_map/far_stats/pallas_call | solution.py:531
  25.4 0.5 %middle_stats.1 = (f32[16,128]{1,0:T(8,128)S(1)}, f32[8,128]{1,0:T(8,128)S(1)}, f32[128,128]{1,0:T(8,128)S(1)}) custom-call(bf16[17,32,128]{2,1,0:T(8,128)(2,1)S(1)} %get-tuple-element.34.refs_0_, bf16[17,32,128]{2,1,0:T(8,128)(2,1)S(1)} %collective-permute-done.refs_0_.refs_1_, bf16[17,32,128]{2,1,0:T(8,128)(2,1)S(1)} %collective-permute-done.1.refs_1_.refs_2_, ...), custom_call_target="tpu_custom_call" | custom-call | flops 33554432 | bytes 655360 | tf_op jit(solution)/shard_map/middle_stats/pallas_call | solution.py:531
  26.0 2.5 %collective-permute-start.9 = (f32[16,128]{1,0:T(8,128)S(1)}, f32[16,128]{1,0:T(8,128)S(1)}, u32[]{:S(2)}, u32[]{:S(2)}) collective-permute-start(f32[16,128]{1,0:T(8,128)S(1)} %get-tuple-element.44.refs_6_.refs_8_.refs_5_), channel_id=1, source_target_pairs={{0,24},{4,28},{8,16},{12,20},{16,8},{20,12},{24,0},{28,4},{1,25},{... | collective-permute-start | bytes 24584 | tf_op jit(solution)/shard_map/ppermute | solution.py:551
  28.5 0.5 collective-permute-start.8
  29.0 0.5 %collective-permute-start.7 = (f32[16,128]{1,0:T(8,128)S(1)}, f32[16,128]{1,0:T(8,128)S(1)}, u32[]{:S(2)}, u32[]{:S(2)}) collective-permute-start(f32[16,128]{1,0:T(8,128)S(1)} %get-tuple-element.44.refs_6_.refs_8_.refs_5_), channel_id=1, source_target_pairs={{0,8},{4,12},{8,0},{12,4},{16,24},{20,28},{24,16},{28,20},{1,9},{5... | collective-permute-start | bytes 24584 | tf_op jit(solution)/shard_map/ppermute | solution.py:551
  29.5 1.1 %collective-permute-done.9.refs_9_.refs_11_.refs_8_ = f32[16,128]{1,0:T(8,128)S(1)} collective-permute-done((f32[16,128]{1,0:T(8,128)S(1)}, f32[16,128]{1,0:T(8,128)S(1)}, u32[]{:S(2)}, u32[]{:S(2)}) %collective-permute-start.9) | collective-permute-done | bytes 8224 | tf_op jit(solution)/shard_map/ppermute | solution.py:551
  30.6 1.6 %collective-permute-done.8.refs_8_.refs_10_.refs_7_ = f32[16,128]{1,0:T(8,128)S(1)} collective-permute-done((f32[16,128]{1,0:T(8,128)S(1)}, f32[16,128]{1,0:T(8,128)S(1)}, u32[]{:S(2)}, u32[]{:S(2)}) %collective-permute-start.8) | collective-permute-done | bytes 8224 | tf_op jit(solution)/shard_map/ppermute | solution.py:551
  32.2 0.5 collective-permute-done.7.refs_7_.refs_9_.refs_6_
  32.6 0.6 %middle_parts.1 = (bf16[17,32,128]{2,1,0:T(8,128)(2,1)S(1)}, bf16[17,32,128]{2,1,0:T(8,128)(2,1)S(1)}, bf16[17,32,128]{2,1,0:T(8,128)(2,1)S(1)}, bf16[17,32,128]{2,1,0:T(8,128)(2,1)S(1)}) custom-call(bf16[17,32,128]{2,1,0:T(8,128)(2,1)S(1)} %get-tuple-element.34.refs_0_, bf16[17,32,128]{2,1,0:T(8,128)(2,1)S(1)} %collective-permute-done.refs_0_.refs_1_, ...), custom_call_target="tpu_custom_call" | custom-call | flops 100663296 | bytes 1216512 | tf_op jit(solution)/shard_map/middle_parts/pallas_call | solution.py:531
  33.3 2.4 %collective-permute-start.10 = (bf16[17,32,128]{2,1,0:T(8,128)(2,1)S(1)}, bf16[17,32,128]{2,1,0:T(8,128)(2,1)S(1)}, u32[]{:S(2)}, u32[]{:S(2)}) collective-permute-start(bf16[17,32,128]{2,1,0:T(8,128)(2,1)S(1)} %get-tuple-element.46), channel_id=1, source_target_pairs={{0,3},{1,2},{2,1},{3,0},{4,7},{5,6},{6,5},{7,4},{8,11},{9,10},{10,... | collective-permute-start | bytes 417800 | tf_op jit(solution)/shard_map/ppermute | solution.py:551
  35.6 2.3 %far_parts.1 = (bf16[4,128,128]{2,1,0:T(8,128)(2,1)S(1)}, bf16[4,128,128]{2,1,0:T(8,128)(2,1)S(1)}, bf16[4,128,128]{2,1,0:T(8,128)(2,1)S(1)}, bf16[4,128,128]{2,...) custom-call(bf16[4,128,128]{2,1,0:T(8,128)(2,1)S(1)} %get-tuple-element.38.refs_0_, ...), custom_call_target="tpu_custom_call" | custom-call | flops 1 | bytes 1 | tf_op jit(solution)/shard_map/far_parts/pallas_call | solution.py:531
  38.1 2.1 %collective-permute-start.16 = (bf16[17,32,128]{2,1,0:T(8,128)(2,1)S(1)}, bf16[17,32,128]{2,1,0:T(8,128)(2,1)S(1)}, u32[]{:S(2)}, u32[]{:S(2)}) collective-permute-start(bf16[17,32,128]{2,1,0:T(8,128)(2,1)S(1)} %get-tuple-element.57), channel_id=1, source_target_pairs={{0,2},{1,3},{2,0},{3,1},{4,6},{5,7},{6,4},{7,5},{8,10},{9,11},{10,... | collective-permute-start | bytes 417800 | tf_op jit(solution)/shard_map/ppermute | solution.py:551
  40.2 0.1 collective-permute-done.10.refs_6_.refs_0_
  40.3 0.1 far_sum.1
  40.4 1.6 %collective-permute-start.13 = (bf16[4,128,128]{2,1,0:T(8,128)(2,1)S(1)}, bf16[4,128,128]{2,1,0:T(8,128)(2,1)S(1)}, u32[]{:S(2)}, u32[]{:S(2)}) collective-permute-start(bf16[4,128,128]{2,1,0:T(8,128)(2,1)S(1)} %get-tuple-element.54), channel_id=1, source_target_pairs={{0,24},{4,28},{8,16},{12,20},{16,8},{20,12},{24,0},{28,4},{1,25},{... | collective-permute-start | bytes 393224 | tf_op jit(solution)/shard_map/ppermute | solution.py:551
  42.0 0.5 collective-permute-start.14
  42.5 1.5 %collective-permute-start.15 = (bf16[4,128,128]{2,1,0:T(8,128)(2,1)S(1)}, bf16[4,128,128]{2,1,0:T(8,128)(2,1)S(1)}, u32[]{:S(2)}, u32[]{:S(2)}) collective-permute-start(bf16[4,128,128]{2,1,0:T(8,128)(2,1)S(1)} %get-tuple-element.56), channel_id=1, source_target_pairs={{0,8},{4,12},{8,0},{12,4},{16,24},{20,28},{24,16},{28,20},{1,9},{5... | collective-permute-start | bytes 393224 | tf_op jit(solution)/shard_map/ppermute | solution.py:551
  44.0 2.0 %collective-permute-done.11.refs_7_ = bf16[17,32,128]{2,1,0:T(8,128)(2,1)S(1)} collective-permute-done((bf16[17,32,128]{2,1,0:T(8,128)(2,1)S(1)}, bf16[17,32,128]{2,1,0:T(8,128)(2,1)S(1)}, u32[]{:S(2)}, u32[]{:S(2)}) %collective-permute-start.11) | collective-permute-done | bytes 139296 | tf_op jit(solution)/shard_map/ppermute | solution.py:551
  46.0 1.4 %near_early.1.refs_5_.early_ref = f32[4,12,128,128]{3,2,1,0:T(8,128)S(1)} custom-call(bf16[128,2048]{1,0:T(8,128)(2,1)S(1)} %copy-done, bf16[128,2048]{1,0:T(8,128)(2,1)S(1)} %copy-done.1, bf16[128,2048]{1,0:T(8,128)(2,1)S(1)} %copy-done.2, bf16[128,2048]{1,0:T(8,128)(2,1)S(1)} %copy-done.3, f32[32,128]{1,0:T(8,128)S(1)} %get-tuple-element.33.refs_0_.refs_4_, ...), custom_call_target="tpu_custom_call" | custom-call | flops 2000000000 | bytes 5709824 | tf_op jit(solution)/shard_map/near_early/pallas_call | solution.py:531
  47.5 0.5 %collective-permute-done.16.refs_8_ = bf16[17,32,128]{2,1,0:T(8,128)(2,1)S(1)} collective-permute-done((bf16[17,32,128]{2,1,0:T(8,128)(2,1)S(1)}, bf16[17,32,128]{2,1,0:T(8,128)(2,1)S(1)}, u32[]{:S(2)}, u32[]{:S(2)}) %collective-permute-start.16) | collective-permute-done | bytes 139296 | tf_op jit(solution)/shard_map/ppermute | solution.py:551
  48.0 1.9 %final_others.1 = (bf16[128,2048]{1,0:T(8,128)(2,1)}, bf16[128,2048]{1,0:T(8,128)(2,1)}, bf16[128,2048]{1,0:T(8,128)(2,1)}, bf16[128,2048]{1,0:T(8,128)(2,1)}) custom-call(bf16[128,2048]{1,0:T(8,128)(2,1)S(1)} %copy-done, bf16[128,2048]{1,0:T(8,128)(2,1)S(1)} %copy-done.1, bf16[128,2048]{1,0:T(8,128)(2,1)S(1)} %copy-done.2, bf16[128,2048]{1,0:T(8,128)(2,1)S(1)} %copy-done.3, ...), custom_call_target="tpu_custom_call" | custom-call | flops 1000000000 | bytes 7774208 | tf_op jit(solution)/shard_map/final_others/pallas_call | solution.py:531
  50.0 1.1 %final_own.1 = (bf16[128,2048]{1,0:T(8,128)(2,1)}, bf16[128,2048]{1,0:T(8,128)(2,1)}, bf16[128,2048]{1,0:T(8,128)(2,1)}, bf16[128,2048]{1,0:T(8,128)(2,1)}) custom-call(f32[4,12,128,128]{3,2,1,0:T(8,128)S(1)} %near_early.1.refs_5_.early_ref, ...), custom_call_target="tpu_custom_call", output_to_operand_aliasing={{0}: (6, {}), {1}: (7, {}), {2}: (8, {}), {3}: (9, {})} | custom-call | flops 16777216 | bytes 8003584 | tf_op jit(solution)/shard_map/final_own/pallas_call | solution.py:531
  (26 shorter events, 0.2 us)
Async XLA Ops:
  4.6 9.7 %collective-permute-start = (bf16[17,32,128]{2,1,0:T(8,128)(2,1)S(1)}, bf16[17,32,128]{2,1,0:T(8,128)(2,1)S(1)}, u32[]{:S(2)}, u32[]{:S(2)}) collective-permute-start(bf16[17,32,128]{2,1,0:T(8,128)(2,1)S(1)} %get-tuple-element.35), channel_id=1, source_target_pairs={{0,3},{1,2},{2,1},{3,0},{4,5},{5,4},{6,7},{7,6},{8,11},{9,10},{10,... | collective-permute-start | bytes 417800 | tf_op jit(solution)/shard_map/ppermute | solution.py:581
  9.7 13.0 %collective-permute-start.1 = (bf16[17,32,128]{2,1,0:T(8,128)(2,1)S(1)}, bf16[17,32,128]{2,1,0:T(8,128)(2,1)S(1)}, u32[]{:S(2)}, u32[]{:S(2)}) collective-permute-start(bf16[17,32,128]{2,1,0:T(8,128)(2,1)S(1)} %get-tuple-element.36), channel_id=1, source_target_pairs={{0,2},{1,3},{2,0},{3,1},{4,7},{5,6},{6,5},{7,4},{8,10},{9,11},{10,... | collective-permute-start | bytes 417800 | tf_op jit(solution)/shard_map/ppermute | solution.py:581
  9.7 13.0 %collective-permute-start.3 = (bf16[4,128,128]{2,1,0:T(8,128)(2,1)S(1)}, bf16[4,128,128]{2,1,0:T(8,128)(2,1)S(1)}, u32[]{:S(2)}, u32[]{:S(2)}) collective-permute-start(bf16[4,128,128]{2,1,0:T(8,128)(2,1)S(1)} %get-tuple-element.39), channel_id=1, source_target_pairs={{0,8},{4,12},{8,0},{12,4},{16,24},{20,28},{24,16},{28,20},{1,9},{5... | collective-permute-start | bytes 393224 | tf_op jit(solution)/shard_map/ppermute | solution.py:551
  11.2 11.5 %collective-permute-start.4 = (bf16[4,128,128]{2,1,0:T(8,128)(2,1)S(1)}, bf16[4,128,128]{2,1,0:T(8,128)(2,1)S(1)}, u32[]{:S(2)}, u32[]{:S(2)}) collective-permute-start(bf16[4,128,128]{2,1,0:T(8,128)(2,1)S(1)} %get-tuple-element.40), channel_id=1, source_target_pairs={{0,16},{4,20},{8,24},{12,28},{16,0},{20,4},{24,8},{28,12},{1,17},{... | collective-permute-start | bytes 393224 | tf_op jit(solution)/shard_map/ppermute | solution.py:551
  12.7 9.9 %collective-permute-start.5 = (bf16[4,128,128]{2,1,0:T(8,128)(2,1)S(1)}, bf16[4,128,128]{2,1,0:T(8,128)(2,1)S(1)}, u32[]{:S(2)}, u32[]{:S(2)}) collective-permute-start(bf16[4,128,128]{2,1,0:T(8,128)(2,1)S(1)} %get-tuple-element.41), channel_id=1, source_target_pairs={{0,24},{4,28},{8,16},{12,20},{16,8},{20,12},{24,0},{28,4},{1,25},{... | collective-permute-start | bytes 393224 | tf_op jit(solution)/shard_map/ppermute | solution.py:551
  14.2 11.2 %collective-permute-start.2 = (bf16[17,32,128]{2,1,0:T(8,128)(2,1)}, bf16[17,32,128]{2,1,0:T(8,128)(2,1)S(1)}, u32[]{:S(2)}, u32[]{:S(2)}) collective-permute-start(bf16[17,32,128]{2,1,0:T(8,128)(2,1)} %get-tuple-element.37), channel_id=1, source_target_pairs={{0,1},{1,0},{2,3},{3,2},{4,6},{5,7},{6,4},{7,5},{8,9},{9,8},{10,11... | collective-permute-start | bytes 417800 | tf_op jit(solution)/shard_map/ppermute | solution.py:581
  22.7 1.6 %collective-permute-start.6 = (bf16[4,2,128,128]{3,2,1,0:T(8,128)(2,1)S(1)}, bf16[4,2,128,128]{3,2,1,0:T(8,128)(2,1)S(1)}, u32[]{:S(2)}, u32[]{:S(2)}) collective-permute-start(bf16[4,2,128,128]{3,2,1,0:T(8,128)(2,1)S(1)} %pack.1), channel_id=1, source_target_pairs={{0,4},{4,0},{8,12},{12,8},{16,20},{20,16},{24,28},{28,24},{1,5},{5... | collective-permute-start | bytes 786440 | tf_op jit(solution)/shard_map/ppermute | solution.py:551
  26.0 4.6 %collective-permute-start.9 = (f32[16,128]{1,0:T(8,128)S(1)}, f32[16,128]{1,0:T(8,128)S(1)}, u32[]{:S(2)}, u32[]{:S(2)}) collective-permute-start(f32[16,128]{1,0:T(8,128)S(1)} %get-tuple-element.44.refs_6_.refs_8_.refs_5_), channel_id=1, source_target_pairs={{0,24},{4,28},{8,16},{12,20},{16,8},{20,12},{24,0},{28,4},{1,25},{... | collective-permute-start | bytes 24584 | tf_op jit(solution)/shard_map/ppermute | solution.py:551
  28.5 3.7 %collective-permute-start.8 = (f32[16,128]{1,0:T(8,128)S(1)}, f32[16,128]{1,0:T(8,128)S(1)}, u32[]{:S(2)}, u32[]{:S(2)}) collective-permute-start(f32[16,128]{1,0:T(8,128)S(1)} %get-tuple-element.44.refs_6_.refs_8_.refs_5_), channel_id=1, source_target_pairs={{0,16},{4,20},{8,24},{12,28},{16,0},{20,4},{24,8},{28,12},{1,17},{... | collective-permute-start | bytes 24584 | tf_op jit(solution)/shard_map/ppermute | solution.py:551
  29.0 3.7 %collective-permute-start.7 = (f32[16,128]{1,0:T(8,128)S(1)}, f32[16,128]{1,0:T(8,128)S(1)}, u32[]{:S(2)}, u32[]{:S(2)}) collective-permute-start(f32[16,128]{1,0:T(8,128)S(1)} %get-tuple-element.44.refs_6_.refs_8_.refs_5_), channel_id=1, source_target_pairs={{0,8},{4,12},{8,0},{12,4},{16,24},{20,28},{24,16},{28,20},{1,9},{5... | collective-permute-start | bytes 24584 | tf_op jit(solution)/shard_map/ppermute | solution.py:551
  33.3 7.0 %collective-permute-start.10 = (bf16[17,32,128]{2,1,0:T(8,128)(2,1)S(1)}, bf16[17,32,128]{2,1,0:T(8,128)(2,1)S(1)}, u32[]{:S(2)}, u32[]{:S(2)}) collective-permute-start(bf16[17,32,128]{2,1,0:T(8,128)(2,1)S(1)} %get-tuple-element.46), channel_id=1, source_target_pairs={{0,3},{1,2},{2,1},{3,0},{4,7},{5,6},{6,5},{7,4},{8,11},{9,10},{10,... | collective-permute-start | bytes 417800 | tf_op jit(solution)/shard_map/ppermute | solution.py:551
  37.9 2.4 %collective-permute-start.12 = (bf16[4,2,128,128]{3,2,1,0:T(8,128)(2,1)S(1)}, bf16[4,2,128,128]{3,2,1,0:T(8,128)(2,1)S(1)}, u32[]{:S(2)}, u32[]{:S(2)}) collective-permute-start(bf16[4,2,128,128]{3,2,1,0:T(8,128)(2,1)S(1)} %get-tuple-element.52), channel_id=1, source_target_pairs={{0,4},{4,0},{8,12},{12,8},{16,20},{20,16},{24,28},{28,24},{1,5},{5... | collective-permute-start | bytes 786440 | tf_op jit(solution)/shard_map/ppermute | solution.py:551
  38.0 8.0 %collective-permute-start.11 = (bf16[17,32,128]{2,1,0:T(8,128)(2,1)S(1)}, bf16[17,32,128]{2,1,0:T(8,128)(2,1)S(1)}, u32[]{:S(2)}, u32[]{:S(2)}) collective-permute-start(bf16[17,32,128]{2,1,0:T(8,128)(2,1)S(1)} %get-tuple-element.47), channel_id=1, source_target_pairs={{0,1},{1,0},{2,3},{3,2},{4,5},{5,4},{6,7},{7,6},{8,9},{9,8},{10,11... | collective-permute-start | bytes 417800 | tf_op jit(solution)/shard_map/ppermute | solution.py:551
  38.1 9.9 %collective-permute-start.16 = (bf16[17,32,128]{2,1,0:T(8,128)(2,1)S(1)}, bf16[17,32,128]{2,1,0:T(8,128)(2,1)S(1)}, u32[]{:S(2)}, u32[]{:S(2)}) collective-permute-start(bf16[17,32,128]{2,1,0:T(8,128)(2,1)S(1)} %get-tuple-element.57), channel_id=1, source_target_pairs={{0,2},{1,3},{2,0},{3,1},{4,6},{5,7},{6,4},{7,5},{8,10},{9,11},{10,... | collective-permute-start | bytes 417800 | tf_op jit(solution)/shard_map/ppermute | solution.py:551
  40.3 5.7 %copy-start = (bf16[128,2048]{1,0:T(8,128)(2,1)S(1)}, bf16[128,2048]{1,0:T(8,128)(2,1)}, u32[]{:S(2)}) copy-start(bf16[128,2048]{1,0:T(8,128)(2,1)} %refs_0_.5) | copy-start | bytes 1572868
  40.3 5.7 %copy-start.1 = (bf16[128,2048]{1,0:T(8,128)(2,1)S(1)}, bf16[128,2048]{1,0:T(8,128)(2,1)}, u32[]{:S(2)}) copy-start(bf16[128,2048]{1,0:T(8,128)(2,1)} %refs_1_.5) | copy-start | bytes 1572868
  40.3 5.7 %copy-start.2 = (bf16[128,2048]{1,0:T(8,128)(2,1)S(1)}, bf16[128,2048]{1,0:T(8,128)(2,1)}, u32[]{:S(2)}) copy-start(bf16[128,2048]{1,0:T(8,128)(2,1)} %refs_2_.5) | copy-start | bytes 1572868
  40.3 5.7 %copy-start.3 = (bf16[128,2048]{1,0:T(8,128)(2,1)S(1)}, bf16[128,2048]{1,0:T(8,128)(2,1)}, u32[]{:S(2)}) copy-start(bf16[128,2048]{1,0:T(8,128)(2,1)} %refs_3_.5) | copy-start | bytes 1572868
  40.4 9.5 %collective-permute-start.13 = (bf16[4,128,128]{2,1,0:T(8,128)(2,1)S(1)}, bf16[4,128,128]{2,1,0:T(8,128)(2,1)S(1)}, u32[]{:S(2)}, u32[]{:S(2)}) collective-permute-start(bf16[4,128,128]{2,1,0:T(8,128)(2,1)S(1)} %get-tuple-element.54), channel_id=1, source_target_pairs={{0,24},{4,28},{8,16},{12,20},{16,8},{20,12},{24,0},{28,4},{1,25},{... | collective-permute-start | bytes 393224 | tf_op jit(solution)/shard_map/ppermute | solution.py:551
  42.0 8.0 %collective-permute-start.14 = (bf16[4,128,128]{2,1,0:T(8,128)(2,1)S(1)}, bf16[4,128,128]{2,1,0:T(8,128)(2,1)S(1)}, u32[]{:S(2)}, u32[]{:S(2)}) collective-permute-start(bf16[4,128,128]{2,1,0:T(8,128)(2,1)S(1)} %get-tuple-element.55), channel_id=1, source_target_pairs={{0,16},{4,20},{8,24},{12,28},{16,0},{20,4},{24,8},{28,12},{1,17},{... | collective-permute-start | bytes 393224 | tf_op jit(solution)/shard_map/ppermute | solution.py:551
  42.5 7.5 %collective-permute-start.15 = (bf16[4,128,128]{2,1,0:T(8,128)(2,1)S(1)}, bf16[4,128,128]{2,1,0:T(8,128)(2,1)S(1)}, u32[]{:S(2)}, u32[]{:S(2)}) collective-permute-start(bf16[4,128,128]{2,1,0:T(8,128)(2,1)S(1)} %get-tuple-element.56), channel_id=1, source_target_pairs={{0,8},{4,12},{8,0},{12,4},{16,24},{20,28},{24,16},{28,20},{1,9},{5... | collective-permute-start | bytes 393224 | tf_op jit(solution)/shard_map/ppermute | solution.py:551

commit v16 on v14

--- a/solution.py
+++ b/solution.py
@@ -17,6 +17,7 @@
 SHORT = 2 * 10**9
 VMEM_LIMIT = 32 * 1024 * 1024
 PICK_LIMIT = 53 * 1024 * 1024
+FIRST_LIMIT = 54784 * 1024
 NEAR_LIMIT = 54784 * 1024
 F32, BF16 = jnp.float32, jnp.bfloat16
 SHAPE = jax.ShapeDtypeStruct
@@ -50,24 +51,17 @@
     return lax.axis_index("seqi"), lax.axis_index("seqo") // width
 
 
-def distance(n_i, step, odd):
-    order = [1, *range(n_i - 1, 1, -1)] if odd else list(range(n_i - 1, 0, -1))
-    return order[step - 1]
+def distance(n_i, step):
+    return n_i - step
 
 
 def distance_back(n_i, step):
     return n_i - 1 if step == 1 else step - 1
 
 
-def is_odd():
-    return lax.axis_index("seqo") % 2 == 1
-
-
 def place_in(n_i, slots, step):
     pos, _ = position(slots)
-    if step == 0:
-        return pos
-    return pos ^ jnp.where(is_odd(), distance(n_i, step, True), distance(n_i, step, False))
+    return pos if step == 0 else pos ^ distance(n_i, step)
 
 
 def first_back(n_i, slots, step):
@@ -76,14 +70,10 @@
 
 
 def in_back_order(n_i, chunks):
-    found = [chunks[0]]
-    for step in range(1, n_i):
-        even, odd = [
-            [distance(n_i, k, parity) for k in range(1, n_i)].index(distance_back(n_i, step)) + 1
-            for parity in (False, True)
-        ]
-        found.append(jnp.where(is_odd(), chunks[odd], chunks[even]))
-    return found
+    order = [distance(n_i, step) for step in range(1, n_i)]
+    return [chunks[0]] + [
+        chunks[order.index(distance_back(n_i, step)) + 1] for step in range(1, n_i)
+    ]
 
 
 def lanes_of(rows):
@@ -138,15 +128,15 @@
     return picked
 
 
-def fetch(sources, buffers, sems):
-    width = DILATION * HEAD_DIM
+def fetch(slots, places, sources, buffers, sems):
+    width = slots * HEAD_DIM
     groups = []
-    for group in range(HEADS // DILATION):
-        cols = pl.ds(group * width, width)
+    for index, place in enumerate(places):
+        cols = pl.ds(pl.multiple_of(place * width, width), width)
         groups.append(
             [
                 pltpu.make_async_copy(
-                    source.at[:, cols], buffers.at[which, :, cols], sems.at[which, group]
+                    source.at[:, cols], buffers.at[index, which], sems.at[index, which]
                 )
                 for which, source in enumerate(sources)
             ]
@@ -170,41 +160,61 @@
     return jnp.where(lanes_of(x.shape[0]) < 2 * HEADS, x, 0.0)
 
 
-def pick_kernel(n_i, slots, *refs):
-    sources, refs = refs[:4], refs[4:]
-    mids, refs = refs[:n_i], refs[n_i:]
-    fulls, refs = refs[:slots], refs[slots:]
-    stats_ref, buffers, sems, wide, picked, turn = refs
+def pick_places(n_i, slots, steps, sources, mids, buffers, sems, wide, turn):
     rows = sources[0].shape[0]
     quarter = rows // DILATION
-    pos, chip = position(slots)
-    turn[...] = jnp.zeros_like(turn)
-    for group, copies in enumerate(fetch(sources, buffers, sems)):
+    places = [place_in(n_i, slots, step) for step in steps]
+    for index, copies in enumerate(fetch(slots, places, sources, buffers, sems)):
+        first = places[index] * slots
         for which, copy in enumerate(copies):
             copy.wait()
-            for residue in range(DILATION):
-                head = group * DILATION + residue
-                wide[which, head] = buffers[which, :, static_columns(head)].astype(F32)
-                rowset = wide[which, head, pl.ds(residue, quarter, stride=DILATION), :]
-                picked[head // slots, which * slots + head % slots] = rowset.astype(BF16)
-        heads = range(group * DILATION, (group + 1) * DILATION)
-        operands = [[buffers[which, :, static_columns(head)] for which in range(4)] for head in heads]
-        for head, (e, d) in zip(heads, level_stats(operands)):
-            turn[head : head + 1, :] = e
-            turn[HEADS + head : HEADS + head + 1, :] = d
+            for slot in range(slots):
+                wide[index, which, slot] = buffers[index, which, :, static_columns(slot)].astype(F32)
+                residue = (first + slot) % DILATION if slots % DILATION else slot % DILATION
+                rowset = wide[index, which, slot, pl.ds(residue, quarter, stride=DILATION), :]
+                mids[index][which * slots + slot] = rowset.astype(BF16)
+        operands = [
+            [buffers[index, which, :, static_columns(slot)] for which in range(4)]
+            for slot in range(slots)
+        ]
+        for slot, (e, d) in enumerate(level_stats(operands)):
+            turn[pl.ds(first + slot, 1), :] = e
+            turn[pl.ds(HEADS + first + slot, 1), :] = d
+
+
+def pick_first_kernel(n_i, slots, *refs):
+    sources, (mid_ref, stats_ref, buffers, sems, wide, turn) = refs[:4], refs[4:]
+    rows = sources[0].shape[0]
+    turn[...] = jnp.zeros_like(turn)
+    pick_places(n_i, slots, [1], sources, [mid_ref], buffers, sems, wide, turn)
+    stats_ref[...] = turn[: 2 * HEADS, :]
+    turn[...] = turn[...].T
+    mid_ref[4 * slots] = split(pick_rows(turn, rows))
+
+
+def pick_rest_kernel(n_i, slots, *refs):
+    sources, first_ref, refs = refs[:4], refs[4], refs[5:]
+    mids, refs = refs[: n_i - 1], refs[n_i - 1 :]
+    fulls, refs = refs[:slots], refs[slots:]
+    stats_ref, buffers, sems, wide, turn = refs
+    rows = sources[0].shape[0]
+    _, chip = position(slots)
+    turn[...] = jnp.zeros_like(turn)
+    turn[: 2 * HEADS, :] = first_ref[...]
+    steps = [0, *range(2, n_i)]
+    pick_places(n_i, slots, steps, sources, mids, buffers, sems, wide, turn)
+    for m in range(slots):
+        fulls[m][...] = buffers[0, :, :, head_columns(chip ^ m)]
     stats_ref[...] = turn[: 2 * HEADS, :]
     turn[...] = turn[...].T
     near = split(pick_rows(turn, rows))
-    for d in range(n_i):
-        mids[d][: 4 * slots] = picked[place_in(n_i, slots, d)]
-        mids[d][4 * slots] = near
-    for m in range(slots):
-        fulls[m][...] = buffers[:, :, head_columns(pos * slots + (chip ^ m))]
+    for ref in mids:
+        ref[4 * slots] = near
 
 
 def pack_kernel(slots, *refs):
     packed_ref = refs[-1]
-    for m, ref in enumerate(refs[:slots]):
+    for m, ref in enumerate(in_back(refs[:slots])):
         packed_ref[m] = ref[:2]
 
 
@@ -571,15 +581,9 @@
         return SHAPE((count, lanes), F32)
 
     def swap_mids(pieces):
-        found = [pieces[0]]
-        for step in range(1, n_i):
-            pairs = [
-                (o * n_i + i, o * n_i + (i ^ distance(n_i, step, o % 2 == 1)))
-                for o in range(n_o)
-                for i in range(n_i)
-            ]
-            found.append(lax.ppermute(pieces[step], ("seqo", "seqi"), pairs))
-        return found
+        return [pieces[0]] + [
+            swap(pieces[step], "seqi", n_i, distance(n_i, step)) for step in range(1, n_i)
+        ]
 
     def swap_back(pieces):
         return [pieces[0]] + [
@@ -589,29 +593,41 @@
     def swap_fulls(pieces):
         return [pieces[0]] + [swap(pieces[m], "seqo", n_o, m * width) for m in range(1, slots)]
 
-    pieces = call(
-        bind(pick_kernel, n_i, slots),
-        "pick",
-        [mid] * n_i + [full] * slots + [stats(2 * HEADS)],
-        [
-            pltpu.VMEM((4, rows, features), BF16),
-            pltpu.SemaphoreType.DMA((4, HEADS // DILATION)),
-            pltpu.VMEM((4, HEADS, rows, HEAD_DIM), F32),
-            pltpu.VMEM((n_i, 4 * slots, quarter, HEAD_DIM), BF16),
+    def pick_scratch(count):
+        return [
+            pltpu.VMEM((count, 4, rows, slots * HEAD_DIM), BF16),
+            pltpu.SemaphoreType.DMA((count, 4)),
+            pltpu.VMEM((count, 4, slots, rows, HEAD_DIM), F32),
             square,
-        ],
-        unit * HEADS * 2,
+        ]
+
+    first, firststats = call(
+        bind(pick_first_kernel, n_i, slots),
+        "pick_first",
+        [mid, stats(2 * HEADS)],
+        pick_scratch(1),
+        unit * slots * 2,
         sources,
         hbm_in=range(4),
+        limit=FIRST_LIMIT,
+    )
+    pieces = call(
+        bind(pick_rest_kernel, n_i, slots),
+        "pick_rest",
+        [mid] * (n_i - 1) + [full] * slots + [stats(2 * HEADS)],
+        pick_scratch(n_i - 1),
+        unit * HEADS * 2,
+        [*sources, firststats],
+        hbm_in=range(4),
         limit=PICK_LIMIT,
     )
-    mids = swap_mids(pieces[:n_i])
-    fulls = swap_fulls(pieces[n_i : n_i + slots])
+    mids = swap_mids([pieces[0], first, *pieces[1 : n_i - 1]])
+    fulls = swap_fulls(pieces[n_i - 1 : n_i - 1 + slots])
     near = pieces[-1]
 
     (settled,) = call(settle_kernel, "far_in", [stats(8)], [], SHORT, [mids[1]])
     (settled,) = call(settle_kernel, "chips_back", [stats(8)], [], LONG, [settled])
-    (packed,) = call(bind(pack_kernel, slots), "pack", [half], [], 1, fulls + [settled])
+    (packed,) = call(bind(pack_kernel, slots), "pack", [half], [], 1, [*in_back(fulls), settled])
     sibs = [swap(packed, "seqo", n_o, part) for part in range(1, width)]
     (settled,) = call(settle_kernel, "packed_back", [stats(8)], [], LONG, [near])
     (far,) = call(

time: 47.7 us -> 47.1 us (0.987)
  waiting for transfers between devices: 12.7 us -> 11.4 us
  Pallas kernels: 13.1 us -> 13.6 us
    ppermute x14 -> x17, starting transfers between devices: 15.2 us -> 21 us  [swap(): return lax.ppermute(x, axis, [(i, i ^ mask) for i in range(n)])]
    ppermute x3 -> x0, starting transfers between devices: 5.76 us -> none  [swap_mids(): found.append(lax.ppermute(pieces[step], ('seqo', 'seqi'), pairs))]
    ppermute x3 -> x0, waiting for transfers between devices: 1.05 us -> none  [swap_mids(): found.append(lax.ppermute(pieces[step], ('seqo', 'seqi'), pairs))]
    pallas_call x16 -> x17, Pallas kernels: 13.1 us -> 13.6 us  [call(): pl.pallas_call(kernel, out_shape=tuple(outs), in_specs=[pl.BlockSpec(memo...]
    ppermute x14 -> x17, waiting for transfers between devices: 11.7 us -> 11.4 us  [swap(): return lax.ppermute(x, axis, [(i, i ^ mask) for i in range(n)])]
  transfers between devices with their start and end apart: 17 -> 17, of which waited for: 12 -> 8; matrix products, arithmetic and copies ran while one was open for 0% -> 0% of each run, Pallas kernels for 14% -> 21%
where the time goes in v16:
time: 47.1 us; the launch traced here: 46.9 us
  starting transfers between devices  21 us (45%)
  Pallas kernels  13.6 us (29%)
  waiting for transfers between devices  11.4 us (24%)
  between operations  0.82 us (2%)
    ppermute x17, starting transfers between devices, swap(): return lax.ppermute(x, axis, [(i, i ^ mask) for i in range(n)])  21 us
    pallas_call x17, Pallas kernels, call(): pl.pallas_call(kernel, out_shape=tuple(outs), in_specs=[pl.BlockSpec(memo...  13.6 us
    ppermute x17, waiting for transfers between devices, swap(): return lax.ppermute(x, axis, [(i, i ^ mask) for i in range(n)])  11.4 us
  transfers between devices with their start and end apart: 17, of which 8 were waited for; matrix products, arithmetic and copies ran while one was open for 0% of the time, Pallas kernels for 21%

profile of v16, /device:TPU:0, one launch (start us, length us, event | category | flops | bytes accessed | tf_op | source)
XLA Modules:
  0.0 46.9 jit_solution(13007890953455104987)
XLA Ops:
  0.6 1.7 %pick_first.1 = (bf16[17,32,128]{2,1,0:T(8,128)(2,1)S(1)}, f32[32,128]{1,0:T(8,128)S(1)}) custom-call(bf16[128,2048]{1,0:T(8,128)(2,1)} %refs_0_.7, bf16[128,2048]{1,0:T(8,128)(2,1)} %refs_1_.7, bf16[128,2048]{1,0:T(8,128)(2,1)} %refs_2_.7, bf16[128,2048]{1,0:T(8,128)(2,1)} %refs_3_.7), custom_call_target="tpu_custom_call" | custom-call | flops 33554432 | bytes 2252800 | tf_op jit(solution)/shard_map/pick_first/pallas_call | solution.py:541
  2.3 5.1 %collective-permute-start = (bf16[17,32,128]{2,1,0:T(8,128)(2,1)S(1)}, bf16[17,32,128]{2,1,0:T(8,128)(2,1)S(1)}, u32[]{:S(2)}, u32[]{:S(2)}) collective-permute-start(bf16[17,32,128]{2,1,0:T(8,128)(2,1)S(1)} %get-tuple-element.37), channel_id=1, source_target_pairs={{0,3},{1,2},{2,1},{3,0},{4,7},{5,6},{6,5},{7,4},{8,11},{9,10},{10,... | collective-permute-start | bytes 417800 | tf_op jit(solution)/shard_map/ppermute | solution.py:561
  7.4 2.7 %pick_rest.1 = (bf16[17,32,128]{2,1,0:T(8,128)(2,1)S(1)}, bf16[17,32,128]{2,1,0:T(8,128)(2,1)S(1)}, bf16[17,32,128]{2,1,0:T(8,128)(2,1)S(1)}, bf16[4,128,128]{2,...) custom-call(bf16[128,2048]{1,0:T(8,128)(2,1)} %refs_0_.7, ...), custom_call_target="tpu_custom_call" | custom-call | flops 134217728 | bytes 3072000 | tf_op jit(solution)/shard_map/pick_rest/pallas_call | solution.py:541
  10.2 1.6 %collective-permute-start.3 = (bf16[4,128,128]{2,1,0:T(8,128)(2,1)S(1)}, bf16[4,128,128]{2,1,0:T(8,128)(2,1)S(1)}, u32[]{:S(2)}, u32[]{:S(2)}) collective-permute-start(bf16[4,128,128]{2,1,0:T(8,128)(2,1)S(1)} %get-tuple-element.41), channel_id=1, source_target_pairs={{0,8},{4,12},{8,0},{12,4},{16,24},{20,28},{24,16},{28,20},{1,9},{5... | collective-permute-start | bytes 393224 | tf_op jit(solution)/shard_map/ppermute | solution.py:561
  11.7 1.5 %collective-permute-start.4 = (bf16[4,128,128]{2,1,0:T(8,128)(2,1)S(1)}, bf16[4,128,128]{2,1,0:T(8,128)(2,1)S(1)}, u32[]{:S(2)}, u32[]{:S(2)}) collective-permute-start(bf16[4,128,128]{2,1,0:T(8,128)(2,1)S(1)} %get-tuple-element.42), channel_id=1, source_target_pairs={{0,16},{4,20},{8,24},{12,28},{16,0},{20,4},{24,8},{28,12},{1,17},{... | collective-permute-start | bytes 393224 | tf_op jit(solution)/shard_map/ppermute | solution.py:561
  13.3 0.5 %collective-permute-start.5 = (bf16[4,128,128]{2,1,0:T(8,128)(2,1)S(1)}, bf16[4,128,128]{2,1,0:T(8,128)(2,1)S(1)}, u32[]{:S(2)}, u32[]{:S(2)}) collective-permute-start(bf16[4,128,128]{2,1,0:T(8,128)(2,1)S(1)} %get-tuple-element.43), channel_id=1, source_target_pairs={{0,24},{4,28},{8,16},{12,20},{16,8},{20,12},{24,0},{28,4},{1,25},{... | collective-permute-start | bytes 393224 | tf_op jit(solution)/shard_map/ppermute | solution.py:561
  13.7 0.6 %collective-permute-start.2 = (bf16[17,32,128]{2,1,0:T(8,128)(2,1)S(1)}, bf16[17,32,128]{2,1,0:T(8,128)(2,1)S(1)}, u32[]{:S(2)}, u32[]{:S(2)}) collective-permute-start(bf16[17,32,128]{2,1,0:T(8,128)(2,1)S(1)} %get-tuple-element.39), channel_id=1, source_target_pairs={{0,1},{1,0},{2,3},{3,2},{4,5},{5,4},{6,7},{7,6},{8,9},{9,8},{10,11... | collective-permute-start | bytes 417800 | tf_op jit(solution)/shard_map/ppermute | solution.py:561
  14.3 1.3 %collective-permute-done.3.refs_3_.refs_1_ = bf16[4,128,128]{2,1,0:T(8,128)(2,1)S(1)} collective-permute-done((bf16[4,128,128]{2,1,0:T(8,128)(2,1)S(1)}, bf16[4,128,128]{2,1,0:T(8,128)(2,1)S(1)}, u32[]{:S(2)}, u32[]{:S(2)}) %collective-permute-start.3) | collective-permute-done | bytes 131104 | tf_op jit(solution)/shard_map/ppermute | solution.py:561
  15.6 3.9 %collective-permute-done.4.refs_2_ = bf16[4,128,128]{2,1,0:T(8,128)(2,1)S(1)} collective-permute-done((bf16[4,128,128]{2,1,0:T(8,128)(2,1)S(1)}, bf16[4,128,128]{2,1,0:T(8,128)(2,1)S(1)}, u32[]{:S(2)}, u32[]{:S(2)}) %collective-permute-start.4) | collective-permute-done | bytes 131104 | tf_op jit(solution)/shard_map/ppermute | solution.py:561
  19.6 1.5 %collective-permute-done.6.refs_4_ = bf16[4,2,128,128]{3,2,1,0:T(8,128)(2,1)S(1)} collective-permute-done((bf16[4,2,128,128]{3,2,1,0:T(8,128)(2,1)S(1)}, bf16[4,2,128,128]{3,2,1,0:T(8,128)(2,1)S(1)}, u32[]{:S(2)}, u32[]{:S(2)}) %collective-permute-start.6) | collective-permute-done | bytes 262176 | tf_op jit(solution)/shard_map/ppermute | solution.py:561
  21.1 1.1 %far_stats.1.refs_5_ = f32[8,128]{1,0:T(8,128)S(1)} custom-call(bf16[4,128,128]{2,1,0:T(8,128)(2,1)S(1)} %get-tuple-element.40.refs_0_, bf16[4,128,128]{2,1,0:T(8,128)(2,1)S(1)} %collective-permute-done.3.refs_3_.refs_1_, bf16[4,128,128]{2,1,0:T(8,128)(2,1)S(1)} %collective-permute-done.4.refs_2_, ...), custom_call_target="tpu_custom_call" | custom-call | flops 1 | bytes 794624 | tf_op jit(solution)/shard_map/far_stats/pallas_call | solution.py:541
  22.3 0.5 %middle_stats.1 = (f32[16,128]{1,0:T(8,128)S(1)}, f32[8,128]{1,0:T(8,128)S(1)}, f32[128,128]{1,0:T(8,128)S(1)}) custom-call(bf16[17,32,128]{2,1,0:T(8,128)(2,1)S(1)} %get-tuple-element.36.refs_0_, bf16[17,32,128]{2,1,0:T(8,128)(2,1)S(1)} %collective-permute-done.refs_0_.refs_1_, bf16[17,32,128]{2,1,0:T(8,128)(2,1)S(1)} %collective-permute-done.1.refs_2_, ...), custom_call_target="tpu_custom_call" | custom-call | flops 33554432 | bytes 655360 | tf_op jit(solution)/shard_map/middle_stats/pallas_call | solution.py:541
  22.8 1.3 %collective-permute-start.9 = (f32[16,128]{1,0:T(8,128)S(1)}, f32[16,128]{1,0:T(8,128)S(1)}, u32[]{:S(2)}, u32[]{:S(2)}) collective-permute-start(f32[16,128]{1,0:T(8,128)S(1)} %get-tuple-element.46.refs_6_.refs_8_.refs_5_), channel_id=1, source_target_pairs={{0,24},{4,28},{8,16},{12,20},{16,8},{20,12},{24,0},{28,4},{1,25},{... | collective-permute-start | bytes 24584 | tf_op jit(solution)/shard_map/ppermute | solution.py:561
  24.1 1.2 %collective-permute-start.8 = (f32[16,128]{1,0:T(8,128)S(1)}, f32[16,128]{1,0:T(8,128)S(1)}, u32[]{:S(2)}, u32[]{:S(2)}) collective-permute-start(f32[16,128]{1,0:T(8,128)S(1)} %get-tuple-element.46.refs_6_.refs_8_.refs_5_), channel_id=1, source_target_pairs={{0,16},{4,20},{8,24},{12,28},{16,0},{20,4},{24,8},{28,12},{1,17},{... | collective-permute-start | bytes 24584 | tf_op jit(solution)/shard_map/ppermute | solution.py:561
  25.3 1.1 %collective-permute-start.7 = (f32[16,128]{1,0:T(8,128)S(1)}, f32[16,128]{1,0:T(8,128)S(1)}, u32[]{:S(2)}, u32[]{:S(2)}) collective-permute-start(f32[16,128]{1,0:T(8,128)S(1)} %get-tuple-element.46.refs_6_.refs_8_.refs_5_), channel_id=1, source_target_pairs={{0,8},{4,12},{8,0},{12,4},{16,24},{20,28},{24,16},{28,20},{1,9},{5... | collective-permute-start | bytes 24584 | tf_op jit(solution)/shard_map/ppermute | solution.py:561
  26.4 1.1 %collective-permute-done.9.refs_9_.refs_11_.refs_8_ = f32[16,128]{1,0:T(8,128)S(1)} collective-permute-done((f32[16,128]{1,0:T(8,128)S(1)}, f32[16,128]{1,0:T(8,128)S(1)}, u32[]{:S(2)}, u32[]{:S(2)}) %collective-permute-start.9) | collective-permute-done | bytes 8224 | tf_op jit(solution)/shard_map/ppermute | solution.py:561
  27.4 0.3 collective-permute-done.8.refs_8_.refs_10_.refs_7_
  27.7 1.2 %collective-permute-done.7.refs_7_.refs_9_.refs_6_ = f32[16,128]{1,0:T(8,128)S(1)} collective-permute-done((f32[16,128]{1,0:T(8,128)S(1)}, f32[16,128]{1,0:T(8,128)S(1)}, u32[]{:S(2)}, u32[]{:S(2)}) %collective-permute-start.7) | collective-permute-done | bytes 8224 | tf_op jit(solution)/shard_map/ppermute | solution.py:561
  28.9 0.6 %middle_parts.1 = (bf16[17,32,128]{2,1,0:T(8,128)(2,1)S(1)}, bf16[17,32,128]{2,1,0:T(8,128)(2,1)S(1)}, bf16[17,32,128]{2,1,0:T(8,128)(2,1)S(1)}, bf16[17,32,128]{2,1,0:T(8,128)(2,1)S(1)}) custom-call(bf16[17,32,128]{2,1,0:T(8,128)(2,1)S(1)} %get-tuple-element.36.refs_0_, bf16[17,32,128]{2,1,0:T(8,128)(2,1)S(1)} %collective-permute-done.refs_0_.refs_1_, ...), custom_call_target="tpu_custom_call" | custom-call | flops 100663296 | bytes 1216512 | tf_op jit(solution)/shard_map/middle_parts/pallas_call | solution.py:541
  29.6 0.8 %collective-permute-start.10 = (bf16[17,32,128]{2,1,0:T(8,128)(2,1)S(1)}, bf16[17,32,128]{2,1,0:T(8,128)(2,1)S(1)}, u32[]{:S(2)}, u32[]{:S(2)}) collective-permute-start(bf16[17,32,128]{2,1,0:T(8,128)(2,1)S(1)} %get-tuple-element.48), channel_id=1, source_target_pairs={{0,3},{1,2},{2,1},{3,0},{4,7},{5,6},{6,5},{7,4},{8,11},{9,10},{10,... | collective-permute-start | bytes 417800 | tf_op jit(solution)/shard_map/ppermute | solution.py:561
  30.3 2.3 %far_parts.1 = (bf16[4,128,128]{2,1,0:T(8,128)(2,1)S(1)}, bf16[4,128,128]{2,1,0:T(8,128)(2,1)S(1)}, bf16[4,128,128]{2,1,0:T(8,128)(2,1)S(1)}, bf16[4,128,128]{2,...) custom-call(bf16[4,128,128]{2,1,0:T(8,128)(2,1)S(1)} %get-tuple-element.40.refs_0_, ...), custom_call_target="tpu_custom_call" | custom-call | flops 1 | bytes 1 | tf_op jit(solution)/shard_map/far_parts/pallas_call | solution.py:541
  32.7 0.3 collective-permute-start.11
  33.0 3.4 %collective-permute-start.16 = (bf16[17,32,128]{2,1,0:T(8,128)(2,1)S(1)}, bf16[17,32,128]{2,1,0:T(8,128)(2,1)S(1)}, u32[]{:S(2)}, u32[]{:S(2)}) collective-permute-start(bf16[17,32,128]{2,1,0:T(8,128)(2,1)S(1)} %get-tuple-element.59), channel_id=1, source_target_pairs={{0,2},{1,3},{2,0},{3,1},{4,6},{5,7},{6,4},{7,5},{8,10},{9,11},{10,... | collective-permute-start | bytes 417800 | tf_op jit(solution)/shard_map/ppermute | solution.py:561
  36.4 0.2 collective-permute-done.10.refs_6_.refs_0_
  36.7 0.1 far_sum.1
  36.8 1.8 %collective-permute-start.13 = (bf16[4,128,128]{2,1,0:T(8,128)(2,1)S(1)}, bf16[4,128,128]{2,1,0:T(8,128)(2,1)S(1)}, u32[]{:S(2)}, u32[]{:S(2)}) collective-permute-start(bf16[4,128,128]{2,1,0:T(8,128)(2,1)S(1)} %get-tuple-element.56), channel_id=1, source_target_pairs={{0,24},{4,28},{8,16},{12,20},{16,8},{20,12},{24,0},{28,4},{1,25},{... | collective-permute-start | bytes 393224 | tf_op jit(solution)/shard_map/ppermute | solution.py:561
  38.6 0.8 %collective-permute-start.14 = (bf16[4,128,128]{2,1,0:T(8,128)(2,1)S(1)}, bf16[4,128,128]{2,1,0:T(8,128)(2,1)S(1)}, u32[]{:S(2)}, u32[]{:S(2)}) collective-permute-start(bf16[4,128,128]{2,1,0:T(8,128)(2,1)S(1)} %get-tuple-element.57), channel_id=1, source_target_pairs={{0,16},{4,20},{8,24},{12,28},{16,0},{20,4},{24,8},{28,12},{1,17},{... | collective-permute-start | bytes 393224 | tf_op jit(solution)/shard_map/ppermute | solution.py:561
  39.4 0.9 %collective-permute-start.15 = (bf16[4,128,128]{2,1,0:T(8,128)(2,1)S(1)}, bf16[4,128,128]{2,1,0:T(8,128)(2,1)S(1)}, u32[]{:S(2)}, u32[]{:S(2)}) collective-permute-start(bf16[4,128,128]{2,1,0:T(8,128)(2,1)S(1)} %get-tuple-element.58), channel_id=1, source_target_pairs={{0,8},{4,12},{8,0},{12,4},{16,24},{20,28},{24,16},{28,20},{1,9},{5... | collective-permute-start | bytes 393224 | tf_op jit(solution)/shard_map/ppermute | solution.py:561
  40.3 2.0 %collective-permute-done.11.refs_7_ = bf16[17,32,128]{2,1,0:T(8,128)(2,1)S(1)} collective-permute-done((bf16[17,32,128]{2,1,0:T(8,128)(2,1)S(1)}, bf16[17,32,128]{2,1,0:T(8,128)(2,1)S(1)}, u32[]{:S(2)}, u32[]{:S(2)}) %collective-permute-start.11) | collective-permute-done | bytes 139296 | tf_op jit(solution)/shard_map/ppermute | solution.py:561
  42.3 1.4 %near_early.1.refs_5_.early_ref = f32[4,12,128,128]{3,2,1,0:T(8,128)S(1)} custom-call(bf16[128,2048]{1,0:T(8,128)(2,1)S(1)} %copy-done, bf16[128,2048]{1,0:T(8,128)(2,1)S(1)} %copy-done.1, bf16[128,2048]{1,0:T(8,128)(2,1)S(1)} %copy-done.2, bf16[128,2048]{1,0:T(8,128)(2,1)S(1)} %copy-done.3, f32[32,128]{1,0:T(8,128)S(1)} %get-tuple-element.35.refs_0_.refs_4_, ...), custom_call_target="tpu_custom_call" | custom-call | flops 2000000000 | bytes 5709824 | tf_op jit(solution)/shard_map/near_early/pallas_call | solution.py:541
  43.8 1.9 %final_others.1 = (bf16[128,2048]{1,0:T(8,128)(2,1)}, bf16[128,2048]{1,0:T(8,128)(2,1)}, bf16[128,2048]{1,0:T(8,128)(2,1)}, bf16[128,2048]{1,0:T(8,128)(2,1)}) custom-call(bf16[128,2048]{1,0:T(8,128)(2,1)S(1)} %copy-done, bf16[128,2048]{1,0:T(8,128)(2,1)S(1)} %copy-done.1, bf16[128,2048]{1,0:T(8,128)(2,1)S(1)} %copy-done.2, bf16[128,2048]{1,0:T(8,128)(2,1)S(1)} %copy-done.3, ...), custom_call_target="tpu_custom_call" | custom-call | flops 1000000000 | bytes 7774208 | tf_op jit(solution)/shard_map/final_others/pallas_call | solution.py:541
  45.8 1.1 %final_own.1 = (bf16[128,2048]{1,0:T(8,128)(2,1)}, bf16[128,2048]{1,0:T(8,128)(2,1)}, bf16[128,2048]{1,0:T(8,128)(2,1)}, bf16[128,2048]{1,0:T(8,128)(2,1)}) custom-call(f32[4,12,128,128]{3,2,1,0:T(8,128)S(1)} %near_early.1.refs_5_.early_ref, ...), custom_call_target="tpu_custom_call", output_to_operand_aliasing={{0}: (6, {}), {1}: (7, {}), {2}: (8, {}), {3}: (9, {})} | custom-call | flops 16777216 | bytes 8003584 | tf_op jit(solution)/shard_map/final_own/pallas_call | solution.py:541
  (27 shorter events, 0.2 us)
Async XLA Ops:
  2.3 11.4 %collective-permute-start = (bf16[17,32,128]{2,1,0:T(8,128)(2,1)S(1)}, bf16[17,32,128]{2,1,0:T(8,128)(2,1)S(1)}, u32[]{:S(2)}, u32[]{:S(2)}) collective-permute-start(bf16[17,32,128]{2,1,0:T(8,128)(2,1)S(1)} %get-tuple-element.37), channel_id=1, source_target_pairs={{0,3},{1,2},{2,1},{3,0},{4,7},{5,6},{6,5},{7,4},{8,11},{9,10},{10,... | collective-permute-start | bytes 417800 | tf_op jit(solution)/shard_map/ppermute | solution.py:561
  10.2 5.5 %collective-permute-start.3 = (bf16[4,128,128]{2,1,0:T(8,128)(2,1)S(1)}, bf16[4,128,128]{2,1,0:T(8,128)(2,1)S(1)}, u32[]{:S(2)}, u32[]{:S(2)}) collective-permute-start(bf16[4,128,128]{2,1,0:T(8,128)(2,1)S(1)} %get-tuple-element.41), channel_id=1, source_target_pairs={{0,8},{4,12},{8,0},{12,4},{16,24},{20,28},{24,16},{28,20},{1,9},{5... | collective-permute-start | bytes 393224 | tf_op jit(solution)/shard_map/ppermute | solution.py:561
  11.7 7.8 %collective-permute-start.4 = (bf16[4,128,128]{2,1,0:T(8,128)(2,1)S(1)}, bf16[4,128,128]{2,1,0:T(8,128)(2,1)S(1)}, u32[]{:S(2)}, u32[]{:S(2)}) collective-permute-start(bf16[4,128,128]{2,1,0:T(8,128)(2,1)S(1)} %get-tuple-element.42), channel_id=1, source_target_pairs={{0,16},{4,20},{8,24},{12,28},{16,0},{20,4},{24,8},{28,12},{1,17},{... | collective-permute-start | bytes 393224 | tf_op jit(solution)/shard_map/ppermute | solution.py:561
  13.3 6.3 %collective-permute-start.5 = (bf16[4,128,128]{2,1,0:T(8,128)(2,1)S(1)}, bf16[4,128,128]{2,1,0:T(8,128)(2,1)S(1)}, u32[]{:S(2)}, u32[]{:S(2)}) collective-permute-start(bf16[4,128,128]{2,1,0:T(8,128)(2,1)S(1)} %get-tuple-element.43), channel_id=1, source_target_pairs={{0,24},{4,28},{8,16},{12,20},{16,8},{20,12},{24,0},{28,4},{1,25},{... | collective-permute-start | bytes 393224 | tf_op jit(solution)/shard_map/ppermute | solution.py:561
  13.7 8.5 %collective-permute-start.1 = (bf16[17,32,128]{2,1,0:T(8,128)(2,1)S(1)}, bf16[17,32,128]{2,1,0:T(8,128)(2,1)S(1)}, u32[]{:S(2)}, u32[]{:S(2)}) collective-permute-start(bf16[17,32,128]{2,1,0:T(8,128)(2,1)S(1)} %get-tuple-element.38), channel_id=1, source_target_pairs={{0,2},{1,3},{2,0},{3,1},{4,6},{5,7},{6,4},{7,5},{8,10},{9,11},{10,... | collective-permute-start | bytes 417800 | tf_op jit(solution)/shard_map/ppermute | solution.py:561
  13.7 8.5 %collective-permute-start.2 = (bf16[17,32,128]{2,1,0:T(8,128)(2,1)S(1)}, bf16[17,32,128]{2,1,0:T(8,128)(2,1)S(1)}, u32[]{:S(2)}, u32[]{:S(2)}) collective-permute-start(bf16[17,32,128]{2,1,0:T(8,128)(2,1)S(1)} %get-tuple-element.39), channel_id=1, source_target_pairs={{0,1},{1,0},{2,3},{3,2},{4,5},{5,4},{6,7},{7,6},{8,9},{9,8},{10,11... | collective-permute-start | bytes 417800 | tf_op jit(solution)/shard_map/ppermute | solution.py:561
  19.5 1.6 %collective-permute-start.6 = (bf16[4,2,128,128]{3,2,1,0:T(8,128)(2,1)S(1)}, bf16[4,2,128,128]{3,2,1,0:T(8,128)(2,1)S(1)}, u32[]{:S(2)}, u32[]{:S(2)}) collective-permute-start(bf16[4,2,128,128]{3,2,1,0:T(8,128)(2,1)S(1)} %pack.1), channel_id=1, source_target_pairs={{0,4},{4,0},{8,12},{12,8},{16,20},{20,16},{24,28},{28,24},{1,5},{5... | collective-permute-start | bytes 786440 | tf_op jit(solution)/shard_map/ppermute | solution.py:561
  22.8 4.6 %collective-permute-start.9 = (f32[16,128]{1,0:T(8,128)S(1)}, f32[16,128]{1,0:T(8,128)S(1)}, u32[]{:S(2)}, u32[]{:S(2)}) collective-permute-start(f32[16,128]{1,0:T(8,128)S(1)} %get-tuple-element.46.refs_6_.refs_8_.refs_5_), channel_id=1, source_target_pairs={{0,24},{4,28},{8,16},{12,20},{16,8},{20,12},{24,0},{28,4},{1,25},{... | collective-permute-start | bytes 24584 | tf_op jit(solution)/shard_map/ppermute | solution.py:561
  24.1 3.7 %collective-permute-start.8 = (f32[16,128]{1,0:T(8,128)S(1)}, f32[16,128]{1,0:T(8,128)S(1)}, u32[]{:S(2)}, u32[]{:S(2)}) collective-permute-start(f32[16,128]{1,0:T(8,128)S(1)} %get-tuple-element.46.refs_6_.refs_8_.refs_5_), channel_id=1, source_target_pairs={{0,16},{4,20},{8,24},{12,28},{16,0},{20,4},{24,8},{28,12},{1,17},{... | collective-permute-start | bytes 24584 | tf_op jit(solution)/shard_map/ppermute | solution.py:561
  25.3 3.7 %collective-permute-start.7 = (f32[16,128]{1,0:T(8,128)S(1)}, f32[16,128]{1,0:T(8,128)S(1)}, u32[]{:S(2)}, u32[]{:S(2)}) collective-permute-start(f32[16,128]{1,0:T(8,128)S(1)} %get-tuple-element.46.refs_6_.refs_8_.refs_5_), channel_id=1, source_target_pairs={{0,8},{4,12},{8,0},{12,4},{16,24},{20,28},{24,16},{28,20},{1,9},{5... | collective-permute-start | bytes 24584 | tf_op jit(solution)/shard_map/ppermute | solution.py:561
  29.6 7.1 %collective-permute-start.10 = (bf16[17,32,128]{2,1,0:T(8,128)(2,1)S(1)}, bf16[17,32,128]{2,1,0:T(8,128)(2,1)S(1)}, u32[]{:S(2)}, u32[]{:S(2)}) collective-permute-start(bf16[17,32,128]{2,1,0:T(8,128)(2,1)S(1)} %get-tuple-element.48), channel_id=1, source_target_pairs={{0,3},{1,2},{2,1},{3,0},{4,7},{5,6},{6,5},{7,4},{8,11},{9,10},{10,... | collective-permute-start | bytes 417800 | tf_op jit(solution)/shard_map/ppermute | solution.py:561
  32.6 4.0 %collective-permute-start.12 = (bf16[4,2,128,128]{3,2,1,0:T(8,128)(2,1)S(1)}, bf16[4,2,128,128]{3,2,1,0:T(8,128)(2,1)S(1)}, u32[]{:S(2)}, u32[]{:S(2)}) collective-permute-start(bf16[4,2,128,128]{3,2,1,0:T(8,128)(2,1)S(1)} %get-tuple-element.54), channel_id=1, source_target_pairs={{0,4},{4,0},{8,12},{12,8},{16,20},{20,16},{24,28},{28,24},{1,5},{5... | collective-permute-start | bytes 786440 | tf_op jit(solution)/shard_map/ppermute | solution.py:561
  32.7 9.6 %collective-permute-start.11 = (bf16[17,32,128]{2,1,0:T(8,128)(2,1)S(1)}, bf16[17,32,128]{2,1,0:T(8,128)(2,1)S(1)}, u32[]{:S(2)}, u32[]{:S(2)}) collective-permute-start(bf16[17,32,128]{2,1,0:T(8,128)(2,1)S(1)} %get-tuple-element.49), channel_id=1, source_target_pairs={{0,1},{1,0},{2,3},{3,2},{4,5},{5,4},{6,7},{7,6},{8,9},{9,8},{10,11... | collective-permute-start | bytes 417800 | tf_op jit(solution)/shard_map/ppermute | solution.py:561
  33.0 10.7 %collective-permute-start.16 = (bf16[17,32,128]{2,1,0:T(8,128)(2,1)S(1)}, bf16[17,32,128]{2,1,0:T(8,128)(2,1)S(1)}, u32[]{:S(2)}, u32[]{:S(2)}) collective-permute-start(bf16[17,32,128]{2,1,0:T(8,128)(2,1)S(1)} %get-tuple-element.59), channel_id=1, source_target_pairs={{0,2},{1,3},{2,0},{3,1},{4,6},{5,7},{6,4},{7,5},{8,10},{9,11},{10,... | collective-permute-start | bytes 417800 | tf_op jit(solution)/shard_map/ppermute | solution.py:561
  36.7 5.6 %copy-start = (bf16[128,2048]{1,0:T(8,128)(2,1)S(1)}, bf16[128,2048]{1,0:T(8,128)(2,1)}, u32[]{:S(2)}) copy-start(bf16[128,2048]{1,0:T(8,128)(2,1)} %refs_0_.7) | copy-start | bytes 1572868
  36.7 5.6 %copy-start.1 = (bf16[128,2048]{1,0:T(8,128)(2,1)S(1)}, bf16[128,2048]{1,0:T(8,128)(2,1)}, u32[]{:S(2)}) copy-start(bf16[128,2048]{1,0:T(8,128)(2,1)} %refs_1_.7) | copy-start | bytes 1572868
  36.7 5.6 %copy-start.2 = (bf16[128,2048]{1,0:T(8,128)(2,1)S(1)}, bf16[128,2048]{1,0:T(8,128)(2,1)}, u32[]{:S(2)}) copy-start(bf16[128,2048]{1,0:T(8,128)(2,1)} %refs_2_.7) | copy-start | bytes 1572868
  36.7 5.6 %copy-start.3 = (bf16[128,2048]{1,0:T(8,128)(2,1)S(1)}, bf16[128,2048]{1,0:T(8,128)(2,1)}, u32[]{:S(2)}) copy-start(bf16[128,2048]{1,0:T(8,128)(2,1)} %refs_3_.7) | copy-start | bytes 1572868
  36.8 8.9 %collective-permute-start.13 = (bf16[4,128,128]{2,1,0:T(8,128)(2,1)S(1)}, bf16[4,128,128]{2,1,0:T(8,128)(2,1)S(1)}, u32[]{:S(2)}, u32[]{:S(2)}) collective-permute-start(bf16[4,128,128]{2,1,0:T(8,128)(2,1)S(1)} %get-tuple-element.56), channel_id=1, source_target_pairs={{0,24},{4,28},{8,16},{12,20},{16,8},{20,12},{24,0},{28,4},{1,25},{... | collective-permute-start | bytes 393224 | tf_op jit(solution)/shard_map/ppermute | solution.py:561
  38.6 7.1 %collective-permute-start.14 = (bf16[4,128,128]{2,1,0:T(8,128)(2,1)S(1)}, bf16[4,128,128]{2,1,0:T(8,128)(2,1)S(1)}, u32[]{:S(2)}, u32[]{:S(2)}) collective-permute-start(bf16[4,128,128]{2,1,0:T(8,128)(2,1)S(1)} %get-tuple-element.57), channel_id=1, source_target_pairs={{0,16},{4,20},{8,24},{12,28},{16,0},{20,4},{24,8},{28,12},{1,17},{... | collective-permute-start | bytes 393224 | tf_op jit(solution)/shard_map/ppermute | solution.py:561
  39.4 6.3 %collective-permute-start.15 = (bf16[4,128,128]{2,1,0:T(8,128)(2,1)S(1)}, bf16[4,128,128]{2,1,0:T(8,128)(2,1)S(1)}, u32[]{:S(2)}, u32[]{:S(2)}) collective-permute-start(bf16[4,128,128]{2,1,0:T(8,128)(2,1)S(1)} %get-tuple-element.58), channel_id=1, source_target_pairs={{0,8},{4,12},{8,0},{12,4},{16,24},{20,28},{24,16},{28,20},{1,9},{5... | collective-permute-start | bytes 393224 | tf_op jit(solution)/shard_map/ppermute | solution.py:561

commit v17 on v16

--- a/solution.py
+++ b/solution.py
@@ -224,7 +224,7 @@
 
 
 def far_stats_kernel(slots, *refs):
-    fulls, sibs, stats_ref = refs[:slots], refs[slots:-2], refs[-1]
+    fulls, sibs, stats_ref = in_back(refs[:slots]), refs[slots:-2], refs[-1]
     keys, values = far_keys(fulls, sibs, 0), far_keys(fulls, sibs, 1)
     for m in range(slots):
         ((e, d),) = level_stats([(keys, values, fulls[m][2], fulls[m][3])])
@@ -314,7 +314,7 @@
 
 
 def far_parts_kernel(slots, width, *refs):
-    fulls, refs = refs[:slots], refs[slots:]
+    fulls, refs = in_back(refs[:slots]), refs[slots:]
     sibs, refs = refs[: width - 1], refs[width - 1 :]
     xmsgs, refs = refs[:slots], refs[slots + 1 :]
     outs, refs = refs[:slots], refs[slots:]
@@ -636,7 +636,7 @@
         [stats(2 * slots)],
         [],
         1,
-        fulls + sibs + [settled],
+        [*in_back(fulls), *sibs, settled],
     )
     xmsg, middle, columns = call(
         bind(middle_stats_kernel, n_i, slots),
@@ -663,7 +663,7 @@
         [full] * slots + [half] * (width - 1),
         [pltpu.VMEM((n_o * rows, slots * rows), BF16)] * 2,
         unit * n_o * slots * 6,
-        fulls + sibs + xmsgs + [midparts[0]],
+        [*in_back(fulls), *sibs, *xmsgs, midparts[0]],
         cheap=True,
     )
     sibparts = [swap(x, "seqo", n_o, part + 1) for part, x in enumerate(farparts[slots:])]

time: 47.1 us -> 47.1 us (level)
  transfers between devices with their start and end apart: 17 -> 17, of which waited for: 8 -> 9; matrix products, arithmetic and copies ran while one was open for 0% -> 0% of each run, Pallas kernels for 21% -> 21%
where the time goes in v17:
time: 47.1 us; the launch traced here: 46.9 us
  starting transfers between devices  21 us (45%)
  Pallas kernels  13.6 us (29%)
  waiting for transfers between devices  11.5 us (24%)
  between operations  0.82 us (2%)
    ppermute x17, starting transfers between devices, swap(): return lax.ppermute(x, axis, [(i, i ^ mask) for i in range(n)])  21 us
    pallas_call x17, Pallas kernels, call(): pl.pallas_call(kernel, out_shape=tuple(outs), in_specs=[pl.BlockSpec(memo...  13.6 us
    ppermute x17, waiting for transfers between devices, swap(): return lax.ppermute(x, axis, [(i, i ^ mask) for i in range(n)])  11.5 us
  transfers between devices with their start and end apart: 17, of which 9 were waited for; matrix products, arithmetic and copies ran while one was open for 0% of the time, Pallas kernels for 21%

profile of v17, /device:TPU:0, one launch (start us, length us, event | category | flops | bytes accessed | tf_op | source)
XLA Modules:
  0.0 46.9 jit_solution(5627586723698670804)
XLA Ops:
  0.6 1.7 %pick_first.1 = (bf16[17,32,128]{2,1,0:T(8,128)(2,1)S(1)}, f32[32,128]{1,0:T(8,128)S(1)}) custom-call(bf16[128,2048]{1,0:T(8,128)(2,1)} %refs_0_.7, bf16[128,2048]{1,0:T(8,128)(2,1)} %refs_1_.7, bf16[128,2048]{1,0:T(8,128)(2,1)} %refs_2_.7, bf16[128,2048]{1,0:T(8,128)(2,1)} %refs_3_.7), custom_call_target="tpu_custom_call" | custom-call | flops 33554432 | bytes 2252800 | tf_op jit(solution)/shard_map/pick_first/pallas_call | solution.py:541
  2.3 5.1 %collective-permute-start = (bf16[17,32,128]{2,1,0:T(8,128)(2,1)S(1)}, bf16[17,32,128]{2,1,0:T(8,128)(2,1)S(1)}, u32[]{:S(2)}, u32[]{:S(2)}) collective-permute-start(bf16[17,32,128]{2,1,0:T(8,128)(2,1)S(1)} %get-tuple-element.37), channel_id=1, source_target_pairs={{0,3},{1,2},{2,1},{3,0},{4,7},{5,6},{6,5},{7,4},{8,11},{9,10},{10,... | collective-permute-start | bytes 417800 | tf_op jit(solution)/shard_map/ppermute | solution.py:561
  7.4 2.7 %pick_rest.1 = (bf16[17,32,128]{2,1,0:T(8,128)(2,1)S(1)}, bf16[17,32,128]{2,1,0:T(8,128)(2,1)S(1)}, bf16[17,32,128]{2,1,0:T(8,128)(2,1)S(1)}, bf16[4,128,128]{2,...) custom-call(bf16[128,2048]{1,0:T(8,128)(2,1)} %refs_0_.7, ...), custom_call_target="tpu_custom_call" | custom-call | flops 134217728 | bytes 3072000 | tf_op jit(solution)/shard_map/pick_rest/pallas_call | solution.py:541
  10.2 2.5 %collective-permute-start.3 = (bf16[4,128,128]{2,1,0:T(8,128)(2,1)S(1)}, bf16[4,128,128]{2,1,0:T(8,128)(2,1)S(1)}, u32[]{:S(2)}, u32[]{:S(2)}) collective-permute-start(bf16[4,128,128]{2,1,0:T(8,128)(2,1)S(1)} %get-tuple-element.41), channel_id=1, source_target_pairs={{0,24},{4,28},{8,16},{12,20},{16,8},{20,12},{24,0},{28,4},{1,25},{... | collective-permute-start | bytes 393224 | tf_op jit(solution)/shard_map/ppermute | solution.py:561
  12.7 0.5 %collective-permute-start.4 = (bf16[4,128,128]{2,1,0:T(8,128)(2,1)S(1)}, bf16[4,128,128]{2,1,0:T(8,128)(2,1)S(1)}, u32[]{:S(2)}, u32[]{:S(2)}) collective-permute-start(bf16[4,128,128]{2,1,0:T(8,128)(2,1)S(1)} %get-tuple-element.42), channel_id=1, source_target_pairs={{0,16},{4,20},{8,24},{12,28},{16,0},{20,4},{24,8},{28,12},{1,17},{... | collective-permute-start | bytes 393224 | tf_op jit(solution)/shard_map/ppermute | solution.py:561
  13.2 0.5 %collective-permute-start.5 = (bf16[4,128,128]{2,1,0:T(8,128)(2,1)S(1)}, bf16[4,128,128]{2,1,0:T(8,128)(2,1)S(1)}, u32[]{:S(2)}, u32[]{:S(2)}) collective-permute-start(bf16[4,128,128]{2,1,0:T(8,128)(2,1)S(1)} %get-tuple-element.43), channel_id=1, source_target_pairs={{0,8},{4,12},{8,0},{12,4},{16,24},{20,28},{24,16},{28,20},{1,9},{5... | collective-permute-start | bytes 393224 | tf_op jit(solution)/shard_map/ppermute | solution.py:561
  13.7 0.6 %collective-permute-start.2 = (bf16[17,32,128]{2,1,0:T(8,128)(2,1)S(1)}, bf16[17,32,128]{2,1,0:T(8,128)(2,1)S(1)}, u32[]{:S(2)}, u32[]{:S(2)}) collective-permute-start(bf16[17,32,128]{2,1,0:T(8,128)(2,1)S(1)} %get-tuple-element.39), channel_id=1, source_target_pairs={{0,1},{1,0},{2,3},{3,2},{4,5},{5,4},{6,7},{7,6},{8,9},{9,8},{10,11... | collective-permute-start | bytes 417800 | tf_op jit(solution)/shard_map/ppermute | solution.py:561
  14.3 2.3 %collective-permute-done.3.refs_1_ = bf16[4,128,128]{2,1,0:T(8,128)(2,1)S(1)} collective-permute-done((bf16[4,128,128]{2,1,0:T(8,128)(2,1)S(1)}, bf16[4,128,128]{2,1,0:T(8,128)(2,1)S(1)}, u32[]{:S(2)}, u32[]{:S(2)}) %collective-permute-start.3) | collective-permute-done | bytes 131104 | tf_op jit(solution)/shard_map/ppermute | solution.py:561
  16.6 2.3 %collective-permute-done.4.refs_2_ = bf16[4,128,128]{2,1,0:T(8,128)(2,1)S(1)} collective-permute-done((bf16[4,128,128]{2,1,0:T(8,128)(2,1)S(1)}, bf16[4,128,128]{2,1,0:T(8,128)(2,1)S(1)}, u32[]{:S(2)}, u32[]{:S(2)}) %collective-permute-start.4) | collective-permute-done | bytes 131104 | tf_op jit(solution)/shard_map/ppermute | solution.py:561
  19.1 1.5 %collective-permute-done.6.refs_4_ = bf16[4,2,128,128]{3,2,1,0:T(8,128)(2,1)S(1)} collective-permute-done((bf16[4,2,128,128]{3,2,1,0:T(8,128)(2,1)S(1)}, bf16[4,2,128,128]{3,2,1,0:T(8,128)(2,1)S(1)}, u32[]{:S(2)}, u32[]{:S(2)}) %collective-permute-start.6) | collective-permute-done | bytes 262176 | tf_op jit(solution)/shard_map/ppermute | solution.py:561
  20.6 1.1 %far_stats.1.refs_5_ = f32[8,128]{1,0:T(8,128)S(1)} custom-call(bf16[4,128,128]{2,1,0:T(8,128)(2,1)S(1)} %get-tuple-element.40.refs_0_, bf16[4,128,128]{2,1,0:T(8,128)(2,1)S(1)} %collective-permute-done.3.refs_1_, bf16[4,128,128]{2,1,0:T(8,128)(2,1)S(1)} %collective-permute-done.4.refs_2_, bf16[4,128,128]{2,1,0:T(8,128)(2,1)S(1)} %collective-permute-done.5.refs_3_, ...), custom_call_target="tpu_custom_call" | custom-call | flops 1 | bytes 794624 | tf_op jit(solution)/shard_map/far_stats/pallas_call | solution.py:541
  21.8 0.5 %middle_stats.1 = (f32[16,128]{1,0:T(8,128)S(1)}, f32[8,128]{1,0:T(8,128)S(1)}, f32[128,128]{1,0:T(8,128)S(1)}) custom-call(bf16[17,32,128]{2,1,0:T(8,128)(2,1)S(1)} %get-tuple-element.36.refs_0_, bf16[17,32,128]{2,1,0:T(8,128)(2,1)S(1)} %collective-permute-done.refs_0_.refs_1_, bf16[17,32,128]{2,1,0:T(8,128)(2,1)S(1)} %collective-permute-done.1.refs_2_, ...), custom_call_target="tpu_custom_call" | custom-call | flops 33554432 | bytes 655360 | tf_op jit(solution)/shard_map/middle_stats/pallas_call | solution.py:541
  22.3 1.8 %collective-permute-start.9 = (f32[16,128]{1,0:T(8,128)S(1)}, f32[16,128]{1,0:T(8,128)S(1)}, u32[]{:S(2)}, u32[]{:S(2)}) collective-permute-start(f32[16,128]{1,0:T(8,128)S(1)} %get-tuple-element.46.refs_6_.refs_8_.refs_5_), channel_id=1, source_target_pairs={{0,24},{4,28},{8,16},{12,20},{16,8},{20,12},{24,0},{28,4},{1,25},{... | collective-permute-start | bytes 24584 | tf_op jit(solution)/shard_map/ppermute | solution.py:561
  24.0 1.3 %collective-permute-start.8 = (f32[16,128]{1,0:T(8,128)S(1)}, f32[16,128]{1,0:T(8,128)S(1)}, u32[]{:S(2)}, u32[]{:S(2)}) collective-permute-start(f32[16,128]{1,0:T(8,128)S(1)} %get-tuple-element.46.refs_6_.refs_8_.refs_5_), channel_id=1, source_target_pairs={{0,16},{4,20},{8,24},{12,28},{16,0},{20,4},{24,8},{28,12},{1,17},{... | collective-permute-start | bytes 24584 | tf_op jit(solution)/shard_map/ppermute | solution.py:561
  25.3 0.5 %collective-permute-start.7 = (f32[16,128]{1,0:T(8,128)S(1)}, f32[16,128]{1,0:T(8,128)S(1)}, u32[]{:S(2)}, u32[]{:S(2)}) collective-permute-start(f32[16,128]{1,0:T(8,128)S(1)} %get-tuple-element.46.refs_6_.refs_8_.refs_5_), channel_id=1, source_target_pairs={{0,8},{4,12},{8,0},{12,4},{16,24},{20,28},{24,16},{28,20},{1,9},{5... | collective-permute-start | bytes 24584 | tf_op jit(solution)/shard_map/ppermute | solution.py:561
  25.8 1.1 %collective-permute-done.9.refs_9_.refs_11_.refs_8_ = f32[16,128]{1,0:T(8,128)S(1)} collective-permute-done((f32[16,128]{1,0:T(8,128)S(1)}, f32[16,128]{1,0:T(8,128)S(1)}, u32[]{:S(2)}, u32[]{:S(2)}) %collective-permute-start.9) | collective-permute-done | bytes 8224 | tf_op jit(solution)/shard_map/ppermute | solution.py:561
  26.9 0.8 %collective-permute-done.8.refs_8_.refs_10_.refs_7_ = f32[16,128]{1,0:T(8,128)S(1)} collective-permute-done((f32[16,128]{1,0:T(8,128)S(1)}, f32[16,128]{1,0:T(8,128)S(1)}, u32[]{:S(2)}, u32[]{:S(2)}) %collective-permute-start.8) | collective-permute-done | bytes 8224 | tf_op jit(solution)/shard_map/ppermute | solution.py:561
  27.7 1.3 %collective-permute-done.7.refs_7_.refs_9_.refs_6_ = f32[16,128]{1,0:T(8,128)S(1)} collective-permute-done((f32[16,128]{1,0:T(8,128)S(1)}, f32[16,128]{1,0:T(8,128)S(1)}, u32[]{:S(2)}, u32[]{:S(2)}) %collective-permute-start.7) | collective-permute-done | bytes 8224 | tf_op jit(solution)/shard_map/ppermute | solution.py:561
  29.0 0.6 %middle_parts.1 = (bf16[17,32,128]{2,1,0:T(8,128)(2,1)S(1)}, bf16[17,32,128]{2,1,0:T(8,128)(2,1)S(1)}, bf16[17,32,128]{2,1,0:T(8,128)(2,1)S(1)}, bf16[17,32,128]{2,1,0:T(8,128)(2,1)S(1)}) custom-call(bf16[17,32,128]{2,1,0:T(8,128)(2,1)S(1)} %get-tuple-element.36.refs_0_, bf16[17,32,128]{2,1,0:T(8,128)(2,1)S(1)} %collective-permute-done.refs_0_.refs_1_, ...), custom_call_target="tpu_custom_call" | custom-call | flops 100663296 | bytes 1216512 | tf_op jit(solution)/shard_map/middle_parts/pallas_call | solution.py:541
  29.6 0.8 %collective-permute-start.10 = (bf16[17,32,128]{2,1,0:T(8,128)(2,1)S(1)}, bf16[17,32,128]{2,1,0:T(8,128)(2,1)S(1)}, u32[]{:S(2)}, u32[]{:S(2)}) collective-permute-start(bf16[17,32,128]{2,1,0:T(8,128)(2,1)S(1)} %get-tuple-element.48), channel_id=1, source_target_pairs={{0,3},{1,2},{2,1},{3,0},{4,7},{5,6},{6,5},{7,4},{8,11},{9,10},{10,... | collective-permute-start | bytes 417800 | tf_op jit(solution)/shard_map/ppermute | solution.py:561
  30.3 2.3 %far_parts.1 = (bf16[4,128,128]{2,1,0:T(8,128)(2,1)S(1)}, bf16[4,128,128]{2,1,0:T(8,128)(2,1)S(1)}, bf16[4,128,128]{2,1,0:T(8,128)(2,1)S(1)}, bf16[4,128,128]{2,...) custom-call(bf16[4,128,128]{2,1,0:T(8,128)(2,1)S(1)} %get-tuple-element.40.refs_0_, ...), custom_call_target="tpu_custom_call" | custom-call | flops 1 | bytes 1 | tf_op jit(solution)/shard_map/far_parts/pallas_call | solution.py:541
  32.7 0.3 collective-permute-start.11
  33.0 3.4 %collective-permute-start.16 = (bf16[17,32,128]{2,1,0:T(8,128)(2,1)S(1)}, bf16[17,32,128]{2,1,0:T(8,128)(2,1)S(1)}, u32[]{:S(2)}, u32[]{:S(2)}) collective-permute-start(bf16[17,32,128]{2,1,0:T(8,128)(2,1)S(1)} %get-tuple-element.59), channel_id=1, source_target_pairs={{0,2},{1,3},{2,0},{3,1},{4,6},{5,7},{6,4},{7,5},{8,10},{9,11},{10,... | collective-permute-start | bytes 417800 | tf_op jit(solution)/shard_map/ppermute | solution.py:561
  36.5 0.2 collective-permute-done.10.refs_6_.refs_0_
  36.8 0.1 far_sum.1
  36.8 1.4 %collective-permute-start.13 = (bf16[4,128,128]{2,1,0:T(8,128)(2,1)S(1)}, bf16[4,128,128]{2,1,0:T(8,128)(2,1)S(1)}, u32[]{:S(2)}, u32[]{:S(2)}) collective-permute-start(bf16[4,128,128]{2,1,0:T(8,128)(2,1)S(1)} %get-tuple-element.56), channel_id=1, source_target_pairs={{0,24},{4,28},{8,16},{12,20},{16,8},{20,12},{24,0},{28,4},{1,25},{... | collective-permute-start | bytes 393224 | tf_op jit(solution)/shard_map/ppermute | solution.py:561
  38.3 0.6 %collective-permute-start.14 = (bf16[4,128,128]{2,1,0:T(8,128)(2,1)S(1)}, bf16[4,128,128]{2,1,0:T(8,128)(2,1)S(1)}, u32[]{:S(2)}, u32[]{:S(2)}) collective-permute-start(bf16[4,128,128]{2,1,0:T(8,128)(2,1)S(1)} %get-tuple-element.57), channel_id=1, source_target_pairs={{0,16},{4,20},{8,24},{12,28},{16,0},{20,4},{24,8},{28,12},{1,17},{... | collective-permute-start | bytes 393224 | tf_op jit(solution)/shard_map/ppermute | solution.py:561
  38.8 1.5 %collective-permute-start.15 = (bf16[4,128,128]{2,1,0:T(8,128)(2,1)S(1)}, bf16[4,128,128]{2,1,0:T(8,128)(2,1)S(1)}, u32[]{:S(2)}, u32[]{:S(2)}) collective-permute-start(bf16[4,128,128]{2,1,0:T(8,128)(2,1)S(1)} %get-tuple-element.58), channel_id=1, source_target_pairs={{0,8},{4,12},{8,0},{12,4},{16,24},{20,28},{24,16},{28,20},{1,9},{5... | collective-permute-start | bytes 393224 | tf_op jit(solution)/shard_map/ppermute | solution.py:561
  40.4 1.9 %collective-permute-done.11.refs_7_ = bf16[17,32,128]{2,1,0:T(8,128)(2,1)S(1)} collective-permute-done((bf16[17,32,128]{2,1,0:T(8,128)(2,1)S(1)}, bf16[17,32,128]{2,1,0:T(8,128)(2,1)S(1)}, u32[]{:S(2)}, u32[]{:S(2)}) %collective-permute-start.11) | collective-permute-done | bytes 139296 | tf_op jit(solution)/shard_map/ppermute | solution.py:561
  42.4 1.4 %near_early.1.refs_5_.early_ref = f32[4,12,128,128]{3,2,1,0:T(8,128)S(1)} custom-call(bf16[128,2048]{1,0:T(8,128)(2,1)S(1)} %copy-done, bf16[128,2048]{1,0:T(8,128)(2,1)S(1)} %copy-done.1, bf16[128,2048]{1,0:T(8,128)(2,1)S(1)} %copy-done.2, bf16[128,2048]{1,0:T(8,128)(2,1)S(1)} %copy-done.3, f32[32,128]{1,0:T(8,128)S(1)} %get-tuple-element.35.refs_0_.refs_4_, ...), custom_call_target="tpu_custom_call" | custom-call | flops 2000000000 | bytes 5709824 | tf_op jit(solution)/shard_map/near_early/pallas_call | solution.py:541
  43.8 1.9 %final_others.1 = (bf16[128,2048]{1,0:T(8,128)(2,1)}, bf16[128,2048]{1,0:T(8,128)(2,1)}, bf16[128,2048]{1,0:T(8,128)(2,1)}, bf16[128,2048]{1,0:T(8,128)(2,1)}) custom-call(bf16[128,2048]{1,0:T(8,128)(2,1)S(1)} %copy-done, bf16[128,2048]{1,0:T(8,128)(2,1)S(1)} %copy-done.1, bf16[128,2048]{1,0:T(8,128)(2,1)S(1)} %copy-done.2, bf16[128,2048]{1,0:T(8,128)(2,1)S(1)} %copy-done.3, ...), custom_call_target="tpu_custom_call" | custom-call | flops 1000000000 | bytes 7774208 | tf_op jit(solution)/shard_map/final_others/pallas_call | solution.py:541
  45.8 1.1 %final_own.1 = (bf16[128,2048]{1,0:T(8,128)(2,1)}, bf16[128,2048]{1,0:T(8,128)(2,1)}, bf16[128,2048]{1,0:T(8,128)(2,1)}, bf16[128,2048]{1,0:T(8,128)(2,1)}) custom-call(f32[4,12,128,128]{3,2,1,0:T(8,128)S(1)} %near_early.1.refs_5_.early_ref, ...), custom_call_target="tpu_custom_call", output_to_operand_aliasing={{0}: (6, {}), {1}: (7, {}), {2}: (8, {}), {3}: (9, {})} | custom-call | flops 16777216 | bytes 8003584 | tf_op jit(solution)/shard_map/final_own/pallas_call | solution.py:541
  (27 shorter events, 0.3 us)
Async XLA Ops:
  2.3 11.4 %collective-permute-start = (bf16[17,32,128]{2,1,0:T(8,128)(2,1)S(1)}, bf16[17,32,128]{2,1,0:T(8,128)(2,1)S(1)}, u32[]{:S(2)}, u32[]{:S(2)}) collective-permute-start(bf16[17,32,128]{2,1,0:T(8,128)(2,1)S(1)} %get-tuple-element.37), channel_id=1, source_target_pairs={{0,3},{1,2},{2,1},{3,0},{4,7},{5,6},{6,5},{7,4},{8,11},{9,10},{10,... | collective-permute-start | bytes 417800 | tf_op jit(solution)/shard_map/ppermute | solution.py:561
  10.2 6.5 %collective-permute-start.3 = (bf16[4,128,128]{2,1,0:T(8,128)(2,1)S(1)}, bf16[4,128,128]{2,1,0:T(8,128)(2,1)S(1)}, u32[]{:S(2)}, u32[]{:S(2)}) collective-permute-start(bf16[4,128,128]{2,1,0:T(8,128)(2,1)S(1)} %get-tuple-element.41), channel_id=1, source_target_pairs={{0,24},{4,28},{8,16},{12,20},{16,8},{20,12},{24,0},{28,4},{1,25},{... | collective-permute-start | bytes 393224 | tf_op jit(solution)/shard_map/ppermute | solution.py:561
  12.7 6.2 %collective-permute-start.4 = (bf16[4,128,128]{2,1,0:T(8,128)(2,1)S(1)}, bf16[4,128,128]{2,1,0:T(8,128)(2,1)S(1)}, u32[]{:S(2)}, u32[]{:S(2)}) collective-permute-start(bf16[4,128,128]{2,1,0:T(8,128)(2,1)S(1)} %get-tuple-element.42), channel_id=1, source_target_pairs={{0,16},{4,20},{8,24},{12,28},{16,0},{20,4},{24,8},{28,12},{1,17},{... | collective-permute-start | bytes 393224 | tf_op jit(solution)/shard_map/ppermute | solution.py:561
  13.2 5.8 %collective-permute-start.5 = (bf16[4,128,128]{2,1,0:T(8,128)(2,1)S(1)}, bf16[4,128,128]{2,1,0:T(8,128)(2,1)S(1)}, u32[]{:S(2)}, u32[]{:S(2)}) collective-permute-start(bf16[4,128,128]{2,1,0:T(8,128)(2,1)S(1)} %get-tuple-element.43), channel_id=1, source_target_pairs={{0,8},{4,12},{8,0},{12,4},{16,24},{20,28},{24,16},{28,20},{1,9},{5... | collective-permute-start | bytes 393224 | tf_op jit(solution)/shard_map/ppermute | solution.py:561
  13.7 8.0 %collective-permute-start.1 = (bf16[17,32,128]{2,1,0:T(8,128)(2,1)S(1)}, bf16[17,32,128]{2,1,0:T(8,128)(2,1)S(1)}, u32[]{:S(2)}, u32[]{:S(2)}) collective-permute-start(bf16[17,32,128]{2,1,0:T(8,128)(2,1)S(1)} %get-tuple-element.38), channel_id=1, source_target_pairs={{0,2},{1,3},{2,0},{3,1},{4,6},{5,7},{6,4},{7,5},{8,10},{9,11},{10,... | collective-permute-start | bytes 417800 | tf_op jit(solution)/shard_map/ppermute | solution.py:561
  13.7 8.0 %collective-permute-start.2 = (bf16[17,32,128]{2,1,0:T(8,128)(2,1)S(1)}, bf16[17,32,128]{2,1,0:T(8,128)(2,1)S(1)}, u32[]{:S(2)}, u32[]{:S(2)}) collective-permute-start(bf16[17,32,128]{2,1,0:T(8,128)(2,1)S(1)} %get-tuple-element.39), channel_id=1, source_target_pairs={{0,1},{1,0},{2,3},{3,2},{4,5},{5,4},{6,7},{7,6},{8,9},{9,8},{10,11... | collective-permute-start | bytes 417800 | tf_op jit(solution)/shard_map/ppermute | solution.py:561
  19.0 1.6 %collective-permute-start.6 = (bf16[4,2,128,128]{3,2,1,0:T(8,128)(2,1)S(1)}, bf16[4,2,128,128]{3,2,1,0:T(8,128)(2,1)S(1)}, u32[]{:S(2)}, u32[]{:S(2)}) collective-permute-start(bf16[4,2,128,128]{3,2,1,0:T(8,128)(2,1)S(1)} %pack.1), channel_id=1, source_target_pairs={{0,4},{4,0},{8,12},{12,8},{16,20},{20,16},{24,28},{28,24},{1,5},{5... | collective-permute-start | bytes 786440 | tf_op jit(solution)/shard_map/ppermute | solution.py:561
  22.3 4.6 %collective-permute-start.9 = (f32[16,128]{1,0:T(8,128)S(1)}, f32[16,128]{1,0:T(8,128)S(1)}, u32[]{:S(2)}, u32[]{:S(2)}) collective-permute-start(f32[16,128]{1,0:T(8,128)S(1)} %get-tuple-element.46.refs_6_.refs_8_.refs_5_), channel_id=1, source_target_pairs={{0,24},{4,28},{8,16},{12,20},{16,8},{20,12},{24,0},{28,4},{1,25},{... | collective-permute-start | bytes 24584 | tf_op jit(solution)/shard_map/ppermute | solution.py:561
  24.0 3.7 %collective-permute-start.8 = (f32[16,128]{1,0:T(8,128)S(1)}, f32[16,128]{1,0:T(8,128)S(1)}, u32[]{:S(2)}, u32[]{:S(2)}) collective-permute-start(f32[16,128]{1,0:T(8,128)S(1)} %get-tuple-element.46.refs_6_.refs_8_.refs_5_), channel_id=1, source_target_pairs={{0,16},{4,20},{8,24},{12,28},{16,0},{20,4},{24,8},{28,12},{1,17},{... | collective-permute-start | bytes 24584 | tf_op jit(solution)/shard_map/ppermute | solution.py:561
  25.3 3.7 %collective-permute-start.7 = (f32[16,128]{1,0:T(8,128)S(1)}, f32[16,128]{1,0:T(8,128)S(1)}, u32[]{:S(2)}, u32[]{:S(2)}) collective-permute-start(f32[16,128]{1,0:T(8,128)S(1)} %get-tuple-element.46.refs_6_.refs_8_.refs_5_), channel_id=1, source_target_pairs={{0,8},{4,12},{8,0},{12,4},{16,24},{20,28},{24,16},{28,20},{1,9},{5... | collective-permute-start | bytes 24584 | tf_op jit(solution)/shard_map/ppermute | solution.py:561
  29.6 7.1 %collective-permute-start.10 = (bf16[17,32,128]{2,1,0:T(8,128)(2,1)S(1)}, bf16[17,32,128]{2,1,0:T(8,128)(2,1)S(1)}, u32[]{:S(2)}, u32[]{:S(2)}) collective-permute-start(bf16[17,32,128]{2,1,0:T(8,128)(2,1)S(1)} %get-tuple-element.48), channel_id=1, source_target_pairs={{0,3},{1,2},{2,1},{3,0},{4,7},{5,6},{6,5},{7,4},{8,11},{9,10},{10,... | collective-permute-start | bytes 417800 | tf_op jit(solution)/shard_map/ppermute | solution.py:561
  32.6 4.1 %collective-permute-start.12 = (bf16[4,2,128,128]{3,2,1,0:T(8,128)(2,1)S(1)}, bf16[4,2,128,128]{3,2,1,0:T(8,128)(2,1)S(1)}, u32[]{:S(2)}, u32[]{:S(2)}) collective-permute-start(bf16[4,2,128,128]{3,2,1,0:T(8,128)(2,1)S(1)} %get-tuple-element.54), channel_id=1, source_target_pairs={{0,4},{4,0},{8,12},{12,8},{16,20},{20,16},{24,28},{28,24},{1,5},{5... | collective-permute-start | bytes 786440 | tf_op jit(solution)/shard_map/ppermute | solution.py:561
  32.7 9.6 %collective-permute-start.11 = (bf16[17,32,128]{2,1,0:T(8,128)(2,1)S(1)}, bf16[17,32,128]{2,1,0:T(8,128)(2,1)S(1)}, u32[]{:S(2)}, u32[]{:S(2)}) collective-permute-start(bf16[17,32,128]{2,1,0:T(8,128)(2,1)S(1)} %get-tuple-element.49), channel_id=1, source_target_pairs={{0,1},{1,0},{2,3},{3,2},{4,5},{5,4},{6,7},{7,6},{8,9},{9,8},{10,11... | collective-permute-start | bytes 417800 | tf_op jit(solution)/shard_map/ppermute | solution.py:561
  33.0 10.7 %collective-permute-start.16 = (bf16[17,32,128]{2,1,0:T(8,128)(2,1)S(1)}, bf16[17,32,128]{2,1,0:T(8,128)(2,1)S(1)}, u32[]{:S(2)}, u32[]{:S(2)}) collective-permute-start(bf16[17,32,128]{2,1,0:T(8,128)(2,1)S(1)} %get-tuple-element.59), channel_id=1, source_target_pairs={{0,2},{1,3},{2,0},{3,1},{4,6},{5,7},{6,4},{7,5},{8,10},{9,11},{10,... | collective-permute-start | bytes 417800 | tf_op jit(solution)/shard_map/ppermute | solution.py:561
  36.7 5.6 %copy-start = (bf16[128,2048]{1,0:T(8,128)(2,1)S(1)}, bf16[128,2048]{1,0:T(8,128)(2,1)}, u32[]{:S(2)}) copy-start(bf16[128,2048]{1,0:T(8,128)(2,1)} %refs_0_.7) | copy-start | bytes 1572868
  36.7 5.6 %copy-start.1 = (bf16[128,2048]{1,0:T(8,128)(2,1)S(1)}, bf16[128,2048]{1,0:T(8,128)(2,1)}, u32[]{:S(2)}) copy-start(bf16[128,2048]{1,0:T(8,128)(2,1)} %refs_1_.7) | copy-start | bytes 1572868
  36.7 5.6 %copy-start.2 = (bf16[128,2048]{1,0:T(8,128)(2,1)S(1)}, bf16[128,2048]{1,0:T(8,128)(2,1)}, u32[]{:S(2)}) copy-start(bf16[128,2048]{1,0:T(8,128)(2,1)} %refs_2_.7) | copy-start | bytes 1572868
  36.7 5.6 %copy-start.3 = (bf16[128,2048]{1,0:T(8,128)(2,1)S(1)}, bf16[128,2048]{1,0:T(8,128)(2,1)}, u32[]{:S(2)}) copy-start(bf16[128,2048]{1,0:T(8,128)(2,1)} %refs_3_.7) | copy-start | bytes 1572868
  36.8 8.9 %collective-permute-start.13 = (bf16[4,128,128]{2,1,0:T(8,128)(2,1)S(1)}, bf16[4,128,128]{2,1,0:T(8,128)(2,1)S(1)}, u32[]{:S(2)}, u32[]{:S(2)}) collective-permute-start(bf16[4,128,128]{2,1,0:T(8,128)(2,1)S(1)} %get-tuple-element.56), channel_id=1, source_target_pairs={{0,24},{4,28},{8,16},{12,20},{16,8},{20,12},{24,0},{28,4},{1,25},{... | collective-permute-start | bytes 393224 | tf_op jit(solution)/shard_map/ppermute | solution.py:561
  38.3 7.5 %collective-permute-start.14 = (bf16[4,128,128]{2,1,0:T(8,128)(2,1)S(1)}, bf16[4,128,128]{2,1,0:T(8,128)(2,1)S(1)}, u32[]{:S(2)}, u32[]{:S(2)}) collective-permute-start(bf16[4,128,128]{2,1,0:T(8,128)(2,1)S(1)} %get-tuple-element.57), channel_id=1, source_target_pairs={{0,16},{4,20},{8,24},{12,28},{16,0},{20,4},{24,8},{28,12},{1,17},{... | collective-permute-start | bytes 393224 | tf_op jit(solution)/shard_map/ppermute | solution.py:561
  38.8 6.9 %collective-permute-start.15 = (bf16[4,128,128]{2,1,0:T(8,128)(2,1)S(1)}, bf16[4,128,128]{2,1,0:T(8,128)(2,1)S(1)}, u32[]{:S(2)}, u32[]{:S(2)}) collective-permute-start(bf16[4,128,128]{2,1,0:T(8,128)(2,1)S(1)} %get-tuple-element.58), channel_id=1, source_target_pairs={{0,8},{4,12},{8,0},{12,4},{16,24},{20,28},{24,16},{28,20},{1,9},{5... | collective-permute-start | bytes 393224 | tf_op jit(solution)/shard_map/ppermute | solution.py:561

commit v18 on v17

--- a/solution.py
+++ b/solution.py
@@ -16,8 +16,8 @@
 LONG = 4 * 10**10
 SHORT = 2 * 10**9
 VMEM_LIMIT = 32 * 1024 * 1024
-PICK_LIMIT = 53 * 1024 * 1024
-FIRST_LIMIT = 54784 * 1024
+PICK_LIMIT = 54784 * 1024
+FIRST_LIMIT = 54272 * 1024
 NEAR_LIMIT = 54784 * 1024
 F32, BF16 = jnp.float32, jnp.bfloat16
 SHAPE = jax.ShapeDtypeStruct
@@ -183,28 +183,29 @@
 
 
 def pick_first_kernel(n_i, slots, *refs):
-    sources, (mid_ref, stats_ref, buffers, sems, wide, turn) = refs[:4], refs[4:]
-    rows = sources[0].shape[0]
-    turn[...] = jnp.zeros_like(turn)
-    pick_places(n_i, slots, [1], sources, [mid_ref], buffers, sems, wide, turn)
-    stats_ref[...] = turn[: 2 * HEADS, :]
-    turn[...] = turn[...].T
-    mid_ref[4 * slots] = split(pick_rows(turn, rows))
-
-
-def pick_rest_kernel(n_i, slots, *refs):
-    sources, first_ref, refs = refs[:4], refs[4], refs[5:]
-    mids, refs = refs[: n_i - 1], refs[n_i - 1 :]
-    fulls, refs = refs[:slots], refs[slots:]
-    stats_ref, buffers, sems, wide, turn = refs
+    sources, (mid_ref, own_ref, *refs) = refs[:4], refs[4:]
+    fulls, (stats_ref, buffers, sems, wide, turn) = refs[:slots], refs[slots:]
     rows = sources[0].shape[0]
     _, chip = position(slots)
     turn[...] = jnp.zeros_like(turn)
+    pick_places(n_i, slots, [1, 0], sources, [mid_ref, own_ref], buffers, sems, wide, turn)
+    for m in range(slots):
+        fulls[m][...] = buffers[1, :, :, head_columns(chip ^ m)]
+    stats_ref[...] = turn[: 2 * HEADS, :]
+    turn[...] = turn[...].T
+    near = split(pick_rows(turn, rows))
+    mid_ref[4 * slots] = near
+    own_ref[4 * slots] = near
+
+
+def pick_rest_kernel(n_i, slots, *refs):
+    sources, first_ref, refs = refs[:4], refs[4], refs[5:]
+    mids, refs = refs[: n_i - 2], refs[n_i - 2 :]
+    stats_ref, buffers, sems, wide, turn = refs
+    rows = sources[0].shape[0]
+    turn[...] = jnp.zeros_like(turn)
     turn[: 2 * HEADS, :] = first_ref[...]
-    steps = [0, *range(2, n_i)]
-    pick_places(n_i, slots, steps, sources, mids, buffers, sems, wide, turn)
-    for m in range(slots):
-        fulls[m][...] = buffers[0, :, :, head_columns(chip ^ m)]
+    pick_places(n_i, slots, range(2, n_i), sources, mids, buffers, sems, wide, turn)
     stats_ref[...] = turn[: 2 * HEADS, :]
     turn[...] = turn[...].T
     near = split(pick_rows(turn, rows))
@@ -601,29 +602,28 @@
             square,
         ]
 
-    first, firststats = call(
+    first, own, *fulls, firststats = call(
         bind(pick_first_kernel, n_i, slots),
         "pick_first",
-        [mid, stats(2 * HEADS)],
-        pick_scratch(1),
-        unit * slots * 2,
+        [mid, mid] + [full] * slots + [stats(2 * HEADS)],
+        pick_scratch(2),
+        unit * slots * 4,
         sources,
         hbm_in=range(4),
         limit=FIRST_LIMIT,
     )
-    pieces = call(
+    *pieces, near = call(
         bind(pick_rest_kernel, n_i, slots),
         "pick_rest",
-        [mid] * (n_i - 1) + [full] * slots + [stats(2 * HEADS)],
-        pick_scratch(n_i - 1),
+        [mid] * (n_i - 2) + [stats(2 * HEADS)],
+        pick_scratch(n_i - 2),
         unit * HEADS * 2,
         [*sources, firststats],
         hbm_in=range(4),
         limit=PICK_LIMIT,
     )
-    mids = swap_mids([pieces[0], first, *pieces[1 : n_i - 1]])
-    fulls = swap_fulls(pieces[n_i - 1 : n_i - 1 + slots])
-    near = pieces[-1]
+    mids = swap_mids([own, first, *pieces])
+    fulls = swap_fulls(fulls)
 
     (settled,) = call(settle_kernel, "far_in", [stats(8)], [], SHORT, [mids[1]])
     (settled,) = call(settle_kernel, "chips_back", [stats(8)], [], LONG, [settled])

time: 47.1 us -> 46.4 us (0.985)
  waiting for transfers between devices: 11.5 us -> 10.8 us
    ppermute x17, waiting for transfers between devices: 11.5 us -> 10.8 us  [swap(): return lax.ppermute(x, axis, [(i, i ^ mask) for i in range(n)])]
  transfers between devices with their start and end apart: 17 -> 17, of which waited for: 9 -> 10; matrix products, arithmetic and copies ran while one was open for 0% -> 0% of each run, Pallas kernels for 21% -> 20%
where the time goes in v18:
time: 46.4 us; the launch traced here: 46.2 us
  starting transfers between devices  21.1 us (45%)
  Pallas kernels  13.5 us (29%)
  waiting for transfers between devices  10.8 us (23%)
  between operations  0.82 us (2%)
    ppermute x17, starting transfers between devices, swap(): return lax.ppermute(x, axis, [(i, i ^ mask) for i in range(n)])  21.1 us
    pallas_call x17, Pallas kernels, call(): pl.pallas_call(kernel, out_shape=tuple(outs), in_specs=[pl.BlockSpec(memo...  13.5 us
    ppermute x17, waiting for transfers between devices, swap(): return lax.ppermute(x, axis, [(i, i ^ mask) for i in range(n)])  10.8 us
  transfers between devices with their start and end apart: 17, of which 10 were waited for; matrix products, arithmetic and copies ran while one was open for 0% of the time, Pallas kernels for 20%

profile of v18, /device:TPU:0, one launch (start us, length us, event | category | flops | bytes accessed | tf_op | source)
XLA Modules:
  0.0 46.2 jit_solution(8099068323234904495)
XLA Ops:
  0.6 2.3 %pick_first.1 = (bf16[17,32,128]{2,1,0:T(8,128)(2,1)S(1)}, bf16[17,32,128]{2,1,0:T(8,128)(2,1)S(1)}, bf16[4,128,128]{2,1,0:T(8,128)(2,1)S(1)}, bf16[4,128,128]{2...) custom-call(bf16[128,2048]{1,0:T(8,128)(2,1)} %refs_0_.7, ...), custom_call_target="tpu_custom_call" | custom-call | flops 67108864 | bytes 2916352 | tf_op jit(solution)/shard_map/pick_first/pallas_call | solution.py:542
  2.9 5.1 %collective-permute-start = (bf16[17,32,128]{2,1,0:T(8,128)(2,1)S(1)}, bf16[17,32,128]{2,1,0:T(8,128)(2,1)S(1)}, u32[]{:S(2)}, u32[]{:S(2)}) collective-permute-start(bf16[17,32,128]{2,1,0:T(8,128)(2,1)S(1)} %get-tuple-element.37), channel_id=1, source_target_pairs={{0,3},{1,2},{2,1},{3,0},{4,7},{5,6},{6,5},{7,4},{8,11},{9,10},{10,... | collective-permute-start | bytes 417800 | tf_op jit(solution)/shard_map/ppermute | solution.py:562
  8.0 2.4 %collective-permute-start.3 = (bf16[4,128,128]{2,1,0:T(8,128)(2,1)S(1)}, bf16[4,128,128]{2,1,0:T(8,128)(2,1)S(1)}, u32[]{:S(2)}, u32[]{:S(2)}) collective-permute-start(bf16[4,128,128]{2,1,0:T(8,128)(2,1)S(1)} %get-tuple-element.41), channel_id=1, source_target_pairs={{0,24},{4,28},{8,16},{12,20},{16,8},{20,12},{24,0},{28,4},{1,25},{... | collective-permute-start | bytes 393224 | tf_op jit(solution)/shard_map/ppermute | solution.py:562
  10.5 0.5 %collective-permute-start.4 = (bf16[4,128,128]{2,1,0:T(8,128)(2,1)S(1)}, bf16[4,128,128]{2,1,0:T(8,128)(2,1)S(1)}, u32[]{:S(2)}, u32[]{:S(2)}) collective-permute-start(bf16[4,128,128]{2,1,0:T(8,128)(2,1)S(1)} %get-tuple-element.42), channel_id=1, source_target_pairs={{0,16},{4,20},{8,24},{12,28},{16,0},{20,4},{24,8},{28,12},{1,17},{... | collective-permute-start | bytes 393224 | tf_op jit(solution)/shard_map/ppermute | solution.py:562
  11.0 0.5 %collective-permute-start.5 = (bf16[4,128,128]{2,1,0:T(8,128)(2,1)S(1)}, bf16[4,128,128]{2,1,0:T(8,128)(2,1)S(1)}, u32[]{:S(2)}, u32[]{:S(2)}) collective-permute-start(bf16[4,128,128]{2,1,0:T(8,128)(2,1)S(1)} %get-tuple-element.43), channel_id=1, source_target_pairs={{0,8},{4,12},{8,0},{12,4},{16,24},{20,28},{24,16},{28,20},{1,9},{5... | collective-permute-start | bytes 393224 | tf_op jit(solution)/shard_map/ppermute | solution.py:562
  11.5 2.1 %pick_rest.1 = (bf16[17,32,128]{2,1,0:T(8,128)(2,1)S(1)}, bf16[17,32,128]{2,1,0:T(8,128)(2,1)S(1)}, f32[32,128]{1,0:T(8,128)S(1)}) custom-call(bf16[128,2048]{1,0:T(8,128)(2,1)} %refs_0_.7, bf16[128,2048]{1,0:T(8,128)(2,1)} %refs_1_.7, bf16[128,2048]{1,0:T(8,128)(2,1)} %refs_2_.7, bf16[128,2048]{1,0:T(8,128)(2,1)} %refs_3_.7, ...), custom_call_target="tpu_custom_call" | custom-call | flops 134217728 | bytes 2408448 | tf_op jit(solution)/shard_map/pick_rest/pallas_call | solution.py:542
  13.8 0.6 %collective-permute-start.2 = (bf16[17,32,128]{2,1,0:T(8,128)(2,1)S(1)}, bf16[17,32,128]{2,1,0:T(8,128)(2,1)S(1)}, u32[]{:S(2)}, u32[]{:S(2)}) collective-permute-start(bf16[17,32,128]{2,1,0:T(8,128)(2,1)S(1)} %get-tuple-element.39), channel_id=1, source_target_pairs={{0,1},{1,0},{2,3},{3,2},{4,5},{5,4},{6,7},{7,6},{8,9},{9,8},{10,11... | collective-permute-start | bytes 417800 | tf_op jit(solution)/shard_map/ppermute | solution.py:562
  14.4 2.3 %collective-permute-done.4.refs_2_ = bf16[4,128,128]{2,1,0:T(8,128)(2,1)S(1)} collective-permute-done((bf16[4,128,128]{2,1,0:T(8,128)(2,1)S(1)}, bf16[4,128,128]{2,1,0:T(8,128)(2,1)S(1)}, u32[]{:S(2)}, u32[]{:S(2)}) %collective-permute-start.4) | collective-permute-done | bytes 131104 | tf_op jit(solution)/shard_map/ppermute | solution.py:562
  16.9 1.5 %collective-permute-done.6.refs_4_ = bf16[4,2,128,128]{3,2,1,0:T(8,128)(2,1)S(1)} collective-permute-done((bf16[4,2,128,128]{3,2,1,0:T(8,128)(2,1)S(1)}, bf16[4,2,128,128]{3,2,1,0:T(8,128)(2,1)S(1)}, u32[]{:S(2)}, u32[]{:S(2)}) %collective-permute-start.6) | collective-permute-done | bytes 262176 | tf_op jit(solution)/shard_map/ppermute | solution.py:562
  18.4 1.1 %far_stats.1.refs_5_ = f32[8,128]{1,0:T(8,128)S(1)} custom-call(bf16[4,128,128]{2,1,0:T(8,128)(2,1)S(1)} %get-tuple-element.40.refs_0_, bf16[4,128,128]{2,1,0:T(8,128)(2,1)S(1)} %collective-permute-done.3.refs_1_, bf16[4,128,128]{2,1,0:T(8,128)(2,1)S(1)} %collective-permute-done.4.refs_2_, bf16[4,128,128]{2,1,0:T(8,128)(2,1)S(1)} %collective-permute-done.5.refs_3_, ...), custom_call_target="tpu_custom_call" | custom-call | flops 1 | bytes 794624 | tf_op jit(solution)/shard_map/far_stats/pallas_call | solution.py:542
  19.5 1.4 %collective-permute-done.1.refs_2_ = bf16[17,32,128]{2,1,0:T(8,128)(2,1)S(1)} collective-permute-done((bf16[17,32,128]{2,1,0:T(8,128)(2,1)S(1)}, bf16[17,32,128]{2,1,0:T(8,128)(2,1)S(1)}, u32[]{:S(2)}, u32[]{:S(2)}) %collective-permute-start.1) | collective-permute-done | bytes 139296 | tf_op jit(solution)/shard_map/ppermute | solution.py:562
  21.0 0.1 collective-permute-done.2.refs_3_
  21.1 0.5 %middle_stats.1 = (f32[16,128]{1,0:T(8,128)S(1)}, f32[8,128]{1,0:T(8,128)S(1)}, f32[128,128]{1,0:T(8,128)S(1)}) custom-call(bf16[17,32,128]{2,1,0:T(8,128)(2,1)S(1)} %get-tuple-element.36.refs_0_, bf16[17,32,128]{2,1,0:T(8,128)(2,1)S(1)} %collective-permute-done.refs_0_.refs_1_, bf16[17,32,128]{2,1,0:T(8,128)(2,1)S(1)} %collective-permute-done.1.refs_2_, ...), custom_call_target="tpu_custom_call" | custom-call | flops 33554432 | bytes 655360 | tf_op jit(solution)/shard_map/middle_stats/pallas_call | solution.py:542
  21.6 2.5 %collective-permute-start.9 = (f32[16,128]{1,0:T(8,128)S(1)}, f32[16,128]{1,0:T(8,128)S(1)}, u32[]{:S(2)}, u32[]{:S(2)}) collective-permute-start(f32[16,128]{1,0:T(8,128)S(1)} %get-tuple-element.46.refs_6_.refs_8_.refs_5_), channel_id=1, source_target_pairs={{0,24},{4,28},{8,16},{12,20},{16,8},{20,12},{24,0},{28,4},{1,25},{... | collective-permute-start | bytes 24584 | tf_op jit(solution)/shard_map/ppermute | solution.py:562
  24.1 0.5 %collective-permute-start.8 = (f32[16,128]{1,0:T(8,128)S(1)}, f32[16,128]{1,0:T(8,128)S(1)}, u32[]{:S(2)}, u32[]{:S(2)}) collective-permute-start(f32[16,128]{1,0:T(8,128)S(1)} %get-tuple-element.46.refs_6_.refs_8_.refs_5_), channel_id=1, source_target_pairs={{0,16},{4,20},{8,24},{12,28},{16,0},{20,4},{24,8},{28,12},{1,17},{... | collective-permute-start | bytes 24584 | tf_op jit(solution)/shard_map/ppermute | solution.py:562
  24.6 0.5 %collective-permute-start.7 = (f32[16,128]{1,0:T(8,128)S(1)}, f32[16,128]{1,0:T(8,128)S(1)}, u32[]{:S(2)}, u32[]{:S(2)}) collective-permute-start(f32[16,128]{1,0:T(8,128)S(1)} %get-tuple-element.46.refs_6_.refs_8_.refs_5_), channel_id=1, source_target_pairs={{0,8},{4,12},{8,0},{12,4},{16,24},{20,28},{24,16},{28,20},{1,9},{5... | collective-permute-start | bytes 24584 | tf_op jit(solution)/shard_map/ppermute | solution.py:562
  25.2 1.1 %collective-permute-done.9.refs_9_.refs_11_.refs_8_ = f32[16,128]{1,0:T(8,128)S(1)} collective-permute-done((f32[16,128]{1,0:T(8,128)S(1)}, f32[16,128]{1,0:T(8,128)S(1)}, u32[]{:S(2)}, u32[]{:S(2)}) %collective-permute-start.9) | collective-permute-done | bytes 8224 | tf_op jit(solution)/shard_map/ppermute | solution.py:562
  26.2 1.5 %collective-permute-done.8.refs_8_.refs_10_.refs_7_ = f32[16,128]{1,0:T(8,128)S(1)} collective-permute-done((f32[16,128]{1,0:T(8,128)S(1)}, f32[16,128]{1,0:T(8,128)S(1)}, u32[]{:S(2)}, u32[]{:S(2)}) %collective-permute-start.8) | collective-permute-done | bytes 8224 | tf_op jit(solution)/shard_map/ppermute | solution.py:562
  27.8 0.5 %collective-permute-done.7.refs_7_.refs_9_.refs_6_ = f32[16,128]{1,0:T(8,128)S(1)} collective-permute-done((f32[16,128]{1,0:T(8,128)S(1)}, f32[16,128]{1,0:T(8,128)S(1)}, u32[]{:S(2)}, u32[]{:S(2)}) %collective-permute-start.7) | collective-permute-done | bytes 8224 | tf_op jit(solution)/shard_map/ppermute | solution.py:562
  28.3 0.6 %middle_parts.1 = (bf16[17,32,128]{2,1,0:T(8,128)(2,1)S(1)}, bf16[17,32,128]{2,1,0:T(8,128)(2,1)S(1)}, bf16[17,32,128]{2,1,0:T(8,128)(2,1)S(1)}, bf16[17,32,128]{2,1,0:T(8,128)(2,1)S(1)}) custom-call(bf16[17,32,128]{2,1,0:T(8,128)(2,1)S(1)} %get-tuple-element.36.refs_0_, bf16[17,32,128]{2,1,0:T(8,128)(2,1)S(1)} %collective-permute-done.refs_0_.refs_1_, ...), custom_call_target="tpu_custom_call" | custom-call | flops 100663296 | bytes 1216512 | tf_op jit(solution)/shard_map/middle_parts/pallas_call | solution.py:542
  28.9 1.5 %collective-permute-start.10 = (bf16[17,32,128]{2,1,0:T(8,128)(2,1)S(1)}, bf16[17,32,128]{2,1,0:T(8,128)(2,1)S(1)}, u32[]{:S(2)}, u32[]{:S(2)}) collective-permute-start(bf16[17,32,128]{2,1,0:T(8,128)(2,1)S(1)} %get-tuple-element.48), channel_id=1, source_target_pairs={{0,3},{1,2},{2,1},{3,0},{4,7},{5,6},{6,5},{7,4},{8,11},{9,10},{10,... | collective-permute-start | bytes 417800 | tf_op jit(solution)/shard_map/ppermute | solution.py:562
  30.4 2.3 %far_parts.1 = (bf16[4,128,128]{2,1,0:T(8,128)(2,1)S(1)}, bf16[4,128,128]{2,1,0:T(8,128)(2,1)S(1)}, bf16[4,128,128]{2,1,0:T(8,128)(2,1)S(1)}, bf16[4,128,128]{2,...) custom-call(bf16[4,128,128]{2,1,0:T(8,128)(2,1)S(1)} %get-tuple-element.40.refs_0_, ...), custom_call_target="tpu_custom_call" | custom-call | flops 1 | bytes 1 | tf_op jit(solution)/shard_map/far_parts/pallas_call | solution.py:542
  32.8 0.3 collective-permute-start.11
  33.1 2.8 %collective-permute-start.16 = (bf16[17,32,128]{2,1,0:T(8,128)(2,1)S(1)}, bf16[17,32,128]{2,1,0:T(8,128)(2,1)S(1)}, u32[]{:S(2)}, u32[]{:S(2)}) collective-permute-start(bf16[17,32,128]{2,1,0:T(8,128)(2,1)S(1)} %get-tuple-element.59), channel_id=1, source_target_pairs={{0,2},{1,3},{2,0},{3,1},{4,6},{5,7},{6,4},{7,5},{8,10},{9,11},{10,... | collective-permute-start | bytes 417800 | tf_op jit(solution)/shard_map/ppermute | solution.py:562
  36.0 1.6 %collective-permute-start.13 = (bf16[4,128,128]{2,1,0:T(8,128)(2,1)S(1)}, bf16[4,128,128]{2,1,0:T(8,128)(2,1)S(1)}, u32[]{:S(2)}, u32[]{:S(2)}) collective-permute-start(bf16[4,128,128]{2,1,0:T(8,128)(2,1)S(1)} %get-tuple-element.56), channel_id=1, source_target_pairs={{0,24},{4,28},{8,16},{12,20},{16,8},{20,12},{24,0},{28,4},{1,25},{... | collective-permute-start | bytes 393224 | tf_op jit(solution)/shard_map/ppermute | solution.py:562
  37.5 0.5 %collective-permute-start.14 = (bf16[4,128,128]{2,1,0:T(8,128)(2,1)S(1)}, bf16[4,128,128]{2,1,0:T(8,128)(2,1)S(1)}, u32[]{:S(2)}, u32[]{:S(2)}) collective-permute-start(bf16[4,128,128]{2,1,0:T(8,128)(2,1)S(1)} %get-tuple-element.57), channel_id=1, source_target_pairs={{0,16},{4,20},{8,24},{12,28},{16,0},{20,4},{24,8},{28,12},{1,17},{... | collective-permute-start | bytes 393224 | tf_op jit(solution)/shard_map/ppermute | solution.py:562
  38.0 1.5 %collective-permute-start.15 = (bf16[4,128,128]{2,1,0:T(8,128)(2,1)S(1)}, bf16[4,128,128]{2,1,0:T(8,128)(2,1)S(1)}, u32[]{:S(2)}, u32[]{:S(2)}) collective-permute-start(bf16[4,128,128]{2,1,0:T(8,128)(2,1)S(1)} %get-tuple-element.58), channel_id=1, source_target_pairs={{0,8},{4,12},{8,0},{12,4},{16,24},{20,28},{24,16},{28,20},{1,9},{5... | collective-permute-start | bytes 393224 | tf_op jit(solution)/shard_map/ppermute | solution.py:562
  39.5 2.1 %collective-permute-done.11.refs_7_ = bf16[17,32,128]{2,1,0:T(8,128)(2,1)S(1)} collective-permute-done((bf16[17,32,128]{2,1,0:T(8,128)(2,1)S(1)}, bf16[17,32,128]{2,1,0:T(8,128)(2,1)S(1)}, u32[]{:S(2)}, u32[]{:S(2)}) %collective-permute-start.11) | collective-permute-done | bytes 139296 | tf_op jit(solution)/shard_map/ppermute | solution.py:562
  41.6 1.4 %near_early.1.refs_5_.early_ref = f32[4,12,128,128]{3,2,1,0:T(8,128)S(1)} custom-call(bf16[128,2048]{1,0:T(8,128)(2,1)S(1)} %copy-done, bf16[128,2048]{1,0:T(8,128)(2,1)S(1)} %copy-done.1, bf16[128,2048]{1,0:T(8,128)(2,1)S(1)} %copy-done.2, bf16[128,2048]{1,0:T(8,128)(2,1)S(1)} %copy-done.3, f32[32,128]{1,0:T(8,128)S(1)} %get-tuple-element.35.refs_0_.refs_4_, ...), custom_call_target="tpu_custom_call" | custom-call | flops 2000000000 | bytes 5709824 | tf_op jit(solution)/shard_map/near_early/pallas_call | solution.py:542
  43.1 1.9 %final_others.1 = (bf16[128,2048]{1,0:T(8,128)(2,1)}, bf16[128,2048]{1,0:T(8,128)(2,1)}, bf16[128,2048]{1,0:T(8,128)(2,1)}, bf16[128,2048]{1,0:T(8,128)(2,1)}) custom-call(bf16[128,2048]{1,0:T(8,128)(2,1)S(1)} %copy-done, bf16[128,2048]{1,0:T(8,128)(2,1)S(1)} %copy-done.1, bf16[128,2048]{1,0:T(8,128)(2,1)S(1)} %copy-done.2, bf16[128,2048]{1,0:T(8,128)(2,1)S(1)} %copy-done.3, ...), custom_call_target="tpu_custom_call" | custom-call | flops 1000000000 | bytes 7774208 | tf_op jit(solution)/shard_map/final_others/pallas_call | solution.py:542
  45.1 0.1 collective-permute-done.15.refs_3_
  45.1 1.1 %final_own.1 = (bf16[128,2048]{1,0:T(8,128)(2,1)}, bf16[128,2048]{1,0:T(8,128)(2,1)}, bf16[128,2048]{1,0:T(8,128)(2,1)}, bf16[128,2048]{1,0:T(8,128)(2,1)}) custom-call(f32[4,12,128,128]{3,2,1,0:T(8,128)S(1)} %near_early.1.refs_5_.early_ref, ...), custom_call_target="tpu_custom_call", output_to_operand_aliasing={{0}: (6, {}), {1}: (7, {}), {2}: (8, {}), {3}: (9, {})} | custom-call | flops 16777216 | bytes 8003584 | tf_op jit(solution)/shard_map/final_own/pallas_call | solution.py:542
  (27 shorter events, 0.5 us)
Async XLA Ops:
  2.9 10.8 %collective-permute-start = (bf16[17,32,128]{2,1,0:T(8,128)(2,1)S(1)}, bf16[17,32,128]{2,1,0:T(8,128)(2,1)S(1)}, u32[]{:S(2)}, u32[]{:S(2)}) collective-permute-start(bf16[17,32,128]{2,1,0:T(8,128)(2,1)S(1)} %get-tuple-element.37), channel_id=1, source_target_pairs={{0,3},{1,2},{2,1},{3,0},{4,7},{5,6},{6,5},{7,4},{8,11},{9,10},{10,... | collective-permute-start | bytes 417800 | tf_op jit(solution)/shard_map/ppermute | solution.py:562
  8.0 6.4 %collective-permute-start.3 = (bf16[4,128,128]{2,1,0:T(8,128)(2,1)S(1)}, bf16[4,128,128]{2,1,0:T(8,128)(2,1)S(1)}, u32[]{:S(2)}, u32[]{:S(2)}) collective-permute-start(bf16[4,128,128]{2,1,0:T(8,128)(2,1)S(1)} %get-tuple-element.41), channel_id=1, source_target_pairs={{0,24},{4,28},{8,16},{12,20},{16,8},{20,12},{24,0},{28,4},{1,25},{... | collective-permute-start | bytes 393224 | tf_op jit(solution)/shard_map/ppermute | solution.py:562
  10.5 6.2 %collective-permute-start.4 = (bf16[4,128,128]{2,1,0:T(8,128)(2,1)S(1)}, bf16[4,128,128]{2,1,0:T(8,128)(2,1)S(1)}, u32[]{:S(2)}, u32[]{:S(2)}) collective-permute-start(bf16[4,128,128]{2,1,0:T(8,128)(2,1)S(1)} %get-tuple-element.42), channel_id=1, source_target_pairs={{0,16},{4,20},{8,24},{12,28},{16,0},{20,4},{24,8},{28,12},{1,17},{... | collective-permute-start | bytes 393224 | tf_op jit(solution)/shard_map/ppermute | solution.py:562
  11.0 5.8 %collective-permute-start.5 = (bf16[4,128,128]{2,1,0:T(8,128)(2,1)S(1)}, bf16[4,128,128]{2,1,0:T(8,128)(2,1)S(1)}, u32[]{:S(2)}, u32[]{:S(2)}) collective-permute-start(bf16[4,128,128]{2,1,0:T(8,128)(2,1)S(1)} %get-tuple-element.43), channel_id=1, source_target_pairs={{0,8},{4,12},{8,0},{12,4},{16,24},{20,28},{24,16},{28,20},{1,9},{5... | collective-permute-start | bytes 393224 | tf_op jit(solution)/shard_map/ppermute | solution.py:562
  13.7 7.3 %collective-permute-start.1 = (bf16[17,32,128]{2,1,0:T(8,128)(2,1)S(1)}, bf16[17,32,128]{2,1,0:T(8,128)(2,1)S(1)}, u32[]{:S(2)}, u32[]{:S(2)}) collective-permute-start(bf16[17,32,128]{2,1,0:T(8,128)(2,1)S(1)} %get-tuple-element.38), channel_id=1, source_target_pairs={{0,2},{1,3},{2,0},{3,1},{4,6},{5,7},{6,4},{7,5},{8,10},{9,11},{10,... | collective-permute-start | bytes 417800 | tf_op jit(solution)/shard_map/ppermute | solution.py:562
  13.8 7.3 %collective-permute-start.2 = (bf16[17,32,128]{2,1,0:T(8,128)(2,1)S(1)}, bf16[17,32,128]{2,1,0:T(8,128)(2,1)S(1)}, u32[]{:S(2)}, u32[]{:S(2)}) collective-permute-start(bf16[17,32,128]{2,1,0:T(8,128)(2,1)S(1)} %get-tuple-element.39), channel_id=1, source_target_pairs={{0,1},{1,0},{2,3},{3,2},{4,5},{5,4},{6,7},{7,6},{8,9},{9,8},{10,11... | collective-permute-start | bytes 417800 | tf_op jit(solution)/shard_map/ppermute | solution.py:562
  16.8 1.6 %collective-permute-start.6 = (bf16[4,2,128,128]{3,2,1,0:T(8,128)(2,1)S(1)}, bf16[4,2,128,128]{3,2,1,0:T(8,128)(2,1)S(1)}, u32[]{:S(2)}, u32[]{:S(2)}) collective-permute-start(bf16[4,2,128,128]{3,2,1,0:T(8,128)(2,1)S(1)} %pack.1), channel_id=1, source_target_pairs={{0,4},{4,0},{8,12},{12,8},{16,20},{20,16},{24,28},{28,24},{1,5},{5... | collective-permute-start | bytes 786440 | tf_op jit(solution)/shard_map/ppermute | solution.py:562
  21.6 4.6 %collective-permute-start.9 = (f32[16,128]{1,0:T(8,128)S(1)}, f32[16,128]{1,0:T(8,128)S(1)}, u32[]{:S(2)}, u32[]{:S(2)}) collective-permute-start(f32[16,128]{1,0:T(8,128)S(1)} %get-tuple-element.46.refs_6_.refs_8_.refs_5_), channel_id=1, source_target_pairs={{0,24},{4,28},{8,16},{12,20},{16,8},{20,12},{24,0},{28,4},{1,25},{... | collective-permute-start | bytes 24584 | tf_op jit(solution)/shard_map/ppermute | solution.py:562
  24.1 3.7 %collective-permute-start.8 = (f32[16,128]{1,0:T(8,128)S(1)}, f32[16,128]{1,0:T(8,128)S(1)}, u32[]{:S(2)}, u32[]{:S(2)}) collective-permute-start(f32[16,128]{1,0:T(8,128)S(1)} %get-tuple-element.46.refs_6_.refs_8_.refs_5_), channel_id=1, source_target_pairs={{0,16},{4,20},{8,24},{12,28},{16,0},{20,4},{24,8},{28,12},{1,17},{... | collective-permute-start | bytes 24584 | tf_op jit(solution)/shard_map/ppermute | solution.py:562
  24.6 3.7 %collective-permute-start.7 = (f32[16,128]{1,0:T(8,128)S(1)}, f32[16,128]{1,0:T(8,128)S(1)}, u32[]{:S(2)}, u32[]{:S(2)}) collective-permute-start(f32[16,128]{1,0:T(8,128)S(1)} %get-tuple-element.46.refs_6_.refs_8_.refs_5_), channel_id=1, source_target_pairs={{0,8},{4,12},{8,0},{12,4},{16,24},{20,28},{24,16},{28,20},{1,9},{5... | collective-permute-start | bytes 24584 | tf_op jit(solution)/shard_map/ppermute | solution.py:562
  28.9 6.9 %collective-permute-start.10 = (bf16[17,32,128]{2,1,0:T(8,128)(2,1)S(1)}, bf16[17,32,128]{2,1,0:T(8,128)(2,1)S(1)}, u32[]{:S(2)}, u32[]{:S(2)}) collective-permute-start(bf16[17,32,128]{2,1,0:T(8,128)(2,1)S(1)} %get-tuple-element.48), channel_id=1, source_target_pairs={{0,3},{1,2},{2,1},{3,0},{4,7},{5,6},{6,5},{7,4},{8,11},{9,10},{10,... | collective-permute-start | bytes 417800 | tf_op jit(solution)/shard_map/ppermute | solution.py:562
  32.7 3.1 %collective-permute-start.12 = (bf16[4,2,128,128]{3,2,1,0:T(8,128)(2,1)S(1)}, bf16[4,2,128,128]{3,2,1,0:T(8,128)(2,1)S(1)}, u32[]{:S(2)}, u32[]{:S(2)}) collective-permute-start(bf16[4,2,128,128]{3,2,1,0:T(8,128)(2,1)S(1)} %get-tuple-element.54), channel_id=1, source_target_pairs={{0,4},{4,0},{8,12},{12,8},{16,20},{20,16},{24,28},{28,24},{1,5},{5... | collective-permute-start | bytes 786440 | tf_op jit(solution)/shard_map/ppermute | solution.py:562
  32.8 8.8 %collective-permute-start.11 = (bf16[17,32,128]{2,1,0:T(8,128)(2,1)S(1)}, bf16[17,32,128]{2,1,0:T(8,128)(2,1)S(1)}, u32[]{:S(2)}, u32[]{:S(2)}) collective-permute-start(bf16[17,32,128]{2,1,0:T(8,128)(2,1)S(1)} %get-tuple-element.49), channel_id=1, source_target_pairs={{0,1},{1,0},{2,3},{3,2},{4,5},{5,4},{6,7},{7,6},{8,9},{9,8},{10,11... | collective-permute-start | bytes 417800 | tf_op jit(solution)/shard_map/ppermute | solution.py:562
  33.1 10.0 %collective-permute-start.16 = (bf16[17,32,128]{2,1,0:T(8,128)(2,1)S(1)}, bf16[17,32,128]{2,1,0:T(8,128)(2,1)S(1)}, u32[]{:S(2)}, u32[]{:S(2)}) collective-permute-start(bf16[17,32,128]{2,1,0:T(8,128)(2,1)S(1)} %get-tuple-element.59), channel_id=1, source_target_pairs={{0,2},{1,3},{2,0},{3,1},{4,6},{5,7},{6,4},{7,5},{8,10},{9,11},{10,... | collective-permute-start | bytes 417800 | tf_op jit(solution)/shard_map/ppermute | solution.py:562
  35.8 5.8 %copy-start = (bf16[128,2048]{1,0:T(8,128)(2,1)S(1)}, bf16[128,2048]{1,0:T(8,128)(2,1)}, u32[]{:S(2)}) copy-start(bf16[128,2048]{1,0:T(8,128)(2,1)} %refs_0_.7) | copy-start | bytes 1572868
  35.9 5.8 %copy-start.1 = (bf16[128,2048]{1,0:T(8,128)(2,1)S(1)}, bf16[128,2048]{1,0:T(8,128)(2,1)}, u32[]{:S(2)}) copy-start(bf16[128,2048]{1,0:T(8,128)(2,1)} %refs_1_.7) | copy-start | bytes 1572868
  35.9 5.8 %copy-start.2 = (bf16[128,2048]{1,0:T(8,128)(2,1)S(1)}, bf16[128,2048]{1,0:T(8,128)(2,1)}, u32[]{:S(2)}) copy-start(bf16[128,2048]{1,0:T(8,128)(2,1)} %refs_2_.7) | copy-start | bytes 1572868
  35.9 5.8 %copy-start.3 = (bf16[128,2048]{1,0:T(8,128)(2,1)S(1)}, bf16[128,2048]{1,0:T(8,128)(2,1)}, u32[]{:S(2)}) copy-start(bf16[128,2048]{1,0:T(8,128)(2,1)} %refs_3_.7) | copy-start | bytes 1572868
  36.0 9.1 %collective-permute-start.13 = (bf16[4,128,128]{2,1,0:T(8,128)(2,1)S(1)}, bf16[4,128,128]{2,1,0:T(8,128)(2,1)S(1)}, u32[]{:S(2)}, u32[]{:S(2)}) collective-permute-start(bf16[4,128,128]{2,1,0:T(8,128)(2,1)S(1)} %get-tuple-element.56), channel_id=1, source_target_pairs={{0,24},{4,28},{8,16},{12,20},{16,8},{20,12},{24,0},{28,4},{1,25},{... | collective-permute-start | bytes 393224 | tf_op jit(solution)/shard_map/ppermute | solution.py:562
  37.5 7.5 %collective-permute-start.14 = (bf16[4,128,128]{2,1,0:T(8,128)(2,1)S(1)}, bf16[4,128,128]{2,1,0:T(8,128)(2,1)S(1)}, u32[]{:S(2)}, u32[]{:S(2)}) collective-permute-start(bf16[4,128,128]{2,1,0:T(8,128)(2,1)S(1)} %get-tuple-element.57), channel_id=1, source_target_pairs={{0,16},{4,20},{8,24},{12,28},{16,0},{20,4},{24,8},{28,12},{1,17},{... | collective-permute-start | bytes 393224 | tf_op jit(solution)/shard_map/ppermute | solution.py:562
  38.0 7.1 %collective-permute-start.15 = (bf16[4,128,128]{2,1,0:T(8,128)(2,1)S(1)}, bf16[4,128,128]{2,1,0:T(8,128)(2,1)S(1)}, u32[]{:S(2)}, u32[]{:S(2)}) collective-permute-start(bf16[4,128,128]{2,1,0:T(8,128)(2,1)S(1)} %get-tuple-element.58), channel_id=1, source_target_pairs={{0,8},{4,12},{8,0},{12,4},{16,24},{20,28},{24,16},{28,20},{1,9},{5... | collective-permute-start | bytes 393224 | tf_op jit(solution)/shard_map/ppermute | solution.py:562

commit v19 on v18

--- a/solution.py
+++ b/solution.py
@@ -51,7 +51,9 @@
     return lax.axis_index("seqi"), lax.axis_index("seqo") // width
 
 
-def distance(n_i, step):
+def distance(n_i, step, odd):
+    if odd and step > 1:
+        return step - 1
     return n_i - step
 
 
@@ -59,9 +61,17 @@
     return n_i - 1 if step == 1 else step - 1
 
 
+def is_odd():
+    return lax.axis_index("seqo") % 2 == 1
+
+
 def place_in(n_i, slots, step):
     pos, _ = position(slots)
-    return pos if step == 0 else pos ^ distance(n_i, step)
+    if step == 0:
+        return pos
+    if distance(n_i, step, False) == distance(n_i, step, True):
+        return pos ^ distance(n_i, step, False)
+    return pos ^ jnp.where(is_odd(), distance(n_i, step, True), distance(n_i, step, False))
 
 
 def first_back(n_i, slots, step):
@@ -70,10 +80,17 @@
 
 
 def in_back_order(n_i, chunks):
-    order = [distance(n_i, step) for step in range(1, n_i)]
-    return [chunks[0]] + [
-        chunks[order.index(distance_back(n_i, step)) + 1] for step in range(1, n_i)
-    ]
+    found = [chunks[0]]
+    for step in range(1, n_i):
+        even, odd = [
+            [distance(n_i, k, parity) for k in range(1, n_i)].index(distance_back(n_i, step)) + 1
+            for parity in (False, True)
+        ]
+        if even == odd:
+            found.append(chunks[even])
+        else:
+            found.append(jnp.where(is_odd(), chunks[odd], chunks[even]))
+    return found
 
 
 def lanes_of(rows):
@@ -498,12 +515,13 @@
     mids, refs = refs[: n_i - 1], refs[n_i - 1 :]
     outs, (ready, sems, stats_ref, spread) = refs[:4], refs[4:]
     last = n_i - 1
-    near_statistics(n_i, slots, [last], near_ref, mids[-1:], (), stats_ref, spread)
-    late = near_place(n_i, slots, last, sources, stats_ref)
     copies = []
     for step in range(1, n_i):
         first = first_back(n_i, slots, step)
         found = [spread_rows(slots, first + slot, slot, mids[step - 1]) for slot in range(slots)]
+        if step == last:
+            near_statistics(n_i, slots, [last], near_ref, mids[-1:], (), stats_ref, spread)
+            late = near_place(n_i, slots, last, sources, stats_ref)
         for slot, parts in enumerate(found):
             for which in range(4):
                 near = late[slot][which] if step == last else early_ref[which, step * slots + slot]
@@ -582,9 +600,15 @@
         return SHAPE((count, lanes), F32)
 
     def swap_mids(pieces):
-        return [pieces[0]] + [
-            swap(pieces[step], "seqi", n_i, distance(n_i, step)) for step in range(1, n_i)
-        ]
+        found = [pieces[0]]
+        for step in range(1, n_i):
+            pairs = [
+                (o * n_i + i, o * n_i + (i ^ distance(n_i, step, o % 2 == 1)))
+                for o in range(n_o)
+                for i in range(n_i)
+            ]
+            found.append(lax.ppermute(pieces[step], ("seqo", "seqi"), pairs))
+        return found
 
     def swap_back(pieces):
         return [pieces[0]] + [

time: 46.4 us -> 47.4 us (1.022)
  waiting for transfers between devices: 10.8 us -> 11.8 us
    ppermute x17 -> x14, starting transfers between devices: 21.1 us -> 15.2 us  [swap(): return lax.ppermute(x, axis, [(i, i ^ mask) for i in range(n)])]
    ppermute x0 -> x3, starting transfers between devices: none -> 5.83 us  [swap_mids(): found.append(lax.ppermute(pieces[step], ('seqo', 'seqi'), pairs))]
    ppermute x0 -> x3, waiting for transfers between devices: none -> 2.55 us  [swap_mids(): found.append(lax.ppermute(pieces[step], ('seqo', 'seqi'), pairs))]
    ppermute x17 -> x14, waiting for transfers between devices: 10.8 us -> 9.24 us  [swap(): return lax.ppermute(x, axis, [(i, i ^ mask) for i in range(n)])]
  transfers between devices with their start and end apart: 17 -> 17, of which waited for: 10 -> 9; matrix products, arithmetic and copies ran while one was open for 0% -> 0% of each run, Pallas kernels for 20% -> 19%
where the time goes in v19:
time: 47.4 us; the launch traced here: 47.2 us
  starting transfers between devices  21.1 us (45%)
  Pallas kernels  13.5 us (28%)
  waiting for transfers between devices  11.8 us (25%)
  between operations  0.82 us (2%)
    ppermute x14, starting transfers between devices, swap(): return lax.ppermute(x, axis, [(i, i ^ mask) for i in range(n)])  15.2 us
    pallas_call x17, Pallas kernels, call(): pl.pallas_call(kernel, out_shape=tuple(outs), in_specs=[pl.BlockSpec(memo...  13.5 us
    ppermute x14, waiting for transfers between devices, swap(): return lax.ppermute(x, axis, [(i, i ^ mask) for i in range(n)])  9.24 us
    ppermute x3, starting transfers between devices, swap_mids(): found.append(lax.ppermute(pieces[step], ('seqo', 'seqi'), pairs))  5.83 us
    ppermute x3, waiting for transfers between devices, swap_mids(): found.append(lax.ppermute(pieces[step], ('seqo', 'seqi'), pairs))  2.55 us
  transfers between devices with their start and end apart: 17, of which 9 were waited for; matrix products, arithmetic and copies ran while one was open for 0% of the time, Pallas kernels for 19%

profile of v19, /device:TPU:0, one launch (start us, length us, event | category | flops | bytes accessed | tf_op | source)
XLA Modules:
  0.0 47.2 jit_solution(17555426090832738801)
XLA Ops:
  0.6 2.3 %pick_first.1 = (bf16[17,32,128]{2,1,0:T(8,128)(2,1)S(1)}, bf16[17,32,128]{2,1,0:T(8,128)(2,1)S(1)}, bf16[4,128,128]{2,1,0:T(8,128)(2,1)S(1)}, bf16[4,128,128]{2...) custom-call(bf16[128,2048]{1,0:T(8,128)(2,1)} %refs_0_.7, ...), custom_call_target="tpu_custom_call" | custom-call | flops 67108864 | bytes 2916352 | tf_op jit(solution)/shard_map/pick_first/pallas_call | solution.py:560
  2.9 5.1 %collective-permute-start = (bf16[17,32,128]{2,1,0:T(8,128)(2,1)S(1)}, bf16[17,32,128]{2,1,0:T(8,128)(2,1)S(1)}, u32[]{:S(2)}, u32[]{:S(2)}) collective-permute-start(bf16[17,32,128]{2,1,0:T(8,128)(2,1)S(1)} %get-tuple-element.37), channel_id=1, source_target_pairs={{0,3},{1,2},{2,1},{3,0},{4,7},{5,6},{6,5},{7,4},{8,11},{9,10},{10,... | collective-permute-start | bytes 417800 | tf_op jit(solution)/shard_map/ppermute | solution.py:610
  8.0 2.4 %collective-permute-start.3 = (bf16[4,128,128]{2,1,0:T(8,128)(2,1)S(1)}, bf16[4,128,128]{2,1,0:T(8,128)(2,1)S(1)}, u32[]{:S(2)}, u32[]{:S(2)}) collective-permute-start(bf16[4,128,128]{2,1,0:T(8,128)(2,1)S(1)} %get-tuple-element.41), channel_id=1, source_target_pairs={{0,24},{4,28},{8,16},{12,20},{16,8},{20,12},{24,0},{28,4},{1,25},{... | collective-permute-start | bytes 393224 | tf_op jit(solution)/shard_map/ppermute | solution.py:580
  10.5 0.5 %collective-permute-start.4 = (bf16[4,128,128]{2,1,0:T(8,128)(2,1)S(1)}, bf16[4,128,128]{2,1,0:T(8,128)(2,1)S(1)}, u32[]{:S(2)}, u32[]{:S(2)}) collective-permute-start(bf16[4,128,128]{2,1,0:T(8,128)(2,1)S(1)} %get-tuple-element.42), channel_id=1, source_target_pairs={{0,16},{4,20},{8,24},{12,28},{16,0},{20,4},{24,8},{28,12},{1,17},{... | collective-permute-start | bytes 393224 | tf_op jit(solution)/shard_map/ppermute | solution.py:580
  11.0 0.5 %collective-permute-start.5 = (bf16[4,128,128]{2,1,0:T(8,128)(2,1)S(1)}, bf16[4,128,128]{2,1,0:T(8,128)(2,1)S(1)}, u32[]{:S(2)}, u32[]{:S(2)}) collective-permute-start(bf16[4,128,128]{2,1,0:T(8,128)(2,1)S(1)} %get-tuple-element.43), channel_id=1, source_target_pairs={{0,8},{4,12},{8,0},{12,4},{16,24},{20,28},{24,16},{28,20},{1,9},{5... | collective-permute-start | bytes 393224 | tf_op jit(solution)/shard_map/ppermute | solution.py:580
  11.5 2.1 %pick_rest.1 = (bf16[17,32,128]{2,1,0:T(8,128)(2,1)S(1)}, bf16[17,32,128]{2,1,0:T(8,128)(2,1)S(1)}, f32[32,128]{1,0:T(8,128)S(1)}) custom-call(bf16[128,2048]{1,0:T(8,128)(2,1)} %refs_0_.7, bf16[128,2048]{1,0:T(8,128)(2,1)} %refs_1_.7, bf16[128,2048]{1,0:T(8,128)(2,1)} %refs_2_.7, bf16[128,2048]{1,0:T(8,128)(2,1)} %refs_3_.7, ...), custom_call_target="tpu_custom_call" | custom-call | flops 134217728 | bytes 2408448 | tf_op jit(solution)/shard_map/pick_rest/pallas_call | solution.py:560
  13.7 0.1 collective-permute-start.1
  13.8 0.6 %collective-permute-start.2 = (bf16[17,32,128]{2,1,0:T(8,128)(2,1)S(1)}, bf16[17,32,128]{2,1,0:T(8,128)(2,1)S(1)}, u32[]{:S(2)}, u32[]{:S(2)}) collective-permute-start(bf16[17,32,128]{2,1,0:T(8,128)(2,1)S(1)} %get-tuple-element.39), channel_id=1, source_target_pairs={{0,1},{1,0},{2,3},{3,2},{4,6},{5,7},{6,4},{7,5},{8,9},{9,8},{10,11... | collective-permute-start | bytes 417800 | tf_op jit(solution)/shard_map/ppermute | solution.py:610
  14.4 2.3 %collective-permute-done.4.refs_2_ = bf16[4,128,128]{2,1,0:T(8,128)(2,1)S(1)} collective-permute-done((bf16[4,128,128]{2,1,0:T(8,128)(2,1)S(1)}, bf16[4,128,128]{2,1,0:T(8,128)(2,1)S(1)}, u32[]{:S(2)}, u32[]{:S(2)}) %collective-permute-start.4) | collective-permute-done | bytes 131104 | tf_op jit(solution)/shard_map/ppermute | solution.py:580
  16.9 1.5 %collective-permute-done.6.refs_4_ = bf16[4,2,128,128]{3,2,1,0:T(8,128)(2,1)S(1)} collective-permute-done((bf16[4,2,128,128]{3,2,1,0:T(8,128)(2,1)S(1)}, bf16[4,2,128,128]{3,2,1,0:T(8,128)(2,1)S(1)}, u32[]{:S(2)}, u32[]{:S(2)}) %collective-permute-start.6) | collective-permute-done | bytes 262176 | tf_op jit(solution)/shard_map/ppermute | solution.py:580
  18.4 1.1 %far_stats.1.refs_5_ = f32[8,128]{1,0:T(8,128)S(1)} custom-call(bf16[4,128,128]{2,1,0:T(8,128)(2,1)S(1)} %get-tuple-element.40.refs_0_, bf16[4,128,128]{2,1,0:T(8,128)(2,1)S(1)} %collective-permute-done.3.refs_1_, bf16[4,128,128]{2,1,0:T(8,128)(2,1)S(1)} %collective-permute-done.4.refs_2_, bf16[4,128,128]{2,1,0:T(8,128)(2,1)S(1)} %collective-permute-done.5.refs_3_, ...), custom_call_target="tpu_custom_call" | custom-call | flops 1 | bytes 794624 | tf_op jit(solution)/shard_map/far_stats/pallas_call | solution.py:560
  19.5 2.5 %collective-permute-done.1.refs_2_ = bf16[17,32,128]{2,1,0:T(8,128)(2,1)S(1)} collective-permute-done((bf16[17,32,128]{2,1,0:T(8,128)(2,1)S(1)}, bf16[17,32,128]{2,1,0:T(8,128)(2,1)S(1)}, u32[]{:S(2)}, u32[]{:S(2)}) %collective-permute-start.1) | collective-permute-done | bytes 139296 | tf_op jit(solution)/shard_map/ppermute | solution.py:610
  22.1 0.5 %middle_stats.1 = (f32[16,128]{1,0:T(8,128)S(1)}, f32[8,128]{1,0:T(8,128)S(1)}, f32[128,128]{1,0:T(8,128)S(1)}) custom-call(bf16[17,32,128]{2,1,0:T(8,128)(2,1)S(1)} %get-tuple-element.36.refs_0_, bf16[17,32,128]{2,1,0:T(8,128)(2,1)S(1)} %collective-permute-done.refs_0_.refs_1_, bf16[17,32,128]{2,1,0:T(8,128)(2,1)S(1)} %collective-permute-done.1.refs_2_, ...), custom_call_target="tpu_custom_call" | custom-call | flops 33554432 | bytes 655360 | tf_op jit(solution)/shard_map/middle_stats/pallas_call | solution.py:560
  22.6 2.5 %collective-permute-start.9 = (f32[16,128]{1,0:T(8,128)S(1)}, f32[16,128]{1,0:T(8,128)S(1)}, u32[]{:S(2)}, u32[]{:S(2)}) collective-permute-start(f32[16,128]{1,0:T(8,128)S(1)} %get-tuple-element.46.refs_6_.refs_8_.refs_5_), channel_id=1, source_target_pairs={{0,24},{4,28},{8,16},{12,20},{16,8},{20,12},{24,0},{28,4},{1,25},{... | collective-permute-start | bytes 24584 | tf_op jit(solution)/shard_map/ppermute | solution.py:580
  25.1 0.5 %collective-permute-start.8 = (f32[16,128]{1,0:T(8,128)S(1)}, f32[16,128]{1,0:T(8,128)S(1)}, u32[]{:S(2)}, u32[]{:S(2)}) collective-permute-start(f32[16,128]{1,0:T(8,128)S(1)} %get-tuple-element.46.refs_6_.refs_8_.refs_5_), channel_id=1, source_target_pairs={{0,16},{4,20},{8,24},{12,28},{16,0},{20,4},{24,8},{28,12},{1,17},{... | collective-permute-start | bytes 24584 | tf_op jit(solution)/shard_map/ppermute | solution.py:580
  25.6 0.5 %collective-permute-start.7 = (f32[16,128]{1,0:T(8,128)S(1)}, f32[16,128]{1,0:T(8,128)S(1)}, u32[]{:S(2)}, u32[]{:S(2)}) collective-permute-start(f32[16,128]{1,0:T(8,128)S(1)} %get-tuple-element.46.refs_6_.refs_8_.refs_5_), channel_id=1, source_target_pairs={{0,8},{4,12},{8,0},{12,4},{16,24},{20,28},{24,16},{28,20},{1,9},{5... | collective-permute-start | bytes 24584 | tf_op jit(solution)/shard_map/ppermute | solution.py:580
  26.1 1.1 %collective-permute-done.9.refs_9_.refs_11_.refs_8_ = f32[16,128]{1,0:T(8,128)S(1)} collective-permute-done((f32[16,128]{1,0:T(8,128)S(1)}, f32[16,128]{1,0:T(8,128)S(1)}, u32[]{:S(2)}, u32[]{:S(2)}) %collective-permute-start.9) | collective-permute-done | bytes 8224 | tf_op jit(solution)/shard_map/ppermute | solution.py:580
  27.2 1.5 %collective-permute-done.8.refs_8_.refs_10_.refs_7_ = f32[16,128]{1,0:T(8,128)S(1)} collective-permute-done((f32[16,128]{1,0:T(8,128)S(1)}, f32[16,128]{1,0:T(8,128)S(1)}, u32[]{:S(2)}, u32[]{:S(2)}) %collective-permute-start.8) | collective-permute-done | bytes 8224 | tf_op jit(solution)/shard_map/ppermute | solution.py:580
  28.7 0.5 %collective-permute-done.7.refs_7_.refs_9_.refs_6_ = f32[16,128]{1,0:T(8,128)S(1)} collective-permute-done((f32[16,128]{1,0:T(8,128)S(1)}, f32[16,128]{1,0:T(8,128)S(1)}, u32[]{:S(2)}, u32[]{:S(2)}) %collective-permute-start.7) | collective-permute-done | bytes 8224 | tf_op jit(solution)/shard_map/ppermute | solution.py:580
  29.2 0.6 %middle_parts.1 = (bf16[17,32,128]{2,1,0:T(8,128)(2,1)S(1)}, bf16[17,32,128]{2,1,0:T(8,128)(2,1)S(1)}, bf16[17,32,128]{2,1,0:T(8,128)(2,1)S(1)}, bf16[17,32,128]{2,1,0:T(8,128)(2,1)S(1)}) custom-call(bf16[17,32,128]{2,1,0:T(8,128)(2,1)S(1)} %get-tuple-element.36.refs_0_, bf16[17,32,128]{2,1,0:T(8,128)(2,1)S(1)} %collective-permute-done.refs_0_.refs_1_, ...), custom_call_target="tpu_custom_call" | custom-call | flops 100663296 | bytes 1216512 | tf_op jit(solution)/shard_map/middle_parts/pallas_call | solution.py:560
  29.9 1.8 %collective-permute-start.10 = (bf16[17,32,128]{2,1,0:T(8,128)(2,1)S(1)}, bf16[17,32,128]{2,1,0:T(8,128)(2,1)S(1)}, u32[]{:S(2)}, u32[]{:S(2)}) collective-permute-start(bf16[17,32,128]{2,1,0:T(8,128)(2,1)S(1)} %get-tuple-element.48), channel_id=1, source_target_pairs={{0,3},{1,2},{2,1},{3,0},{4,7},{5,6},{6,5},{7,4},{8,11},{9,10},{10,... | collective-permute-start | bytes 417800 | tf_op jit(solution)/shard_map/ppermute | solution.py:580
  31.6 2.3 %far_parts.1 = (bf16[4,128,128]{2,1,0:T(8,128)(2,1)S(1)}, bf16[4,128,128]{2,1,0:T(8,128)(2,1)S(1)}, bf16[4,128,128]{2,1,0:T(8,128)(2,1)S(1)}, bf16[4,128,128]{2,...) custom-call(bf16[4,128,128]{2,1,0:T(8,128)(2,1)S(1)} %get-tuple-element.40.refs_0_, ...), custom_call_target="tpu_custom_call" | custom-call | flops 1 | bytes 1 | tf_op jit(solution)/shard_map/far_parts/pallas_call | solution.py:560
  34.1 2.7 %collective-permute-start.16 = (bf16[17,32,128]{2,1,0:T(8,128)(2,1)S(1)}, bf16[17,32,128]{2,1,0:T(8,128)(2,1)S(1)}, u32[]{:S(2)}, u32[]{:S(2)}) collective-permute-start(bf16[17,32,128]{2,1,0:T(8,128)(2,1)S(1)} %get-tuple-element.59), channel_id=1, source_target_pairs={{0,2},{1,3},{2,0},{3,1},{4,6},{5,7},{6,4},{7,5},{8,10},{9,11},{10,... | collective-permute-start | bytes 417800 | tf_op jit(solution)/shard_map/ppermute | solution.py:580
  36.9 0.1 far_sum.1
  36.9 1.6 %collective-permute-start.13 = (bf16[4,128,128]{2,1,0:T(8,128)(2,1)S(1)}, bf16[4,128,128]{2,1,0:T(8,128)(2,1)S(1)}, u32[]{:S(2)}, u32[]{:S(2)}) collective-permute-start(bf16[4,128,128]{2,1,0:T(8,128)(2,1)S(1)} %get-tuple-element.56), channel_id=1, source_target_pairs={{0,24},{4,28},{8,16},{12,20},{16,8},{20,12},{24,0},{28,4},{1,25},{... | collective-permute-start | bytes 393224 | tf_op jit(solution)/shard_map/ppermute | solution.py:580
  38.5 0.5 %collective-permute-start.14 = (bf16[4,128,128]{2,1,0:T(8,128)(2,1)S(1)}, bf16[4,128,128]{2,1,0:T(8,128)(2,1)S(1)}, u32[]{:S(2)}, u32[]{:S(2)}) collective-permute-start(bf16[4,128,128]{2,1,0:T(8,128)(2,1)S(1)} %get-tuple-element.57), channel_id=1, source_target_pairs={{0,16},{4,20},{8,24},{12,28},{16,0},{20,4},{24,8},{28,12},{1,17},{... | collective-permute-start | bytes 393224 | tf_op jit(solution)/shard_map/ppermute | solution.py:580
  39.0 1.5 %collective-permute-start.15 = (bf16[4,128,128]{2,1,0:T(8,128)(2,1)S(1)}, bf16[4,128,128]{2,1,0:T(8,128)(2,1)S(1)}, u32[]{:S(2)}, u32[]{:S(2)}) collective-permute-start(bf16[4,128,128]{2,1,0:T(8,128)(2,1)S(1)} %get-tuple-element.58), channel_id=1, source_target_pairs={{0,8},{4,12},{8,0},{12,4},{16,24},{20,28},{24,16},{28,20},{1,9},{5... | collective-permute-start | bytes 393224 | tf_op jit(solution)/shard_map/ppermute | solution.py:580
  40.5 2.1 %collective-permute-done.11.refs_7_ = bf16[17,32,128]{2,1,0:T(8,128)(2,1)S(1)} collective-permute-done((bf16[17,32,128]{2,1,0:T(8,128)(2,1)S(1)}, bf16[17,32,128]{2,1,0:T(8,128)(2,1)S(1)}, u32[]{:S(2)}, u32[]{:S(2)}) %collective-permute-start.11) | collective-permute-done | bytes 139296 | tf_op jit(solution)/shard_map/ppermute | solution.py:580
  42.6 1.4 %near_early.1.refs_5_.early_ref = f32[4,12,128,128]{3,2,1,0:T(8,128)S(1)} custom-call(bf16[128,2048]{1,0:T(8,128)(2,1)S(1)} %copy-done, bf16[128,2048]{1,0:T(8,128)(2,1)S(1)} %copy-done.1, bf16[128,2048]{1,0:T(8,128)(2,1)S(1)} %copy-done.2, bf16[128,2048]{1,0:T(8,128)(2,1)S(1)} %copy-done.3, f32[32,128]{1,0:T(8,128)S(1)} %get-tuple-element.35.refs_0_.refs_4_, ...), custom_call_target="tpu_custom_call" | custom-call | flops 2000000000 | bytes 5709824 | tf_op jit(solution)/shard_map/near_early/pallas_call | solution.py:560
  44.1 1.9 %final_others.1 = (bf16[128,2048]{1,0:T(8,128)(2,1)}, bf16[128,2048]{1,0:T(8,128)(2,1)}, bf16[128,2048]{1,0:T(8,128)(2,1)}, bf16[128,2048]{1,0:T(8,128)(2,1)}) custom-call(bf16[128,2048]{1,0:T(8,128)(2,1)S(1)} %copy-done, bf16[128,2048]{1,0:T(8,128)(2,1)S(1)} %copy-done.1, bf16[128,2048]{1,0:T(8,128)(2,1)S(1)} %copy-done.2, bf16[128,2048]{1,0:T(8,128)(2,1)S(1)} %copy-done.3, ...), custom_call_target="tpu_custom_call" | custom-call | flops 1000000000 | bytes 7774208 | tf_op jit(solution)/shard_map/final_others/pallas_call | solution.py:560
  46.0 0.1 collective-permute-done.15.refs_3_
  46.1 1.1 %final_own.1 = (bf16[128,2048]{1,0:T(8,128)(2,1)}, bf16[128,2048]{1,0:T(8,128)(2,1)}, bf16[128,2048]{1,0:T(8,128)(2,1)}, bf16[128,2048]{1,0:T(8,128)(2,1)}) custom-call(f32[4,12,128,128]{3,2,1,0:T(8,128)S(1)} %near_early.1.refs_5_.early_ref, ...), custom_call_target="tpu_custom_call", output_to_operand_aliasing={{0}: (6, {}), {1}: (7, {}), {2}: (8, {}), {3}: (9, {})} | custom-call | flops 16777216 | bytes 8003584 | tf_op jit(solution)/shard_map/final_own/pallas_call | solution.py:560
  (27 shorter events, 0.4 us)
Async XLA Ops:
  2.9 10.8 %collective-permute-start = (bf16[17,32,128]{2,1,0:T(8,128)(2,1)S(1)}, bf16[17,32,128]{2,1,0:T(8,128)(2,1)S(1)}, u32[]{:S(2)}, u32[]{:S(2)}) collective-permute-start(bf16[17,32,128]{2,1,0:T(8,128)(2,1)S(1)} %get-tuple-element.37), channel_id=1, source_target_pairs={{0,3},{1,2},{2,1},{3,0},{4,7},{5,6},{6,5},{7,4},{8,11},{9,10},{10,... | collective-permute-start | bytes 417800 | tf_op jit(solution)/shard_map/ppermute | solution.py:610
  8.0 6.4 %collective-permute-start.3 = (bf16[4,128,128]{2,1,0:T(8,128)(2,1)S(1)}, bf16[4,128,128]{2,1,0:T(8,128)(2,1)S(1)}, u32[]{:S(2)}, u32[]{:S(2)}) collective-permute-start(bf16[4,128,128]{2,1,0:T(8,128)(2,1)S(1)} %get-tuple-element.41), channel_id=1, source_target_pairs={{0,24},{4,28},{8,16},{12,20},{16,8},{20,12},{24,0},{28,4},{1,25},{... | collective-permute-start | bytes 393224 | tf_op jit(solution)/shard_map/ppermute | solution.py:580
  10.5 6.2 %collective-permute-start.4 = (bf16[4,128,128]{2,1,0:T(8,128)(2,1)S(1)}, bf16[4,128,128]{2,1,0:T(8,128)(2,1)S(1)}, u32[]{:S(2)}, u32[]{:S(2)}) collective-permute-start(bf16[4,128,128]{2,1,0:T(8,128)(2,1)S(1)} %get-tuple-element.42), channel_id=1, source_target_pairs={{0,16},{4,20},{8,24},{12,28},{16,0},{20,4},{24,8},{28,12},{1,17},{... | collective-permute-start | bytes 393224 | tf_op jit(solution)/shard_map/ppermute | solution.py:580
  11.0 5.8 %collective-permute-start.5 = (bf16[4,128,128]{2,1,0:T(8,128)(2,1)S(1)}, bf16[4,128,128]{2,1,0:T(8,128)(2,1)S(1)}, u32[]{:S(2)}, u32[]{:S(2)}) collective-permute-start(bf16[4,128,128]{2,1,0:T(8,128)(2,1)S(1)} %get-tuple-element.43), channel_id=1, source_target_pairs={{0,8},{4,12},{8,0},{12,4},{16,24},{20,28},{24,16},{28,20},{1,9},{5... | collective-permute-start | bytes 393224 | tf_op jit(solution)/shard_map/ppermute | solution.py:580
  13.7 8.4 %collective-permute-start.1 = (bf16[17,32,128]{2,1,0:T(8,128)(2,1)S(1)}, bf16[17,32,128]{2,1,0:T(8,128)(2,1)S(1)}, u32[]{:S(2)}, u32[]{:S(2)}) collective-permute-start(bf16[17,32,128]{2,1,0:T(8,128)(2,1)S(1)} %get-tuple-element.38), channel_id=1, source_target_pairs={{0,2},{1,3},{2,0},{3,1},{4,5},{5,4},{6,7},{7,6},{8,10},{9,11},{10,... | collective-permute-start | bytes 417800 | tf_op jit(solution)/shard_map/ppermute | solution.py:610
  13.8 8.3 %collective-permute-start.2 = (bf16[17,32,128]{2,1,0:T(8,128)(2,1)S(1)}, bf16[17,32,128]{2,1,0:T(8,128)(2,1)S(1)}, u32[]{:S(2)}, u32[]{:S(2)}) collective-permute-start(bf16[17,32,128]{2,1,0:T(8,128)(2,1)S(1)} %get-tuple-element.39), channel_id=1, source_target_pairs={{0,1},{1,0},{2,3},{3,2},{4,6},{5,7},{6,4},{7,5},{8,9},{9,8},{10,11... | collective-permute-start | bytes 417800 | tf_op jit(solution)/shard_map/ppermute | solution.py:610
  16.8 1.6 %collective-permute-start.6 = (bf16[4,2,128,128]{3,2,1,0:T(8,128)(2,1)S(1)}, bf16[4,2,128,128]{3,2,1,0:T(8,128)(2,1)S(1)}, u32[]{:S(2)}, u32[]{:S(2)}) collective-permute-start(bf16[4,2,128,128]{3,2,1,0:T(8,128)(2,1)S(1)} %pack.1), channel_id=1, source_target_pairs={{0,4},{4,0},{8,12},{12,8},{16,20},{20,16},{24,28},{28,24},{1,5},{5... | collective-permute-start | bytes 786440 | tf_op jit(solution)/shard_map/ppermute | solution.py:580
  22.6 4.6 %collective-permute-start.9 = (f32[16,128]{1,0:T(8,128)S(1)}, f32[16,128]{1,0:T(8,128)S(1)}, u32[]{:S(2)}, u32[]{:S(2)}) collective-permute-start(f32[16,128]{1,0:T(8,128)S(1)} %get-tuple-element.46.refs_6_.refs_8_.refs_5_), channel_id=1, source_target_pairs={{0,24},{4,28},{8,16},{12,20},{16,8},{20,12},{24,0},{28,4},{1,25},{... | collective-permute-start | bytes 24584 | tf_op jit(solution)/shard_map/ppermute | solution.py:580
  25.1 3.7 %collective-permute-start.8 = (f32[16,128]{1,0:T(8,128)S(1)}, f32[16,128]{1,0:T(8,128)S(1)}, u32[]{:S(2)}, u32[]{:S(2)}) collective-permute-start(f32[16,128]{1,0:T(8,128)S(1)} %get-tuple-element.46.refs_6_.refs_8_.refs_5_), channel_id=1, source_target_pairs={{0,16},{4,20},{8,24},{12,28},{16,0},{20,4},{24,8},{28,12},{1,17},{... | collective-permute-start | bytes 24584 | tf_op jit(solution)/shard_map/ppermute | solution.py:580
  25.6 3.7 %collective-permute-start.7 = (f32[16,128]{1,0:T(8,128)S(1)}, f32[16,128]{1,0:T(8,128)S(1)}, u32[]{:S(2)}, u32[]{:S(2)}) collective-permute-start(f32[16,128]{1,0:T(8,128)S(1)} %get-tuple-element.46.refs_6_.refs_8_.refs_5_), channel_id=1, source_target_pairs={{0,8},{4,12},{8,0},{12,4},{16,24},{20,28},{24,16},{28,20},{1,9},{5... | collective-permute-start | bytes 24584 | tf_op jit(solution)/shard_map/ppermute | solution.py:580
  29.9 6.9 %collective-permute-start.10 = (bf16[17,32,128]{2,1,0:T(8,128)(2,1)S(1)}, bf16[17,32,128]{2,1,0:T(8,128)(2,1)S(1)}, u32[]{:S(2)}, u32[]{:S(2)}) collective-permute-start(bf16[17,32,128]{2,1,0:T(8,128)(2,1)S(1)} %get-tuple-element.48), channel_id=1, source_target_pairs={{0,3},{1,2},{2,1},{3,0},{4,7},{5,6},{6,5},{7,4},{8,11},{9,10},{10,... | collective-permute-start | bytes 417800 | tf_op jit(solution)/shard_map/ppermute | solution.py:580
  33.9 2.9 %collective-permute-start.12 = (bf16[4,2,128,128]{3,2,1,0:T(8,128)(2,1)S(1)}, bf16[4,2,128,128]{3,2,1,0:T(8,128)(2,1)S(1)}, u32[]{:S(2)}, u32[]{:S(2)}) collective-permute-start(bf16[4,2,128,128]{3,2,1,0:T(8,128)(2,1)S(1)} %get-tuple-element.54), channel_id=1, source_target_pairs={{0,4},{4,0},{8,12},{12,8},{16,20},{20,16},{24,28},{28,24},{1,5},{5... | collective-permute-start | bytes 786440 | tf_op jit(solution)/shard_map/ppermute | solution.py:580
  34.0 8.6 %collective-permute-start.11 = (bf16[17,32,128]{2,1,0:T(8,128)(2,1)S(1)}, bf16[17,32,128]{2,1,0:T(8,128)(2,1)S(1)}, u32[]{:S(2)}, u32[]{:S(2)}) collective-permute-start(bf16[17,32,128]{2,1,0:T(8,128)(2,1)S(1)} %get-tuple-element.49), channel_id=1, source_target_pairs={{0,1},{1,0},{2,3},{3,2},{4,5},{5,4},{6,7},{7,6},{8,9},{9,8},{10,11... | collective-permute-start | bytes 417800 | tf_op jit(solution)/shard_map/ppermute | solution.py:580
  34.1 10.0 %collective-permute-start.16 = (bf16[17,32,128]{2,1,0:T(8,128)(2,1)S(1)}, bf16[17,32,128]{2,1,0:T(8,128)(2,1)S(1)}, u32[]{:S(2)}, u32[]{:S(2)}) collective-permute-start(bf16[17,32,128]{2,1,0:T(8,128)(2,1)S(1)} %get-tuple-element.59), channel_id=1, source_target_pairs={{0,2},{1,3},{2,0},{3,1},{4,6},{5,7},{6,4},{7,5},{8,10},{9,11},{10,... | collective-permute-start | bytes 417800 | tf_op jit(solution)/shard_map/ppermute | solution.py:580
  36.8 5.8 %copy-start = (bf16[128,2048]{1,0:T(8,128)(2,1)S(1)}, bf16[128,2048]{1,0:T(8,128)(2,1)}, u32[]{:S(2)}) copy-start(bf16[128,2048]{1,0:T(8,128)(2,1)} %refs_0_.7) | copy-start | bytes 1572868
  36.8 5.8 %copy-start.1 = (bf16[128,2048]{1,0:T(8,128)(2,1)S(1)}, bf16[128,2048]{1,0:T(8,128)(2,1)}, u32[]{:S(2)}) copy-start(bf16[128,2048]{1,0:T(8,128)(2,1)} %refs_1_.7) | copy-start | bytes 1572868
  36.8 5.8 %copy-start.2 = (bf16[128,2048]{1,0:T(8,128)(2,1)S(1)}, bf16[128,2048]{1,0:T(8,128)(2,1)}, u32[]{:S(2)}) copy-start(bf16[128,2048]{1,0:T(8,128)(2,1)} %refs_2_.7) | copy-start | bytes 1572868
  36.8 5.8 %copy-start.3 = (bf16[128,2048]{1,0:T(8,128)(2,1)S(1)}, bf16[128,2048]{1,0:T(8,128)(2,1)}, u32[]{:S(2)}) copy-start(bf16[128,2048]{1,0:T(8,128)(2,1)} %refs_3_.7) | copy-start | bytes 1572868
  36.9 9.1 %collective-permute-start.13 = (bf16[4,128,128]{2,1,0:T(8,128)(2,1)S(1)}, bf16[4,128,128]{2,1,0:T(8,128)(2,1)S(1)}, u32[]{:S(2)}, u32[]{:S(2)}) collective-permute-start(bf16[4,128,128]{2,1,0:T(8,128)(2,1)S(1)} %get-tuple-element.56), channel_id=1, source_target_pairs={{0,24},{4,28},{8,16},{12,20},{16,8},{20,12},{24,0},{28,4},{1,25},{... | collective-permute-start | bytes 393224 | tf_op jit(solution)/shard_map/ppermute | solution.py:580
  38.5 7.5 %collective-permute-start.14 = (bf16[4,128,128]{2,1,0:T(8,128)(2,1)S(1)}, bf16[4,128,128]{2,1,0:T(8,128)(2,1)S(1)}, u32[]{:S(2)}, u32[]{:S(2)}) collective-permute-start(bf16[4,128,128]{2,1,0:T(8,128)(2,1)S(1)} %get-tuple-element.57), channel_id=1, source_target_pairs={{0,16},{4,20},{8,24},{12,28},{16,0},{20,4},{24,8},{28,12},{1,17},{... | collective-permute-start | bytes 393224 | tf_op jit(solution)/shard_map/ppermute | solution.py:580
  39.0 7.1 %collective-permute-start.15 = (bf16[4,128,128]{2,1,0:T(8,128)(2,1)S(1)}, bf16[4,128,128]{2,1,0:T(8,128)(2,1)S(1)}, u32[]{:S(2)}, u32[]{:S(2)}) collective-permute-start(bf16[4,128,128]{2,1,0:T(8,128)(2,1)S(1)} %get-tuple-element.58), channel_id=1, source_target_pairs={{0,8},{4,12},{8,0},{12,4},{16,24},{20,28},{24,16},{28,20},{1,9},{5... | collective-permute-start | bytes 393224 | tf_op jit(solution)/shard_map/ppermute | solution.py:580

commit v20 on v18

--- a/solution.py
+++ b/solution.py
@@ -198,14 +198,14 @@
     own_ref[4 * slots] = near
 
 
-def pick_rest_kernel(n_i, slots, *refs):
-    sources, first_ref, refs = refs[:4], refs[4], refs[5:]
-    mids, refs = refs[: n_i - 2], refs[n_i - 2 :]
+def pick_rest_kernel(n_i, slots, steps, *refs):
+    sources, first_ref, refs = refs[:4], refs[4], refs[6:]
+    mids, refs = refs[: len(steps)], refs[len(steps) :]
     stats_ref, buffers, sems, wide, turn = refs
     rows = sources[0].shape[0]
     turn[...] = jnp.zeros_like(turn)
     turn[: 2 * HEADS, :] = first_ref[...]
-    pick_places(n_i, slots, range(2, n_i), sources, mids, buffers, sems, wide, turn)
+    pick_places(n_i, slots, steps, sources, mids, buffers, sems, wide, turn)
     stats_ref[...] = turn[: 2 * HEADS, :]
     turn[...] = turn[...].T
     near = split(pick_rows(turn, rows))
@@ -498,12 +498,13 @@
     mids, refs = refs[: n_i - 1], refs[n_i - 1 :]
     outs, (ready, sems, stats_ref, spread) = refs[:4], refs[4:]
     last = n_i - 1
-    near_statistics(n_i, slots, [last], near_ref, mids[-1:], (), stats_ref, spread)
-    late = near_place(n_i, slots, last, sources, stats_ref)
     copies = []
     for step in range(1, n_i):
         first = first_back(n_i, slots, step)
         found = [spread_rows(slots, first + slot, slot, mids[step - 1]) for slot in range(slots)]
+        if step == last:
+            near_statistics(n_i, slots, [last], near_ref, mids[-1:], (), stats_ref, spread)
+            late = near_place(n_i, slots, last, sources, stats_ref)
         for slot, parts in enumerate(found):
             for which in range(4):
                 near = late[slot][which] if step == last else early_ref[which, step * slots + slot]
@@ -581,9 +582,9 @@
     def stats(count, lanes=rows):
         return SHAPE((count, lanes), F32)
 
-    def swap_mids(pieces):
-        return [pieces[0]] + [
-            swap(pieces[step], "seqi", n_i, distance(n_i, step)) for step in range(1, n_i)
+    def swap_mids(pieces, begin):
+        return [
+            swap(pieces[step], "seqi", n_i, distance(n_i, step)) for step in range(begin, len(pieces))
         ]
 
     def swap_back(pieces):
@@ -612,17 +613,23 @@
         hbm_in=range(4),
         limit=FIRST_LIMIT,
     )
-    *pieces, near = call(
-        bind(pick_rest_kernel, n_i, slots),
-        "pick_rest",
-        [mid] * (n_i - 2) + [stats(2 * HEADS)],
-        pick_scratch(n_i - 2),
-        unit * HEADS * 2,
-        [*sources, firststats],
-        hbm_in=range(4),
-        limit=PICK_LIMIT,
-    )
-    mids = swap_mids([own, first, *pieces])
+    mids = [own, *swap_mids([own, first], 1)]
+    near, pieces, after = firststats, [], own
+    for name, steps in (("pick_second", [2]), ("pick_rest", list(range(3, n_i)))):
+        *picked, near = call(
+            bind(pick_rest_kernel, n_i, slots, steps),
+            name,
+            [mid] * len(steps) + [stats(2 * HEADS)],
+            pick_scratch(len(steps)),
+            unit * HEADS,
+            [*sources, near, after],
+            hbm_in=range(4),
+            limit=PICK_LIMIT,
+        )
+        pieces += picked
+        after = mids[1]
+
+    mids += swap_mids([own, first, *pieces], 2)
     fulls = swap_fulls(fulls)
 
     (settled,) = call(settle_kernel, "far_in", [stats(8)], [], SHORT, [mids[1]])

time: 46.4 us -> 47.3 us (1.019)
  Pallas kernels: 13.5 us -> 14.7 us
  waiting for transfers between devices: 10.8 us -> 9.97 us
  starting transfers between devices: 21.1 us -> 21.6 us
    pallas_call x17 -> x18, Pallas kernels: 13.5 us -> 14.7 us  [call(): pl.pallas_call(kernel, out_shape=tuple(outs), in_specs=[pl.BlockSpec(memo...]
    ppermute x17, waiting for transfers between devices: 10.8 us -> 9.97 us  [swap(): return lax.ppermute(x, axis, [(i, i ^ mask) for i in range(n)])]
    ppermute x17, starting transfers between devices: 21.1 us -> 21.6 us  [swap(): return lax.ppermute(x, axis, [(i, i ^ mask) for i in range(n)])]
  transfers between devices with their start and end apart: 17 -> 17, of which waited for: 10 -> 10; matrix products, arithmetic and copies ran while one was open for 0% -> 0% of each run, Pallas kernels for 20% -> 22%
where the time goes in v20:
time: 47.3 us; the launch traced here: 47.1 us
  starting transfers between devices  21.6 us (46%)
  Pallas kernels  14.7 us (31%)
  waiting for transfers between devices  9.97 us (21%)
  between operations  0.84 us (2%)
    ppermute x17, starting transfers between devices, swap(): return lax.ppermute(x, axis, [(i, i ^ mask) for i in range(n)])  21.6 us
    pallas_call x18, Pallas kernels, call(): pl.pallas_call(kernel, out_shape=tuple(outs), in_specs=[pl.BlockSpec(memo...  14.7 us
    ppermute x17, waiting for transfers between devices, swap(): return lax.ppermute(x, axis, [(i, i ^ mask) for i in range(n)])  9.97 us
  transfers between devices with their start and end apart: 17, of which 10 were waited for; matrix products, arithmetic and copies ran while one was open for 0% of the time, Pallas kernels for 22%

profile of v20, /device:TPU:0, one launch (start us, length us, event | category | flops | bytes accessed | tf_op | source)
XLA Modules:
  0.0 47.1 jit_solution(6296972532011201521)
XLA Ops:
  0.6 2.3 %pick_first.1 = (bf16[17,32,128]{2,1,0:T(8,128)(2,1)S(1)}, bf16[17,32,128]{2,1,0:T(8,128)(2,1)S(1)}, bf16[4,128,128]{2,1,0:T(8,128)(2,1)S(1)}, bf16[4,128,128]{2...) custom-call(bf16[128,2048]{1,0:T(8,128)(2,1)} %refs_0_.9, ...), custom_call_target="tpu_custom_call" | custom-call | flops 67108864 | bytes 2916352 | tf_op jit(solution)/shard_map/pick_first/pallas_call | solution.py:543
  2.9 5.1 %collective-permute-start = (bf16[17,32,128]{2,1,0:T(8,128)(2,1)S(1)}, bf16[17,32,128]{2,1,0:T(8,128)(2,1)S(1)}, u32[]{:S(2)}, u32[]{:S(2)}) collective-permute-start(bf16[17,32,128]{2,1,0:T(8,128)(2,1)S(1)} %get-tuple-element.38), channel_id=1, source_target_pairs={{0,3},{1,2},{2,1},{3,0},{4,7},{5,6},{6,5},{7,4},{8,11},{9,10},{10,... | collective-permute-start | bytes 417800 | tf_op jit(solution)/shard_map/ppermute | solution.py:563
  8.0 2.4 %collective-permute-start.3 = (bf16[4,128,128]{2,1,0:T(8,128)(2,1)S(1)}, bf16[4,128,128]{2,1,0:T(8,128)(2,1)S(1)}, u32[]{:S(2)}, u32[]{:S(2)}) collective-permute-start(bf16[4,128,128]{2,1,0:T(8,128)(2,1)S(1)} %get-tuple-element.43), channel_id=1, source_target_pairs={{0,24},{4,28},{8,16},{12,20},{16,8},{20,12},{24,0},{28,4},{1,25},{... | collective-permute-start | bytes 393224 | tf_op jit(solution)/shard_map/ppermute | solution.py:563
  10.5 0.5 %collective-permute-start.4 = (bf16[4,128,128]{2,1,0:T(8,128)(2,1)S(1)}, bf16[4,128,128]{2,1,0:T(8,128)(2,1)S(1)}, u32[]{:S(2)}, u32[]{:S(2)}) collective-permute-start(bf16[4,128,128]{2,1,0:T(8,128)(2,1)S(1)} %get-tuple-element.44), channel_id=1, source_target_pairs={{0,16},{4,20},{8,24},{12,28},{16,0},{20,4},{24,8},{28,12},{1,17},{... | collective-permute-start | bytes 393224 | tf_op jit(solution)/shard_map/ppermute | solution.py:563
  11.0 0.5 %collective-permute-start.5 = (bf16[4,128,128]{2,1,0:T(8,128)(2,1)S(1)}, bf16[4,128,128]{2,1,0:T(8,128)(2,1)S(1)}, u32[]{:S(2)}, u32[]{:S(2)}) collective-permute-start(bf16[4,128,128]{2,1,0:T(8,128)(2,1)S(1)} %get-tuple-element.45), channel_id=1, source_target_pairs={{0,8},{4,12},{8,0},{12,4},{16,24},{20,28},{24,16},{28,20},{1,9},{5... | collective-permute-start | bytes 393224 | tf_op jit(solution)/shard_map/ppermute | solution.py:563
  11.5 1.7 %pick_second.1 = (bf16[17,32,128]{2,1,0:T(8,128)(2,1)S(1)}, f32[32,128]{1,0:T(8,128)S(1)}) custom-call(bf16[128,2048]{1,0:T(8,128)(2,1)} %refs_0_.9, bf16[128,2048]{1,0:T(8,128)(2,1)} %refs_1_.9, bf16[128,2048]{1,0:T(8,128)(2,1)} %refs_2_.9, bf16[128,2048]{1,0:T(8,128)(2,1)} %refs_3_.9, f32[32,128]{1,0:T(8,128)S(1)} %get-tuple-element.35.refs_4_, ...), custom_call_target="tpu_custom_call" | custom-call | flops 67108864 | bytes 2408448 | tf_op jit(solution)/shard_map/pick_second/pallas_call | solution.py:543
  13.3 1.7 %pick_rest.1 = (bf16[17,32,128]{2,1,0:T(8,128)(2,1)S(1)}, f32[32,128]{1,0:T(8,128)S(1)}) custom-call(bf16[128,2048]{1,0:T(8,128)(2,1)} %refs_0_.9, bf16[128,2048]{1,0:T(8,128)(2,1)} %refs_1_.9, bf16[128,2048]{1,0:T(8,128)(2,1)} %refs_2_.9, bf16[128,2048]{1,0:T(8,128)(2,1)} %refs_3_.9, f32[32,128]{1,0:T(8,128)S(1)} %get-tuple-element.37.refs_4_, ...), custom_call_target="tpu_custom_call" | custom-call | flops 67108864 | bytes 2408448 | tf_op jit(solution)/shard_map/pick_rest/pallas_call | solution.py:543
  15.0 1.2 %collective-permute-start.2 = (bf16[17,32,128]{2,1,0:T(8,128)(2,1)S(1)}, bf16[17,32,128]{2,1,0:T(8,128)(2,1)S(1)}, u32[]{:S(2)}, u32[]{:S(2)}) collective-permute-start(bf16[17,32,128]{2,1,0:T(8,128)(2,1)S(1)} %get-tuple-element.41), channel_id=1, source_target_pairs={{0,1},{1,0},{2,3},{3,2},{4,5},{5,4},{6,7},{7,6},{8,9},{9,8},{10,11... | collective-permute-start | bytes 417800 | tf_op jit(solution)/shard_map/ppermute | solution.py:563
  16.2 0.5 %collective-permute-done.4.refs_2_ = bf16[4,128,128]{2,1,0:T(8,128)(2,1)S(1)} collective-permute-done((bf16[4,128,128]{2,1,0:T(8,128)(2,1)S(1)}, bf16[4,128,128]{2,1,0:T(8,128)(2,1)S(1)}, u32[]{:S(2)}, u32[]{:S(2)}) %collective-permute-start.4) | collective-permute-done | bytes 131104 | tf_op jit(solution)/shard_map/ppermute | solution.py:563
  16.9 1.5 %collective-permute-done.6.refs_4_ = bf16[4,2,128,128]{3,2,1,0:T(8,128)(2,1)S(1)} collective-permute-done((bf16[4,2,128,128]{3,2,1,0:T(8,128)(2,1)S(1)}, bf16[4,2,128,128]{3,2,1,0:T(8,128)(2,1)S(1)}, u32[]{:S(2)}, u32[]{:S(2)}) %collective-permute-start.6) | collective-permute-done | bytes 262176 | tf_op jit(solution)/shard_map/ppermute | solution.py:563
  18.4 1.1 %far_stats.1.refs_5_ = f32[8,128]{1,0:T(8,128)S(1)} custom-call(bf16[4,128,128]{2,1,0:T(8,128)(2,1)S(1)} %get-tuple-element.42.refs_0_, bf16[4,128,128]{2,1,0:T(8,128)(2,1)S(1)} %collective-permute-done.3.refs_1_, bf16[4,128,128]{2,1,0:T(8,128)(2,1)S(1)} %collective-permute-done.4.refs_2_, bf16[4,128,128]{2,1,0:T(8,128)(2,1)S(1)} %collective-permute-done.5.refs_3_, ...), custom_call_target="tpu_custom_call" | custom-call | flops 1 | bytes 794624 | tf_op jit(solution)/shard_map/far_stats/pallas_call | solution.py:543
  19.5 1.0 %collective-permute-done.1.refs_2_ = bf16[17,32,128]{2,1,0:T(8,128)(2,1)S(1)} collective-permute-done((bf16[17,32,128]{2,1,0:T(8,128)(2,1)S(1)}, bf16[17,32,128]{2,1,0:T(8,128)(2,1)S(1)}, u32[]{:S(2)}, u32[]{:S(2)}) %collective-permute-start.1) | collective-permute-done | bytes 139296 | tf_op jit(solution)/shard_map/ppermute | solution.py:563
  20.5 1.4 %collective-permute-done.2.refs_3_ = bf16[17,32,128]{2,1,0:T(8,128)(2,1)S(1)} collective-permute-done((bf16[17,32,128]{2,1,0:T(8,128)(2,1)S(1)}, bf16[17,32,128]{2,1,0:T(8,128)(2,1)S(1)}, u32[]{:S(2)}, u32[]{:S(2)}) %collective-permute-start.2) | collective-permute-done | bytes 139296 | tf_op jit(solution)/shard_map/ppermute | solution.py:563
  21.9 0.5 %middle_stats.1 = (f32[16,128]{1,0:T(8,128)S(1)}, f32[8,128]{1,0:T(8,128)S(1)}, f32[128,128]{1,0:T(8,128)S(1)}) custom-call(bf16[17,32,128]{2,1,0:T(8,128)(2,1)S(1)} %get-tuple-element.36.refs_5_.refs_0_, bf16[17,32,128]{2,1,0:T(8,128)(2,1)S(1)} %collective-permute-done.refs_5_.refs_0_.refs_1_, bf16[17,32,128]{2,1,0:T(8,128)(2,1)S(1)} %collective-permute-done.1.refs_2_, ...), custom_call_target="tpu_custom_call" | custom-call | flops 33554432 | bytes 655360 | tf_op jit(solution)/shard_map/middle_stats/pallas_call | solution.py:543
  22.4 2.5 %collective-permute-start.9 = (f32[16,128]{1,0:T(8,128)S(1)}, f32[16,128]{1,0:T(8,128)S(1)}, u32[]{:S(2)}, u32[]{:S(2)}) collective-permute-start(f32[16,128]{1,0:T(8,128)S(1)} %get-tuple-element.48.refs_6_.refs_8_.refs_5_), channel_id=1, source_target_pairs={{0,24},{4,28},{8,16},{12,20},{16,8},{20,12},{24,0},{28,4},{1,25},{... | collective-permute-start | bytes 24584 | tf_op jit(solution)/shard_map/ppermute | solution.py:563
  24.9 0.5 %collective-permute-start.8 = (f32[16,128]{1,0:T(8,128)S(1)}, f32[16,128]{1,0:T(8,128)S(1)}, u32[]{:S(2)}, u32[]{:S(2)}) collective-permute-start(f32[16,128]{1,0:T(8,128)S(1)} %get-tuple-element.48.refs_6_.refs_8_.refs_5_), channel_id=1, source_target_pairs={{0,16},{4,20},{8,24},{12,28},{16,0},{20,4},{24,8},{28,12},{1,17},{... | collective-permute-start | bytes 24584 | tf_op jit(solution)/shard_map/ppermute | solution.py:563
  25.5 0.5 %collective-permute-start.7 = (f32[16,128]{1,0:T(8,128)S(1)}, f32[16,128]{1,0:T(8,128)S(1)}, u32[]{:S(2)}, u32[]{:S(2)}) collective-permute-start(f32[16,128]{1,0:T(8,128)S(1)} %get-tuple-element.48.refs_6_.refs_8_.refs_5_), channel_id=1, source_target_pairs={{0,8},{4,12},{8,0},{12,4},{16,24},{20,28},{24,16},{28,20},{1,9},{5... | collective-permute-start | bytes 24584 | tf_op jit(solution)/shard_map/ppermute | solution.py:563
  26.0 1.1 %collective-permute-done.9.refs_9_.refs_11_.refs_8_ = f32[16,128]{1,0:T(8,128)S(1)} collective-permute-done((f32[16,128]{1,0:T(8,128)S(1)}, f32[16,128]{1,0:T(8,128)S(1)}, u32[]{:S(2)}, u32[]{:S(2)}) %collective-permute-start.9) | collective-permute-done | bytes 8224 | tf_op jit(solution)/shard_map/ppermute | solution.py:563
  27.1 1.5 %collective-permute-done.8.refs_8_.refs_10_.refs_7_ = f32[16,128]{1,0:T(8,128)S(1)} collective-permute-done((f32[16,128]{1,0:T(8,128)S(1)}, f32[16,128]{1,0:T(8,128)S(1)}, u32[]{:S(2)}, u32[]{:S(2)}) %collective-permute-start.8) | collective-permute-done | bytes 8224 | tf_op jit(solution)/shard_map/ppermute | solution.py:563
  28.6 0.5 %collective-permute-done.7.refs_7_.refs_9_.refs_6_ = f32[16,128]{1,0:T(8,128)S(1)} collective-permute-done((f32[16,128]{1,0:T(8,128)S(1)}, f32[16,128]{1,0:T(8,128)S(1)}, u32[]{:S(2)}, u32[]{:S(2)}) %collective-permute-start.7) | collective-permute-done | bytes 8224 | tf_op jit(solution)/shard_map/ppermute | solution.py:563
  29.1 0.6 %middle_parts.1 = (bf16[17,32,128]{2,1,0:T(8,128)(2,1)S(1)}, bf16[17,32,128]{2,1,0:T(8,128)(2,1)S(1)}, bf16[17,32,128]{2,1,0:T(8,128)(2,1)S(1)}, bf16[17,32,128]{2,1,0:T(8,128)(2,1)S(1)}) custom-call(bf16[17,32,128]{2,1,0:T(8,128)(2,1)S(1)} %get-tuple-element.36.refs_5_.refs_0_, bf16[17,32,128]{2,1,0:T(8,128)(2,1)S(1)} %collective-permute-done.refs_5_.refs_0_.refs_1_, ...), custom_call_target="tpu_custom_call" | custom-call | flops 100663296 | bytes 1216512 | tf_op jit(solution)/shard_map/middle_parts/pallas_call | solution.py:543
  29.7 2.0 %collective-permute-start.10 = (bf16[17,32,128]{2,1,0:T(8,128)(2,1)S(1)}, bf16[17,32,128]{2,1,0:T(8,128)(2,1)S(1)}, u32[]{:S(2)}, u32[]{:S(2)}) collective-permute-start(bf16[17,32,128]{2,1,0:T(8,128)(2,1)S(1)} %get-tuple-element.50), channel_id=1, source_target_pairs={{0,3},{1,2},{2,1},{3,0},{4,7},{5,6},{6,5},{7,4},{8,11},{9,10},{10,... | collective-permute-start | bytes 417800 | tf_op jit(solution)/shard_map/ppermute | solution.py:563
  31.7 2.3 %far_parts.1 = (bf16[4,128,128]{2,1,0:T(8,128)(2,1)S(1)}, bf16[4,128,128]{2,1,0:T(8,128)(2,1)S(1)}, bf16[4,128,128]{2,1,0:T(8,128)(2,1)S(1)}, bf16[4,128,128]{2,...) custom-call(bf16[4,128,128]{2,1,0:T(8,128)(2,1)S(1)} %get-tuple-element.42.refs_0_, ...), custom_call_target="tpu_custom_call" | custom-call | flops 1 | bytes 1 | tf_op jit(solution)/shard_map/far_parts/pallas_call | solution.py:543
  34.2 2.5 %collective-permute-start.16 = (bf16[17,32,128]{2,1,0:T(8,128)(2,1)S(1)}, bf16[17,32,128]{2,1,0:T(8,128)(2,1)S(1)}, u32[]{:S(2)}, u32[]{:S(2)}) collective-permute-start(bf16[17,32,128]{2,1,0:T(8,128)(2,1)S(1)} %get-tuple-element.61), channel_id=1, source_target_pairs={{0,2},{1,3},{2,0},{3,1},{4,6},{5,7},{6,4},{7,5},{8,10},{9,11},{10,... | collective-permute-start | bytes 417800 | tf_op jit(solution)/shard_map/ppermute | solution.py:563
  36.8 1.6 %collective-permute-start.13 = (bf16[4,128,128]{2,1,0:T(8,128)(2,1)S(1)}, bf16[4,128,128]{2,1,0:T(8,128)(2,1)S(1)}, u32[]{:S(2)}, u32[]{:S(2)}) collective-permute-start(bf16[4,128,128]{2,1,0:T(8,128)(2,1)S(1)} %get-tuple-element.58), channel_id=1, source_target_pairs={{0,24},{4,28},{8,16},{12,20},{16,8},{20,12},{24,0},{28,4},{1,25},{... | collective-permute-start | bytes 393224 | tf_op jit(solution)/shard_map/ppermute | solution.py:563
  38.3 0.5 %collective-permute-start.14 = (bf16[4,128,128]{2,1,0:T(8,128)(2,1)S(1)}, bf16[4,128,128]{2,1,0:T(8,128)(2,1)S(1)}, u32[]{:S(2)}, u32[]{:S(2)}) collective-permute-start(bf16[4,128,128]{2,1,0:T(8,128)(2,1)S(1)} %get-tuple-element.59), channel_id=1, source_target_pairs={{0,16},{4,20},{8,24},{12,28},{16,0},{20,4},{24,8},{28,12},{1,17},{... | collective-permute-start | bytes 393224 | tf_op jit(solution)/shard_map/ppermute | solution.py:563
  38.9 1.5 %collective-permute-start.15 = (bf16[4,128,128]{2,1,0:T(8,128)(2,1)S(1)}, bf16[4,128,128]{2,1,0:T(8,128)(2,1)S(1)}, u32[]{:S(2)}, u32[]{:S(2)}) collective-permute-start(bf16[4,128,128]{2,1,0:T(8,128)(2,1)S(1)} %get-tuple-element.60), channel_id=1, source_target_pairs={{0,8},{4,12},{8,0},{12,4},{16,24},{20,28},{24,16},{28,20},{1,9},{5... | collective-permute-start | bytes 393224 | tf_op jit(solution)/shard_map/ppermute | solution.py:563
  40.3 2.1 %collective-permute-done.11.refs_7_ = bf16[17,32,128]{2,1,0:T(8,128)(2,1)S(1)} collective-permute-done((bf16[17,32,128]{2,1,0:T(8,128)(2,1)S(1)}, bf16[17,32,128]{2,1,0:T(8,128)(2,1)S(1)}, u32[]{:S(2)}, u32[]{:S(2)}) %collective-permute-start.11) | collective-permute-done | bytes 139296 | tf_op jit(solution)/shard_map/ppermute | solution.py:563
  42.5 1.4 %near_early.1.refs_5_.early_ref = f32[4,12,128,128]{3,2,1,0:T(8,128)S(1)} custom-call(bf16[128,2048]{1,0:T(8,128)(2,1)S(1)} %copy-done, bf16[128,2048]{1,0:T(8,128)(2,1)S(1)} %copy-done.1, bf16[128,2048]{1,0:T(8,128)(2,1)S(1)} %copy-done.2, bf16[128,2048]{1,0:T(8,128)(2,1)S(1)} %copy-done.3, f32[32,128]{1,0:T(8,128)S(1)} %get-tuple-element.39.refs_0_.refs_4_, ...), custom_call_target="tpu_custom_call" | custom-call | flops 2000000000 | bytes 5709824 | tf_op jit(solution)/shard_map/near_early/pallas_call | solution.py:543
  43.9 0.2 collective-permute-done.16.refs_8_
  44.1 1.9 %final_others.1 = (bf16[128,2048]{1,0:T(8,128)(2,1)}, bf16[128,2048]{1,0:T(8,128)(2,1)}, bf16[128,2048]{1,0:T(8,128)(2,1)}, bf16[128,2048]{1,0:T(8,128)(2,1)}) custom-call(bf16[128,2048]{1,0:T(8,128)(2,1)S(1)} %copy-done, bf16[128,2048]{1,0:T(8,128)(2,1)S(1)} %copy-done.1, bf16[128,2048]{1,0:T(8,128)(2,1)S(1)} %copy-done.2, bf16[128,2048]{1,0:T(8,128)(2,1)S(1)} %copy-done.3, ...), custom_call_target="tpu_custom_call" | custom-call | flops 1000000000 | bytes 7774208 | tf_op jit(solution)/shard_map/final_others/pallas_call | solution.py:543
  46.0 1.1 %final_own.1 = (bf16[128,2048]{1,0:T(8,128)(2,1)}, bf16[128,2048]{1,0:T(8,128)(2,1)}, bf16[128,2048]{1,0:T(8,128)(2,1)}, bf16[128,2048]{1,0:T(8,128)(2,1)}) custom-call(f32[4,12,128,128]{3,2,1,0:T(8,128)S(1)} %near_early.1.refs_5_.early_ref, ...), custom_call_target="tpu_custom_call", output_to_operand_aliasing={{0}: (6, {}), {1}: (7, {}), {2}: (8, {}), {3}: (9, {})} | custom-call | flops 16777216 | bytes 8003584 | tf_op jit(solution)/shard_map/final_own/pallas_call | solution.py:543
  (28 shorter events, 0.5 us)
Async XLA Ops:
  2.9 10.4 %collective-permute-start = (bf16[17,32,128]{2,1,0:T(8,128)(2,1)S(1)}, bf16[17,32,128]{2,1,0:T(8,128)(2,1)S(1)}, u32[]{:S(2)}, u32[]{:S(2)}) collective-permute-start(bf16[17,32,128]{2,1,0:T(8,128)(2,1)S(1)} %get-tuple-element.38), channel_id=1, source_target_pairs={{0,3},{1,2},{2,1},{3,0},{4,7},{5,6},{6,5},{7,4},{8,11},{9,10},{10,... | collective-permute-start | bytes 417800 | tf_op jit(solution)/shard_map/ppermute | solution.py:563
  8.0 8.1 %collective-permute-start.3 = (bf16[4,128,128]{2,1,0:T(8,128)(2,1)S(1)}, bf16[4,128,128]{2,1,0:T(8,128)(2,1)S(1)}, u32[]{:S(2)}, u32[]{:S(2)}) collective-permute-start(bf16[4,128,128]{2,1,0:T(8,128)(2,1)S(1)} %get-tuple-element.43), channel_id=1, source_target_pairs={{0,24},{4,28},{8,16},{12,20},{16,8},{20,12},{24,0},{28,4},{1,25},{... | collective-permute-start | bytes 393224 | tf_op jit(solution)/shard_map/ppermute | solution.py:563
  10.5 6.2 %collective-permute-start.4 = (bf16[4,128,128]{2,1,0:T(8,128)(2,1)S(1)}, bf16[4,128,128]{2,1,0:T(8,128)(2,1)S(1)}, u32[]{:S(2)}, u32[]{:S(2)}) collective-permute-start(bf16[4,128,128]{2,1,0:T(8,128)(2,1)S(1)} %get-tuple-element.44), channel_id=1, source_target_pairs={{0,16},{4,20},{8,24},{12,28},{16,0},{20,4},{24,8},{28,12},{1,17},{... | collective-permute-start | bytes 393224 | tf_op jit(solution)/shard_map/ppermute | solution.py:563
  11.0 5.8 %collective-permute-start.5 = (bf16[4,128,128]{2,1,0:T(8,128)(2,1)S(1)}, bf16[4,128,128]{2,1,0:T(8,128)(2,1)S(1)}, u32[]{:S(2)}, u32[]{:S(2)}) collective-permute-start(bf16[4,128,128]{2,1,0:T(8,128)(2,1)S(1)} %get-tuple-element.45), channel_id=1, source_target_pairs={{0,8},{4,12},{8,0},{12,4},{16,24},{20,28},{24,16},{28,20},{1,9},{5... | collective-permute-start | bytes 393224 | tf_op jit(solution)/shard_map/ppermute | solution.py:563
  13.2 7.3 %collective-permute-start.1 = (bf16[17,32,128]{2,1,0:T(8,128)(2,1)S(1)}, bf16[17,32,128]{2,1,0:T(8,128)(2,1)S(1)}, u32[]{:S(2)}, u32[]{:S(2)}) collective-permute-start(bf16[17,32,128]{2,1,0:T(8,128)(2,1)S(1)} %get-tuple-element.40), channel_id=1, source_target_pairs={{0,2},{1,3},{2,0},{3,1},{4,6},{5,7},{6,4},{7,5},{8,10},{9,11},{10,... | collective-permute-start | bytes 417800 | tf_op jit(solution)/shard_map/ppermute | solution.py:563
  15.0 6.9 %collective-permute-start.2 = (bf16[17,32,128]{2,1,0:T(8,128)(2,1)S(1)}, bf16[17,32,128]{2,1,0:T(8,128)(2,1)S(1)}, u32[]{:S(2)}, u32[]{:S(2)}) collective-permute-start(bf16[17,32,128]{2,1,0:T(8,128)(2,1)S(1)} %get-tuple-element.41), channel_id=1, source_target_pairs={{0,1},{1,0},{2,3},{3,2},{4,5},{5,4},{6,7},{7,6},{8,9},{9,8},{10,11... | collective-permute-start | bytes 417800 | tf_op jit(solution)/shard_map/ppermute | solution.py:563
  16.8 1.6 %collective-permute-start.6 = (bf16[4,2,128,128]{3,2,1,0:T(8,128)(2,1)S(1)}, bf16[4,2,128,128]{3,2,1,0:T(8,128)(2,1)S(1)}, u32[]{:S(2)}, u32[]{:S(2)}) collective-permute-start(bf16[4,2,128,128]{3,2,1,0:T(8,128)(2,1)S(1)} %pack.1), channel_id=1, source_target_pairs={{0,4},{4,0},{8,12},{12,8},{16,20},{20,16},{24,28},{28,24},{1,5},{5... | collective-permute-start | bytes 786440 | tf_op jit(solution)/shard_map/ppermute | solution.py:563
  22.4 4.6 %collective-permute-start.9 = (f32[16,128]{1,0:T(8,128)S(1)}, f32[16,128]{1,0:T(8,128)S(1)}, u32[]{:S(2)}, u32[]{:S(2)}) collective-permute-start(f32[16,128]{1,0:T(8,128)S(1)} %get-tuple-element.48.refs_6_.refs_8_.refs_5_), channel_id=1, source_target_pairs={{0,24},{4,28},{8,16},{12,20},{16,8},{20,12},{24,0},{28,4},{1,25},{... | collective-permute-start | bytes 24584 | tf_op jit(solution)/shard_map/ppermute | solution.py:563
  24.9 3.7 %collective-permute-start.8 = (f32[16,128]{1,0:T(8,128)S(1)}, f32[16,128]{1,0:T(8,128)S(1)}, u32[]{:S(2)}, u32[]{:S(2)}) collective-permute-start(f32[16,128]{1,0:T(8,128)S(1)} %get-tuple-element.48.refs_6_.refs_8_.refs_5_), channel_id=1, source_target_pairs={{0,16},{4,20},{8,24},{12,28},{16,0},{20,4},{24,8},{28,12},{1,17},{... | collective-permute-start | bytes 24584 | tf_op jit(solution)/shard_map/ppermute | solution.py:563
  25.5 3.7 %collective-permute-start.7 = (f32[16,128]{1,0:T(8,128)S(1)}, f32[16,128]{1,0:T(8,128)S(1)}, u32[]{:S(2)}, u32[]{:S(2)}) collective-permute-start(f32[16,128]{1,0:T(8,128)S(1)} %get-tuple-element.48.refs_6_.refs_8_.refs_5_), channel_id=1, source_target_pairs={{0,8},{4,12},{8,0},{12,4},{16,24},{20,28},{24,16},{28,20},{1,9},{5... | collective-permute-start | bytes 24584 | tf_op jit(solution)/shard_map/ppermute | solution.py:563
  29.7 6.9 %collective-permute-start.10 = (bf16[17,32,128]{2,1,0:T(8,128)(2,1)S(1)}, bf16[17,32,128]{2,1,0:T(8,128)(2,1)S(1)}, u32[]{:S(2)}, u32[]{:S(2)}) collective-permute-start(bf16[17,32,128]{2,1,0:T(8,128)(2,1)S(1)} %get-tuple-element.50), channel_id=1, source_target_pairs={{0,3},{1,2},{2,1},{3,0},{4,7},{5,6},{6,5},{7,4},{8,11},{9,10},{10,... | collective-permute-start | bytes 417800 | tf_op jit(solution)/shard_map/ppermute | solution.py:563
  34.0 2.6 %collective-permute-start.12 = (bf16[4,2,128,128]{3,2,1,0:T(8,128)(2,1)S(1)}, bf16[4,2,128,128]{3,2,1,0:T(8,128)(2,1)S(1)}, u32[]{:S(2)}, u32[]{:S(2)}) collective-permute-start(bf16[4,2,128,128]{3,2,1,0:T(8,128)(2,1)S(1)} %get-tuple-element.56), channel_id=1, source_target_pairs={{0,4},{4,0},{8,12},{12,8},{16,20},{20,16},{24,28},{28,24},{1,5},{5... | collective-permute-start | bytes 786440 | tf_op jit(solution)/shard_map/ppermute | solution.py:563
  34.1 8.4 %collective-permute-start.11 = (bf16[17,32,128]{2,1,0:T(8,128)(2,1)S(1)}, bf16[17,32,128]{2,1,0:T(8,128)(2,1)S(1)}, u32[]{:S(2)}, u32[]{:S(2)}) collective-permute-start(bf16[17,32,128]{2,1,0:T(8,128)(2,1)S(1)} %get-tuple-element.51), channel_id=1, source_target_pairs={{0,1},{1,0},{2,3},{3,2},{4,5},{5,4},{6,7},{7,6},{8,9},{9,8},{10,11... | collective-permute-start | bytes 417800 | tf_op jit(solution)/shard_map/ppermute | solution.py:563
  34.2 9.9 %collective-permute-start.16 = (bf16[17,32,128]{2,1,0:T(8,128)(2,1)S(1)}, bf16[17,32,128]{2,1,0:T(8,128)(2,1)S(1)}, u32[]{:S(2)}, u32[]{:S(2)}) collective-permute-start(bf16[17,32,128]{2,1,0:T(8,128)(2,1)S(1)} %get-tuple-element.61), channel_id=1, source_target_pairs={{0,2},{1,3},{2,0},{3,1},{4,6},{5,7},{6,4},{7,5},{8,10},{9,11},{10,... | collective-permute-start | bytes 417800 | tf_op jit(solution)/shard_map/ppermute | solution.py:563
  36.7 5.8 %copy-start = (bf16[128,2048]{1,0:T(8,128)(2,1)S(1)}, bf16[128,2048]{1,0:T(8,128)(2,1)}, u32[]{:S(2)}) copy-start(bf16[128,2048]{1,0:T(8,128)(2,1)} %refs_0_.9) | copy-start | bytes 1572868
  36.7 5.8 %copy-start.1 = (bf16[128,2048]{1,0:T(8,128)(2,1)S(1)}, bf16[128,2048]{1,0:T(8,128)(2,1)}, u32[]{:S(2)}) copy-start(bf16[128,2048]{1,0:T(8,128)(2,1)} %refs_1_.9) | copy-start | bytes 1572868
  36.7 5.8 %copy-start.2 = (bf16[128,2048]{1,0:T(8,128)(2,1)S(1)}, bf16[128,2048]{1,0:T(8,128)(2,1)}, u32[]{:S(2)}) copy-start(bf16[128,2048]{1,0:T(8,128)(2,1)} %refs_2_.9) | copy-start | bytes 1572868
  36.7 5.8 %copy-start.3 = (bf16[128,2048]{1,0:T(8,128)(2,1)S(1)}, bf16[128,2048]{1,0:T(8,128)(2,1)}, u32[]{:S(2)}) copy-start(bf16[128,2048]{1,0:T(8,128)(2,1)} %refs_3_.9) | copy-start | bytes 1572868
  36.8 9.2 %collective-permute-start.13 = (bf16[4,128,128]{2,1,0:T(8,128)(2,1)S(1)}, bf16[4,128,128]{2,1,0:T(8,128)(2,1)S(1)}, u32[]{:S(2)}, u32[]{:S(2)}) collective-permute-start(bf16[4,128,128]{2,1,0:T(8,128)(2,1)S(1)} %get-tuple-element.58), channel_id=1, source_target_pairs={{0,24},{4,28},{8,16},{12,20},{16,8},{20,12},{24,0},{28,4},{1,25},{... | collective-permute-start | bytes 393224 | tf_op jit(solution)/shard_map/ppermute | solution.py:563
  38.3 7.6 %collective-permute-start.14 = (bf16[4,128,128]{2,1,0:T(8,128)(2,1)S(1)}, bf16[4,128,128]{2,1,0:T(8,128)(2,1)S(1)}, u32[]{:S(2)}, u32[]{:S(2)}) collective-permute-start(bf16[4,128,128]{2,1,0:T(8,128)(2,1)S(1)} %get-tuple-element.59), channel_id=1, source_target_pairs={{0,16},{4,20},{8,24},{12,28},{16,0},{20,4},{24,8},{28,12},{1,17},{... | collective-permute-start | bytes 393224 | tf_op jit(solution)/shard_map/ppermute | solution.py:563
  38.9 7.1 %collective-permute-start.15 = (bf16[4,128,128]{2,1,0:T(8,128)(2,1)S(1)}, bf16[4,128,128]{2,1,0:T(8,128)(2,1)S(1)}, u32[]{:S(2)}, u32[]{:S(2)}) collective-permute-start(bf16[4,128,128]{2,1,0:T(8,128)(2,1)S(1)} %get-tuple-element.60), channel_id=1, source_target_pairs={{0,8},{4,12},{8,0},{12,4},{16,24},{20,28},{24,16},{28,20},{1,9},{5... | collective-permute-start | bytes 393224 | tf_op jit(solution)/shard_map/ppermute | solution.py:563

commit v21 on v18

--- a/solution.py
+++ b/solution.py
@@ -227,8 +227,8 @@
 def far_stats_kernel(slots, *refs):
     fulls, sibs, stats_ref = in_back(refs[:slots]), refs[slots:-2], refs[-1]
     keys, values = far_keys(fulls, sibs, 0), far_keys(fulls, sibs, 1)
-    for m in range(slots):
-        ((e, d),) = level_stats([(keys, values, fulls[m][2], fulls[m][3])])
+    operands = [(keys, values, ref[2], ref[3]) for ref in fulls]
+    for m, (e, d) in enumerate(level_stats(operands)):
         stats_ref[m : m + 1, :] = e
         stats_ref[slots + m : slots + m + 1, :] = d
 
@@ -324,19 +324,23 @@
     rows = fulls[0].shape[1]
     _, chip = position(slots)
     keys, values = far_keys(fulls, sibs, 0), far_keys(fulls, sibs, 1)
-    for m in range(slots):
-        lse, delta = merge_stats(
+    merged = [
+        merge_stats(
             xmsgs[m][pl.ds(chip, 1), :],
             xmsgs[m][pl.ds(slots + chip, 1), :],
             xmsgs[0][2 * slots + m : 2 * slots + m + 1, :],
             xmsgs[0][3 * slots + m : 3 * slots + m + 1, :],
         )
-        operands = (keys, values, fulls[m][2], fulls[m][3])
-        ((p, ds),) = level_weights([operands], [(lse, delta)])
+        for m in range(slots)
+    ]
+    operands = [(keys, values, ref[2], ref[3]) for ref in fulls]
+    found = level_weights(operands, merged)
+    for m, (p, ds) in enumerate(found):
+        weights[:, m * rows : (m + 1) * rows] = p
+        score_grads[:, m * rows : (m + 1) * rows] = ds
+    for m, (p, ds) in enumerate(found):
         outs[m][0] = dot_tn(p, values).astype(BF16)
         outs[m][1] = (dot_tn(ds, keys) * SCALE).astype(BF16)
-        weights[:, m * rows : (m + 1) * rows] = p
-        score_grads[:, m * rows : (m + 1) * rows] = ds
     queries = jnp.concatenate([ref[2] for ref in fulls], axis=0)
     ups = jnp.concatenate([ref[3] for ref in fulls], axis=0)
     key_part = (dot(score_grads[...], queries) * SCALE).astype(BF16)
@@ -498,12 +502,13 @@
     mids, refs = refs[: n_i - 1], refs[n_i - 1 :]
     outs, (ready, sems, stats_ref, spread) = refs[:4], refs[4:]
     last = n_i - 1
-    near_statistics(n_i, slots, [last], near_ref, mids[-1:], (), stats_ref, spread)
-    late = near_place(n_i, slots, last, sources, stats_ref)
     copies = []
     for step in range(1, n_i):
         first = first_back(n_i, slots, step)
         found = [spread_rows(slots, first + slot, slot, mids[step - 1]) for slot in range(slots)]
+        if step == last:
+            near_statistics(n_i, slots, [last], near_ref, mids[-1:], (), stats_ref, spread)
+            late = near_place(n_i, slots, last, sources, stats_ref)
         for slot, parts in enumerate(found):
             for which in range(4):
                 near = late[slot][which] if step == last else early_ref[which, step * slots + slot]

time: 46.4 us -> 46.2 us (level)
  transfers between devices with their start and end apart: 17 -> 17, of which waited for: 10 -> 10; matrix products, arithmetic and copies ran while one was open for 0% -> 0% of each run, Pallas kernels for 20% -> 19%
where the time goes in v21:
time: 46.2 us; the launch traced here: 46.1 us
  starting transfers between devices  21.1 us (46%)
  Pallas kernels  13.3 us (29%)
  waiting for transfers between devices  10.8 us (23%)
  between operations  0.83 us (2%)
    ppermute x17, starting transfers between devices, swap(): return lax.ppermute(x, axis, [(i, i ^ mask) for i in range(n)])  21.1 us
    pallas_call x17, Pallas kernels, call(): pl.pallas_call(kernel, out_shape=tuple(outs), in_specs=[pl.BlockSpec(memo...  13.3 us
    ppermute x17, waiting for transfers between devices, swap(): return lax.ppermute(x, axis, [(i, i ^ mask) for i in range(n)])  10.8 us
  transfers between devices with their start and end apart: 17, of which 10 were waited for; matrix products, arithmetic and copies ran while one was open for 0% of the time, Pallas kernels for 19%

profile of v21, /device:TPU:0, one launch (start us, length us, event | category | flops | bytes accessed | tf_op | source)
XLA Modules:
  0.0 46.1 jit_solution(4362513651145602799)
XLA Ops:
  0.6 2.3 %pick_first.1 = (bf16[17,32,128]{2,1,0:T(8,128)(2,1)S(1)}, bf16[17,32,128]{2,1,0:T(8,128)(2,1)S(1)}, bf16[4,128,128]{2,1,0:T(8,128)(2,1)S(1)}, bf16[4,128,128]{2...) custom-call(bf16[128,2048]{1,0:T(8,128)(2,1)} %refs_0_.7, ...), custom_call_target="tpu_custom_call" | custom-call | flops 67108864 | bytes 2916352 | tf_op jit(solution)/shard_map/pick_first/pallas_call | solution.py:547
  2.9 5.1 %collective-permute-start = (bf16[17,32,128]{2,1,0:T(8,128)(2,1)S(1)}, bf16[17,32,128]{2,1,0:T(8,128)(2,1)S(1)}, u32[]{:S(2)}, u32[]{:S(2)}) collective-permute-start(bf16[17,32,128]{2,1,0:T(8,128)(2,1)S(1)} %get-tuple-element.37), channel_id=1, source_target_pairs={{0,3},{1,2},{2,1},{3,0},{4,7},{5,6},{6,5},{7,4},{8,11},{9,10},{10,... | collective-permute-start | bytes 417800 | tf_op jit(solution)/shard_map/ppermute | solution.py:567
  8.0 2.4 %collective-permute-start.3 = (bf16[4,128,128]{2,1,0:T(8,128)(2,1)S(1)}, bf16[4,128,128]{2,1,0:T(8,128)(2,1)S(1)}, u32[]{:S(2)}, u32[]{:S(2)}) collective-permute-start(bf16[4,128,128]{2,1,0:T(8,128)(2,1)S(1)} %get-tuple-element.41), channel_id=1, source_target_pairs={{0,24},{4,28},{8,16},{12,20},{16,8},{20,12},{24,0},{28,4},{1,25},{... | collective-permute-start | bytes 393224 | tf_op jit(solution)/shard_map/ppermute | solution.py:567
  10.5 0.5 %collective-permute-start.4 = (bf16[4,128,128]{2,1,0:T(8,128)(2,1)S(1)}, bf16[4,128,128]{2,1,0:T(8,128)(2,1)S(1)}, u32[]{:S(2)}, u32[]{:S(2)}) collective-permute-start(bf16[4,128,128]{2,1,0:T(8,128)(2,1)S(1)} %get-tuple-element.42), channel_id=1, source_target_pairs={{0,16},{4,20},{8,24},{12,28},{16,0},{20,4},{24,8},{28,12},{1,17},{... | collective-permute-start | bytes 393224 | tf_op jit(solution)/shard_map/ppermute | solution.py:567
  11.0 0.5 %collective-permute-start.5 = (bf16[4,128,128]{2,1,0:T(8,128)(2,1)S(1)}, bf16[4,128,128]{2,1,0:T(8,128)(2,1)S(1)}, u32[]{:S(2)}, u32[]{:S(2)}) collective-permute-start(bf16[4,128,128]{2,1,0:T(8,128)(2,1)S(1)} %get-tuple-element.43), channel_id=1, source_target_pairs={{0,8},{4,12},{8,0},{12,4},{16,24},{20,28},{24,16},{28,20},{1,9},{5... | collective-permute-start | bytes 393224 | tf_op jit(solution)/shard_map/ppermute | solution.py:567
  11.5 2.1 %pick_rest.1 = (bf16[17,32,128]{2,1,0:T(8,128)(2,1)S(1)}, bf16[17,32,128]{2,1,0:T(8,128)(2,1)S(1)}, f32[32,128]{1,0:T(8,128)S(1)}) custom-call(bf16[128,2048]{1,0:T(8,128)(2,1)} %refs_0_.7, bf16[128,2048]{1,0:T(8,128)(2,1)} %refs_1_.7, bf16[128,2048]{1,0:T(8,128)(2,1)} %refs_2_.7, bf16[128,2048]{1,0:T(8,128)(2,1)} %refs_3_.7, ...), custom_call_target="tpu_custom_call" | custom-call | flops 134217728 | bytes 2408448 | tf_op jit(solution)/shard_map/pick_rest/pallas_call | solution.py:547
  13.8 0.6 %collective-permute-start.2 = (bf16[17,32,128]{2,1,0:T(8,128)(2,1)S(1)}, bf16[17,32,128]{2,1,0:T(8,128)(2,1)S(1)}, u32[]{:S(2)}, u32[]{:S(2)}) collective-permute-start(bf16[17,32,128]{2,1,0:T(8,128)(2,1)S(1)} %get-tuple-element.39), channel_id=1, source_target_pairs={{0,1},{1,0},{2,3},{3,2},{4,5},{5,4},{6,7},{7,6},{8,9},{9,8},{10,11... | collective-permute-start | bytes 417800 | tf_op jit(solution)/shard_map/ppermute | solution.py:567
  14.4 2.3 %collective-permute-done.4.refs_2_ = bf16[4,128,128]{2,1,0:T(8,128)(2,1)S(1)} collective-permute-done((bf16[4,128,128]{2,1,0:T(8,128)(2,1)S(1)}, bf16[4,128,128]{2,1,0:T(8,128)(2,1)S(1)}, u32[]{:S(2)}, u32[]{:S(2)}) %collective-permute-start.4) | collective-permute-done | bytes 131104 | tf_op jit(solution)/shard_map/ppermute | solution.py:567
  16.9 1.5 %collective-permute-done.6.refs_4_ = bf16[4,2,128,128]{3,2,1,0:T(8,128)(2,1)S(1)} collective-permute-done((bf16[4,2,128,128]{3,2,1,0:T(8,128)(2,1)S(1)}, bf16[4,2,128,128]{3,2,1,0:T(8,128)(2,1)S(1)}, u32[]{:S(2)}, u32[]{:S(2)}) %collective-permute-start.6) | collective-permute-done | bytes 262176 | tf_op jit(solution)/shard_map/ppermute | solution.py:567
  18.4 1.1 %far_stats.1.refs_5_ = f32[8,128]{1,0:T(8,128)S(1)} custom-call(bf16[4,128,128]{2,1,0:T(8,128)(2,1)S(1)} %get-tuple-element.40.refs_0_, bf16[4,128,128]{2,1,0:T(8,128)(2,1)S(1)} %collective-permute-done.3.refs_1_, bf16[4,128,128]{2,1,0:T(8,128)(2,1)S(1)} %collective-permute-done.4.refs_2_, bf16[4,128,128]{2,1,0:T(8,128)(2,1)S(1)} %collective-permute-done.5.refs_3_, ...), custom_call_target="tpu_custom_call" | custom-call | flops 1 | bytes 794624 | tf_op jit(solution)/shard_map/far_stats/pallas_call | solution.py:547
  19.5 1.4 %collective-permute-done.1.refs_2_ = bf16[17,32,128]{2,1,0:T(8,128)(2,1)S(1)} collective-permute-done((bf16[17,32,128]{2,1,0:T(8,128)(2,1)S(1)}, bf16[17,32,128]{2,1,0:T(8,128)(2,1)S(1)}, u32[]{:S(2)}, u32[]{:S(2)}) %collective-permute-start.1) | collective-permute-done | bytes 139296 | tf_op jit(solution)/shard_map/ppermute | solution.py:567
  21.0 0.1 collective-permute-done.2.refs_3_
  21.1 0.5 %middle_stats.1 = (f32[16,128]{1,0:T(8,128)S(1)}, f32[8,128]{1,0:T(8,128)S(1)}, f32[128,128]{1,0:T(8,128)S(1)}) custom-call(bf16[17,32,128]{2,1,0:T(8,128)(2,1)S(1)} %get-tuple-element.36.refs_0_, bf16[17,32,128]{2,1,0:T(8,128)(2,1)S(1)} %collective-permute-done.refs_0_.refs_1_, bf16[17,32,128]{2,1,0:T(8,128)(2,1)S(1)} %collective-permute-done.1.refs_2_, ...), custom_call_target="tpu_custom_call" | custom-call | flops 33554432 | bytes 655360 | tf_op jit(solution)/shard_map/middle_stats/pallas_call | solution.py:547
  21.6 2.5 %collective-permute-start.9 = (f32[16,128]{1,0:T(8,128)S(1)}, f32[16,128]{1,0:T(8,128)S(1)}, u32[]{:S(2)}, u32[]{:S(2)}) collective-permute-start(f32[16,128]{1,0:T(8,128)S(1)} %get-tuple-element.46.refs_6_.refs_8_.refs_5_), channel_id=1, source_target_pairs={{0,24},{4,28},{8,16},{12,20},{16,8},{20,12},{24,0},{28,4},{1,25},{... | collective-permute-start | bytes 24584 | tf_op jit(solution)/shard_map/ppermute | solution.py:567
  24.1 0.5 %collective-permute-start.8 = (f32[16,128]{1,0:T(8,128)S(1)}, f32[16,128]{1,0:T(8,128)S(1)}, u32[]{:S(2)}, u32[]{:S(2)}) collective-permute-start(f32[16,128]{1,0:T(8,128)S(1)} %get-tuple-element.46.refs_6_.refs_8_.refs_5_), channel_id=1, source_target_pairs={{0,16},{4,20},{8,24},{12,28},{16,0},{20,4},{24,8},{28,12},{1,17},{... | collective-permute-start | bytes 24584 | tf_op jit(solution)/shard_map/ppermute | solution.py:567
  24.6 0.5 %collective-permute-start.7 = (f32[16,128]{1,0:T(8,128)S(1)}, f32[16,128]{1,0:T(8,128)S(1)}, u32[]{:S(2)}, u32[]{:S(2)}) collective-permute-start(f32[16,128]{1,0:T(8,128)S(1)} %get-tuple-element.46.refs_6_.refs_8_.refs_5_), channel_id=1, source_target_pairs={{0,8},{4,12},{8,0},{12,4},{16,24},{20,28},{24,16},{28,20},{1,9},{5... | collective-permute-start | bytes 24584 | tf_op jit(solution)/shard_map/ppermute | solution.py:567
  25.2 1.1 %collective-permute-done.9.refs_9_.refs_11_.refs_8_ = f32[16,128]{1,0:T(8,128)S(1)} collective-permute-done((f32[16,128]{1,0:T(8,128)S(1)}, f32[16,128]{1,0:T(8,128)S(1)}, u32[]{:S(2)}, u32[]{:S(2)}) %collective-permute-start.9) | collective-permute-done | bytes 8224 | tf_op jit(solution)/shard_map/ppermute | solution.py:567
  26.2 1.5 %collective-permute-done.8.refs_8_.refs_10_.refs_7_ = f32[16,128]{1,0:T(8,128)S(1)} collective-permute-done((f32[16,128]{1,0:T(8,128)S(1)}, f32[16,128]{1,0:T(8,128)S(1)}, u32[]{:S(2)}, u32[]{:S(2)}) %collective-permute-start.8) | collective-permute-done | bytes 8224 | tf_op jit(solution)/shard_map/ppermute | solution.py:567
  27.8 0.5 %collective-permute-done.7.refs_7_.refs_9_.refs_6_ = f32[16,128]{1,0:T(8,128)S(1)} collective-permute-done((f32[16,128]{1,0:T(8,128)S(1)}, f32[16,128]{1,0:T(8,128)S(1)}, u32[]{:S(2)}, u32[]{:S(2)}) %collective-permute-start.7) | collective-permute-done | bytes 8224 | tf_op jit(solution)/shard_map/ppermute | solution.py:567
  28.3 0.6 %middle_parts.1 = (bf16[17,32,128]{2,1,0:T(8,128)(2,1)S(1)}, bf16[17,32,128]{2,1,0:T(8,128)(2,1)S(1)}, bf16[17,32,128]{2,1,0:T(8,128)(2,1)S(1)}, bf16[17,32,128]{2,1,0:T(8,128)(2,1)S(1)}) custom-call(bf16[17,32,128]{2,1,0:T(8,128)(2,1)S(1)} %get-tuple-element.36.refs_0_, bf16[17,32,128]{2,1,0:T(8,128)(2,1)S(1)} %collective-permute-done.refs_0_.refs_1_, ...), custom_call_target="tpu_custom_call" | custom-call | flops 100663296 | bytes 1216512 | tf_op jit(solution)/shard_map/middle_parts/pallas_call | solution.py:547
  28.9 1.5 %collective-permute-start.10 = (bf16[17,32,128]{2,1,0:T(8,128)(2,1)S(1)}, bf16[17,32,128]{2,1,0:T(8,128)(2,1)S(1)}, u32[]{:S(2)}, u32[]{:S(2)}) collective-permute-start(bf16[17,32,128]{2,1,0:T(8,128)(2,1)S(1)} %get-tuple-element.48), channel_id=1, source_target_pairs={{0,3},{1,2},{2,1},{3,0},{4,7},{5,6},{6,5},{7,4},{8,11},{9,10},{10,... | collective-permute-start | bytes 417800 | tf_op jit(solution)/shard_map/ppermute | solution.py:567
  30.4 2.1 %far_parts.1 = (bf16[4,128,128]{2,1,0:T(8,128)(2,1)S(1)}, bf16[4,128,128]{2,1,0:T(8,128)(2,1)S(1)}, bf16[4,128,128]{2,1,0:T(8,128)(2,1)S(1)}, bf16[4,128,128]{2,...) custom-call(bf16[4,128,128]{2,1,0:T(8,128)(2,1)S(1)} %get-tuple-element.40.refs_0_, ...), custom_call_target="tpu_custom_call" | custom-call | flops 1 | bytes 1 | tf_op jit(solution)/shard_map/far_parts/pallas_call | solution.py:547
  32.6 0.3 collective-permute-start.11
  32.9 2.8 %collective-permute-start.16 = (bf16[17,32,128]{2,1,0:T(8,128)(2,1)S(1)}, bf16[17,32,128]{2,1,0:T(8,128)(2,1)S(1)}, u32[]{:S(2)}, u32[]{:S(2)}) collective-permute-start(bf16[17,32,128]{2,1,0:T(8,128)(2,1)S(1)} %get-tuple-element.59), channel_id=1, source_target_pairs={{0,2},{1,3},{2,0},{3,1},{4,6},{5,7},{6,4},{7,5},{8,10},{9,11},{10,... | collective-permute-start | bytes 417800 | tf_op jit(solution)/shard_map/ppermute | solution.py:567
  35.6 0.2 collective-permute-done.10.refs_6_.refs_0_
  36.0 1.6 %collective-permute-start.13 = (bf16[4,128,128]{2,1,0:T(8,128)(2,1)S(1)}, bf16[4,128,128]{2,1,0:T(8,128)(2,1)S(1)}, u32[]{:S(2)}, u32[]{:S(2)}) collective-permute-start(bf16[4,128,128]{2,1,0:T(8,128)(2,1)S(1)} %get-tuple-element.56), channel_id=1, source_target_pairs={{0,24},{4,28},{8,16},{12,20},{16,8},{20,12},{24,0},{28,4},{1,25},{... | collective-permute-start | bytes 393224 | tf_op jit(solution)/shard_map/ppermute | solution.py:567
  37.5 0.5 %collective-permute-start.14 = (bf16[4,128,128]{2,1,0:T(8,128)(2,1)S(1)}, bf16[4,128,128]{2,1,0:T(8,128)(2,1)S(1)}, u32[]{:S(2)}, u32[]{:S(2)}) collective-permute-start(bf16[4,128,128]{2,1,0:T(8,128)(2,1)S(1)} %get-tuple-element.57), channel_id=1, source_target_pairs={{0,16},{4,20},{8,24},{12,28},{16,0},{20,4},{24,8},{28,12},{1,17},{... | collective-permute-start | bytes 393224 | tf_op jit(solution)/shard_map/ppermute | solution.py:567
  38.1 1.5 %collective-permute-start.15 = (bf16[4,128,128]{2,1,0:T(8,128)(2,1)S(1)}, bf16[4,128,128]{2,1,0:T(8,128)(2,1)S(1)}, u32[]{:S(2)}, u32[]{:S(2)}) collective-permute-start(bf16[4,128,128]{2,1,0:T(8,128)(2,1)S(1)} %get-tuple-element.58), channel_id=1, source_target_pairs={{0,8},{4,12},{8,0},{12,4},{16,24},{20,28},{24,16},{28,20},{1,9},{5... | collective-permute-start | bytes 393224 | tf_op jit(solution)/shard_map/ppermute | solution.py:567
  39.5 2.0 %collective-permute-done.11.refs_7_ = bf16[17,32,128]{2,1,0:T(8,128)(2,1)S(1)} collective-permute-done((bf16[17,32,128]{2,1,0:T(8,128)(2,1)S(1)}, bf16[17,32,128]{2,1,0:T(8,128)(2,1)S(1)}, u32[]{:S(2)}, u32[]{:S(2)}) %collective-permute-start.11) | collective-permute-done | bytes 139296 | tf_op jit(solution)/shard_map/ppermute | solution.py:567
  41.6 1.4 %near_early.1.refs_5_.early_ref = f32[4,12,128,128]{3,2,1,0:T(8,128)S(1)} custom-call(bf16[128,2048]{1,0:T(8,128)(2,1)S(1)} %copy-done, bf16[128,2048]{1,0:T(8,128)(2,1)S(1)} %copy-done.1, bf16[128,2048]{1,0:T(8,128)(2,1)S(1)} %copy-done.2, bf16[128,2048]{1,0:T(8,128)(2,1)S(1)} %copy-done.3, f32[32,128]{1,0:T(8,128)S(1)} %get-tuple-element.35.refs_0_.refs_4_, ...), custom_call_target="tpu_custom_call" | custom-call | flops 2000000000 | bytes 5709824 | tf_op jit(solution)/shard_map/near_early/pallas_call | solution.py:547
  43.0 1.9 %final_others.1 = (bf16[128,2048]{1,0:T(8,128)(2,1)}, bf16[128,2048]{1,0:T(8,128)(2,1)}, bf16[128,2048]{1,0:T(8,128)(2,1)}, bf16[128,2048]{1,0:T(8,128)(2,1)}) custom-call(bf16[128,2048]{1,0:T(8,128)(2,1)S(1)} %copy-done, bf16[128,2048]{1,0:T(8,128)(2,1)S(1)} %copy-done.1, bf16[128,2048]{1,0:T(8,128)(2,1)S(1)} %copy-done.2, bf16[128,2048]{1,0:T(8,128)(2,1)S(1)} %copy-done.3, ...), custom_call_target="tpu_custom_call" | custom-call | flops 1000000000 | bytes 7774208 | tf_op jit(solution)/shard_map/final_others/pallas_call | solution.py:547
  45.0 1.1 %final_own.1 = (bf16[128,2048]{1,0:T(8,128)(2,1)}, bf16[128,2048]{1,0:T(8,128)(2,1)}, bf16[128,2048]{1,0:T(8,128)(2,1)}, bf16[128,2048]{1,0:T(8,128)(2,1)}) custom-call(f32[4,12,128,128]{3,2,1,0:T(8,128)S(1)} %near_early.1.refs_5_.early_ref, ...), custom_call_target="tpu_custom_call", output_to_operand_aliasing={{0}: (6, {}), {1}: (7, {}), {2}: (8, {}), {3}: (9, {})} | custom-call | flops 16777216 | bytes 8003584 | tf_op jit(solution)/shard_map/final_own/pallas_call | solution.py:547
  (27 shorter events, 0.4 us)
Async XLA Ops:
  2.9 10.8 %collective-permute-start = (bf16[17,32,128]{2,1,0:T(8,128)(2,1)S(1)}, bf16[17,32,128]{2,1,0:T(8,128)(2,1)S(1)}, u32[]{:S(2)}, u32[]{:S(2)}) collective-permute-start(bf16[17,32,128]{2,1,0:T(8,128)(2,1)S(1)} %get-tuple-element.37), channel_id=1, source_target_pairs={{0,3},{1,2},{2,1},{3,0},{4,7},{5,6},{6,5},{7,4},{8,11},{9,10},{10,... | collective-permute-start | bytes 417800 | tf_op jit(solution)/shard_map/ppermute | solution.py:567
  8.0 6.4 %collective-permute-start.3 = (bf16[4,128,128]{2,1,0:T(8,128)(2,1)S(1)}, bf16[4,128,128]{2,1,0:T(8,128)(2,1)S(1)}, u32[]{:S(2)}, u32[]{:S(2)}) collective-permute-start(bf16[4,128,128]{2,1,0:T(8,128)(2,1)S(1)} %get-tuple-element.41), channel_id=1, source_target_pairs={{0,24},{4,28},{8,16},{12,20},{16,8},{20,12},{24,0},{28,4},{1,25},{... | collective-permute-start | bytes 393224 | tf_op jit(solution)/shard_map/ppermute | solution.py:567
  10.5 6.2 %collective-permute-start.4 = (bf16[4,128,128]{2,1,0:T(8,128)(2,1)S(1)}, bf16[4,128,128]{2,1,0:T(8,128)(2,1)S(1)}, u32[]{:S(2)}, u32[]{:S(2)}) collective-permute-start(bf16[4,128,128]{2,1,0:T(8,128)(2,1)S(1)} %get-tuple-element.42), channel_id=1, source_target_pairs={{0,16},{4,20},{8,24},{12,28},{16,0},{20,4},{24,8},{28,12},{1,17},{... | collective-permute-start | bytes 393224 | tf_op jit(solution)/shard_map/ppermute | solution.py:567
  11.0 5.8 %collective-permute-start.5 = (bf16[4,128,128]{2,1,0:T(8,128)(2,1)S(1)}, bf16[4,128,128]{2,1,0:T(8,128)(2,1)S(1)}, u32[]{:S(2)}, u32[]{:S(2)}) collective-permute-start(bf16[4,128,128]{2,1,0:T(8,128)(2,1)S(1)} %get-tuple-element.43), channel_id=1, source_target_pairs={{0,8},{4,12},{8,0},{12,4},{16,24},{20,28},{24,16},{28,20},{1,9},{5... | collective-permute-start | bytes 393224 | tf_op jit(solution)/shard_map/ppermute | solution.py:567
  13.7 7.3 %collective-permute-start.1 = (bf16[17,32,128]{2,1,0:T(8,128)(2,1)S(1)}, bf16[17,32,128]{2,1,0:T(8,128)(2,1)S(1)}, u32[]{:S(2)}, u32[]{:S(2)}) collective-permute-start(bf16[17,32,128]{2,1,0:T(8,128)(2,1)S(1)} %get-tuple-element.38), channel_id=1, source_target_pairs={{0,2},{1,3},{2,0},{3,1},{4,6},{5,7},{6,4},{7,5},{8,10},{9,11},{10,... | collective-permute-start | bytes 417800 | tf_op jit(solution)/shard_map/ppermute | solution.py:567
  13.8 7.3 %collective-permute-start.2 = (bf16[17,32,128]{2,1,0:T(8,128)(2,1)S(1)}, bf16[17,32,128]{2,1,0:T(8,128)(2,1)S(1)}, u32[]{:S(2)}, u32[]{:S(2)}) collective-permute-start(bf16[17,32,128]{2,1,0:T(8,128)(2,1)S(1)} %get-tuple-element.39), channel_id=1, source_target_pairs={{0,1},{1,0},{2,3},{3,2},{4,5},{5,4},{6,7},{7,6},{8,9},{9,8},{10,11... | collective-permute-start | bytes 417800 | tf_op jit(solution)/shard_map/ppermute | solution.py:567
  16.8 1.6 %collective-permute-start.6 = (bf16[4,2,128,128]{3,2,1,0:T(8,128)(2,1)S(1)}, bf16[4,2,128,128]{3,2,1,0:T(8,128)(2,1)S(1)}, u32[]{:S(2)}, u32[]{:S(2)}) collective-permute-start(bf16[4,2,128,128]{3,2,1,0:T(8,128)(2,1)S(1)} %pack.1), channel_id=1, source_target_pairs={{0,4},{4,0},{8,12},{12,8},{16,20},{20,16},{24,28},{28,24},{1,5},{5... | collective-permute-start | bytes 786440 | tf_op jit(solution)/shard_map/ppermute | solution.py:567
  21.6 4.6 %collective-permute-start.9 = (f32[16,128]{1,0:T(8,128)S(1)}, f32[16,128]{1,0:T(8,128)S(1)}, u32[]{:S(2)}, u32[]{:S(2)}) collective-permute-start(f32[16,128]{1,0:T(8,128)S(1)} %get-tuple-element.46.refs_6_.refs_8_.refs_5_), channel_id=1, source_target_pairs={{0,24},{4,28},{8,16},{12,20},{16,8},{20,12},{24,0},{28,4},{1,25},{... | collective-permute-start | bytes 24584 | tf_op jit(solution)/shard_map/ppermute | solution.py:567
  24.1 3.7 %collective-permute-start.8 = (f32[16,128]{1,0:T(8,128)S(1)}, f32[16,128]{1,0:T(8,128)S(1)}, u32[]{:S(2)}, u32[]{:S(2)}) collective-permute-start(f32[16,128]{1,0:T(8,128)S(1)} %get-tuple-element.46.refs_6_.refs_8_.refs_5_), channel_id=1, source_target_pairs={{0,16},{4,20},{8,24},{12,28},{16,0},{20,4},{24,8},{28,12},{1,17},{... | collective-permute-start | bytes 24584 | tf_op jit(solution)/shard_map/ppermute | solution.py:567
  24.6 3.7 %collective-permute-start.7 = (f32[16,128]{1,0:T(8,128)S(1)}, f32[16,128]{1,0:T(8,128)S(1)}, u32[]{:S(2)}, u32[]{:S(2)}) collective-permute-start(f32[16,128]{1,0:T(8,128)S(1)} %get-tuple-element.46.refs_6_.refs_8_.refs_5_), channel_id=1, source_target_pairs={{0,8},{4,12},{8,0},{12,4},{16,24},{20,28},{24,16},{28,20},{1,9},{5... | collective-permute-start | bytes 24584 | tf_op jit(solution)/shard_map/ppermute | solution.py:567
  28.9 6.9 %collective-permute-start.10 = (bf16[17,32,128]{2,1,0:T(8,128)(2,1)S(1)}, bf16[17,32,128]{2,1,0:T(8,128)(2,1)S(1)}, u32[]{:S(2)}, u32[]{:S(2)}) collective-permute-start(bf16[17,32,128]{2,1,0:T(8,128)(2,1)S(1)} %get-tuple-element.48), channel_id=1, source_target_pairs={{0,3},{1,2},{2,1},{3,0},{4,7},{5,6},{6,5},{7,4},{8,11},{9,10},{10,... | collective-permute-start | bytes 417800 | tf_op jit(solution)/shard_map/ppermute | solution.py:567
  32.5 3.3 %collective-permute-start.12 = (bf16[4,2,128,128]{3,2,1,0:T(8,128)(2,1)S(1)}, bf16[4,2,128,128]{3,2,1,0:T(8,128)(2,1)S(1)}, u32[]{:S(2)}, u32[]{:S(2)}) collective-permute-start(bf16[4,2,128,128]{3,2,1,0:T(8,128)(2,1)S(1)} %get-tuple-element.54), channel_id=1, source_target_pairs={{0,4},{4,0},{8,12},{12,8},{16,20},{20,16},{24,28},{28,24},{1,5},{5... | collective-permute-start | bytes 786440 | tf_op jit(solution)/shard_map/ppermute | solution.py:567
  32.6 9.0 %collective-permute-start.11 = (bf16[17,32,128]{2,1,0:T(8,128)(2,1)S(1)}, bf16[17,32,128]{2,1,0:T(8,128)(2,1)S(1)}, u32[]{:S(2)}, u32[]{:S(2)}) collective-permute-start(bf16[17,32,128]{2,1,0:T(8,128)(2,1)S(1)} %get-tuple-element.49), channel_id=1, source_target_pairs={{0,1},{1,0},{2,3},{3,2},{4,5},{5,4},{6,7},{7,6},{8,9},{9,8},{10,11... | collective-permute-start | bytes 417800 | tf_op jit(solution)/shard_map/ppermute | solution.py:567
  32.9 10.2 %collective-permute-start.16 = (bf16[17,32,128]{2,1,0:T(8,128)(2,1)S(1)}, bf16[17,32,128]{2,1,0:T(8,128)(2,1)S(1)}, u32[]{:S(2)}, u32[]{:S(2)}) collective-permute-start(bf16[17,32,128]{2,1,0:T(8,128)(2,1)S(1)} %get-tuple-element.59), channel_id=1, source_target_pairs={{0,2},{1,3},{2,0},{3,1},{4,6},{5,7},{6,4},{7,5},{8,10},{9,11},{10,... | collective-permute-start | bytes 417800 | tf_op jit(solution)/shard_map/ppermute | solution.py:567
  35.9 5.7 %copy-start = (bf16[128,2048]{1,0:T(8,128)(2,1)S(1)}, bf16[128,2048]{1,0:T(8,128)(2,1)}, u32[]{:S(2)}) copy-start(bf16[128,2048]{1,0:T(8,128)(2,1)} %refs_0_.7) | copy-start | bytes 1572868
  35.9 5.7 %copy-start.1 = (bf16[128,2048]{1,0:T(8,128)(2,1)S(1)}, bf16[128,2048]{1,0:T(8,128)(2,1)}, u32[]{:S(2)}) copy-start(bf16[128,2048]{1,0:T(8,128)(2,1)} %refs_1_.7) | copy-start | bytes 1572868
  35.9 5.7 %copy-start.2 = (bf16[128,2048]{1,0:T(8,128)(2,1)S(1)}, bf16[128,2048]{1,0:T(8,128)(2,1)}, u32[]{:S(2)}) copy-start(bf16[128,2048]{1,0:T(8,128)(2,1)} %refs_2_.7) | copy-start | bytes 1572868
  35.9 5.7 %copy-start.3 = (bf16[128,2048]{1,0:T(8,128)(2,1)S(1)}, bf16[128,2048]{1,0:T(8,128)(2,1)}, u32[]{:S(2)}) copy-start(bf16[128,2048]{1,0:T(8,128)(2,1)} %refs_3_.7) | copy-start | bytes 1572868
  36.0 8.9 %collective-permute-start.13 = (bf16[4,128,128]{2,1,0:T(8,128)(2,1)S(1)}, bf16[4,128,128]{2,1,0:T(8,128)(2,1)S(1)}, u32[]{:S(2)}, u32[]{:S(2)}) collective-permute-start(bf16[4,128,128]{2,1,0:T(8,128)(2,1)S(1)} %get-tuple-element.56), channel_id=1, source_target_pairs={{0,24},{4,28},{8,16},{12,20},{16,8},{20,12},{24,0},{28,4},{1,25},{... | collective-permute-start | bytes 393224 | tf_op jit(solution)/shard_map/ppermute | solution.py:567
  37.5 7.4 %collective-permute-start.14 = (bf16[4,128,128]{2,1,0:T(8,128)(2,1)S(1)}, bf16[4,128,128]{2,1,0:T(8,128)(2,1)S(1)}, u32[]{:S(2)}, u32[]{:S(2)}) collective-permute-start(bf16[4,128,128]{2,1,0:T(8,128)(2,1)S(1)} %get-tuple-element.57), channel_id=1, source_target_pairs={{0,16},{4,20},{8,24},{12,28},{16,0},{20,4},{24,8},{28,12},{1,17},{... | collective-permute-start | bytes 393224 | tf_op jit(solution)/shard_map/ppermute | solution.py:567
  38.1 6.9 %collective-permute-start.15 = (bf16[4,128,128]{2,1,0:T(8,128)(2,1)S(1)}, bf16[4,128,128]{2,1,0:T(8,128)(2,1)S(1)}, u32[]{:S(2)}, u32[]{:S(2)}) collective-permute-start(bf16[4,128,128]{2,1,0:T(8,128)(2,1)S(1)} %get-tuple-element.58), channel_id=1, source_target_pairs={{0,8},{4,12},{8,0},{12,4},{16,24},{20,28},{24,16},{28,20},{1,9},{5... | collective-permute-start | bytes 393224 | tf_op jit(solution)/shard_map/ppermute | solution.py:567

commit v22 on v21

--- a/solution.py
+++ b/solution.py
@@ -275,7 +275,7 @@
     mids, refs = refs[:n_i], refs[n_i:]
     stats_ref, columns_ref = refs[:2]
     refs = refs[2:]
-    xmsgs, refs = refs[:slots], refs[slots:]
+    xmsgs, refs = in_back(refs[:slots]), refs[slots:]
     outs, (far, turn, spread) = refs[:n_i], refs[n_i:]
     rows = xmsgs[0].shape[1]
     quarter = rows // DILATION
@@ -317,7 +317,7 @@
 def far_parts_kernel(slots, width, *refs):
     fulls, refs = in_back(refs[:slots]), refs[slots:]
     sibs, refs = refs[: width - 1], refs[width - 1 :]
-    xmsgs, refs = refs[:slots], refs[slots + 1 :]
+    xmsgs, refs = in_back(refs[:slots]), refs[slots + 1 :]
     outs, refs = refs[:slots], refs[slots:]
     kvouts, refs = refs[: width - 1], refs[width - 1 :]
     weights, score_grads = refs
@@ -409,7 +409,7 @@
 def near_early_kernel(n_i, slots, *refs):
     sources, near_ref, refs = refs[:4], refs[4], refs[5:]
     mids, refs = refs[: n_i - 1], refs[n_i - 1 :]
-    xmsgs, (out_ref, stats_ref, spread) = refs[:slots], refs[slots:]
+    xmsgs, (out_ref, stats_ref, spread) = in_back(refs[:slots]), refs[slots:]
     near_statistics(n_i, slots, range(n_i - 1), near_ref, mids, xmsgs, stats_ref, spread)
     for step in range(n_i - 1):
         for slot, parts in enumerate(near_place(n_i, slots, step, sources, stats_ref)):
@@ -659,7 +659,7 @@
         [mid] * n_i,
         [pltpu.VMEM((2 * slots, rows), F32), pltpu.VMEM((LANES, n_i * quarter), F32), square],
         unit * slots * 6,
-        mids + [middle, columns] + xmsgs,
+        mids + [middle, columns] + in_back(xmsgs),
     )
     midparts = swap_back(midparts)
     farparts = call(
@@ -668,7 +668,7 @@
         [full] * slots + [half] * (width - 1),
         [pltpu.VMEM((n_o * rows, slots * rows), BF16)] * 2,
         unit * n_o * slots * 6,
-        [*in_back(fulls), *sibs, *xmsgs, midparts[0]],
+        [*in_back(fulls), *sibs, *in_back(xmsgs), midparts[0]],
         cheap=True,
     )
     sibparts = [swap(x, "seqo", n_o, part + 1) for part, x in enumerate(farparts[slots:])]
@@ -694,7 +694,7 @@
         [SHAPE((4, (n_i - 1) * slots, rows, HEAD_DIM), F32)],
         kept,
         SHORT,
-        [*sources, near, *back[:-1], *xmsgs],
+        [*sources, near, *back[:-1], *in_back(xmsgs)],
     )
     whole = [SHAPE((rows, features), BF16)] * 4
     outs = call(

time: 46.2 us -> 47.2 us (1.022)
  waiting for transfers between devices: 10.8 us -> 11.8 us
    ppermute x17, waiting for transfers between devices: 10.8 us -> 11.8 us  [swap(): return lax.ppermute(x, axis, [(i, i ^ mask) for i in range(n)])]
where the time goes in v22:
time: 47.2 us; the launch traced here: 47 us
  starting transfers between devices  21.1 us (45%)
  Pallas kernels  13.3 us (28%)
  waiting for transfers between devices  11.8 us (25%)
  between operations  0.83 us (2%)
    ppermute x17, starting transfers between devices, swap(): return lax.ppermute(x, axis, [(i, i ^ mask) for i in range(n)])  21.1 us
    pallas_call x17, Pallas kernels, call(): pl.pallas_call(kernel, out_shape=tuple(outs), in_specs=[pl.BlockSpec(memo...  13.3 us
    ppermute x17, waiting for transfers between devices, swap(): return lax.ppermute(x, axis, [(i, i ^ mask) for i in range(n)])  11.8 us
  transfers between devices with their start and end apart: 17, of which 10 were waited for; matrix products, arithmetic and copies ran while one was open for 0% of the time, Pallas kernels for 19%

profile of v22, /device:TPU:0, one launch (start us, length us, event | category | flops | bytes accessed | tf_op | source)
XLA Modules:
  0.0 47.0 jit_solution(8287757019026039409)
XLA Ops:
  0.6 2.3 %pick_first.1 = (bf16[17,32,128]{2,1,0:T(8,128)(2,1)S(1)}, bf16[17,32,128]{2,1,0:T(8,128)(2,1)S(1)}, bf16[4,128,128]{2,1,0:T(8,128)(2,1)S(1)}, bf16[4,128,128]{2...) custom-call(bf16[128,2048]{1,0:T(8,128)(2,1)} %refs_0_.7, ...), custom_call_target="tpu_custom_call" | custom-call | flops 67108864 | bytes 2916352 | tf_op jit(solution)/shard_map/pick_first/pallas_call | solution.py:547
  2.9 5.1 %collective-permute-start = (bf16[17,32,128]{2,1,0:T(8,128)(2,1)S(1)}, bf16[17,32,128]{2,1,0:T(8,128)(2,1)S(1)}, u32[]{:S(2)}, u32[]{:S(2)}) collective-permute-start(bf16[17,32,128]{2,1,0:T(8,128)(2,1)S(1)} %get-tuple-element.37), channel_id=1, source_target_pairs={{0,3},{1,2},{2,1},{3,0},{4,7},{5,6},{6,5},{7,4},{8,11},{9,10},{10,... | collective-permute-start | bytes 417800 | tf_op jit(solution)/shard_map/ppermute | solution.py:567
  8.0 2.4 %collective-permute-start.3 = (bf16[4,128,128]{2,1,0:T(8,128)(2,1)S(1)}, bf16[4,128,128]{2,1,0:T(8,128)(2,1)S(1)}, u32[]{:S(2)}, u32[]{:S(2)}) collective-permute-start(bf16[4,128,128]{2,1,0:T(8,128)(2,1)S(1)} %get-tuple-element.41), channel_id=1, source_target_pairs={{0,24},{4,28},{8,16},{12,20},{16,8},{20,12},{24,0},{28,4},{1,25},{... | collective-permute-start | bytes 393224 | tf_op jit(solution)/shard_map/ppermute | solution.py:567
  10.5 0.5 %collective-permute-start.4 = (bf16[4,128,128]{2,1,0:T(8,128)(2,1)S(1)}, bf16[4,128,128]{2,1,0:T(8,128)(2,1)S(1)}, u32[]{:S(2)}, u32[]{:S(2)}) collective-permute-start(bf16[4,128,128]{2,1,0:T(8,128)(2,1)S(1)} %get-tuple-element.42), channel_id=1, source_target_pairs={{0,16},{4,20},{8,24},{12,28},{16,0},{20,4},{24,8},{28,12},{1,17},{... | collective-permute-start | bytes 393224 | tf_op jit(solution)/shard_map/ppermute | solution.py:567
  11.0 0.5 %collective-permute-start.5 = (bf16[4,128,128]{2,1,0:T(8,128)(2,1)S(1)}, bf16[4,128,128]{2,1,0:T(8,128)(2,1)S(1)}, u32[]{:S(2)}, u32[]{:S(2)}) collective-permute-start(bf16[4,128,128]{2,1,0:T(8,128)(2,1)S(1)} %get-tuple-element.43), channel_id=1, source_target_pairs={{0,8},{4,12},{8,0},{12,4},{16,24},{20,28},{24,16},{28,20},{1,9},{5... | collective-permute-start | bytes 393224 | tf_op jit(solution)/shard_map/ppermute | solution.py:567
  11.5 2.1 %pick_rest.1 = (bf16[17,32,128]{2,1,0:T(8,128)(2,1)S(1)}, bf16[17,32,128]{2,1,0:T(8,128)(2,1)S(1)}, f32[32,128]{1,0:T(8,128)S(1)}) custom-call(bf16[128,2048]{1,0:T(8,128)(2,1)} %refs_0_.7, bf16[128,2048]{1,0:T(8,128)(2,1)} %refs_1_.7, bf16[128,2048]{1,0:T(8,128)(2,1)} %refs_2_.7, bf16[128,2048]{1,0:T(8,128)(2,1)} %refs_3_.7, ...), custom_call_target="tpu_custom_call" | custom-call | flops 134217728 | bytes 2408448 | tf_op jit(solution)/shard_map/pick_rest/pallas_call | solution.py:547
  13.8 0.6 %collective-permute-start.2 = (bf16[17,32,128]{2,1,0:T(8,128)(2,1)S(1)}, bf16[17,32,128]{2,1,0:T(8,128)(2,1)S(1)}, u32[]{:S(2)}, u32[]{:S(2)}) collective-permute-start(bf16[17,32,128]{2,1,0:T(8,128)(2,1)S(1)} %get-tuple-element.39), channel_id=1, source_target_pairs={{0,1},{1,0},{2,3},{3,2},{4,5},{5,4},{6,7},{7,6},{8,9},{9,8},{10,11... | collective-permute-start | bytes 417800 | tf_op jit(solution)/shard_map/ppermute | solution.py:567
  14.4 2.3 %collective-permute-done.4.refs_2_ = bf16[4,128,128]{2,1,0:T(8,128)(2,1)S(1)} collective-permute-done((bf16[4,128,128]{2,1,0:T(8,128)(2,1)S(1)}, bf16[4,128,128]{2,1,0:T(8,128)(2,1)S(1)}, u32[]{:S(2)}, u32[]{:S(2)}) %collective-permute-start.4) | collective-permute-done | bytes 131104 | tf_op jit(solution)/shard_map/ppermute | solution.py:567
  16.9 1.5 %collective-permute-done.6.refs_4_ = bf16[4,2,128,128]{3,2,1,0:T(8,128)(2,1)S(1)} collective-permute-done((bf16[4,2,128,128]{3,2,1,0:T(8,128)(2,1)S(1)}, bf16[4,2,128,128]{3,2,1,0:T(8,128)(2,1)S(1)}, u32[]{:S(2)}, u32[]{:S(2)}) %collective-permute-start.6) | collective-permute-done | bytes 262176 | tf_op jit(solution)/shard_map/ppermute | solution.py:567
  18.4 1.1 %far_stats.1.refs_5_ = f32[8,128]{1,0:T(8,128)S(1)} custom-call(bf16[4,128,128]{2,1,0:T(8,128)(2,1)S(1)} %get-tuple-element.40.refs_0_, bf16[4,128,128]{2,1,0:T(8,128)(2,1)S(1)} %collective-permute-done.3.refs_1_, bf16[4,128,128]{2,1,0:T(8,128)(2,1)S(1)} %collective-permute-done.4.refs_2_, bf16[4,128,128]{2,1,0:T(8,128)(2,1)S(1)} %collective-permute-done.5.refs_3_, ...), custom_call_target="tpu_custom_call" | custom-call | flops 1 | bytes 794624 | tf_op jit(solution)/shard_map/far_stats/pallas_call | solution.py:547
  19.5 1.4 %collective-permute-done.1.refs_2_ = bf16[17,32,128]{2,1,0:T(8,128)(2,1)S(1)} collective-permute-done((bf16[17,32,128]{2,1,0:T(8,128)(2,1)S(1)}, bf16[17,32,128]{2,1,0:T(8,128)(2,1)S(1)}, u32[]{:S(2)}, u32[]{:S(2)}) %collective-permute-start.1) | collective-permute-done | bytes 139296 | tf_op jit(solution)/shard_map/ppermute | solution.py:567
  21.0 0.1 collective-permute-done.2.refs_3_
  21.1 0.5 %middle_stats.1 = (f32[16,128]{1,0:T(8,128)S(1)}, f32[8,128]{1,0:T(8,128)S(1)}, f32[128,128]{1,0:T(8,128)S(1)}) custom-call(bf16[17,32,128]{2,1,0:T(8,128)(2,1)S(1)} %get-tuple-element.36.refs_0_, bf16[17,32,128]{2,1,0:T(8,128)(2,1)S(1)} %collective-permute-done.refs_0_.refs_1_, bf16[17,32,128]{2,1,0:T(8,128)(2,1)S(1)} %collective-permute-done.1.refs_2_, ...), custom_call_target="tpu_custom_call" | custom-call | flops 33554432 | bytes 655360 | tf_op jit(solution)/shard_map/middle_stats/pallas_call | solution.py:547
  21.6 1.6 %collective-permute-start.9 = (f32[16,128]{1,0:T(8,128)S(1)}, f32[16,128]{1,0:T(8,128)S(1)}, u32[]{:S(2)}, u32[]{:S(2)}) collective-permute-start(f32[16,128]{1,0:T(8,128)S(1)} %get-tuple-element.46.refs_6_.refs_8_.refs_5_), channel_id=1, source_target_pairs={{0,8},{4,12},{8,0},{12,4},{16,24},{20,28},{24,16},{28,20},{1,9},{5... | collective-permute-start | bytes 24584 | tf_op jit(solution)/shard_map/ppermute | solution.py:567
  23.2 1.5 %collective-permute-start.8 = (f32[16,128]{1,0:T(8,128)S(1)}, f32[16,128]{1,0:T(8,128)S(1)}, u32[]{:S(2)}, u32[]{:S(2)}) collective-permute-start(f32[16,128]{1,0:T(8,128)S(1)} %get-tuple-element.46.refs_6_.refs_8_.refs_5_), channel_id=1, source_target_pairs={{0,16},{4,20},{8,24},{12,28},{16,0},{20,4},{24,8},{28,12},{1,17},{... | collective-permute-start | bytes 24584 | tf_op jit(solution)/shard_map/ppermute | solution.py:567
  24.7 0.5 %collective-permute-start.7 = (f32[16,128]{1,0:T(8,128)S(1)}, f32[16,128]{1,0:T(8,128)S(1)}, u32[]{:S(2)}, u32[]{:S(2)}) collective-permute-start(f32[16,128]{1,0:T(8,128)S(1)} %get-tuple-element.46.refs_6_.refs_8_.refs_5_), channel_id=1, source_target_pairs={{0,24},{4,28},{8,16},{12,20},{16,8},{20,12},{24,0},{28,4},{1,25},{... | collective-permute-start | bytes 24584 | tf_op jit(solution)/shard_map/ppermute | solution.py:567
  25.2 0.2 collective-permute-done.9.refs_9_.refs_11_.refs_8_
  25.4 1.4 %collective-permute-done.8.refs_8_.refs_10_.refs_7_ = f32[16,128]{1,0:T(8,128)S(1)} collective-permute-done((f32[16,128]{1,0:T(8,128)S(1)}, f32[16,128]{1,0:T(8,128)S(1)}, u32[]{:S(2)}, u32[]{:S(2)}) %collective-permute-start.8) | collective-permute-done | bytes 8224 | tf_op jit(solution)/shard_map/ppermute | solution.py:567
  26.8 2.4 %collective-permute-done.7.refs_7_.refs_9_.refs_6_ = f32[16,128]{1,0:T(8,128)S(1)} collective-permute-done((f32[16,128]{1,0:T(8,128)S(1)}, f32[16,128]{1,0:T(8,128)S(1)}, u32[]{:S(2)}, u32[]{:S(2)}) %collective-permute-start.7) | collective-permute-done | bytes 8224 | tf_op jit(solution)/shard_map/ppermute | solution.py:567
  29.2 0.6 %middle_parts.1 = (bf16[17,32,128]{2,1,0:T(8,128)(2,1)S(1)}, bf16[17,32,128]{2,1,0:T(8,128)(2,1)S(1)}, bf16[17,32,128]{2,1,0:T(8,128)(2,1)S(1)}, bf16[17,32,128]{2,1,0:T(8,128)(2,1)S(1)}) custom-call(bf16[17,32,128]{2,1,0:T(8,128)(2,1)S(1)} %get-tuple-element.36.refs_0_, bf16[17,32,128]{2,1,0:T(8,128)(2,1)S(1)} %collective-permute-done.refs_0_.refs_1_, ...), custom_call_target="tpu_custom_call" | custom-call | flops 100663296 | bytes 1216512 | tf_op jit(solution)/shard_map/middle_parts/pallas_call | solution.py:547
  29.9 1.5 %collective-permute-start.10 = (bf16[17,32,128]{2,1,0:T(8,128)(2,1)S(1)}, bf16[17,32,128]{2,1,0:T(8,128)(2,1)S(1)}, u32[]{:S(2)}, u32[]{:S(2)}) collective-permute-start(bf16[17,32,128]{2,1,0:T(8,128)(2,1)S(1)} %get-tuple-element.48), channel_id=1, source_target_pairs={{0,3},{1,2},{2,1},{3,0},{4,7},{5,6},{6,5},{7,4},{8,11},{9,10},{10,... | collective-permute-start | bytes 417800 | tf_op jit(solution)/shard_map/ppermute | solution.py:567
  31.4 2.1 %far_parts.1 = (bf16[4,128,128]{2,1,0:T(8,128)(2,1)S(1)}, bf16[4,128,128]{2,1,0:T(8,128)(2,1)S(1)}, bf16[4,128,128]{2,1,0:T(8,128)(2,1)S(1)}, bf16[4,128,128]{2,...) custom-call(bf16[4,128,128]{2,1,0:T(8,128)(2,1)S(1)} %get-tuple-element.40.refs_0_, ...), custom_call_target="tpu_custom_call" | custom-call | flops 1 | bytes 1 | tf_op jit(solution)/shard_map/far_parts/pallas_call | solution.py:547
  33.5 0.3 collective-permute-start.11
  33.8 2.8 %collective-permute-start.16 = (bf16[17,32,128]{2,1,0:T(8,128)(2,1)S(1)}, bf16[17,32,128]{2,1,0:T(8,128)(2,1)S(1)}, u32[]{:S(2)}, u32[]{:S(2)}) collective-permute-start(bf16[17,32,128]{2,1,0:T(8,128)(2,1)S(1)} %get-tuple-element.59), channel_id=1, source_target_pairs={{0,2},{1,3},{2,0},{3,1},{4,6},{5,7},{6,4},{7,5},{8,10},{9,11},{10,... | collective-permute-start | bytes 417800 | tf_op jit(solution)/shard_map/ppermute | solution.py:567
  36.6 0.2 collective-permute-done.10.refs_6_.refs_0_
  36.9 0.5 %collective-permute-start.13 = (bf16[4,128,128]{2,1,0:T(8,128)(2,1)S(1)}, bf16[4,128,128]{2,1,0:T(8,128)(2,1)S(1)}, u32[]{:S(2)}, u32[]{:S(2)}) collective-permute-start(bf16[4,128,128]{2,1,0:T(8,128)(2,1)S(1)} %get-tuple-element.56), channel_id=1, source_target_pairs={{0,24},{4,28},{8,16},{12,20},{16,8},{20,12},{24,0},{28,4},{1,25},{... | collective-permute-start | bytes 393224 | tf_op jit(solution)/shard_map/ppermute | solution.py:567
  37.5 1.5 %collective-permute-start.14 = (bf16[4,128,128]{2,1,0:T(8,128)(2,1)S(1)}, bf16[4,128,128]{2,1,0:T(8,128)(2,1)S(1)}, u32[]{:S(2)}, u32[]{:S(2)}) collective-permute-start(bf16[4,128,128]{2,1,0:T(8,128)(2,1)S(1)} %get-tuple-element.57), channel_id=1, source_target_pairs={{0,16},{4,20},{8,24},{12,28},{16,0},{20,4},{24,8},{28,12},{1,17},{... | collective-permute-start | bytes 393224 | tf_op jit(solution)/shard_map/ppermute | solution.py:567
  39.0 1.5 %collective-permute-start.15 = (bf16[4,128,128]{2,1,0:T(8,128)(2,1)S(1)}, bf16[4,128,128]{2,1,0:T(8,128)(2,1)S(1)}, u32[]{:S(2)}, u32[]{:S(2)}) collective-permute-start(bf16[4,128,128]{2,1,0:T(8,128)(2,1)S(1)} %get-tuple-element.58), channel_id=1, source_target_pairs={{0,8},{4,12},{8,0},{12,4},{16,24},{20,28},{24,16},{28,20},{1,9},{5... | collective-permute-start | bytes 393224 | tf_op jit(solution)/shard_map/ppermute | solution.py:567
  40.5 2.0 %collective-permute-done.11.refs_7_ = bf16[17,32,128]{2,1,0:T(8,128)(2,1)S(1)} collective-permute-done((bf16[17,32,128]{2,1,0:T(8,128)(2,1)S(1)}, bf16[17,32,128]{2,1,0:T(8,128)(2,1)S(1)}, u32[]{:S(2)}, u32[]{:S(2)}) %collective-permute-start.11) | collective-permute-done | bytes 139296 | tf_op jit(solution)/shard_map/ppermute | solution.py:567
  42.5 1.4 %near_early.1.refs_5_.early_ref = f32[4,12,128,128]{3,2,1,0:T(8,128)S(1)} custom-call(bf16[128,2048]{1,0:T(8,128)(2,1)S(1)} %copy-done, bf16[128,2048]{1,0:T(8,128)(2,1)S(1)} %copy-done.1, bf16[128,2048]{1,0:T(8,128)(2,1)S(1)} %copy-done.2, bf16[128,2048]{1,0:T(8,128)(2,1)S(1)} %copy-done.3, f32[32,128]{1,0:T(8,128)S(1)} %get-tuple-element.35.refs_0_.refs_4_, ...), custom_call_target="tpu_custom_call" | custom-call | flops 2000000000 | bytes 5709824 | tf_op jit(solution)/shard_map/near_early/pallas_call | solution.py:547
  44.0 1.9 %final_others.1 = (bf16[128,2048]{1,0:T(8,128)(2,1)}, bf16[128,2048]{1,0:T(8,128)(2,1)}, bf16[128,2048]{1,0:T(8,128)(2,1)}, bf16[128,2048]{1,0:T(8,128)(2,1)}) custom-call(bf16[128,2048]{1,0:T(8,128)(2,1)S(1)} %copy-done, bf16[128,2048]{1,0:T(8,128)(2,1)S(1)} %copy-done.1, bf16[128,2048]{1,0:T(8,128)(2,1)S(1)} %copy-done.2, bf16[128,2048]{1,0:T(8,128)(2,1)S(1)} %copy-done.3, ...), custom_call_target="tpu_custom_call" | custom-call | flops 1000000000 | bytes 7774208 | tf_op jit(solution)/shard_map/final_others/pallas_call | solution.py:547
  45.9 1.1 %final_own.1 = (bf16[128,2048]{1,0:T(8,128)(2,1)}, bf16[128,2048]{1,0:T(8,128)(2,1)}, bf16[128,2048]{1,0:T(8,128)(2,1)}, bf16[128,2048]{1,0:T(8,128)(2,1)}) custom-call(f32[4,12,128,128]{3,2,1,0:T(8,128)S(1)} %near_early.1.refs_5_.early_ref, ...), custom_call_target="tpu_custom_call", output_to_operand_aliasing={{0}: (6, {}), {1}: (7, {}), {2}: (8, {}), {3}: (9, {})} | custom-call | flops 16777216 | bytes 8003584 | tf_op jit(solution)/shard_map/final_own/pallas_call | solution.py:547
  (27 shorter events, 0.4 us)
Async XLA Ops:
  2.9 10.8 %collective-permute-start = (bf16[17,32,128]{2,1,0:T(8,128)(2,1)S(1)}, bf16[17,32,128]{2,1,0:T(8,128)(2,1)S(1)}, u32[]{:S(2)}, u32[]{:S(2)}) collective-permute-start(bf16[17,32,128]{2,1,0:T(8,128)(2,1)S(1)} %get-tuple-element.37), channel_id=1, source_target_pairs={{0,3},{1,2},{2,1},{3,0},{4,7},{5,6},{6,5},{7,4},{8,11},{9,10},{10,... | collective-permute-start | bytes 417800 | tf_op jit(solution)/shard_map/ppermute | solution.py:567
  8.0 6.4 %collective-permute-start.3 = (bf16[4,128,128]{2,1,0:T(8,128)(2,1)S(1)}, bf16[4,128,128]{2,1,0:T(8,128)(2,1)S(1)}, u32[]{:S(2)}, u32[]{:S(2)}) collective-permute-start(bf16[4,128,128]{2,1,0:T(8,128)(2,1)S(1)} %get-tuple-element.41), channel_id=1, source_target_pairs={{0,24},{4,28},{8,16},{12,20},{16,8},{20,12},{24,0},{28,4},{1,25},{... | collective-permute-start | bytes 393224 | tf_op jit(solution)/shard_map/ppermute | solution.py:567
  10.5 6.2 %collective-permute-start.4 = (bf16[4,128,128]{2,1,0:T(8,128)(2,1)S(1)}, bf16[4,128,128]{2,1,0:T(8,128)(2,1)S(1)}, u32[]{:S(2)}, u32[]{:S(2)}) collective-permute-start(bf16[4,128,128]{2,1,0:T(8,128)(2,1)S(1)} %get-tuple-element.42), channel_id=1, source_target_pairs={{0,16},{4,20},{8,24},{12,28},{16,0},{20,4},{24,8},{28,12},{1,17},{... | collective-permute-start | bytes 393224 | tf_op jit(solution)/shard_map/ppermute | solution.py:567
  11.0 5.8 %collective-permute-start.5 = (bf16[4,128,128]{2,1,0:T(8,128)(2,1)S(1)}, bf16[4,128,128]{2,1,0:T(8,128)(2,1)S(1)}, u32[]{:S(2)}, u32[]{:S(2)}) collective-permute-start(bf16[4,128,128]{2,1,0:T(8,128)(2,1)S(1)} %get-tuple-element.43), channel_id=1, source_target_pairs={{0,8},{4,12},{8,0},{12,4},{16,24},{20,28},{24,16},{28,20},{1,9},{5... | collective-permute-start | bytes 393224 | tf_op jit(solution)/shard_map/ppermute | solution.py:567
  13.7 7.3 %collective-permute-start.1 = (bf16[17,32,128]{2,1,0:T(8,128)(2,1)S(1)}, bf16[17,32,128]{2,1,0:T(8,128)(2,1)S(1)}, u32[]{:S(2)}, u32[]{:S(2)}) collective-permute-start(bf16[17,32,128]{2,1,0:T(8,128)(2,1)S(1)} %get-tuple-element.38), channel_id=1, source_target_pairs={{0,2},{1,3},{2,0},{3,1},{4,6},{5,7},{6,4},{7,5},{8,10},{9,11},{10,... | collective-permute-start | bytes 417800 | tf_op jit(solution)/shard_map/ppermute | solution.py:567
  13.8 7.3 %collective-permute-start.2 = (bf16[17,32,128]{2,1,0:T(8,128)(2,1)S(1)}, bf16[17,32,128]{2,1,0:T(8,128)(2,1)S(1)}, u32[]{:S(2)}, u32[]{:S(2)}) collective-permute-start(bf16[17,32,128]{2,1,0:T(8,128)(2,1)S(1)} %get-tuple-element.39), channel_id=1, source_target_pairs={{0,1},{1,0},{2,3},{3,2},{4,5},{5,4},{6,7},{7,6},{8,9},{9,8},{10,11... | collective-permute-start | bytes 417800 | tf_op jit(solution)/shard_map/ppermute | solution.py:567
  16.8 1.6 %collective-permute-start.6 = (bf16[4,2,128,128]{3,2,1,0:T(8,128)(2,1)S(1)}, bf16[4,2,128,128]{3,2,1,0:T(8,128)(2,1)S(1)}, u32[]{:S(2)}, u32[]{:S(2)}) collective-permute-start(bf16[4,2,128,128]{3,2,1,0:T(8,128)(2,1)S(1)} %pack.1), channel_id=1, source_target_pairs={{0,4},{4,0},{8,12},{12,8},{16,20},{20,16},{24,28},{28,24},{1,5},{5... | collective-permute-start | bytes 786440 | tf_op jit(solution)/shard_map/ppermute | solution.py:567
  21.6 3.8 %collective-permute-start.9 = (f32[16,128]{1,0:T(8,128)S(1)}, f32[16,128]{1,0:T(8,128)S(1)}, u32[]{:S(2)}, u32[]{:S(2)}) collective-permute-start(f32[16,128]{1,0:T(8,128)S(1)} %get-tuple-element.46.refs_6_.refs_8_.refs_5_), channel_id=1, source_target_pairs={{0,8},{4,12},{8,0},{12,4},{16,24},{20,28},{24,16},{28,20},{1,9},{5... | collective-permute-start | bytes 24584 | tf_op jit(solution)/shard_map/ppermute | solution.py:567
  23.2 3.7 %collective-permute-start.8 = (f32[16,128]{1,0:T(8,128)S(1)}, f32[16,128]{1,0:T(8,128)S(1)}, u32[]{:S(2)}, u32[]{:S(2)}) collective-permute-start(f32[16,128]{1,0:T(8,128)S(1)} %get-tuple-element.46.refs_6_.refs_8_.refs_5_), channel_id=1, source_target_pairs={{0,16},{4,20},{8,24},{12,28},{16,0},{20,4},{24,8},{28,12},{1,17},{... | collective-permute-start | bytes 24584 | tf_op jit(solution)/shard_map/ppermute | solution.py:567
  24.7 4.5 %collective-permute-start.7 = (f32[16,128]{1,0:T(8,128)S(1)}, f32[16,128]{1,0:T(8,128)S(1)}, u32[]{:S(2)}, u32[]{:S(2)}) collective-permute-start(f32[16,128]{1,0:T(8,128)S(1)} %get-tuple-element.46.refs_6_.refs_8_.refs_5_), channel_id=1, source_target_pairs={{0,24},{4,28},{8,16},{12,20},{16,8},{20,12},{24,0},{28,4},{1,25},{... | collective-permute-start | bytes 24584 | tf_op jit(solution)/shard_map/ppermute | solution.py:567
  29.9 6.9 %collective-permute-start.10 = (bf16[17,32,128]{2,1,0:T(8,128)(2,1)S(1)}, bf16[17,32,128]{2,1,0:T(8,128)(2,1)S(1)}, u32[]{:S(2)}, u32[]{:S(2)}) collective-permute-start(bf16[17,32,128]{2,1,0:T(8,128)(2,1)S(1)} %get-tuple-element.48), channel_id=1, source_target_pairs={{0,3},{1,2},{2,1},{3,0},{4,7},{5,6},{6,5},{7,4},{8,11},{9,10},{10,... | collective-permute-start | bytes 417800 | tf_op jit(solution)/shard_map/ppermute | solution.py:567
  33.5 3.3 %collective-permute-start.12 = (bf16[4,2,128,128]{3,2,1,0:T(8,128)(2,1)S(1)}, bf16[4,2,128,128]{3,2,1,0:T(8,128)(2,1)S(1)}, u32[]{:S(2)}, u32[]{:S(2)}) collective-permute-start(bf16[4,2,128,128]{3,2,1,0:T(8,128)(2,1)S(1)} %get-tuple-element.54), channel_id=1, source_target_pairs={{0,4},{4,0},{8,12},{12,8},{16,20},{20,16},{24,28},{28,24},{1,5},{5... | collective-permute-start | bytes 786440 | tf_op jit(solution)/shard_map/ppermute | solution.py:567
  33.5 9.0 %collective-permute-start.11 = (bf16[17,32,128]{2,1,0:T(8,128)(2,1)S(1)}, bf16[17,32,128]{2,1,0:T(8,128)(2,1)S(1)}, u32[]{:S(2)}, u32[]{:S(2)}) collective-permute-start(bf16[17,32,128]{2,1,0:T(8,128)(2,1)S(1)} %get-tuple-element.49), channel_id=1, source_target_pairs={{0,1},{1,0},{2,3},{3,2},{4,5},{5,4},{6,7},{7,6},{8,9},{9,8},{10,11... | collective-permute-start | bytes 417800 | tf_op jit(solution)/shard_map/ppermute | solution.py:567
  33.8 10.2 %collective-permute-start.16 = (bf16[17,32,128]{2,1,0:T(8,128)(2,1)S(1)}, bf16[17,32,128]{2,1,0:T(8,128)(2,1)S(1)}, u32[]{:S(2)}, u32[]{:S(2)}) collective-permute-start(bf16[17,32,128]{2,1,0:T(8,128)(2,1)S(1)} %get-tuple-element.59), channel_id=1, source_target_pairs={{0,2},{1,3},{2,0},{3,1},{4,6},{5,7},{6,4},{7,5},{8,10},{9,11},{10,... | collective-permute-start | bytes 417800 | tf_op jit(solution)/shard_map/ppermute | solution.py:567
  36.8 5.7 %copy-start = (bf16[128,2048]{1,0:T(8,128)(2,1)S(1)}, bf16[128,2048]{1,0:T(8,128)(2,1)}, u32[]{:S(2)}) copy-start(bf16[128,2048]{1,0:T(8,128)(2,1)} %refs_0_.7) | copy-start | bytes 1572868
  36.8 5.7 %copy-start.1 = (bf16[128,2048]{1,0:T(8,128)(2,1)S(1)}, bf16[128,2048]{1,0:T(8,128)(2,1)}, u32[]{:S(2)}) copy-start(bf16[128,2048]{1,0:T(8,128)(2,1)} %refs_1_.7) | copy-start | bytes 1572868
  36.8 5.7 %copy-start.2 = (bf16[128,2048]{1,0:T(8,128)(2,1)S(1)}, bf16[128,2048]{1,0:T(8,128)(2,1)}, u32[]{:S(2)}) copy-start(bf16[128,2048]{1,0:T(8,128)(2,1)} %refs_2_.7) | copy-start | bytes 1572868
  36.8 5.7 %copy-start.3 = (bf16[128,2048]{1,0:T(8,128)(2,1)S(1)}, bf16[128,2048]{1,0:T(8,128)(2,1)}, u32[]{:S(2)}) copy-start(bf16[128,2048]{1,0:T(8,128)(2,1)} %refs_3_.7) | copy-start | bytes 1572868
  36.9 8.9 %collective-permute-start.13 = (bf16[4,128,128]{2,1,0:T(8,128)(2,1)S(1)}, bf16[4,128,128]{2,1,0:T(8,128)(2,1)S(1)}, u32[]{:S(2)}, u32[]{:S(2)}) collective-permute-start(bf16[4,128,128]{2,1,0:T(8,128)(2,1)S(1)} %get-tuple-element.56), channel_id=1, source_target_pairs={{0,24},{4,28},{8,16},{12,20},{16,8},{20,12},{24,0},{28,4},{1,25},{... | collective-permute-start | bytes 393224 | tf_op jit(solution)/shard_map/ppermute | solution.py:567
  37.5 8.4 %collective-permute-start.14 = (bf16[4,128,128]{2,1,0:T(8,128)(2,1)S(1)}, bf16[4,128,128]{2,1,0:T(8,128)(2,1)S(1)}, u32[]{:S(2)}, u32[]{:S(2)}) collective-permute-start(bf16[4,128,128]{2,1,0:T(8,128)(2,1)S(1)} %get-tuple-element.57), channel_id=1, source_target_pairs={{0,16},{4,20},{8,24},{12,28},{16,0},{20,4},{24,8},{28,12},{1,17},{... | collective-permute-start | bytes 393224 | tf_op jit(solution)/shard_map/ppermute | solution.py:567
  39.0 6.9 %collective-permute-start.15 = (bf16[4,128,128]{2,1,0:T(8,128)(2,1)S(1)}, bf16[4,128,128]{2,1,0:T(8,128)(2,1)S(1)}, u32[]{:S(2)}, u32[]{:S(2)}) collective-permute-start(bf16[4,128,128]{2,1,0:T(8,128)(2,1)S(1)} %get-tuple-element.58), channel_id=1, source_target_pairs={{0,8},{4,12},{8,0},{12,4},{16,24},{20,28},{24,16},{28,20},{1,9},{5... | collective-permute-start | bytes 393224 | tf_op jit(solution)/shard_map/ppermute | solution.py:567

commit v23 on v21

--- a/solution.py
+++ b/solution.py
@@ -56,7 +56,7 @@
 
 
 def distance_back(n_i, step):
-    return n_i - 1 if step == 1 else step - 1
+    return n_i - step
 
 
 def place_in(n_i, slots, step):

time: 46.2 us -> 47.1 us (1.019)
  waiting for transfers between devices: 10.8 us -> 11.7 us
    ppermute x17, waiting for transfers between devices: 10.8 us -> 11.7 us  [swap(): return lax.ppermute(x, axis, [(i, i ^ mask) for i in range(n)])]
where the time goes in v23:
time: 47.1 us; the launch traced here: 46.9 us
  starting transfers between devices  21.1 us (45%)
  Pallas kernels  13.3 us (28%)
  waiting for transfers between devices  11.7 us (25%)
  between operations  0.83 us (2%)
    ppermute x17, starting transfers between devices, swap(): return lax.ppermute(x, axis, [(i, i ^ mask) for i in range(n)])  21.1 us
    pallas_call x17, Pallas kernels, call(): pl.pallas_call(kernel, out_shape=tuple(outs), in_specs=[pl.BlockSpec(memo...  13.3 us
    ppermute x17, waiting for transfers between devices, swap(): return lax.ppermute(x, axis, [(i, i ^ mask) for i in range(n)])  11.7 us
  transfers between devices with their start and end apart: 17, of which 10 were waited for; matrix products, arithmetic and copies ran while one was open for 0% of the time, Pallas kernels for 19%

profile of v23, /device:TPU:0, one launch (start us, length us, event | category | flops | bytes accessed | tf_op | source)
XLA Modules:
  0.0 46.9 jit_solution(1859390992926098768)
XLA Ops:
  0.6 2.3 %pick_first.1 = (bf16[17,32,128]{2,1,0:T(8,128)(2,1)S(1)}, bf16[17,32,128]{2,1,0:T(8,128)(2,1)S(1)}, bf16[4,128,128]{2,1,0:T(8,128)(2,1)S(1)}, bf16[4,128,128]{2...) custom-call(bf16[128,2048]{1,0:T(8,128)(2,1)} %refs_0_.7, ...), custom_call_target="tpu_custom_call" | custom-call | flops 67108864 | bytes 2916352 | tf_op jit(solution)/shard_map/pick_first/pallas_call | solution.py:547
  2.9 5.1 %collective-permute-start = (bf16[17,32,128]{2,1,0:T(8,128)(2,1)S(1)}, bf16[17,32,128]{2,1,0:T(8,128)(2,1)S(1)}, u32[]{:S(2)}, u32[]{:S(2)}) collective-permute-start(bf16[17,32,128]{2,1,0:T(8,128)(2,1)S(1)} %get-tuple-element.37), channel_id=1, source_target_pairs={{0,3},{1,2},{2,1},{3,0},{4,7},{5,6},{6,5},{7,4},{8,11},{9,10},{10,... | collective-permute-start | bytes 417800 | tf_op jit(solution)/shard_map/ppermute | solution.py:567
  8.0 2.4 %collective-permute-start.3 = (bf16[4,128,128]{2,1,0:T(8,128)(2,1)S(1)}, bf16[4,128,128]{2,1,0:T(8,128)(2,1)S(1)}, u32[]{:S(2)}, u32[]{:S(2)}) collective-permute-start(bf16[4,128,128]{2,1,0:T(8,128)(2,1)S(1)} %get-tuple-element.41), channel_id=1, source_target_pairs={{0,24},{4,28},{8,16},{12,20},{16,8},{20,12},{24,0},{28,4},{1,25},{... | collective-permute-start | bytes 393224 | tf_op jit(solution)/shard_map/ppermute | solution.py:567
  10.5 0.5 %collective-permute-start.4 = (bf16[4,128,128]{2,1,0:T(8,128)(2,1)S(1)}, bf16[4,128,128]{2,1,0:T(8,128)(2,1)S(1)}, u32[]{:S(2)}, u32[]{:S(2)}) collective-permute-start(bf16[4,128,128]{2,1,0:T(8,128)(2,1)S(1)} %get-tuple-element.42), channel_id=1, source_target_pairs={{0,16},{4,20},{8,24},{12,28},{16,0},{20,4},{24,8},{28,12},{1,17},{... | collective-permute-start | bytes 393224 | tf_op jit(solution)/shard_map/ppermute | solution.py:567
  11.0 0.5 %collective-permute-start.5 = (bf16[4,128,128]{2,1,0:T(8,128)(2,1)S(1)}, bf16[4,128,128]{2,1,0:T(8,128)(2,1)S(1)}, u32[]{:S(2)}, u32[]{:S(2)}) collective-permute-start(bf16[4,128,128]{2,1,0:T(8,128)(2,1)S(1)} %get-tuple-element.43), channel_id=1, source_target_pairs={{0,8},{4,12},{8,0},{12,4},{16,24},{20,28},{24,16},{28,20},{1,9},{5... | collective-permute-start | bytes 393224 | tf_op jit(solution)/shard_map/ppermute | solution.py:567
  11.5 2.1 %pick_rest.1 = (bf16[17,32,128]{2,1,0:T(8,128)(2,1)S(1)}, bf16[17,32,128]{2,1,0:T(8,128)(2,1)S(1)}, f32[32,128]{1,0:T(8,128)S(1)}) custom-call(bf16[128,2048]{1,0:T(8,128)(2,1)} %refs_0_.7, bf16[128,2048]{1,0:T(8,128)(2,1)} %refs_1_.7, bf16[128,2048]{1,0:T(8,128)(2,1)} %refs_2_.7, bf16[128,2048]{1,0:T(8,128)(2,1)} %refs_3_.7, ...), custom_call_target="tpu_custom_call" | custom-call | flops 134217728 | bytes 2408448 | tf_op jit(solution)/shard_map/pick_rest/pallas_call | solution.py:547
  13.8 0.6 %collective-permute-start.2 = (bf16[17,32,128]{2,1,0:T(8,128)(2,1)S(1)}, bf16[17,32,128]{2,1,0:T(8,128)(2,1)S(1)}, u32[]{:S(2)}, u32[]{:S(2)}) collective-permute-start(bf16[17,32,128]{2,1,0:T(8,128)(2,1)S(1)} %get-tuple-element.39), channel_id=1, source_target_pairs={{0,1},{1,0},{2,3},{3,2},{4,5},{5,4},{6,7},{7,6},{8,9},{9,8},{10,11... | collective-permute-start | bytes 417800 | tf_op jit(solution)/shard_map/ppermute | solution.py:567
  14.4 2.3 %collective-permute-done.4.refs_2_ = bf16[4,128,128]{2,1,0:T(8,128)(2,1)S(1)} collective-permute-done((bf16[4,128,128]{2,1,0:T(8,128)(2,1)S(1)}, bf16[4,128,128]{2,1,0:T(8,128)(2,1)S(1)}, u32[]{:S(2)}, u32[]{:S(2)}) %collective-permute-start.4) | collective-permute-done | bytes 131104 | tf_op jit(solution)/shard_map/ppermute | solution.py:567
  16.9 1.5 %collective-permute-done.6.refs_4_ = bf16[4,2,128,128]{3,2,1,0:T(8,128)(2,1)S(1)} collective-permute-done((bf16[4,2,128,128]{3,2,1,0:T(8,128)(2,1)S(1)}, bf16[4,2,128,128]{3,2,1,0:T(8,128)(2,1)S(1)}, u32[]{:S(2)}, u32[]{:S(2)}) %collective-permute-start.6) | collective-permute-done | bytes 262176 | tf_op jit(solution)/shard_map/ppermute | solution.py:567
  18.4 1.1 %far_stats.1.refs_5_ = f32[8,128]{1,0:T(8,128)S(1)} custom-call(bf16[4,128,128]{2,1,0:T(8,128)(2,1)S(1)} %get-tuple-element.40.refs_0_, bf16[4,128,128]{2,1,0:T(8,128)(2,1)S(1)} %collective-permute-done.3.refs_1_, bf16[4,128,128]{2,1,0:T(8,128)(2,1)S(1)} %collective-permute-done.4.refs_2_, bf16[4,128,128]{2,1,0:T(8,128)(2,1)S(1)} %collective-permute-done.5.refs_3_, ...), custom_call_target="tpu_custom_call" | custom-call | flops 1 | bytes 794624 | tf_op jit(solution)/shard_map/far_stats/pallas_call | solution.py:547
  19.5 1.4 %collective-permute-done.1.refs_2_ = bf16[17,32,128]{2,1,0:T(8,128)(2,1)S(1)} collective-permute-done((bf16[17,32,128]{2,1,0:T(8,128)(2,1)S(1)}, bf16[17,32,128]{2,1,0:T(8,128)(2,1)S(1)}, u32[]{:S(2)}, u32[]{:S(2)}) %collective-permute-start.1) | collective-permute-done | bytes 139296 | tf_op jit(solution)/shard_map/ppermute | solution.py:567
  21.0 0.1 collective-permute-done.2.refs_3_
  21.1 0.5 %middle_stats.1 = (f32[16,128]{1,0:T(8,128)S(1)}, f32[8,128]{1,0:T(8,128)S(1)}, f32[128,128]{1,0:T(8,128)S(1)}) custom-call(bf16[17,32,128]{2,1,0:T(8,128)(2,1)S(1)} %get-tuple-element.36.refs_0_, bf16[17,32,128]{2,1,0:T(8,128)(2,1)S(1)} %collective-permute-done.refs_0_.refs_1_, bf16[17,32,128]{2,1,0:T(8,128)(2,1)S(1)} %collective-permute-done.1.refs_2_, ...), custom_call_target="tpu_custom_call" | custom-call | flops 33554432 | bytes 655360 | tf_op jit(solution)/shard_map/middle_stats/pallas_call | solution.py:547
  21.6 2.5 %collective-permute-start.9 = (f32[16,128]{1,0:T(8,128)S(1)}, f32[16,128]{1,0:T(8,128)S(1)}, u32[]{:S(2)}, u32[]{:S(2)}) collective-permute-start(f32[16,128]{1,0:T(8,128)S(1)} %get-tuple-element.46.refs_6_.refs_8_.refs_5_), channel_id=1, source_target_pairs={{0,24},{4,28},{8,16},{12,20},{16,8},{20,12},{24,0},{28,4},{1,25},{... | collective-permute-start | bytes 24584 | tf_op jit(solution)/shard_map/ppermute | solution.py:567
  24.1 0.5 %collective-permute-start.8 = (f32[16,128]{1,0:T(8,128)S(1)}, f32[16,128]{1,0:T(8,128)S(1)}, u32[]{:S(2)}, u32[]{:S(2)}) collective-permute-start(f32[16,128]{1,0:T(8,128)S(1)} %get-tuple-element.46.refs_6_.refs_8_.refs_5_), channel_id=1, source_target_pairs={{0,16},{4,20},{8,24},{12,28},{16,0},{20,4},{24,8},{28,12},{1,17},{... | collective-permute-start | bytes 24584 | tf_op jit(solution)/shard_map/ppermute | solution.py:567
  24.6 0.5 %collective-permute-start.7 = (f32[16,128]{1,0:T(8,128)S(1)}, f32[16,128]{1,0:T(8,128)S(1)}, u32[]{:S(2)}, u32[]{:S(2)}) collective-permute-start(f32[16,128]{1,0:T(8,128)S(1)} %get-tuple-element.46.refs_6_.refs_8_.refs_5_), channel_id=1, source_target_pairs={{0,8},{4,12},{8,0},{12,4},{16,24},{20,28},{24,16},{28,20},{1,9},{5... | collective-permute-start | bytes 24584 | tf_op jit(solution)/shard_map/ppermute | solution.py:567
  25.2 1.1 %collective-permute-done.9.refs_9_.refs_11_.refs_8_ = f32[16,128]{1,0:T(8,128)S(1)} collective-permute-done((f32[16,128]{1,0:T(8,128)S(1)}, f32[16,128]{1,0:T(8,128)S(1)}, u32[]{:S(2)}, u32[]{:S(2)}) %collective-permute-start.9) | collective-permute-done | bytes 8224 | tf_op jit(solution)/shard_map/ppermute | solution.py:567
  26.2 1.5 %collective-permute-done.8.refs_8_.refs_10_.refs_7_ = f32[16,128]{1,0:T(8,128)S(1)} collective-permute-done((f32[16,128]{1,0:T(8,128)S(1)}, f32[16,128]{1,0:T(8,128)S(1)}, u32[]{:S(2)}, u32[]{:S(2)}) %collective-permute-start.8) | collective-permute-done | bytes 8224 | tf_op jit(solution)/shard_map/ppermute | solution.py:567
  27.8 0.5 %collective-permute-done.7.refs_7_.refs_9_.refs_6_ = f32[16,128]{1,0:T(8,128)S(1)} collective-permute-done((f32[16,128]{1,0:T(8,128)S(1)}, f32[16,128]{1,0:T(8,128)S(1)}, u32[]{:S(2)}, u32[]{:S(2)}) %collective-permute-start.7) | collective-permute-done | bytes 8224 | tf_op jit(solution)/shard_map/ppermute | solution.py:567
  28.3 0.6 %middle_parts.1 = (bf16[17,32,128]{2,1,0:T(8,128)(2,1)S(1)}, bf16[17,32,128]{2,1,0:T(8,128)(2,1)S(1)}, bf16[17,32,128]{2,1,0:T(8,128)(2,1)S(1)}, bf16[17,32,128]{2,1,0:T(8,128)(2,1)S(1)}) custom-call(bf16[17,32,128]{2,1,0:T(8,128)(2,1)S(1)} %get-tuple-element.36.refs_0_, bf16[17,32,128]{2,1,0:T(8,128)(2,1)S(1)} %collective-permute-done.refs_0_.refs_1_, ...), custom_call_target="tpu_custom_call" | custom-call | flops 100663296 | bytes 1216512 | tf_op jit(solution)/shard_map/middle_parts/pallas_call | solution.py:547
  28.9 1.5 %collective-permute-start.10 = (bf16[17,32,128]{2,1,0:T(8,128)(2,1)S(1)}, bf16[17,32,128]{2,1,0:T(8,128)(2,1)S(1)}, u32[]{:S(2)}, u32[]{:S(2)}) collective-permute-start(bf16[17,32,128]{2,1,0:T(8,128)(2,1)S(1)} %get-tuple-element.48), channel_id=1, source_target_pairs={{0,3},{1,2},{2,1},{3,0},{4,7},{5,6},{6,5},{7,4},{8,11},{9,10},{10,... | collective-permute-start | bytes 417800 | tf_op jit(solution)/shard_map/ppermute | solution.py:567
  30.4 2.1 %far_parts.1 = (bf16[4,128,128]{2,1,0:T(8,128)(2,1)S(1)}, bf16[4,128,128]{2,1,0:T(8,128)(2,1)S(1)}, bf16[4,128,128]{2,1,0:T(8,128)(2,1)S(1)}, bf16[4,128,128]{2,...) custom-call(bf16[4,128,128]{2,1,0:T(8,128)(2,1)S(1)} %get-tuple-element.40.refs_0_, ...), custom_call_target="tpu_custom_call" | custom-call | flops 1 | bytes 1 | tf_op jit(solution)/shard_map/far_parts/pallas_call | solution.py:547
  32.6 0.3 collective-permute-start.11
  32.9 2.7 %collective-permute-start.16 = (bf16[17,32,128]{2,1,0:T(8,128)(2,1)S(1)}, bf16[17,32,128]{2,1,0:T(8,128)(2,1)S(1)}, u32[]{:S(2)}, u32[]{:S(2)}) collective-permute-start(bf16[17,32,128]{2,1,0:T(8,128)(2,1)S(1)} %get-tuple-element.59), channel_id=1, source_target_pairs={{0,1},{1,0},{2,3},{3,2},{4,5},{5,4},{6,7},{7,6},{8,9},{9,8},{10,11... | collective-permute-start | bytes 417800 | tf_op jit(solution)/shard_map/ppermute | solution.py:567
  35.6 0.2 collective-permute-done.10.refs_6_.refs_0_
  36.0 1.6 %collective-permute-start.13 = (bf16[4,128,128]{2,1,0:T(8,128)(2,1)S(1)}, bf16[4,128,128]{2,1,0:T(8,128)(2,1)S(1)}, u32[]{:S(2)}, u32[]{:S(2)}) collective-permute-start(bf16[4,128,128]{2,1,0:T(8,128)(2,1)S(1)} %get-tuple-element.56), channel_id=1, source_target_pairs={{0,24},{4,28},{8,16},{12,20},{16,8},{20,12},{24,0},{28,4},{1,25},{... | collective-permute-start | bytes 393224 | tf_op jit(solution)/shard_map/ppermute | solution.py:567
  37.5 0.5 %collective-permute-start.14 = (bf16[4,128,128]{2,1,0:T(8,128)(2,1)S(1)}, bf16[4,128,128]{2,1,0:T(8,128)(2,1)S(1)}, u32[]{:S(2)}, u32[]{:S(2)}) collective-permute-start(bf16[4,128,128]{2,1,0:T(8,128)(2,1)S(1)} %get-tuple-element.57), channel_id=1, source_target_pairs={{0,16},{4,20},{8,24},{12,28},{16,0},{20,4},{24,8},{28,12},{1,17},{... | collective-permute-start | bytes 393224 | tf_op jit(solution)/shard_map/ppermute | solution.py:567
  38.0 1.5 %collective-permute-start.15 = (bf16[4,128,128]{2,1,0:T(8,128)(2,1)S(1)}, bf16[4,128,128]{2,1,0:T(8,128)(2,1)S(1)}, u32[]{:S(2)}, u32[]{:S(2)}) collective-permute-start(bf16[4,128,128]{2,1,0:T(8,128)(2,1)S(1)} %get-tuple-element.58), channel_id=1, source_target_pairs={{0,8},{4,12},{8,0},{12,4},{16,24},{20,28},{24,16},{28,20},{1,9},{5... | collective-permute-start | bytes 393224 | tf_op jit(solution)/shard_map/ppermute | solution.py:567
  39.5 2.9 %collective-permute-done.11.refs_7_ = bf16[17,32,128]{2,1,0:T(8,128)(2,1)S(1)} collective-permute-done((bf16[17,32,128]{2,1,0:T(8,128)(2,1)S(1)}, bf16[17,32,128]{2,1,0:T(8,128)(2,1)S(1)}, u32[]{:S(2)}, u32[]{:S(2)}) %collective-permute-start.11) | collective-permute-done | bytes 139296 | tf_op jit(solution)/shard_map/ppermute | solution.py:567
  42.4 1.4 %near_early.1.refs_5_.early_ref = f32[4,12,128,128]{3,2,1,0:T(8,128)S(1)} custom-call(bf16[128,2048]{1,0:T(8,128)(2,1)S(1)} %copy-done, bf16[128,2048]{1,0:T(8,128)(2,1)S(1)} %copy-done.1, bf16[128,2048]{1,0:T(8,128)(2,1)S(1)} %copy-done.2, bf16[128,2048]{1,0:T(8,128)(2,1)S(1)} %copy-done.3, f32[32,128]{1,0:T(8,128)S(1)} %get-tuple-element.35.refs_0_.refs_4_, ...), custom_call_target="tpu_custom_call" | custom-call | flops 2000000000 | bytes 5709824 | tf_op jit(solution)/shard_map/near_early/pallas_call | solution.py:547
  43.9 1.9 %final_others.1 = (bf16[128,2048]{1,0:T(8,128)(2,1)}, bf16[128,2048]{1,0:T(8,128)(2,1)}, bf16[128,2048]{1,0:T(8,128)(2,1)}, bf16[128,2048]{1,0:T(8,128)(2,1)}) custom-call(bf16[128,2048]{1,0:T(8,128)(2,1)S(1)} %copy-done, bf16[128,2048]{1,0:T(8,128)(2,1)S(1)} %copy-done.1, bf16[128,2048]{1,0:T(8,128)(2,1)S(1)} %copy-done.2, bf16[128,2048]{1,0:T(8,128)(2,1)S(1)} %copy-done.3, ...), custom_call_target="tpu_custom_call" | custom-call | flops 1000000000 | bytes 7774208 | tf_op jit(solution)/shard_map/final_others/pallas_call | solution.py:547
  45.8 1.1 %final_own.1 = (bf16[128,2048]{1,0:T(8,128)(2,1)}, bf16[128,2048]{1,0:T(8,128)(2,1)}, bf16[128,2048]{1,0:T(8,128)(2,1)}, bf16[128,2048]{1,0:T(8,128)(2,1)}) custom-call(f32[4,12,128,128]{3,2,1,0:T(8,128)S(1)} %near_early.1.refs_5_.early_ref, ...), custom_call_target="tpu_custom_call", output_to_operand_aliasing={{0}: (6, {}), {1}: (7, {}), {2}: (8, {}), {3}: (9, {})} | custom-call | flops 16777216 | bytes 8003584 | tf_op jit(solution)/shard_map/final_own/pallas_call | solution.py:547
  (27 shorter events, 0.4 us)
Async XLA Ops:
  2.9 10.8 %collective-permute-start = (bf16[17,32,128]{2,1,0:T(8,128)(2,1)S(1)}, bf16[17,32,128]{2,1,0:T(8,128)(2,1)S(1)}, u32[]{:S(2)}, u32[]{:S(2)}) collective-permute-start(bf16[17,32,128]{2,1,0:T(8,128)(2,1)S(1)} %get-tuple-element.37), channel_id=1, source_target_pairs={{0,3},{1,2},{2,1},{3,0},{4,7},{5,6},{6,5},{7,4},{8,11},{9,10},{10,... | collective-permute-start | bytes 417800 | tf_op jit(solution)/shard_map/ppermute | solution.py:567
  8.0 6.4 %collective-permute-start.3 = (bf16[4,128,128]{2,1,0:T(8,128)(2,1)S(1)}, bf16[4,128,128]{2,1,0:T(8,128)(2,1)S(1)}, u32[]{:S(2)}, u32[]{:S(2)}) collective-permute-start(bf16[4,128,128]{2,1,0:T(8,128)(2,1)S(1)} %get-tuple-element.41), channel_id=1, source_target_pairs={{0,24},{4,28},{8,16},{12,20},{16,8},{20,12},{24,0},{28,4},{1,25},{... | collective-permute-start | bytes 393224 | tf_op jit(solution)/shard_map/ppermute | solution.py:567
  10.5 6.2 %collective-permute-start.4 = (bf16[4,128,128]{2,1,0:T(8,128)(2,1)S(1)}, bf16[4,128,128]{2,1,0:T(8,128)(2,1)S(1)}, u32[]{:S(2)}, u32[]{:S(2)}) collective-permute-start(bf16[4,128,128]{2,1,0:T(8,128)(2,1)S(1)} %get-tuple-element.42), channel_id=1, source_target_pairs={{0,16},{4,20},{8,24},{12,28},{16,0},{20,4},{24,8},{28,12},{1,17},{... | collective-permute-start | bytes 393224 | tf_op jit(solution)/shard_map/ppermute | solution.py:567
  11.0 5.8 %collective-permute-start.5 = (bf16[4,128,128]{2,1,0:T(8,128)(2,1)S(1)}, bf16[4,128,128]{2,1,0:T(8,128)(2,1)S(1)}, u32[]{:S(2)}, u32[]{:S(2)}) collective-permute-start(bf16[4,128,128]{2,1,0:T(8,128)(2,1)S(1)} %get-tuple-element.43), channel_id=1, source_target_pairs={{0,8},{4,12},{8,0},{12,4},{16,24},{20,28},{24,16},{28,20},{1,9},{5... | collective-permute-start | bytes 393224 | tf_op jit(solution)/shard_map/ppermute | solution.py:567
  13.7 7.3 %collective-permute-start.1 = (bf16[17,32,128]{2,1,0:T(8,128)(2,1)S(1)}, bf16[17,32,128]{2,1,0:T(8,128)(2,1)S(1)}, u32[]{:S(2)}, u32[]{:S(2)}) collective-permute-start(bf16[17,32,128]{2,1,0:T(8,128)(2,1)S(1)} %get-tuple-element.38), channel_id=1, source_target_pairs={{0,2},{1,3},{2,0},{3,1},{4,6},{5,7},{6,4},{7,5},{8,10},{9,11},{10,... | collective-permute-start | bytes 417800 | tf_op jit(solution)/shard_map/ppermute | solution.py:567
  13.8 7.3 %collective-permute-start.2 = (bf16[17,32,128]{2,1,0:T(8,128)(2,1)S(1)}, bf16[17,32,128]{2,1,0:T(8,128)(2,1)S(1)}, u32[]{:S(2)}, u32[]{:S(2)}) collective-permute-start(bf16[17,32,128]{2,1,0:T(8,128)(2,1)S(1)} %get-tuple-element.39), channel_id=1, source_target_pairs={{0,1},{1,0},{2,3},{3,2},{4,5},{5,4},{6,7},{7,6},{8,9},{9,8},{10,11... | collective-permute-start | bytes 417800 | tf_op jit(solution)/shard_map/ppermute | solution.py:567
  16.8 1.6 %collective-permute-start.6 = (bf16[4,2,128,128]{3,2,1,0:T(8,128)(2,1)S(1)}, bf16[4,2,128,128]{3,2,1,0:T(8,128)(2,1)S(1)}, u32[]{:S(2)}, u32[]{:S(2)}) collective-permute-start(bf16[4,2,128,128]{3,2,1,0:T(8,128)(2,1)S(1)} %pack.1), channel_id=1, source_target_pairs={{0,4},{4,0},{8,12},{12,8},{16,20},{20,16},{24,28},{28,24},{1,5},{5... | collective-permute-start | bytes 786440 | tf_op jit(solution)/shard_map/ppermute | solution.py:567
  21.6 4.6 %collective-permute-start.9 = (f32[16,128]{1,0:T(8,128)S(1)}, f32[16,128]{1,0:T(8,128)S(1)}, u32[]{:S(2)}, u32[]{:S(2)}) collective-permute-start(f32[16,128]{1,0:T(8,128)S(1)} %get-tuple-element.46.refs_6_.refs_8_.refs_5_), channel_id=1, source_target_pairs={{0,24},{4,28},{8,16},{12,20},{16,8},{20,12},{24,0},{28,4},{1,25},{... | collective-permute-start | bytes 24584 | tf_op jit(solution)/shard_map/ppermute | solution.py:567
  24.1 3.7 %collective-permute-start.8 = (f32[16,128]{1,0:T(8,128)S(1)}, f32[16,128]{1,0:T(8,128)S(1)}, u32[]{:S(2)}, u32[]{:S(2)}) collective-permute-start(f32[16,128]{1,0:T(8,128)S(1)} %get-tuple-element.46.refs_6_.refs_8_.refs_5_), channel_id=1, source_target_pairs={{0,16},{4,20},{8,24},{12,28},{16,0},{20,4},{24,8},{28,12},{1,17},{... | collective-permute-start | bytes 24584 | tf_op jit(solution)/shard_map/ppermute | solution.py:567
  24.6 3.7 %collective-permute-start.7 = (f32[16,128]{1,0:T(8,128)S(1)}, f32[16,128]{1,0:T(8,128)S(1)}, u32[]{:S(2)}, u32[]{:S(2)}) collective-permute-start(f32[16,128]{1,0:T(8,128)S(1)} %get-tuple-element.46.refs_6_.refs_8_.refs_5_), channel_id=1, source_target_pairs={{0,8},{4,12},{8,0},{12,4},{16,24},{20,28},{24,16},{28,20},{1,9},{5... | collective-permute-start | bytes 24584 | tf_op jit(solution)/shard_map/ppermute | solution.py:567
  28.9 6.9 %collective-permute-start.10 = (bf16[17,32,128]{2,1,0:T(8,128)(2,1)S(1)}, bf16[17,32,128]{2,1,0:T(8,128)(2,1)S(1)}, u32[]{:S(2)}, u32[]{:S(2)}) collective-permute-start(bf16[17,32,128]{2,1,0:T(8,128)(2,1)S(1)} %get-tuple-element.48), channel_id=1, source_target_pairs={{0,3},{1,2},{2,1},{3,0},{4,7},{5,6},{6,5},{7,4},{8,11},{9,10},{10,... | collective-permute-start | bytes 417800 | tf_op jit(solution)/shard_map/ppermute | solution.py:567
  32.5 3.3 %collective-permute-start.12 = (bf16[4,2,128,128]{3,2,1,0:T(8,128)(2,1)S(1)}, bf16[4,2,128,128]{3,2,1,0:T(8,128)(2,1)S(1)}, u32[]{:S(2)}, u32[]{:S(2)}) collective-permute-start(bf16[4,2,128,128]{3,2,1,0:T(8,128)(2,1)S(1)} %get-tuple-element.54), channel_id=1, source_target_pairs={{0,4},{4,0},{8,12},{12,8},{16,20},{20,16},{24,28},{28,24},{1,5},{5... | collective-permute-start | bytes 786440 | tf_op jit(solution)/shard_map/ppermute | solution.py:567
  32.6 9.8 %collective-permute-start.11 = (bf16[17,32,128]{2,1,0:T(8,128)(2,1)S(1)}, bf16[17,32,128]{2,1,0:T(8,128)(2,1)S(1)}, u32[]{:S(2)}, u32[]{:S(2)}) collective-permute-start(bf16[17,32,128]{2,1,0:T(8,128)(2,1)S(1)} %get-tuple-element.49), channel_id=1, source_target_pairs={{0,2},{1,3},{2,0},{3,1},{4,6},{5,7},{6,4},{7,5},{8,10},{9,11},{10,... | collective-permute-start | bytes 417800 | tf_op jit(solution)/shard_map/ppermute | solution.py:567
  32.9 10.9 %collective-permute-start.16 = (bf16[17,32,128]{2,1,0:T(8,128)(2,1)S(1)}, bf16[17,32,128]{2,1,0:T(8,128)(2,1)S(1)}, u32[]{:S(2)}, u32[]{:S(2)}) collective-permute-start(bf16[17,32,128]{2,1,0:T(8,128)(2,1)S(1)} %get-tuple-element.59), channel_id=1, source_target_pairs={{0,1},{1,0},{2,3},{3,2},{4,5},{5,4},{6,7},{7,6},{8,9},{9,8},{10,11... | collective-permute-start | bytes 417800 | tf_op jit(solution)/shard_map/ppermute | solution.py:567
  35.8 6.6 %copy-start = (bf16[128,2048]{1,0:T(8,128)(2,1)S(1)}, bf16[128,2048]{1,0:T(8,128)(2,1)}, u32[]{:S(2)}) copy-start(bf16[128,2048]{1,0:T(8,128)(2,1)} %refs_0_.7) | copy-start | bytes 1572868
  35.9 6.6 %copy-start.1 = (bf16[128,2048]{1,0:T(8,128)(2,1)S(1)}, bf16[128,2048]{1,0:T(8,128)(2,1)}, u32[]{:S(2)}) copy-start(bf16[128,2048]{1,0:T(8,128)(2,1)} %refs_1_.7) | copy-start | bytes 1572868
  35.9 6.6 %copy-start.2 = (bf16[128,2048]{1,0:T(8,128)(2,1)S(1)}, bf16[128,2048]{1,0:T(8,128)(2,1)}, u32[]{:S(2)}) copy-start(bf16[128,2048]{1,0:T(8,128)(2,1)} %refs_2_.7) | copy-start | bytes 1572868
  35.9 6.6 %copy-start.3 = (bf16[128,2048]{1,0:T(8,128)(2,1)S(1)}, bf16[128,2048]{1,0:T(8,128)(2,1)}, u32[]{:S(2)}) copy-start(bf16[128,2048]{1,0:T(8,128)(2,1)} %refs_3_.7) | copy-start | bytes 1572868
  36.0 9.8 %collective-permute-start.13 = (bf16[4,128,128]{2,1,0:T(8,128)(2,1)S(1)}, bf16[4,128,128]{2,1,0:T(8,128)(2,1)S(1)}, u32[]{:S(2)}, u32[]{:S(2)}) collective-permute-start(bf16[4,128,128]{2,1,0:T(8,128)(2,1)S(1)} %get-tuple-element.56), channel_id=1, source_target_pairs={{0,24},{4,28},{8,16},{12,20},{16,8},{20,12},{24,0},{28,4},{1,25},{... | collective-permute-start | bytes 393224 | tf_op jit(solution)/shard_map/ppermute | solution.py:567
  37.5 8.3 %collective-permute-start.14 = (bf16[4,128,128]{2,1,0:T(8,128)(2,1)S(1)}, bf16[4,128,128]{2,1,0:T(8,128)(2,1)S(1)}, u32[]{:S(2)}, u32[]{:S(2)}) collective-permute-start(bf16[4,128,128]{2,1,0:T(8,128)(2,1)S(1)} %get-tuple-element.57), channel_id=1, source_target_pairs={{0,16},{4,20},{8,24},{12,28},{16,0},{20,4},{24,8},{28,12},{1,17},{... | collective-permute-start | bytes 393224 | tf_op jit(solution)/shard_map/ppermute | solution.py:567
  38.0 7.8 %collective-permute-start.15 = (bf16[4,128,128]{2,1,0:T(8,128)(2,1)S(1)}, bf16[4,128,128]{2,1,0:T(8,128)(2,1)S(1)}, u32[]{:S(2)}, u32[]{:S(2)}) collective-permute-start(bf16[4,128,128]{2,1,0:T(8,128)(2,1)S(1)} %get-tuple-element.58), channel_id=1, source_target_pairs={{0,8},{4,12},{8,0},{12,4},{16,24},{20,28},{24,16},{28,20},{1,9},{5... | collective-permute-start | bytes 393224 | tf_op jit(solution)/shard_map/ppermute | solution.py:567

commit v24 on v21

--- a/solution.py
+++ b/solution.py
@@ -173,13 +173,14 @@
                 residue = (first + slot) % DILATION if slots % DILATION else slot % DILATION
                 rowset = wide[index, which, slot, pl.ds(residue, quarter, stride=DILATION), :]
                 mids[index][which * slots + slot] = rowset.astype(BF16)
-        operands = [
-            [buffers[index, which, :, static_columns(slot)] for which in range(4)]
-            for slot in range(slots)
-        ]
-        for slot, (e, d) in enumerate(level_stats(operands)):
-            turn[pl.ds(first + slot, 1), :] = e
-            turn[pl.ds(HEADS + first + slot, 1), :] = d
+    heads = [(index, slot) for index in range(len(places)) for slot in range(slots)]
+    operands = [
+        [buffers[index, which, :, static_columns(slot)] for which in range(4)]
+        for index, slot in heads
+    ]
+    for (index, slot), (e, d) in zip(heads, level_stats(operands)):
+        turn[pl.ds(places[index] * slots + slot, 1), :] = e
+        turn[pl.ds(HEADS + places[index] * slots + slot, 1), :] = d
 
 
 def pick_first_kernel(n_i, slots, *refs):

time: 46.2 us -> 46.1 us (level)
  no operation moved by 1% of the time
where the time goes in v24:
time: 46.1 us; the launch traced here: 46 us
  starting transfers between devices  21.1 us (46%)
  Pallas kernels  13.2 us (29%)
  waiting for transfers between devices  10.8 us (23%)
  between operations  0.82 us (2%)
    ppermute x17, starting transfers between devices, swap(): return lax.ppermute(x, axis, [(i, i ^ mask) for i in range(n)])  21.1 us
    pallas_call x17, Pallas kernels, call(): pl.pallas_call(kernel, out_shape=tuple(outs), in_specs=[pl.BlockSpec(memo...  13.2 us
    ppermute x17, waiting for transfers between devices, swap(): return lax.ppermute(x, axis, [(i, i ^ mask) for i in range(n)])  10.8 us
  transfers between devices with their start and end apart: 17, of which 10 were waited for; matrix products, arithmetic and copies ran while one was open for 0% of the time, Pallas kernels for 19%

profile of v24, /device:TPU:0, one launch (start us, length us, event | category | flops | bytes accessed | tf_op | source)
XLA Modules:
  0.0 46.0 jit_solution(10810775252591311217)
XLA Ops:
  0.6 2.2 %pick_first.1 = (bf16[17,32,128]{2,1,0:T(8,128)(2,1)S(1)}, bf16[17,32,128]{2,1,0:T(8,128)(2,1)S(1)}, bf16[4,128,128]{2,1,0:T(8,128)(2,1)S(1)}, bf16[4,128,128]{2...) custom-call(bf16[128,2048]{1,0:T(8,128)(2,1)} %refs_0_.7, ...), custom_call_target="tpu_custom_call" | custom-call | flops 67108864 | bytes 2916352 | tf_op jit(solution)/shard_map/pick_first/pallas_call | solution.py:548
  2.9 5.1 %collective-permute-start = (bf16[17,32,128]{2,1,0:T(8,128)(2,1)S(1)}, bf16[17,32,128]{2,1,0:T(8,128)(2,1)S(1)}, u32[]{:S(2)}, u32[]{:S(2)}) collective-permute-start(bf16[17,32,128]{2,1,0:T(8,128)(2,1)S(1)} %get-tuple-element.37), channel_id=1, source_target_pairs={{0,3},{1,2},{2,1},{3,0},{4,7},{5,6},{6,5},{7,4},{8,11},{9,10},{10,... | collective-permute-start | bytes 417800 | tf_op jit(solution)/shard_map/ppermute | solution.py:568
  8.0 2.4 %collective-permute-start.3 = (bf16[4,128,128]{2,1,0:T(8,128)(2,1)S(1)}, bf16[4,128,128]{2,1,0:T(8,128)(2,1)S(1)}, u32[]{:S(2)}, u32[]{:S(2)}) collective-permute-start(bf16[4,128,128]{2,1,0:T(8,128)(2,1)S(1)} %get-tuple-element.41), channel_id=1, source_target_pairs={{0,24},{4,28},{8,16},{12,20},{16,8},{20,12},{24,0},{28,4},{1,25},{... | collective-permute-start | bytes 393224 | tf_op jit(solution)/shard_map/ppermute | solution.py:568
  10.4 0.5 %collective-permute-start.4 = (bf16[4,128,128]{2,1,0:T(8,128)(2,1)S(1)}, bf16[4,128,128]{2,1,0:T(8,128)(2,1)S(1)}, u32[]{:S(2)}, u32[]{:S(2)}) collective-permute-start(bf16[4,128,128]{2,1,0:T(8,128)(2,1)S(1)} %get-tuple-element.42), channel_id=1, source_target_pairs={{0,16},{4,20},{8,24},{12,28},{16,0},{20,4},{24,8},{28,12},{1,17},{... | collective-permute-start | bytes 393224 | tf_op jit(solution)/shard_map/ppermute | solution.py:568
  10.9 0.5 %collective-permute-start.5 = (bf16[4,128,128]{2,1,0:T(8,128)(2,1)S(1)}, bf16[4,128,128]{2,1,0:T(8,128)(2,1)S(1)}, u32[]{:S(2)}, u32[]{:S(2)}) collective-permute-start(bf16[4,128,128]{2,1,0:T(8,128)(2,1)S(1)} %get-tuple-element.43), channel_id=1, source_target_pairs={{0,8},{4,12},{8,0},{12,4},{16,24},{20,28},{24,16},{28,20},{1,9},{5... | collective-permute-start | bytes 393224 | tf_op jit(solution)/shard_map/ppermute | solution.py:568
  11.5 2.1 %pick_rest.1 = (bf16[17,32,128]{2,1,0:T(8,128)(2,1)S(1)}, bf16[17,32,128]{2,1,0:T(8,128)(2,1)S(1)}, f32[32,128]{1,0:T(8,128)S(1)}) custom-call(bf16[128,2048]{1,0:T(8,128)(2,1)} %refs_0_.7, bf16[128,2048]{1,0:T(8,128)(2,1)} %refs_1_.7, bf16[128,2048]{1,0:T(8,128)(2,1)} %refs_2_.7, bf16[128,2048]{1,0:T(8,128)(2,1)} %refs_3_.7, ...), custom_call_target="tpu_custom_call" | custom-call | flops 134217728 | bytes 2408448 | tf_op jit(solution)/shard_map/pick_rest/pallas_call | solution.py:548
  13.7 0.7 %collective-permute-start.2 = (bf16[17,32,128]{2,1,0:T(8,128)(2,1)S(1)}, bf16[17,32,128]{2,1,0:T(8,128)(2,1)S(1)}, u32[]{:S(2)}, u32[]{:S(2)}) collective-permute-start(bf16[17,32,128]{2,1,0:T(8,128)(2,1)S(1)} %get-tuple-element.39), channel_id=1, source_target_pairs={{0,1},{1,0},{2,3},{3,2},{4,5},{5,4},{6,7},{7,6},{8,9},{9,8},{10,11... | collective-permute-start | bytes 417800 | tf_op jit(solution)/shard_map/ppermute | solution.py:568
  14.4 2.3 %collective-permute-done.4.refs_2_ = bf16[4,128,128]{2,1,0:T(8,128)(2,1)S(1)} collective-permute-done((bf16[4,128,128]{2,1,0:T(8,128)(2,1)S(1)}, bf16[4,128,128]{2,1,0:T(8,128)(2,1)S(1)}, u32[]{:S(2)}, u32[]{:S(2)}) %collective-permute-start.4) | collective-permute-done | bytes 131104 | tf_op jit(solution)/shard_map/ppermute | solution.py:568
  16.8 1.5 %collective-permute-done.6.refs_4_ = bf16[4,2,128,128]{3,2,1,0:T(8,128)(2,1)S(1)} collective-permute-done((bf16[4,2,128,128]{3,2,1,0:T(8,128)(2,1)S(1)}, bf16[4,2,128,128]{3,2,1,0:T(8,128)(2,1)S(1)}, u32[]{:S(2)}, u32[]{:S(2)}) %collective-permute-start.6) | collective-permute-done | bytes 262176 | tf_op jit(solution)/shard_map/ppermute | solution.py:568
  18.3 1.1 %far_stats.1.refs_5_ = f32[8,128]{1,0:T(8,128)S(1)} custom-call(bf16[4,128,128]{2,1,0:T(8,128)(2,1)S(1)} %get-tuple-element.40.refs_0_, bf16[4,128,128]{2,1,0:T(8,128)(2,1)S(1)} %collective-permute-done.3.refs_1_, bf16[4,128,128]{2,1,0:T(8,128)(2,1)S(1)} %collective-permute-done.4.refs_2_, bf16[4,128,128]{2,1,0:T(8,128)(2,1)S(1)} %collective-permute-done.5.refs_3_, ...), custom_call_target="tpu_custom_call" | custom-call | flops 1 | bytes 794624 | tf_op jit(solution)/shard_map/far_stats/pallas_call | solution.py:548
  19.5 1.4 %collective-permute-done.1.refs_2_ = bf16[17,32,128]{2,1,0:T(8,128)(2,1)S(1)} collective-permute-done((bf16[17,32,128]{2,1,0:T(8,128)(2,1)S(1)}, bf16[17,32,128]{2,1,0:T(8,128)(2,1)S(1)}, u32[]{:S(2)}, u32[]{:S(2)}) %collective-permute-start.1) | collective-permute-done | bytes 139296 | tf_op jit(solution)/shard_map/ppermute | solution.py:568
  20.9 0.1 collective-permute-done.2.refs_3_
  21.0 0.5 %middle_stats.1 = (f32[16,128]{1,0:T(8,128)S(1)}, f32[8,128]{1,0:T(8,128)S(1)}, f32[128,128]{1,0:T(8,128)S(1)}) custom-call(bf16[17,32,128]{2,1,0:T(8,128)(2,1)S(1)} %get-tuple-element.36.refs_0_, bf16[17,32,128]{2,1,0:T(8,128)(2,1)S(1)} %collective-permute-done.refs_0_.refs_1_, bf16[17,32,128]{2,1,0:T(8,128)(2,1)S(1)} %collective-permute-done.1.refs_2_, ...), custom_call_target="tpu_custom_call" | custom-call | flops 33554432 | bytes 655360 | tf_op jit(solution)/shard_map/middle_stats/pallas_call | solution.py:548
  21.5 2.5 %collective-permute-start.9 = (f32[16,128]{1,0:T(8,128)S(1)}, f32[16,128]{1,0:T(8,128)S(1)}, u32[]{:S(2)}, u32[]{:S(2)}) collective-permute-start(f32[16,128]{1,0:T(8,128)S(1)} %get-tuple-element.46.refs_6_.refs_8_.refs_5_), channel_id=1, source_target_pairs={{0,24},{4,28},{8,16},{12,20},{16,8},{20,12},{24,0},{28,4},{1,25},{... | collective-permute-start | bytes 24584 | tf_op jit(solution)/shard_map/ppermute | solution.py:568
  24.0 0.5 %collective-permute-start.8 = (f32[16,128]{1,0:T(8,128)S(1)}, f32[16,128]{1,0:T(8,128)S(1)}, u32[]{:S(2)}, u32[]{:S(2)}) collective-permute-start(f32[16,128]{1,0:T(8,128)S(1)} %get-tuple-element.46.refs_6_.refs_8_.refs_5_), channel_id=1, source_target_pairs={{0,16},{4,20},{8,24},{12,28},{16,0},{20,4},{24,8},{28,12},{1,17},{... | collective-permute-start | bytes 24584 | tf_op jit(solution)/shard_map/ppermute | solution.py:568
  24.5 0.5 %collective-permute-start.7 = (f32[16,128]{1,0:T(8,128)S(1)}, f32[16,128]{1,0:T(8,128)S(1)}, u32[]{:S(2)}, u32[]{:S(2)}) collective-permute-start(f32[16,128]{1,0:T(8,128)S(1)} %get-tuple-element.46.refs_6_.refs_8_.refs_5_), channel_id=1, source_target_pairs={{0,8},{4,12},{8,0},{12,4},{16,24},{20,28},{24,16},{28,20},{1,9},{5... | collective-permute-start | bytes 24584 | tf_op jit(solution)/shard_map/ppermute | solution.py:568
  25.1 1.1 %collective-permute-done.9.refs_9_.refs_11_.refs_8_ = f32[16,128]{1,0:T(8,128)S(1)} collective-permute-done((f32[16,128]{1,0:T(8,128)S(1)}, f32[16,128]{1,0:T(8,128)S(1)}, u32[]{:S(2)}, u32[]{:S(2)}) %collective-permute-start.9) | collective-permute-done | bytes 8224 | tf_op jit(solution)/shard_map/ppermute | solution.py:568
  26.1 1.5 %collective-permute-done.8.refs_8_.refs_10_.refs_7_ = f32[16,128]{1,0:T(8,128)S(1)} collective-permute-done((f32[16,128]{1,0:T(8,128)S(1)}, f32[16,128]{1,0:T(8,128)S(1)}, u32[]{:S(2)}, u32[]{:S(2)}) %collective-permute-start.8) | collective-permute-done | bytes 8224 | tf_op jit(solution)/shard_map/ppermute | solution.py:568
  27.7 0.5 %collective-permute-done.7.refs_7_.refs_9_.refs_6_ = f32[16,128]{1,0:T(8,128)S(1)} collective-permute-done((f32[16,128]{1,0:T(8,128)S(1)}, f32[16,128]{1,0:T(8,128)S(1)}, u32[]{:S(2)}, u32[]{:S(2)}) %collective-permute-start.7) | collective-permute-done | bytes 8224 | tf_op jit(solution)/shard_map/ppermute | solution.py:568
  28.2 0.6 %middle_parts.1 = (bf16[17,32,128]{2,1,0:T(8,128)(2,1)S(1)}, bf16[17,32,128]{2,1,0:T(8,128)(2,1)S(1)}, bf16[17,32,128]{2,1,0:T(8,128)(2,1)S(1)}, bf16[17,32,128]{2,1,0:T(8,128)(2,1)S(1)}) custom-call(bf16[17,32,128]{2,1,0:T(8,128)(2,1)S(1)} %get-tuple-element.36.refs_0_, bf16[17,32,128]{2,1,0:T(8,128)(2,1)S(1)} %collective-permute-done.refs_0_.refs_1_, ...), custom_call_target="tpu_custom_call" | custom-call | flops 100663296 | bytes 1216512 | tf_op jit(solution)/shard_map/middle_parts/pallas_call | solution.py:548
  28.8 1.5 %collective-permute-start.10 = (bf16[17,32,128]{2,1,0:T(8,128)(2,1)S(1)}, bf16[17,32,128]{2,1,0:T(8,128)(2,1)S(1)}, u32[]{:S(2)}, u32[]{:S(2)}) collective-permute-start(bf16[17,32,128]{2,1,0:T(8,128)(2,1)S(1)} %get-tuple-element.48), channel_id=1, source_target_pairs={{0,3},{1,2},{2,1},{3,0},{4,7},{5,6},{6,5},{7,4},{8,11},{9,10},{10,... | collective-permute-start | bytes 417800 | tf_op jit(solution)/shard_map/ppermute | solution.py:568
  30.3 2.1 %far_parts.1 = (bf16[4,128,128]{2,1,0:T(8,128)(2,1)S(1)}, bf16[4,128,128]{2,1,0:T(8,128)(2,1)S(1)}, bf16[4,128,128]{2,1,0:T(8,128)(2,1)S(1)}, bf16[4,128,128]{2,...) custom-call(bf16[4,128,128]{2,1,0:T(8,128)(2,1)S(1)} %get-tuple-element.40.refs_0_, ...), custom_call_target="tpu_custom_call" | custom-call | flops 1 | bytes 1 | tf_op jit(solution)/shard_map/far_parts/pallas_call | solution.py:548
  32.5 0.2 collective-permute-start.11
  32.7 2.8 %collective-permute-start.16 = (bf16[17,32,128]{2,1,0:T(8,128)(2,1)S(1)}, bf16[17,32,128]{2,1,0:T(8,128)(2,1)S(1)}, u32[]{:S(2)}, u32[]{:S(2)}) collective-permute-start(bf16[17,32,128]{2,1,0:T(8,128)(2,1)S(1)} %get-tuple-element.59), channel_id=1, source_target_pairs={{0,2},{1,3},{2,0},{3,1},{4,6},{5,7},{6,4},{7,5},{8,10},{9,11},{10,... | collective-permute-start | bytes 417800 | tf_op jit(solution)/shard_map/ppermute | solution.py:568
  35.5 0.2 collective-permute-done.10.refs_6_.refs_0_
  35.9 1.6 %collective-permute-start.13 = (bf16[4,128,128]{2,1,0:T(8,128)(2,1)S(1)}, bf16[4,128,128]{2,1,0:T(8,128)(2,1)S(1)}, u32[]{:S(2)}, u32[]{:S(2)}) collective-permute-start(bf16[4,128,128]{2,1,0:T(8,128)(2,1)S(1)} %get-tuple-element.56), channel_id=1, source_target_pairs={{0,24},{4,28},{8,16},{12,20},{16,8},{20,12},{24,0},{28,4},{1,25},{... | collective-permute-start | bytes 393224 | tf_op jit(solution)/shard_map/ppermute | solution.py:568
  37.4 0.5 %collective-permute-start.14 = (bf16[4,128,128]{2,1,0:T(8,128)(2,1)S(1)}, bf16[4,128,128]{2,1,0:T(8,128)(2,1)S(1)}, u32[]{:S(2)}, u32[]{:S(2)}) collective-permute-start(bf16[4,128,128]{2,1,0:T(8,128)(2,1)S(1)} %get-tuple-element.57), channel_id=1, source_target_pairs={{0,16},{4,20},{8,24},{12,28},{16,0},{20,4},{24,8},{28,12},{1,17},{... | collective-permute-start | bytes 393224 | tf_op jit(solution)/shard_map/ppermute | solution.py:568
  37.9 1.5 %collective-permute-start.15 = (bf16[4,128,128]{2,1,0:T(8,128)(2,1)S(1)}, bf16[4,128,128]{2,1,0:T(8,128)(2,1)S(1)}, u32[]{:S(2)}, u32[]{:S(2)}) collective-permute-start(bf16[4,128,128]{2,1,0:T(8,128)(2,1)S(1)} %get-tuple-element.58), channel_id=1, source_target_pairs={{0,8},{4,12},{8,0},{12,4},{16,24},{20,28},{24,16},{28,20},{1,9},{5... | collective-permute-start | bytes 393224 | tf_op jit(solution)/shard_map/ppermute | solution.py:568
  39.4 2.0 %collective-permute-done.11.refs_7_ = bf16[17,32,128]{2,1,0:T(8,128)(2,1)S(1)} collective-permute-done((bf16[17,32,128]{2,1,0:T(8,128)(2,1)S(1)}, bf16[17,32,128]{2,1,0:T(8,128)(2,1)S(1)}, u32[]{:S(2)}, u32[]{:S(2)}) %collective-permute-start.11) | collective-permute-done | bytes 139296 | tf_op jit(solution)/shard_map/ppermute | solution.py:568
  41.5 1.4 %near_early.1.refs_5_.early_ref = f32[4,12,128,128]{3,2,1,0:T(8,128)S(1)} custom-call(bf16[128,2048]{1,0:T(8,128)(2,1)S(1)} %copy-done, bf16[128,2048]{1,0:T(8,128)(2,1)S(1)} %copy-done.1, bf16[128,2048]{1,0:T(8,128)(2,1)S(1)} %copy-done.2, bf16[128,2048]{1,0:T(8,128)(2,1)S(1)} %copy-done.3, f32[32,128]{1,0:T(8,128)S(1)} %get-tuple-element.35.refs_0_.refs_4_, ...), custom_call_target="tpu_custom_call" | custom-call | flops 2000000000 | bytes 5709824 | tf_op jit(solution)/shard_map/near_early/pallas_call | solution.py:548
  42.9 1.9 %final_others.1 = (bf16[128,2048]{1,0:T(8,128)(2,1)}, bf16[128,2048]{1,0:T(8,128)(2,1)}, bf16[128,2048]{1,0:T(8,128)(2,1)}, bf16[128,2048]{1,0:T(8,128)(2,1)}) custom-call(bf16[128,2048]{1,0:T(8,128)(2,1)S(1)} %copy-done, bf16[128,2048]{1,0:T(8,128)(2,1)S(1)} %copy-done.1, bf16[128,2048]{1,0:T(8,128)(2,1)S(1)} %copy-done.2, bf16[128,2048]{1,0:T(8,128)(2,1)S(1)} %copy-done.3, ...), custom_call_target="tpu_custom_call" | custom-call | flops 1000000000 | bytes 7774208 | tf_op jit(solution)/shard_map/final_others/pallas_call | solution.py:548
  44.8 1.1 %final_own.1 = (bf16[128,2048]{1,0:T(8,128)(2,1)}, bf16[128,2048]{1,0:T(8,128)(2,1)}, bf16[128,2048]{1,0:T(8,128)(2,1)}, bf16[128,2048]{1,0:T(8,128)(2,1)}) custom-call(f32[4,12,128,128]{3,2,1,0:T(8,128)S(1)} %near_early.1.refs_5_.early_ref, ...), custom_call_target="tpu_custom_call", output_to_operand_aliasing={{0}: (6, {}), {1}: (7, {}), {2}: (8, {}), {3}: (9, {})} | custom-call | flops 16777216 | bytes 8003584 | tf_op jit(solution)/shard_map/final_own/pallas_call | solution.py:548
  (27 shorter events, 0.4 us)
Async XLA Ops:
  2.9 10.8 %collective-permute-start = (bf16[17,32,128]{2,1,0:T(8,128)(2,1)S(1)}, bf16[17,32,128]{2,1,0:T(8,128)(2,1)S(1)}, u32[]{:S(2)}, u32[]{:S(2)}) collective-permute-start(bf16[17,32,128]{2,1,0:T(8,128)(2,1)S(1)} %get-tuple-element.37), channel_id=1, source_target_pairs={{0,3},{1,2},{2,1},{3,0},{4,7},{5,6},{6,5},{7,4},{8,11},{9,10},{10,... | collective-permute-start | bytes 417800 | tf_op jit(solution)/shard_map/ppermute | solution.py:568
  8.0 6.4 %collective-permute-start.3 = (bf16[4,128,128]{2,1,0:T(8,128)(2,1)S(1)}, bf16[4,128,128]{2,1,0:T(8,128)(2,1)S(1)}, u32[]{:S(2)}, u32[]{:S(2)}) collective-permute-start(bf16[4,128,128]{2,1,0:T(8,128)(2,1)S(1)} %get-tuple-element.41), channel_id=1, source_target_pairs={{0,24},{4,28},{8,16},{12,20},{16,8},{20,12},{24,0},{28,4},{1,25},{... | collective-permute-start | bytes 393224 | tf_op jit(solution)/shard_map/ppermute | solution.py:568
  10.4 6.2 %collective-permute-start.4 = (bf16[4,128,128]{2,1,0:T(8,128)(2,1)S(1)}, bf16[4,128,128]{2,1,0:T(8,128)(2,1)S(1)}, u32[]{:S(2)}, u32[]{:S(2)}) collective-permute-start(bf16[4,128,128]{2,1,0:T(8,128)(2,1)S(1)} %get-tuple-element.42), channel_id=1, source_target_pairs={{0,16},{4,20},{8,24},{12,28},{16,0},{20,4},{24,8},{28,12},{1,17},{... | collective-permute-start | bytes 393224 | tf_op jit(solution)/shard_map/ppermute | solution.py:568
  10.9 5.8 %collective-permute-start.5 = (bf16[4,128,128]{2,1,0:T(8,128)(2,1)S(1)}, bf16[4,128,128]{2,1,0:T(8,128)(2,1)S(1)}, u32[]{:S(2)}, u32[]{:S(2)}) collective-permute-start(bf16[4,128,128]{2,1,0:T(8,128)(2,1)S(1)} %get-tuple-element.43), channel_id=1, source_target_pairs={{0,8},{4,12},{8,0},{12,4},{16,24},{20,28},{24,16},{28,20},{1,9},{5... | collective-permute-start | bytes 393224 | tf_op jit(solution)/shard_map/ppermute | solution.py:568
  13.6 7.3 %collective-permute-start.1 = (bf16[17,32,128]{2,1,0:T(8,128)(2,1)S(1)}, bf16[17,32,128]{2,1,0:T(8,128)(2,1)S(1)}, u32[]{:S(2)}, u32[]{:S(2)}) collective-permute-start(bf16[17,32,128]{2,1,0:T(8,128)(2,1)S(1)} %get-tuple-element.38), channel_id=1, source_target_pairs={{0,2},{1,3},{2,0},{3,1},{4,6},{5,7},{6,4},{7,5},{8,10},{9,11},{10,... | collective-permute-start | bytes 417800 | tf_op jit(solution)/shard_map/ppermute | solution.py:568
  13.7 7.3 %collective-permute-start.2 = (bf16[17,32,128]{2,1,0:T(8,128)(2,1)S(1)}, bf16[17,32,128]{2,1,0:T(8,128)(2,1)S(1)}, u32[]{:S(2)}, u32[]{:S(2)}) collective-permute-start(bf16[17,32,128]{2,1,0:T(8,128)(2,1)S(1)} %get-tuple-element.39), channel_id=1, source_target_pairs={{0,1},{1,0},{2,3},{3,2},{4,5},{5,4},{6,7},{7,6},{8,9},{9,8},{10,11... | collective-permute-start | bytes 417800 | tf_op jit(solution)/shard_map/ppermute | solution.py:568
  16.7 1.6 %collective-permute-start.6 = (bf16[4,2,128,128]{3,2,1,0:T(8,128)(2,1)S(1)}, bf16[4,2,128,128]{3,2,1,0:T(8,128)(2,1)S(1)}, u32[]{:S(2)}, u32[]{:S(2)}) collective-permute-start(bf16[4,2,128,128]{3,2,1,0:T(8,128)(2,1)S(1)} %pack.1), channel_id=1, source_target_pairs={{0,4},{4,0},{8,12},{12,8},{16,20},{20,16},{24,28},{28,24},{1,5},{5... | collective-permute-start | bytes 786440 | tf_op jit(solution)/shard_map/ppermute | solution.py:568
  21.5 4.6 %collective-permute-start.9 = (f32[16,128]{1,0:T(8,128)S(1)}, f32[16,128]{1,0:T(8,128)S(1)}, u32[]{:S(2)}, u32[]{:S(2)}) collective-permute-start(f32[16,128]{1,0:T(8,128)S(1)} %get-tuple-element.46.refs_6_.refs_8_.refs_5_), channel_id=1, source_target_pairs={{0,24},{4,28},{8,16},{12,20},{16,8},{20,12},{24,0},{28,4},{1,25},{... | collective-permute-start | bytes 24584 | tf_op jit(solution)/shard_map/ppermute | solution.py:568
  24.0 3.7 %collective-permute-start.8 = (f32[16,128]{1,0:T(8,128)S(1)}, f32[16,128]{1,0:T(8,128)S(1)}, u32[]{:S(2)}, u32[]{:S(2)}) collective-permute-start(f32[16,128]{1,0:T(8,128)S(1)} %get-tuple-element.46.refs_6_.refs_8_.refs_5_), channel_id=1, source_target_pairs={{0,16},{4,20},{8,24},{12,28},{16,0},{20,4},{24,8},{28,12},{1,17},{... | collective-permute-start | bytes 24584 | tf_op jit(solution)/shard_map/ppermute | solution.py:568
  24.5 3.7 %collective-permute-start.7 = (f32[16,128]{1,0:T(8,128)S(1)}, f32[16,128]{1,0:T(8,128)S(1)}, u32[]{:S(2)}, u32[]{:S(2)}) collective-permute-start(f32[16,128]{1,0:T(8,128)S(1)} %get-tuple-element.46.refs_6_.refs_8_.refs_5_), channel_id=1, source_target_pairs={{0,8},{4,12},{8,0},{12,4},{16,24},{20,28},{24,16},{28,20},{1,9},{5... | collective-permute-start | bytes 24584 | tf_op jit(solution)/shard_map/ppermute | solution.py:568
  28.8 6.9 %collective-permute-start.10 = (bf16[17,32,128]{2,1,0:T(8,128)(2,1)S(1)}, bf16[17,32,128]{2,1,0:T(8,128)(2,1)S(1)}, u32[]{:S(2)}, u32[]{:S(2)}) collective-permute-start(bf16[17,32,128]{2,1,0:T(8,128)(2,1)S(1)} %get-tuple-element.48), channel_id=1, source_target_pairs={{0,3},{1,2},{2,1},{3,0},{4,7},{5,6},{6,5},{7,4},{8,11},{9,10},{10,... | collective-permute-start | bytes 417800 | tf_op jit(solution)/shard_map/ppermute | solution.py:568
  32.5 3.3 %collective-permute-start.12 = (bf16[4,2,128,128]{3,2,1,0:T(8,128)(2,1)S(1)}, bf16[4,2,128,128]{3,2,1,0:T(8,128)(2,1)S(1)}, u32[]{:S(2)}, u32[]{:S(2)}) collective-permute-start(bf16[4,2,128,128]{3,2,1,0:T(8,128)(2,1)S(1)} %get-tuple-element.54), channel_id=1, source_target_pairs={{0,4},{4,0},{8,12},{12,8},{16,20},{20,16},{24,28},{28,24},{1,5},{5... | collective-permute-start | bytes 786440 | tf_op jit(solution)/shard_map/ppermute | solution.py:568
  32.5 8.9 %collective-permute-start.11 = (bf16[17,32,128]{2,1,0:T(8,128)(2,1)S(1)}, bf16[17,32,128]{2,1,0:T(8,128)(2,1)S(1)}, u32[]{:S(2)}, u32[]{:S(2)}) collective-permute-start(bf16[17,32,128]{2,1,0:T(8,128)(2,1)S(1)} %get-tuple-element.49), channel_id=1, source_target_pairs={{0,1},{1,0},{2,3},{3,2},{4,5},{5,4},{6,7},{7,6},{8,9},{9,8},{10,11... | collective-permute-start | bytes 417800 | tf_op jit(solution)/shard_map/ppermute | solution.py:568
  32.7 10.1 %collective-permute-start.16 = (bf16[17,32,128]{2,1,0:T(8,128)(2,1)S(1)}, bf16[17,32,128]{2,1,0:T(8,128)(2,1)S(1)}, u32[]{:S(2)}, u32[]{:S(2)}) collective-permute-start(bf16[17,32,128]{2,1,0:T(8,128)(2,1)S(1)} %get-tuple-element.59), channel_id=1, source_target_pairs={{0,2},{1,3},{2,0},{3,1},{4,6},{5,7},{6,4},{7,5},{8,10},{9,11},{10,... | collective-permute-start | bytes 417800 | tf_op jit(solution)/shard_map/ppermute | solution.py:568
  35.7 5.7 %copy-start = (bf16[128,2048]{1,0:T(8,128)(2,1)S(1)}, bf16[128,2048]{1,0:T(8,128)(2,1)}, u32[]{:S(2)}) copy-start(bf16[128,2048]{1,0:T(8,128)(2,1)} %refs_0_.7) | copy-start | bytes 1572868
  35.7 5.7 %copy-start.1 = (bf16[128,2048]{1,0:T(8,128)(2,1)S(1)}, bf16[128,2048]{1,0:T(8,128)(2,1)}, u32[]{:S(2)}) copy-start(bf16[128,2048]{1,0:T(8,128)(2,1)} %refs_1_.7) | copy-start | bytes 1572868
  35.8 5.7 %copy-start.2 = (bf16[128,2048]{1,0:T(8,128)(2,1)S(1)}, bf16[128,2048]{1,0:T(8,128)(2,1)}, u32[]{:S(2)}) copy-start(bf16[128,2048]{1,0:T(8,128)(2,1)} %refs_2_.7) | copy-start | bytes 1572868
  35.8 5.7 %copy-start.3 = (bf16[128,2048]{1,0:T(8,128)(2,1)S(1)}, bf16[128,2048]{1,0:T(8,128)(2,1)}, u32[]{:S(2)}) copy-start(bf16[128,2048]{1,0:T(8,128)(2,1)} %refs_3_.7) | copy-start | bytes 1572868
  35.9 8.9 %collective-permute-start.13 = (bf16[4,128,128]{2,1,0:T(8,128)(2,1)S(1)}, bf16[4,128,128]{2,1,0:T(8,128)(2,1)S(1)}, u32[]{:S(2)}, u32[]{:S(2)}) collective-permute-start(bf16[4,128,128]{2,1,0:T(8,128)(2,1)S(1)} %get-tuple-element.56), channel_id=1, source_target_pairs={{0,24},{4,28},{8,16},{12,20},{16,8},{20,12},{24,0},{28,4},{1,25},{... | collective-permute-start | bytes 393224 | tf_op jit(solution)/shard_map/ppermute | solution.py:568
  37.4 7.4 %collective-permute-start.14 = (bf16[4,128,128]{2,1,0:T(8,128)(2,1)S(1)}, bf16[4,128,128]{2,1,0:T(8,128)(2,1)S(1)}, u32[]{:S(2)}, u32[]{:S(2)}) collective-permute-start(bf16[4,128,128]{2,1,0:T(8,128)(2,1)S(1)} %get-tuple-element.57), channel_id=1, source_target_pairs={{0,16},{4,20},{8,24},{12,28},{16,0},{20,4},{24,8},{28,12},{1,17},{... | collective-permute-start | bytes 393224 | tf_op jit(solution)/shard_map/ppermute | solution.py:568
  37.9 6.9 %collective-permute-start.15 = (bf16[4,128,128]{2,1,0:T(8,128)(2,1)S(1)}, bf16[4,128,128]{2,1,0:T(8,128)(2,1)S(1)}, u32[]{:S(2)}, u32[]{:S(2)}) collective-permute-start(bf16[4,128,128]{2,1,0:T(8,128)(2,1)S(1)} %get-tuple-element.58), channel_id=1, source_target_pairs={{0,8},{4,12},{8,0},{12,4},{16,24},{20,28},{24,16},{28,20},{1,9},{5... | collective-permute-start | bytes 393224 | tf_op jit(solution)/shard_map/ppermute | solution.py:568
